TPU v7x, 32 devices: a whole 2x2x4 slice. The times are simulated.
32 devices in a mesh: grp: 2 (over x), layer: 8 (over z, y), ex: 2 (over core).
Axes of the slice: x: 2, y: 2, z: 4, core: 2. Of those that a mesh axis runs over, the one named last changes fastest.
Arguments:
- store: bfloat16 [8, 4096, 4096], P('layer', ('grp', 'ex')), parts along dimension 1, may hold values from -0.03125 to 0.03125
- queries: bfloat16 [8, 1024, 4096], P('layer', ('grp', 'ex')), parts along dimension 1, may hold values from -6 to 6
- left_inv: bfloat16 [8, 32, 32], P('layer')
- right_inv: bfloat16 [8, 128, 128], P('layer')
- query_prompt: int32 [1024], P('grp'), parts along dimension 0, may hold values from 0 to 127, as said below
- winner: int32 [256], P('grp'), parts along dimension 0, may hold values from 0 to 511, as said below
Outputs:
- scores: bfloat16 [512, 4096], P(None, ('grp', 'ex')), parts along dimension 1
- advantage: bfloat16 [128, 4096], P(None, ('grp', 'ex')), parts along dimension 1
There are 2 independent parts, one for each index of `grp`. A program takes and returns all parts, laid end to end along the dimension named above; an argument that names none is the same for every part. Nothing has to cross between parts.
Inputs may be any that keep to these rules, and one draw needn't show every extreme that they name: `query_prompt`: each prompt id appears for exactly 4 responses. winner[p] is a response whose query_prompt is p.
All inputs are finite; a program needn't handle non-finite values.
Results may differ from a plain program's by a relative error of at most 0.0067.
Values may be sent and summed in bfloat16 or wider, within the bound.
No kernel may reach another device: no remote copies, remote signals or barrier semaphores. Data moves between devices by JAX's collectives and lax.ppermute only.
A program may use at most 64 MiB of HBM per device.

v0:
```python
import jax
import jax.numpy as jnp
from jax import lax
from jax.sharding import PartitionSpec as P

KIN = 32
KOUT = 128
BEST = 4


def passed_along(block, axis, distance):
    devices = range(lax.axis_size(axis))
    route = [((i - distance) % len(devices), i) for i in devices]
    return lax.ppermute(block, axis, route)


def precondition(block, left_inv, right_inv):
    layers = block.shape[0]
    count = block.shape[1]
    blocks = block.reshape(layers, count, KIN, KOUT)
    half = jnp.einsum(
        "lqik,lkm->lqim", blocks, right_inv, preferred_element_type=jnp.float32
    ).astype(jnp.bfloat16)
    pre = jnp.einsum("lij,lqjm->lqim", left_inv, half, preferred_element_type=jnp.float32).astype(
        jnp.bfloat16
    )
    return pre.reshape(layers, count, KIN * KOUT)


def score_block(ready, store):
    return jnp.einsum("lqp,lep->qe", ready, store, preferred_element_type=jnp.float32)


def shards(store, queries, left_inv, right_inv, query_prompt, winner):
    block_rows = queries.shape[1]
    mine = precondition(queries, left_inv, right_inv)
    ex_count = lax.axis_size("ex")
    position = lax.axis_index("ex")
    partial_value = jnp.zeros((block_rows * ex_count, store.shape[1]), jnp.float32)
    current = mine
    for step in range(ex_count):
        if step > 0:
            current = passed_along(current, "ex", 1)
        source = (position - step) % ex_count
        tile = score_block(current, store)
        partial_value = lax.dynamic_update_slice_in_dim(partial_value, tile, source * block_rows, 0)
    scores = lax.psum(partial_value, "layer").astype(jnp.bfloat16)
    ids = jnp.arange(scores.shape[0], dtype=jnp.int32)
    prompts = jnp.arange(winner.shape[0], dtype=jnp.int32)
    picks = (winner[:, None] == ids[None, :]).astype(jnp.float32)
    member = (query_prompt[None, :] == prompts[:, None]).astype(jnp.float32)
    weights = (picks - member / BEST).astype(jnp.bfloat16)
    advantage = jnp.dot(weights, scores, preferred_element_type=jnp.float32)
    return (scores, advantage.astype(jnp.bfloat16))


def solution(mesh):
    return jax.shard_map(
        shards,
        mesh=mesh,
        in_specs=(
            P("layer", ("grp", "ex"), None),
            P("layer", ("grp", "ex"), None),
            P("layer", None, None),
            P("layer", None, None),
            P("grp"),
            P("grp"),
        ),
        out_specs=(P(None, ("grp", "ex")), P(None, ("grp", "ex"))),
        check_vma=False,
    )
```

profile of v0, /device:TPU:0, one launch (start us, length us, event | category | flops | bytes accessed | tf_op | source)
XLA Modules:
  0.0 116.5 jit_solution(9075131086210205770)
XLA Ops:
  0.6 0.0 copy-start
  0.6 0.0 copy-start.4
  0.7 3.4 %copy.8 = bf16[32,8,32,128]{3,2,1,0:T(8,128)(2,1)} copy(bf16[32,8,32,128]{3,1,2,0:T(8,128)(2,1)} %bitcast.43) | data formatting | bytes 4194304
  4.1 0.0 copy-done
  4.1 0.0 copy-done.4
  4.1 2.9 %fusion.11 = bf16[256,128,32]{1,2,0:T(8,128)(2,1)S(1)} fusion(bf16[256,32,128]{2,1,0:T(8,128)(2,1)} %bitcast.42, bf16[1,128,128]{2,1,0:T(8,128)(2,1)S(1)} %copy-done, bf16[1,32,32]{2,1,0:T(8,128)(2,1)S(1)} %copy-done.4), kind=kOutput, calls=%fused_computation.10 | convolution fusion | flops 337641472 | bytes 4229120 | tf_op jit(solution)/shard_map/lij,lqjm->lqim/dot_general | solution.py:24
  7.0 0.0 copy-start.1
  7.0 2.6 %reshape.42 = bf16[1,256,4096]{2,1,0:T(8,128)(2,1)} reshape(bf16[1,256,32,128]{3,2,1,0:T(8,128)(2,1)S(1)} %bitcast.40) | data formatting | bytes 4194304 | tf_op jit(solution)/shard_map/reshape | solution.py:27
  9.7 0.0 copy-done.1
  9.7 0.5 collective-permute-start
  10.1 0.0 copy-start.2
  10.1 0.0 slice-start
  10.1 0.2 broadcast_in_dim.2
  10.4 1.3 %copy-done.2 = bf16[256,128,32]{1,2,0:T(8,128)(2,1)S(1)} copy-done((bf16[256,128,32]{1,2,0:T(8,128)(2,1)S(1)}, bf16[256,128,32]{1,2,0:T(8,128)(2,1)}, u32[]{:S(2)}) %copy-start.2) | copy-done | bytes 2097176
  11.7 0.0 slice-start.1
  11.7 6.2 %fusion.14 = f32[512,1024]{1,0:T(8,128)S(1)} fusion(f32[512,1024]{1,0:T(8,128)S(1)} %broadcast_in_dim.2, s32[]{:T(128)S(6)} %select_n.18, bf16[1,1024,4096]{2,1,0:T(8,128)(2,1)} %param.6, bf16[32,8,32,128]{3,2,1,0:T(8,128)(2,1)S(1)} %bitcast.41), kind=kOutput, calls=%fused_computation.11 | convolution fusion | flops 2147483648 | bytes 11534340 | tf_op jit(solution)/shard_map/lqp,lep->qe/dot_general | solution.py:31
  18.0 0.0 collective-permute-done
  18.0 0.0 slice-done
  18.0 0.0 slice-done.1
  18.0 4.0 %fusion.19 = f32[512,1024]{1,0:T(8,128)S(1)} fusion(f32[512,1024]{1,0:T(8,128)S(1)} %fusion.14, s32[]{:T(128)S(6)} %select_n.20, bf16[1,1024,4096]{2,1,0:T(8,128)(2,1)S(1)} %bitcast.45, bf16[1,256,4096]{2,1,0:T(8,128)(2,1)} %collective-permute-done), kind=kOutput, calls=%fused_computation.12 | convolution fusion | flops 2147483648 | bytes 11534340 | tf_op jit(solution)/shard_map/lqp,lep->qe/dot_general | solution.py:31
  22.0 0.0 copy-start.5
  22.0 0.0 copy-start.6
  22.0 93.4 %all-reduce.1 = bf16[512,1024]{1,0:T(8,128)(2,1)S(1)} all-reduce(f32[512,1024]{1,0:T(8,128)S(1)} %fusion.19), channel_id=1, replica_groups=mesh['grp'=2,'layer'=8,'ex'=2] {'layer'}, use_global_device_ids=true, to_apply=%region_0.1 | all-reduce | flops 524288 | bytes 3145728 | tf_op jit(solution)/shard_map/psum | solution.py:47
  115.4 0.0 copy-done.5
  115.4 0.0 copy-done.6
  115.4 0.0 copy-start.3
  115.5 1.1 convolution_convert_fusion
  116.5 0.0 copy-done.3
  (1 shorter events, 0.0 us)
Async XLA Ops:
  0.6 3.5 %copy-start = (bf16[1,128,128]{2,1,0:T(8,128)(2,1)S(1)}, bf16[1,128,128]{2,1,0:T(8,128)(2,1)}, u32[]{:S(2)}) copy-start(bf16[1,128,128]{2,1,0:T(8,128)(2,1)} %param.9) | copy-start | bytes 98308
  0.6 3.4 %copy-start.4 = (bf16[1,32,32]{2,1,0:T(8,128)(2,1)S(1)}, bf16[1,32,32]{2,1,0:T(8,128)(2,1)}, u32[]{:S(2)}) copy-start(bf16[1,32,32]{2,1,0:T(8,128)(2,1)} %param.8) | copy-start | bytes 6148
  7.0 2.7 %copy-start.1 = (bf16[256,128,32]{1,2,0:T(8,128)(2,1)}, bf16[256,128,32]{1,2,0:T(8,128)(2,1)S(1)}, u32[]{:S(2)}) copy-start(bf16[256,128,32]{1,2,0:T(8,128)(2,1)S(1)} %fusion.11) | copy-start | bytes 6291460
  9.7 8.3 %collective-permute-start = (bf16[1,256,4096]{2,1,0:T(8,128)(2,1)}, bf16[1,256,4096]{2,1,0:T(8,128)(2,1)}, u32[]{:S(2)}, u32[]{:S(2)}) collective-permute-start(bf16[1,256,4096]{2,1,0:T(8,128)(2,1)} %reshape.42), channel_id=1, source_target_pairs={{1,0},{0,1},{3,2},{2,3},{5,4},{4,5},{7,6},{6,7},{9,8},{8,9},{11,10... | collective-permute-start | bytes 6291464 | tf_op jit(solution)/shard_map/ppermute | solution.py:14
  10.1 1.6 %copy-start.2 = (bf16[256,128,32]{1,2,0:T(8,128)(2,1)S(1)}, bf16[256,128,32]{1,2,0:T(8,128)(2,1)}, u32[]{:S(2)}) copy-start(bf16[256,128,32]{1,2,0:T(8,128)(2,1)} %copy-done.1) | copy-start | bytes 6291460
  10.1 7.9 %slice-start = ((s8[8388608]{0:T(1024)(128)(4,1)}), s8[4194304]{0:T(1024)(128)(4,1)S(1)}, s32[]{:S(2)}) async-start(s8[8388608]{0:T(1024)(128)(4,1)} %bitcast.44), calls=%async_computation | async-start | bytes 8388608
  11.7 6.3 %slice-start.1 = ((s8[8388608]{0:T(1024)(128)(4,1)}), s8[4194304]{0:T(1024)(128)(4,1)S(1)}, s32[]{:S(2)}) async-start(s8[8388608]{0:T(1024)(128)(4,1)} %bitcast.44), calls=%async_computation.1 | async-start | bytes 8388608
  22.0 93.4 %copy-start.5 = (s32[512]{0:T(512)S(1)}, s32[512]{0:T(512)}, u32[]{:S(2)}) copy-start(s32[512]{0:T(512)} %param.10) | copy-start | bytes 6148
  22.0 93.4 %copy-start.6 = (s32[128]{0:T(128)S(1)}, s32[128]{0:T(128)}, u32[]{:S(2)}) copy-start(s32[128]{0:T(128)} %param.11) | copy-start | bytes 1540
  115.4 1.1 copy-start.3
where the time goes:
time: 117 us
  blocking collectives  93.4 us (80%)
  matrix products  14.2 us (12%)
  local copies, waits for them, and re-layouts  7.69 us (7%)
    psum x1, blocking collectives, shards(): scores = lax.psum(partial_value, 'layer').astype(jnp.bfloat16)  93.4 us
    dot_general x2, matrix products, score_block(): jnp.einsum('lqp,lep->qe', ready, store, preferred_element_type=jnp.float32)  10.2 us
    unnamed x19, local copies, waits for them, and re-layouts  4.81 us
    dot_general x1, matrix products, precondition(): jnp.einsum('lij,lqjm->lqim', left_inv, half, preferred_element_type=jnp.f...  2.94 us
    reshape x1, local copies, waits for them, and re-layouts, precondition(): return pre.reshape(layers, count, KIN * KOUT)  2.64 us
  transfers between devices with their start and end apart: 1, of which 0 were waited for; matrix products, arithmetic and copies ran while one was open for 6% of the time, Pallas kernels for 0%

commit v1 on v0

--- a/solution.py
+++ b/solution.py
@@ -6,12 +6,7 @@
 KIN = 32
 KOUT = 128
 BEST = 4
-
-
-def passed_along(block, axis, distance):
-    devices = range(lax.axis_size(axis))
-    route = [((i - distance) % len(devices), i) for i in devices]
-    return lax.ppermute(block, axis, route)
+LANES = 128
 
 
 def precondition(block, left_inv, right_inv):
@@ -31,20 +26,112 @@
     return jnp.einsum("lqp,lep->qe", ready, store, preferred_element_type=jnp.float32)
 
 
+class Grid:
+    def __init__(self):
+        self.count = lax.axis_size("layer")
+        self.y_count = 2 if self.count % 2 == 0 else 1
+        self.z_count = self.count // self.y_count
+        index = lax.axis_index("layer")
+        self.y = index % self.y_count
+        self.z = index // self.y_count
+
+    def along_y(self, block):
+        route = [(i, i ^ 1) for i in range(self.count)]
+        return lax.ppermute(block, "layer", route)
+
+    def along_z(self, block, distance):
+        step = distance * self.y_count
+        route = [(i, (i + step) % self.count) for i in range(self.count)]
+        return lax.ppermute(block, "layer", route)
+
+
+def z_slots(grid, shape):
+    columns = min(grid.z_count, shape[1] // LANES)
+    return grid.z_count // columns, columns
+
+
+def z_slot(grid, block, slot):
+    row_blocks, column_blocks = z_slots(grid, block.shape)
+    rows, columns = block.shape[0] // row_blocks, block.shape[1] // column_blocks
+    return lax.dynamic_slice(
+        block, ((slot // column_blocks) * rows, (slot % column_blocks) * columns), (rows, columns)
+    )
+
+
+def scatter_z(grid, block):
+    narrow = block.astype(jnp.bfloat16)
+    total = z_slot(grid, block, grid.z)
+    for d in range(1, grid.z_count):
+        sent = z_slot(grid, narrow, (grid.z + d) % grid.z_count)
+        total = total + grid.along_z(sent, d).astype(jnp.float32)
+    return total
+
+
+def gather_z(grid, mine, shape):
+    row_blocks, column_blocks = z_slots(grid, shape)
+    rows, columns = mine.shape
+    out = jnp.zeros(shape, mine.dtype)
+    for d in range(grid.z_count):
+        piece = grid.along_z(mine, d) if d else mine
+        slot = (grid.z - d) % grid.z_count
+        out = lax.dynamic_update_slice(
+            out, piece, ((slot // column_blocks) * rows, (slot % column_blocks) * columns)
+        )
+    return out
+
+
+def scatter_y(grid, block):
+    if grid.y_count == 1:
+        return block
+    rows = block.shape[0] // 2
+    mine = lax.dynamic_slice_in_dim(block, grid.y * rows, rows, 0)
+    sent = lax.dynamic_slice_in_dim(block, (1 - grid.y) * rows, rows, 0).astype(jnp.bfloat16)
+    return mine + grid.along_y(sent).astype(jnp.float32)
+
+
+def gather_y(grid, mine):
+    if grid.y_count == 1:
+        return mine
+    other = grid.along_y(mine)
+    first = jnp.where(grid.y == 0, mine, other)
+    second = jnp.where(grid.y == 0, other, mine)
+    return jnp.concatenate([first, second], 0)
+
+
+def sum_y_first(grid, block):
+    half = scatter_y(grid, block)
+    piece = scatter_z(grid, half).astype(jnp.bfloat16)
+    return gather_y(grid, gather_z(grid, piece, half.shape))
+
+
+def sum_z_first(grid, block):
+    slot = scatter_z(grid, block)
+    piece = scatter_y(grid, slot).astype(jnp.bfloat16)
+    return gather_z(grid, gather_y(grid, piece), block.shape)
+
+
 def shards(store, queries, left_inv, right_inv, query_prompt, winner):
     block_rows = queries.shape[1]
-    mine = precondition(queries, left_inv, right_inv)
+    columns = store.shape[1]
+    grid = Grid()
     ex_count = lax.axis_size("ex")
     position = lax.axis_index("ex")
-    partial_value = jnp.zeros((block_rows * ex_count, store.shape[1]), jnp.float32)
+    mine = precondition(queries, left_inv, right_inv)
+    scores = jnp.zeros((block_rows * ex_count, columns), jnp.bfloat16)
     current = mine
     for step in range(ex_count):
         if step > 0:
-            current = passed_along(current, "ex", 1)
+            route = [((i - 1) % ex_count, i) for i in range(ex_count)]
+            current = lax.ppermute(current, "ex", route)
         source = (position - step) % ex_count
         tile = score_block(current, store)
-        partial_value = lax.dynamic_update_slice_in_dim(partial_value, tile, source * block_rows, 0)
-    scores = lax.psum(partial_value, "layer").astype(jnp.bfloat16)
+        if step == 0:
+            first = sum_z_first(grid, tile[:, : columns // 2])
+            second = sum_y_first(grid, tile[:, columns // 2 :])
+            done = jnp.concatenate([first, second], 1)
+        else:
+            done = sum_y_first(grid, tile)
+        scores = lax.dynamic_update_slice_in_dim(scores, done, source * block_rows, 0)
     ids = jnp.arange(scores.shape[0], dtype=jnp.int32)
     prompts = jnp.arange(winner.shape[0], dtype=jnp.int32)
     picks = (winner[:, None] == ids[None, :]).astype(jnp.float32)

time: 117 us -> 86.8 us (0.74)
  blocking collectives: 93.4 us -> 0 us
  starting transfers between devices: 0.45 us -> 32.2 us
  waiting for transfers between devices: 0.01 us -> 30.2 us
  matrix products: 14.2 us -> 16.4 us
  local copies, waits for them, and re-layouts: 7.69 us -> 6.4 us
    psum x1 -> x0, blocking collectives: 93.4 us -> none  [shards(): scores = lax.psum(partial_value, 'layer').astype(jnp.bfloat16)]
    ppermute x1 -> x25, starting transfers between devices: 0.45 us -> 32.2 us  [the longest x18 24.9 us: along_z(): return lax.ppermute(block, 'layer', route)]
    ppermute x1 -> x25, waiting for transfers between devices: 0.01 us -> 30.2 us  [the longest x18 16.5 us: along_z(): return lax.ppermute(block, 'layer', route)]
    dot_general x2, matrix products: 10.2 us -> 12.4 us  [score_block(): jnp.einsum('lqp,lep->qe', ready, store, preferred_element_type=jnp.float32)]
    unnamed x19 -> x11, local copies, waits for them, and re-layouts: 4.81 us -> 3.47 us
  transfers between devices with their start and end apart: 1 -> 25, of which waited for: 0 -> 12; matrix products, arithmetic and copies ran while one was open for 6% -> 15% of each run, Pallas kernels for 0% -> 0%
where the time goes in v1:
time: 86.8 us; the launch traced here: 86.6 us
  starting transfers between devices  32.2 us (37%)
  waiting for transfers between devices  30.2 us (35%)
  matrix products  16.4 us (19%)
  local copies, waits for them, and re-layouts  6.4 us (7%)
  between operations  1.02 us (1%)
    ppermute x18, starting transfers between devices, along_z(): return lax.ppermute(block, 'layer', route)  24.9 us
    ppermute x18, waiting for transfers between devices, along_z(): return lax.ppermute(block, 'layer', route)  16.5 us
    ppermute x6, waiting for transfers between devices, along_y(): return lax.ppermute(block, 'layer', route)  13.6 us
    dot_general x2, matrix products, score_block(): jnp.einsum('lqp,lep->qe', ready, store, preferred_element_type=jnp.float32)  12.4 us
    ppermute x6, starting transfers between devices, along_y(): return lax.ppermute(block, 'layer', route)  6.83 us
    unnamed x11, local copies, waits for them, and re-layouts  3.47 us
    dot_general x1, matrix products, precondition(): jnp.einsum('lij,lqjm->lqim', left_inv, half, preferred_element_type=jnp.f...  2.94 us
    reshape x1, local copies, waits for them, and re-layouts, precondition(): return pre.reshape(layers, count, KIN * KOUT)  2.33 us
  transfers between devices with their start and end apart: 25, of which 12 were waited for; matrix products, arithmetic and copies ran while one was open for 15% of the time, Pallas kernels for 0%

profile of v1, /device:TPU:0, one launch (start us, length us, event | category | flops | bytes accessed | tf_op | source)
XLA Modules:
  0.0 86.6 jit_solution(7628697051896838769)
XLA Ops:
  0.6 0.0 copy-start
  0.7 3.4 %copy.8 = bf16[32,8,32,128]{3,2,1,0:T(8,128)(2,1)} copy(bf16[32,8,32,128]{3,1,2,0:T(8,128)(2,1)} %bitcast.35) | data formatting | bytes 4194304
  4.1 2.9 %fusion.11 = bf16[256,128,32]{1,2,0:T(8,128)(2,1)S(1)} fusion(bf16[256,32,128]{2,1,0:T(8,128)(2,1)} %bitcast.34, bf16[1,128,128]{2,1,0:T(8,128)(2,1)S(1)} %copy-done, bf16[1,32,32]{2,1,0:T(8,128)(2,1)S(1)} %copy-done.2), kind=kOutput, calls=%fused_computation.10 | convolution fusion | flops 337641472 | bytes 4229120 | tf_op jit(solution)/shard_map/lij,lqjm->lqim/dot_general | solution.py:19
  7.0 2.3 %reshape.42 = bf16[1,256,4096]{2,1,0:T(8,128)(2,1)} reshape(bf16[1,256,32,128]{3,2,1,0:T(8,128)(2,1)S(1)} %bitcast.32) | data formatting | bytes 4194304 | tf_op jit(solution)/shard_map/reshape | solution.py:22
  9.4 0.5 collective-permute-start.16
  9.8 6.0 %fusion.2 = f32[256,1024]{1,0:T(8,128)S(1)} fusion(bf16[1,1024,4096]{2,1,0:T(8,128)(2,1)} %param.6, bf16[32,8,32,128]{3,2,1,0:T(8,128)(2,1)S(1)} %bitcast.33), kind=kOutput, calls=%fused_computation.2 | convolution fusion | flops 2147483648 | bytes 11534336 | tf_op jit(solution)/shard_map/lqp,lep->qe/dot_general | solution.py:26
  15.9 4.7 %collective-permute-start.2 = (bf16[256,128]{1,0:T(8,128)(2,1)S(1)}, bf16[256,128]{1,0:T(8,128)(2,1)S(1)}, u32[]{:S(2)}, u32[]{:S(2)}) collective-permute-start(bf16[256,128]{1,0:T(8,128)(2,1)S(1)} %get-tuple-element.18), channel_id=1, source_target_pairs={{0,12},{2,14},{4,0},{6,2},{8,4},{10,6},{12,8},{14,10},{1,13},{3,15... | collective-permute-start | bytes 196616 | tf_op jit(solution)/shard_map/ppermute | solution.py:45
  20.6 0.0 collective-permute-start.1
  20.6 1.0 %collective-permute-start = (bf16[256,128]{1,0:T(8,128)(2,1)S(1)}, bf16[256,128]{1,0:T(8,128)(2,1)S(1)}, u32[]{:S(2)}, u32[]{:S(2)}) collective-permute-start(bf16[256,128]{1,0:T(8,128)(2,1)S(1)} %get-tuple-element.17), channel_id=1, source_target_pairs={{0,4},{2,6},{4,8},{6,10},{8,12},{10,14},{12,0},{14,2},{1,5},{3,7},... | collective-permute-start | bytes 196616 | tf_op jit(solution)/shard_map/ppermute | solution.py:45
  21.6 0.1 fusion.25
  21.7 1.3 %collective-permute-done.2 = bf16[256,128]{1,0:T(8,128)(2,1)S(1)} collective-permute-done((bf16[256,128]{1,0:T(8,128)(2,1)S(1)}, bf16[256,128]{1,0:T(8,128)(2,1)S(1)}, u32[]{:S(2)}, u32[]{:S(2)}) %collective-permute-start.2) | collective-permute-done | bytes 65568 | tf_op jit(solution)/shard_map/ppermute | solution.py:45
  23.0 4.7 %collective-permute-done.1 = bf16[256,128]{1,0:T(8,128)(2,1)S(1)} collective-permute-done((bf16[256,128]{1,0:T(8,128)(2,1)S(1)}, bf16[256,128]{1,0:T(8,128)(2,1)S(1)}, u32[]{:S(2)}, u32[]{:S(2)}) %collective-permute-start.1) | collective-permute-done | bytes 65568 | tf_op jit(solution)/shard_map/ppermute | solution.py:45
  27.7 0.0 collective-permute-done
  27.8 1.6 %collective-permute-start.3 = (bf16[128,128]{1,0:T(8,128)(2,1)S(1)}, bf16[128,128]{1,0:T(8,128)(2,1)S(1)}, u32[]{:S(2)}, u32[]{:S(2)}) collective-permute-start(bf16[128,128]{1,0:T(8,128)(2,1)S(1)} %dynamic-slice_convert_fusion.2), channel_id=1, source_target_pairs={{0,2},{2,0},{4,6},{6,4},{8,10},{10,8},{12,14},{14,12},{1,3},{3,1},... | collective-permute-start | bytes 98312 | tf_op jit(solution)/shard_map/ppermute | solution.py:40
  29.4 0.6 collective-permute-start.8
  30.0 1.8 %collective-permute-done.3 = bf16[128,128]{1,0:T(8,128)(2,1)S(1)} collective-permute-done((bf16[128,128]{1,0:T(8,128)(2,1)S(1)}, bf16[128,128]{1,0:T(8,128)(2,1)S(1)}, u32[]{:S(2)}, u32[]{:S(2)}) %collective-permute-start.3) | collective-permute-done | bytes 32800 | tf_op jit(solution)/shard_map/ppermute | solution.py:40
  31.8 1.9 %collective-permute-start.4 = (bf16[128,128]{1,0:T(8,128)(2,1)S(1)}, bf16[128,128]{1,0:T(8,128)(2,1)S(1)}, u32[]{:S(2)}, u32[]{:S(2)}) collective-permute-start(bf16[128,128]{1,0:T(8,128)(2,1)S(1)} %add_convert_fusion.2), channel_id=1, source_target_pairs={{0,2},{2,0},{4,6},{6,4},{8,10},{10,8},{12,14},{14,12},{1,3},{3,1},... | collective-permute-start | bytes 98312 | tf_op jit(solution)/shard_map/ppermute | solution.py:40
  33.7 1.2 %collective-permute-done.8 = bf16[128,512]{1,0:T(8,128)(2,1)S(1)} collective-permute-done((bf16[128,512]{1,0:T(8,128)(2,1)S(1)}, bf16[128,512]{1,0:T(8,128)(2,1)S(1)}, u32[]{:S(2)}, u32[]{:S(2)}) %collective-permute-start.8) | collective-permute-done | bytes 131104 | tf_op jit(solution)/shard_map/ppermute | solution.py:40
  35.0 1.4 %collective-permute-start.11 = (bf16[128,128]{1,0:T(8,128)(2,1)S(1)}, bf16[128,128]{1,0:T(8,128)(2,1)S(1)}, u32[]{:S(2)}, u32[]{:S(2)}) collective-permute-start(bf16[128,128]{1,0:T(8,128)(2,1)S(1)} %get-tuple-element.23), channel_id=1, source_target_pairs={{0,12},{2,14},{4,0},{6,2},{8,4},{10,6},{12,8},{14,10},{1,13},{3,15... | collective-permute-start | bytes 98312 | tf_op jit(solution)/shard_map/ppermute | solution.py:45
  36.4 0.3 collective-permute-start.10
  36.8 1.9 %collective-permute-start.9 = (bf16[128,128]{1,0:T(8,128)(2,1)S(1)}, bf16[128,128]{1,0:T(8,128)(2,1)S(1)}, u32[]{:S(2)}, u32[]{:S(2)}) collective-permute-start(bf16[128,128]{1,0:T(8,128)(2,1)S(1)} %get-tuple-element.22), channel_id=1, source_target_pairs={{0,4},{2,6},{4,8},{6,10},{8,12},{10,14},{12,0},{14,2},{1,5},{3,7},... | collective-permute-start | bytes 98312 | tf_op jit(solution)/shard_map/ppermute | solution.py:45
  38.7 0.0 collective-permute-done.4
  38.8 1.3 %collective-permute-start.5 = (bf16[256,128]{1,0:T(8,128)(2,1)S(1)}, bf16[256,128]{1,0:T(8,128)(2,1)S(1)}, u32[]{:S(2)}, u32[]{:S(2)}) collective-permute-start(bf16[256,128]{1,0:T(8,128)(2,1)S(1)} %get-tuple-element.25), channel_id=1, source_target_pairs={{0,4},{2,6},{4,8},{6,10},{8,12},{10,14},{12,0},{14,2},{1,5},{3,7},... | collective-permute-start | bytes 196616 | tf_op jit(solution)/shard_map/ppermute | solution.py:45
  40.1 0.0 collective-permute-done.11
  40.1 1.2 %collective-permute-start.6 = (bf16[256,128]{1,0:T(8,128)(2,1)S(1)}, bf16[256,128]{1,0:T(8,128)(2,1)S(1)}, u32[]{:S(2)}, u32[]{:S(2)}) collective-permute-start(bf16[256,128]{1,0:T(8,128)(2,1)S(1)} %get-tuple-element.25), channel_id=1, source_target_pairs={{0,8},{2,10},{4,12},{6,14},{8,0},{10,2},{12,4},{14,6},{1,9},{3,11}... | collective-permute-start | bytes 196616 | tf_op jit(solution)/shard_map/ppermute | solution.py:45
  41.3 2.1 %collective-permute-done.10 = bf16[128,128]{1,0:T(8,128)(2,1)S(1)} collective-permute-done((bf16[128,128]{1,0:T(8,128)(2,1)S(1)}, bf16[128,128]{1,0:T(8,128)(2,1)S(1)}, u32[]{:S(2)}, u32[]{:S(2)}) %collective-permute-start.10) | collective-permute-done | bytes 32800 | tf_op jit(solution)/shard_map/ppermute | solution.py:45
  43.4 0.9 collective-permute-start.7
  44.2 0.0 collective-permute-done.9
  44.3 1.2 %collective-permute-start.12 = (bf16[128,128]{1,0:T(8,128)(2,1)S(1)}, bf16[128,128]{1,0:T(8,128)(2,1)S(1)}, u32[]{:S(2)}, u32[]{:S(2)}) collective-permute-start(bf16[128,128]{1,0:T(8,128)(2,1)S(1)} %get-tuple-element.7), channel_id=1, source_target_pairs={{0,4},{2,6},{4,8},{6,10},{8,12},{10,14},{12,0},{14,2},{1,5},{3,7},... | collective-permute-start | bytes 98312 | tf_op jit(solution)/shard_map/ppermute | solution.py:45
  45.5 0.0 collective-permute-done.5
  45.6 1.5 %collective-permute-start.13 = (bf16[128,128]{1,0:T(8,128)(2,1)S(1)}, bf16[128,128]{1,0:T(8,128)(2,1)S(1)}, u32[]{:S(2)}, u32[]{:S(2)}) collective-permute-start(bf16[128,128]{1,0:T(8,128)(2,1)S(1)} %get-tuple-element.7), channel_id=1, source_target_pairs={{0,8},{2,10},{4,12},{6,14},{8,0},{10,2},{12,4},{14,6},{1,9},{3,11}... | collective-permute-start | bytes 98312 | tf_op jit(solution)/shard_map/ppermute | solution.py:45
  47.1 0.0 collective-permute-done.16
  47.1 1.1 %collective-permute-start.14 = (bf16[128,128]{1,0:T(8,128)(2,1)S(1)}, bf16[128,128]{1,0:T(8,128)(2,1)S(1)}, u32[]{:S(2)}, u32[]{:S(2)}) collective-permute-start(bf16[128,128]{1,0:T(8,128)(2,1)S(1)} %get-tuple-element.7), channel_id=1, source_target_pairs={{0,12},{2,14},{4,0},{6,2},{8,4},{10,6},{12,8},{14,10},{1,13},{3,15... | collective-permute-start | bytes 98312 | tf_op jit(solution)/shard_map/ppermute | solution.py:45
  48.3 6.4 %fusion = f32[256,1024]{1,0:T(8,128)S(1)} fusion(bf16[1,1024,4096]{2,1,0:T(8,128)(2,1)} %param.6, bf16[1,256,4096]{2,1,0:T(8,128)(2,1)} %collective-permute-done.16), kind=kOutput, calls=%fused_computation | convolution fusion | flops 2147483648 | bytes 11534336 | tf_op jit(solution)/shard_map/lqp,lep->qe/dot_general | solution.py:26
  54.7 0.0 collective-permute-done.6
  54.7 0.8 collective-permute-start.17
  55.5 0.0 collective-permute-done.7
  55.5 0.0 collective-permute-done.12
  55.6 5.6 %collective-permute-done.17 = bf16[128,1024]{1,0:T(8,128)(2,1)S(1)} collective-permute-done((bf16[128,1024]{1,0:T(8,128)(2,1)S(1)}, bf16[128,1024]{1,0:T(8,128)(2,1)S(1)}, u32[]{:S(2)}, u32[]{:S(2)}) %collective-permute-start.17) | collective-permute-done | bytes 262176 | tf_op jit(solution)/shard_map/ppermute | solution.py:40
  61.1 0.1 fusion.23
  61.3 1.8 %collective-permute-start.20 = (bf16[128,256]{1,0:T(8,128)(2,1)S(1)}, bf16[128,256]{1,0:T(8,128)(2,1)S(1)}, u32[]{:S(2)}, u32[]{:S(2)}) collective-permute-start(bf16[128,256]{1,0:T(8,128)(2,1)S(1)} %get-tuple-element.15), channel_id=1, source_target_pairs={{0,12},{2,14},{4,0},{6,2},{8,4},{10,6},{12,8},{14,10},{1,13},{3,15... | collective-permute-start | bytes 196616 | tf_op jit(solution)/shard_map/ppermute | solution.py:45
  63.1 0.6 collective-permute-start.19
  63.7 1.6 %collective-permute-start.18 = (bf16[128,256]{1,0:T(8,128)(2,1)S(1)}, bf16[128,256]{1,0:T(8,128)(2,1)S(1)}, u32[]{:S(2)}, u32[]{:S(2)}) collective-permute-start(bf16[128,256]{1,0:T(8,128)(2,1)S(1)} %get-tuple-element.14), channel_id=1, source_target_pairs={{0,4},{2,6},{4,8},{6,10},{8,12},{10,14},{12,0},{14,2},{1,5},{3,7},... | collective-permute-start | bytes 196616 | tf_op jit(solution)/shard_map/ppermute | solution.py:45
  65.4 0.0 collective-permute-done.13
  65.4 0.2 collective-permute-done.20
  65.6 5.6 %collective-permute-done.19 = bf16[128,256]{1,0:T(8,128)(2,1)S(1)} collective-permute-done((bf16[128,256]{1,0:T(8,128)(2,1)S(1)}, bf16[128,256]{1,0:T(8,128)(2,1)S(1)}, u32[]{:S(2)}, u32[]{:S(2)}) %collective-permute-start.19) | collective-permute-done | bytes 65568 | tf_op jit(solution)/shard_map/ppermute | solution.py:45
  71.2 0.0 collective-permute-done.18
  71.3 0.1 collective-permute-start.21
  71.3 0.0 collective-permute-done.14
  71.4 0.8 collective-permute-start.15
  72.2 1.9 %collective-permute-start.22 = (bf16[128,256]{1,0:T(8,128)(2,1)S(1)}, bf16[128,256]{1,0:T(8,128)(2,1)S(1)}, u32[]{:S(2)}, u32[]{:S(2)}) collective-permute-start(bf16[128,256]{1,0:T(8,128)(2,1)S(1)} %get-tuple-element.3), channel_id=1, source_target_pairs={{0,8},{2,10},{4,12},{6,14},{8,0},{10,2},{12,4},{14,6},{1,9},{3,11}... | collective-permute-start | bytes 196616 | tf_op jit(solution)/shard_map/ppermute | solution.py:45
  74.1 2.2 %collective-permute-start.23 = (bf16[128,256]{1,0:T(8,128)(2,1)S(1)}, bf16[128,256]{1,0:T(8,128)(2,1)S(1)}, u32[]{:S(2)}, u32[]{:S(2)}) collective-permute-start(bf16[128,256]{1,0:T(8,128)(2,1)S(1)} %get-tuple-element.3), channel_id=1, source_target_pairs={{0,12},{2,14},{4,0},{6,2},{8,4},{10,6},{12,8},{14,10},{1,13},{3,15... | collective-permute-start | bytes 196616 | tf_op jit(solution)/shard_map/ppermute | solution.py:45
  76.3 1.2 %collective-permute-done.21 = bf16[128,256]{1,0:T(8,128)(2,1)S(1)} collective-permute-done((bf16[128,256]{1,0:T(8,128)(2,1)S(1)}, bf16[128,256]{1,0:T(8,128)(2,1)S(1)}, u32[]{:S(2)}, u32[]{:S(2)}) %collective-permute-start.21) | collective-permute-done | bytes 65568 | tf_op jit(solution)/shard_map/ppermute | solution.py:45
  77.5 1.4 %collective-permute-done.22 = bf16[128,256]{1,0:T(8,128)(2,1)S(1)} collective-permute-done((bf16[128,256]{1,0:T(8,128)(2,1)S(1)}, bf16[128,256]{1,0:T(8,128)(2,1)S(1)}, u32[]{:S(2)}, u32[]{:S(2)}) %collective-permute-start.22) | collective-permute-done | bytes 65568 | tf_op jit(solution)/shard_map/ppermute | solution.py:45
  78.9 0.1 collective-permute-done.23
  79.0 1.2 %collective-permute-start.24 = (bf16[128,1024]{1,0:T(8,128)(2,1)S(1)}, bf16[128,1024]{1,0:T(8,128)(2,1)S(1)}, u32[]{:S(2)}, u32[]{:S(2)}) collective-permute-start(bf16[128,1024]{1,0:T(8,128)(2,1)S(1)} %constant_dynamic-update-slice_fusion), channel_id=1, source_target_pairs={{0,2},{2,0},{4,6},{6,4},{8,10},{10,8},{12,14},{14,12},{1,3},{3,1},... | collective-permute-start | bytes 786440 | tf_op jit(solution)/shard_map/ppermute | solution.py:40
  80.1 0.0 collective-permute-done.15
  80.2 0.0 copy-start.3
  80.2 0.0 copy-start.4
  80.2 0.1 broadcast_in_dim.16
  80.3 0.1 maximum_dynamic-update-slice_fusion
  80.4 5.0 %collective-permute-done.24 = bf16[128,1024]{1,0:T(8,128)(2,1)S(1)} collective-permute-done((bf16[128,1024]{1,0:T(8,128)(2,1)S(1)}, bf16[128,1024]{1,0:T(8,128)(2,1)S(1)}, u32[]{:S(2)}, u32[]{:S(2)}) %collective-permute-start.24) | collective-permute-done | bytes 262176 | tf_op jit(solution)/shard_map/ppermute | solution.py:40
  85.5 0.0 copy-start.1
  85.5 1.1 %convolution_convert_fusion = bf16[128,1024]{1,0:T(8,128)(2,1)} fusion(bf16[512,1024]{1,0:T(8,128)(2,1)S(1)} %maximum_dynamic-update-slice_fusion.1, s32[512]{0:T(512)S(1)} %copy-done.3, s32[128]{0:T(128)S(1)} %copy-done.4), kind=kOutput, calls=%fused_computation.11 | convolution fusion | flops 134742016 | bytes 1313280 | tf_op jit(solution)/shard_map/dot_general | solution.py:140
  (35 shorter events, 0.7 us)
Async XLA Ops:
  0.6 3.5 %copy-start = (bf16[1,128,128]{2,1,0:T(8,128)(2,1)S(1)}, bf16[1,128,128]{2,1,0:T(8,128)(2,1)}, u32[]{:S(2)}) copy-start(bf16[1,128,128]{2,1,0:T(8,128)(2,1)} %param.9) | copy-start | bytes 98308
  0.6 3.5 %copy-start.2 = (bf16[1,32,32]{2,1,0:T(8,128)(2,1)S(1)}, bf16[1,32,32]{2,1,0:T(8,128)(2,1)}, u32[]{:S(2)}) copy-start(bf16[1,32,32]{2,1,0:T(8,128)(2,1)} %param.8) | copy-start | bytes 6148
  9.4 37.7 %collective-permute-start.16 = (bf16[1,256,4096]{2,1,0:T(8,128)(2,1)}, bf16[1,256,4096]{2,1,0:T(8,128)(2,1)}, u32[]{:S(2)}, u32[]{:S(2)}) collective-permute-start(bf16[1,256,4096]{2,1,0:T(8,128)(2,1)} %reshape.42), channel_id=1, source_target_pairs={{1,0},{0,1},{3,2},{2,3},{5,4},{4,5},{7,6},{6,7},{9,8},{8,9},{11,10... | collective-permute-start | bytes 6291464 | tf_op jit(solution)/shard_map/ppermute | solution.py:125
  15.9 7.1 %collective-permute-start.2 = (bf16[256,128]{1,0:T(8,128)(2,1)S(1)}, bf16[256,128]{1,0:T(8,128)(2,1)S(1)}, u32[]{:S(2)}, u32[]{:S(2)}) collective-permute-start(bf16[256,128]{1,0:T(8,128)(2,1)S(1)} %get-tuple-element.18), channel_id=1, source_target_pairs={{0,12},{2,14},{4,0},{6,2},{8,4},{10,6},{12,8},{14,10},{1,13},{3,15... | collective-permute-start | bytes 196616 | tf_op jit(solution)/shard_map/ppermute | solution.py:45
  20.6 7.1 %collective-permute-start.1 = (bf16[256,128]{1,0:T(8,128)(2,1)S(1)}, bf16[256,128]{1,0:T(8,128)(2,1)S(1)}, u32[]{:S(2)}, u32[]{:S(2)}) collective-permute-start(bf16[256,128]{1,0:T(8,128)(2,1)S(1)} %get-tuple-element.19), channel_id=1, source_target_pairs={{0,8},{2,10},{4,12},{6,14},{8,0},{10,2},{12,4},{14,6},{1,9},{3,11}... | collective-permute-start | bytes 196616 | tf_op jit(solution)/shard_map/ppermute | solution.py:45
  20.6 7.1 %collective-permute-start = (bf16[256,128]{1,0:T(8,128)(2,1)S(1)}, bf16[256,128]{1,0:T(8,128)(2,1)S(1)}, u32[]{:S(2)}, u32[]{:S(2)}) collective-permute-start(bf16[256,128]{1,0:T(8,128)(2,1)S(1)} %get-tuple-element.17), channel_id=1, source_target_pairs={{0,4},{2,6},{4,8},{6,10},{8,12},{10,14},{12,0},{14,2},{1,5},{3,7},... | collective-permute-start | bytes 196616 | tf_op jit(solution)/shard_map/ppermute | solution.py:45
  27.8 4.0 %collective-permute-start.3 = (bf16[128,128]{1,0:T(8,128)(2,1)S(1)}, bf16[128,128]{1,0:T(8,128)(2,1)S(1)}, u32[]{:S(2)}, u32[]{:S(2)}) collective-permute-start(bf16[128,128]{1,0:T(8,128)(2,1)S(1)} %dynamic-slice_convert_fusion.2), channel_id=1, source_target_pairs={{0,2},{2,0},{4,6},{6,4},{8,10},{10,8},{12,14},{14,12},{1,3},{3,1},... | collective-permute-start | bytes 98312 | tf_op jit(solution)/shard_map/ppermute | solution.py:40
  29.4 5.5 %collective-permute-start.8 = (bf16[128,512]{1,0:T(8,128)(2,1)S(1)}, bf16[128,512]{1,0:T(8,128)(2,1)S(1)}, u32[]{:S(2)}, u32[]{:S(2)}) collective-permute-start(bf16[128,512]{1,0:T(8,128)(2,1)S(1)} %dynamic-slice_convert_fusion.1), channel_id=1, source_target_pairs={{0,2},{2,0},{4,6},{6,4},{8,10},{10,8},{12,14},{14,12},{1,3},{3,1},... | collective-permute-start | bytes 393224 | tf_op jit(solution)/shard_map/ppermute | solution.py:40
  31.8 6.9 %collective-permute-start.4 = (bf16[128,128]{1,0:T(8,128)(2,1)S(1)}, bf16[128,128]{1,0:T(8,128)(2,1)S(1)}, u32[]{:S(2)}, u32[]{:S(2)}) collective-permute-start(bf16[128,128]{1,0:T(8,128)(2,1)S(1)} %add_convert_fusion.2), channel_id=1, source_target_pairs={{0,2},{2,0},{4,6},{6,4},{8,10},{10,8},{12,14},{14,12},{1,3},{3,1},... | collective-permute-start | bytes 98312 | tf_op jit(solution)/shard_map/ppermute | solution.py:40
  35.0 5.0 %collective-permute-start.11 = (bf16[128,128]{1,0:T(8,128)(2,1)S(1)}, bf16[128,128]{1,0:T(8,128)(2,1)S(1)}, u32[]{:S(2)}, u32[]{:S(2)}) collective-permute-start(bf16[128,128]{1,0:T(8,128)(2,1)S(1)} %get-tuple-element.23), channel_id=1, source_target_pairs={{0,12},{2,14},{4,0},{6,2},{8,4},{10,6},{12,8},{14,10},{1,13},{3,15... | collective-permute-start | bytes 98312 | tf_op jit(solution)/shard_map/ppermute | solution.py:45
  36.4 6.9 %collective-permute-start.10 = (bf16[128,128]{1,0:T(8,128)(2,1)S(1)}, bf16[128,128]{1,0:T(8,128)(2,1)S(1)}, u32[]{:S(2)}, u32[]{:S(2)}) collective-permute-start(bf16[128,128]{1,0:T(8,128)(2,1)S(1)} %get-tuple-element.24), channel_id=1, source_target_pairs={{0,8},{2,10},{4,12},{6,14},{8,0},{10,2},{12,4},{14,6},{1,9},{3,11}... | collective-permute-start | bytes 98312 | tf_op jit(solution)/shard_map/ppermute | solution.py:45
  36.8 7.5 %collective-permute-start.9 = (bf16[128,128]{1,0:T(8,128)(2,1)S(1)}, bf16[128,128]{1,0:T(8,128)(2,1)S(1)}, u32[]{:S(2)}, u32[]{:S(2)}) collective-permute-start(bf16[128,128]{1,0:T(8,128)(2,1)S(1)} %get-tuple-element.22), channel_id=1, source_target_pairs={{0,4},{2,6},{4,8},{6,10},{8,12},{10,14},{12,0},{14,2},{1,5},{3,7},... | collective-permute-start | bytes 98312 | tf_op jit(solution)/shard_map/ppermute | solution.py:45
  38.8 6.8 %collective-permute-start.5 = (bf16[256,128]{1,0:T(8,128)(2,1)S(1)}, bf16[256,128]{1,0:T(8,128)(2,1)S(1)}, u32[]{:S(2)}, u32[]{:S(2)}) collective-permute-start(bf16[256,128]{1,0:T(8,128)(2,1)S(1)} %get-tuple-element.25), channel_id=1, source_target_pairs={{0,4},{2,6},{4,8},{6,10},{8,12},{10,14},{12,0},{14,2},{1,5},{3,7},... | collective-permute-start | bytes 196616 | tf_op jit(solution)/shard_map/ppermute | solution.py:45
  40.1 14.6 %collective-permute-start.6 = (bf16[256,128]{1,0:T(8,128)(2,1)S(1)}, bf16[256,128]{1,0:T(8,128)(2,1)S(1)}, u32[]{:S(2)}, u32[]{:S(2)}) collective-permute-start(bf16[256,128]{1,0:T(8,128)(2,1)S(1)} %get-tuple-element.25), channel_id=1, source_target_pairs={{0,8},{2,10},{4,12},{6,14},{8,0},{10,2},{12,4},{14,6},{1,9},{3,11}... | collective-permute-start | bytes 196616 | tf_op jit(solution)/shard_map/ppermute | solution.py:45
  43.4 12.1 %collective-permute-start.7 = (bf16[256,128]{1,0:T(8,128)(2,1)S(1)}, bf16[256,128]{1,0:T(8,128)(2,1)S(1)}, u32[]{:S(2)}, u32[]{:S(2)}) collective-permute-start(bf16[256,128]{1,0:T(8,128)(2,1)S(1)} %get-tuple-element.25), channel_id=1, source_target_pairs={{0,12},{2,14},{4,0},{6,2},{8,4},{10,6},{12,8},{14,10},{1,13},{3,15... | collective-permute-start | bytes 196616 | tf_op jit(solution)/shard_map/ppermute | solution.py:45
  44.3 11.2 %collective-permute-start.12 = (bf16[128,128]{1,0:T(8,128)(2,1)S(1)}, bf16[128,128]{1,0:T(8,128)(2,1)S(1)}, u32[]{:S(2)}, u32[]{:S(2)}) collective-permute-start(bf16[128,128]{1,0:T(8,128)(2,1)S(1)} %get-tuple-element.7), channel_id=1, source_target_pairs={{0,4},{2,6},{4,8},{6,10},{8,12},{10,14},{12,0},{14,2},{1,5},{3,7},... | collective-permute-start | bytes 98312 | tf_op jit(solution)/shard_map/ppermute | solution.py:45
  45.6 19.8 %collective-permute-start.13 = (bf16[128,128]{1,0:T(8,128)(2,1)S(1)}, bf16[128,128]{1,0:T(8,128)(2,1)S(1)}, u32[]{:S(2)}, u32[]{:S(2)}) collective-permute-start(bf16[128,128]{1,0:T(8,128)(2,1)S(1)} %get-tuple-element.7), channel_id=1, source_target_pairs={{0,8},{2,10},{4,12},{6,14},{8,0},{10,2},{12,4},{14,6},{1,9},{3,11}... | collective-permute-start | bytes 98312 | tf_op jit(solution)/shard_map/ppermute | solution.py:45
  47.1 24.2 %collective-permute-start.14 = (bf16[128,128]{1,0:T(8,128)(2,1)S(1)}, bf16[128,128]{1,0:T(8,128)(2,1)S(1)}, u32[]{:S(2)}, u32[]{:S(2)}) collective-permute-start(bf16[128,128]{1,0:T(8,128)(2,1)S(1)} %get-tuple-element.7), channel_id=1, source_target_pairs={{0,12},{2,14},{4,0},{6,2},{8,4},{10,6},{12,8},{14,10},{1,13},{3,15... | collective-permute-start | bytes 98312 | tf_op jit(solution)/shard_map/ppermute | solution.py:45
  54.7 6.4 %collective-permute-start.17 = (bf16[128,1024]{1,0:T(8,128)(2,1)S(1)}, bf16[128,1024]{1,0:T(8,128)(2,1)S(1)}, u32[]{:S(2)}, u32[]{:S(2)}) collective-permute-start(bf16[128,1024]{1,0:T(8,128)(2,1)S(1)} %dynamic-slice_convert_fusion), channel_id=1, source_target_pairs={{0,2},{2,0},{4,6},{6,4},{8,10},{10,8},{12,14},{14,12},{1,3},{3,1},... | collective-permute-start | bytes 786440 | tf_op jit(solution)/shard_map/ppermute | solution.py:40
  61.3 4.3 %collective-permute-start.20 = (bf16[128,256]{1,0:T(8,128)(2,1)S(1)}, bf16[128,256]{1,0:T(8,128)(2,1)S(1)}, u32[]{:S(2)}, u32[]{:S(2)}) collective-permute-start(bf16[128,256]{1,0:T(8,128)(2,1)S(1)} %get-tuple-element.15), channel_id=1, source_target_pairs={{0,12},{2,14},{4,0},{6,2},{8,4},{10,6},{12,8},{14,10},{1,13},{3,15... | collective-permute-start | bytes 196616 | tf_op jit(solution)/shard_map/ppermute | solution.py:45
  63.1 8.1 %collective-permute-start.19 = (bf16[128,256]{1,0:T(8,128)(2,1)S(1)}, bf16[128,256]{1,0:T(8,128)(2,1)S(1)}, u32[]{:S(2)}, u32[]{:S(2)}) collective-permute-start(bf16[128,256]{1,0:T(8,128)(2,1)S(1)} %get-tuple-element.16), channel_id=1, source_target_pairs={{0,8},{2,10},{4,12},{6,14},{8,0},{10,2},{12,4},{14,6},{1,9},{3,11}... | collective-permute-start | bytes 196616 | tf_op jit(solution)/shard_map/ppermute | solution.py:45
  63.7 7.5 %collective-permute-start.18 = (bf16[128,256]{1,0:T(8,128)(2,1)S(1)}, bf16[128,256]{1,0:T(8,128)(2,1)S(1)}, u32[]{:S(2)}, u32[]{:S(2)}) collective-permute-start(bf16[128,256]{1,0:T(8,128)(2,1)S(1)} %get-tuple-element.14), channel_id=1, source_target_pairs={{0,4},{2,6},{4,8},{6,10},{8,12},{10,14},{12,0},{14,2},{1,5},{3,7},... | collective-permute-start | bytes 196616 | tf_op jit(solution)/shard_map/ppermute | solution.py:45
  71.3 6.2 %collective-permute-start.21 = (bf16[128,256]{1,0:T(8,128)(2,1)S(1)}, bf16[128,256]{1,0:T(8,128)(2,1)S(1)}, u32[]{:S(2)}, u32[]{:S(2)}) collective-permute-start(bf16[128,256]{1,0:T(8,128)(2,1)S(1)} %get-tuple-element.3), channel_id=1, source_target_pairs={{0,4},{2,6},{4,8},{6,10},{8,12},{10,14},{12,0},{14,2},{1,5},{3,7},... | collective-permute-start | bytes 196616 | tf_op jit(solution)/shard_map/ppermute | solution.py:45
  71.4 8.8 %collective-permute-start.15 = (bf16[128,512]{1,0:T(8,128)(2,1)S(1)}, bf16[128,512]{1,0:T(8,128)(2,1)S(1)}, u32[]{:S(2)}, u32[]{:S(2)}) collective-permute-start(bf16[128,512]{1,0:T(8,128)(2,1)S(1)} %constant_dynamic-update-slice_fusion.4), channel_id=1, source_target_pairs={{0,2},{2,0},{4,6},{6,4},{8,10},{10,8},{12,14},{14,12},{1,3},{3,1},... | collective-permute-start | bytes 393224 | tf_op jit(solution)/shard_map/ppermute | solution.py:40
  72.2 6.7 %collective-permute-start.22 = (bf16[128,256]{1,0:T(8,128)(2,1)S(1)}, bf16[128,256]{1,0:T(8,128)(2,1)S(1)}, u32[]{:S(2)}, u32[]{:S(2)}) collective-permute-start(bf16[128,256]{1,0:T(8,128)(2,1)S(1)} %get-tuple-element.3), channel_id=1, source_target_pairs={{0,8},{2,10},{4,12},{6,14},{8,0},{10,2},{12,4},{14,6},{1,9},{3,11}... | collective-permute-start | bytes 196616 | tf_op jit(solution)/shard_map/ppermute | solution.py:45
  74.1 4.9 %collective-permute-start.23 = (bf16[128,256]{1,0:T(8,128)(2,1)S(1)}, bf16[128,256]{1,0:T(8,128)(2,1)S(1)}, u32[]{:S(2)}, u32[]{:S(2)}) collective-permute-start(bf16[128,256]{1,0:T(8,128)(2,1)S(1)} %get-tuple-element.3), channel_id=1, source_target_pairs={{0,12},{2,14},{4,0},{6,2},{8,4},{10,6},{12,8},{14,10},{1,13},{3,15... | collective-permute-start | bytes 196616 | tf_op jit(solution)/shard_map/ppermute | solution.py:45
  79.0 6.4 %collective-permute-start.24 = (bf16[128,1024]{1,0:T(8,128)(2,1)S(1)}, bf16[128,1024]{1,0:T(8,128)(2,1)S(1)}, u32[]{:S(2)}, u32[]{:S(2)}) collective-permute-start(bf16[128,1024]{1,0:T(8,128)(2,1)S(1)} %constant_dynamic-update-slice_fusion), channel_id=1, source_target_pairs={{0,2},{2,0},{4,6},{6,4},{8,10},{10,8},{12,14},{14,12},{1,3},{3,1},... | collective-permute-start | bytes 786440 | tf_op jit(solution)/shard_map/ppermute | solution.py:40
  80.2 5.3 %copy-start.3 = (s32[512]{0:T(512)S(1)}, s32[512]{0:T(512)}, u32[]{:S(2)}) copy-start(s32[512]{0:T(512)} %param.10) | copy-start | bytes 6148
  80.2 5.3 %copy-start.4 = (s32[128]{0:T(128)S(1)}, s32[128]{0:T(128)}, u32[]{:S(2)}) copy-start(s32[128]{0:T(128)} %param.11) | copy-start | bytes 1540
  85.5 1.1 %copy-start.1 = (bf16[512,1024]{1,0:T(8,128)(2,1)}, bf16[512,1024]{1,0:T(8,128)(2,1)S(1)}, u32[]{:S(2)}) copy-start(bf16[512,1024]{1,0:T(8,128)(2,1)S(1)} %maximum_dynamic-update-slice_fusion.1) | copy-start | bytes 3145732

commit v2 on v0

--- a/solution.py
+++ b/solution.py
@@ -36,15 +36,15 @@
     mine = precondition(queries, left_inv, right_inv)
     ex_count = lax.axis_size("ex")
     position = lax.axis_index("ex")
-    partial_value = jnp.zeros((block_rows * ex_count, store.shape[1]), jnp.float32)
+    scores = jnp.zeros((block_rows * ex_count, store.shape[1]), jnp.bfloat16)
     current = mine
     for step in range(ex_count):
         if step > 0:
             current = passed_along(current, "ex", 1)
         source = (position - step) % ex_count
         tile = score_block(current, store)
-        partial_value = lax.dynamic_update_slice_in_dim(partial_value, tile, source * block_rows, 0)
-    scores = lax.psum(partial_value, "layer").astype(jnp.bfloat16)
+        done = lax.psum(tile.astype(jnp.bfloat16), "layer")
+        scores = lax.dynamic_update_slice_in_dim(scores, done, source * block_rows, 0)
     ids = jnp.arange(scores.shape[0], dtype=jnp.int32)
     prompts = jnp.arange(winner.shape[0], dtype=jnp.int32)
     picks = (winner[:, None] == ids[None, :]).astype(jnp.float32)

time: 117 us -> 120 us (1.026)
  blocking collectives: 93.4 us -> 0 us
  waiting for transfers between devices: 0.01 us -> 81 us
  between operations: 0.77 us -> 14.1 us
  matrix products: 14.2 us -> 17.4 us
    psum x1 -> x0, blocking collectives: 93.4 us -> none  [shards(): scores = lax.psum(partial_value, 'layer').astype(jnp.bfloat16)]
    psum x0 -> x1, waiting for transfers between devices: none -> 81 us  [shards(): done = lax.psum(tile.astype(jnp.bfloat16), 'layer')]
    dot_general x2, matrix products: 10.2 us -> 13.4 us  [score_block(): jnp.einsum('lqp,lep->qe', ready, store, preferred_element_type=jnp.float32)]
    unnamed x19 -> x13, local copies, waits for them, and re-layouts: 4.81 us -> 3.45 us
  transfers between devices with their start and end apart: 1 -> 2, of which waited for: 0 -> 1; matrix products, arithmetic and copies ran while one was open for 6% -> 6% of each run, Pallas kernels for 0% -> 0%
where the time goes in v2:
time: 120 us
  waiting for transfers between devices  81 us (68%)
  matrix products  17.4 us (14%)
  between operations  14.1 us (12%)
  local copies, waits for them, and re-layouts  7.02 us (6%)
    psum x1, waiting for transfers between devices, shards(): done = lax.psum(tile.astype(jnp.bfloat16), 'layer')  81 us
    dot_general x2, matrix products, score_block(): jnp.einsum('lqp,lep->qe', ready, store, preferred_element_type=jnp.float32)  13.4 us
    unnamed x13, local copies, waits for them, and re-layouts  3.45 us
    dot_general x1, matrix products, precondition(): jnp.einsum('lij,lqjm->lqim', left_inv, half, preferred_element_type=jnp.f...  2.94 us
  transfers between devices with their start and end apart: 2, of which 1 were waited for; matrix products, arithmetic and copies ran while one was open for 6% of the time, Pallas kernels for 0%

profile of v2, /device:TPU:0, one launch (start us, length us, event | category | flops | bytes accessed | tf_op | source)
XLA Modules:
  0.0 120.0 jit_solution(3327198320319682710)
XLA Ops:
  7.2 0.0 copy-start
  7.2 0.0 all-reduce.3.cloned.1.call-start
  7.2 0.0 copy-start.3
  7.2 3.4 %copy.8 = bf16[32,8,32,128]{3,2,1,0:T(8,128)(2,1)} copy(bf16[32,8,32,128]{3,1,2,0:T(8,128)(2,1)} %bitcast.43) | data formatting | bytes 4194304
  10.7 0.0 copy-done
  10.7 0.0 copy-done.3
  10.7 2.9 %fusion.11 = bf16[256,128,32]{1,2,0:T(8,128)(2,1)S(1)} fusion(bf16[256,32,128]{2,1,0:T(8,128)(2,1)} %bitcast.42, bf16[1,128,128]{2,1,0:T(8,128)(2,1)S(1)} %copy-done, bf16[1,32,32]{2,1,0:T(8,128)(2,1)S(1)} %copy-done.3), kind=kOutput, calls=%fused_computation.10 | convolution fusion | flops 337641472 | bytes 4229120 | tf_op jit(solution)/shard_map/lij,lqjm->lqim/dot_general | solution.py:24
  13.6 2.3 %reshape.42 = bf16[1,256,4096]{2,1,0:T(8,128)(2,1)} reshape(bf16[1,256,32,128]{3,2,1,0:T(8,128)(2,1)S(1)} %bitcast.40) | data formatting | bytes 4194304 | tf_op jit(solution)/shard_map/reshape | solution.py:27
  15.9 0.5 collective-permute-start
  16.4 6.8 %fusion.14 = bf16[256,1024]{1,0:T(8,128)(2,1)} fusion(bf16[1,1024,4096]{2,1,0:T(8,128)(2,1)} %param.6, bf16[32,8,32,128]{3,2,1,0:T(8,128)(2,1)S(1)} %bitcast.41), kind=kOutput, calls=%fused_computation.11 | convolution fusion | flops 2147745792 | bytes 11010048 | tf_op jit(solution)/shard_map/lqp,lep->qe/dot_general | solution.py:31
  23.1 0.0 collective-permute-done
  23.1 6.6 %fusion.19 = bf16[256,1024]{1,0:T(8,128)(2,1)} fusion(bf16[1,1024,4096]{2,1,0:T(8,128)(2,1)} %param.6, bf16[1,256,4096]{2,1,0:T(8,128)(2,1)S(1)} %collective-permute-done), kind=kOutput, calls=%fused_computation.12 | convolution fusion | flops 2147745792 | bytes 11010048 | tf_op jit(solution)/shard_map/lqp,lep->qe/dot_general | solution.py:31
  29.7 0.0 copy-start.4
  29.7 0.0 copy-start.5
  29.7 0.0 all-reduce.3.cloned.1.call-update
  29.8 81.0 %all-reduce.3.cloned.1.call-done = (bf16[256,1024]{1,0:T(8,128)(2,1)}, bf16[256,1024]{1,0:T(8,128)(2,1)}) async-done(((bf16[256,1024]{1,0:T(8,128)(2,1)}, bf16[256,1024]{1,0:T(8,128)(2,1)}), (bf16[256,1024]{1,0:T(8,128)(2,1)}, bf16[256,1024]{1,0:T(8,128)(2,1)})) %all-reduce.3.cloned.1.call-update) | async-done | bytes 1048592 | tf_op jit(solution)/shard_map/psum | solution.py:46
  110.7 0.0 copy-start.2
  110.7 0.1 broadcast_in_dim.2
  110.9 1.1 constant_dynamic-update-slice_fusion.1
  112.0 0.0 copy-done.2
  112.1 0.0 copy-done.4
  112.1 0.0 copy-done.5
  112.1 0.0 copy-start.1
  112.1 1.1 convolution_convert_fusion
  113.2 0.0 copy-done.1
  (1 shorter events, 0.0 us)
Async XLA Ops:
  7.2 3.5 %copy-start = (bf16[1,128,128]{2,1,0:T(8,128)(2,1)S(1)}, bf16[1,128,128]{2,1,0:T(8,128)(2,1)}, u32[]{:S(2)}) copy-start(bf16[1,128,128]{2,1,0:T(8,128)(2,1)} %param.9) | copy-start | bytes 98308
  7.2 103.6 %all-reduce.3.cloned.1.call-start = ((), (), s32[]{:S(2)}) async-start(), calls=%async_computation | async-start | bytes 2097152 | tf_op jit(solution)/shard_map/psum | solution.py:46
  7.2 3.4 %copy-start.3 = (bf16[1,32,32]{2,1,0:T(8,128)(2,1)S(1)}, bf16[1,32,32]{2,1,0:T(8,128)(2,1)}, u32[]{:S(2)}) copy-start(bf16[1,32,32]{2,1,0:T(8,128)(2,1)} %param.8) | copy-start | bytes 6148
  15.9 7.2 %collective-permute-start = (bf16[1,256,4096]{2,1,0:T(8,128)(2,1)}, bf16[1,256,4096]{2,1,0:T(8,128)(2,1)S(1)}, u32[]{:S(2)}, u32[]{:S(2)}) collective-permute-start(bf16[1,256,4096]{2,1,0:T(8,128)(2,1)} %reshape.42), channel_id=1, source_target_pairs={{1,0},{0,1},{3,2},{2,3},{5,4},{4,5},{7,6},{6,7},{9,8},{8,9},{11,10... | collective-permute-start | bytes 6291464 | tf_op jit(solution)/shard_map/ppermute | solution.py:14
  29.7 82.3 %copy-start.4 = (s32[512]{0:T(512)S(1)}, s32[512]{0:T(512)}, u32[]{:S(2)}) copy-start(s32[512]{0:T(512)} %param.10) | copy-start | bytes 6148
  29.7 82.4 %copy-start.5 = (s32[128]{0:T(128)S(1)}, s32[128]{0:T(128)}, u32[]{:S(2)}) copy-start(s32[128]{0:T(128)} %param.11) | copy-start | bytes 1540
  110.7 1.2 %copy-start.2 = (bf16[256,1024]{1,0:T(8,128)(2,1)S(1)}, bf16[256,1024]{1,0:T(8,128)(2,1)}, u32[]{:S(2)}) copy-start(bf16[256,1024]{1,0:T(8,128)(2,1)} %get-tuple-element.3) | copy-start | bytes 1572868
  112.1 1.1 copy-start.1
Sparse Core Ops, SparseCore 0:
  29.9 80.8 all-reduce.2

commit v3 on v2

v3 whole, which is shorter than its diff:
```python
import functools

import jax
import jax.numpy as jnp
from jax import lax
from jax.experimental import pallas as pl
from jax.experimental.pallas import tpu as pltpu
from jax.sharding import PartitionSpec as P

KIN = 32
KOUT = 128
BEST = 4
TILE = 16
PAIR = 2 * KOUT
BLOCK = 256
VMEM_LIMIT = 40 * 1024 * 1024


def block_rows_of(count):
    return min(BLOCK, count)


def left_matrix(left):
    wide = KIN * TILE
    row = lax.broadcasted_iota(jnp.int32, (wide, KIN), 0)
    column = lax.broadcasted_iota(jnp.int32, (wide, KIN), 1)
    spread = jnp.where((row >> 4) == column, 1.0, 0.0).astype(jnp.bfloat16)
    tall = jnp.dot(spread, left, preferred_element_type=jnp.float32).astype(jnp.bfloat16)
    full = lax.dot_general(
        tall, spread, (((1,), (1,)), ((), ())), preferred_element_type=jnp.float32
    )
    row = lax.broadcasted_iota(jnp.int32, (wide, wide), 0)
    column = lax.broadcasted_iota(jnp.int32, (wide, wide), 1)
    return jnp.where((row & (TILE - 1)) == (column & (TILE - 1)), full, 0.0).astype(jnp.bfloat16)


def right_matrix(right):
    zero = jnp.zeros_like(right)
    return jnp.concatenate(
        [jnp.concatenate([right, zero], 1), jnp.concatenate([zero, right], 1)], 0
    )


def precondition(rows_ref, left, right, half_ref, pre_ref):
    count = rows_ref.shape[0]
    both = right_matrix(right)
    for pair in range(KIN // 2):
        block = rows_ref[:, pair * PAIR : (pair + 1) * PAIR]
        half = jnp.dot(block, both, preferred_element_type=jnp.float32).astype(jnp.bfloat16)
        half_ref[2 * pair] = half[:, :KOUT]
        half_ref[2 * pair + 1] = half[:, KOUT:]
    mixer = left_matrix(left)

    def groups(index, carry):
        at = [pl.multiple_of(index * 2 * TILE + k * TILE, TILE) for k in range(2)]
        stacked = jnp.concatenate(
            [half_ref[:, pl.ds(a, TILE), :].reshape(KIN * TILE, KOUT) for a in at], 1
        )
        mixed = jnp.dot(mixer, stacked, preferred_element_type=jnp.float32).astype(jnp.bfloat16)
        for k in range(2):
            for i in range(KIN):
                pre_ref[pl.ds(at[k], TILE), i * KOUT : (i + 1) * KOUT] = mixed[
                    i * TILE : (i + 1) * TILE, k * KOUT : (k + 1) * KOUT
                ]
        return carry

    lax.fori_loop(0, count // (2 * TILE), groups, 0)


def store_copies(store_ref, store_vmem, sems, first):
    size = store_vmem.shape[1]
    return [
        pltpu.make_async_copy(
            store_ref.at[0, pl.ds(first + b * size, size)], store_vmem.at[b], sems.at[b]
        )
        for b in range(store_vmem.shape[0])
    ]


def dots(pre_ref, store_vmem, copies, out_ref):
    size = store_vmem.shape[1]
    for b, copy in enumerate(copies):
        copy.wait()
        out_ref[:, b * size : (b + 1) * size] = lax.dot_general(
            pre_ref[...],
            store_vmem[b],
            (((1,), (1,)), ((), ())),
            preferred_element_type=jnp.float32,
        )


def first_kernel(
    first, rows_ref, left_ref, right_ref, store_ref, pre_ref, out_ref,
    rows_vmem, half_ref, store_vmem, rows_sem, sems,
):
    rows_copy = pltpu.make_async_copy(rows_ref.at[0], rows_vmem, rows_sem)
    rows_copy.start()
    copies = store_copies(store_ref, store_vmem, sems, first)
    for copy in copies:
        copy.start()
    rows_copy.wait()
    precondition(rows_vmem, left_ref[0], right_ref[0], half_ref, pre_ref)
    dots(pre_ref, store_vmem, copies, out_ref)


def dot_kernel(first, pre_ref, store_ref, out_ref, store_vmem, sems):
    copies = store_copies(store_ref, store_vmem, sems, first)
    for copy in copies:
        copy.start()
    dots(pre_ref, store_vmem, copies, out_ref)


def store_scratch(columns, depth):
    size = block_rows_of(columns)
    return [
        pltpu.VMEM((columns // size, size, depth), jnp.bfloat16),
        pltpu.SemaphoreType.DMA((columns // size,)),
    ]


def precondition_and_score(queries, left_inv, right_inv, store, first, columns):
    count, depth = queries.shape[1:]
    store_vmem, sems = store_scratch(columns, depth)
    vmem = pl.BlockSpec(memory_space=pltpu.VMEM)
    anywhere = pl.BlockSpec(memory_space=pl.ANY)
    return pl.pallas_call(
        functools.partial(first_kernel, first),
        out_shape=(
            jax.ShapeDtypeStruct((count, depth), jnp.bfloat16),
            jax.ShapeDtypeStruct((count, columns), jnp.float32),
        ),
        in_specs=[anywhere, vmem, vmem, anywhere],
        out_specs=(vmem, vmem),
        scratch_shapes=[
            pltpu.VMEM((count, depth), jnp.bfloat16),
            pltpu.VMEM((KIN, count, KOUT), jnp.bfloat16),
            store_vmem,
            pltpu.SemaphoreType.DMA(()),
            sems,
        ],
        compiler_params=pltpu.CompilerParams(vmem_limit_bytes=VMEM_LIMIT),
        cost_estimate=pl.CostEstimate(
            flops=2 * count * depth * (columns + 1024),
            bytes_accessed=2 * depth * (2 * count + columns),
            transcendentals=0,
        ),
    )(queries, left_inv, right_inv, store)


def score(pre, store, first, columns):
    count, depth = pre.shape
    vmem = pl.BlockSpec(memory_space=pltpu.VMEM)
    anywhere = pl.BlockSpec(memory_space=pl.ANY)
    return pl.pallas_call(
        functools.partial(dot_kernel, first),
        out_shape=jax.ShapeDtypeStruct((count, columns), jnp.float32),
        in_specs=[vmem, anywhere],
        out_specs=vmem,
        scratch_shapes=store_scratch(columns, depth),
        compiler_params=pltpu.CompilerParams(vmem_limit_bytes=VMEM_LIMIT),
        cost_estimate=pl.CostEstimate(
            flops=2 * count * depth * columns,
            bytes_accessed=2 * depth * (count + columns),
            transcendentals=0,
        ),
    )(pre, store)


def swap(block, bit):
    route = [(i, i ^ bit) for i in range(lax.axis_size("layer"))]
    return lax.ppermute(block, "layer", route)


def sum_layers(block):
    count = lax.axis_size("layer")
    if count & (count - 1):
        return lax.psum(block, "layer").astype(jnp.bfloat16)
    index = lax.axis_index("layer")
    bits = [1 << k for k in range(count.bit_length() - 1)]
    for bit in bits:
        rows = block.shape[0] // 2
        upper = (index & bit) // bit
        kept = lax.dynamic_slice_in_dim(block, upper * rows, rows, 0)
        sent = lax.dynamic_slice_in_dim(block, (1 - upper) * rows, rows, 0)
        block = kept + swap(sent.astype(jnp.bfloat16), bit).astype(jnp.float32)
    block = block.astype(jnp.bfloat16)
    for bit in reversed(bits):
        other = swap(block, bit)
        low = (index & bit) == 0
        block = jnp.concatenate(
            [jnp.where(low, block, other), jnp.where(low, other, block)], 0
        )
    return block


def shards(store, queries, left_inv, right_inv, query_prompt, winner):
    rows = queries.shape[1]
    columns = store.shape[1]
    half = columns // 2
    ex_count = lax.axis_size("ex")
    position = lax.axis_index("ex")
    pre, left_part = precondition_and_score(queries, left_inv, right_inv, store, 0, half)
    scores = jnp.zeros((rows * ex_count, columns), jnp.bfloat16)
    current = pre
    for step in range(ex_count):
        source = (position - step) % ex_count
        if step == 0:
            parts = [(0, left_part), (half, score(pre, store, half, columns - half))]
        else:
            route = [((i - 1) % ex_count, i) for i in range(ex_count)]
            current = lax.ppermute(current, "ex", route)
            parts = [(0, score(current, store, 0, columns))]
        for first, part in parts:
            scores = lax.dynamic_update_slice(
                scores, sum_layers(part), (source * rows, jnp.int32(first))
            )
    ids = jnp.arange(scores.shape[0], dtype=jnp.int32)
    prompts = jnp.arange(winner.shape[0], dtype=jnp.int32)
    picks = (winner[:, None] == ids[None, :]).astype(jnp.float32)
    member = (query_prompt[None, :] == prompts[:, None]).astype(jnp.float32)
    weights = (picks - member / BEST).astype(jnp.bfloat16)
    advantage = jnp.dot(weights, scores, preferred_element_type=jnp.float32)
    return (scores, advantage.astype(jnp.bfloat16))


def solution(mesh):
    return jax.shard_map(
        shards,
        mesh=mesh,
        in_specs=(
            P("layer", ("grp", "ex"), None),
            P("layer", ("grp", "ex"), None),
            P("layer", None, None),
            P("layer", None, None),
            P("grp"),
            P("grp"),
        ),
        out_specs=(P(None, ("grp", "ex")), P(None, ("grp", "ex"))),
        check_vma=False,
    )
```

time: 120 us -> 86.8 us (0.72)
  waiting for transfers between devices: 81 us -> 31.4 us
  starting transfers between devices: 0.49 us -> 24.6 us
  Pallas kernels: 0 us -> 16.6 us
  matrix products: 17.4 us -> 1.08 us
  between operations: 14.1 us -> 1 us
  local copies, waits for them, and re-layouts: 7.02 us -> 10.1 us
  other arithmetic: 0 us -> 1.61 us
    psum x1 -> x0, waiting for transfers between devices: 81 us -> none  [shards(): done = lax.psum(tile.astype(jnp.bfloat16), 'layer')]
    ppermute x1 -> x19, waiting for transfers between devices: 0.01 us -> 31.4 us  [the longest x18 31.3 us: swap(): return lax.ppermute(block, 'layer', route)]
    ppermute x1 -> x19, starting transfers between devices: 0.45 us -> 24.6 us  [the longest x18 24.6 us: swap(): return lax.ppermute(block, 'layer', route)]
    pallas_call x0 -> x3, Pallas kernels: none -> 16.6 us  [the longest x2 10.1 us: score(): pl.pallas_call(functools.partial(dot_kernel, first), out_shape=jax.ShapeD...]
    dot_general x3 -> x0, matrix products: 16.3 us -> none  [the longest x2 13.4 us: score_block(): jnp.einsum('lqp,lep->qe', ready, store, preferred_element_type=jnp.float32)]
    unnamed x13 -> x18, local copies, waits for them, and re-layouts: 3.45 us -> 9.83 us
    reshape x1 -> x0, local copies, waits for them, and re-layouts: 2.29 us -> none  [precondition(): return pre.reshape(layers, count, KIN * KOUT)]
  transfers between devices with their start and end apart: 2 -> 19, of which waited for: 1 -> 10; matrix products, arithmetic and copies ran while one was open for 6% -> 2% of each run, Pallas kernels for 0% -> 12%
where the time goes in v3:
time: 86.8 us; the launch traced here: 86.4 us
  waiting for transfers between devices  31.4 us (36%)
  starting transfers between devices  24.6 us (28%)
  Pallas kernels  16.6 us (19%)
  local copies, waits for them, and re-layouts  10.1 us (12%)
  other arithmetic  1.61 us (2%)
  matrix products  1.08 us (1%)
  between operations  1 us (1%)
    ppermute x18, waiting for transfers between devices, swap(): return lax.ppermute(block, 'layer', route)  31.3 us
    ppermute x18, starting transfers between devices, swap(): return lax.ppermute(block, 'layer', route)  24.6 us
    pallas_call x2, Pallas kernels, score(): pl.pallas_call(functools.partial(dot_kernel, first), out_shape=jax.ShapeD...  10.1 us
    unnamed x18, local copies, waits for them, and re-layouts  9.83 us
    pallas_call x1, Pallas kernels, precondition_and_score(): pl.pallas_call(functools.partial(first_kernel, first), out_shape=(jax.Sha...  6.52 us
  transfers between devices with their start and end apart: 19, of which 10 were waited for; matrix products, arithmetic and copies ran while one was open for 2% of the time, Pallas kernels for 12%

profile of v3, /device:TPU:0, one launch (start us, length us, event | category | flops | bytes accessed | tf_op | source)
XLA Modules:
  0.0 86.4 jit_solution(15529038496579334856)
XLA Ops:
  0.6 0.0 copy-start
  0.7 3.4 %copy-done = bf16[1,1024,4096]{2,1,0:T(8,128)(2,1)S(1)} copy-done((bf16[1,1024,4096]{2,1,0:T(8,128)(2,1)S(1)}, bf16[1,1024,4096]{2,1,0:T(8,128)(2,1)}, u32[]{:S(2)}) %copy-start) | copy-done | bytes 8388632
  4.0 0.0 copy-start.3
  4.0 1.6 %copy-done.3 = bf16[1,256,4096]{2,1,0:T(8,128)(2,1)S(1)} copy-done((bf16[1,256,4096]{2,1,0:T(8,128)(2,1)S(1)}, bf16[1,256,4096]{2,1,0:T(8,128)(2,1)}, u32[]{:S(2)}) %copy-start.3) | copy-done | bytes 2097176
  5.6 0.0 copy-start.4
  5.6 0.8 copy-done.4
  6.4 0.0 copy-start.5
  6.4 0.7 copy-done.5
  7.1 0.0 copy-start.1
  7.1 6.5 %shard_map.77 = (bf16[256,4096]{1,0:T(8,128)(2,1)S(1)}, f32[256,512]{1,0:T(8,128)S(1)}) custom-call(bf16[1,256,4096]{2,1,0:T(8,128)(2,1)S(1)} %copy-done.3, bf16[1,32,32]{2,1,0:T(8,128)(2,1)S(1)} %copy-done.5, bf16[1,128,128]{2,1,0:T(8,128)(2,1)S(1)} %copy-done.4, bf16[1,1024,4096]{2,1,0:T(8,128)(2,1)S(1)} %copy-done), custom_call_target="tpu_custom_call" | custom-call | flops 3221225472 | bytes 8388608 | tf_op jit(solution)/shard_map/pallas_call | solution.py:126
  13.6 3.0 %collective-permute-start = (bf16[128,512]{1,0:T(8,128)(2,1)S(1)}, bf16[128,512]{1,0:T(8,128)(2,1)}, u32[]{:S(2)}, u32[]{:S(2)}) collective-permute-start(bf16[128,512]{1,0:T(8,128)(2,1)S(1)} %dynamic-slice_convert_fusion.3), channel_id=1, source_target_pairs={{0,2},{2,0},{4,6},{6,4},{8,10},{10,8},{12,14},{14,12},{1,3},{3,1},... | collective-permute-start | bytes 393224 | tf_op jit(solution)/shard_map/ppermute | solution.py:171
  16.7 0.0 collective-permute-start.12
  16.7 0.0 copy-done.1
  16.7 2.8 %shard_map.78 = f32[256,512]{1,0:T(8,128)S(1)} custom-call(bf16[256,4096]{1,0:T(8,128)(2,1)S(1)} %get-tuple-element.5.pre_ref, bf16[1,1024,4096]{2,1,0:T(8,128)(2,1)S(1)} %copy-done.1), custom_call_target="tpu_custom_call" | custom-call | flops 1073741824 | bytes 6291456 | tf_op jit(solution)/shard_map/pallas_call | solution.py:154
  19.5 0.2 collective-permute-start.6
  19.7 0.5 collective-permute-done
  20.2 0.9 %convert_add_fusion.3 = f32[128,512]{1,0:T(8,128)S(1)} fusion(bf16[128,512]{1,0:T(8,128)(2,1)} %collective-permute-done, f32[256,512]{1,0:T(8,128)S(1)} %get-tuple-element.4, s32[]{:T(128)S(6)} %select_n.161), kind=kLoop, calls=%fused_computation.14 | loop fusion | flops 131072 | bytes 655364 | tf_op jit(solution)/shard_map/add | solution.py:185
  21.2 1.9 %collective-permute-start.1 = (bf16[64,512]{1,0:T(8,128)(2,1)S(1)}, bf16[64,512]{1,0:T(8,128)(2,1)S(1)}, u32[]{:S(2)}, u32[]{:S(2)}) collective-permute-start(bf16[64,512]{1,0:T(8,128)(2,1)S(1)} %dynamic-slice_convert_fusion.6), channel_id=1, source_target_pairs={{0,4},{2,6},{4,0},{6,2},{8,12},{10,14},{12,8},{14,10},{1,5},{3,7},... | collective-permute-start | bytes 196616 | tf_op jit(solution)/shard_map/ppermute | solution.py:171
  23.1 2.4 %collective-permute-done.6 = bf16[128,512]{1,0:T(8,128)(2,1)S(1)} collective-permute-done((bf16[128,512]{1,0:T(8,128)(2,1)S(1)}, bf16[128,512]{1,0:T(8,128)(2,1)S(1)}, u32[]{:S(2)}, u32[]{:S(2)}) %collective-permute-start.6) | collective-permute-done | bytes 131104 | tf_op jit(solution)/shard_map/ppermute | solution.py:171
  25.6 1.6 %collective-permute-start.7 = (bf16[64,512]{1,0:T(8,128)(2,1)S(1)}, bf16[64,512]{1,0:T(8,128)(2,1)S(1)}, u32[]{:S(2)}, u32[]{:S(2)}) collective-permute-start(bf16[64,512]{1,0:T(8,128)(2,1)S(1)} %dynamic-slice_convert_fusion.5), channel_id=1, source_target_pairs={{0,4},{2,6},{4,0},{6,2},{8,12},{10,14},{12,8},{14,10},{1,5},{3,7},... | collective-permute-start | bytes 196616 | tf_op jit(solution)/shard_map/ppermute | solution.py:171
  27.2 0.0 collective-permute-done.1
  27.2 2.6 %collective-permute-start.2 = (bf16[32,512]{1,0:T(8,128)(2,1)S(1)}, bf16[32,512]{1,0:T(8,128)(2,1)S(1)}, u32[]{:S(2)}, u32[]{:S(2)}) collective-permute-start(bf16[32,512]{1,0:T(8,128)(2,1)S(1)} %dynamic-slice_convert_fusion.8), channel_id=1, source_target_pairs={{0,8},{2,10},{4,12},{6,14},{8,0},{10,2},{12,4},{14,6},{1,9},{3,11}... | collective-permute-start | bytes 98312 | tf_op jit(solution)/shard_map/ppermute | solution.py:171
  29.9 0.0 collective-permute-done.7
  29.9 2.6 %collective-permute-start.8 = (bf16[32,512]{1,0:T(8,128)(2,1)S(1)}, bf16[32,512]{1,0:T(8,128)(2,1)S(1)}, u32[]{:S(2)}, u32[]{:S(2)}) collective-permute-start(bf16[32,512]{1,0:T(8,128)(2,1)S(1)} %dynamic-slice_convert_fusion.7), channel_id=1, source_target_pairs={{0,8},{2,10},{4,12},{6,14},{8,0},{10,2},{12,4},{14,6},{1,9},{3,11}... | collective-permute-start | bytes 98312 | tf_op jit(solution)/shard_map/ppermute | solution.py:171
  32.6 0.0 collective-permute-done.2
  32.6 2.2 %collective-permute-start.3 = (bf16[32,512]{1,0:T(8,128)(2,1)S(1)}, bf16[32,512]{1,0:T(8,128)(2,1)S(1)}, u32[]{:S(2)}, u32[]{:S(2)}) collective-permute-start(bf16[32,512]{1,0:T(8,128)(2,1)S(1)} %add_convert_fusion.2), channel_id=1, source_target_pairs={{0,8},{2,10},{4,12},{6,14},{8,0},{10,2},{12,4},{14,6},{1,9},{3,11}... | collective-permute-start | bytes 98312 | tf_op jit(solution)/shard_map/ppermute | solution.py:171
  34.8 0.3 collective-permute-done.8
  35.2 2.3 %collective-permute-start.9 = (bf16[32,512]{1,0:T(8,128)(2,1)S(1)}, bf16[32,512]{1,0:T(8,128)(2,1)S(1)}, u32[]{:S(2)}, u32[]{:S(2)}) collective-permute-start(bf16[32,512]{1,0:T(8,128)(2,1)S(1)} %add_convert_fusion.1), channel_id=1, source_target_pairs={{0,8},{2,10},{4,12},{6,14},{8,0},{10,2},{12,4},{14,6},{1,9},{3,11}... | collective-permute-start | bytes 98312 | tf_op jit(solution)/shard_map/ppermute | solution.py:171
  37.5 0.3 collective-permute-done.3
  37.8 1.6 %collective-permute-start.4 = (bf16[64,512]{1,0:T(8,128)(2,1)S(1)}, bf16[64,512]{1,0:T(8,128)(2,1)S(1)}, u32[]{:S(2)}, u32[]{:S(2)}) collective-permute-start(bf16[64,512]{1,0:T(8,128)(2,1)S(1)} %pad_maximum_fusion.4), channel_id=1, source_target_pairs={{0,4},{2,6},{4,0},{6,2},{8,12},{10,14},{12,8},{14,10},{1,5},{3,7},... | collective-permute-start | bytes 196616 | tf_op jit(solution)/shard_map/ppermute | solution.py:171
  39.4 0.0 collective-permute-done.12.pre_ref
  39.4 0.0 copy-start.2
  39.4 3.4 %copy-done.2 = bf16[1,1024,4096]{2,1,0:T(8,128)(2,1)S(1)} copy-done((bf16[1,1024,4096]{2,1,0:T(8,128)(2,1)S(1)}, bf16[1,1024,4096]{2,1,0:T(8,128)(2,1)}, u32[]{:S(2)}) %copy-start.2) | copy-done | bytes 8388632
  42.8 7.2 %shard_map.79 = f32[256,1024]{1,0:T(8,128)S(1)} custom-call(bf16[256,4096]{1,0:T(8,128)(2,1)} %collective-permute-done.12.pre_ref, bf16[1,1024,4096]{2,1,0:T(8,128)(2,1)S(1)} %copy-done.2), custom_call_target="tpu_custom_call" | custom-call | flops 2147483648 | bytes 10485760 | tf_op jit(solution)/shard_map/pallas_call | solution.py:154
  50.1 0.6 collective-permute-start.13
  50.7 0.0 collective-permute-done.9
  50.8 0.5 collective-permute-start.10
  51.3 6.1 %collective-permute-done.13 = bf16[128,1024]{1,0:T(8,128)(2,1)S(1)} collective-permute-done((bf16[128,1024]{1,0:T(8,128)(2,1)S(1)}, bf16[128,1024]{1,0:T(8,128)(2,1)S(1)}, u32[]{:S(2)}, u32[]{:S(2)}) %collective-permute-start.13) | collective-permute-done | bytes 262176 | tf_op jit(solution)/shard_map/ppermute | solution.py:171
  57.4 0.1 convert_add_fusion
  57.5 0.1 collective-permute-start.14
  57.6 0.0 collective-permute-done.4
  57.6 0.7 collective-permute-start.5
  58.3 4.6 %collective-permute-done.14 = bf16[64,1024]{1,0:T(8,128)(2,1)S(1)} collective-permute-done((bf16[64,1024]{1,0:T(8,128)(2,1)S(1)}, bf16[64,1024]{1,0:T(8,128)(2,1)S(1)}, u32[]{:S(2)}, u32[]{:S(2)}) %collective-permute-start.14) | collective-permute-done | bytes 131104 | tf_op jit(solution)/shard_map/ppermute | solution.py:171
  63.0 0.3 collective-permute-start.15
  63.3 0.0 collective-permute-done.10
  63.4 4.9 %collective-permute-done.15 = bf16[32,1024]{1,0:T(8,128)(2,1)S(1)} collective-permute-done((bf16[32,1024]{1,0:T(8,128)(2,1)S(1)}, bf16[32,1024]{1,0:T(8,128)(2,1)S(1)}, u32[]{:S(2)}, u32[]{:S(2)}) %collective-permute-start.15) | collective-permute-done | bytes 65568 | tf_op jit(solution)/shard_map/ppermute | solution.py:171
  68.3 0.3 collective-permute-start.16
  68.6 3.0 %collective-permute-start.11 = (bf16[128,512]{1,0:T(8,128)(2,1)S(1)}, bf16[128,512]{1,0:T(8,128)(2,1)S(1)}, u32[]{:S(2)}, u32[]{:S(2)}) collective-permute-start(bf16[128,512]{1,0:T(8,128)(2,1)S(1)} %pad_maximum_fusion.2), channel_id=1, source_target_pairs={{0,2},{2,0},{4,6},{6,4},{8,10},{10,8},{12,14},{14,12},{1,3},{3,1},... | collective-permute-start | bytes 393224 | tf_op jit(solution)/shard_map/ppermute | solution.py:171
  71.5 2.0 %collective-permute-done.16 = bf16[32,1024]{1,0:T(8,128)(2,1)S(1)} collective-permute-done((bf16[32,1024]{1,0:T(8,128)(2,1)S(1)}, bf16[32,1024]{1,0:T(8,128)(2,1)S(1)}, u32[]{:S(2)}, u32[]{:S(2)}) %collective-permute-start.16) | collective-permute-done | bytes 65568 | tf_op jit(solution)/shard_map/ppermute | solution.py:171
  73.5 0.1 collective-permute-start.17
  73.6 0.0 collective-permute-done.5
  73.7 4.9 %collective-permute-done.17 = bf16[64,1024]{1,0:T(8,128)(2,1)S(1)} collective-permute-done((bf16[64,1024]{1,0:T(8,128)(2,1)S(1)}, bf16[64,1024]{1,0:T(8,128)(2,1)S(1)}, u32[]{:S(2)}, u32[]{:S(2)}) %collective-permute-start.17) | collective-permute-done | bytes 131104 | tf_op jit(solution)/shard_map/ppermute | solution.py:171
  78.7 0.9 %collective-permute-start.18 = (bf16[128,1024]{1,0:T(8,128)(2,1)S(1)}, bf16[128,1024]{1,0:T(8,128)(2,1)S(1)}, u32[]{:S(2)}, u32[]{:S(2)}) collective-permute-start(bf16[128,1024]{1,0:T(8,128)(2,1)S(1)} %pad_maximum_fusion), channel_id=1, source_target_pairs={{0,2},{2,0},{4,6},{6,4},{8,10},{10,8},{12,14},{14,12},{1,3},{3,1},... | collective-permute-start | bytes 786440 | tf_op jit(solution)/shard_map/ppermute | solution.py:171
  79.6 0.0 collective-permute-done.11
  79.7 0.0 copy-start.7
  79.7 0.0 copy-start.8
  79.7 0.1 broadcast_in_dim.2
  79.9 5.2 %collective-permute-done.18 = bf16[128,1024]{1,0:T(8,128)(2,1)S(1)} collective-permute-done((bf16[128,1024]{1,0:T(8,128)(2,1)S(1)}, bf16[128,1024]{1,0:T(8,128)(2,1)S(1)}, u32[]{:S(2)}, u32[]{:S(2)}) %collective-permute-start.18) | collective-permute-done | bytes 262176 | tf_op jit(solution)/shard_map/ppermute | solution.py:171
  85.1 0.1 broadcast_select_fusion.1
  85.3 0.0 copy-done.7
  85.3 0.0 copy-done.8
  85.3 0.0 copy-start.6
  85.3 1.1 %convolution_convert_fusion = bf16[128,1024]{1,0:T(8,128)(2,1)} fusion(bf16[512,1024]{1,0:T(8,128)(2,1)S(1)} %maximum_dynamic-update-slice_fusion, s32[512]{0:T(512)S(1)} %copy-done.7, s32[128]{0:T(128)S(1)} %copy-done.8), kind=kOutput, calls=%fused_computation | convolution fusion | flops 134742016 | bytes 1313280 | tf_op jit(solution)/shard_map/dot_general | solution.py:222
  86.4 0.0 copy-done.6
  (33 shorter events, 0.7 us)
Async XLA Ops:
  0.6 3.4 %copy-start = (bf16[1,1024,4096]{2,1,0:T(8,128)(2,1)S(1)}, bf16[1,1024,4096]{2,1,0:T(8,128)(2,1)}, u32[]{:S(2)}) copy-start(bf16[1,1024,4096]{2,1,0:T(8,128)(2,1)} %store_ref.5) | copy-start | bytes 25165828
  4.0 1.6 %copy-start.3 = (bf16[1,256,4096]{2,1,0:T(8,128)(2,1)S(1)}, bf16[1,256,4096]{2,1,0:T(8,128)(2,1)}, u32[]{:S(2)}) copy-start(bf16[1,256,4096]{2,1,0:T(8,128)(2,1)} %rows_ref.1) | copy-start | bytes 6291460
  5.6 0.8 copy-start.4
  6.4 0.7 copy-start.5
  7.1 9.6 %copy-start.1 = (bf16[1,1024,4096]{2,1,0:T(8,128)(2,1)S(1)}, bf16[1,1024,4096]{2,1,0:T(8,128)(2,1)}, u32[]{:S(2)}) copy-start(bf16[1,1024,4096]{2,1,0:T(8,128)(2,1)} %store_ref.5) | copy-start | bytes 25165828
  13.6 6.6 %collective-permute-start = (bf16[128,512]{1,0:T(8,128)(2,1)S(1)}, bf16[128,512]{1,0:T(8,128)(2,1)}, u32[]{:S(2)}, u32[]{:S(2)}) collective-permute-start(bf16[128,512]{1,0:T(8,128)(2,1)S(1)} %dynamic-slice_convert_fusion.3), channel_id=1, source_target_pairs={{0,2},{2,0},{4,6},{6,4},{8,10},{10,8},{12,14},{14,12},{1,3},{3,1},... | collective-permute-start | bytes 393224 | tf_op jit(solution)/shard_map/ppermute | solution.py:171
  16.7 22.8 %collective-permute-start.12 = (bf16[256,4096]{1,0:T(8,128)(2,1)S(1)}, bf16[256,4096]{1,0:T(8,128)(2,1)}, u32[]{:S(2)}, u32[]{:S(2)}) collective-permute-start(bf16[256,4096]{1,0:T(8,128)(2,1)S(1)} %get-tuple-element.5.pre_ref), channel_id=1, source_target_pairs={{1,0},{0,1},{3,2},{2,3},{5,4},{4,5},{7,6},{6,7},{9,8},{8,9},{11,10... | collective-permute-start | bytes 6291464 | tf_op jit(solution)/shard_map/ppermute | solution.py:211
  19.5 6.0 %collective-permute-start.6 = (bf16[128,512]{1,0:T(8,128)(2,1)S(1)}, bf16[128,512]{1,0:T(8,128)(2,1)S(1)}, u32[]{:S(2)}, u32[]{:S(2)}) collective-permute-start(bf16[128,512]{1,0:T(8,128)(2,1)S(1)} %dynamic-slice_convert_fusion.2), channel_id=1, source_target_pairs={{0,2},{2,0},{4,6},{6,4},{8,10},{10,8},{12,14},{14,12},{1,3},{3,1},... | collective-permute-start | bytes 393224 | tf_op jit(solution)/shard_map/ppermute | solution.py:171
  21.2 6.0 %collective-permute-start.1 = (bf16[64,512]{1,0:T(8,128)(2,1)S(1)}, bf16[64,512]{1,0:T(8,128)(2,1)S(1)}, u32[]{:S(2)}, u32[]{:S(2)}) collective-permute-start(bf16[64,512]{1,0:T(8,128)(2,1)S(1)} %dynamic-slice_convert_fusion.6), channel_id=1, source_target_pairs={{0,4},{2,6},{4,0},{6,2},{8,12},{10,14},{12,8},{14,10},{1,5},{3,7},... | collective-permute-start | bytes 196616 | tf_op jit(solution)/shard_map/ppermute | solution.py:171
  25.6 4.3 %collective-permute-start.7 = (bf16[64,512]{1,0:T(8,128)(2,1)S(1)}, bf16[64,512]{1,0:T(8,128)(2,1)S(1)}, u32[]{:S(2)}, u32[]{:S(2)}) collective-permute-start(bf16[64,512]{1,0:T(8,128)(2,1)S(1)} %dynamic-slice_convert_fusion.5), channel_id=1, source_target_pairs={{0,4},{2,6},{4,0},{6,2},{8,12},{10,14},{12,8},{14,10},{1,5},{3,7},... | collective-permute-start | bytes 196616 | tf_op jit(solution)/shard_map/ppermute | solution.py:171
  27.2 5.3 %collective-permute-start.2 = (bf16[32,512]{1,0:T(8,128)(2,1)S(1)}, bf16[32,512]{1,0:T(8,128)(2,1)S(1)}, u32[]{:S(2)}, u32[]{:S(2)}) collective-permute-start(bf16[32,512]{1,0:T(8,128)(2,1)S(1)} %dynamic-slice_convert_fusion.8), channel_id=1, source_target_pairs={{0,8},{2,10},{4,12},{6,14},{8,0},{10,2},{12,4},{14,6},{1,9},{3,11}... | collective-permute-start | bytes 98312 | tf_op jit(solution)/shard_map/ppermute | solution.py:171
  29.9 5.2 %collective-permute-start.8 = (bf16[32,512]{1,0:T(8,128)(2,1)S(1)}, bf16[32,512]{1,0:T(8,128)(2,1)S(1)}, u32[]{:S(2)}, u32[]{:S(2)}) collective-permute-start(bf16[32,512]{1,0:T(8,128)(2,1)S(1)} %dynamic-slice_convert_fusion.7), channel_id=1, source_target_pairs={{0,8},{2,10},{4,12},{6,14},{8,0},{10,2},{12,4},{14,6},{1,9},{3,11}... | collective-permute-start | bytes 98312 | tf_op jit(solution)/shard_map/ppermute | solution.py:171
  32.6 5.2 %collective-permute-start.3 = (bf16[32,512]{1,0:T(8,128)(2,1)S(1)}, bf16[32,512]{1,0:T(8,128)(2,1)S(1)}, u32[]{:S(2)}, u32[]{:S(2)}) collective-permute-start(bf16[32,512]{1,0:T(8,128)(2,1)S(1)} %add_convert_fusion.2), channel_id=1, source_target_pairs={{0,8},{2,10},{4,12},{6,14},{8,0},{10,2},{12,4},{14,6},{1,9},{3,11}... | collective-permute-start | bytes 98312 | tf_op jit(solution)/shard_map/ppermute | solution.py:171
  35.2 15.6 %collective-permute-start.9 = (bf16[32,512]{1,0:T(8,128)(2,1)S(1)}, bf16[32,512]{1,0:T(8,128)(2,1)S(1)}, u32[]{:S(2)}, u32[]{:S(2)}) collective-permute-start(bf16[32,512]{1,0:T(8,128)(2,1)S(1)} %add_convert_fusion.1), channel_id=1, source_target_pairs={{0,8},{2,10},{4,12},{6,14},{8,0},{10,2},{12,4},{14,6},{1,9},{3,11}... | collective-permute-start | bytes 98312 | tf_op jit(solution)/shard_map/ppermute | solution.py:171
  37.8 19.8 %collective-permute-start.4 = (bf16[64,512]{1,0:T(8,128)(2,1)S(1)}, bf16[64,512]{1,0:T(8,128)(2,1)S(1)}, u32[]{:S(2)}, u32[]{:S(2)}) collective-permute-start(bf16[64,512]{1,0:T(8,128)(2,1)S(1)} %pad_maximum_fusion.4), channel_id=1, source_target_pairs={{0,4},{2,6},{4,0},{6,2},{8,12},{10,14},{12,8},{14,10},{1,5},{3,7},... | collective-permute-start | bytes 196616 | tf_op jit(solution)/shard_map/ppermute | solution.py:171
  39.4 3.4 %copy-start.2 = (bf16[1,1024,4096]{2,1,0:T(8,128)(2,1)S(1)}, bf16[1,1024,4096]{2,1,0:T(8,128)(2,1)}, u32[]{:S(2)}) copy-start(bf16[1,1024,4096]{2,1,0:T(8,128)(2,1)} %store_ref.5) | copy-start | bytes 25165828
  50.1 7.3 %collective-permute-start.13 = (bf16[128,1024]{1,0:T(8,128)(2,1)S(1)}, bf16[128,1024]{1,0:T(8,128)(2,1)S(1)}, u32[]{:S(2)}, u32[]{:S(2)}) collective-permute-start(bf16[128,1024]{1,0:T(8,128)(2,1)S(1)} %dynamic-slice_convert_fusion), channel_id=1, source_target_pairs={{0,2},{2,0},{4,6},{6,4},{8,10},{10,8},{12,14},{14,12},{1,3},{3,1},... | collective-permute-start | bytes 786440 | tf_op jit(solution)/shard_map/ppermute | solution.py:171
  50.8 12.5 %collective-permute-start.10 = (bf16[64,512]{1,0:T(8,128)(2,1)S(1)}, bf16[64,512]{1,0:T(8,128)(2,1)S(1)}, u32[]{:S(2)}, u32[]{:S(2)}) collective-permute-start(bf16[64,512]{1,0:T(8,128)(2,1)S(1)} %pad_maximum_fusion.5), channel_id=1, source_target_pairs={{0,4},{2,6},{4,0},{6,2},{8,12},{10,14},{12,8},{14,10},{1,5},{3,7},... | collective-permute-start | bytes 196616 | tf_op jit(solution)/shard_map/ppermute | solution.py:171
  57.5 5.5 %collective-permute-start.14 = (bf16[64,1024]{1,0:T(8,128)(2,1)S(1)}, bf16[64,1024]{1,0:T(8,128)(2,1)S(1)}, u32[]{:S(2)}, u32[]{:S(2)}) collective-permute-start(bf16[64,1024]{1,0:T(8,128)(2,1)S(1)} %dynamic-slice_convert_fusion.1), channel_id=1, source_target_pairs={{0,4},{2,6},{4,0},{6,2},{8,12},{10,14},{12,8},{14,10},{1,5},{3,7},... | collective-permute-start | bytes 393224 | tf_op jit(solution)/shard_map/ppermute | solution.py:171
  57.6 16.0 %collective-permute-start.5 = (bf16[128,512]{1,0:T(8,128)(2,1)S(1)}, bf16[128,512]{1,0:T(8,128)(2,1)S(1)}, u32[]{:S(2)}, u32[]{:S(2)}) collective-permute-start(bf16[128,512]{1,0:T(8,128)(2,1)S(1)} %pad_maximum_fusion.1), channel_id=1, source_target_pairs={{0,2},{2,0},{4,6},{6,4},{8,10},{10,8},{12,14},{14,12},{1,3},{3,1},... | collective-permute-start | bytes 393224 | tf_op jit(solution)/shard_map/ppermute | solution.py:171
  63.0 5.2 %collective-permute-start.15 = (bf16[32,1024]{1,0:T(8,128)(2,1)S(1)}, bf16[32,1024]{1,0:T(8,128)(2,1)S(1)}, u32[]{:S(2)}, u32[]{:S(2)}) collective-permute-start(bf16[32,1024]{1,0:T(8,128)(2,1)S(1)} %dynamic-slice_convert_fusion.4), channel_id=1, source_target_pairs={{0,8},{2,10},{4,12},{6,14},{8,0},{10,2},{12,4},{14,6},{1,9},{3,11}... | collective-permute-start | bytes 196616 | tf_op jit(solution)/shard_map/ppermute | solution.py:171
  68.3 5.2 %collective-permute-start.16 = (bf16[32,1024]{1,0:T(8,128)(2,1)S(1)}, bf16[32,1024]{1,0:T(8,128)(2,1)S(1)}, u32[]{:S(2)}, u32[]{:S(2)}) collective-permute-start(bf16[32,1024]{1,0:T(8,128)(2,1)S(1)} %add_convert_fusion), channel_id=1, source_target_pairs={{0,8},{2,10},{4,12},{6,14},{8,0},{10,2},{12,4},{14,6},{1,9},{3,11}... | collective-permute-start | bytes 196616 | tf_op jit(solution)/shard_map/ppermute | solution.py:171
  68.6 11.0 %collective-permute-start.11 = (bf16[128,512]{1,0:T(8,128)(2,1)S(1)}, bf16[128,512]{1,0:T(8,128)(2,1)S(1)}, u32[]{:S(2)}, u32[]{:S(2)}) collective-permute-start(bf16[128,512]{1,0:T(8,128)(2,1)S(1)} %pad_maximum_fusion.2), channel_id=1, source_target_pairs={{0,2},{2,0},{4,6},{6,4},{8,10},{10,8},{12,14},{14,12},{1,3},{3,1},... | collective-permute-start | bytes 393224 | tf_op jit(solution)/shard_map/ppermute | solution.py:171
  73.5 5.0 %collective-permute-start.17 = (bf16[64,1024]{1,0:T(8,128)(2,1)S(1)}, bf16[64,1024]{1,0:T(8,128)(2,1)S(1)}, u32[]{:S(2)}, u32[]{:S(2)}) collective-permute-start(bf16[64,1024]{1,0:T(8,128)(2,1)S(1)} %pad_maximum_fusion.3), channel_id=1, source_target_pairs={{0,4},{2,6},{4,0},{6,2},{8,12},{10,14},{12,8},{14,10},{1,5},{3,7},... | collective-permute-start | bytes 393224 | tf_op jit(solution)/shard_map/ppermute | solution.py:171
  78.7 6.4 %collective-permute-start.18 = (bf16[128,1024]{1,0:T(8,128)(2,1)S(1)}, bf16[128,1024]{1,0:T(8,128)(2,1)S(1)}, u32[]{:S(2)}, u32[]{:S(2)}) collective-permute-start(bf16[128,1024]{1,0:T(8,128)(2,1)S(1)} %pad_maximum_fusion), channel_id=1, source_target_pairs={{0,2},{2,0},{4,6},{6,4},{8,10},{10,8},{12,14},{14,12},{1,3},{3,1},... | collective-permute-start | bytes 786440 | tf_op jit(solution)/shard_map/ppermute | solution.py:171
  79.7 5.6 %copy-start.7 = (s32[512]{0:T(512)S(1)}, s32[512]{0:T(512)}, u32[]{:S(2)}) copy-start(s32[512]{0:T(512)} %param.10) | copy-start | bytes 6148
  79.7 5.6 %copy-start.8 = (s32[128]{0:T(128)S(1)}, s32[128]{0:T(128)}, u32[]{:S(2)}) copy-start(s32[128]{0:T(128)} %param.11) | copy-start | bytes 1540
  85.3 1.1 %copy-start.6 = (bf16[512,1024]{1,0:T(8,128)(2,1)}, bf16[512,1024]{1,0:T(8,128)(2,1)S(1)}, u32[]{:S(2)}) copy-start(bf16[512,1024]{1,0:T(8,128)(2,1)S(1)} %maximum_dynamic-update-slice_fusion) | copy-start | bytes 3145732

commit v4 on v3

--- a/solution.py
+++ b/solution.py
@@ -91,15 +91,22 @@
 
 def first_kernel(
     first, rows_ref, left_ref, right_ref, store_ref, pre_ref, out_ref,
-    rows_vmem, half_ref, store_vmem, rows_sem, sems,
+    left_vmem, right_vmem, rows_vmem, half_ref, store_vmem, head_sems, sems,
 ):
-    rows_copy = pltpu.make_async_copy(rows_ref.at[0], rows_vmem, rows_sem)
-    rows_copy.start()
+    heads = [
+        pltpu.make_async_copy(source.at[0], target, head_sems.at[k])
+        for k, (source, target) in enumerate(
+            ((right_ref, right_vmem), (left_ref, left_vmem), (rows_ref, rows_vmem))
+        )
+    ]
+    for copy in heads:
+        copy.start()
     copies = store_copies(store_ref, store_vmem, sems, first)
     for copy in copies:
         copy.start()
-    rows_copy.wait()
-    precondition(rows_vmem, left_ref[0], right_ref[0], half_ref, pre_ref)
+    for copy in heads:
+        copy.wait()
+    precondition(rows_vmem, left_vmem[...], right_vmem[...], half_ref, pre_ref)
     dots(pre_ref, store_vmem, copies, out_ref)
 
 
@@ -108,6 +115,10 @@
     for copy in copies:
         copy.start()
     dots(pre_ref, store_vmem, copies, out_ref)
+
+
+def in_hbm(array):
+    return pltpu.with_memory_space_constraint(array, pltpu.HBM)
 
 
 def store_scratch(columns, depth):
@@ -122,20 +133,22 @@
     count, depth = queries.shape[1:]
     store_vmem, sems = store_scratch(columns, depth)
     vmem = pl.BlockSpec(memory_space=pltpu.VMEM)
-    anywhere = pl.BlockSpec(memory_space=pl.ANY)
+    hbm = pl.BlockSpec(memory_space=pltpu.HBM)
     return pl.pallas_call(
         functools.partial(first_kernel, first),
         out_shape=(
             jax.ShapeDtypeStruct((count, depth), jnp.bfloat16),
             jax.ShapeDtypeStruct((count, columns), jnp.float32),
         ),
-        in_specs=[anywhere, vmem, vmem, anywhere],
+        in_specs=[hbm] * 4,
         out_specs=(vmem, vmem),
         scratch_shapes=[
+            pltpu.VMEM((KIN, KIN), jnp.bfloat16),
+            pltpu.VMEM((KOUT, KOUT), jnp.bfloat16),
             pltpu.VMEM((count, depth), jnp.bfloat16),
             pltpu.VMEM((KIN, count, KOUT), jnp.bfloat16),
             store_vmem,
-            pltpu.SemaphoreType.DMA(()),
+            pltpu.SemaphoreType.DMA((3,)),
             sems,
         ],
         compiler_params=pltpu.CompilerParams(vmem_limit_bytes=VMEM_LIMIT),
@@ -144,17 +157,17 @@
             bytes_accessed=2 * depth * (2 * count + columns),
             transcendentals=0,
         ),
-    )(queries, left_inv, right_inv, store)
+    )(*map(in_hbm, (queries, left_inv, right_inv, store)))
 
 
 def score(pre, store, first, columns):
     count, depth = pre.shape
     vmem = pl.BlockSpec(memory_space=pltpu.VMEM)
-    anywhere = pl.BlockSpec(memory_space=pl.ANY)
+    hbm = pl.BlockSpec(memory_space=pltpu.HBM)
     return pl.pallas_call(
         functools.partial(dot_kernel, first),
         out_shape=jax.ShapeDtypeStruct((count, columns), jnp.float32),
-        in_specs=[vmem, anywhere],
+        in_specs=[vmem, hbm],
         out_specs=vmem,
         scratch_shapes=store_scratch(columns, depth),
         compiler_params=pltpu.CompilerParams(vmem_limit_bytes=VMEM_LIMIT),
@@ -163,7 +176,7 @@
             bytes_accessed=2 * depth * (count + columns),
             transcendentals=0,
         ),
-    )(pre, store)
+    )(pre, in_hbm(store))
 
 
 def swap(block, bit):
@@ -171,26 +184,40 @@
     return lax.ppermute(block, "layer", route)
 
 
-def sum_layers(block):
-    count = lax.axis_size("layer")
-    if count & (count - 1):
-        return lax.psum(block, "layer").astype(jnp.bfloat16)
-    index = lax.axis_index("layer")
-    bits = [1 << k for k in range(count.bit_length() - 1)]
-    for bit in bits:
-        rows = block.shape[0] // 2
-        upper = (index & bit) // bit
-        kept = lax.dynamic_slice_in_dim(block, upper * rows, rows, 0)
-        sent = lax.dynamic_slice_in_dim(block, (1 - upper) * rows, rows, 0)
-        block = kept + swap(sent.astype(jnp.bfloat16), bit).astype(jnp.float32)
-    block = block.astype(jnp.bfloat16)
-    for bit in reversed(bits):
-        other = swap(block, bit)
-        low = (index & bit) == 0
-        block = jnp.concatenate(
-            [jnp.where(low, block, other), jnp.where(low, other, block)], 0
-        )
-    return block
+def halves(block, upper):
+    rows = block.shape[0] // 2
+    kept = lax.dynamic_slice_in_dim(block, upper * rows, rows, 0)
+    sent = lax.dynamic_slice_in_dim(block, (1 - upper) * rows, rows, 0)
+    return kept, sent.astype(jnp.bfloat16)
+
+
+class LayerSum:
+    def __init__(self):
+        self.count = lax.axis_size("layer")
+        self.index = lax.axis_index("layer")
+        self.bits = [1 << k for k in range(self.count.bit_length() - 1)]
+
+    def begin(self, block):
+        if not self.bits:
+            return block, None
+        kept, sent = halves(block, (self.index & self.bits[0]) // self.bits[0])
+        return kept, swap(sent, self.bits[0])
+
+    def finish(self, kept, received):
+        if received is None:
+            return kept.astype(jnp.bfloat16)
+        block = kept + received.astype(jnp.float32)
+        for bit in self.bits[1:]:
+            kept, sent = halves(block, (self.index & bit) // bit)
+            block = kept + swap(sent, bit).astype(jnp.float32)
+        block = block.astype(jnp.bfloat16)
+        for bit in reversed(self.bits):
+            other = swap(block, bit)
+            low = (self.index & bit) == 0
+            block = jnp.concatenate(
+                [jnp.where(low, block, other), jnp.where(low, other, block)], 0
+            )
+        return block
 
 
 def shards(store, queries, left_inv, right_inv, query_prompt, winner):
@@ -201,19 +228,20 @@
     position = lax.axis_index("ex")
     pre, left_part = precondition_and_score(queries, left_inv, right_inv, store, 0, half)
     scores = jnp.zeros((rows * ex_count, columns), jnp.bfloat16)
+    layers = LayerSum()
+    parts = [(position, 0, left_part), (position, half, score(pre, store, half, columns - half))]
     current = pre
-    for step in range(ex_count):
-        source = (position - step) % ex_count
-        if step == 0:
-            parts = [(0, left_part), (half, score(pre, store, half, columns - half))]
-        else:
-            route = [((i - 1) % ex_count, i) for i in range(ex_count)]
-            current = lax.ppermute(current, "ex", route)
-            parts = [(0, score(current, store, 0, columns))]
-        for first, part in parts:
-            scores = lax.dynamic_update_slice(
-                scores, sum_layers(part), (source * rows, jnp.int32(first))
-            )
+    for step in range(1, ex_count):
+        route = [((i - 1) % ex_count, i) for i in range(ex_count)]
+        current = lax.ppermute(current, "ex", route)
+        parts.append(((position - step) % ex_count, 0, score(current, store, 0, columns)))
+    last = parts[-1][2]
+    begun = [layers.begin(part) for _, _, part in parts]
+    for (source, first, _), (kept, received) in zip(parts, begun):
+        if kept.shape != begun[-1][0].shape:
+            received, _ = lax.optimization_barrier((received, last))
+        done = layers.finish(kept, received)
+        scores = lax.dynamic_update_slice(scores, done, (source * rows, jnp.int32(first)))
     ids = jnp.arange(scores.shape[0], dtype=jnp.int32)
     prompts = jnp.arange(winner.shape[0], dtype=jnp.int32)
     picks = (winner[:, None] == ids[None, :]).astype(jnp.float32)

time: 86.8 us -> 76.9 us (0.89)
  local copies, waits for them, and re-layouts: 10.1 us -> 0.33 us
  Pallas kernels: 16.6 us -> 20.8 us
  starting transfers between devices: 24.6 us -> 21.3 us
    unnamed x18 -> x6, local copies, waits for them, and re-layouts: 9.83 us -> 0.02 us
    ppermute x18, starting transfers between devices: 24.6 us -> 20.8 us  [swap(): return lax.ppermute(block, 'layer', route)]
    pallas_call x2, Pallas kernels: 10.1 us -> 12.4 us  [score(): pl.pallas_call(functools.partial(dot_kernel, first), out_shape=jax.ShapeD...]
    pallas_call x1, Pallas kernels: 6.52 us -> 8.36 us  [precondition_and_score(): pl.pallas_call(functools.partial(first_kernel, first), out_shape=(jax.Sha...]
  transfers between devices with their start and end apart: 19 -> 19, of which waited for: 10 -> 9; matrix products, arithmetic and copies ran while one was open for 2% -> 2% of each run, Pallas kernels for 12% -> 16%
where the time goes in v4:
time: 76.9 us; the launch traced here: 76.7 us
  waiting for transfers between devices  30.6 us (40%)
  starting transfers between devices  21.3 us (28%)
  Pallas kernels  20.8 us (27%)
  other arithmetic  1.61 us (2%)
  matrix products  1.08 us (1%)
  between operations  1.01 us (1%)
    ppermute x18, waiting for transfers between devices, swap(): return lax.ppermute(block, 'layer', route)  30.6 us
    ppermute x18, starting transfers between devices, swap(): return lax.ppermute(block, 'layer', route)  20.8 us
    pallas_call x2, Pallas kernels, score(): pl.pallas_call(functools.partial(dot_kernel, first), out_shape=jax.ShapeD...  12.4 us
    pallas_call x1, Pallas kernels, precondition_and_score(): pl.pallas_call(functools.partial(first_kernel, first), out_shape=(jax.Sha...  8.36 us
  transfers between devices with their start and end apart: 19, of which 9 were waited for; matrix products, arithmetic and copies ran while one was open for 2% of the time, Pallas kernels for 16%

profile of v4, /device:TPU:0, one launch (start us, length us, event | category | flops | bytes accessed | tf_op | source)
XLA Modules:
  0.0 76.7 jit_solution(10018645469007382024)
XLA Ops:
  0.6 8.4 %shard_map.77 = (bf16[256,4096]{1,0:T(8,128)(2,1)S(1)}, f32[256,512]{1,0:T(8,128)S(1)}) custom-call(bf16[1,256,4096]{2,1,0:T(8,128)(2,1)} %rows_ref.1, bf16[1,32,32]{2,1,0:T(8,128)(2,1)} %left_ref.1, bf16[1,128,128]{2,1,0:T(8,128)(2,1)} %right_ref.1, bf16[1,1024,4096]{2,1,0:T(8,128)(2,1)} %store_ref.5), custom_call_target="tpu_custom_call" | custom-call | flops 3221225472 | bytes 8388608 | tf_op jit(solution)/shard_map/pallas_call | solution.py:137
  9.0 0.5 collective-permute-start.1
  9.5 4.1 %shard_map.79 = f32[256,512]{1,0:T(8,128)S(1)} custom-call(bf16[256,4096]{1,0:T(8,128)(2,1)S(1)} %get-tuple-element.7.pre_ref, bf16[1,1024,4096]{2,1,0:T(8,128)(2,1)} %store_ref.5), custom_call_target="tpu_custom_call" | custom-call | flops 1073741824 | bytes 6291456 | tf_op jit(solution)/shard_map/pallas_call | solution.py:167
  13.7 2.6 %collective-permute-start.7 = (bf16[128,512]{1,0:T(8,128)(2,1)S(1)}, bf16[128,512]{1,0:T(8,128)(2,1)}, u32[]{:S(2)}, u32[]{:S(2)}) collective-permute-start(bf16[128,512]{1,0:T(8,128)(2,1)S(1)} %dynamic-slice_convert_fusion.2), channel_id=1, source_target_pairs={{0,2},{2,0},{4,6},{6,4},{8,10},{10,8},{12,14},{14,12},{1,3},{3,1},... | collective-permute-start | bytes 393224 | tf_op jit(solution)/shard_map/ppermute | solution.py:184
  16.3 0.1 collective-permute-start
  16.5 0.0 collective-permute-done.1.pre_ref
  16.5 8.3 %shard_map.78 = f32[256,1024]{1,0:T(8,128)S(1)} custom-call(bf16[256,4096]{1,0:T(8,128)(2,1)} %collective-permute-done.1.pre_ref, bf16[1,1024,4096]{2,1,0:T(8,128)(2,1)} %store_ref.5), custom_call_target="tpu_custom_call" | custom-call | flops 2147483648 | bytes 10485760 | tf_op jit(solution)/shard_map/pallas_call | solution.py:167
  24.8 2.0 %collective-permute-start.13 = (bf16[128,1024]{1,0:T(8,128)(2,1)S(1)}, bf16[128,1024]{1,0:T(8,128)(2,1)S(1)}, u32[]{:S(2)}, u32[]{:S(2)}) collective-permute-start(bf16[128,1024]{1,0:T(8,128)(2,1)S(1)} %dynamic-slice_convert_fusion), channel_id=1, source_target_pairs={{0,2},{2,0},{4,6},{6,4},{8,10},{10,8},{12,14},{14,12},{1,3},{3,1},... | collective-permute-start | bytes 786440 | tf_op jit(solution)/shard_map/ppermute | solution.py:184
  26.8 0.0 collective-permute-done.7
  26.8 0.9 %convert_add_fusion.2 = f32[128,512]{1,0:T(8,128)S(1)} fusion(bf16[128,512]{1,0:T(8,128)(2,1)} %collective-permute-done.7, f32[256,512]{1,0:T(8,128)S(1)} %shard_map.79, s32[]{:T(128)S(6)} %select_n.157), kind=kLoop, calls=%fused_computation.12 | loop fusion | flops 131072 | bytes 655364 | tf_op jit(solution)/shard_map/add | solution.py:209
  27.8 1.6 %collective-permute-start.8 = (bf16[64,512]{1,0:T(8,128)(2,1)S(1)}, bf16[64,512]{1,0:T(8,128)(2,1)S(1)}, u32[]{:S(2)}, u32[]{:S(2)}) collective-permute-start(bf16[64,512]{1,0:T(8,128)(2,1)S(1)} %dynamic-slice_convert_fusion.5), channel_id=1, source_target_pairs={{0,4},{2,6},{4,0},{6,2},{8,12},{10,14},{12,8},{14,10},{1,5},{3,7},... | collective-permute-start | bytes 196616 | tf_op jit(solution)/shard_map/ppermute | solution.py:184
  29.4 0.0 collective-permute-done
  29.5 0.5 collective-permute-start.2
  30.0 2.7 %collective-permute-done.8 = bf16[64,512]{1,0:T(8,128)(2,1)S(1)} collective-permute-done((bf16[64,512]{1,0:T(8,128)(2,1)S(1)}, bf16[64,512]{1,0:T(8,128)(2,1)S(1)}, u32[]{:S(2)}, u32[]{:S(2)}) %collective-permute-start.8) | collective-permute-done | bytes 65568 | tf_op jit(solution)/shard_map/ppermute | solution.py:184
  32.8 2.6 %collective-permute-start.9 = (bf16[32,512]{1,0:T(8,128)(2,1)S(1)}, bf16[32,512]{1,0:T(8,128)(2,1)S(1)}, u32[]{:S(2)}, u32[]{:S(2)}) collective-permute-start(bf16[32,512]{1,0:T(8,128)(2,1)S(1)} %dynamic-slice_convert_fusion.7), channel_id=1, source_target_pairs={{0,8},{2,10},{4,12},{6,14},{8,0},{10,2},{12,4},{14,6},{1,9},{3,11}... | collective-permute-start | bytes 98312 | tf_op jit(solution)/shard_map/ppermute | solution.py:184
  35.4 0.0 collective-permute-done.2
  35.4 1.4 %collective-permute-start.3 = (bf16[32,512]{1,0:T(8,128)(2,1)S(1)}, bf16[32,512]{1,0:T(8,128)(2,1)S(1)}, u32[]{:S(2)}, u32[]{:S(2)}) collective-permute-start(bf16[32,512]{1,0:T(8,128)(2,1)S(1)} %dynamic-slice_convert_fusion.8), channel_id=1, source_target_pairs={{0,8},{2,10},{4,12},{6,14},{8,0},{10,2},{12,4},{14,6},{1,9},{3,11}... | collective-permute-start | bytes 98312 | tf_op jit(solution)/shard_map/ppermute | solution.py:184
  36.8 0.8 %collective-permute-done.9 = bf16[32,512]{1,0:T(8,128)(2,1)S(1)} collective-permute-done((bf16[32,512]{1,0:T(8,128)(2,1)S(1)}, bf16[32,512]{1,0:T(8,128)(2,1)S(1)}, u32[]{:S(2)}, u32[]{:S(2)}) %collective-permute-start.9) | collective-permute-done | bytes 32800 | tf_op jit(solution)/shard_map/ppermute | solution.py:184
  37.6 2.6 %collective-permute-start.10 = (bf16[32,512]{1,0:T(8,128)(2,1)S(1)}, bf16[32,512]{1,0:T(8,128)(2,1)S(1)}, u32[]{:S(2)}, u32[]{:S(2)}) collective-permute-start(bf16[32,512]{1,0:T(8,128)(2,1)S(1)} %add_convert_fusion.1), channel_id=1, source_target_pairs={{0,8},{2,10},{4,12},{6,14},{8,0},{10,2},{12,4},{14,6},{1,9},{3,11}... | collective-permute-start | bytes 98312 | tf_op jit(solution)/shard_map/ppermute | solution.py:184
  40.3 0.0 collective-permute-done.3
  40.3 1.4 %collective-permute-start.4 = (bf16[32,512]{1,0:T(8,128)(2,1)S(1)}, bf16[32,512]{1,0:T(8,128)(2,1)S(1)}, u32[]{:S(2)}, u32[]{:S(2)}) collective-permute-start(bf16[32,512]{1,0:T(8,128)(2,1)S(1)} %add_convert_fusion.2), channel_id=1, source_target_pairs={{0,8},{2,10},{4,12},{6,14},{8,0},{10,2},{12,4},{14,6},{1,9},{3,11}... | collective-permute-start | bytes 98312 | tf_op jit(solution)/shard_map/ppermute | solution.py:184
  41.7 1.0 %collective-permute-done.10 = bf16[32,512]{1,0:T(8,128)(2,1)S(1)} collective-permute-done((bf16[32,512]{1,0:T(8,128)(2,1)S(1)}, bf16[32,512]{1,0:T(8,128)(2,1)S(1)}, u32[]{:S(2)}, u32[]{:S(2)}) %collective-permute-start.10) | collective-permute-done | bytes 32800 | tf_op jit(solution)/shard_map/ppermute | solution.py:184
  42.8 1.0 %collective-permute-start.11 = (bf16[64,512]{1,0:T(8,128)(2,1)S(1)}, bf16[64,512]{1,0:T(8,128)(2,1)S(1)}, u32[]{:S(2)}, u32[]{:S(2)}) collective-permute-start(bf16[64,512]{1,0:T(8,128)(2,1)S(1)} %pad_maximum_fusion.5), channel_id=1, source_target_pairs={{0,4},{2,6},{4,0},{6,2},{8,12},{10,14},{12,8},{14,10},{1,5},{3,7},... | collective-permute-start | bytes 196616 | tf_op jit(solution)/shard_map/ppermute | solution.py:184
  43.8 1.4 %collective-permute-done.4 = bf16[32,512]{1,0:T(8,128)(2,1)S(1)} collective-permute-done((bf16[32,512]{1,0:T(8,128)(2,1)S(1)}, bf16[32,512]{1,0:T(8,128)(2,1)S(1)}, u32[]{:S(2)}, u32[]{:S(2)}) %collective-permute-start.4) | collective-permute-done | bytes 32800 | tf_op jit(solution)/shard_map/ppermute | solution.py:184
  45.2 1.5 %collective-permute-start.5 = (bf16[64,512]{1,0:T(8,128)(2,1)S(1)}, bf16[64,512]{1,0:T(8,128)(2,1)S(1)}, u32[]{:S(2)}, u32[]{:S(2)}) collective-permute-start(bf16[64,512]{1,0:T(8,128)(2,1)S(1)} %pad_maximum_fusion.4), channel_id=1, source_target_pairs={{0,4},{2,6},{4,0},{6,2},{8,12},{10,14},{12,8},{14,10},{1,5},{3,7},... | collective-permute-start | bytes 196616 | tf_op jit(solution)/shard_map/ppermute | solution.py:184
  46.7 0.0 collective-permute-done.13
  46.7 0.1 convert_add_fusion
  46.8 0.7 collective-permute-start.14
  47.5 0.0 collective-permute-done.11
  47.5 0.6 collective-permute-start.12
  48.1 4.4 %collective-permute-done.14 = bf16[64,1024]{1,0:T(8,128)(2,1)S(1)} collective-permute-done((bf16[64,1024]{1,0:T(8,128)(2,1)S(1)}, bf16[64,1024]{1,0:T(8,128)(2,1)S(1)}, u32[]{:S(2)}, u32[]{:S(2)}) %collective-permute-start.14) | collective-permute-done | bytes 131104 | tf_op jit(solution)/shard_map/ppermute | solution.py:184
  52.6 0.8 %collective-permute-start.15 = (bf16[32,1024]{1,0:T(8,128)(2,1)S(1)}, bf16[32,1024]{1,0:T(8,128)(2,1)S(1)}, u32[]{:S(2)}, u32[]{:S(2)}) collective-permute-start(bf16[32,1024]{1,0:T(8,128)(2,1)S(1)} %dynamic-slice_convert_fusion.4), channel_id=1, source_target_pairs={{0,8},{2,10},{4,12},{6,14},{8,0},{10,2},{12,4},{14,6},{1,9},{3,11}... | collective-permute-start | bytes 196616 | tf_op jit(solution)/shard_map/ppermute | solution.py:184
  53.4 0.0 collective-permute-done.5
  53.4 5.1 %collective-permute-done.15 = bf16[32,1024]{1,0:T(8,128)(2,1)S(1)} collective-permute-done((bf16[32,1024]{1,0:T(8,128)(2,1)S(1)}, bf16[32,1024]{1,0:T(8,128)(2,1)S(1)}, u32[]{:S(2)}, u32[]{:S(2)}) %collective-permute-start.15) | collective-permute-done | bytes 65568 | tf_op jit(solution)/shard_map/ppermute | solution.py:184
  58.6 0.1 collective-permute-start.16
  58.7 0.6 collective-permute-start.6
  59.3 4.5 %collective-permute-done.16 = bf16[32,1024]{1,0:T(8,128)(2,1)S(1)} collective-permute-done((bf16[32,1024]{1,0:T(8,128)(2,1)S(1)}, bf16[32,1024]{1,0:T(8,128)(2,1)S(1)}, u32[]{:S(2)}, u32[]{:S(2)}) %collective-permute-start.16) | collective-permute-done | bytes 65568 | tf_op jit(solution)/shard_map/ppermute | solution.py:184
  63.9 0.1 collective-permute-start.17
  63.9 0.0 collective-permute-done.12
  64.0 4.9 %collective-permute-done.17 = bf16[64,1024]{1,0:T(8,128)(2,1)S(1)} collective-permute-done((bf16[64,1024]{1,0:T(8,128)(2,1)S(1)}, bf16[64,1024]{1,0:T(8,128)(2,1)S(1)}, u32[]{:S(2)}, u32[]{:S(2)}) %collective-permute-start.17) | collective-permute-done | bytes 131104 | tf_op jit(solution)/shard_map/ppermute | solution.py:184
  69.0 0.6 collective-permute-start.18
  69.5 0.0 collective-permute-done.6
  69.6 0.0 copy-start.1
  69.6 0.0 copy-start.2
  69.6 0.1 broadcast_in_dim.2
  69.8 5.6 %collective-permute-done.18 = bf16[128,1024]{1,0:T(8,128)(2,1)S(1)} collective-permute-done((bf16[128,1024]{1,0:T(8,128)(2,1)S(1)}, bf16[128,1024]{1,0:T(8,128)(2,1)S(1)}, u32[]{:S(2)}, u32[]{:S(2)}) %collective-permute-start.18) | collective-permute-done | bytes 262176 | tf_op jit(solution)/shard_map/ppermute | solution.py:184
  75.4 0.1 broadcast_select_fusion.1
  75.6 0.0 copy-done.1
  75.6 0.0 copy-done.2
  75.6 0.0 copy-start
  75.6 1.1 %convolution_convert_fusion = bf16[128,1024]{1,0:T(8,128)(2,1)} fusion(bf16[512,1024]{1,0:T(8,128)(2,1)S(1)} %maximum_dynamic-update-slice_fusion, s32[512]{0:T(512)S(1)} %copy-done.1, s32[128]{0:T(128)S(1)} %copy-done.2), kind=kOutput, calls=%fused_computation | convolution fusion | flops 134742016 | bytes 1313280 | tf_op jit(solution)/shard_map/dot_general | solution.py:250
  76.7 0.0 copy-done
  (33 shorter events, 0.7 us)
Async XLA Ops:
  9.0 7.5 %collective-permute-start.1 = (bf16[256,4096]{1,0:T(8,128)(2,1)S(1)}, bf16[256,4096]{1,0:T(8,128)(2,1)}, u32[]{:S(2)}, u32[]{:S(2)}) collective-permute-start(bf16[256,4096]{1,0:T(8,128)(2,1)S(1)} %get-tuple-element.7.pre_ref), channel_id=1, source_target_pairs={{1,0},{0,1},{3,2},{2,3},{5,4},{4,5},{7,6},{6,7},{9,8},{8,9},{11,10... | collective-permute-start | bytes 6291464 | tf_op jit(solution)/shard_map/ppermute | solution.py:236
  13.7 13.1 %collective-permute-start.7 = (bf16[128,512]{1,0:T(8,128)(2,1)S(1)}, bf16[128,512]{1,0:T(8,128)(2,1)}, u32[]{:S(2)}, u32[]{:S(2)}) collective-permute-start(bf16[128,512]{1,0:T(8,128)(2,1)S(1)} %dynamic-slice_convert_fusion.2), channel_id=1, source_target_pairs={{0,2},{2,0},{4,6},{6,4},{8,10},{10,8},{12,14},{14,12},{1,3},{3,1},... | collective-permute-start | bytes 393224 | tf_op jit(solution)/shard_map/ppermute | solution.py:184
  16.3 13.1 %collective-permute-start = (bf16[128,512]{1,0:T(8,128)(2,1)S(1)}, bf16[128,512]{1,0:T(8,128)(2,1)S(1)}, u32[]{:S(2)}, u32[]{:S(2)}) collective-permute-start(bf16[128,512]{1,0:T(8,128)(2,1)S(1)} %dynamic-slice_convert_fusion.3), channel_id=1, source_target_pairs={{0,2},{2,0},{4,6},{6,4},{8,10},{10,8},{12,14},{14,12},{1,3},{3,1},... | collective-permute-start | bytes 393224 | tf_op jit(solution)/shard_map/ppermute | solution.py:184
  24.8 21.9 %collective-permute-start.13 = (bf16[128,1024]{1,0:T(8,128)(2,1)S(1)}, bf16[128,1024]{1,0:T(8,128)(2,1)S(1)}, u32[]{:S(2)}, u32[]{:S(2)}) collective-permute-start(bf16[128,1024]{1,0:T(8,128)(2,1)S(1)} %dynamic-slice_convert_fusion), channel_id=1, source_target_pairs={{0,2},{2,0},{4,6},{6,4},{8,10},{10,8},{12,14},{14,12},{1,3},{3,1},... | collective-permute-start | bytes 786440 | tf_op jit(solution)/shard_map/ppermute | solution.py:184
  27.8 4.9 %collective-permute-start.8 = (bf16[64,512]{1,0:T(8,128)(2,1)S(1)}, bf16[64,512]{1,0:T(8,128)(2,1)S(1)}, u32[]{:S(2)}, u32[]{:S(2)}) collective-permute-start(bf16[64,512]{1,0:T(8,128)(2,1)S(1)} %dynamic-slice_convert_fusion.5), channel_id=1, source_target_pairs={{0,4},{2,6},{4,0},{6,2},{8,12},{10,14},{12,8},{14,10},{1,5},{3,7},... | collective-permute-start | bytes 196616 | tf_op jit(solution)/shard_map/ppermute | solution.py:184
  29.5 5.9 %collective-permute-start.2 = (bf16[64,512]{1,0:T(8,128)(2,1)S(1)}, bf16[64,512]{1,0:T(8,128)(2,1)S(1)}, u32[]{:S(2)}, u32[]{:S(2)}) collective-permute-start(bf16[64,512]{1,0:T(8,128)(2,1)S(1)} %dynamic-slice_convert_fusion.6), channel_id=1, source_target_pairs={{0,4},{2,6},{4,0},{6,2},{8,12},{10,14},{12,8},{14,10},{1,5},{3,7},... | collective-permute-start | bytes 196616 | tf_op jit(solution)/shard_map/ppermute | solution.py:184
  32.8 4.9 %collective-permute-start.9 = (bf16[32,512]{1,0:T(8,128)(2,1)S(1)}, bf16[32,512]{1,0:T(8,128)(2,1)S(1)}, u32[]{:S(2)}, u32[]{:S(2)}) collective-permute-start(bf16[32,512]{1,0:T(8,128)(2,1)S(1)} %dynamic-slice_convert_fusion.7), channel_id=1, source_target_pairs={{0,8},{2,10},{4,12},{6,14},{8,0},{10,2},{12,4},{14,6},{1,9},{3,11}... | collective-permute-start | bytes 98312 | tf_op jit(solution)/shard_map/ppermute | solution.py:184
  35.4 4.9 %collective-permute-start.3 = (bf16[32,512]{1,0:T(8,128)(2,1)S(1)}, bf16[32,512]{1,0:T(8,128)(2,1)S(1)}, u32[]{:S(2)}, u32[]{:S(2)}) collective-permute-start(bf16[32,512]{1,0:T(8,128)(2,1)S(1)} %dynamic-slice_convert_fusion.8), channel_id=1, source_target_pairs={{0,8},{2,10},{4,12},{6,14},{8,0},{10,2},{12,4},{14,6},{1,9},{3,11}... | collective-permute-start | bytes 98312 | tf_op jit(solution)/shard_map/ppermute | solution.py:184
  37.6 5.1 %collective-permute-start.10 = (bf16[32,512]{1,0:T(8,128)(2,1)S(1)}, bf16[32,512]{1,0:T(8,128)(2,1)S(1)}, u32[]{:S(2)}, u32[]{:S(2)}) collective-permute-start(bf16[32,512]{1,0:T(8,128)(2,1)S(1)} %add_convert_fusion.1), channel_id=1, source_target_pairs={{0,8},{2,10},{4,12},{6,14},{8,0},{10,2},{12,4},{14,6},{1,9},{3,11}... | collective-permute-start | bytes 98312 | tf_op jit(solution)/shard_map/ppermute | solution.py:184
  40.3 4.9 %collective-permute-start.4 = (bf16[32,512]{1,0:T(8,128)(2,1)S(1)}, bf16[32,512]{1,0:T(8,128)(2,1)S(1)}, u32[]{:S(2)}, u32[]{:S(2)}) collective-permute-start(bf16[32,512]{1,0:T(8,128)(2,1)S(1)} %add_convert_fusion.2), channel_id=1, source_target_pairs={{0,8},{2,10},{4,12},{6,14},{8,0},{10,2},{12,4},{14,6},{1,9},{3,11}... | collective-permute-start | bytes 98312 | tf_op jit(solution)/shard_map/ppermute | solution.py:184
  42.8 4.7 %collective-permute-start.11 = (bf16[64,512]{1,0:T(8,128)(2,1)S(1)}, bf16[64,512]{1,0:T(8,128)(2,1)S(1)}, u32[]{:S(2)}, u32[]{:S(2)}) collective-permute-start(bf16[64,512]{1,0:T(8,128)(2,1)S(1)} %pad_maximum_fusion.5), channel_id=1, source_target_pairs={{0,4},{2,6},{4,0},{6,2},{8,12},{10,14},{12,8},{14,10},{1,5},{3,7},... | collective-permute-start | bytes 196616 | tf_op jit(solution)/shard_map/ppermute | solution.py:184
  45.2 8.2 %collective-permute-start.5 = (bf16[64,512]{1,0:T(8,128)(2,1)S(1)}, bf16[64,512]{1,0:T(8,128)(2,1)S(1)}, u32[]{:S(2)}, u32[]{:S(2)}) collective-permute-start(bf16[64,512]{1,0:T(8,128)(2,1)S(1)} %pad_maximum_fusion.4), channel_id=1, source_target_pairs={{0,4},{2,6},{4,0},{6,2},{8,12},{10,14},{12,8},{14,10},{1,5},{3,7},... | collective-permute-start | bytes 196616 | tf_op jit(solution)/shard_map/ppermute | solution.py:184
  46.8 5.7 %collective-permute-start.14 = (bf16[64,1024]{1,0:T(8,128)(2,1)S(1)}, bf16[64,1024]{1,0:T(8,128)(2,1)S(1)}, u32[]{:S(2)}, u32[]{:S(2)}) collective-permute-start(bf16[64,1024]{1,0:T(8,128)(2,1)S(1)} %dynamic-slice_convert_fusion.1), channel_id=1, source_target_pairs={{0,4},{2,6},{4,0},{6,2},{8,12},{10,14},{12,8},{14,10},{1,5},{3,7},... | collective-permute-start | bytes 393224 | tf_op jit(solution)/shard_map/ppermute | solution.py:184
  47.5 16.4 %collective-permute-start.12 = (bf16[128,512]{1,0:T(8,128)(2,1)S(1)}, bf16[128,512]{1,0:T(8,128)(2,1)S(1)}, u32[]{:S(2)}, u32[]{:S(2)}) collective-permute-start(bf16[128,512]{1,0:T(8,128)(2,1)S(1)} %pad_maximum_fusion.2), channel_id=1, source_target_pairs={{0,2},{2,0},{4,6},{6,4},{8,10},{10,8},{12,14},{14,12},{1,3},{3,1},... | collective-permute-start | bytes 393224 | tf_op jit(solution)/shard_map/ppermute | solution.py:184
  52.6 6.0 %collective-permute-start.15 = (bf16[32,1024]{1,0:T(8,128)(2,1)S(1)}, bf16[32,1024]{1,0:T(8,128)(2,1)S(1)}, u32[]{:S(2)}, u32[]{:S(2)}) collective-permute-start(bf16[32,1024]{1,0:T(8,128)(2,1)S(1)} %dynamic-slice_convert_fusion.4), channel_id=1, source_target_pairs={{0,8},{2,10},{4,12},{6,14},{8,0},{10,2},{12,4},{14,6},{1,9},{3,11}... | collective-permute-start | bytes 196616 | tf_op jit(solution)/shard_map/ppermute | solution.py:184
  58.6 5.3 %collective-permute-start.16 = (bf16[32,1024]{1,0:T(8,128)(2,1)S(1)}, bf16[32,1024]{1,0:T(8,128)(2,1)S(1)}, u32[]{:S(2)}, u32[]{:S(2)}) collective-permute-start(bf16[32,1024]{1,0:T(8,128)(2,1)S(1)} %add_convert_fusion), channel_id=1, source_target_pairs={{0,8},{2,10},{4,12},{6,14},{8,0},{10,2},{12,4},{14,6},{1,9},{3,11}... | collective-permute-start | bytes 196616 | tf_op jit(solution)/shard_map/ppermute | solution.py:184
  58.7 10.8 %collective-permute-start.6 = (bf16[128,512]{1,0:T(8,128)(2,1)S(1)}, bf16[128,512]{1,0:T(8,128)(2,1)S(1)}, u32[]{:S(2)}, u32[]{:S(2)}) collective-permute-start(bf16[128,512]{1,0:T(8,128)(2,1)S(1)} %pad_maximum_fusion.1), channel_id=1, source_target_pairs={{0,2},{2,0},{4,6},{6,4},{8,10},{10,8},{12,14},{14,12},{1,3},{3,1},... | collective-permute-start | bytes 393224 | tf_op jit(solution)/shard_map/ppermute | solution.py:184
  63.9 5.0 %collective-permute-start.17 = (bf16[64,1024]{1,0:T(8,128)(2,1)S(1)}, bf16[64,1024]{1,0:T(8,128)(2,1)S(1)}, u32[]{:S(2)}, u32[]{:S(2)}) collective-permute-start(bf16[64,1024]{1,0:T(8,128)(2,1)S(1)} %pad_maximum_fusion.3), channel_id=1, source_target_pairs={{0,4},{2,6},{4,0},{6,2},{8,12},{10,14},{12,8},{14,10},{1,5},{3,7},... | collective-permute-start | bytes 393224 | tf_op jit(solution)/shard_map/ppermute | solution.py:184
  69.0 6.4 %collective-permute-start.18 = (bf16[128,1024]{1,0:T(8,128)(2,1)S(1)}, bf16[128,1024]{1,0:T(8,128)(2,1)S(1)}, u32[]{:S(2)}, u32[]{:S(2)}) collective-permute-start(bf16[128,1024]{1,0:T(8,128)(2,1)S(1)} %pad_maximum_fusion), channel_id=1, source_target_pairs={{0,2},{2,0},{4,6},{6,4},{8,10},{10,8},{12,14},{14,12},{1,3},{3,1},... | collective-permute-start | bytes 786440 | tf_op jit(solution)/shard_map/ppermute | solution.py:184
  69.6 6.0 %copy-start.1 = (s32[512]{0:T(512)S(1)}, s32[512]{0:T(512)}, u32[]{:S(2)}) copy-start(s32[512]{0:T(512)} %param.10) | copy-start | bytes 6148
  69.6 6.0 %copy-start.2 = (s32[128]{0:T(128)S(1)}, s32[128]{0:T(128)}, u32[]{:S(2)}) copy-start(s32[128]{0:T(128)} %param.11) | copy-start | bytes 1540
  75.6 1.1 %copy-start = (bf16[512,1024]{1,0:T(8,128)(2,1)}, bf16[512,1024]{1,0:T(8,128)(2,1)S(1)}, u32[]{:S(2)}) copy-start(bf16[512,1024]{1,0:T(8,128)(2,1)S(1)} %maximum_dynamic-update-slice_fusion) | copy-start | bytes 3145732

commit v5 on v4

v5 whole, which is shorter than its diff:
```python
import functools

import jax
import jax.numpy as jnp
from jax import lax
from jax.experimental import pallas as pl
from jax.experimental.pallas import tpu as pltpu
from jax.sharding import PartitionSpec as P

KIN = 32
KOUT = 128
BEST = 4
ROWS = 8
WIDE = KIN * ROWS
PAIR = 2 * KOUT
DEPTH_BLOCK = 512
AHEAD = 3
VMEM_LIMIT = 40 * 1024 * 1024
NT = (((1,), (1,)), ((), ()))


def left_matrix(left):
    row = lax.broadcasted_iota(jnp.int32, (WIDE, KIN), 0)
    column = lax.broadcasted_iota(jnp.int32, (WIDE, KIN), 1)
    spread = jnp.where((row >> 3) == column, 1.0, 0.0).astype(jnp.bfloat16)
    tall = jnp.dot(spread, left, preferred_element_type=jnp.float32).astype(jnp.bfloat16)
    full = lax.dot_general(tall, spread, NT, preferred_element_type=jnp.float32)
    row = lax.broadcasted_iota(jnp.int32, (WIDE, WIDE), 0)
    column = lax.broadcasted_iota(jnp.int32, (WIDE, WIDE), 1)
    return jnp.where((row & (ROWS - 1)) == (column & (ROWS - 1)), full, 0.0).astype(jnp.bfloat16)


def right_matrix(right):
    zero = jnp.zeros_like(right)
    return jnp.concatenate(
        [jnp.concatenate([right, zero], 1), jnp.concatenate([zero, right], 1)], 0
    )


def side_by_side_to_stacked(block):
    tiles = block.reshape(block.shape[0] // ROWS, ROWS, PAIR)
    return jnp.concatenate([tiles[:, :, :KOUT], tiles[:, :, KOUT:]], 1)


def precondition(rows_ref, left, right, half_ref, pre_ref):
    count = rows_ref.shape[0]
    both = right_matrix(right)
    together = 4
    for start in range(0, KIN // 2, together):
        block = jnp.concatenate(
            [rows_ref[:, p * PAIR : (p + 1) * PAIR] for p in range(start, start + together)], 0
        )
        half = jnp.dot(block, both, preferred_element_type=jnp.float32)
        for k in range(together):
            at = 2 * ROWS * (start + k)
            half_ref[:, at : at + 2 * ROWS, :] = side_by_side_to_stacked(
                half[k * count : (k + 1) * count]
            ).astype(jnp.bfloat16)
    mixer = left_matrix(left)

    def groups(index, carry):
        stacked = jnp.concatenate([half_ref[2 * index], half_ref[2 * index + 1]], 1)
        mixed = side_by_side_to_stacked(
            jnp.dot(mixer, stacked, preferred_element_type=jnp.float32)
        ).astype(jnp.bfloat16)
        at = pl.ds(pl.multiple_of(index * 2 * ROWS, 2 * ROWS), 2 * ROWS)
        for i in range(KIN):
            pre_ref[at, i * KOUT : (i + 1) * KOUT] = mixed[i]
        return carry

    lax.fori_loop(0, count // (2 * ROWS), groups, 0, unroll=4)


def store_copies(store_ref, store_vmem, sems, first):
    blocks, columns, depth = store_vmem.shape
    return [
        pltpu.make_async_copy(
            store_ref.at[0, pl.ds(first, columns), pl.ds(b * depth, depth)],
            store_vmem.at[b],
            sems.at[b],
        )
        for b in range(blocks)
    ]


def dots(pre_ref, store_vmem, copies, total_ref, out_ref):
    depth = store_vmem.shape[2]
    for b, copy in enumerate(copies):
        copy.wait()
        if b + AHEAD < len(copies):
            copies[b + AHEAD].start()
        term = lax.dot_general(
            store_vmem[b],
            pre_ref[:, b * depth : (b + 1) * depth],
            NT,
            preferred_element_type=jnp.float32,
        )
        if b == 0:
            total_ref[...] = term
        elif b + 1 < len(copies):
            total_ref[...] += term
        else:
            out_ref[...] = (total_ref[...] + term).T


def first_kernel(
    first, rows_ref, left_ref, right_ref, store_ref, pre_ref, out_ref,
    left_vmem, right_vmem, rows_vmem, half_ref, store_vmem, total_ref, head_sems, sems,
):
    heads = [
        pltpu.make_async_copy(source.at[0], target, head_sems.at[k])
        for k, (source, target) in enumerate(
            ((right_ref, right_vmem), (left_ref, left_vmem), (rows_ref, rows_vmem))
        )
    ]
    for copy in heads:
        copy.start()
    copies = store_copies(store_ref, store_vmem, sems, first)
    for copy in copies[:AHEAD]:
        copy.start()
    for copy in heads:
        copy.wait()
    precondition(rows_vmem, left_vmem[...], right_vmem[...], half_ref, pre_ref)
    dots(pre_ref, store_vmem, copies, total_ref, out_ref)


def dot_kernel(first, pre_ref, store_ref, out_ref, store_vmem, total_ref, sems):
    copies = store_copies(store_ref, store_vmem, sems, first)
    for copy in copies[:AHEAD]:
        copy.start()
    dots(pre_ref, store_vmem, copies, total_ref, out_ref)


def in_hbm(array):
    return pltpu.with_memory_space_constraint(array, pltpu.HBM)


def scratch(count, columns, depth):
    blocks = depth // DEPTH_BLOCK
    return (
        pltpu.VMEM((blocks, columns, DEPTH_BLOCK), jnp.bfloat16),
        pltpu.VMEM((columns, count), jnp.float32),
        pltpu.SemaphoreType.DMA((blocks,)),
    )


def precondition_and_score(queries, left_inv, right_inv, store, first, columns):
    count, depth = queries.shape[1:]
    store_vmem, total, sems = scratch(count, columns, depth)
    vmem = pl.BlockSpec(memory_space=pltpu.VMEM)
    hbm = pl.BlockSpec(memory_space=pltpu.HBM)
    return pl.pallas_call(
        functools.partial(first_kernel, first),
        out_shape=(
            jax.ShapeDtypeStruct((count, depth), jnp.bfloat16),
            jax.ShapeDtypeStruct((count, columns), jnp.float32),
        ),
        in_specs=[hbm] * 4,
        out_specs=(vmem, vmem),
        scratch_shapes=[
            pltpu.VMEM((KIN, KIN), jnp.bfloat16),
            pltpu.VMEM((KOUT, KOUT), jnp.bfloat16),
            pltpu.VMEM((count, depth), jnp.bfloat16),
            pltpu.VMEM((count // ROWS, WIDE, KOUT), jnp.bfloat16),
            store_vmem,
            total,
            pltpu.SemaphoreType.DMA((3,)),
            sems,
        ],
        compiler_params=pltpu.CompilerParams(vmem_limit_bytes=VMEM_LIMIT),
        cost_estimate=pl.CostEstimate(
            flops=2 * count * depth * (columns + 1024),
            bytes_accessed=2 * depth * (2 * count + columns),
            transcendentals=0,
        ),
    )(*map(in_hbm, (queries, left_inv, right_inv, store)))


def score(pre, store, first, columns):
    count, depth = pre.shape
    vmem = pl.BlockSpec(memory_space=pltpu.VMEM)
    hbm = pl.BlockSpec(memory_space=pltpu.HBM)
    return pl.pallas_call(
        functools.partial(dot_kernel, first),
        out_shape=jax.ShapeDtypeStruct((count, columns), jnp.float32),
        in_specs=[vmem, hbm],
        out_specs=vmem,
        scratch_shapes=scratch(count, columns, depth),
        compiler_params=pltpu.CompilerParams(vmem_limit_bytes=VMEM_LIMIT),
        cost_estimate=pl.CostEstimate(
            flops=2 * count * depth * columns,
            bytes_accessed=2 * depth * (count + columns),
            transcendentals=0,
        ),
    )(pre, in_hbm(store))


def swap(block, bit):
    route = [(i, i ^ bit) for i in range(lax.axis_size("layer"))]
    return lax.ppermute(block, "layer", route)


class LayerSum:
    def __init__(self, block, bits, index):
        self.block, self.index = block, index
        self.moves = [(bit, True) for bit in bits] + [(bit, False) for bit in reversed(bits)]
        self.steps = len(self.moves)
        if not bits:
            self.block = block.astype(jnp.bfloat16)

    def sizes(self):
        size = self.block.size
        for _, halving in self.moves:
            size = size // 2 if halving else size
            yield 2 * size
            size = size if halving else size * 2

    def send(self, order):
        bit, halving = self.moves[0]
        if halving:
            rows = self.block.shape[0] // 2
            upper = (self.index & bit) // bit
            sent = lax.dynamic_slice_in_dim(self.block, (1 - upper) * rows, rows, 0)
            sent = sent.astype(jnp.bfloat16)
            self.block = lax.dynamic_slice_in_dim(self.block, upper * rows, rows, 0)
        else:
            sent = self.block
        self.received = swap(order.after(sent), bit)

    def take(self, order):
        bit, halving = self.moves.pop(0)
        received = order.mark(self.received)
        if halving:
            self.block = self.block + received.astype(jnp.float32)
            if not (self.moves and self.moves[0][1]):
                self.block = self.block.astype(jnp.bfloat16)
        else:
            low = (self.index & bit) == 0
            mine = self.block
            self.block = jnp.concatenate(
                [jnp.where(low, mine, received), jnp.where(low, received, mine)], 0
            )


class Order:
    def __init__(self):
        self.last = jnp.zeros((), jnp.float32)

    def after(self, value):
        value, _ = lax.optimization_barrier((value, self.last))
        return value

    def mark(self, value):
        value, self.last = lax.optimization_barrier((value, self.last))
        return value


STEP_US = 1.5
BYTES_PER_US = 50000


def sum_layers(chunks):
    order = Order()
    events = []
    for number, (start, chunk) in enumerate(chunks):
        chunk.send(order)
        at = start
        for size in chunk.sizes():
            at += STEP_US + size / BYTES_PER_US
            events.append((at, number))
    order.mark(chunks[-1][1].block)
    for _, number in sorted(events):
        chunk = chunks[number][1]
        chunk.take(order)
        if chunk.moves:
            chunk.send(order)
    return [chunk.block for _, chunk in chunks]


def shards(store, queries, left_inv, right_inv, query_prompt, winner):
    rows = queries.shape[1]
    columns = store.shape[1]
    half = columns // 2
    ex_count = lax.axis_size("ex")
    position = lax.axis_index("ex")
    pre, left_part = precondition_and_score(queries, left_inv, right_inv, store, 0, half)
    parts = [(position, 0, left_part), (position, half, score(pre, store, half, columns - half))]
    current = pre
    for step in range(1, ex_count):
        route = [((i - 1) % ex_count, i) for i in range(ex_count)]
        current = lax.ppermute(current, "ex", route)
        parts.append(((position - step) % ex_count, 0, score(current, store, 0, columns)))
    count = lax.axis_size("layer")
    index = lax.axis_index("layer")
    bits = [1 << k for k in range(count.bit_length() - 1)]
    done = sum_layers(
        [(2 * k, LayerSum(part, bits, index)) for k, (_, _, part) in enumerate(parts)]
    )
    scores = jnp.zeros((rows * ex_count, columns), jnp.bfloat16)
    for (source, first, _), block in zip(parts, done):
        scores = lax.dynamic_update_slice(scores, block, (source * rows, jnp.int32(first)))
    ids = jnp.arange(scores.shape[0], dtype=jnp.int32)
    prompts = jnp.arange(winner.shape[0], dtype=jnp.int32)
    picks = (winner[:, None] == ids[None, :]).astype(jnp.float32)
    member = (query_prompt[None, :] == prompts[:, None]).astype(jnp.float32)
    weights = (picks - member / BEST).astype(jnp.bfloat16)
    advantage = jnp.dot(weights, scores, preferred_element_type=jnp.float32)
    return (scores, advantage.astype(jnp.bfloat16))


def solution(mesh):
    return jax.shard_map(
        shards,
        mesh=mesh,
        in_specs=(
            P("layer", ("grp", "ex"), None),
            P("layer", ("grp", "ex"), None),
            P("layer", None, None),
            P("layer", None, None),
            P("grp"),
            P("grp"),
        ),
        out_specs=(P(None, ("grp", "ex")), P(None, ("grp", "ex"))),
        check_vma=False,
    )
```

time: 76.9 us -> 76.1 us (0.990)
  waiting for transfers between devices: 30.6 us -> 24.5 us
  starting transfers between devices: 21.3 us -> 27.4 us
  Pallas kernels: 20.8 us -> 19.8 us
    ppermute x18, starting transfers between devices: 20.8 us -> 26.9 us  [swap(): return lax.ppermute(block, 'layer', route)]
    ppermute x18, waiting for transfers between devices: 30.6 us -> 24.5 us  [swap(): return lax.ppermute(block, 'layer', route)]
    pallas_call x1, Pallas kernels: 8.36 us -> 7.4 us  [precondition_and_score(): pl.pallas_call(functools.partial(first_kernel, first), out_shape=(jax.Sha...]
  transfers between devices with their start and end apart: 19 -> 19, of which waited for: 9 -> 12; matrix products, arithmetic and copies ran while one was open for 2% -> 1% of each run, Pallas kernels for 16% -> 16%
where the time goes in v5:
time: 76.1 us; the launch traced here: 75.8 us
  starting transfers between devices  27.4 us (36%)
  waiting for transfers between devices  24.5 us (32%)
  Pallas kernels  19.8 us (26%)
  other arithmetic  1.63 us (2%)
  matrix products  1.08 us (1%)
  between operations  0.98 us (1%)
    ppermute x18, starting transfers between devices, swap(): return lax.ppermute(block, 'layer', route)  26.9 us
    ppermute x18, waiting for transfers between devices, swap(): return lax.ppermute(block, 'layer', route)  24.5 us
    pallas_call x2, Pallas kernels, score(): pl.pallas_call(functools.partial(dot_kernel, first), out_shape=jax.ShapeD...  12.4 us
    pallas_call x1, Pallas kernels, precondition_and_score(): pl.pallas_call(functools.partial(first_kernel, first), out_shape=(jax.Sha...  7.4 us
  transfers between devices with their start and end apart: 19, of which 12 were waited for; matrix products, arithmetic and copies ran while one was open for 1% of the time, Pallas kernels for 16%

profile of v5, /device:TPU:0, one launch (start us, length us, event | category | flops | bytes accessed | tf_op | source)
XLA Modules:
  0.0 75.8 jit_solution(8713121426812332639)
XLA Ops:
  0.6 7.4 %shard_map.77 = (bf16[256,4096]{1,0:T(8,128)(2,1)S(1)}, f32[256,512]{1,0:T(8,128)S(1)}) custom-call(bf16[1,256,4096]{2,1,0:T(8,128)(2,1)} %rows_ref.1, bf16[1,32,32]{2,1,0:T(8,128)(2,1)} %left_ref.1, bf16[1,128,128]{2,1,0:T(8,128)(2,1)} %right_ref.1, bf16[1,1024,4096]{2,1,0:T(8,128)(2,1)} %store_ref.5), custom_call_target="tpu_custom_call" | custom-call | flops 3221225472 | bytes 8388608 | tf_op jit(solution)/shard_map/pallas_call | solution.py:152
  8.0 0.5 collective-permute-start.1
  8.6 4.3 %shard_map.79 = f32[256,512]{1,0:T(8,128)S(1)} custom-call(bf16[256,4096]{1,0:T(8,128)(2,1)S(1)} %get-tuple-element.60.pre_ref, bf16[1,1024,4096]{2,1,0:T(8,128)(2,1)} %store_ref.5), custom_call_target="tpu_custom_call" | custom-call | flops 1073741824 | bytes 6291456 | tf_op jit(solution)/shard_map/pallas_call | solution.py:183
  12.9 2.6 %collective-permute-start = (bf16[128,512]{1,0:T(8,128)(2,1)S(1)}, bf16[128,512]{1,0:T(8,128)(2,1)S(1)}, u32[]{:S(2)}, u32[]{:S(2)}) collective-permute-start(bf16[128,512]{1,0:T(8,128)(2,1)S(1)} %get-tuple-element.59), channel_id=1, source_target_pairs={{0,2},{2,0},{4,6},{6,4},{8,10},{10,8},{12,14},{14,12},{1,3},{3,1},... | collective-permute-start | bytes 393224 | tf_op jit(solution)/shard_map/ppermute | solution.py:200
  15.6 0.1 collective-permute-start.3
  15.6 0.0 collective-permute-done.1.pre_ref
  15.6 8.0 %shard_map.78 = f32[256,1024]{1,0:T(8,128)S(1)} custom-call(bf16[256,4096]{1,0:T(8,128)(2,1)} %collective-permute-done.1.pre_ref, bf16[1,1024,4096]{2,1,0:T(8,128)(2,1)} %store_ref.5), custom_call_target="tpu_custom_call" | custom-call | flops 2147483648 | bytes 10485760 | tf_op jit(solution)/shard_map/pallas_call | solution.py:183
  23.7 0.0 collective-permute-done
  23.7 0.0 collective-permute-done.3
  23.7 0.9 %convert_add_fusion.2 = f32[128,512]{1,0:T(8,128)S(1)} fusion(bf16[128,512]{1,0:T(8,128)(2,1)} %collective-permute-done.3, f32[256,512]{1,0:T(8,128)S(1)} %shard_map.79, s32[]{:T(128)S(6)} %select_n.157), kind=kLoop, calls=%fused_computation.12 | loop fusion | flops 131072 | bytes 655364 | tf_op jit(solution)/shard_map/add | solution.py:234
  24.7 2.1 %collective-permute-start.2 = (bf16[64,512]{1,0:T(8,128)(2,1)S(1)}, bf16[64,512]{1,0:T(8,128)(2,1)S(1)}, u32[]{:S(2)}, u32[]{:S(2)}) collective-permute-start(bf16[64,512]{1,0:T(8,128)(2,1)S(1)} %dynamic-slice_convert_fusion.6), channel_id=1, source_target_pairs={{0,4},{2,6},{4,0},{6,2},{8,12},{10,14},{12,8},{14,10},{1,5},{3,7},... | collective-permute-start | bytes 196616 | tf_op jit(solution)/shard_map/ppermute | solution.py:200
  26.8 0.1 collective-permute-start.7
  26.9 2.2 %collective-permute-done.2 = bf16[64,512]{1,0:T(8,128)(2,1)S(1)} collective-permute-done((bf16[64,512]{1,0:T(8,128)(2,1)S(1)}, bf16[64,512]{1,0:T(8,128)(2,1)S(1)}, u32[]{:S(2)}, u32[]{:S(2)}) %collective-permute-start.2) | collective-permute-done | bytes 65568 | tf_op jit(solution)/shard_map/ppermute | solution.py:200
  29.1 3.5 %collective-permute-start.4 = (bf16[32,512]{1,0:T(8,128)(2,1)S(1)}, bf16[32,512]{1,0:T(8,128)(2,1)S(1)}, u32[]{:S(2)}, u32[]{:S(2)}) collective-permute-start(bf16[32,512]{1,0:T(8,128)(2,1)S(1)} %dynamic-slice_convert_fusion.8), channel_id=1, source_target_pairs={{0,8},{2,10},{4,12},{6,14},{8,0},{10,2},{12,4},{14,6},{1,9},{3,11}... | collective-permute-start | bytes 98312 | tf_op jit(solution)/shard_map/ppermute | solution.py:200
  32.6 1.6 %collective-permute-start.6 = (bf16[128,1024]{1,0:T(8,128)(2,1)S(1)}, bf16[128,1024]{1,0:T(8,128)(2,1)S(1)}, u32[]{:S(2)}, u32[]{:S(2)}) collective-permute-start(bf16[128,1024]{1,0:T(8,128)(2,1)S(1)} %dynamic-slice_convert_fusion), channel_id=1, source_target_pairs={{0,2},{2,0},{4,6},{6,4},{8,10},{10,8},{12,14},{14,12},{1,3},{3,1},... | collective-permute-start | bytes 786440 | tf_op jit(solution)/shard_map/ppermute | solution.py:200
  34.2 0.3 collective-permute-done.4
  34.4 0.0 collective-permute-done.7
  34.5 3.0 %collective-permute-start.5 = (bf16[32,512]{1,0:T(8,128)(2,1)S(1)}, bf16[32,512]{1,0:T(8,128)(2,1)S(1)}, u32[]{:S(2)}, u32[]{:S(2)}) collective-permute-start(bf16[32,512]{1,0:T(8,128)(2,1)S(1)} %add_convert_fusion.2), channel_id=1, source_target_pairs={{0,8},{2,10},{4,12},{6,14},{8,0},{10,2},{12,4},{14,6},{1,9},{3,11}... | collective-permute-start | bytes 98312 | tf_op jit(solution)/shard_map/ppermute | solution.py:200
  37.5 0.1 collective-permute-start.9
  37.6 1.4 %collective-permute-done.6 = bf16[128,1024]{1,0:T(8,128)(2,1)S(1)} collective-permute-done((bf16[128,1024]{1,0:T(8,128)(2,1)S(1)}, bf16[128,1024]{1,0:T(8,128)(2,1)S(1)}, u32[]{:S(2)}, u32[]{:S(2)}) %collective-permute-start.6) | collective-permute-done | bytes 262176 | tf_op jit(solution)/shard_map/ppermute | solution.py:200
  39.0 0.3 collective-permute-done.5
  39.4 3.2 %collective-permute-done.9 = bf16[32,512]{1,0:T(8,128)(2,1)S(1)} collective-permute-done((bf16[32,512]{1,0:T(8,128)(2,1)S(1)}, bf16[32,512]{1,0:T(8,128)(2,1)S(1)}, u32[]{:S(2)}, u32[]{:S(2)}) %collective-permute-start.9) | collective-permute-done | bytes 32800 | tf_op jit(solution)/shard_map/ppermute | solution.py:200
  42.6 0.5 collective-permute-start.10
  43.1 0.1 convert_add_fusion
  43.2 2.5 %collective-permute-start.12 = (bf16[64,1024]{1,0:T(8,128)(2,1)S(1)}, bf16[64,1024]{1,0:T(8,128)(2,1)S(1)}, u32[]{:S(2)}, u32[]{:S(2)}) collective-permute-start(bf16[64,1024]{1,0:T(8,128)(2,1)S(1)} %dynamic-slice_convert_fusion.1), channel_id=1, source_target_pairs={{0,4},{2,6},{4,0},{6,2},{8,12},{10,14},{12,8},{14,10},{1,5},{3,7},... | collective-permute-start | bytes 393224 | tf_op jit(solution)/shard_map/ppermute | solution.py:200
  45.8 0.1 collective-permute-start.8
  45.9 1.6 %collective-permute-done.10 = bf16[32,512]{1,0:T(8,128)(2,1)S(1)} collective-permute-done((bf16[32,512]{1,0:T(8,128)(2,1)S(1)}, bf16[32,512]{1,0:T(8,128)(2,1)S(1)}, u32[]{:S(2)}, u32[]{:S(2)}) %collective-permute-start.10) | collective-permute-done | bytes 32800 | tf_op jit(solution)/shard_map/ppermute | solution.py:200
  47.5 2.0 %collective-permute-start.14 = (bf16[64,512]{1,0:T(8,128)(2,1)S(1)}, bf16[64,512]{1,0:T(8,128)(2,1)S(1)}, u32[]{:S(2)}, u32[]{:S(2)}) collective-permute-start(bf16[64,512]{1,0:T(8,128)(2,1)S(1)} %pad_maximum_fusion.5), channel_id=1, source_target_pairs={{0,4},{2,6},{4,0},{6,2},{8,12},{10,14},{12,8},{14,10},{1,5},{3,7},... | collective-permute-start | bytes 196616 | tf_op jit(solution)/shard_map/ppermute | solution.py:200
  49.5 1.3 %collective-permute-done.8 = bf16[64,512]{1,0:T(8,128)(2,1)S(1)} collective-permute-done((bf16[64,512]{1,0:T(8,128)(2,1)S(1)}, bf16[64,512]{1,0:T(8,128)(2,1)S(1)}, u32[]{:S(2)}, u32[]{:S(2)}) %collective-permute-start.8) | collective-permute-done | bytes 65568 | tf_op jit(solution)/shard_map/ppermute | solution.py:200
  50.9 1.4 %collective-permute-start.11 = (bf16[128,512]{1,0:T(8,128)(2,1)S(1)}, bf16[128,512]{1,0:T(8,128)(2,1)S(1)}, u32[]{:S(2)}, u32[]{:S(2)}) collective-permute-start(bf16[128,512]{1,0:T(8,128)(2,1)S(1)} %pad_maximum_fusion.1), channel_id=1, source_target_pairs={{0,2},{2,0},{4,6},{6,4},{8,10},{10,8},{12,14},{14,12},{1,3},{3,1},... | collective-permute-start | bytes 393224 | tf_op jit(solution)/shard_map/ppermute | solution.py:200
  52.3 0.0 collective-permute-done.12
  52.3 0.0 collective-permute-done.14
  52.4 2.0 %collective-permute-start.13 = (bf16[32,1024]{1,0:T(8,128)(2,1)S(1)}, bf16[32,1024]{1,0:T(8,128)(2,1)S(1)}, u32[]{:S(2)}, u32[]{:S(2)}) collective-permute-start(bf16[32,1024]{1,0:T(8,128)(2,1)S(1)} %dynamic-slice_convert_fusion.4), channel_id=1, source_target_pairs={{0,8},{2,10},{4,12},{6,14},{8,0},{10,2},{12,4},{14,6},{1,9},{3,11}... | collective-permute-start | bytes 196616 | tf_op jit(solution)/shard_map/ppermute | solution.py:200
  54.4 3.2 %collective-permute-done.13 = bf16[32,1024]{1,0:T(8,128)(2,1)S(1)} collective-permute-done((bf16[32,1024]{1,0:T(8,128)(2,1)S(1)}, bf16[32,1024]{1,0:T(8,128)(2,1)S(1)}, u32[]{:S(2)}, u32[]{:S(2)}) %collective-permute-start.13) | collective-permute-done | bytes 65568 | tf_op jit(solution)/shard_map/ppermute | solution.py:200
  57.6 2.1 %collective-permute-start.16 = (bf16[32,1024]{1,0:T(8,128)(2,1)S(1)}, bf16[32,1024]{1,0:T(8,128)(2,1)S(1)}, u32[]{:S(2)}, u32[]{:S(2)}) collective-permute-start(bf16[32,1024]{1,0:T(8,128)(2,1)S(1)} %add_convert_fusion), channel_id=1, source_target_pairs={{0,8},{2,10},{4,12},{6,14},{8,0},{10,2},{12,4},{14,6},{1,9},{3,11}... | collective-permute-start | bytes 196616 | tf_op jit(solution)/shard_map/ppermute | solution.py:200
  59.7 0.6 collective-permute-start.15
  60.4 0.0 collective-permute-done.11
  60.4 2.5 %collective-permute-done.16 = bf16[32,1024]{1,0:T(8,128)(2,1)S(1)} collective-permute-done((bf16[32,1024]{1,0:T(8,128)(2,1)S(1)}, bf16[32,1024]{1,0:T(8,128)(2,1)S(1)}, u32[]{:S(2)}, u32[]{:S(2)}) %collective-permute-start.16) | collective-permute-done | bytes 65568 | tf_op jit(solution)/shard_map/ppermute | solution.py:200
  62.9 1.5 %collective-permute-start.17 = (bf16[64,1024]{1,0:T(8,128)(2,1)S(1)}, bf16[64,1024]{1,0:T(8,128)(2,1)S(1)}, u32[]{:S(2)}, u32[]{:S(2)}) collective-permute-start(bf16[64,1024]{1,0:T(8,128)(2,1)S(1)} %pad_maximum_fusion.3), channel_id=1, source_target_pairs={{0,4},{2,6},{4,0},{6,2},{8,12},{10,14},{12,8},{14,10},{1,5},{3,7},... | collective-permute-start | bytes 393224 | tf_op jit(solution)/shard_map/ppermute | solution.py:200
  64.5 0.1 broadcast_in_dim.2
  64.6 0.0 copy-start.1
  64.6 0.0 copy-start.2
  64.7 1.1 %collective-permute-done.15 = bf16[128,512]{1,0:T(8,128)(2,1)S(1)} collective-permute-done((bf16[128,512]{1,0:T(8,128)(2,1)S(1)}, bf16[128,512]{1,0:T(8,128)(2,1)S(1)}, u32[]{:S(2)}, u32[]{:S(2)}) %collective-permute-start.15) | collective-permute-done | bytes 131104 | tf_op jit(solution)/shard_map/ppermute | solution.py:200
  65.8 2.2 %collective-permute-done.17 = bf16[64,1024]{1,0:T(8,128)(2,1)S(1)} collective-permute-done((bf16[64,1024]{1,0:T(8,128)(2,1)S(1)}, bf16[64,1024]{1,0:T(8,128)(2,1)S(1)}, u32[]{:S(2)}, u32[]{:S(2)}) %collective-permute-start.17) | collective-permute-done | bytes 131104 | tf_op jit(solution)/shard_map/ppermute | solution.py:200
  68.0 1.1 %collective-permute-start.18 = (bf16[128,1024]{1,0:T(8,128)(2,1)S(1)}, bf16[128,1024]{1,0:T(8,128)(2,1)S(1)}, u32[]{:S(2)}, u32[]{:S(2)}) collective-permute-start(bf16[128,1024]{1,0:T(8,128)(2,1)S(1)} %pad_maximum_fusion), channel_id=1, source_target_pairs={{0,2},{2,0},{4,6},{6,4},{8,10},{10,8},{12,14},{14,12},{1,3},{3,1},... | collective-permute-start | bytes 786440 | tf_op jit(solution)/shard_map/ppermute | solution.py:200
  69.2 5.2 %collective-permute-done.18 = bf16[128,1024]{1,0:T(8,128)(2,1)S(1)} collective-permute-done((bf16[128,1024]{1,0:T(8,128)(2,1)S(1)}, bf16[128,1024]{1,0:T(8,128)(2,1)S(1)}, u32[]{:S(2)}, u32[]{:S(2)}) %collective-permute-start.18) | collective-permute-done | bytes 262176 | tf_op jit(solution)/shard_map/ppermute | solution.py:200
  74.5 0.1 broadcast_select_fusion.1
  74.6 0.0 copy-done.1
  74.6 0.0 copy-done.2
  74.7 0.0 copy-start
  74.7 1.1 %convolution_convert_fusion = bf16[128,1024]{1,0:T(8,128)(2,1)} fusion(bf16[512,1024]{1,0:T(8,128)(2,1)S(1)} %maximum_dynamic-update-slice_fusion, s32[512]{0:T(512)S(1)} %copy-done.1, s32[128]{0:T(128)S(1)} %copy-done.2), kind=kOutput, calls=%fused_computation | convolution fusion | flops 134742016 | bytes 1313280 | tf_op jit(solution)/shard_map/dot_general | solution.py:307
  75.8 0.0 copy-done
  (32 shorter events, 0.7 us)
Async XLA Ops:
  8.0 7.6 %collective-permute-start.1 = (bf16[256,4096]{1,0:T(8,128)(2,1)S(1)}, bf16[256,4096]{1,0:T(8,128)(2,1)}, u32[]{:S(2)}, u32[]{:S(2)}) collective-permute-start(bf16[256,4096]{1,0:T(8,128)(2,1)S(1)} %get-tuple-element.60.pre_ref), channel_id=1, source_target_pairs={{1,0},{0,1},{3,2},{2,3},{5,4},{4,5},{7,6},{6,7},{9,8},{8,9},{11,10... | collective-permute-start | bytes 6291464 | tf_op jit(solution)/shard_map/ppermute | solution.py:291
  12.9 10.8 %collective-permute-start = (bf16[128,512]{1,0:T(8,128)(2,1)S(1)}, bf16[128,512]{1,0:T(8,128)(2,1)S(1)}, u32[]{:S(2)}, u32[]{:S(2)}) collective-permute-start(bf16[128,512]{1,0:T(8,128)(2,1)S(1)} %get-tuple-element.59), channel_id=1, source_target_pairs={{0,2},{2,0},{4,6},{6,4},{8,10},{10,8},{12,14},{14,12},{1,3},{3,1},... | collective-permute-start | bytes 393224 | tf_op jit(solution)/shard_map/ppermute | solution.py:200
  15.6 8.1 %collective-permute-start.3 = (bf16[128,512]{1,0:T(8,128)(2,1)S(1)}, bf16[128,512]{1,0:T(8,128)(2,1)}, u32[]{:S(2)}, u32[]{:S(2)}) collective-permute-start(bf16[128,512]{1,0:T(8,128)(2,1)S(1)} %get-tuple-element.65), channel_id=1, source_target_pairs={{0,2},{2,0},{4,6},{6,4},{8,10},{10,8},{12,14},{14,12},{1,3},{3,1},... | collective-permute-start | bytes 393224 | tf_op jit(solution)/shard_map/ppermute | solution.py:200
  24.7 4.3 %collective-permute-start.2 = (bf16[64,512]{1,0:T(8,128)(2,1)S(1)}, bf16[64,512]{1,0:T(8,128)(2,1)S(1)}, u32[]{:S(2)}, u32[]{:S(2)}) collective-permute-start(bf16[64,512]{1,0:T(8,128)(2,1)S(1)} %dynamic-slice_convert_fusion.6), channel_id=1, source_target_pairs={{0,4},{2,6},{4,0},{6,2},{8,12},{10,14},{12,8},{14,10},{1,5},{3,7},... | collective-permute-start | bytes 196616 | tf_op jit(solution)/shard_map/ppermute | solution.py:200
  26.8 7.6 %collective-permute-start.7 = (bf16[64,512]{1,0:T(8,128)(2,1)S(1)}, bf16[64,512]{1,0:T(8,128)(2,1)S(1)}, u32[]{:S(2)}, u32[]{:S(2)}) collective-permute-start(bf16[64,512]{1,0:T(8,128)(2,1)S(1)} %dynamic-slice_convert_fusion.5), channel_id=1, source_target_pairs={{0,4},{2,6},{4,0},{6,2},{8,12},{10,14},{12,8},{14,10},{1,5},{3,7},... | collective-permute-start | bytes 196616 | tf_op jit(solution)/shard_map/ppermute | solution.py:200
  29.1 5.3 %collective-permute-start.4 = (bf16[32,512]{1,0:T(8,128)(2,1)S(1)}, bf16[32,512]{1,0:T(8,128)(2,1)S(1)}, u32[]{:S(2)}, u32[]{:S(2)}) collective-permute-start(bf16[32,512]{1,0:T(8,128)(2,1)S(1)} %dynamic-slice_convert_fusion.8), channel_id=1, source_target_pairs={{0,8},{2,10},{4,12},{6,14},{8,0},{10,2},{12,4},{14,6},{1,9},{3,11}... | collective-permute-start | bytes 98312 | tf_op jit(solution)/shard_map/ppermute | solution.py:200
  32.6 6.4 %collective-permute-start.6 = (bf16[128,1024]{1,0:T(8,128)(2,1)S(1)}, bf16[128,1024]{1,0:T(8,128)(2,1)S(1)}, u32[]{:S(2)}, u32[]{:S(2)}) collective-permute-start(bf16[128,1024]{1,0:T(8,128)(2,1)S(1)} %dynamic-slice_convert_fusion), channel_id=1, source_target_pairs={{0,2},{2,0},{4,6},{6,4},{8,10},{10,8},{12,14},{14,12},{1,3},{3,1},... | collective-permute-start | bytes 786440 | tf_op jit(solution)/shard_map/ppermute | solution.py:200
  34.5 4.9 %collective-permute-start.5 = (bf16[32,512]{1,0:T(8,128)(2,1)S(1)}, bf16[32,512]{1,0:T(8,128)(2,1)S(1)}, u32[]{:S(2)}, u32[]{:S(2)}) collective-permute-start(bf16[32,512]{1,0:T(8,128)(2,1)S(1)} %add_convert_fusion.2), channel_id=1, source_target_pairs={{0,8},{2,10},{4,12},{6,14},{8,0},{10,2},{12,4},{14,6},{1,9},{3,11}... | collective-permute-start | bytes 98312 | tf_op jit(solution)/shard_map/ppermute | solution.py:200
  37.5 5.1 %collective-permute-start.9 = (bf16[32,512]{1,0:T(8,128)(2,1)S(1)}, bf16[32,512]{1,0:T(8,128)(2,1)S(1)}, u32[]{:S(2)}, u32[]{:S(2)}) collective-permute-start(bf16[32,512]{1,0:T(8,128)(2,1)S(1)} %dynamic-slice_convert_fusion.7), channel_id=1, source_target_pairs={{0,8},{2,10},{4,12},{6,14},{8,0},{10,2},{12,4},{14,6},{1,9},{3,11}... | collective-permute-start | bytes 98312 | tf_op jit(solution)/shard_map/ppermute | solution.py:200
  42.6 4.9 %collective-permute-start.10 = (bf16[32,512]{1,0:T(8,128)(2,1)S(1)}, bf16[32,512]{1,0:T(8,128)(2,1)S(1)}, u32[]{:S(2)}, u32[]{:S(2)}) collective-permute-start(bf16[32,512]{1,0:T(8,128)(2,1)S(1)} %add_convert_fusion.1), channel_id=1, source_target_pairs={{0,8},{2,10},{4,12},{6,14},{8,0},{10,2},{12,4},{14,6},{1,9},{3,11}... | collective-permute-start | bytes 98312 | tf_op jit(solution)/shard_map/ppermute | solution.py:200
  43.2 9.1 %collective-permute-start.12 = (bf16[64,1024]{1,0:T(8,128)(2,1)S(1)}, bf16[64,1024]{1,0:T(8,128)(2,1)S(1)}, u32[]{:S(2)}, u32[]{:S(2)}) collective-permute-start(bf16[64,1024]{1,0:T(8,128)(2,1)S(1)} %dynamic-slice_convert_fusion.1), channel_id=1, source_target_pairs={{0,4},{2,6},{4,0},{6,2},{8,12},{10,14},{12,8},{14,10},{1,5},{3,7},... | collective-permute-start | bytes 393224 | tf_op jit(solution)/shard_map/ppermute | solution.py:200
  45.8 5.0 %collective-permute-start.8 = (bf16[64,512]{1,0:T(8,128)(2,1)S(1)}, bf16[64,512]{1,0:T(8,128)(2,1)S(1)}, u32[]{:S(2)}, u32[]{:S(2)}) collective-permute-start(bf16[64,512]{1,0:T(8,128)(2,1)S(1)} %pad_maximum_fusion.4), channel_id=1, source_target_pairs={{0,4},{2,6},{4,0},{6,2},{8,12},{10,14},{12,8},{14,10},{1,5},{3,7},... | collective-permute-start | bytes 196616 | tf_op jit(solution)/shard_map/ppermute | solution.py:200
  47.5 4.8 %collective-permute-start.14 = (bf16[64,512]{1,0:T(8,128)(2,1)S(1)}, bf16[64,512]{1,0:T(8,128)(2,1)S(1)}, u32[]{:S(2)}, u32[]{:S(2)}) collective-permute-start(bf16[64,512]{1,0:T(8,128)(2,1)S(1)} %pad_maximum_fusion.5), channel_id=1, source_target_pairs={{0,4},{2,6},{4,0},{6,2},{8,12},{10,14},{12,8},{14,10},{1,5},{3,7},... | collective-permute-start | bytes 196616 | tf_op jit(solution)/shard_map/ppermute | solution.py:200
  50.9 9.5 %collective-permute-start.11 = (bf16[128,512]{1,0:T(8,128)(2,1)S(1)}, bf16[128,512]{1,0:T(8,128)(2,1)S(1)}, u32[]{:S(2)}, u32[]{:S(2)}) collective-permute-start(bf16[128,512]{1,0:T(8,128)(2,1)S(1)} %pad_maximum_fusion.1), channel_id=1, source_target_pairs={{0,2},{2,0},{4,6},{6,4},{8,10},{10,8},{12,14},{14,12},{1,3},{3,1},... | collective-permute-start | bytes 393224 | tf_op jit(solution)/shard_map/ppermute | solution.py:200
  52.4 5.3 %collective-permute-start.13 = (bf16[32,1024]{1,0:T(8,128)(2,1)S(1)}, bf16[32,1024]{1,0:T(8,128)(2,1)S(1)}, u32[]{:S(2)}, u32[]{:S(2)}) collective-permute-start(bf16[32,1024]{1,0:T(8,128)(2,1)S(1)} %dynamic-slice_convert_fusion.4), channel_id=1, source_target_pairs={{0,8},{2,10},{4,12},{6,14},{8,0},{10,2},{12,4},{14,6},{1,9},{3,11}... | collective-permute-start | bytes 196616 | tf_op jit(solution)/shard_map/ppermute | solution.py:200
  57.6 5.2 %collective-permute-start.16 = (bf16[32,1024]{1,0:T(8,128)(2,1)S(1)}, bf16[32,1024]{1,0:T(8,128)(2,1)S(1)}, u32[]{:S(2)}, u32[]{:S(2)}) collective-permute-start(bf16[32,1024]{1,0:T(8,128)(2,1)S(1)} %add_convert_fusion), channel_id=1, source_target_pairs={{0,8},{2,10},{4,12},{6,14},{8,0},{10,2},{12,4},{14,6},{1,9},{3,11}... | collective-permute-start | bytes 196616 | tf_op jit(solution)/shard_map/ppermute | solution.py:200
  59.7 6.0 %collective-permute-start.15 = (bf16[128,512]{1,0:T(8,128)(2,1)S(1)}, bf16[128,512]{1,0:T(8,128)(2,1)S(1)}, u32[]{:S(2)}, u32[]{:S(2)}) collective-permute-start(bf16[128,512]{1,0:T(8,128)(2,1)S(1)} %pad_maximum_fusion.2), channel_id=1, source_target_pairs={{0,2},{2,0},{4,6},{6,4},{8,10},{10,8},{12,14},{14,12},{1,3},{3,1},... | collective-permute-start | bytes 393224 | tf_op jit(solution)/shard_map/ppermute | solution.py:200
  62.9 5.0 %collective-permute-start.17 = (bf16[64,1024]{1,0:T(8,128)(2,1)S(1)}, bf16[64,1024]{1,0:T(8,128)(2,1)S(1)}, u32[]{:S(2)}, u32[]{:S(2)}) collective-permute-start(bf16[64,1024]{1,0:T(8,128)(2,1)S(1)} %pad_maximum_fusion.3), channel_id=1, source_target_pairs={{0,4},{2,6},{4,0},{6,2},{8,12},{10,14},{12,8},{14,10},{1,5},{3,7},... | collective-permute-start | bytes 393224 | tf_op jit(solution)/shard_map/ppermute | solution.py:200
  64.6 10.0 %copy-start.1 = (s32[512]{0:T(512)S(1)}, s32[512]{0:T(512)}, u32[]{:S(2)}) copy-start(s32[512]{0:T(512)} %param.10) | copy-start | bytes 6148
  64.6 10.0 %copy-start.2 = (s32[128]{0:T(128)S(1)}, s32[128]{0:T(128)}, u32[]{:S(2)}) copy-start(s32[128]{0:T(128)} %param.11) | copy-start | bytes 1540
  68.0 6.4 %collective-permute-start.18 = (bf16[128,1024]{1,0:T(8,128)(2,1)S(1)}, bf16[128,1024]{1,0:T(8,128)(2,1)S(1)}, u32[]{:S(2)}, u32[]{:S(2)}) collective-permute-start(bf16[128,1024]{1,0:T(8,128)(2,1)S(1)} %pad_maximum_fusion), channel_id=1, source_target_pairs={{0,2},{2,0},{4,6},{6,4},{8,10},{10,8},{12,14},{14,12},{1,3},{3,1},... | collective-permute-start | bytes 786440 | tf_op jit(solution)/shard_map/ppermute | solution.py:200
  74.7 1.1 %copy-start = (bf16[512,1024]{1,0:T(8,128)(2,1)}, bf16[512,1024]{1,0:T(8,128)(2,1)S(1)}, u32[]{:S(2)}) copy-start(bf16[512,1024]{1,0:T(8,128)(2,1)S(1)} %maximum_dynamic-update-slice_fusion) | copy-start | bytes 3145732

commit v6 on v5

--- a/solution.py
+++ b/solution.py
@@ -14,8 +14,7 @@
 WIDE = KIN * ROWS
 PAIR = 2 * KOUT
 DEPTH_BLOCK = 512
-AHEAD = 3
-VMEM_LIMIT = 40 * 1024 * 1024
+VMEM_LIMIT = 24 * 1024 * 1024
 NT = (((1,), (1,)), ((), ()))
 
 
@@ -71,128 +70,65 @@
     lax.fori_loop(0, count // (2 * ROWS), groups, 0, unroll=4)
 
 
-def store_copies(store_ref, store_vmem, sems, first):
-    blocks, columns, depth = store_vmem.shape
-    return [
-        pltpu.make_async_copy(
-            store_ref.at[0, pl.ds(first, columns), pl.ds(b * depth, depth)],
-            store_vmem.at[b],
-            sems.at[b],
-        )
-        for b in range(blocks)
-    ]
-
-
-def dots(pre_ref, store_vmem, copies, total_ref, out_ref):
-    depth = store_vmem.shape[2]
-    for b, copy in enumerate(copies):
-        copy.wait()
-        if b + AHEAD < len(copies):
-            copies[b + AHEAD].start()
+def precondition_kernel(rows_ref, left_ref, right_ref, pre_ref, half_ref):
+    precondition(rows_ref.at[0], left_ref[0], right_ref[0], half_ref, pre_ref)
+
+
+def dot_kernel(first, pre_ref, store_ref, out_ref, total_ref):
+    depth = pre_ref.shape[1]
+    columns = total_ref.shape[0]
+    for at in range(0, depth, DEPTH_BLOCK):
+        block = slice(at, at + DEPTH_BLOCK)
         term = lax.dot_general(
-            store_vmem[b],
-            pre_ref[:, b * depth : (b + 1) * depth],
+            store_ref[0, first : first + columns, block],
+            pre_ref[:, block],
             NT,
             preferred_element_type=jnp.float32,
         )
-        if b == 0:
+        if at == 0:
             total_ref[...] = term
-        elif b + 1 < len(copies):
+        elif at + DEPTH_BLOCK < depth:
             total_ref[...] += term
         else:
             out_ref[...] = (total_ref[...] + term).T
 
 
-def first_kernel(
-    first, rows_ref, left_ref, right_ref, store_ref, pre_ref, out_ref,
-    left_vmem, right_vmem, rows_vmem, half_ref, store_vmem, total_ref, head_sems, sems,
-):
-    heads = [
-        pltpu.make_async_copy(source.at[0], target, head_sems.at[k])
-        for k, (source, target) in enumerate(
-            ((right_ref, right_vmem), (left_ref, left_vmem), (rows_ref, rows_vmem))
-        )
-    ]
-    for copy in heads:
-        copy.start()
-    copies = store_copies(store_ref, store_vmem, sems, first)
-    for copy in copies[:AHEAD]:
-        copy.start()
-    for copy in heads:
-        copy.wait()
-    precondition(rows_vmem, left_vmem[...], right_vmem[...], half_ref, pre_ref)
-    dots(pre_ref, store_vmem, copies, total_ref, out_ref)
-
-
-def dot_kernel(first, pre_ref, store_ref, out_ref, store_vmem, total_ref, sems):
-    copies = store_copies(store_ref, store_vmem, sems, first)
-    for copy in copies[:AHEAD]:
-        copy.start()
-    dots(pre_ref, store_vmem, copies, total_ref, out_ref)
-
-
-def in_hbm(array):
-    return pltpu.with_memory_space_constraint(array, pltpu.HBM)
-
-
-def scratch(count, columns, depth):
-    blocks = depth // DEPTH_BLOCK
-    return (
-        pltpu.VMEM((blocks, columns, DEPTH_BLOCK), jnp.bfloat16),
-        pltpu.VMEM((columns, count), jnp.float32),
-        pltpu.SemaphoreType.DMA((blocks,)),
-    )
-
-
-def precondition_and_score(queries, left_inv, right_inv, store, first, columns):
+def in_vmem(array):
+    return pltpu.with_memory_space_constraint(array, pltpu.VMEM)
+
+
+def preconditioned(queries, left_inv, right_inv):
     count, depth = queries.shape[1:]
-    store_vmem, total, sems = scratch(count, columns, depth)
     vmem = pl.BlockSpec(memory_space=pltpu.VMEM)
-    hbm = pl.BlockSpec(memory_space=pltpu.HBM)
     return pl.pallas_call(
-        functools.partial(first_kernel, first),
-        out_shape=(
-            jax.ShapeDtypeStruct((count, depth), jnp.bfloat16),
-            jax.ShapeDtypeStruct((count, columns), jnp.float32),
-        ),
-        in_specs=[hbm] * 4,
-        out_specs=(vmem, vmem),
-        scratch_shapes=[
-            pltpu.VMEM((KIN, KIN), jnp.bfloat16),
-            pltpu.VMEM((KOUT, KOUT), jnp.bfloat16),
-            pltpu.VMEM((count, depth), jnp.bfloat16),
-            pltpu.VMEM((count // ROWS, WIDE, KOUT), jnp.bfloat16),
-            store_vmem,
-            total,
-            pltpu.SemaphoreType.DMA((3,)),
-            sems,
-        ],
+        precondition_kernel,
+        out_shape=jax.ShapeDtypeStruct((count, depth), jnp.bfloat16),
+        in_specs=[vmem] * 3,
+        out_specs=vmem,
+        scratch_shapes=[pltpu.VMEM((count // ROWS, WIDE, KOUT), jnp.bfloat16)],
         compiler_params=pltpu.CompilerParams(vmem_limit_bytes=VMEM_LIMIT),
         cost_estimate=pl.CostEstimate(
-            flops=2 * count * depth * (columns + 1024),
-            bytes_accessed=2 * depth * (2 * count + columns),
-            transcendentals=0,
+            flops=2 * count * depth * 1024, bytes_accessed=4 * depth * count, transcendentals=0
         ),
-    )(*map(in_hbm, (queries, left_inv, right_inv, store)))
+    )(in_vmem(queries), left_inv, right_inv)
 
 
 def score(pre, store, first, columns):
     count, depth = pre.shape
     vmem = pl.BlockSpec(memory_space=pltpu.VMEM)
-    hbm = pl.BlockSpec(memory_space=pltpu.HBM)
     return pl.pallas_call(
         functools.partial(dot_kernel, first),
         out_shape=jax.ShapeDtypeStruct((count, columns), jnp.float32),
-        in_specs=[vmem, hbm],
+        in_specs=[vmem] * 2,
         out_specs=vmem,
-        scratch_shapes=scratch(count, columns, depth),
+        scratch_shapes=[pltpu.VMEM((columns, count), jnp.float32)],
         compiler_params=pltpu.CompilerParams(vmem_limit_bytes=VMEM_LIMIT),
         cost_estimate=pl.CostEstimate(
             flops=2 * count * depth * columns,
             bytes_accessed=2 * depth * (count + columns),
             transcendentals=0,
         ),
-    )(pre, in_hbm(store))
+    )(pre, store)
 
 
 def swap(block, bit):
@@ -283,8 +219,12 @@
     half = columns // 2
     ex_count = lax.axis_size("ex")
     position = lax.axis_index("ex")
-    pre, left_part = precondition_and_score(queries, left_inv, right_inv, store, 0, half)
-    parts = [(position, 0, left_part), (position, half, score(pre, store, half, columns - half))]
+    pre = preconditioned(queries, left_inv, right_inv)
+    store = in_vmem(store)
+    parts = [
+        (position, 0, score(pre, store, 0, half)),
+        (position, half, score(pre, store, half, columns - half)),
+    ]
     current = pre
     for step in range(1, ex_count):
         route = [((i - 1) % ex_count, i) for i in range(ex_count)]

time: 76.1 us -> 75.1 us (0.987)
  Pallas kernels: 19.8 us -> 8.89 us
  local copies, waits for them, and re-layouts: 0.31 us -> 10.1 us
    unnamed x6 -> x16, local copies, waits for them, and re-layouts: 0.02 us -> 9.82 us
    pallas_call x2 -> x3, Pallas kernels: 12.4 us -> 6.72 us  [score(): pl.pallas_call(functools.partial(dot_kernel, first), out_shape=jax.ShapeD...]
    pallas_call x1, Pallas kernels: 7.4 us -> 2.17 us  [preconditioned(): pl.pallas_call(precondition_kernel, out_shape=jax.ShapeDtypeStruct((count...]
  transfers between devices with their start and end apart: 19 -> 19, of which waited for: 12 -> 12; matrix products, arithmetic and copies ran while one was open for 1% -> 1% of each run, Pallas kernels for 16% -> 9%
where the time goes in v6:
time: 75.1 us; the launch traced here: 74.7 us
  starting transfers between devices  27.4 us (36%)
  waiting for transfers between devices  24.6 us (33%)
  local copies, waits for them, and re-layouts  10.1 us (13%)
  Pallas kernels  8.89 us (12%)
  other arithmetic  1.63 us (2%)
  matrix products  1.08 us (1%)
  between operations  0.99 us (1%)
    ppermute x18, starting transfers between devices, swap(): return lax.ppermute(block, 'layer', route)  26.9 us
    ppermute x18, waiting for transfers between devices, swap(): return lax.ppermute(block, 'layer', route)  24.6 us
    unnamed x16, local copies, waits for them, and re-layouts  9.82 us
    pallas_call x3, Pallas kernels, score(): pl.pallas_call(functools.partial(dot_kernel, first), out_shape=jax.ShapeD...  6.72 us
    pallas_call x1, Pallas kernels, preconditioned(): pl.pallas_call(precondition_kernel, out_shape=jax.ShapeDtypeStruct((count...  2.17 us
  transfers between devices with their start and end apart: 19, of which 12 were waited for; matrix products, arithmetic and copies ran while one was open for 1% of the time, Pallas kernels for 9%

profile of v6, /device:TPU:0, one launch (start us, length us, event | category | flops | bytes accessed | tf_op | source)
XLA Modules:
  0.0 74.7 jit_solution(8443072154130721730)
XLA Ops:
  0.6 0.0 copy-start.2
  0.6 1.6 %copy-done.2 = bf16[1,256,4096]{2,1,0:T(8,128)(2,1)S(1)} copy-done((bf16[1,256,4096]{2,1,0:T(8,128)(2,1)S(1)}, bf16[1,256,4096]{2,1,0:T(8,128)(2,1)}, u32[]{:S(2)}) %copy-start.2) | copy-done | bytes 2097176
  2.2 0.0 copy-start.3
  2.2 0.8 %copy-done.3 = bf16[1,128,128]{2,1,0:T(8,128)(2,1)S(1)} copy-done((bf16[1,128,128]{2,1,0:T(8,128)(2,1)S(1)}, bf16[1,128,128]{2,1,0:T(8,128)(2,1)}, u32[]{:S(2)}) %copy-start.3) | copy-done | bytes 32792
  3.0 0.0 copy-start.4
  3.0 0.7 copy-done.4
  3.7 2.2 %shard_map.77.pre_ref = bf16[256,4096]{1,0:T(8,128)(2,1)S(1)} custom-call(bf16[1,256,4096]{2,1,0:T(8,128)(2,1)S(1)} %copy-done.2, bf16[1,32,32]{2,1,0:T(8,128)(2,1)S(1)} %copy-done.4, bf16[1,128,128]{2,1,0:T(8,128)(2,1)S(1)} %copy-done.3), custom_call_target="tpu_custom_call" | custom-call | flops 2147483648 | bytes 4194304 | tf_op jit(solution)/shard_map/pallas_call | solution.py:103
  5.9 0.5 collective-permute-start.1
  6.4 0.0 copy-start
  6.4 3.4 %copy-done = bf16[1,1024,4096]{2,1,0:T(8,128)(2,1)S(1)} copy-done((bf16[1,1024,4096]{2,1,0:T(8,128)(2,1)S(1)}, bf16[1,1024,4096]{2,1,0:T(8,128)(2,1)}, u32[]{:S(2)}) %copy-start) | copy-done | bytes 8388632
  9.8 1.3 %shard_map.78 = f32[256,512]{1,0:T(8,128)S(1)} custom-call(bf16[256,4096]{1,0:T(8,128)(2,1)S(1)} %shard_map.77.pre_ref, bf16[1,1024,4096]{2,1,0:T(8,128)(2,1)S(1)} %copy-done), custom_call_target="tpu_custom_call" | custom-call | flops 1073741824 | bytes 6291456 | tf_op jit(solution)/shard_map/pallas_call | solution.py:119
  11.1 1.4 %shard_map.80 = f32[256,512]{1,0:T(8,128)S(1)} custom-call(bf16[256,4096]{1,0:T(8,128)(2,1)S(1)} %shard_map.77.pre_ref, bf16[1,1024,4096]{2,1,0:T(8,128)(2,1)S(1)} %copy-done), custom_call_target="tpu_custom_call" | custom-call | flops 1073741824 | bytes 6291456 | tf_op jit(solution)/shard_map/pallas_call | solution.py:119
  12.5 2.6 %collective-permute-start = (bf16[128,512]{1,0:T(8,128)(2,1)S(1)}, bf16[128,512]{1,0:T(8,128)(2,1)S(1)}, u32[]{:S(2)}, u32[]{:S(2)}) collective-permute-start(bf16[128,512]{1,0:T(8,128)(2,1)S(1)} %get-tuple-element.56), channel_id=1, source_target_pairs={{0,2},{2,0},{4,6},{6,4},{8,10},{10,8},{12,14},{14,12},{1,3},{3,1},... | collective-permute-start | bytes 393224 | tf_op jit(solution)/shard_map/ppermute | solution.py:136
  15.1 0.1 collective-permute-start.3
  15.2 0.0 collective-permute-done.1.pre_ref
  15.2 0.0 copy-start.1
  15.2 3.4 %copy-done.1 = bf16[1,1024,4096]{2,1,0:T(8,128)(2,1)S(1)} copy-done((bf16[1,1024,4096]{2,1,0:T(8,128)(2,1)S(1)}, bf16[1,1024,4096]{2,1,0:T(8,128)(2,1)}, u32[]{:S(2)}) %copy-start.1) | copy-done | bytes 8388632
  18.6 4.0 %shard_map.79 = f32[256,1024]{1,0:T(8,128)S(1)} custom-call(bf16[256,4096]{1,0:T(8,128)(2,1)} %collective-permute-done.1.pre_ref, bf16[1,1024,4096]{2,1,0:T(8,128)(2,1)S(1)} %copy-done.1), custom_call_target="tpu_custom_call" | custom-call | flops 2147483648 | bytes 10485760 | tf_op jit(solution)/shard_map/pallas_call | solution.py:119
  22.6 0.0 collective-permute-done
  22.6 0.0 collective-permute-done.3
  22.6 0.9 %convert_add_fusion.2 = f32[128,512]{1,0:T(8,128)S(1)} fusion(bf16[128,512]{1,0:T(8,128)(2,1)} %collective-permute-done.3, f32[256,512]{1,0:T(8,128)S(1)} %shard_map.80, s32[]{:T(128)S(6)} %select_n.157), kind=kLoop, calls=%fused_computation.12 | loop fusion | flops 131072 | bytes 655364 | tf_op jit(solution)/shard_map/add | solution.py:170
  23.6 2.1 %collective-permute-start.2 = (bf16[64,512]{1,0:T(8,128)(2,1)S(1)}, bf16[64,512]{1,0:T(8,128)(2,1)S(1)}, u32[]{:S(2)}, u32[]{:S(2)}) collective-permute-start(bf16[64,512]{1,0:T(8,128)(2,1)S(1)} %dynamic-slice_convert_fusion.6), channel_id=1, source_target_pairs={{0,4},{2,6},{4,0},{6,2},{8,12},{10,14},{12,8},{14,10},{1,5},{3,7},... | collective-permute-start | bytes 196616 | tf_op jit(solution)/shard_map/ppermute | solution.py:136
  25.7 0.1 collective-permute-start.7
  25.8 2.2 %collective-permute-done.2 = bf16[64,512]{1,0:T(8,128)(2,1)S(1)} collective-permute-done((bf16[64,512]{1,0:T(8,128)(2,1)S(1)}, bf16[64,512]{1,0:T(8,128)(2,1)S(1)}, u32[]{:S(2)}, u32[]{:S(2)}) %collective-permute-start.2) | collective-permute-done | bytes 65568 | tf_op jit(solution)/shard_map/ppermute | solution.py:136
  28.0 3.5 %collective-permute-start.4 = (bf16[32,512]{1,0:T(8,128)(2,1)S(1)}, bf16[32,512]{1,0:T(8,128)(2,1)S(1)}, u32[]{:S(2)}, u32[]{:S(2)}) collective-permute-start(bf16[32,512]{1,0:T(8,128)(2,1)S(1)} %dynamic-slice_convert_fusion.8), channel_id=1, source_target_pairs={{0,8},{2,10},{4,12},{6,14},{8,0},{10,2},{12,4},{14,6},{1,9},{3,11}... | collective-permute-start | bytes 98312 | tf_op jit(solution)/shard_map/ppermute | solution.py:136
  31.5 1.6 %collective-permute-start.6 = (bf16[128,1024]{1,0:T(8,128)(2,1)S(1)}, bf16[128,1024]{1,0:T(8,128)(2,1)S(1)}, u32[]{:S(2)}, u32[]{:S(2)}) collective-permute-start(bf16[128,1024]{1,0:T(8,128)(2,1)S(1)} %dynamic-slice_convert_fusion), channel_id=1, source_target_pairs={{0,2},{2,0},{4,6},{6,4},{8,10},{10,8},{12,14},{14,12},{1,3},{3,1},... | collective-permute-start | bytes 786440 | tf_op jit(solution)/shard_map/ppermute | solution.py:136
  33.1 0.3 collective-permute-done.4
  33.4 0.0 collective-permute-done.7
  33.4 3.0 %collective-permute-start.5 = (bf16[32,512]{1,0:T(8,128)(2,1)S(1)}, bf16[32,512]{1,0:T(8,128)(2,1)S(1)}, u32[]{:S(2)}, u32[]{:S(2)}) collective-permute-start(bf16[32,512]{1,0:T(8,128)(2,1)S(1)} %add_convert_fusion.2), channel_id=1, source_target_pairs={{0,8},{2,10},{4,12},{6,14},{8,0},{10,2},{12,4},{14,6},{1,9},{3,11}... | collective-permute-start | bytes 98312 | tf_op jit(solution)/shard_map/ppermute | solution.py:136
  36.4 0.1 collective-permute-start.9
  36.5 1.4 %collective-permute-done.6 = bf16[128,1024]{1,0:T(8,128)(2,1)S(1)} collective-permute-done((bf16[128,1024]{1,0:T(8,128)(2,1)S(1)}, bf16[128,1024]{1,0:T(8,128)(2,1)S(1)}, u32[]{:S(2)}, u32[]{:S(2)}) %collective-permute-start.6) | collective-permute-done | bytes 262176 | tf_op jit(solution)/shard_map/ppermute | solution.py:136
  37.9 0.3 collective-permute-done.5
  38.3 3.2 %collective-permute-done.9 = bf16[32,512]{1,0:T(8,128)(2,1)S(1)} collective-permute-done((bf16[32,512]{1,0:T(8,128)(2,1)S(1)}, bf16[32,512]{1,0:T(8,128)(2,1)S(1)}, u32[]{:S(2)}, u32[]{:S(2)}) %collective-permute-start.9) | collective-permute-done | bytes 32800 | tf_op jit(solution)/shard_map/ppermute | solution.py:136
  41.5 0.5 collective-permute-start.10
  42.1 0.1 convert_add_fusion
  42.2 2.5 %collective-permute-start.12 = (bf16[64,1024]{1,0:T(8,128)(2,1)S(1)}, bf16[64,1024]{1,0:T(8,128)(2,1)S(1)}, u32[]{:S(2)}, u32[]{:S(2)}) collective-permute-start(bf16[64,1024]{1,0:T(8,128)(2,1)S(1)} %dynamic-slice_convert_fusion.1), channel_id=1, source_target_pairs={{0,4},{2,6},{4,0},{6,2},{8,12},{10,14},{12,8},{14,10},{1,5},{3,7},... | collective-permute-start | bytes 393224 | tf_op jit(solution)/shard_map/ppermute | solution.py:136
  44.7 0.1 collective-permute-start.8
  44.8 1.6 %collective-permute-done.10 = bf16[32,512]{1,0:T(8,128)(2,1)S(1)} collective-permute-done((bf16[32,512]{1,0:T(8,128)(2,1)S(1)}, bf16[32,512]{1,0:T(8,128)(2,1)S(1)}, u32[]{:S(2)}, u32[]{:S(2)}) %collective-permute-start.10) | collective-permute-done | bytes 32800 | tf_op jit(solution)/shard_map/ppermute | solution.py:136
  46.4 2.0 %collective-permute-start.14 = (bf16[64,512]{1,0:T(8,128)(2,1)S(1)}, bf16[64,512]{1,0:T(8,128)(2,1)S(1)}, u32[]{:S(2)}, u32[]{:S(2)}) collective-permute-start(bf16[64,512]{1,0:T(8,128)(2,1)S(1)} %pad_maximum_fusion.5), channel_id=1, source_target_pairs={{0,4},{2,6},{4,0},{6,2},{8,12},{10,14},{12,8},{14,10},{1,5},{3,7},... | collective-permute-start | bytes 196616 | tf_op jit(solution)/shard_map/ppermute | solution.py:136
  48.4 1.3 %collective-permute-done.8 = bf16[64,512]{1,0:T(8,128)(2,1)S(1)} collective-permute-done((bf16[64,512]{1,0:T(8,128)(2,1)S(1)}, bf16[64,512]{1,0:T(8,128)(2,1)S(1)}, u32[]{:S(2)}, u32[]{:S(2)}) %collective-permute-start.8) | collective-permute-done | bytes 65568 | tf_op jit(solution)/shard_map/ppermute | solution.py:136
  49.8 1.4 %collective-permute-start.11 = (bf16[128,512]{1,0:T(8,128)(2,1)S(1)}, bf16[128,512]{1,0:T(8,128)(2,1)S(1)}, u32[]{:S(2)}, u32[]{:S(2)}) collective-permute-start(bf16[128,512]{1,0:T(8,128)(2,1)S(1)} %pad_maximum_fusion.1), channel_id=1, source_target_pairs={{0,2},{2,0},{4,6},{6,4},{8,10},{10,8},{12,14},{14,12},{1,3},{3,1},... | collective-permute-start | bytes 393224 | tf_op jit(solution)/shard_map/ppermute | solution.py:136
  51.2 0.0 collective-permute-done.12
  51.2 0.0 collective-permute-done.14
  51.3 2.0 %collective-permute-start.13 = (bf16[32,1024]{1,0:T(8,128)(2,1)S(1)}, bf16[32,1024]{1,0:T(8,128)(2,1)S(1)}, u32[]{:S(2)}, u32[]{:S(2)}) collective-permute-start(bf16[32,1024]{1,0:T(8,128)(2,1)S(1)} %dynamic-slice_convert_fusion.4), channel_id=1, source_target_pairs={{0,8},{2,10},{4,12},{6,14},{8,0},{10,2},{12,4},{14,6},{1,9},{3,11}... | collective-permute-start | bytes 196616 | tf_op jit(solution)/shard_map/ppermute | solution.py:136
  53.3 3.2 %collective-permute-done.13 = bf16[32,1024]{1,0:T(8,128)(2,1)S(1)} collective-permute-done((bf16[32,1024]{1,0:T(8,128)(2,1)S(1)}, bf16[32,1024]{1,0:T(8,128)(2,1)S(1)}, u32[]{:S(2)}, u32[]{:S(2)}) %collective-permute-start.13) | collective-permute-done | bytes 65568 | tf_op jit(solution)/shard_map/ppermute | solution.py:136
  56.6 2.1 %collective-permute-start.16 = (bf16[32,1024]{1,0:T(8,128)(2,1)S(1)}, bf16[32,1024]{1,0:T(8,128)(2,1)S(1)}, u32[]{:S(2)}, u32[]{:S(2)}) collective-permute-start(bf16[32,1024]{1,0:T(8,128)(2,1)S(1)} %add_convert_fusion), channel_id=1, source_target_pairs={{0,8},{2,10},{4,12},{6,14},{8,0},{10,2},{12,4},{14,6},{1,9},{3,11}... | collective-permute-start | bytes 196616 | tf_op jit(solution)/shard_map/ppermute | solution.py:136
  58.7 0.6 collective-permute-start.15
  59.3 0.0 collective-permute-done.11
  59.3 2.5 %collective-permute-done.16 = bf16[32,1024]{1,0:T(8,128)(2,1)S(1)} collective-permute-done((bf16[32,1024]{1,0:T(8,128)(2,1)S(1)}, bf16[32,1024]{1,0:T(8,128)(2,1)S(1)}, u32[]{:S(2)}, u32[]{:S(2)}) %collective-permute-start.16) | collective-permute-done | bytes 65568 | tf_op jit(solution)/shard_map/ppermute | solution.py:136
  61.8 1.5 %collective-permute-start.17 = (bf16[64,1024]{1,0:T(8,128)(2,1)S(1)}, bf16[64,1024]{1,0:T(8,128)(2,1)S(1)}, u32[]{:S(2)}, u32[]{:S(2)}) collective-permute-start(bf16[64,1024]{1,0:T(8,128)(2,1)S(1)} %pad_maximum_fusion.3), channel_id=1, source_target_pairs={{0,4},{2,6},{4,0},{6,2},{8,12},{10,14},{12,8},{14,10},{1,5},{3,7},... | collective-permute-start | bytes 393224 | tf_op jit(solution)/shard_map/ppermute | solution.py:136
  63.4 0.1 broadcast_in_dim.2
  63.5 0.0 copy-start.6
  63.6 0.0 copy-start.7
  63.6 1.1 %collective-permute-done.15 = bf16[128,512]{1,0:T(8,128)(2,1)S(1)} collective-permute-done((bf16[128,512]{1,0:T(8,128)(2,1)S(1)}, bf16[128,512]{1,0:T(8,128)(2,1)S(1)}, u32[]{:S(2)}, u32[]{:S(2)}) %collective-permute-start.15) | collective-permute-done | bytes 131104 | tf_op jit(solution)/shard_map/ppermute | solution.py:136
  64.7 2.2 %collective-permute-done.17 = bf16[64,1024]{1,0:T(8,128)(2,1)S(1)} collective-permute-done((bf16[64,1024]{1,0:T(8,128)(2,1)S(1)}, bf16[64,1024]{1,0:T(8,128)(2,1)S(1)}, u32[]{:S(2)}, u32[]{:S(2)}) %collective-permute-start.17) | collective-permute-done | bytes 131104 | tf_op jit(solution)/shard_map/ppermute | solution.py:136
  66.9 1.1 %collective-permute-start.18 = (bf16[128,1024]{1,0:T(8,128)(2,1)S(1)}, bf16[128,1024]{1,0:T(8,128)(2,1)S(1)}, u32[]{:S(2)}, u32[]{:S(2)}) collective-permute-start(bf16[128,1024]{1,0:T(8,128)(2,1)S(1)} %pad_maximum_fusion), channel_id=1, source_target_pairs={{0,2},{2,0},{4,6},{6,4},{8,10},{10,8},{12,14},{14,12},{1,3},{3,1},... | collective-permute-start | bytes 786440 | tf_op jit(solution)/shard_map/ppermute | solution.py:136
  68.2 5.2 %collective-permute-done.18 = bf16[128,1024]{1,0:T(8,128)(2,1)S(1)} collective-permute-done((bf16[128,1024]{1,0:T(8,128)(2,1)S(1)}, bf16[128,1024]{1,0:T(8,128)(2,1)S(1)}, u32[]{:S(2)}, u32[]{:S(2)}) %collective-permute-start.18) | collective-permute-done | bytes 262176 | tf_op jit(solution)/shard_map/ppermute | solution.py:136
  73.4 0.1 broadcast_select_fusion.1
  73.6 0.0 copy-done.6
  73.6 0.0 copy-done.7
  73.6 0.0 copy-start.5
  73.6 1.1 %convolution_convert_fusion = bf16[128,1024]{1,0:T(8,128)(2,1)} fusion(bf16[512,1024]{1,0:T(8,128)(2,1)S(1)} %maximum_dynamic-update-slice_fusion, s32[512]{0:T(512)S(1)} %copy-done.6, s32[128]{0:T(128)S(1)} %copy-done.7), kind=kOutput, calls=%fused_computation | convolution fusion | flops 134742016 | bytes 1313280 | tf_op jit(solution)/shard_map/dot_general | solution.py:247
  74.7 0.0 copy-done.5
  (32 shorter events, 0.7 us)
Async XLA Ops:
  0.6 1.6 %copy-start.2 = (bf16[1,256,4096]{2,1,0:T(8,128)(2,1)S(1)}, bf16[1,256,4096]{2,1,0:T(8,128)(2,1)}, u32[]{:S(2)}) copy-start(bf16[1,256,4096]{2,1,0:T(8,128)(2,1)} %rows_ref.1) | copy-start | bytes 6291460
  2.2 0.8 %copy-start.3 = (bf16[1,128,128]{2,1,0:T(8,128)(2,1)S(1)}, bf16[1,128,128]{2,1,0:T(8,128)(2,1)}, u32[]{:S(2)}) copy-start(bf16[1,128,128]{2,1,0:T(8,128)(2,1)} %right_ref.1) | copy-start | bytes 98308
  3.0 0.7 copy-start.4
  5.9 9.3 %collective-permute-start.1 = (bf16[256,4096]{1,0:T(8,128)(2,1)S(1)}, bf16[256,4096]{1,0:T(8,128)(2,1)}, u32[]{:S(2)}, u32[]{:S(2)}) collective-permute-start(bf16[256,4096]{1,0:T(8,128)(2,1)S(1)} %shard_map.77.pre_ref), channel_id=1, source_target_pairs={{1,0},{0,1},{3,2},{2,3},{5,4},{4,5},{7,6},{6,7},{9,8},{8,9},{11,10... | collective-permute-start | bytes 6291464 | tf_op jit(solution)/shard_map/ppermute | solution.py:231
  6.4 3.4 %copy-start = (bf16[1,1024,4096]{2,1,0:T(8,128)(2,1)S(1)}, bf16[1,1024,4096]{2,1,0:T(8,128)(2,1)}, u32[]{:S(2)}) copy-start(bf16[1,1024,4096]{2,1,0:T(8,128)(2,1)} %store_ref.5) | copy-start | bytes 25165828
  12.5 10.1 %collective-permute-start = (bf16[128,512]{1,0:T(8,128)(2,1)S(1)}, bf16[128,512]{1,0:T(8,128)(2,1)S(1)}, u32[]{:S(2)}, u32[]{:S(2)}) collective-permute-start(bf16[128,512]{1,0:T(8,128)(2,1)S(1)} %get-tuple-element.56), channel_id=1, source_target_pairs={{0,2},{2,0},{4,6},{6,4},{8,10},{10,8},{12,14},{14,12},{1,3},{3,1},... | collective-permute-start | bytes 393224 | tf_op jit(solution)/shard_map/ppermute | solution.py:136
  15.1 7.5 %collective-permute-start.3 = (bf16[128,512]{1,0:T(8,128)(2,1)S(1)}, bf16[128,512]{1,0:T(8,128)(2,1)}, u32[]{:S(2)}, u32[]{:S(2)}) collective-permute-start(bf16[128,512]{1,0:T(8,128)(2,1)S(1)} %get-tuple-element.61), channel_id=1, source_target_pairs={{0,2},{2,0},{4,6},{6,4},{8,10},{10,8},{12,14},{14,12},{1,3},{3,1},... | collective-permute-start | bytes 393224 | tf_op jit(solution)/shard_map/ppermute | solution.py:136
  15.2 3.4 %copy-start.1 = (bf16[1,1024,4096]{2,1,0:T(8,128)(2,1)S(1)}, bf16[1,1024,4096]{2,1,0:T(8,128)(2,1)}, u32[]{:S(2)}) copy-start(bf16[1,1024,4096]{2,1,0:T(8,128)(2,1)} %store_ref.5) | copy-start | bytes 25165828
  23.6 4.3 %collective-permute-start.2 = (bf16[64,512]{1,0:T(8,128)(2,1)S(1)}, bf16[64,512]{1,0:T(8,128)(2,1)S(1)}, u32[]{:S(2)}, u32[]{:S(2)}) collective-permute-start(bf16[64,512]{1,0:T(8,128)(2,1)S(1)} %dynamic-slice_convert_fusion.6), channel_id=1, source_target_pairs={{0,4},{2,6},{4,0},{6,2},{8,12},{10,14},{12,8},{14,10},{1,5},{3,7},... | collective-permute-start | bytes 196616 | tf_op jit(solution)/shard_map/ppermute | solution.py:136
  25.7 7.6 %collective-permute-start.7 = (bf16[64,512]{1,0:T(8,128)(2,1)S(1)}, bf16[64,512]{1,0:T(8,128)(2,1)S(1)}, u32[]{:S(2)}, u32[]{:S(2)}) collective-permute-start(bf16[64,512]{1,0:T(8,128)(2,1)S(1)} %dynamic-slice_convert_fusion.5), channel_id=1, source_target_pairs={{0,4},{2,6},{4,0},{6,2},{8,12},{10,14},{12,8},{14,10},{1,5},{3,7},... | collective-permute-start | bytes 196616 | tf_op jit(solution)/shard_map/ppermute | solution.py:136
  28.0 5.3 %collective-permute-start.4 = (bf16[32,512]{1,0:T(8,128)(2,1)S(1)}, bf16[32,512]{1,0:T(8,128)(2,1)S(1)}, u32[]{:S(2)}, u32[]{:S(2)}) collective-permute-start(bf16[32,512]{1,0:T(8,128)(2,1)S(1)} %dynamic-slice_convert_fusion.8), channel_id=1, source_target_pairs={{0,8},{2,10},{4,12},{6,14},{8,0},{10,2},{12,4},{14,6},{1,9},{3,11}... | collective-permute-start | bytes 98312 | tf_op jit(solution)/shard_map/ppermute | solution.py:136
  31.5 6.4 %collective-permute-start.6 = (bf16[128,1024]{1,0:T(8,128)(2,1)S(1)}, bf16[128,1024]{1,0:T(8,128)(2,1)S(1)}, u32[]{:S(2)}, u32[]{:S(2)}) collective-permute-start(bf16[128,1024]{1,0:T(8,128)(2,1)S(1)} %dynamic-slice_convert_fusion), channel_id=1, source_target_pairs={{0,2},{2,0},{4,6},{6,4},{8,10},{10,8},{12,14},{14,12},{1,3},{3,1},... | collective-permute-start | bytes 786440 | tf_op jit(solution)/shard_map/ppermute | solution.py:136
  33.4 4.9 %collective-permute-start.5 = (bf16[32,512]{1,0:T(8,128)(2,1)S(1)}, bf16[32,512]{1,0:T(8,128)(2,1)S(1)}, u32[]{:S(2)}, u32[]{:S(2)}) collective-permute-start(bf16[32,512]{1,0:T(8,128)(2,1)S(1)} %add_convert_fusion.2), channel_id=1, source_target_pairs={{0,8},{2,10},{4,12},{6,14},{8,0},{10,2},{12,4},{14,6},{1,9},{3,11}... | collective-permute-start | bytes 98312 | tf_op jit(solution)/shard_map/ppermute | solution.py:136
  36.4 5.1 %collective-permute-start.9 = (bf16[32,512]{1,0:T(8,128)(2,1)S(1)}, bf16[32,512]{1,0:T(8,128)(2,1)S(1)}, u32[]{:S(2)}, u32[]{:S(2)}) collective-permute-start(bf16[32,512]{1,0:T(8,128)(2,1)S(1)} %dynamic-slice_convert_fusion.7), channel_id=1, source_target_pairs={{0,8},{2,10},{4,12},{6,14},{8,0},{10,2},{12,4},{14,6},{1,9},{3,11}... | collective-permute-start | bytes 98312 | tf_op jit(solution)/shard_map/ppermute | solution.py:136
  41.5 4.9 %collective-permute-start.10 = (bf16[32,512]{1,0:T(8,128)(2,1)S(1)}, bf16[32,512]{1,0:T(8,128)(2,1)S(1)}, u32[]{:S(2)}, u32[]{:S(2)}) collective-permute-start(bf16[32,512]{1,0:T(8,128)(2,1)S(1)} %add_convert_fusion.1), channel_id=1, source_target_pairs={{0,8},{2,10},{4,12},{6,14},{8,0},{10,2},{12,4},{14,6},{1,9},{3,11}... | collective-permute-start | bytes 98312 | tf_op jit(solution)/shard_map/ppermute | solution.py:136
  42.2 9.1 %collective-permute-start.12 = (bf16[64,1024]{1,0:T(8,128)(2,1)S(1)}, bf16[64,1024]{1,0:T(8,128)(2,1)S(1)}, u32[]{:S(2)}, u32[]{:S(2)}) collective-permute-start(bf16[64,1024]{1,0:T(8,128)(2,1)S(1)} %dynamic-slice_convert_fusion.1), channel_id=1, source_target_pairs={{0,4},{2,6},{4,0},{6,2},{8,12},{10,14},{12,8},{14,10},{1,5},{3,7},... | collective-permute-start | bytes 393224 | tf_op jit(solution)/shard_map/ppermute | solution.py:136
  44.7 5.0 %collective-permute-start.8 = (bf16[64,512]{1,0:T(8,128)(2,1)S(1)}, bf16[64,512]{1,0:T(8,128)(2,1)S(1)}, u32[]{:S(2)}, u32[]{:S(2)}) collective-permute-start(bf16[64,512]{1,0:T(8,128)(2,1)S(1)} %pad_maximum_fusion.4), channel_id=1, source_target_pairs={{0,4},{2,6},{4,0},{6,2},{8,12},{10,14},{12,8},{14,10},{1,5},{3,7},... | collective-permute-start | bytes 196616 | tf_op jit(solution)/shard_map/ppermute | solution.py:136
  46.4 4.8 %collective-permute-start.14 = (bf16[64,512]{1,0:T(8,128)(2,1)S(1)}, bf16[64,512]{1,0:T(8,128)(2,1)S(1)}, u32[]{:S(2)}, u32[]{:S(2)}) collective-permute-start(bf16[64,512]{1,0:T(8,128)(2,1)S(1)} %pad_maximum_fusion.5), channel_id=1, source_target_pairs={{0,4},{2,6},{4,0},{6,2},{8,12},{10,14},{12,8},{14,10},{1,5},{3,7},... | collective-permute-start | bytes 196616 | tf_op jit(solution)/shard_map/ppermute | solution.py:136
  49.8 9.5 %collective-permute-start.11 = (bf16[128,512]{1,0:T(8,128)(2,1)S(1)}, bf16[128,512]{1,0:T(8,128)(2,1)S(1)}, u32[]{:S(2)}, u32[]{:S(2)}) collective-permute-start(bf16[128,512]{1,0:T(8,128)(2,1)S(1)} %pad_maximum_fusion.1), channel_id=1, source_target_pairs={{0,2},{2,0},{4,6},{6,4},{8,10},{10,8},{12,14},{14,12},{1,3},{3,1},... | collective-permute-start | bytes 393224 | tf_op jit(solution)/shard_map/ppermute | solution.py:136
  51.3 5.3 %collective-permute-start.13 = (bf16[32,1024]{1,0:T(8,128)(2,1)S(1)}, bf16[32,1024]{1,0:T(8,128)(2,1)S(1)}, u32[]{:S(2)}, u32[]{:S(2)}) collective-permute-start(bf16[32,1024]{1,0:T(8,128)(2,1)S(1)} %dynamic-slice_convert_fusion.4), channel_id=1, source_target_pairs={{0,8},{2,10},{4,12},{6,14},{8,0},{10,2},{12,4},{14,6},{1,9},{3,11}... | collective-permute-start | bytes 196616 | tf_op jit(solution)/shard_map/ppermute | solution.py:136
  56.6 5.2 %collective-permute-start.16 = (bf16[32,1024]{1,0:T(8,128)(2,1)S(1)}, bf16[32,1024]{1,0:T(8,128)(2,1)S(1)}, u32[]{:S(2)}, u32[]{:S(2)}) collective-permute-start(bf16[32,1024]{1,0:T(8,128)(2,1)S(1)} %add_convert_fusion), channel_id=1, source_target_pairs={{0,8},{2,10},{4,12},{6,14},{8,0},{10,2},{12,4},{14,6},{1,9},{3,11}... | collective-permute-start | bytes 196616 | tf_op jit(solution)/shard_map/ppermute | solution.py:136
  58.7 6.0 %collective-permute-start.15 = (bf16[128,512]{1,0:T(8,128)(2,1)S(1)}, bf16[128,512]{1,0:T(8,128)(2,1)S(1)}, u32[]{:S(2)}, u32[]{:S(2)}) collective-permute-start(bf16[128,512]{1,0:T(8,128)(2,1)S(1)} %pad_maximum_fusion.2), channel_id=1, source_target_pairs={{0,2},{2,0},{4,6},{6,4},{8,10},{10,8},{12,14},{14,12},{1,3},{3,1},... | collective-permute-start | bytes 393224 | tf_op jit(solution)/shard_map/ppermute | solution.py:136
  61.8 5.0 %collective-permute-start.17 = (bf16[64,1024]{1,0:T(8,128)(2,1)S(1)}, bf16[64,1024]{1,0:T(8,128)(2,1)S(1)}, u32[]{:S(2)}, u32[]{:S(2)}) collective-permute-start(bf16[64,1024]{1,0:T(8,128)(2,1)S(1)} %pad_maximum_fusion.3), channel_id=1, source_target_pairs={{0,4},{2,6},{4,0},{6,2},{8,12},{10,14},{12,8},{14,10},{1,5},{3,7},... | collective-permute-start | bytes 393224 | tf_op jit(solution)/shard_map/ppermute | solution.py:136
  63.5 10.0 %copy-start.6 = (s32[512]{0:T(512)S(1)}, s32[512]{0:T(512)}, u32[]{:S(2)}) copy-start(s32[512]{0:T(512)} %param.10) | copy-start | bytes 6148
  63.6 10.0 %copy-start.7 = (s32[128]{0:T(128)S(1)}, s32[128]{0:T(128)}, u32[]{:S(2)}) copy-start(s32[128]{0:T(128)} %param.11) | copy-start | bytes 1540
  66.9 6.4 %collective-permute-start.18 = (bf16[128,1024]{1,0:T(8,128)(2,1)S(1)}, bf16[128,1024]{1,0:T(8,128)(2,1)S(1)}, u32[]{:S(2)}, u32[]{:S(2)}) collective-permute-start(bf16[128,1024]{1,0:T(8,128)(2,1)S(1)} %pad_maximum_fusion), channel_id=1, source_target_pairs={{0,2},{2,0},{4,6},{6,4},{8,10},{10,8},{12,14},{14,12},{1,3},{3,1},... | collective-permute-start | bytes 786440 | tf_op jit(solution)/shard_map/ppermute | solution.py:136
  73.6 1.1 %copy-start.5 = (bf16[512,1024]{1,0:T(8,128)(2,1)}, bf16[512,1024]{1,0:T(8,128)(2,1)S(1)}, u32[]{:S(2)}) copy-start(bf16[512,1024]{1,0:T(8,128)(2,1)S(1)} %maximum_dynamic-update-slice_fusion) | copy-start | bytes 3145732

commit v7 on v6

v7 whole, which is shorter than its diff:
```python
import functools

import jax
import jax.numpy as jnp
from jax import lax
from jax.experimental import pallas as pl
from jax.experimental.pallas import tpu as pltpu
from jax.sharding import PartitionSpec as P

KIN = 32
KOUT = 128
BEST = 4
ROWS = 8
WIDE = KIN * ROWS
PAIR = 2 * KOUT
DEPTH_BLOCK = 512
COLUMNS = 512
VMEM_LIMIT = 32 * 1024 * 1024
NT = (((1,), (1,)), ((), ()))


def left_matrix(left):
    row = lax.broadcasted_iota(jnp.int32, (WIDE, KIN), 0)
    column = lax.broadcasted_iota(jnp.int32, (WIDE, KIN), 1)
    spread = jnp.where((row >> 3) == column, 1.0, 0.0).astype(jnp.bfloat16)
    tall = jnp.dot(spread, left, preferred_element_type=jnp.float32).astype(jnp.bfloat16)
    full = lax.dot_general(tall, spread, NT, preferred_element_type=jnp.float32)
    row = lax.broadcasted_iota(jnp.int32, (WIDE, WIDE), 0)
    column = lax.broadcasted_iota(jnp.int32, (WIDE, WIDE), 1)
    return jnp.where((row & (ROWS - 1)) == (column & (ROWS - 1)), full, 0.0).astype(jnp.bfloat16)


def right_matrix(right):
    zero = jnp.zeros_like(right)
    return jnp.concatenate(
        [jnp.concatenate([right, zero], 1), jnp.concatenate([zero, right], 1)], 0
    )


def side_by_side_to_stacked(block):
    tiles = block.reshape(block.shape[0] // ROWS, ROWS, PAIR)
    return jnp.concatenate([tiles[:, :, :KOUT], tiles[:, :, KOUT:]], 1)


def precondition(rows_ref, left, right, half_ref, pre_ref):
    count = rows_ref.shape[0]
    both = right_matrix(right)
    together = 4
    for start in range(0, KIN // 2, together):
        block = jnp.concatenate(
            [rows_ref[:, p * PAIR : (p + 1) * PAIR] for p in range(start, start + together)], 0
        )
        half = jnp.dot(block, both, preferred_element_type=jnp.float32)
        for k in range(together):
            at = 2 * ROWS * (start + k)
            half_ref[:, at : at + 2 * ROWS, :] = side_by_side_to_stacked(
                half[k * count : (k + 1) * count]
            ).astype(jnp.bfloat16)
    mixer = left_matrix(left)

    def groups(index, carry):
        stacked = jnp.concatenate([half_ref[2 * index], half_ref[2 * index + 1]], 1)
        mixed = side_by_side_to_stacked(
            jnp.dot(mixer, stacked, preferred_element_type=jnp.float32)
        ).astype(jnp.bfloat16)
        at = pl.ds(pl.multiple_of(index * 2 * ROWS, 2 * ROWS), 2 * ROWS)
        for i in range(KIN):
            pre_ref[at, i * KOUT : (i + 1) * KOUT] = mixed[i]
        return carry

    lax.fori_loop(0, count // (2 * ROWS), groups, 0, unroll=4)


def dot(pre_ref, store_ref, first, total_ref, out_ref):
    depth = pre_ref.shape[1]
    columns = total_ref.shape[0]
    for at in range(0, depth, DEPTH_BLOCK):
        block = slice(at, at + DEPTH_BLOCK)
        term = lax.dot_general(
            store_ref[first : first + columns, block],
            pre_ref[:, block],
            NT,
            preferred_element_type=jnp.float32,
        )
        if at == 0:
            total_ref[...] = term
        elif at + DEPTH_BLOCK < depth:
            total_ref[...] += term
        else:
            out_ref[...] = (total_ref[...] + term).T


def first_kernel(
    rows_ref, left_ref, right_ref, store_ref, out_ref, pre_ref, store_vmem, rows_vmem,
    left_vmem, right_vmem, half_ref, total_ref, head_sems, sems,
):
    heads = [
        pltpu.make_async_copy(source.at[0], target, head_sems.at[k])
        for k, (source, target) in enumerate(
            ((right_ref, right_vmem), (left_ref, left_vmem), (rows_ref, rows_vmem))
        )
    ]
    columns = total_ref.shape[0]
    copies = [
        pltpu.make_async_copy(
            store_ref.at[0, pl.ds(first, columns)],
            store_vmem.at[pl.ds(first, columns)],
            sems.at[k],
        )
        for k, first in enumerate(range(0, store_vmem.shape[0], columns))
    ]
    for copy in heads + copies:
        copy.start()
    for copy in heads:
        copy.wait()
    precondition(rows_vmem, left_vmem[...], right_vmem[...], half_ref, pre_ref)
    copies[0].wait()
    dot(pre_ref, store_vmem, 0, total_ref, out_ref)
    for copy in copies[1:]:
        copy.wait()


def later_kernel(first, pre_ref, store_ref, out_ref, total_ref):
    dot(pre_ref, store_ref, first, total_ref, out_ref)


VMEM = pl.BlockSpec(memory_space=pltpu.VMEM)
HBM = pl.BlockSpec(memory_space=pltpu.HBM)


def in_hbm(array):
    return pltpu.with_memory_space_constraint(array, pltpu.HBM)


def first_scores(queries, left_inv, right_inv, store, columns):
    count, depth = queries.shape[1:]
    examples = store.shape[1]
    out, pre, store_vmem, _ = pl.pallas_call(
        first_kernel,
        out_shape=(
            pltpu.VMEM((count, columns), jnp.float32),
            pltpu.VMEM((count, depth), jnp.bfloat16),
            pltpu.VMEM((examples, depth), jnp.bfloat16),
            pltpu.VMEM((count, depth), jnp.bfloat16),
        ),
        in_specs=[HBM] * 4,
        out_specs=(VMEM,) * 4,
        scratch_shapes=[
            pltpu.VMEM((KIN, KIN), jnp.bfloat16),
            pltpu.VMEM((KOUT, KOUT), jnp.bfloat16),
            pltpu.VMEM((count // ROWS, WIDE, KOUT), jnp.bfloat16),
            pltpu.VMEM((columns, count), jnp.float32),
            pltpu.SemaphoreType.DMA((3,)),
            pltpu.SemaphoreType.DMA((examples // columns,)),
        ],
        compiler_params=pltpu.CompilerParams(vmem_limit_bytes=VMEM_LIMIT),
        cost_estimate=pl.CostEstimate(
            flops=2 * count * depth * (columns + 1024),
            bytes_accessed=2 * depth * (2 * count + examples),
            transcendentals=0,
        ),
    )(*map(in_hbm, (queries, left_inv, right_inv, store)))
    return out, pre, store_vmem


def later_scores(pre, store_vmem, first, columns):
    count, depth = pre.shape
    return pl.pallas_call(
        functools.partial(later_kernel, first),
        out_shape=pltpu.VMEM((count, columns), jnp.float32),
        in_specs=[VMEM] * 2,
        out_specs=VMEM,
        scratch_shapes=[pltpu.VMEM((columns, count), jnp.float32)],
        compiler_params=pltpu.CompilerParams(vmem_limit_bytes=VMEM_LIMIT),
        cost_estimate=pl.CostEstimate(
            flops=2 * count * depth * columns,
            bytes_accessed=2 * depth * (count + columns),
            transcendentals=0,
        ),
    )(pre, store_vmem)


def swap(block, bit):
    route = [(i, i ^ bit) for i in range(lax.axis_size("layer"))]
    return lax.ppermute(block, "layer", route)


HALVE, EXCHANGE, DOUBLE = range(3)


class LayerSum:
    def __init__(self, block, bits, index):
        self.block, self.index = block, index
        self.moves = [(bit, HALVE) for bit in bits[:-1]]
        self.moves += [(bit, EXCHANGE) for bit in bits[-1:]]
        self.moves += [(bit, DOUBLE) for bit in reversed(bits[:-1])]
        if len(bits) < 2:
            self.block = block.astype(jnp.bfloat16)

    def send(self, order):
        bit, kind = self.moves[0]
        sent = self.block
        if kind == HALVE:
            rows = self.block.shape[0] // 2
            upper = (self.index & bit) // bit
            sent = lax.dynamic_slice_in_dim(self.block, (1 - upper) * rows, rows, 0)
            sent = sent.astype(jnp.bfloat16)
            self.block = lax.dynamic_slice_in_dim(self.block, upper * rows, rows, 0)
        self.received = swap(order.after(sent), bit)

    def take(self, order):
        bit, kind = self.moves.pop(0)
        received = order.mark(self.received)
        mine = self.block
        if kind == DOUBLE:
            low = (self.index & bit) == 0
            self.block = jnp.concatenate(
                [jnp.where(low, mine, received), jnp.where(low, received, mine)], 0
            )
            return
        self.block = mine.astype(jnp.float32) + received.astype(jnp.float32)
        if not (self.moves and self.moves[0][1] == HALVE):
            self.block = self.block.astype(jnp.bfloat16)


class Order:
    def __init__(self):
        self.last = jnp.zeros((), jnp.float32)

    def after(self, value):
        value, _ = lax.optimization_barrier((value, self.last))
        return value

    def mark(self, value):
        value, self.last = lax.optimization_barrier((value, self.last))
        return value


STEP_US = 1.7
BYTES_PER_US = 50000


def step_times(size, bits):
    at, sent = 0.0, size
    sizes = []
    for _ in range(bits - 1):
        sent //= 2
        sizes.append(sent)
    for size in sizes + [sent] + sizes[::-1]:
        at += STEP_US + 2 * size / BYTES_PER_US
        yield at


def sum_layers(makers, bits, index):
    order = Order()
    chunks = {}
    events = []
    for number, (start, size, _) in enumerate(makers):
        events.append((start, number))
        events.extend((start + 2 + at, number) for at in step_times(size, len(bits)) if bits)
    for _, number in sorted(events):
        if number not in chunks:
            chunk = chunks[number] = LayerSum(makers[number][2](order), bits, index)
        else:
            chunk = chunks[number]
            chunk.take(order)
        if chunk.moves:
            chunk.send(order)
    return [chunks[number].block for number in range(len(makers))]


def shards(store, queries, left_inv, right_inv, query_prompt, winner):
    rows = queries.shape[1]
    columns = store.shape[1]
    width = min(COLUMNS, columns)
    ex_count = lax.axis_size("ex")
    position = lax.axis_index("ex")
    first_part, pre, store_vmem = first_scores(queries, left_inv, right_inv, store, width)
    places, makers = [], []
    current = pre
    for step in range(ex_count):
        if step > 0:
            route = [((i - 1) % ex_count, i) for i in range(ex_count)]
            current = lax.ppermute(current, "ex", route)
        for first in range(0, columns, width):

            def make(order, first=first, step=step, current=current):
                if step == 0 and first == 0:
                    return first_part
                return order.mark(later_scores(order.after(current), store_vmem, first, width))

            start = 4.5 + 4.5 * step + 1.5 * (first // width)
            makers.append((start, rows * width, make))
            places.append(((position - step) % ex_count * rows, jnp.int32(first)))
    count = lax.axis_size("layer")
    bits = [1 << k for k in range(count.bit_length() - 1)]
    done = sum_layers(makers, bits, lax.axis_index("layer"))
    scores = jnp.zeros((rows * ex_count, columns), jnp.bfloat16)
    for place, block in zip(places, done):
        scores = lax.dynamic_update_slice(scores, block, place)
    ids = jnp.arange(scores.shape[0], dtype=jnp.int32)
    prompts = jnp.arange(winner.shape[0], dtype=jnp.int32)
    picks = (winner[:, None] == ids[None, :]).astype(jnp.float32)
    member = (query_prompt[None, :] == prompts[:, None]).astype(jnp.float32)
    weights = (picks - member / BEST).astype(jnp.bfloat16)
    advantage = jnp.dot(weights, scores, preferred_element_type=jnp.float32)
    return (scores, advantage.astype(jnp.bfloat16))


def solution(mesh):
    return jax.shard_map(
        shards,
        mesh=mesh,
        in_specs=(
            P("layer", ("grp", "ex"), None),
            P("layer", ("grp", "ex"), None),
            P("layer", None, None),
            P("layer", None, None),
            P("grp"),
            P("grp"),
        ),
        out_specs=(P(None, ("grp", "ex")), P(None, ("grp", "ex"))),
        check_vma=False,
    )
```

time: 75.1 us -> 70.4 us (0.937)
  waiting for transfers between devices: 24.6 us -> 16.5 us
  Pallas kernels: 8.89 us -> 14.1 us
  starting transfers between devices: 27.4 us -> 25.8 us
  other arithmetic: 1.63 us -> 0.68 us
  local copies, waits for them, and re-layouts: 10.1 us -> 11 us
    ppermute x18 -> x20, waiting for transfers between devices: 24.6 us -> 16.5 us  [swap(): return lax.ppermute(block, 'layer', route)]
    pallas_call x4, Pallas kernels: 8.89 us -> 14.1 us  [the longest x1 8.48 us: first_scores(): pl.pallas_call(first_kernel, out_shape=(pltpu.VMEM((count, columns), jnp....]
    ppermute x18 -> x20, starting transfers between devices: 26.9 us -> 25.4 us  [swap(): return lax.ppermute(block, 'layer', route)]
    add x6 -> x3, other arithmetic: 1.1 us -> 0.13 us  [take(): self.block = mine.astype(jnp.float32) + received.astype(jnp.float32)]
    unnamed x16 -> x12, local copies, waits for them, and re-layouts: 9.82 us -> 10.1 us
  transfers between devices with their start and end apart: 19 -> 21, of which waited for: 12 -> 8; matrix products, arithmetic and copies ran while one was open for 1% -> 2% of each run, Pallas kernels for 9% -> 8%
where the time goes in v7:
time: 70.4 us; the launch traced here: 70.1 us
  starting transfers between devices  25.8 us (37%)
  waiting for transfers between devices  16.5 us (23%)
  Pallas kernels  14.1 us (20%)
  local copies, waits for them, and re-layouts  11 us (16%)
  matrix products  1.08 us (2%)
  between operations  0.96 us (1%)
    ppermute x20, starting transfers between devices, swap(): return lax.ppermute(block, 'layer', route)  25.4 us
    ppermute x20, waiting for transfers between devices, swap(): return lax.ppermute(block, 'layer', route)  16.5 us
    unnamed x12, local copies, waits for them, and re-layouts  10.1 us
    pallas_call x1, Pallas kernels, first_scores(): pl.pallas_call(first_kernel, out_shape=(pltpu.VMEM((count, columns), jnp....  8.48 us
    pallas_call x3, Pallas kernels, later_scores(): pl.pallas_call(functools.partial(later_kernel, first), out_shape=pltpu.VM...  5.63 us
  transfers between devices with their start and end apart: 21, of which 8 were waited for; matrix products, arithmetic and copies ran while one was open for 2% of the time, Pallas kernels for 8%

profile of v7, /device:TPU:0, one launch (start us, length us, event | category | flops | bytes accessed | tf_op | source)
XLA Modules:
  0.0 70.1 jit_solution(4935902322416462210)
XLA Ops:
  0.6 8.5 %shard_map.77 = (f32[256,512]{1,0:T(8,128)S(1)}, bf16[256,4096]{1,0:T(8,128)(2,1)}, bf16[1024,4096]{1,0:T(8,128)(2,1)S(1)}, bf16[256,4096]{1,0:T(8,128)(2,1)}) custom-call(bf16[1,256,4096]{2,1,0:T(8,128)(2,1)} %rows_ref.1, bf16[1,32,32]{2,1,0:T(8,128)(2,1)} %left_ref.1, bf16[1,128,128]{2,1,0:T(8,128)(2,1)} %right_ref.1, bf16[1,1024,4096]{2,1,0:T(8,128)(2,1)} %store_ref.1), custom_call_target="tpu_custom_call" | custom-call | flops 3221225472 | bytes 12582912 | tf_op jit(solution)/shard_map/pallas_call | solution.py:138
  9.1 0.0 copy-start
  9.1 3.3 %copy-done = bf16[1024,4096]{1,0:T(8,128)(2,1)} copy-done((bf16[1024,4096]{1,0:T(8,128)(2,1)}, bf16[1024,4096]{1,0:T(8,128)(2,1)S(1)}, u32[]{:S(2)}) %copy-start) | copy-done | bytes 8388632
  12.4 0.4 collective-permute-start.1
  12.9 2.6 %collective-permute-start = (bf16[128,512]{1,0:T(8,128)(2,1)S(1)}, bf16[128,512]{1,0:T(8,128)(2,1)S(1)}, u32[]{:S(2)}, u32[]{:S(2)}) collective-permute-start(bf16[128,512]{1,0:T(8,128)(2,1)S(1)} %dynamic-slice_convert_fusion.3), channel_id=1, source_target_pairs={{0,2},{2,0},{4,6},{6,4},{8,10},{10,8},{12,14},{14,12},{1,3},{3,1},... | collective-permute-start | bytes 393224 | tf_op jit(solution)/shard_map/ppermute | solution.py:185
  15.4 0.0 copy-start.1
  15.4 3.4 %copy-done.1 = bf16[1024,4096]{1,0:T(8,128)(2,1)S(1)} copy-done((bf16[1024,4096]{1,0:T(8,128)(2,1)S(1)}, bf16[1024,4096]{1,0:T(8,128)(2,1)}, u32[]{:S(2)}) %copy-start.1) | copy-done | bytes 8388632
  18.8 2.9 %shard_map.78 = f32[256,512]{1,0:T(8,128)S(1)} custom-call(bf16[256,4096]{1,0:T(8,128)(2,1)} %get-tuple-element.74.pre_ref, bf16[1024,4096]{1,0:T(8,128)(2,1)S(1)} %copy-done.1), custom_call_target="tpu_custom_call" | custom-call | flops 1073741824 | bytes 6291456 | tf_op jit(solution)/shard_map/pallas_call | solution.py:168
  21.8 0.7 dynamic-slice_convert_fusion.2
  22.5 0.0 collective-permute-start.3
  22.5 0.0 collective-permute-done.1.pre_ref
  22.5 0.0 copy-start.2
  22.5 3.4 %copy-done.2 = bf16[1024,4096]{1,0:T(8,128)(2,1)S(1)} copy-done((bf16[1024,4096]{1,0:T(8,128)(2,1)S(1)}, bf16[1024,4096]{1,0:T(8,128)(2,1)}, u32[]{:S(2)}) %copy-start.2) | copy-done | bytes 8388632
  25.9 1.3 %shard_map.79 = f32[256,512]{1,0:T(8,128)S(1)} custom-call(bf16[256,4096]{1,0:T(8,128)(2,1)S(1)} %collective-permute-done.1.pre_ref, bf16[1024,4096]{1,0:T(8,128)(2,1)S(1)} %copy-done.2), custom_call_target="tpu_custom_call" | custom-call | flops 1073741824 | bytes 6291456 | tf_op jit(solution)/shard_map/pallas_call | solution.py:168
  27.2 1.3 %shard_map.80 = f32[256,512]{1,0:T(8,128)S(1)} custom-call(bf16[256,4096]{1,0:T(8,128)(2,1)S(1)} %collective-permute-done.1.pre_ref, bf16[1024,4096]{1,0:T(8,128)(2,1)S(1)} %copy-done.2), custom_call_target="tpu_custom_call" | custom-call | flops 1073741824 | bytes 6291456 | tf_op jit(solution)/shard_map/pallas_call | solution.py:168
  28.6 0.0 collective-permute-done
  28.6 0.0 collective-permute-done.3
  28.6 0.1 convert_add_fusion.2
  28.7 2.1 %collective-permute-start.2 = (bf16[64,512]{1,0:T(8,128)(2,1)S(1)}, bf16[64,512]{1,0:T(8,128)(2,1)S(1)}, u32[]{:S(2)}, u32[]{:S(2)}) collective-permute-start(bf16[64,512]{1,0:T(8,128)(2,1)S(1)} %dynamic-slice_convert_fusion.7), channel_id=1, source_target_pairs={{0,4},{2,6},{4,0},{6,2},{8,12},{10,14},{12,8},{14,10},{1,5},{3,7},... | collective-permute-start | bytes 196616 | tf_op jit(solution)/shard_map/ppermute | solution.py:185
  30.9 1.6 %collective-permute-start.7 = (bf16[128,512]{1,0:T(8,128)(2,1)S(1)}, bf16[128,512]{1,0:T(8,128)(2,1)S(1)}, u32[]{:S(2)}, u32[]{:S(2)}) collective-permute-start(bf16[128,512]{1,0:T(8,128)(2,1)S(1)} %get-tuple-element.95), channel_id=1, source_target_pairs={{0,2},{2,0},{4,6},{6,4},{8,10},{10,8},{12,14},{14,12},{1,3},{3,1},... | collective-permute-start | bytes 393224 | tf_op jit(solution)/shard_map/ppermute | solution.py:185
  32.5 0.5 collective-permute-start.6
  33.0 0.1 collective-permute-start.5
  33.1 0.0 collective-permute-done.2
  33.1 3.1 %collective-permute-start.4 = (bf16[64,512]{1,0:T(8,128)(2,1)S(1)}, bf16[64,512]{1,0:T(8,128)(2,1)S(1)}, u32[]{:S(2)}, u32[]{:S(2)}) collective-permute-start(bf16[64,512]{1,0:T(8,128)(2,1)S(1)} %add_convert_fusion.7), channel_id=1, source_target_pairs={{0,8},{2,10},{4,12},{6,14},{8,0},{10,2},{12,4},{14,6},{1,9},{3,11}... | collective-permute-start | bytes 196616 | tf_op jit(solution)/shard_map/ppermute | solution.py:185
  36.2 1.1 %collective-permute-done.7 = bf16[128,512]{1,0:T(8,128)(2,1)S(1)} collective-permute-done((bf16[128,512]{1,0:T(8,128)(2,1)S(1)}, bf16[128,512]{1,0:T(8,128)(2,1)S(1)}, u32[]{:S(2)}, u32[]{:S(2)}) %collective-permute-start.7) | collective-permute-done | bytes 131104 | tf_op jit(solution)/shard_map/ppermute | solution.py:185
  37.4 0.7 %collective-permute-start.11 = (bf16[64,512]{1,0:T(8,128)(2,1)S(1)}, bf16[64,512]{1,0:T(8,128)(2,1)S(1)}, u32[]{:S(2)}, u32[]{:S(2)}) collective-permute-start(bf16[64,512]{1,0:T(8,128)(2,1)S(1)} %dynamic-slice_convert_fusion.4), channel_id=1, source_target_pairs={{0,4},{2,6},{4,0},{6,2},{8,12},{10,14},{12,8},{14,10},{1,5},{3,7},... | collective-permute-start | bytes 196616 | tf_op jit(solution)/shard_map/ppermute | solution.py:185
  38.1 0.0 collective-permute-done.6
  38.1 0.7 collective-permute-done.5
  38.8 0.0 collective-permute-done.4
  38.8 2.7 %collective-permute-start.10 = (bf16[64,512]{1,0:T(8,128)(2,1)S(1)}, bf16[64,512]{1,0:T(8,128)(2,1)S(1)}, u32[]{:S(2)}, u32[]{:S(2)}) collective-permute-start(bf16[64,512]{1,0:T(8,128)(2,1)S(1)} %add_convert_fusion.5), channel_id=1, source_target_pairs={{0,8},{2,10},{4,12},{6,14},{8,0},{10,2},{12,4},{14,6},{1,9},{3,11}... | collective-permute-start | bytes 196616 | tf_op jit(solution)/shard_map/ppermute | solution.py:185
  41.5 2.2 %collective-permute-start.9 = (bf16[64,512]{1,0:T(8,128)(2,1)S(1)}, bf16[64,512]{1,0:T(8,128)(2,1)S(1)}, u32[]{:S(2)}, u32[]{:S(2)}) collective-permute-start(bf16[64,512]{1,0:T(8,128)(2,1)S(1)} %dynamic-slice_convert_fusion.5), channel_id=1, source_target_pairs={{0,4},{2,6},{4,0},{6,2},{8,12},{10,14},{12,8},{14,10},{1,5},{3,7},... | collective-permute-start | bytes 196616 | tf_op jit(solution)/shard_map/ppermute | solution.py:185
  43.7 0.1 collective-permute-start.8
  43.8 0.0 collective-permute-done.11
  43.9 1.2 %collective-permute-start.15 = (bf16[64,512]{1,0:T(8,128)(2,1)S(1)}, bf16[64,512]{1,0:T(8,128)(2,1)S(1)}, u32[]{:S(2)}, u32[]{:S(2)}) collective-permute-start(bf16[64,512]{1,0:T(8,128)(2,1)S(1)} %add_convert_fusion.2), channel_id=1, source_target_pairs={{0,8},{2,10},{4,12},{6,14},{8,0},{10,2},{12,4},{14,6},{1,9},{3,11}... | collective-permute-start | bytes 196616 | tf_op jit(solution)/shard_map/ppermute | solution.py:185
  45.0 0.0 collective-permute-done.10
  45.0 1.4 %collective-permute-done.9 = bf16[64,512]{1,0:T(8,128)(2,1)S(1)} collective-permute-done((bf16[64,512]{1,0:T(8,128)(2,1)S(1)}, bf16[64,512]{1,0:T(8,128)(2,1)S(1)}, u32[]{:S(2)}, u32[]{:S(2)}) %collective-permute-start.9) | collective-permute-done | bytes 65568 | tf_op jit(solution)/shard_map/ppermute | solution.py:185
  46.4 3.5 %collective-permute-done.8 = bf16[64,512]{1,0:T(8,128)(2,1)S(1)} collective-permute-done((bf16[64,512]{1,0:T(8,128)(2,1)S(1)}, bf16[64,512]{1,0:T(8,128)(2,1)S(1)}, u32[]{:S(2)}, u32[]{:S(2)}) %collective-permute-start.8) | collective-permute-done | bytes 65568 | tf_op jit(solution)/shard_map/ppermute | solution.py:185
  49.9 0.1 collective-permute-start.14
  50.0 0.1 collective-permute-start.13
  50.2 1.9 %collective-permute-start.12 = (bf16[128,512]{1,0:T(8,128)(2,1)S(1)}, bf16[128,512]{1,0:T(8,128)(2,1)S(1)}, u32[]{:S(2)}, u32[]{:S(2)}) collective-permute-start(bf16[128,512]{1,0:T(8,128)(2,1)S(1)} %pad_maximum_fusion), channel_id=1, source_target_pairs={{0,2},{2,0},{4,6},{6,4},{8,10},{10,8},{12,14},{14,12},{1,3},{3,1},... | collective-permute-start | bytes 393224 | tf_op jit(solution)/shard_map/ppermute | solution.py:185
  52.1 0.0 collective-permute-done.15
  52.1 3.3 %collective-permute-done.14 = bf16[64,512]{1,0:T(8,128)(2,1)S(1)} collective-permute-done((bf16[64,512]{1,0:T(8,128)(2,1)S(1)}, bf16[64,512]{1,0:T(8,128)(2,1)S(1)}, u32[]{:S(2)}, u32[]{:S(2)}) %collective-permute-start.14) | collective-permute-done | bytes 65568 | tf_op jit(solution)/shard_map/ppermute | solution.py:185
  55.5 0.0 collective-permute-done.13
  55.5 1.9 %collective-permute-start.19 = (bf16[64,512]{1,0:T(8,128)(2,1)S(1)}, bf16[64,512]{1,0:T(8,128)(2,1)S(1)}, u32[]{:S(2)}, u32[]{:S(2)}) collective-permute-start(bf16[64,512]{1,0:T(8,128)(2,1)S(1)} %add_convert_fusion), channel_id=1, source_target_pairs={{0,4},{2,6},{4,0},{6,2},{8,12},{10,14},{12,8},{14,10},{1,5},{3,7},... | collective-permute-start | bytes 196616 | tf_op jit(solution)/shard_map/ppermute | solution.py:185
  57.4 0.3 collective-permute-start.17
  57.7 1.7 %collective-permute-start.16 = (bf16[128,512]{1,0:T(8,128)(2,1)S(1)}, bf16[128,512]{1,0:T(8,128)(2,1)S(1)}, u32[]{:S(2)}, u32[]{:S(2)}) collective-permute-start(bf16[128,512]{1,0:T(8,128)(2,1)S(1)} %pad_maximum_fusion.1), channel_id=1, source_target_pairs={{0,2},{2,0},{4,6},{6,4},{8,10},{10,8},{12,14},{14,12},{1,3},{3,1},... | collective-permute-start | bytes 393224 | tf_op jit(solution)/shard_map/ppermute | solution.py:185
  59.4 0.0 collective-permute-done.12
  59.4 2.3 %collective-permute-done.17 = bf16[64,512]{1,0:T(8,128)(2,1)S(1)} collective-permute-done((bf16[64,512]{1,0:T(8,128)(2,1)S(1)}, bf16[64,512]{1,0:T(8,128)(2,1)S(1)}, u32[]{:S(2)}, u32[]{:S(2)}) %collective-permute-start.17) | collective-permute-done | bytes 65568 | tf_op jit(solution)/shard_map/ppermute | solution.py:185
  61.7 1.9 %collective-permute-start.18 = (bf16[128,512]{1,0:T(8,128)(2,1)S(1)}, bf16[128,512]{1,0:T(8,128)(2,1)S(1)}, u32[]{:S(2)}, u32[]{:S(2)}) collective-permute-start(bf16[128,512]{1,0:T(8,128)(2,1)S(1)} %pad_maximum_fusion.2), channel_id=1, source_target_pairs={{0,2},{2,0},{4,6},{6,4},{8,10},{10,8},{12,14},{14,12},{1,3},{3,1},... | collective-permute-start | bytes 393224 | tf_op jit(solution)/shard_map/ppermute | solution.py:185
  63.7 0.1 broadcast_in_dim.2
  63.8 0.0 copy-start.4
  63.8 0.0 copy-start.5
  63.9 0.0 collective-permute-done.16
  63.9 0.0 collective-permute-done.19
  63.9 0.7 %collective-permute-start.20 = (bf16[128,512]{1,0:T(8,128)(2,1)S(1)}, bf16[128,512]{1,0:T(8,128)(2,1)S(1)}, u32[]{:S(2)}, u32[]{:S(2)}) collective-permute-start(bf16[128,512]{1,0:T(8,128)(2,1)S(1)} %pad_maximum_fusion.3), channel_id=1, source_target_pairs={{0,2},{2,0},{4,6},{6,4},{8,10},{10,8},{12,14},{14,12},{1,3},{3,1},... | collective-permute-start | bytes 393224 | tf_op jit(solution)/shard_map/ppermute | solution.py:185
  64.7 2.1 %collective-permute-done.18 = bf16[128,512]{1,0:T(8,128)(2,1)S(1)} collective-permute-done((bf16[128,512]{1,0:T(8,128)(2,1)S(1)}, bf16[128,512]{1,0:T(8,128)(2,1)S(1)}, u32[]{:S(2)}, u32[]{:S(2)}) %collective-permute-start.18) | collective-permute-done | bytes 131104 | tf_op jit(solution)/shard_map/ppermute | solution.py:185
  66.9 2.1 %collective-permute-done.20 = bf16[128,512]{1,0:T(8,128)(2,1)S(1)} collective-permute-done((bf16[128,512]{1,0:T(8,128)(2,1)S(1)}, bf16[128,512]{1,0:T(8,128)(2,1)S(1)}, u32[]{:S(2)}, u32[]{:S(2)}) %collective-permute-start.20) | collective-permute-done | bytes 131104 | tf_op jit(solution)/shard_map/ppermute | solution.py:185
  69.0 0.0 copy-done.4
  69.0 0.0 copy-done.5
  69.1 0.0 copy-start.3
  69.1 1.1 %convolution_convert_fusion = bf16[128,1024]{1,0:T(8,128)(2,1)} fusion(bf16[512,1024]{1,0:T(8,128)(2,1)S(1)} %maximum_dynamic-update-slice_fusion.3, s32[512]{0:T(512)S(1)} %copy-done.4, s32[128]{0:T(128)S(1)} %copy-done.5), kind=kOutput, calls=%fused_computation | convolution fusion | flops 134742016 | bytes 1313280 | tf_op jit(solution)/shard_map/dot_general | solution.py:306
  70.1 0.0 copy-done.3
  (32 shorter events, 0.7 us)
Async XLA Ops:
  9.1 3.3 %copy-start = (bf16[1024,4096]{1,0:T(8,128)(2,1)}, bf16[1024,4096]{1,0:T(8,128)(2,1)S(1)}, u32[]{:S(2)}) copy-start(bf16[1024,4096]{1,0:T(8,128)(2,1)S(1)} %get-tuple-element.75.store_ref) | copy-start | bytes 25165828
  12.4 10.1 %collective-permute-start.1 = (bf16[256,4096]{1,0:T(8,128)(2,1)}, bf16[256,4096]{1,0:T(8,128)(2,1)S(1)}, u32[]{:S(2)}, u32[]{:S(2)}) collective-permute-start(bf16[256,4096]{1,0:T(8,128)(2,1)} %get-tuple-element.74.pre_ref), channel_id=1, source_target_pairs={{1,0},{0,1},{3,2},{2,3},{5,4},{4,5},{7,6},{6,7},{9,8},{8,9},{11,10... | collective-permute-start | bytes 6291464 | tf_op jit(solution)/shard_map/ppermute | solution.py:284
  12.9 15.7 %collective-permute-start = (bf16[128,512]{1,0:T(8,128)(2,1)S(1)}, bf16[128,512]{1,0:T(8,128)(2,1)S(1)}, u32[]{:S(2)}, u32[]{:S(2)}) collective-permute-start(bf16[128,512]{1,0:T(8,128)(2,1)S(1)} %dynamic-slice_convert_fusion.3), channel_id=1, source_target_pairs={{0,2},{2,0},{4,6},{6,4},{8,10},{10,8},{12,14},{14,12},{1,3},{3,1},... | collective-permute-start | bytes 393224 | tf_op jit(solution)/shard_map/ppermute | solution.py:185
  15.4 3.4 %copy-start.1 = (bf16[1024,4096]{1,0:T(8,128)(2,1)S(1)}, bf16[1024,4096]{1,0:T(8,128)(2,1)}, u32[]{:S(2)}) copy-start(bf16[1024,4096]{1,0:T(8,128)(2,1)} %copy-done) | copy-start | bytes 25165828
  22.5 6.1 %collective-permute-start.3 = (bf16[128,512]{1,0:T(8,128)(2,1)}, bf16[128,512]{1,0:T(8,128)(2,1)S(1)}, u32[]{:S(2)}, u32[]{:S(2)}) collective-permute-start(bf16[128,512]{1,0:T(8,128)(2,1)} %dynamic-slice_convert_fusion.2), channel_id=1, source_target_pairs={{0,2},{2,0},{4,6},{6,4},{8,10},{10,8},{12,14},{14,12},{1,3},{3,1},... | collective-permute-start | bytes 393224 | tf_op jit(solution)/shard_map/ppermute | solution.py:185
  22.5 3.4 %copy-start.2 = (bf16[1024,4096]{1,0:T(8,128)(2,1)S(1)}, bf16[1024,4096]{1,0:T(8,128)(2,1)}, u32[]{:S(2)}) copy-start(bf16[1024,4096]{1,0:T(8,128)(2,1)} %copy-done) | copy-start | bytes 25165828
  28.7 4.4 %collective-permute-start.2 = (bf16[64,512]{1,0:T(8,128)(2,1)S(1)}, bf16[64,512]{1,0:T(8,128)(2,1)S(1)}, u32[]{:S(2)}, u32[]{:S(2)}) collective-permute-start(bf16[64,512]{1,0:T(8,128)(2,1)S(1)} %dynamic-slice_convert_fusion.7), channel_id=1, source_target_pairs={{0,4},{2,6},{4,0},{6,2},{8,12},{10,14},{12,8},{14,10},{1,5},{3,7},... | collective-permute-start | bytes 196616 | tf_op jit(solution)/shard_map/ppermute | solution.py:185
  30.9 6.5 %collective-permute-start.7 = (bf16[128,512]{1,0:T(8,128)(2,1)S(1)}, bf16[128,512]{1,0:T(8,128)(2,1)S(1)}, u32[]{:S(2)}, u32[]{:S(2)}) collective-permute-start(bf16[128,512]{1,0:T(8,128)(2,1)S(1)} %get-tuple-element.95), channel_id=1, source_target_pairs={{0,2},{2,0},{4,6},{6,4},{8,10},{10,8},{12,14},{14,12},{1,3},{3,1},... | collective-permute-start | bytes 393224 | tf_op jit(solution)/shard_map/ppermute | solution.py:185
  32.5 5.6 %collective-permute-start.6 = (bf16[64,512]{1,0:T(8,128)(2,1)S(1)}, bf16[64,512]{1,0:T(8,128)(2,1)S(1)}, u32[]{:S(2)}, u32[]{:S(2)}) collective-permute-start(bf16[64,512]{1,0:T(8,128)(2,1)S(1)} %dynamic-slice_convert_fusion.6), channel_id=1, source_target_pairs={{0,4},{2,6},{4,0},{6,2},{8,12},{10,14},{12,8},{14,10},{1,5},{3,7},... | collective-permute-start | bytes 196616 | tf_op jit(solution)/shard_map/ppermute | solution.py:185
  33.0 5.8 %collective-permute-start.5 = (bf16[128,512]{1,0:T(8,128)(2,1)S(1)}, bf16[128,512]{1,0:T(8,128)(2,1)S(1)}, u32[]{:S(2)}, u32[]{:S(2)}) collective-permute-start(bf16[128,512]{1,0:T(8,128)(2,1)S(1)} %get-tuple-element.91), channel_id=1, source_target_pairs={{0,2},{2,0},{4,6},{6,4},{8,10},{10,8},{12,14},{14,12},{1,3},{3,1},... | collective-permute-start | bytes 393224 | tf_op jit(solution)/shard_map/ppermute | solution.py:185
  33.1 5.7 %collective-permute-start.4 = (bf16[64,512]{1,0:T(8,128)(2,1)S(1)}, bf16[64,512]{1,0:T(8,128)(2,1)S(1)}, u32[]{:S(2)}, u32[]{:S(2)}) collective-permute-start(bf16[64,512]{1,0:T(8,128)(2,1)S(1)} %add_convert_fusion.7), channel_id=1, source_target_pairs={{0,8},{2,10},{4,12},{6,14},{8,0},{10,2},{12,4},{14,6},{1,9},{3,11}... | collective-permute-start | bytes 196616 | tf_op jit(solution)/shard_map/ppermute | solution.py:185
  37.4 6.5 %collective-permute-start.11 = (bf16[64,512]{1,0:T(8,128)(2,1)S(1)}, bf16[64,512]{1,0:T(8,128)(2,1)S(1)}, u32[]{:S(2)}, u32[]{:S(2)}) collective-permute-start(bf16[64,512]{1,0:T(8,128)(2,1)S(1)} %dynamic-slice_convert_fusion.4), channel_id=1, source_target_pairs={{0,4},{2,6},{4,0},{6,2},{8,12},{10,14},{12,8},{14,10},{1,5},{3,7},... | collective-permute-start | bytes 196616 | tf_op jit(solution)/shard_map/ppermute | solution.py:185
  38.8 6.2 %collective-permute-start.10 = (bf16[64,512]{1,0:T(8,128)(2,1)S(1)}, bf16[64,512]{1,0:T(8,128)(2,1)S(1)}, u32[]{:S(2)}, u32[]{:S(2)}) collective-permute-start(bf16[64,512]{1,0:T(8,128)(2,1)S(1)} %add_convert_fusion.5), channel_id=1, source_target_pairs={{0,8},{2,10},{4,12},{6,14},{8,0},{10,2},{12,4},{14,6},{1,9},{3,11}... | collective-permute-start | bytes 196616 | tf_op jit(solution)/shard_map/ppermute | solution.py:185
  41.5 4.9 %collective-permute-start.9 = (bf16[64,512]{1,0:T(8,128)(2,1)S(1)}, bf16[64,512]{1,0:T(8,128)(2,1)S(1)}, u32[]{:S(2)}, u32[]{:S(2)}) collective-permute-start(bf16[64,512]{1,0:T(8,128)(2,1)S(1)} %dynamic-slice_convert_fusion.5), channel_id=1, source_target_pairs={{0,4},{2,6},{4,0},{6,2},{8,12},{10,14},{12,8},{14,10},{1,5},{3,7},... | collective-permute-start | bytes 196616 | tf_op jit(solution)/shard_map/ppermute | solution.py:185
  43.7 6.2 %collective-permute-start.8 = (bf16[64,512]{1,0:T(8,128)(2,1)S(1)}, bf16[64,512]{1,0:T(8,128)(2,1)S(1)}, u32[]{:S(2)}, u32[]{:S(2)}) collective-permute-start(bf16[64,512]{1,0:T(8,128)(2,1)S(1)} %add_convert_fusion.6), channel_id=1, source_target_pairs={{0,4},{2,6},{4,0},{6,2},{8,12},{10,14},{12,8},{14,10},{1,5},{3,7},... | collective-permute-start | bytes 196616 | tf_op jit(solution)/shard_map/ppermute | solution.py:185
  43.9 8.3 %collective-permute-start.15 = (bf16[64,512]{1,0:T(8,128)(2,1)S(1)}, bf16[64,512]{1,0:T(8,128)(2,1)S(1)}, u32[]{:S(2)}, u32[]{:S(2)}) collective-permute-start(bf16[64,512]{1,0:T(8,128)(2,1)S(1)} %add_convert_fusion.2), channel_id=1, source_target_pairs={{0,8},{2,10},{4,12},{6,14},{8,0},{10,2},{12,4},{14,6},{1,9},{3,11}... | collective-permute-start | bytes 196616 | tf_op jit(solution)/shard_map/ppermute | solution.py:185
  49.9 5.5 %collective-permute-start.14 = (bf16[64,512]{1,0:T(8,128)(2,1)S(1)}, bf16[64,512]{1,0:T(8,128)(2,1)S(1)}, u32[]{:S(2)}, u32[]{:S(2)}) collective-permute-start(bf16[64,512]{1,0:T(8,128)(2,1)S(1)} %add_convert_fusion.3), channel_id=1, source_target_pairs={{0,4},{2,6},{4,0},{6,2},{8,12},{10,14},{12,8},{14,10},{1,5},{3,7},... | collective-permute-start | bytes 196616 | tf_op jit(solution)/shard_map/ppermute | solution.py:185
  50.0 5.4 %collective-permute-start.13 = (bf16[64,512]{1,0:T(8,128)(2,1)S(1)}, bf16[64,512]{1,0:T(8,128)(2,1)S(1)}, u32[]{:S(2)}, u32[]{:S(2)}) collective-permute-start(bf16[64,512]{1,0:T(8,128)(2,1)S(1)} %add_convert_fusion.4), channel_id=1, source_target_pairs={{0,8},{2,10},{4,12},{6,14},{8,0},{10,2},{12,4},{14,6},{1,9},{3,11}... | collective-permute-start | bytes 196616 | tf_op jit(solution)/shard_map/ppermute | solution.py:185
  50.2 9.2 %collective-permute-start.12 = (bf16[128,512]{1,0:T(8,128)(2,1)S(1)}, bf16[128,512]{1,0:T(8,128)(2,1)S(1)}, u32[]{:S(2)}, u32[]{:S(2)}) collective-permute-start(bf16[128,512]{1,0:T(8,128)(2,1)S(1)} %pad_maximum_fusion), channel_id=1, source_target_pairs={{0,2},{2,0},{4,6},{6,4},{8,10},{10,8},{12,14},{14,12},{1,3},{3,1},... | collective-permute-start | bytes 393224 | tf_op jit(solution)/shard_map/ppermute | solution.py:185
  55.5 8.4 %collective-permute-start.19 = (bf16[64,512]{1,0:T(8,128)(2,1)S(1)}, bf16[64,512]{1,0:T(8,128)(2,1)S(1)}, u32[]{:S(2)}, u32[]{:S(2)}) collective-permute-start(bf16[64,512]{1,0:T(8,128)(2,1)S(1)} %add_convert_fusion), channel_id=1, source_target_pairs={{0,4},{2,6},{4,0},{6,2},{8,12},{10,14},{12,8},{14,10},{1,5},{3,7},... | collective-permute-start | bytes 196616 | tf_op jit(solution)/shard_map/ppermute | solution.py:185
  57.4 4.3 %collective-permute-start.17 = (bf16[64,512]{1,0:T(8,128)(2,1)S(1)}, bf16[64,512]{1,0:T(8,128)(2,1)S(1)}, u32[]{:S(2)}, u32[]{:S(2)}) collective-permute-start(bf16[64,512]{1,0:T(8,128)(2,1)S(1)} %add_convert_fusion.1), channel_id=1, source_target_pairs={{0,4},{2,6},{4,0},{6,2},{8,12},{10,14},{12,8},{14,10},{1,5},{3,7},... | collective-permute-start | bytes 196616 | tf_op jit(solution)/shard_map/ppermute | solution.py:185
  57.7 6.2 %collective-permute-start.16 = (bf16[128,512]{1,0:T(8,128)(2,1)S(1)}, bf16[128,512]{1,0:T(8,128)(2,1)S(1)}, u32[]{:S(2)}, u32[]{:S(2)}) collective-permute-start(bf16[128,512]{1,0:T(8,128)(2,1)S(1)} %pad_maximum_fusion.1), channel_id=1, source_target_pairs={{0,2},{2,0},{4,6},{6,4},{8,10},{10,8},{12,14},{14,12},{1,3},{3,1},... | collective-permute-start | bytes 393224 | tf_op jit(solution)/shard_map/ppermute | solution.py:185
  61.7 5.0 %collective-permute-start.18 = (bf16[128,512]{1,0:T(8,128)(2,1)S(1)}, bf16[128,512]{1,0:T(8,128)(2,1)S(1)}, u32[]{:S(2)}, u32[]{:S(2)}) collective-permute-start(bf16[128,512]{1,0:T(8,128)(2,1)S(1)} %pad_maximum_fusion.2), channel_id=1, source_target_pairs={{0,2},{2,0},{4,6},{6,4},{8,10},{10,8},{12,14},{14,12},{1,3},{3,1},... | collective-permute-start | bytes 393224 | tf_op jit(solution)/shard_map/ppermute | solution.py:185
  63.8 5.2 %copy-start.4 = (s32[512]{0:T(512)S(1)}, s32[512]{0:T(512)}, u32[]{:S(2)}) copy-start(s32[512]{0:T(512)} %param.10) | copy-start | bytes 6148
  63.8 5.2 %copy-start.5 = (s32[128]{0:T(128)S(1)}, s32[128]{0:T(128)}, u32[]{:S(2)}) copy-start(s32[128]{0:T(128)} %param.11) | copy-start | bytes 1540
  63.9 5.0 %collective-permute-start.20 = (bf16[128,512]{1,0:T(8,128)(2,1)S(1)}, bf16[128,512]{1,0:T(8,128)(2,1)S(1)}, u32[]{:S(2)}, u32[]{:S(2)}) collective-permute-start(bf16[128,512]{1,0:T(8,128)(2,1)S(1)} %pad_maximum_fusion.3), channel_id=1, source_target_pairs={{0,2},{2,0},{4,6},{6,4},{8,10},{10,8},{12,14},{14,12},{1,3},{3,1},... | collective-permute-start | bytes 393224 | tf_op jit(solution)/shard_map/ppermute | solution.py:185
  69.1 1.1 %copy-start.3 = (bf16[512,1024]{1,0:T(8,128)(2,1)}, bf16[512,1024]{1,0:T(8,128)(2,1)S(1)}, u32[]{:S(2)}) copy-start(bf16[512,1024]{1,0:T(8,128)(2,1)S(1)} %maximum_dynamic-update-slice_fusion.3) | copy-start | bytes 3145732

commit v8 on v7

--- a/solution.py
+++ b/solution.py
@@ -15,6 +15,7 @@
 PAIR = 2 * KOUT
 DEPTH_BLOCK = 512
 COLUMNS = 512
+COPY_ROWS = 32
 VMEM_LIMIT = 32 * 1024 * 1024
 NT = (((1,), (1,)), ((), ()))
 
@@ -90,94 +91,78 @@
             out_ref[...] = (total_ref[...] + term).T
 
 
-def first_kernel(
-    rows_ref, left_ref, right_ref, store_ref, out_ref, pre_ref, store_vmem, rows_vmem,
-    left_vmem, right_vmem, half_ref, total_ref, head_sems, sems,
+def copies_of(source_ref, target_ref, sems):
+    rows = target_ref.shape[0] // sems.shape[0]
+    return [
+        pltpu.make_async_copy(
+            source_ref.at[0, pl.ds(k * rows, rows)], target_ref.at[pl.ds(k * rows, rows)], sems.at[k]
+        )
+        for k in range(sems.shape[0])
+    ]
+
+
+def score_kernel(
+    rows_ref, left_ref, right_ref, store_ref, *refs,
 ):
-    heads = [
-        pltpu.make_async_copy(source.at[0], target, head_sems.at[k])
-        for k, (source, target) in enumerate(
-            ((right_ref, right_vmem), (left_ref, left_vmem), (rows_ref, rows_vmem))
-        )
-    ]
-    columns = total_ref.shape[0]
-    copies = [
-        pltpu.make_async_copy(
-            store_ref.at[0, pl.ds(first, columns)],
-            store_vmem.at[pl.ds(first, columns)],
-            sems.at[k],
-        )
-        for k, first in enumerate(range(0, store_vmem.shape[0], columns))
-    ]
+    *out_refs, left_vmem, right_vmem, rows_vmem, store_vmem, half_ref, total_ref = refs[:-4]
+    left_sems, right_sems, rows_sems, store_sems = refs[-4:]
+    heads = (
+        copies_of(right_ref, right_vmem, right_sems)
+        + copies_of(left_ref, left_vmem, left_sems)
+        + copies_of(rows_ref, rows_vmem, rows_sems)
+    )
+    copies = copies_of(store_ref, store_vmem, store_sems)
     for copy in heads + copies:
         copy.start()
     for copy in heads:
         copy.wait()
+    pre_ref = rows_vmem
     precondition(rows_vmem, left_vmem[...], right_vmem[...], half_ref, pre_ref)
-    copies[0].wait()
-    dot(pre_ref, store_vmem, 0, total_ref, out_ref)
-    for copy in copies[1:]:
-        copy.wait()
-
-
-def later_kernel(first, pre_ref, store_ref, out_ref, total_ref):
-    dot(pre_ref, store_ref, first, total_ref, out_ref)
+    share = len(copies) // len(out_refs)
+    columns = total_ref.shape[0]
+    for k, out_ref in enumerate(out_refs):
+        for copy in copies[k * share : (k + 1) * share]:
+            copy.wait()
+        dot(pre_ref, store_vmem, k * columns, total_ref, out_ref)
 
 
 VMEM = pl.BlockSpec(memory_space=pltpu.VMEM)
 HBM = pl.BlockSpec(memory_space=pltpu.HBM)
+ANYWHERE = pl.BlockSpec(memory_space=pl.ANY)
 
 
 def in_hbm(array):
     return pltpu.with_memory_space_constraint(array, pltpu.HBM)
 
 
-def first_scores(queries, left_inv, right_inv, store, columns):
+def score(queries, left_inv, right_inv, store, columns):
     count, depth = queries.shape[1:]
     examples = store.shape[1]
-    out, pre, store_vmem, _ = pl.pallas_call(
-        first_kernel,
-        out_shape=(
-            pltpu.VMEM((count, columns), jnp.float32),
-            pltpu.VMEM((count, depth), jnp.bfloat16),
-            pltpu.VMEM((examples, depth), jnp.bfloat16),
-            pltpu.VMEM((count, depth), jnp.bfloat16),
-        ),
-        in_specs=[HBM] * 4,
-        out_specs=(VMEM,) * 4,
+    blocks = examples // columns
+    return pl.pallas_call(
+        score_kernel,
+        out_shape=(pltpu.VMEM((count, columns), jnp.float32),) * blocks,
+        in_specs=[ANYWHERE] + [HBM] * 3,
+        out_specs=(VMEM,) * blocks,
         scratch_shapes=[
             pltpu.VMEM((KIN, KIN), jnp.bfloat16),
             pltpu.VMEM((KOUT, KOUT), jnp.bfloat16),
+            pltpu.VMEM((count, depth), jnp.bfloat16),
+            pltpu.VMEM((examples, depth), jnp.bfloat16),
             pltpu.VMEM((count // ROWS, WIDE, KOUT), jnp.bfloat16),
             pltpu.VMEM((columns, count), jnp.float32),
-            pltpu.SemaphoreType.DMA((3,)),
-            pltpu.SemaphoreType.DMA((examples // columns,)),
+            pltpu.SemaphoreType.DMA((1,)),
+            pltpu.SemaphoreType.DMA((1,)),
+            pltpu.SemaphoreType.DMA((count // COPY_ROWS,)),
+            pltpu.SemaphoreType.DMA((examples // COPY_ROWS,)),
         ],
         compiler_params=pltpu.CompilerParams(vmem_limit_bytes=VMEM_LIMIT),
         cost_estimate=pl.CostEstimate(
-            flops=2 * count * depth * (columns + 1024),
+            flops=2 * count * depth * (examples + 1024),
             bytes_accessed=2 * depth * (2 * count + examples),
             transcendentals=0,
         ),
-    )(*map(in_hbm, (queries, left_inv, right_inv, store)))
-    return out, pre, store_vmem
-
-
-def later_scores(pre, store_vmem, first, columns):
-    count, depth = pre.shape
-    return pl.pallas_call(
-        functools.partial(later_kernel, first),
-        out_shape=pltpu.VMEM((count, columns), jnp.float32),
-        in_specs=[VMEM] * 2,
-        out_specs=VMEM,
-        scratch_shapes=[pltpu.VMEM((columns, count), jnp.float32)],
-        compiler_params=pltpu.CompilerParams(vmem_limit_bytes=VMEM_LIMIT),
-        cost_estimate=pl.CostEstimate(
-            flops=2 * count * depth * columns,
-            bytes_accessed=2 * depth * (count + columns),
-            transcendentals=0,
-        ),
-    )(pre, store_vmem)
+    )(queries, *map(in_hbm, (left_inv, right_inv, store)))
 
 
 def swap(block, bit):
@@ -255,12 +240,12 @@
     order = Order()
     chunks = {}
     events = []
-    for number, (start, size, _) in enumerate(makers):
+    for number, (start, ready, size, _) in enumerate(makers):
         events.append((start, number))
-        events.extend((start + 2 + at, number) for at in step_times(size, len(bits)) if bits)
+        events.extend((ready + 2 + at, number) for at in step_times(size, len(bits)) if bits)
     for _, number in sorted(events):
         if number not in chunks:
-            chunk = chunks[number] = LayerSum(makers[number][2](order), bits, index)
+            chunk = chunks[number] = LayerSum(makers[number][3](order), bits, index)
         else:
             chunk = chunks[number]
             chunk.take(order)
@@ -275,22 +260,24 @@
     width = min(COLUMNS, columns)
     ex_count = lax.axis_size("ex")
     position = lax.axis_index("ex")
-    first_part, pre, store_vmem = first_scores(queries, left_inv, right_inv, store, width)
     places, makers = [], []
-    current = pre
+    current = queries
     for step in range(ex_count):
         if step > 0:
             route = [((i - 1) % ex_count, i) for i in range(ex_count)]
             current = lax.ppermute(current, "ex", route)
-        for first in range(0, columns, width):
-
-            def make(order, first=first, step=step, current=current):
-                if step == 0 and first == 0:
-                    return first_part
-                return order.mark(later_scores(order.after(current), store_vmem, first, width))
-
-            start = 4.5 + 4.5 * step + 1.5 * (first // width)
-            makers.append((start, rows * width, make))
+        made = []
+        for number, first in enumerate(range(0, columns, width)):
+
+            def make(order, number=number, step=step, current=current, made=made):
+                if number == 0:
+                    block = order.after(current) if step else in_hbm(current)
+                    made.extend(score(block, left_inv, right_inv, store, width))
+                    if step:
+                        made[0] = order.mark(made[0])
+                return made[number]
+
+            makers.append((6.0 + 2.0 * step, 6.0 + 7.0 * step, rows * width, make))
             places.append(((position - step) % ex_count * rows, jnp.int32(first)))
     count = lax.axis_size("layer")
     bits = [1 << k for k in range(count.bit_length() - 1)]

time: 70.4 us -> 71.2 us (1.011)
  local copies, waits for them, and re-layouts: 11 us -> 3.89 us
  Pallas kernels: 14.1 us -> 19.5 us
  waiting for transfers between devices: 16.5 us -> 20.3 us
  starting transfers between devices: 25.8 us -> 24.7 us
    unnamed x12 -> x10, local copies, waits for them, and re-layouts: 10.1 us -> 2.96 us
    pallas_call x4 -> x2, Pallas kernels: 14.1 us -> 19.5 us  [score(): pl.pallas_call(score_kernel, out_shape=(pltpu.VMEM((count, columns), jnp....]
    ppermute x20, waiting for transfers between devices: 16.5 us -> 20.3 us  [swap(): return lax.ppermute(block, 'layer', route)]
    ppermute x20, starting transfers between devices: 25.4 us -> 24.2 us  [swap(): return lax.ppermute(block, 'layer', route)]
  transfers between devices with their start and end apart: 21 -> 21, of which waited for: 8 -> 11; matrix products, arithmetic and copies ran while one was open for 2% -> 2% of each run, Pallas kernels for 8% -> 27%
where the time goes in v8:
time: 71.2 us; the launch traced here: 71.1 us
  starting transfers between devices  24.7 us (35%)
  waiting for transfers between devices  20.3 us (29%)
  Pallas kernels  19.5 us (27%)
  local copies, waits for them, and re-layouts  3.89 us (5%)
  matrix products  1.08 us (2%)
  between operations  0.92 us (1%)
    ppermute x20, starting transfers between devices, swap(): return lax.ppermute(block, 'layer', route)  24.2 us
    ppermute x20, waiting for transfers between devices, swap(): return lax.ppermute(block, 'layer', route)  20.3 us
    pallas_call x2, Pallas kernels, score(): pl.pallas_call(score_kernel, out_shape=(pltpu.VMEM((count, columns), jnp....  19.5 us
    unnamed x10, local copies, waits for them, and re-layouts  2.96 us
  transfers between devices with their start and end apart: 21, of which 11 were waited for; matrix products, arithmetic and copies ran while one was open for 2% of the time, Pallas kernels for 27%

profile of v8, /device:TPU:0, one launch (start us, length us, event | category | flops | bytes accessed | tf_op | source)
XLA Modules:
  0.0 71.1 jit_solution(473450260498804145)
XLA Ops:
  0.6 0.5 collective-permute-start.1
  1.1 11.3 %shard_map.77 = (f32[256,512]{1,0:T(8,128)S(1)}, f32[256,512]{1,0:T(8,128)S(1)}) custom-call(bf16[1,256,4096]{2,1,0:T(8,128)(2,1)} %rows_ref.1, bf16[1,32,32]{2,1,0:T(8,128)(2,1)} %left_ref.3, bf16[1,128,128]{2,1,0:T(8,128)(2,1)} %right_ref.3, bf16[1,1024,4096]{2,1,0:T(8,128)(2,1)} %store_ref.3), custom_call_target="tpu_custom_call" | custom-call | flops 4294967296 | bytes 12582912 | tf_op jit(solution)/shard_map/pallas_call | solution.py:142
  12.5 2.6 %collective-permute-start = (bf16[128,512]{1,0:T(8,128)(2,1)S(1)}, bf16[128,512]{1,0:T(8,128)(2,1)S(1)}, u32[]{:S(2)}, u32[]{:S(2)}) collective-permute-start(bf16[128,512]{1,0:T(8,128)(2,1)S(1)} %dynamic-slice_convert_fusion.3), channel_id=1, source_target_pairs={{0,2},{2,0},{4,6},{6,4},{8,10},{10,8},{12,14},{14,12},{1,3},{3,1},... | collective-permute-start | bytes 393224 | tf_op jit(solution)/shard_map/ppermute | solution.py:170
  15.1 0.7 dynamic-slice_convert_fusion.2
  15.8 0.0 collective-permute-start.3
  15.8 0.0 collective-permute-done.1.rows_ref
  15.8 0.0 copy-start
  15.8 1.4 %copy-done = bf16[1,256,4096]{2,1,0:T(8,128)(2,1)} copy-done((bf16[1,256,4096]{2,1,0:T(8,128)(2,1)}, bf16[1,256,4096]{2,1,0:T(8,128)(2,1)S(1)}, u32[]{:S(2)}) %copy-start) | copy-done | bytes 2097176
  17.2 0.0 copy-start.1
  17.2 1.6 %copy-done.1 = bf16[1,256,4096]{2,1,0:T(8,128)(2,1)S(1)} copy-done((bf16[1,256,4096]{2,1,0:T(8,128)(2,1)S(1)}, bf16[1,256,4096]{2,1,0:T(8,128)(2,1)}, u32[]{:S(2)}) %copy-start.1) | copy-done | bytes 2097176
  18.8 8.2 %shard_map.78 = (f32[256,512]{1,0:T(8,128)S(1)}, f32[256,512]{1,0:T(8,128)S(1)}) custom-call(bf16[1,256,4096]{2,1,0:T(8,128)(2,1)S(1)} %copy-done.1, bf16[1,32,32]{2,1,0:T(8,128)(2,1)} %left_ref.3, bf16[1,128,128]{2,1,0:T(8,128)(2,1)} %right_ref.3, bf16[1,1024,4096]{2,1,0:T(8,128)(2,1)} %store_ref.3), custom_call_target="tpu_custom_call" | custom-call | flops 4294967296 | bytes 12582912 | tf_op jit(solution)/shard_map/pallas_call | solution.py:142
  27.0 0.0 collective-permute-done
  27.0 0.0 collective-permute-done.3
  27.0 0.1 convert_add_fusion.2
  27.1 2.1 %collective-permute-start.2 = (bf16[64,512]{1,0:T(8,128)(2,1)S(1)}, bf16[64,512]{1,0:T(8,128)(2,1)S(1)}, u32[]{:S(2)}, u32[]{:S(2)}) collective-permute-start(bf16[64,512]{1,0:T(8,128)(2,1)S(1)} %dynamic-slice_convert_fusion.7), channel_id=1, source_target_pairs={{0,4},{2,6},{4,0},{6,2},{8,12},{10,14},{12,8},{14,10},{1,5},{3,7},... | collective-permute-start | bytes 196616 | tf_op jit(solution)/shard_map/ppermute | solution.py:170
  29.3 0.1 collective-permute-start.5
  29.3 2.2 %collective-permute-done.2 = bf16[64,512]{1,0:T(8,128)(2,1)S(1)} collective-permute-done((bf16[64,512]{1,0:T(8,128)(2,1)S(1)}, bf16[64,512]{1,0:T(8,128)(2,1)S(1)}, u32[]{:S(2)}, u32[]{:S(2)}) %collective-permute-start.2) | collective-permute-done | bytes 65568 | tf_op jit(solution)/shard_map/ppermute | solution.py:170
  31.6 2.0 %collective-permute-done.5 = bf16[64,512]{1,0:T(8,128)(2,1)S(1)} collective-permute-done((bf16[64,512]{1,0:T(8,128)(2,1)S(1)}, bf16[64,512]{1,0:T(8,128)(2,1)S(1)}, u32[]{:S(2)}, u32[]{:S(2)}) %collective-permute-start.5) | collective-permute-done | bytes 65568 | tf_op jit(solution)/shard_map/ppermute | solution.py:170
  33.6 2.7 %collective-permute-start.9 = (bf16[64,512]{1,0:T(8,128)(2,1)S(1)}, bf16[64,512]{1,0:T(8,128)(2,1)S(1)}, u32[]{:S(2)}, u32[]{:S(2)}) collective-permute-start(bf16[64,512]{1,0:T(8,128)(2,1)S(1)} %add_convert_fusion.5), channel_id=1, source_target_pairs={{0,8},{2,10},{4,12},{6,14},{8,0},{10,2},{12,4},{14,6},{1,9},{3,11}... | collective-permute-start | bytes 196616 | tf_op jit(solution)/shard_map/ppermute | solution.py:170
  36.2 0.4 collective-permute-start.4
  36.7 1.6 %collective-permute-start.8 = (bf16[128,512]{1,0:T(8,128)(2,1)S(1)}, bf16[128,512]{1,0:T(8,128)(2,1)S(1)}, u32[]{:S(2)}, u32[]{:S(2)}) collective-permute-start(bf16[128,512]{1,0:T(8,128)(2,1)S(1)} %get-tuple-element.89), channel_id=1, source_target_pairs={{0,2},{2,0},{4,6},{6,4},{8,10},{10,8},{12,14},{14,12},{1,3},{3,1},... | collective-permute-start | bytes 393224 | tf_op jit(solution)/shard_map/ppermute | solution.py:170
  38.2 0.5 collective-permute-start.7
  38.8 3.5 %collective-permute-done.4 = bf16[64,512]{1,0:T(8,128)(2,1)S(1)} collective-permute-done((bf16[64,512]{1,0:T(8,128)(2,1)S(1)}, bf16[64,512]{1,0:T(8,128)(2,1)S(1)}, u32[]{:S(2)}, u32[]{:S(2)}) %collective-permute-start.4) | collective-permute-done | bytes 65568 | tf_op jit(solution)/shard_map/ppermute | solution.py:170
  42.3 0.0 collective-permute-done.9
  42.3 0.4 collective-permute-start.13
  42.7 0.0 collective-permute-done.8
  42.7 0.6 collective-permute-done.7
  43.4 1.2 %collective-permute-start.6 = (bf16[64,512]{1,0:T(8,128)(2,1)S(1)}, bf16[64,512]{1,0:T(8,128)(2,1)S(1)}, u32[]{:S(2)}, u32[]{:S(2)}) collective-permute-start(bf16[64,512]{1,0:T(8,128)(2,1)S(1)} %add_convert_fusion.6), channel_id=1, source_target_pairs={{0,4},{2,6},{4,0},{6,2},{8,12},{10,14},{12,8},{14,10},{1,5},{3,7},... | collective-permute-start | bytes 196616 | tf_op jit(solution)/shard_map/ppermute | solution.py:170
  44.6 0.9 %collective-permute-start.12 = (bf16[64,512]{1,0:T(8,128)(2,1)S(1)}, bf16[64,512]{1,0:T(8,128)(2,1)S(1)}, u32[]{:S(2)}, u32[]{:S(2)}) collective-permute-start(bf16[64,512]{1,0:T(8,128)(2,1)S(1)} %dynamic-slice_convert_fusion.4), channel_id=1, source_target_pairs={{0,4},{2,6},{4,0},{6,2},{8,12},{10,14},{12,8},{14,10},{1,5},{3,7},... | collective-permute-start | bytes 196616 | tf_op jit(solution)/shard_map/ppermute | solution.py:170
  45.6 1.2 %collective-permute-start.11 = (bf16[64,512]{1,0:T(8,128)(2,1)S(1)}, bf16[64,512]{1,0:T(8,128)(2,1)S(1)}, u32[]{:S(2)}, u32[]{:S(2)}) collective-permute-start(bf16[64,512]{1,0:T(8,128)(2,1)S(1)} %dynamic-slice_convert_fusion.5), channel_id=1, source_target_pairs={{0,4},{2,6},{4,0},{6,2},{8,12},{10,14},{12,8},{14,10},{1,5},{3,7},... | collective-permute-start | bytes 196616 | tf_op jit(solution)/shard_map/ppermute | solution.py:170
  46.9 1.4 %collective-permute-done.6 = bf16[64,512]{1,0:T(8,128)(2,1)S(1)} collective-permute-done((bf16[64,512]{1,0:T(8,128)(2,1)S(1)}, bf16[64,512]{1,0:T(8,128)(2,1)S(1)}, u32[]{:S(2)}, u32[]{:S(2)}) %collective-permute-start.6) | collective-permute-done | bytes 65568 | tf_op jit(solution)/shard_map/ppermute | solution.py:170
  48.3 0.0 collective-permute-done.13
  48.3 0.7 %collective-permute-done.12 = bf16[64,512]{1,0:T(8,128)(2,1)S(1)} collective-permute-done((bf16[64,512]{1,0:T(8,128)(2,1)S(1)}, bf16[64,512]{1,0:T(8,128)(2,1)S(1)}, u32[]{:S(2)}, u32[]{:S(2)}) %collective-permute-start.12) | collective-permute-done | bytes 65568 | tf_op jit(solution)/shard_map/ppermute | solution.py:170
  49.0 3.0 %collective-permute-start.15 = (bf16[64,512]{1,0:T(8,128)(2,1)S(1)}, bf16[64,512]{1,0:T(8,128)(2,1)S(1)}, u32[]{:S(2)}, u32[]{:S(2)}) collective-permute-start(bf16[64,512]{1,0:T(8,128)(2,1)S(1)} %add_convert_fusion.2), channel_id=1, source_target_pairs={{0,8},{2,10},{4,12},{6,14},{8,0},{10,2},{12,4},{14,6},{1,9},{3,11}... | collective-permute-start | bytes 196616 | tf_op jit(solution)/shard_map/ppermute | solution.py:170
  52.0 0.0 collective-permute-done.11
  52.0 1.1 %collective-permute-start.14 = (bf16[64,512]{1,0:T(8,128)(2,1)S(1)}, bf16[64,512]{1,0:T(8,128)(2,1)S(1)}, u32[]{:S(2)}, u32[]{:S(2)}) collective-permute-start(bf16[64,512]{1,0:T(8,128)(2,1)S(1)} %add_convert_fusion.3), channel_id=1, source_target_pairs={{0,8},{2,10},{4,12},{6,14},{8,0},{10,2},{12,4},{14,6},{1,9},{3,11}... | collective-permute-start | bytes 196616 | tf_op jit(solution)/shard_map/ppermute | solution.py:170
  53.1 1.6 %collective-permute-start.16 = (bf16[128,512]{1,0:T(8,128)(2,1)S(1)}, bf16[128,512]{1,0:T(8,128)(2,1)S(1)}, u32[]{:S(2)}, u32[]{:S(2)}) collective-permute-start(bf16[128,512]{1,0:T(8,128)(2,1)S(1)} %pad_maximum_fusion.1), channel_id=1, source_target_pairs={{0,2},{2,0},{4,6},{6,4},{8,10},{10,8},{12,14},{14,12},{1,3},{3,1},... | collective-permute-start | bytes 393224 | tf_op jit(solution)/shard_map/ppermute | solution.py:170
  54.7 0.6 collective-permute-start.10
  55.3 0.0 collective-permute-done.15
  55.3 2.8 %collective-permute-done.14 = bf16[64,512]{1,0:T(8,128)(2,1)S(1)} collective-permute-done((bf16[64,512]{1,0:T(8,128)(2,1)S(1)}, bf16[64,512]{1,0:T(8,128)(2,1)S(1)}, u32[]{:S(2)}, u32[]{:S(2)}) %collective-permute-start.14) | collective-permute-done | bytes 65568 | tf_op jit(solution)/shard_map/ppermute | solution.py:170
  58.1 0.4 collective-permute-start.17
  58.5 1.7 %collective-permute-start.19 = (bf16[64,512]{1,0:T(8,128)(2,1)S(1)}, bf16[64,512]{1,0:T(8,128)(2,1)S(1)}, u32[]{:S(2)}, u32[]{:S(2)}) collective-permute-start(bf16[64,512]{1,0:T(8,128)(2,1)S(1)} %add_convert_fusion), channel_id=1, source_target_pairs={{0,4},{2,6},{4,0},{6,2},{8,12},{10,14},{12,8},{14,10},{1,5},{3,7},... | collective-permute-start | bytes 196616 | tf_op jit(solution)/shard_map/ppermute | solution.py:170
  60.2 0.0 collective-permute-done.10
  60.2 0.0 collective-permute-done.16
  60.2 2.2 %collective-permute-done.17 = bf16[64,512]{1,0:T(8,128)(2,1)S(1)} collective-permute-done((bf16[64,512]{1,0:T(8,128)(2,1)S(1)}, bf16[64,512]{1,0:T(8,128)(2,1)S(1)}, u32[]{:S(2)}, u32[]{:S(2)}) %collective-permute-start.17) | collective-permute-done | bytes 65568 | tf_op jit(solution)/shard_map/ppermute | solution.py:170
  62.4 0.7 collective-permute-done.19
  63.2 1.6 %collective-permute-start.20 = (bf16[128,512]{1,0:T(8,128)(2,1)S(1)}, bf16[128,512]{1,0:T(8,128)(2,1)S(1)}, u32[]{:S(2)}, u32[]{:S(2)}) collective-permute-start(bf16[128,512]{1,0:T(8,128)(2,1)S(1)} %pad_maximum_fusion.3), channel_id=1, source_target_pairs={{0,2},{2,0},{4,6},{6,4},{8,10},{10,8},{12,14},{14,12},{1,3},{3,1},... | collective-permute-start | bytes 393224 | tf_op jit(solution)/shard_map/ppermute | solution.py:170
  64.8 0.6 collective-permute-start.18
  65.5 0.0 copy-start.3
  65.5 0.0 copy-start.4
  65.5 0.1 broadcast_in_dim.2
  65.7 2.5 %collective-permute-done.20 = bf16[128,512]{1,0:T(8,128)(2,1)S(1)} collective-permute-done((bf16[128,512]{1,0:T(8,128)(2,1)S(1)}, bf16[128,512]{1,0:T(8,128)(2,1)S(1)}, u32[]{:S(2)}, u32[]{:S(2)}) %collective-permute-start.20) | collective-permute-done | bytes 131104 | tf_op jit(solution)/shard_map/ppermute | solution.py:170
  68.2 1.6 %collective-permute-done.18 = bf16[128,512]{1,0:T(8,128)(2,1)S(1)} collective-permute-done((bf16[128,512]{1,0:T(8,128)(2,1)S(1)}, bf16[128,512]{1,0:T(8,128)(2,1)S(1)}, u32[]{:S(2)}, u32[]{:S(2)}) %collective-permute-start.18) | collective-permute-done | bytes 131104 | tf_op jit(solution)/shard_map/ppermute | solution.py:170
  69.9 0.0 copy-done.3
  70.0 0.0 copy-done.4
  70.0 0.0 copy-start.2
  70.0 1.1 %convolution_convert_fusion = bf16[128,1024]{1,0:T(8,128)(2,1)} fusion(bf16[512,1024]{1,0:T(8,128)(2,1)S(1)} %maximum_dynamic-update-slice_fusion.3, s32[512]{0:T(512)S(1)} %copy-done.3, s32[128]{0:T(128)S(1)} %copy-done.4), kind=kOutput, calls=%fused_computation | convolution fusion | flops 134742016 | bytes 1313280 | tf_op jit(solution)/shard_map/dot_general | solution.py:293
  71.1 0.0 copy-done.2
  (32 shorter events, 0.7 us)
Async XLA Ops:
  0.6 15.2 %collective-permute-start.1 = (bf16[1,256,4096]{2,1,0:T(8,128)(2,1)}, bf16[1,256,4096]{2,1,0:T(8,128)(2,1)S(1)}, u32[]{:S(2)}, u32[]{:S(2)}) collective-permute-start(bf16[1,256,4096]{2,1,0:T(8,128)(2,1)} %rows_ref.1), channel_id=1, source_target_pairs={{1,0},{0,1},{3,2},{2,3},{5,4},{4,5},{7,6},{6,7},{9,8},{8,9},{11,10... | collective-permute-start | bytes 6291464 | tf_op jit(solution)/shard_map/ppermute | solution.py:268
  12.5 14.5 %collective-permute-start = (bf16[128,512]{1,0:T(8,128)(2,1)S(1)}, bf16[128,512]{1,0:T(8,128)(2,1)S(1)}, u32[]{:S(2)}, u32[]{:S(2)}) collective-permute-start(bf16[128,512]{1,0:T(8,128)(2,1)S(1)} %dynamic-slice_convert_fusion.3), channel_id=1, source_target_pairs={{0,2},{2,0},{4,6},{6,4},{8,10},{10,8},{12,14},{14,12},{1,3},{3,1},... | collective-permute-start | bytes 393224 | tf_op jit(solution)/shard_map/ppermute | solution.py:170
  15.8 11.2 %collective-permute-start.3 = (bf16[128,512]{1,0:T(8,128)(2,1)}, bf16[128,512]{1,0:T(8,128)(2,1)S(1)}, u32[]{:S(2)}, u32[]{:S(2)}) collective-permute-start(bf16[128,512]{1,0:T(8,128)(2,1)} %dynamic-slice_convert_fusion.2), channel_id=1, source_target_pairs={{0,2},{2,0},{4,6},{6,4},{8,10},{10,8},{12,14},{14,12},{1,3},{3,1},... | collective-permute-start | bytes 393224 | tf_op jit(solution)/shard_map/ppermute | solution.py:170
  15.8 1.4 %copy-start = (bf16[1,256,4096]{2,1,0:T(8,128)(2,1)}, bf16[1,256,4096]{2,1,0:T(8,128)(2,1)S(1)}, u32[]{:S(2)}) copy-start(bf16[1,256,4096]{2,1,0:T(8,128)(2,1)S(1)} %collective-permute-done.1.rows_ref) | copy-start | bytes 6291460
  17.2 1.6 %copy-start.1 = (bf16[1,256,4096]{2,1,0:T(8,128)(2,1)S(1)}, bf16[1,256,4096]{2,1,0:T(8,128)(2,1)}, u32[]{:S(2)}) copy-start(bf16[1,256,4096]{2,1,0:T(8,128)(2,1)} %copy-done) | copy-start | bytes 6291460
  27.1 4.4 %collective-permute-start.2 = (bf16[64,512]{1,0:T(8,128)(2,1)S(1)}, bf16[64,512]{1,0:T(8,128)(2,1)S(1)}, u32[]{:S(2)}, u32[]{:S(2)}) collective-permute-start(bf16[64,512]{1,0:T(8,128)(2,1)S(1)} %dynamic-slice_convert_fusion.7), channel_id=1, source_target_pairs={{0,4},{2,6},{4,0},{6,2},{8,12},{10,14},{12,8},{14,10},{1,5},{3,7},... | collective-permute-start | bytes 196616 | tf_op jit(solution)/shard_map/ppermute | solution.py:170
  29.3 4.3 %collective-permute-start.5 = (bf16[64,512]{1,0:T(8,128)(2,1)S(1)}, bf16[64,512]{1,0:T(8,128)(2,1)S(1)}, u32[]{:S(2)}, u32[]{:S(2)}) collective-permute-start(bf16[64,512]{1,0:T(8,128)(2,1)S(1)} %dynamic-slice_convert_fusion.6), channel_id=1, source_target_pairs={{0,4},{2,6},{4,0},{6,2},{8,12},{10,14},{12,8},{14,10},{1,5},{3,7},... | collective-permute-start | bytes 196616 | tf_op jit(solution)/shard_map/ppermute | solution.py:170
  33.6 8.7 %collective-permute-start.9 = (bf16[64,512]{1,0:T(8,128)(2,1)S(1)}, bf16[64,512]{1,0:T(8,128)(2,1)S(1)}, u32[]{:S(2)}, u32[]{:S(2)}) collective-permute-start(bf16[64,512]{1,0:T(8,128)(2,1)S(1)} %add_convert_fusion.5), channel_id=1, source_target_pairs={{0,8},{2,10},{4,12},{6,14},{8,0},{10,2},{12,4},{14,6},{1,9},{3,11}... | collective-permute-start | bytes 196616 | tf_op jit(solution)/shard_map/ppermute | solution.py:170
  36.2 6.1 %collective-permute-start.4 = (bf16[64,512]{1,0:T(8,128)(2,1)S(1)}, bf16[64,512]{1,0:T(8,128)(2,1)S(1)}, u32[]{:S(2)}, u32[]{:S(2)}) collective-permute-start(bf16[64,512]{1,0:T(8,128)(2,1)S(1)} %add_convert_fusion.7), channel_id=1, source_target_pairs={{0,8},{2,10},{4,12},{6,14},{8,0},{10,2},{12,4},{14,6},{1,9},{3,11}... | collective-permute-start | bytes 196616 | tf_op jit(solution)/shard_map/ppermute | solution.py:170
  36.7 6.0 %collective-permute-start.8 = (bf16[128,512]{1,0:T(8,128)(2,1)S(1)}, bf16[128,512]{1,0:T(8,128)(2,1)S(1)}, u32[]{:S(2)}, u32[]{:S(2)}) collective-permute-start(bf16[128,512]{1,0:T(8,128)(2,1)S(1)} %get-tuple-element.89), channel_id=1, source_target_pairs={{0,2},{2,0},{4,6},{6,4},{8,10},{10,8},{12,14},{14,12},{1,3},{3,1},... | collective-permute-start | bytes 393224 | tf_op jit(solution)/shard_map/ppermute | solution.py:170
  38.2 5.1 %collective-permute-start.7 = (bf16[128,512]{1,0:T(8,128)(2,1)S(1)}, bf16[128,512]{1,0:T(8,128)(2,1)S(1)}, u32[]{:S(2)}, u32[]{:S(2)}) collective-permute-start(bf16[128,512]{1,0:T(8,128)(2,1)S(1)} %get-tuple-element.87), channel_id=1, source_target_pairs={{0,2},{2,0},{4,6},{6,4},{8,10},{10,8},{12,14},{14,12},{1,3},{3,1},... | collective-permute-start | bytes 393224 | tf_op jit(solution)/shard_map/ppermute | solution.py:170
  42.3 5.9 %collective-permute-start.13 = (bf16[64,512]{1,0:T(8,128)(2,1)S(1)}, bf16[64,512]{1,0:T(8,128)(2,1)S(1)}, u32[]{:S(2)}, u32[]{:S(2)}) collective-permute-start(bf16[64,512]{1,0:T(8,128)(2,1)S(1)} %add_convert_fusion.4), channel_id=1, source_target_pairs={{0,4},{2,6},{4,0},{6,2},{8,12},{10,14},{12,8},{14,10},{1,5},{3,7},... | collective-permute-start | bytes 196616 | tf_op jit(solution)/shard_map/ppermute | solution.py:170
  43.4 4.9 %collective-permute-start.6 = (bf16[64,512]{1,0:T(8,128)(2,1)S(1)}, bf16[64,512]{1,0:T(8,128)(2,1)S(1)}, u32[]{:S(2)}, u32[]{:S(2)}) collective-permute-start(bf16[64,512]{1,0:T(8,128)(2,1)S(1)} %add_convert_fusion.6), channel_id=1, source_target_pairs={{0,4},{2,6},{4,0},{6,2},{8,12},{10,14},{12,8},{14,10},{1,5},{3,7},... | collective-permute-start | bytes 196616 | tf_op jit(solution)/shard_map/ppermute | solution.py:170
  44.6 4.3 %collective-permute-start.12 = (bf16[64,512]{1,0:T(8,128)(2,1)S(1)}, bf16[64,512]{1,0:T(8,128)(2,1)S(1)}, u32[]{:S(2)}, u32[]{:S(2)}) collective-permute-start(bf16[64,512]{1,0:T(8,128)(2,1)S(1)} %dynamic-slice_convert_fusion.4), channel_id=1, source_target_pairs={{0,4},{2,6},{4,0},{6,2},{8,12},{10,14},{12,8},{14,10},{1,5},{3,7},... | collective-permute-start | bytes 196616 | tf_op jit(solution)/shard_map/ppermute | solution.py:170
  45.6 6.3 %collective-permute-start.11 = (bf16[64,512]{1,0:T(8,128)(2,1)S(1)}, bf16[64,512]{1,0:T(8,128)(2,1)S(1)}, u32[]{:S(2)}, u32[]{:S(2)}) collective-permute-start(bf16[64,512]{1,0:T(8,128)(2,1)S(1)} %dynamic-slice_convert_fusion.5), channel_id=1, source_target_pairs={{0,4},{2,6},{4,0},{6,2},{8,12},{10,14},{12,8},{14,10},{1,5},{3,7},... | collective-permute-start | bytes 196616 | tf_op jit(solution)/shard_map/ppermute | solution.py:170
  49.0 6.3 %collective-permute-start.15 = (bf16[64,512]{1,0:T(8,128)(2,1)S(1)}, bf16[64,512]{1,0:T(8,128)(2,1)S(1)}, u32[]{:S(2)}, u32[]{:S(2)}) collective-permute-start(bf16[64,512]{1,0:T(8,128)(2,1)S(1)} %add_convert_fusion.2), channel_id=1, source_target_pairs={{0,8},{2,10},{4,12},{6,14},{8,0},{10,2},{12,4},{14,6},{1,9},{3,11}... | collective-permute-start | bytes 196616 | tf_op jit(solution)/shard_map/ppermute | solution.py:170
  52.0 6.0 %collective-permute-start.14 = (bf16[64,512]{1,0:T(8,128)(2,1)S(1)}, bf16[64,512]{1,0:T(8,128)(2,1)S(1)}, u32[]{:S(2)}, u32[]{:S(2)}) collective-permute-start(bf16[64,512]{1,0:T(8,128)(2,1)S(1)} %add_convert_fusion.3), channel_id=1, source_target_pairs={{0,8},{2,10},{4,12},{6,14},{8,0},{10,2},{12,4},{14,6},{1,9},{3,11}... | collective-permute-start | bytes 196616 | tf_op jit(solution)/shard_map/ppermute | solution.py:170
  53.1 7.1 %collective-permute-start.16 = (bf16[128,512]{1,0:T(8,128)(2,1)S(1)}, bf16[128,512]{1,0:T(8,128)(2,1)S(1)}, u32[]{:S(2)}, u32[]{:S(2)}) collective-permute-start(bf16[128,512]{1,0:T(8,128)(2,1)S(1)} %pad_maximum_fusion.1), channel_id=1, source_target_pairs={{0,2},{2,0},{4,6},{6,4},{8,10},{10,8},{12,14},{14,12},{1,3},{3,1},... | collective-permute-start | bytes 393224 | tf_op jit(solution)/shard_map/ppermute | solution.py:170
  54.7 5.5 %collective-permute-start.10 = (bf16[128,512]{1,0:T(8,128)(2,1)S(1)}, bf16[128,512]{1,0:T(8,128)(2,1)S(1)}, u32[]{:S(2)}, u32[]{:S(2)}) collective-permute-start(bf16[128,512]{1,0:T(8,128)(2,1)S(1)} %pad_maximum_fusion), channel_id=1, source_target_pairs={{0,2},{2,0},{4,6},{6,4},{8,10},{10,8},{12,14},{14,12},{1,3},{3,1},... | collective-permute-start | bytes 393224 | tf_op jit(solution)/shard_map/ppermute | solution.py:170
  58.1 4.3 %collective-permute-start.17 = (bf16[64,512]{1,0:T(8,128)(2,1)S(1)}, bf16[64,512]{1,0:T(8,128)(2,1)S(1)}, u32[]{:S(2)}, u32[]{:S(2)}) collective-permute-start(bf16[64,512]{1,0:T(8,128)(2,1)S(1)} %add_convert_fusion.1), channel_id=1, source_target_pairs={{0,4},{2,6},{4,0},{6,2},{8,12},{10,14},{12,8},{14,10},{1,5},{3,7},... | collective-permute-start | bytes 196616 | tf_op jit(solution)/shard_map/ppermute | solution.py:170
  58.5 4.7 %collective-permute-start.19 = (bf16[64,512]{1,0:T(8,128)(2,1)S(1)}, bf16[64,512]{1,0:T(8,128)(2,1)S(1)}, u32[]{:S(2)}, u32[]{:S(2)}) collective-permute-start(bf16[64,512]{1,0:T(8,128)(2,1)S(1)} %add_convert_fusion), channel_id=1, source_target_pairs={{0,4},{2,6},{4,0},{6,2},{8,12},{10,14},{12,8},{14,10},{1,5},{3,7},... | collective-permute-start | bytes 196616 | tf_op jit(solution)/shard_map/ppermute | solution.py:170
  63.2 5.0 %collective-permute-start.20 = (bf16[128,512]{1,0:T(8,128)(2,1)S(1)}, bf16[128,512]{1,0:T(8,128)(2,1)S(1)}, u32[]{:S(2)}, u32[]{:S(2)}) collective-permute-start(bf16[128,512]{1,0:T(8,128)(2,1)S(1)} %pad_maximum_fusion.3), channel_id=1, source_target_pairs={{0,2},{2,0},{4,6},{6,4},{8,10},{10,8},{12,14},{14,12},{1,3},{3,1},... | collective-permute-start | bytes 393224 | tf_op jit(solution)/shard_map/ppermute | solution.py:170
  64.8 5.0 %collective-permute-start.18 = (bf16[128,512]{1,0:T(8,128)(2,1)S(1)}, bf16[128,512]{1,0:T(8,128)(2,1)S(1)}, u32[]{:S(2)}, u32[]{:S(2)}) collective-permute-start(bf16[128,512]{1,0:T(8,128)(2,1)S(1)} %pad_maximum_fusion.2), channel_id=1, source_target_pairs={{0,2},{2,0},{4,6},{6,4},{8,10},{10,8},{12,14},{14,12},{1,3},{3,1},... | collective-permute-start | bytes 393224 | tf_op jit(solution)/shard_map/ppermute | solution.py:170
  65.5 4.5 %copy-start.3 = (s32[512]{0:T(512)S(1)}, s32[512]{0:T(512)}, u32[]{:S(2)}) copy-start(s32[512]{0:T(512)} %param.10) | copy-start | bytes 6148
  65.5 4.5 %copy-start.4 = (s32[128]{0:T(128)S(1)}, s32[128]{0:T(128)}, u32[]{:S(2)}) copy-start(s32[128]{0:T(128)} %param.11) | copy-start | bytes 1540
  70.0 1.1 %copy-start.2 = (bf16[512,1024]{1,0:T(8,128)(2,1)}, bf16[512,1024]{1,0:T(8,128)(2,1)S(1)}, u32[]{:S(2)}) copy-start(bf16[512,1024]{1,0:T(8,128)(2,1)S(1)} %maximum_dynamic-update-slice_fusion.3) | copy-start | bytes 3145732

commit v9 on v8

--- a/solution.py
+++ b/solution.py
@@ -16,6 +16,7 @@
 DEPTH_BLOCK = 512
 COLUMNS = 512
 COPY_ROWS = 32
+QUEUES = 2
 VMEM_LIMIT = 32 * 1024 * 1024
 NT = (((1,), (1,)), ((), ()))
 
@@ -102,22 +103,23 @@
 
 
 def score_kernel(
-    rows_ref, left_ref, right_ref, store_ref, *refs,
+    fetch, rows_ref, left_ref, right_ref, store_ref, *refs,
 ):
     *out_refs, left_vmem, right_vmem, rows_vmem, store_vmem, half_ref, total_ref = refs[:-4]
     left_sems, right_sems, rows_sems, store_sems = refs[-4:]
     heads = (
         copies_of(right_ref, right_vmem, right_sems)
         + copies_of(left_ref, left_vmem, left_sems)
-        + copies_of(rows_ref, rows_vmem, rows_sems)
+        + (copies_of(rows_ref, rows_vmem, rows_sems) if fetch else [])
     )
     copies = copies_of(store_ref, store_vmem, store_sems)
-    for copy in heads + copies:
-        copy.start()
+    for k, copy in enumerate(heads + copies):
+        copy.start(priority=k % QUEUES)
     for copy in heads:
         copy.wait()
     pre_ref = rows_vmem
-    precondition(rows_vmem, left_vmem[...], right_vmem[...], half_ref, pre_ref)
+    given_ref = rows_vmem if fetch else rows_ref.at[0]
+    precondition(given_ref, left_vmem[...], right_vmem[...], half_ref, pre_ref)
     share = len(copies) // len(out_refs)
     columns = total_ref.shape[0]
     for k, out_ref in enumerate(out_refs):
@@ -128,21 +130,24 @@
 
 VMEM = pl.BlockSpec(memory_space=pltpu.VMEM)
 HBM = pl.BlockSpec(memory_space=pltpu.HBM)
-ANYWHERE = pl.BlockSpec(memory_space=pl.ANY)
 
 
 def in_hbm(array):
     return pltpu.with_memory_space_constraint(array, pltpu.HBM)
 
 
-def score(queries, left_inv, right_inv, store, columns):
+def in_vmem(array):
+    return pltpu.with_memory_space_constraint(array, pltpu.VMEM)
+
+
+def score(queries, fetch, left_inv, right_inv, store, columns):
     count, depth = queries.shape[1:]
     examples = store.shape[1]
     blocks = examples // columns
     return pl.pallas_call(
-        score_kernel,
+        functools.partial(score_kernel, fetch),
         out_shape=(pltpu.VMEM((count, columns), jnp.float32),) * blocks,
-        in_specs=[ANYWHERE] + [HBM] * 3,
+        in_specs=[HBM if fetch else VMEM] + [HBM] * 3,
         out_specs=(VMEM,) * blocks,
         scratch_shapes=[
             pltpu.VMEM((KIN, KIN), jnp.bfloat16),
@@ -162,7 +167,7 @@
             bytes_accessed=2 * depth * (2 * count + examples),
             transcendentals=0,
         ),
-    )(queries, *map(in_hbm, (left_inv, right_inv, store)))
+    )(in_hbm(queries) if fetch else in_vmem(queries), *map(in_hbm, (left_inv, right_inv, store)))
 
 
 def swap(block, bit):
@@ -271,8 +276,8 @@
 
             def make(order, number=number, step=step, current=current, made=made):
                 if number == 0:
-                    block = order.after(current) if step else in_hbm(current)
-                    made.extend(score(block, left_inv, right_inv, store, width))
+                    block = order.after(current) if step else current
+                    made.extend(score(block, step == 0, left_inv, right_inv, store, width))
                     if step:
                         made[0] = order.mark(made[0])
                 return made[number]

time: 71.2 us -> 73.6 us (1.034)
  Pallas kernels: 19.5 us -> 22 us
    pallas_call x2, Pallas kernels: 19.5 us -> 22 us  [score(): pl.pallas_call(functools.partial(score_kernel, fetch), out_shape=(pltpu.V...]
  transfers between devices with their start and end apart: 21 -> 21, of which waited for: 11 -> 11; matrix products, arithmetic and copies ran while one was open for 2% -> 2% of each run, Pallas kernels for 27% -> 30%
where the time goes in v9:
time: 73.6 us; the launch traced here: 73.4 us
  starting transfers between devices  24.7 us (34%)
  Pallas kernels  22 us (30%)
  waiting for transfers between devices  20.3 us (28%)
  local copies, waits for them, and re-layouts  3.89 us (5%)
  matrix products  1.07 us (1%)
  between operations  0.92 us (1%)
    ppermute x20, starting transfers between devices, swap(): return lax.ppermute(block, 'layer', route)  24.2 us
    pallas_call x2, Pallas kernels, score(): pl.pallas_call(functools.partial(score_kernel, fetch), out_shape=(pltpu.V...  22 us
    ppermute x20, waiting for transfers between devices, swap(): return lax.ppermute(block, 'layer', route)  20.3 us
    unnamed x10, local copies, waits for them, and re-layouts  2.96 us
  transfers between devices with their start and end apart: 21, of which 11 were waited for; matrix products, arithmetic and copies ran while one was open for 2% of the time, Pallas kernels for 30%

profile of v9, /device:TPU:0, one launch (start us, length us, event | category | flops | bytes accessed | tf_op | source)
XLA Modules:
  0.0 73.4 jit_solution(6042272486350313856)
XLA Ops:
  0.6 0.5 collective-permute-start.1
  1.1 11.4 %shard_map.77 = (f32[256,512]{1,0:T(8,128)S(1)}, f32[256,512]{1,0:T(8,128)S(1)}) custom-call(bf16[1,256,4096]{2,1,0:T(8,128)(2,1)} %rows_ref.1, bf16[1,32,32]{2,1,0:T(8,128)(2,1)} %left_ref.3, bf16[1,128,128]{2,1,0:T(8,128)(2,1)} %right_ref.3, bf16[1,1024,4096]{2,1,0:T(8,128)(2,1)} %store_ref.3), custom_call_target="tpu_custom_call" | custom-call | flops 4294967296 | bytes 12582912 | tf_op jit(solution)/shard_map/pallas_call | solution.py:147
  12.6 2.6 %collective-permute-start = (bf16[128,512]{1,0:T(8,128)(2,1)S(1)}, bf16[128,512]{1,0:T(8,128)(2,1)S(1)}, u32[]{:S(2)}, u32[]{:S(2)}) collective-permute-start(bf16[128,512]{1,0:T(8,128)(2,1)S(1)} %dynamic-slice_convert_fusion.3), channel_id=1, source_target_pairs={{0,2},{2,0},{4,6},{6,4},{8,10},{10,8},{12,14},{14,12},{1,3},{3,1},... | collective-permute-start | bytes 393224 | tf_op jit(solution)/shard_map/ppermute | solution.py:175
  15.2 0.7 dynamic-slice_convert_fusion.2
  15.8 0.0 collective-permute-start.3
  15.9 0.0 collective-permute-done.1.rows_ref
  15.9 0.0 copy-start
  15.9 1.4 %copy-done = bf16[1,256,4096]{2,1,0:T(8,128)(2,1)} copy-done((bf16[1,256,4096]{2,1,0:T(8,128)(2,1)}, bf16[1,256,4096]{2,1,0:T(8,128)(2,1)S(1)}, u32[]{:S(2)}) %copy-start) | copy-done | bytes 2097176
  17.2 0.0 copy-start.1
  17.2 1.6 %copy-done.1 = bf16[1,256,4096]{2,1,0:T(8,128)(2,1)S(1)} copy-done((bf16[1,256,4096]{2,1,0:T(8,128)(2,1)S(1)}, bf16[1,256,4096]{2,1,0:T(8,128)(2,1)}, u32[]{:S(2)}) %copy-start.1) | copy-done | bytes 2097176
  18.8 10.6 %shard_map.78 = (f32[256,512]{1,0:T(8,128)S(1)}, f32[256,512]{1,0:T(8,128)S(1)}) custom-call(bf16[1,256,4096]{2,1,0:T(8,128)(2,1)S(1)} %copy-done.1, bf16[1,32,32]{2,1,0:T(8,128)(2,1)} %left_ref.3, bf16[1,128,128]{2,1,0:T(8,128)(2,1)} %right_ref.3, bf16[1,1024,4096]{2,1,0:T(8,128)(2,1)} %store_ref.3), custom_call_target="tpu_custom_call" | custom-call | flops 4294967296 | bytes 12582912 | tf_op jit(solution)/shard_map/pallas_call | solution.py:147
  29.4 0.0 collective-permute-done
  29.4 0.0 collective-permute-done.3
  29.4 0.1 convert_add_fusion.2
  29.6 2.1 %collective-permute-start.2 = (bf16[64,512]{1,0:T(8,128)(2,1)S(1)}, bf16[64,512]{1,0:T(8,128)(2,1)S(1)}, u32[]{:S(2)}, u32[]{:S(2)}) collective-permute-start(bf16[64,512]{1,0:T(8,128)(2,1)S(1)} %dynamic-slice_convert_fusion.7), channel_id=1, source_target_pairs={{0,4},{2,6},{4,0},{6,2},{8,12},{10,14},{12,8},{14,10},{1,5},{3,7},... | collective-permute-start | bytes 196616 | tf_op jit(solution)/shard_map/ppermute | solution.py:175
  31.7 0.1 collective-permute-start.5
  31.8 2.2 %collective-permute-done.2 = bf16[64,512]{1,0:T(8,128)(2,1)S(1)} collective-permute-done((bf16[64,512]{1,0:T(8,128)(2,1)S(1)}, bf16[64,512]{1,0:T(8,128)(2,1)S(1)}, u32[]{:S(2)}, u32[]{:S(2)}) %collective-permute-start.2) | collective-permute-done | bytes 65568 | tf_op jit(solution)/shard_map/ppermute | solution.py:175
  34.0 2.0 %collective-permute-done.5 = bf16[64,512]{1,0:T(8,128)(2,1)S(1)} collective-permute-done((bf16[64,512]{1,0:T(8,128)(2,1)S(1)}, bf16[64,512]{1,0:T(8,128)(2,1)S(1)}, u32[]{:S(2)}, u32[]{:S(2)}) %collective-permute-start.5) | collective-permute-done | bytes 65568 | tf_op jit(solution)/shard_map/ppermute | solution.py:175
  36.0 2.7 %collective-permute-start.9 = (bf16[64,512]{1,0:T(8,128)(2,1)S(1)}, bf16[64,512]{1,0:T(8,128)(2,1)S(1)}, u32[]{:S(2)}, u32[]{:S(2)}) collective-permute-start(bf16[64,512]{1,0:T(8,128)(2,1)S(1)} %add_convert_fusion.5), channel_id=1, source_target_pairs={{0,8},{2,10},{4,12},{6,14},{8,0},{10,2},{12,4},{14,6},{1,9},{3,11}... | collective-permute-start | bytes 196616 | tf_op jit(solution)/shard_map/ppermute | solution.py:175
  38.6 0.4 collective-permute-start.4
  39.1 1.6 %collective-permute-start.8 = (bf16[128,512]{1,0:T(8,128)(2,1)S(1)}, bf16[128,512]{1,0:T(8,128)(2,1)S(1)}, u32[]{:S(2)}, u32[]{:S(2)}) collective-permute-start(bf16[128,512]{1,0:T(8,128)(2,1)S(1)} %get-tuple-element.89), channel_id=1, source_target_pairs={{0,2},{2,0},{4,6},{6,4},{8,10},{10,8},{12,14},{14,12},{1,3},{3,1},... | collective-permute-start | bytes 393224 | tf_op jit(solution)/shard_map/ppermute | solution.py:175
  40.7 0.5 collective-permute-start.7
  41.2 3.5 %collective-permute-done.4 = bf16[64,512]{1,0:T(8,128)(2,1)S(1)} collective-permute-done((bf16[64,512]{1,0:T(8,128)(2,1)S(1)}, bf16[64,512]{1,0:T(8,128)(2,1)S(1)}, u32[]{:S(2)}, u32[]{:S(2)}) %collective-permute-start.4) | collective-permute-done | bytes 65568 | tf_op jit(solution)/shard_map/ppermute | solution.py:175
  44.7 0.0 collective-permute-done.9
  44.7 0.4 collective-permute-start.13
  45.1 0.0 collective-permute-done.8
  45.1 0.6 collective-permute-done.7
  45.8 1.2 %collective-permute-start.6 = (bf16[64,512]{1,0:T(8,128)(2,1)S(1)}, bf16[64,512]{1,0:T(8,128)(2,1)S(1)}, u32[]{:S(2)}, u32[]{:S(2)}) collective-permute-start(bf16[64,512]{1,0:T(8,128)(2,1)S(1)} %add_convert_fusion.6), channel_id=1, source_target_pairs={{0,4},{2,6},{4,0},{6,2},{8,12},{10,14},{12,8},{14,10},{1,5},{3,7},... | collective-permute-start | bytes 196616 | tf_op jit(solution)/shard_map/ppermute | solution.py:175
  47.1 0.9 %collective-permute-start.12 = (bf16[64,512]{1,0:T(8,128)(2,1)S(1)}, bf16[64,512]{1,0:T(8,128)(2,1)S(1)}, u32[]{:S(2)}, u32[]{:S(2)}) collective-permute-start(bf16[64,512]{1,0:T(8,128)(2,1)S(1)} %dynamic-slice_convert_fusion.4), channel_id=1, source_target_pairs={{0,4},{2,6},{4,0},{6,2},{8,12},{10,14},{12,8},{14,10},{1,5},{3,7},... | collective-permute-start | bytes 196616 | tf_op jit(solution)/shard_map/ppermute | solution.py:175
  48.1 1.2 %collective-permute-start.11 = (bf16[64,512]{1,0:T(8,128)(2,1)S(1)}, bf16[64,512]{1,0:T(8,128)(2,1)S(1)}, u32[]{:S(2)}, u32[]{:S(2)}) collective-permute-start(bf16[64,512]{1,0:T(8,128)(2,1)S(1)} %dynamic-slice_convert_fusion.5), channel_id=1, source_target_pairs={{0,4},{2,6},{4,0},{6,2},{8,12},{10,14},{12,8},{14,10},{1,5},{3,7},... | collective-permute-start | bytes 196616 | tf_op jit(solution)/shard_map/ppermute | solution.py:175
  49.3 1.4 %collective-permute-done.6 = bf16[64,512]{1,0:T(8,128)(2,1)S(1)} collective-permute-done((bf16[64,512]{1,0:T(8,128)(2,1)S(1)}, bf16[64,512]{1,0:T(8,128)(2,1)S(1)}, u32[]{:S(2)}, u32[]{:S(2)}) %collective-permute-start.6) | collective-permute-done | bytes 65568 | tf_op jit(solution)/shard_map/ppermute | solution.py:175
  50.7 0.0 collective-permute-done.13
  50.7 0.7 collective-permute-done.12
  51.4 3.0 %collective-permute-start.15 = (bf16[64,512]{1,0:T(8,128)(2,1)S(1)}, bf16[64,512]{1,0:T(8,128)(2,1)S(1)}, u32[]{:S(2)}, u32[]{:S(2)}) collective-permute-start(bf16[64,512]{1,0:T(8,128)(2,1)S(1)} %add_convert_fusion.2), channel_id=1, source_target_pairs={{0,8},{2,10},{4,12},{6,14},{8,0},{10,2},{12,4},{14,6},{1,9},{3,11}... | collective-permute-start | bytes 196616 | tf_op jit(solution)/shard_map/ppermute | solution.py:175
  54.4 0.0 collective-permute-done.11
  54.4 1.1 %collective-permute-start.14 = (bf16[64,512]{1,0:T(8,128)(2,1)S(1)}, bf16[64,512]{1,0:T(8,128)(2,1)S(1)}, u32[]{:S(2)}, u32[]{:S(2)}) collective-permute-start(bf16[64,512]{1,0:T(8,128)(2,1)S(1)} %add_convert_fusion.3), channel_id=1, source_target_pairs={{0,8},{2,10},{4,12},{6,14},{8,0},{10,2},{12,4},{14,6},{1,9},{3,11}... | collective-permute-start | bytes 196616 | tf_op jit(solution)/shard_map/ppermute | solution.py:175
  55.5 1.6 %collective-permute-start.16 = (bf16[128,512]{1,0:T(8,128)(2,1)S(1)}, bf16[128,512]{1,0:T(8,128)(2,1)S(1)}, u32[]{:S(2)}, u32[]{:S(2)}) collective-permute-start(bf16[128,512]{1,0:T(8,128)(2,1)S(1)} %pad_maximum_fusion.1), channel_id=1, source_target_pairs={{0,2},{2,0},{4,6},{6,4},{8,10},{10,8},{12,14},{14,12},{1,3},{3,1},... | collective-permute-start | bytes 393224 | tf_op jit(solution)/shard_map/ppermute | solution.py:175
  57.1 0.6 collective-permute-start.10
  57.7 0.0 collective-permute-done.15
  57.7 2.7 %collective-permute-done.14 = bf16[64,512]{1,0:T(8,128)(2,1)S(1)} collective-permute-done((bf16[64,512]{1,0:T(8,128)(2,1)S(1)}, bf16[64,512]{1,0:T(8,128)(2,1)S(1)}, u32[]{:S(2)}, u32[]{:S(2)}) %collective-permute-start.14) | collective-permute-done | bytes 65568 | tf_op jit(solution)/shard_map/ppermute | solution.py:175
  60.5 0.4 collective-permute-start.17
  60.9 1.7 %collective-permute-start.19 = (bf16[64,512]{1,0:T(8,128)(2,1)S(1)}, bf16[64,512]{1,0:T(8,128)(2,1)S(1)}, u32[]{:S(2)}, u32[]{:S(2)}) collective-permute-start(bf16[64,512]{1,0:T(8,128)(2,1)S(1)} %add_convert_fusion), channel_id=1, source_target_pairs={{0,4},{2,6},{4,0},{6,2},{8,12},{10,14},{12,8},{14,10},{1,5},{3,7},... | collective-permute-start | bytes 196616 | tf_op jit(solution)/shard_map/ppermute | solution.py:175
  62.6 0.0 collective-permute-done.10
  62.6 0.0 collective-permute-done.16
  62.6 2.2 %collective-permute-done.17 = bf16[64,512]{1,0:T(8,128)(2,1)S(1)} collective-permute-done((bf16[64,512]{1,0:T(8,128)(2,1)S(1)}, bf16[64,512]{1,0:T(8,128)(2,1)S(1)}, u32[]{:S(2)}, u32[]{:S(2)}) %collective-permute-start.17) | collective-permute-done | bytes 65568 | tf_op jit(solution)/shard_map/ppermute | solution.py:175
  64.8 0.7 collective-permute-done.19
  65.6 1.6 %collective-permute-start.20 = (bf16[128,512]{1,0:T(8,128)(2,1)S(1)}, bf16[128,512]{1,0:T(8,128)(2,1)S(1)}, u32[]{:S(2)}, u32[]{:S(2)}) collective-permute-start(bf16[128,512]{1,0:T(8,128)(2,1)S(1)} %pad_maximum_fusion.3), channel_id=1, source_target_pairs={{0,2},{2,0},{4,6},{6,4},{8,10},{10,8},{12,14},{14,12},{1,3},{3,1},... | collective-permute-start | bytes 393224 | tf_op jit(solution)/shard_map/ppermute | solution.py:175
  67.2 0.6 collective-permute-start.18
  67.9 0.0 copy-start.3
  67.9 0.0 copy-start.4
  67.9 0.1 broadcast_in_dim.2
  68.1 2.5 %collective-permute-done.20 = bf16[128,512]{1,0:T(8,128)(2,1)S(1)} collective-permute-done((bf16[128,512]{1,0:T(8,128)(2,1)S(1)}, bf16[128,512]{1,0:T(8,128)(2,1)S(1)}, u32[]{:S(2)}, u32[]{:S(2)}) %collective-permute-start.20) | collective-permute-done | bytes 131104 | tf_op jit(solution)/shard_map/ppermute | solution.py:175
  70.6 1.6 %collective-permute-done.18 = bf16[128,512]{1,0:T(8,128)(2,1)S(1)} collective-permute-done((bf16[128,512]{1,0:T(8,128)(2,1)S(1)}, bf16[128,512]{1,0:T(8,128)(2,1)S(1)}, u32[]{:S(2)}, u32[]{:S(2)}) %collective-permute-start.18) | collective-permute-done | bytes 131104 | tf_op jit(solution)/shard_map/ppermute | solution.py:175
  72.3 0.0 copy-done.3
  72.3 0.0 copy-done.4
  72.4 0.0 copy-start.2
  72.4 1.1 %convolution_convert_fusion = bf16[128,1024]{1,0:T(8,128)(2,1)} fusion(bf16[512,1024]{1,0:T(8,128)(2,1)S(1)} %maximum_dynamic-update-slice_fusion.3, s32[512]{0:T(512)S(1)} %copy-done.3, s32[128]{0:T(128)S(1)} %copy-done.4), kind=kOutput, calls=%fused_computation | convolution fusion | flops 134742016 | bytes 1313280 | tf_op jit(solution)/shard_map/dot_general | solution.py:298
  73.4 0.0 copy-done.2
  (32 shorter events, 0.7 us)
Async XLA Ops:
  0.6 15.2 %collective-permute-start.1 = (bf16[1,256,4096]{2,1,0:T(8,128)(2,1)}, bf16[1,256,4096]{2,1,0:T(8,128)(2,1)S(1)}, u32[]{:S(2)}, u32[]{:S(2)}) collective-permute-start(bf16[1,256,4096]{2,1,0:T(8,128)(2,1)} %rows_ref.1), channel_id=1, source_target_pairs={{1,0},{0,1},{3,2},{2,3},{5,4},{4,5},{7,6},{6,7},{9,8},{8,9},{11,10... | collective-permute-start | bytes 6291464 | tf_op jit(solution)/shard_map/ppermute | solution.py:273
  12.6 16.8 %collective-permute-start = (bf16[128,512]{1,0:T(8,128)(2,1)S(1)}, bf16[128,512]{1,0:T(8,128)(2,1)S(1)}, u32[]{:S(2)}, u32[]{:S(2)}) collective-permute-start(bf16[128,512]{1,0:T(8,128)(2,1)S(1)} %dynamic-slice_convert_fusion.3), channel_id=1, source_target_pairs={{0,2},{2,0},{4,6},{6,4},{8,10},{10,8},{12,14},{14,12},{1,3},{3,1},... | collective-permute-start | bytes 393224 | tf_op jit(solution)/shard_map/ppermute | solution.py:175
  15.8 13.6 %collective-permute-start.3 = (bf16[128,512]{1,0:T(8,128)(2,1)}, bf16[128,512]{1,0:T(8,128)(2,1)S(1)}, u32[]{:S(2)}, u32[]{:S(2)}) collective-permute-start(bf16[128,512]{1,0:T(8,128)(2,1)} %dynamic-slice_convert_fusion.2), channel_id=1, source_target_pairs={{0,2},{2,0},{4,6},{6,4},{8,10},{10,8},{12,14},{14,12},{1,3},{3,1},... | collective-permute-start | bytes 393224 | tf_op jit(solution)/shard_map/ppermute | solution.py:175
  15.9 1.4 %copy-start = (bf16[1,256,4096]{2,1,0:T(8,128)(2,1)}, bf16[1,256,4096]{2,1,0:T(8,128)(2,1)S(1)}, u32[]{:S(2)}) copy-start(bf16[1,256,4096]{2,1,0:T(8,128)(2,1)S(1)} %collective-permute-done.1.rows_ref) | copy-start | bytes 6291460
  17.2 1.6 %copy-start.1 = (bf16[1,256,4096]{2,1,0:T(8,128)(2,1)S(1)}, bf16[1,256,4096]{2,1,0:T(8,128)(2,1)}, u32[]{:S(2)}) copy-start(bf16[1,256,4096]{2,1,0:T(8,128)(2,1)} %copy-done) | copy-start | bytes 6291460
  29.6 4.4 %collective-permute-start.2 = (bf16[64,512]{1,0:T(8,128)(2,1)S(1)}, bf16[64,512]{1,0:T(8,128)(2,1)S(1)}, u32[]{:S(2)}, u32[]{:S(2)}) collective-permute-start(bf16[64,512]{1,0:T(8,128)(2,1)S(1)} %dynamic-slice_convert_fusion.7), channel_id=1, source_target_pairs={{0,4},{2,6},{4,0},{6,2},{8,12},{10,14},{12,8},{14,10},{1,5},{3,7},... | collective-permute-start | bytes 196616 | tf_op jit(solution)/shard_map/ppermute | solution.py:175
  31.7 4.3 %collective-permute-start.5 = (bf16[64,512]{1,0:T(8,128)(2,1)S(1)}, bf16[64,512]{1,0:T(8,128)(2,1)S(1)}, u32[]{:S(2)}, u32[]{:S(2)}) collective-permute-start(bf16[64,512]{1,0:T(8,128)(2,1)S(1)} %dynamic-slice_convert_fusion.6), channel_id=1, source_target_pairs={{0,4},{2,6},{4,0},{6,2},{8,12},{10,14},{12,8},{14,10},{1,5},{3,7},... | collective-permute-start | bytes 196616 | tf_op jit(solution)/shard_map/ppermute | solution.py:175
  36.0 8.7 %collective-permute-start.9 = (bf16[64,512]{1,0:T(8,128)(2,1)S(1)}, bf16[64,512]{1,0:T(8,128)(2,1)S(1)}, u32[]{:S(2)}, u32[]{:S(2)}) collective-permute-start(bf16[64,512]{1,0:T(8,128)(2,1)S(1)} %add_convert_fusion.5), channel_id=1, source_target_pairs={{0,8},{2,10},{4,12},{6,14},{8,0},{10,2},{12,4},{14,6},{1,9},{3,11}... | collective-permute-start | bytes 196616 | tf_op jit(solution)/shard_map/ppermute | solution.py:175
  38.6 6.1 %collective-permute-start.4 = (bf16[64,512]{1,0:T(8,128)(2,1)S(1)}, bf16[64,512]{1,0:T(8,128)(2,1)S(1)}, u32[]{:S(2)}, u32[]{:S(2)}) collective-permute-start(bf16[64,512]{1,0:T(8,128)(2,1)S(1)} %add_convert_fusion.7), channel_id=1, source_target_pairs={{0,8},{2,10},{4,12},{6,14},{8,0},{10,2},{12,4},{14,6},{1,9},{3,11}... | collective-permute-start | bytes 196616 | tf_op jit(solution)/shard_map/ppermute | solution.py:175
  39.1 6.0 %collective-permute-start.8 = (bf16[128,512]{1,0:T(8,128)(2,1)S(1)}, bf16[128,512]{1,0:T(8,128)(2,1)S(1)}, u32[]{:S(2)}, u32[]{:S(2)}) collective-permute-start(bf16[128,512]{1,0:T(8,128)(2,1)S(1)} %get-tuple-element.89), channel_id=1, source_target_pairs={{0,2},{2,0},{4,6},{6,4},{8,10},{10,8},{12,14},{14,12},{1,3},{3,1},... | collective-permute-start | bytes 393224 | tf_op jit(solution)/shard_map/ppermute | solution.py:175
  40.7 5.1 %collective-permute-start.7 = (bf16[128,512]{1,0:T(8,128)(2,1)S(1)}, bf16[128,512]{1,0:T(8,128)(2,1)S(1)}, u32[]{:S(2)}, u32[]{:S(2)}) collective-permute-start(bf16[128,512]{1,0:T(8,128)(2,1)S(1)} %get-tuple-element.87), channel_id=1, source_target_pairs={{0,2},{2,0},{4,6},{6,4},{8,10},{10,8},{12,14},{14,12},{1,3},{3,1},... | collective-permute-start | bytes 393224 | tf_op jit(solution)/shard_map/ppermute | solution.py:175
  44.7 5.9 %collective-permute-start.13 = (bf16[64,512]{1,0:T(8,128)(2,1)S(1)}, bf16[64,512]{1,0:T(8,128)(2,1)S(1)}, u32[]{:S(2)}, u32[]{:S(2)}) collective-permute-start(bf16[64,512]{1,0:T(8,128)(2,1)S(1)} %add_convert_fusion.4), channel_id=1, source_target_pairs={{0,4},{2,6},{4,0},{6,2},{8,12},{10,14},{12,8},{14,10},{1,5},{3,7},... | collective-permute-start | bytes 196616 | tf_op jit(solution)/shard_map/ppermute | solution.py:175
  45.8 4.9 %collective-permute-start.6 = (bf16[64,512]{1,0:T(8,128)(2,1)S(1)}, bf16[64,512]{1,0:T(8,128)(2,1)S(1)}, u32[]{:S(2)}, u32[]{:S(2)}) collective-permute-start(bf16[64,512]{1,0:T(8,128)(2,1)S(1)} %add_convert_fusion.6), channel_id=1, source_target_pairs={{0,4},{2,6},{4,0},{6,2},{8,12},{10,14},{12,8},{14,10},{1,5},{3,7},... | collective-permute-start | bytes 196616 | tf_op jit(solution)/shard_map/ppermute | solution.py:175
  47.1 4.3 %collective-permute-start.12 = (bf16[64,512]{1,0:T(8,128)(2,1)S(1)}, bf16[64,512]{1,0:T(8,128)(2,1)S(1)}, u32[]{:S(2)}, u32[]{:S(2)}) collective-permute-start(bf16[64,512]{1,0:T(8,128)(2,1)S(1)} %dynamic-slice_convert_fusion.4), channel_id=1, source_target_pairs={{0,4},{2,6},{4,0},{6,2},{8,12},{10,14},{12,8},{14,10},{1,5},{3,7},... | collective-permute-start | bytes 196616 | tf_op jit(solution)/shard_map/ppermute | solution.py:175
  48.1 6.3 %collective-permute-start.11 = (bf16[64,512]{1,0:T(8,128)(2,1)S(1)}, bf16[64,512]{1,0:T(8,128)(2,1)S(1)}, u32[]{:S(2)}, u32[]{:S(2)}) collective-permute-start(bf16[64,512]{1,0:T(8,128)(2,1)S(1)} %dynamic-slice_convert_fusion.5), channel_id=1, source_target_pairs={{0,4},{2,6},{4,0},{6,2},{8,12},{10,14},{12,8},{14,10},{1,5},{3,7},... | collective-permute-start | bytes 196616 | tf_op jit(solution)/shard_map/ppermute | solution.py:175
  51.4 6.3 %collective-permute-start.15 = (bf16[64,512]{1,0:T(8,128)(2,1)S(1)}, bf16[64,512]{1,0:T(8,128)(2,1)S(1)}, u32[]{:S(2)}, u32[]{:S(2)}) collective-permute-start(bf16[64,512]{1,0:T(8,128)(2,1)S(1)} %add_convert_fusion.2), channel_id=1, source_target_pairs={{0,8},{2,10},{4,12},{6,14},{8,0},{10,2},{12,4},{14,6},{1,9},{3,11}... | collective-permute-start | bytes 196616 | tf_op jit(solution)/shard_map/ppermute | solution.py:175
  54.4 6.0 %collective-permute-start.14 = (bf16[64,512]{1,0:T(8,128)(2,1)S(1)}, bf16[64,512]{1,0:T(8,128)(2,1)S(1)}, u32[]{:S(2)}, u32[]{:S(2)}) collective-permute-start(bf16[64,512]{1,0:T(8,128)(2,1)S(1)} %add_convert_fusion.3), channel_id=1, source_target_pairs={{0,8},{2,10},{4,12},{6,14},{8,0},{10,2},{12,4},{14,6},{1,9},{3,11}... | collective-permute-start | bytes 196616 | tf_op jit(solution)/shard_map/ppermute | solution.py:175
  55.5 7.1 %collective-permute-start.16 = (bf16[128,512]{1,0:T(8,128)(2,1)S(1)}, bf16[128,512]{1,0:T(8,128)(2,1)S(1)}, u32[]{:S(2)}, u32[]{:S(2)}) collective-permute-start(bf16[128,512]{1,0:T(8,128)(2,1)S(1)} %pad_maximum_fusion.1), channel_id=1, source_target_pairs={{0,2},{2,0},{4,6},{6,4},{8,10},{10,8},{12,14},{14,12},{1,3},{3,1},... | collective-permute-start | bytes 393224 | tf_op jit(solution)/shard_map/ppermute | solution.py:175
  57.1 5.5 %collective-permute-start.10 = (bf16[128,512]{1,0:T(8,128)(2,1)S(1)}, bf16[128,512]{1,0:T(8,128)(2,1)S(1)}, u32[]{:S(2)}, u32[]{:S(2)}) collective-permute-start(bf16[128,512]{1,0:T(8,128)(2,1)S(1)} %pad_maximum_fusion), channel_id=1, source_target_pairs={{0,2},{2,0},{4,6},{6,4},{8,10},{10,8},{12,14},{14,12},{1,3},{3,1},... | collective-permute-start | bytes 393224 | tf_op jit(solution)/shard_map/ppermute | solution.py:175
  60.5 4.3 %collective-permute-start.17 = (bf16[64,512]{1,0:T(8,128)(2,1)S(1)}, bf16[64,512]{1,0:T(8,128)(2,1)S(1)}, u32[]{:S(2)}, u32[]{:S(2)}) collective-permute-start(bf16[64,512]{1,0:T(8,128)(2,1)S(1)} %add_convert_fusion.1), channel_id=1, source_target_pairs={{0,4},{2,6},{4,0},{6,2},{8,12},{10,14},{12,8},{14,10},{1,5},{3,7},... | collective-permute-start | bytes 196616 | tf_op jit(solution)/shard_map/ppermute | solution.py:175
  60.9 4.6 %collective-permute-start.19 = (bf16[64,512]{1,0:T(8,128)(2,1)S(1)}, bf16[64,512]{1,0:T(8,128)(2,1)S(1)}, u32[]{:S(2)}, u32[]{:S(2)}) collective-permute-start(bf16[64,512]{1,0:T(8,128)(2,1)S(1)} %add_convert_fusion), channel_id=1, source_target_pairs={{0,4},{2,6},{4,0},{6,2},{8,12},{10,14},{12,8},{14,10},{1,5},{3,7},... | collective-permute-start | bytes 196616 | tf_op jit(solution)/shard_map/ppermute | solution.py:175
  65.6 5.0 %collective-permute-start.20 = (bf16[128,512]{1,0:T(8,128)(2,1)S(1)}, bf16[128,512]{1,0:T(8,128)(2,1)S(1)}, u32[]{:S(2)}, u32[]{:S(2)}) collective-permute-start(bf16[128,512]{1,0:T(8,128)(2,1)S(1)} %pad_maximum_fusion.3), channel_id=1, source_target_pairs={{0,2},{2,0},{4,6},{6,4},{8,10},{10,8},{12,14},{14,12},{1,3},{3,1},... | collective-permute-start | bytes 393224 | tf_op jit(solution)/shard_map/ppermute | solution.py:175
  67.2 5.0 %collective-permute-start.18 = (bf16[128,512]{1,0:T(8,128)(2,1)S(1)}, bf16[128,512]{1,0:T(8,128)(2,1)S(1)}, u32[]{:S(2)}, u32[]{:S(2)}) collective-permute-start(bf16[128,512]{1,0:T(8,128)(2,1)S(1)} %pad_maximum_fusion.2), channel_id=1, source_target_pairs={{0,2},{2,0},{4,6},{6,4},{8,10},{10,8},{12,14},{14,12},{1,3},{3,1},... | collective-permute-start | bytes 393224 | tf_op jit(solution)/shard_map/ppermute | solution.py:175
  67.9 4.5 %copy-start.3 = (s32[512]{0:T(512)S(1)}, s32[512]{0:T(512)}, u32[]{:S(2)}) copy-start(s32[512]{0:T(512)} %param.10) | copy-start | bytes 6148
  67.9 4.5 %copy-start.4 = (s32[128]{0:T(128)S(1)}, s32[128]{0:T(128)}, u32[]{:S(2)}) copy-start(s32[128]{0:T(128)} %param.11) | copy-start | bytes 1540
  72.4 1.1 %copy-start.2 = (bf16[512,1024]{1,0:T(8,128)(2,1)}, bf16[512,1024]{1,0:T(8,128)(2,1)S(1)}, u32[]{:S(2)}) copy-start(bf16[512,1024]{1,0:T(8,128)(2,1)S(1)} %maximum_dynamic-update-slice_fusion.3) | copy-start | bytes 3145732

commit v10 on v8

--- a/solution.py
+++ b/solution.py
@@ -15,8 +15,7 @@
 PAIR = 2 * KOUT
 DEPTH_BLOCK = 512
 COLUMNS = 512
-COPY_ROWS = 32
-VMEM_LIMIT = 32 * 1024 * 1024
+VMEM_LIMIT = 28 * 1024 * 1024
 NT = (((1,), (1,)), ((), ()))
 
 
@@ -91,78 +90,70 @@
             out_ref[...] = (total_ref[...] + term).T
 
 
-def copies_of(source_ref, target_ref, sems):
-    rows = target_ref.shape[0] // sems.shape[0]
-    return [
-        pltpu.make_async_copy(
-            source_ref.at[0, pl.ds(k * rows, rows)], target_ref.at[pl.ds(k * rows, rows)], sems.at[k]
-        )
-        for k in range(sems.shape[0])
+def precondition_kernel(rows_ref, left_ref, right_ref, pre_ref, left_vmem, right_vmem, half_ref, sems):
+    heads = [
+        pltpu.make_async_copy(source.at[0], target, sems.at[k])
+        for k, (source, target) in enumerate(((right_ref, right_vmem), (left_ref, left_vmem)))
     ]
-
-
-def score_kernel(
-    rows_ref, left_ref, right_ref, store_ref, *refs,
-):
-    *out_refs, left_vmem, right_vmem, rows_vmem, store_vmem, half_ref, total_ref = refs[:-4]
-    left_sems, right_sems, rows_sems, store_sems = refs[-4:]
-    heads = (
-        copies_of(right_ref, right_vmem, right_sems)
-        + copies_of(left_ref, left_vmem, left_sems)
-        + copies_of(rows_ref, rows_vmem, rows_sems)
-    )
-    copies = copies_of(store_ref, store_vmem, store_sems)
-    for copy in heads + copies:
+    for copy in heads:
         copy.start()
     for copy in heads:
         copy.wait()
-    pre_ref = rows_vmem
-    precondition(rows_vmem, left_vmem[...], right_vmem[...], half_ref, pre_ref)
-    share = len(copies) // len(out_refs)
+    precondition(rows_ref.at[0], left_vmem[...], right_vmem[...], half_ref, pre_ref)
+
+
+def score_kernel(pre_ref, store_ref, *refs):
+    *out_refs, total_ref = refs
     columns = total_ref.shape[0]
     for k, out_ref in enumerate(out_refs):
-        for copy in copies[k * share : (k + 1) * share]:
-            copy.wait()
-        dot(pre_ref, store_vmem, k * columns, total_ref, out_ref)
+        dot(pre_ref, store_ref.at[0], k * columns, total_ref, out_ref)
 
 
 VMEM = pl.BlockSpec(memory_space=pltpu.VMEM)
 HBM = pl.BlockSpec(memory_space=pltpu.HBM)
-ANYWHERE = pl.BlockSpec(memory_space=pl.ANY)
 
 
 def in_hbm(array):
     return pltpu.with_memory_space_constraint(array, pltpu.HBM)
 
 
-def score(queries, left_inv, right_inv, store, columns):
+def preconditioned(queries, left_inv, right_inv):
     count, depth = queries.shape[1:]
+    return pl.pallas_call(
+        precondition_kernel,
+        out_shape=jax.ShapeDtypeStruct((count, depth), jnp.bfloat16),
+        in_specs=[VMEM, HBM, HBM],
+        out_specs=VMEM,
+        scratch_shapes=[
+            pltpu.VMEM((KIN, KIN), jnp.bfloat16),
+            pltpu.VMEM((KOUT, KOUT), jnp.bfloat16),
+            pltpu.VMEM((count // ROWS, WIDE, KOUT), jnp.bfloat16),
+            pltpu.SemaphoreType.DMA((2,)),
+        ],
+        compiler_params=pltpu.CompilerParams(vmem_limit_bytes=VMEM_LIMIT),
+        cost_estimate=pl.CostEstimate(
+            flops=2 * count * depth * 1024, bytes_accessed=4 * depth * count, transcendentals=0
+        ),
+    )(queries, in_hbm(left_inv), in_hbm(right_inv))
+
+
+def score(pre, store, columns):
+    count, depth = pre.shape
     examples = store.shape[1]
     blocks = examples // columns
     return pl.pallas_call(
         score_kernel,
-        out_shape=(pltpu.VMEM((count, columns), jnp.float32),) * blocks,
-        in_specs=[ANYWHERE] + [HBM] * 3,
+        out_shape=(jax.ShapeDtypeStruct((count, columns), jnp.float32),) * blocks,
+        in_specs=[VMEM] * 2,
         out_specs=(VMEM,) * blocks,
-        scratch_shapes=[
-            pltpu.VMEM((KIN, KIN), jnp.bfloat16),
-            pltpu.VMEM((KOUT, KOUT), jnp.bfloat16),
-            pltpu.VMEM((count, depth), jnp.bfloat16),
-            pltpu.VMEM((examples, depth), jnp.bfloat16),
-            pltpu.VMEM((count // ROWS, WIDE, KOUT), jnp.bfloat16),
-            pltpu.VMEM((columns, count), jnp.float32),
-            pltpu.SemaphoreType.DMA((1,)),
-            pltpu.SemaphoreType.DMA((1,)),
-            pltpu.SemaphoreType.DMA((count // COPY_ROWS,)),
-            pltpu.SemaphoreType.DMA((examples // COPY_ROWS,)),
-        ],
+        scratch_shapes=[pltpu.VMEM((columns, count), jnp.float32)],
         compiler_params=pltpu.CompilerParams(vmem_limit_bytes=VMEM_LIMIT),
         cost_estimate=pl.CostEstimate(
-            flops=2 * count * depth * (examples + 1024),
-            bytes_accessed=2 * depth * (2 * count + examples),
+            flops=2 * count * depth * examples,
+            bytes_accessed=2 * depth * (count + examples),
             transcendentals=0,
         ),
-    )(queries, *map(in_hbm, (left_inv, right_inv, store)))
+    )(pre, store)
 
 
 def swap(block, bit):
@@ -261,7 +252,7 @@
     ex_count = lax.axis_size("ex")
     position = lax.axis_index("ex")
     places, makers = [], []
-    current = queries
+    current = preconditioned(queries, left_inv, right_inv)
     for step in range(ex_count):
         if step > 0:
             route = [((i - 1) % ex_count, i) for i in range(ex_count)]
@@ -271,8 +262,8 @@
 
             def make(order, number=number, step=step, current=current, made=made):
                 if number == 0:
-                    block = order.after(current) if step else in_hbm(current)
-                    made.extend(score(block, left_inv, right_inv, store, width))
+                    block = order.after(current) if step else current
+                    made.extend(score(block, store, width))
                     if step:
                         made[0] = order.mark(made[0])
                 return made[number]

time: 71.2 us -> 70.7 us (level)
  Pallas kernels: 19.5 us -> 11 us
  local copies, waits for them, and re-layouts: 3.89 us -> 10.9 us
  other arithmetic: 0.67 us -> 1.62 us
    pallas_call x2 -> x3, Pallas kernels: 19.5 us -> 11 us  [the longest x2 6.71 us: score(): pl.pallas_call(score_kernel, out_shape=(jax.ShapeDtypeStruct((count, colu...]
    unnamed x10 -> x18, local copies, waits for them, and re-layouts: 2.96 us -> 8.96 us
    convert_element_type x7, local copies, waits for them, and re-layouts: 0.81 us -> 1.83 us  [send(): sent = sent.astype(jnp.bfloat16)]
    add x3, other arithmetic: 0.13 us -> 1.08 us  [take(): self.block = mine.astype(jnp.float32) + received.astype(jnp.float32)]
  transfers between devices with their start and end apart: 21 -> 21, of which waited for: 11 -> 13; matrix products, arithmetic and copies ran while one was open for 2% -> 5% of each run, Pallas kernels for 27% -> 10%
where the time goes in v10:
time: 70.7 us; the launch traced here: 70.3 us
  starting transfers between devices  24.2 us (34%)
  waiting for transfers between devices  20.6 us (29%)
  Pallas kernels  11 us (16%)
  local copies, waits for them, and re-layouts  10.9 us (15%)
  other arithmetic  1.62 us (2%)
  matrix products  1.08 us (2%)
  between operations  0.94 us (1%)
    ppermute x20, starting transfers between devices, swap(): return lax.ppermute(block, 'layer', route)  23.7 us
    ppermute x20, waiting for transfers between devices, swap(): return lax.ppermute(block, 'layer', route)  20.6 us
    unnamed x18, local copies, waits for them, and re-layouts  8.96 us
    pallas_call x2, Pallas kernels, score(): pl.pallas_call(score_kernel, out_shape=(jax.ShapeDtypeStruct((count, colu...  6.71 us
    pallas_call x1, Pallas kernels, preconditioned(): pl.pallas_call(precondition_kernel, out_shape=jax.ShapeDtypeStruct((count...  4.32 us
    convert_element_type x7, local copies, waits for them, and re-layouts, send(): sent = sent.astype(jnp.bfloat16)  1.83 us
  transfers between devices with their start and end apart: 21, of which 13 were waited for; matrix products, arithmetic and copies ran while one was open for 5% of the time, Pallas kernels for 10%

profile of v10, /device:TPU:0, one launch (start us, length us, event | category | flops | bytes accessed | tf_op | source)
XLA Modules:
  0.0 70.3 jit_solution(12032664822298947603)
XLA Ops:
  0.6 0.0 copy-start.5
  0.6 1.6 %copy-done.5 = bf16[1,256,4096]{2,1,0:T(8,128)(2,1)S(1)} copy-done((bf16[1,256,4096]{2,1,0:T(8,128)(2,1)S(1)}, bf16[1,256,4096]{2,1,0:T(8,128)(2,1)}, u32[]{:S(2)}) %copy-start.5) | copy-done | bytes 2097176
  2.2 4.3 %shard_map.77.pre_ref = bf16[256,4096]{1,0:T(8,128)(2,1)} custom-call(bf16[1,256,4096]{2,1,0:T(8,128)(2,1)S(1)} %copy-done.5, bf16[1,32,32]{2,1,0:T(8,128)(2,1)} %left_ref.1, bf16[1,128,128]{2,1,0:T(8,128)(2,1)} %right_ref.1), custom_call_target="tpu_custom_call" | custom-call | flops 2147483648 | bytes 4194304 | tf_op jit(solution)/shard_map/pallas_call | solution.py:122
  6.6 0.5 collective-permute-start.1
  7.1 3.4 %copy-done = bf16[1,1024,4096]{2,1,0:T(8,128)(2,1)S(1)} copy-done((bf16[1,1024,4096]{2,1,0:T(8,128)(2,1)S(1)}, bf16[1,1024,4096]{2,1,0:T(8,128)(2,1)}, u32[]{:S(2)}) %copy-start) | copy-done | bytes 8388632
  10.5 4.2 %shard_map.78 = (f32[256,512]{1,0:T(8,128)S(1)}, f32[256,512]{1,0:T(8,128)S(1)}) custom-call(bf16[256,4096]{1,0:T(8,128)(2,1)} %shard_map.77.pre_ref, bf16[1,1024,4096]{2,1,0:T(8,128)(2,1)S(1)} %copy-done), custom_call_target="tpu_custom_call" | custom-call | flops 2147483648 | bytes 10485760 | tf_op jit(solution)/shard_map/pallas_call | solution.py:144
  14.6 2.6 %collective-permute-start = (bf16[128,512]{1,0:T(8,128)(2,1)S(1)}, bf16[128,512]{1,0:T(8,128)(2,1)S(1)}, u32[]{:S(2)}, u32[]{:S(2)}) collective-permute-start(bf16[128,512]{1,0:T(8,128)(2,1)S(1)} %dynamic-slice_convert_fusion.3), channel_id=1, source_target_pairs={{0,2},{2,0},{4,6},{6,4},{8,10},{10,8},{12,14},{14,12},{1,3},{3,1},... | collective-permute-start | bytes 393224 | tf_op jit(solution)/shard_map/ppermute | solution.py:161
  17.3 0.7 dynamic-slice_convert_fusion.2
  17.9 0.0 collective-permute-start.3
  17.9 0.0 collective-permute-done.1.pre_ref
  18.0 3.4 %copy-done.1 = bf16[1,1024,4096]{2,1,0:T(8,128)(2,1)S(1)} copy-done((bf16[1,1024,4096]{2,1,0:T(8,128)(2,1)S(1)}, bf16[1,1024,4096]{2,1,0:T(8,128)(2,1)}, u32[]{:S(2)}) %copy-start.1) | copy-done | bytes 8388632
  21.3 2.6 %shard_map.79 = (f32[256,512]{1,0:T(8,128)S(1)}, f32[256,512]{1,0:T(8,128)S(1)}) custom-call(bf16[256,4096]{1,0:T(8,128)(2,1)S(1)} %collective-permute-done.1.pre_ref, bf16[1,1024,4096]{2,1,0:T(8,128)(2,1)S(1)} %copy-done.1), custom_call_target="tpu_custom_call" | custom-call | flops 2147483648 | bytes 10485760 | tf_op jit(solution)/shard_map/pallas_call | solution.py:144
  23.9 0.0 copy-start.2
  23.9 0.0 copy-start.4
  23.9 0.0 collective-permute-done
  23.9 0.3 collective-permute-done.3
  24.2 0.1 convert_add_fusion.2
  24.3 0.4 copy-done.2
  24.7 0.2 copy-done.4
  24.9 2.1 %collective-permute-start.2 = (bf16[64,512]{1,0:T(8,128)(2,1)S(1)}, bf16[64,512]{1,0:T(8,128)(2,1)S(1)}, u32[]{:S(2)}, u32[]{:S(2)}) collective-permute-start(bf16[64,512]{1,0:T(8,128)(2,1)S(1)} %dynamic-slice_convert_fusion.7), channel_id=1, source_target_pairs={{0,4},{2,6},{4,0},{6,2},{8,12},{10,14},{12,8},{14,10},{1,5},{3,7},... | collective-permute-start | bytes 196616 | tf_op jit(solution)/shard_map/ppermute | solution.py:161
  27.0 0.1 collective-permute-start.5
  27.1 2.2 %collective-permute-done.2 = bf16[64,512]{1,0:T(8,128)(2,1)S(1)} collective-permute-done((bf16[64,512]{1,0:T(8,128)(2,1)S(1)}, bf16[64,512]{1,0:T(8,128)(2,1)S(1)}, u32[]{:S(2)}, u32[]{:S(2)}) %collective-permute-start.2) | collective-permute-done | bytes 65568 | tf_op jit(solution)/shard_map/ppermute | solution.py:161
  29.3 2.0 %collective-permute-done.5 = bf16[64,512]{1,0:T(8,128)(2,1)S(1)} collective-permute-done((bf16[64,512]{1,0:T(8,128)(2,1)S(1)}, bf16[64,512]{1,0:T(8,128)(2,1)S(1)}, u32[]{:S(2)}, u32[]{:S(2)}) %collective-permute-start.5) | collective-permute-done | bytes 65568 | tf_op jit(solution)/shard_map/ppermute | solution.py:161
  31.3 2.7 %collective-permute-start.9 = (bf16[64,512]{1,0:T(8,128)(2,1)S(1)}, bf16[64,512]{1,0:T(8,128)(2,1)S(1)}, u32[]{:S(2)}, u32[]{:S(2)}) collective-permute-start(bf16[64,512]{1,0:T(8,128)(2,1)S(1)} %add_convert_fusion.5), channel_id=1, source_target_pairs={{0,8},{2,10},{4,12},{6,14},{8,0},{10,2},{12,4},{14,6},{1,9},{3,11}... | collective-permute-start | bytes 196616 | tf_op jit(solution)/shard_map/ppermute | solution.py:161
  34.0 0.4 collective-permute-start.4
  34.4 1.1 %dynamic-slice_convert_fusion = (bf16[128,512]{1,0:T(8,128)(2,1)S(1)}, bf16[128,512]{1,0:T(8,128)(2,1)S(1)}) fusion(f32[256,512]{1,0:T(8,128)} %copy-done.4, s32[]{:T(128)S(6)} %select_n.133, f32[256,512]{1,0:T(8,128)} %copy-done.2), kind=kLoop, calls=%fused_computation.10 | loop fusion | bytes 524292 | tf_op jit(solution)/shard_map/convert_element_type | solution.py:183
  35.5 1.6 %collective-permute-start.8 = (bf16[128,512]{1,0:T(8,128)(2,1)S(1)}, bf16[128,512]{1,0:T(8,128)(2,1)S(1)}, u32[]{:S(2)}, u32[]{:S(2)}) collective-permute-start(bf16[128,512]{1,0:T(8,128)(2,1)S(1)} %get-tuple-element.89), channel_id=1, source_target_pairs={{0,2},{2,0},{4,6},{6,4},{8,10},{10,8},{12,14},{14,12},{1,3},{3,1},... | collective-permute-start | bytes 393224 | tf_op jit(solution)/shard_map/ppermute | solution.py:161
  37.0 0.5 collective-permute-start.7
  37.6 2.5 %collective-permute-done.4 = bf16[64,512]{1,0:T(8,128)(2,1)S(1)} collective-permute-done((bf16[64,512]{1,0:T(8,128)(2,1)S(1)}, bf16[64,512]{1,0:T(8,128)(2,1)S(1)}, u32[]{:S(2)}, u32[]{:S(2)}) %collective-permute-start.4) | collective-permute-done | bytes 65568 | tf_op jit(solution)/shard_map/ppermute | solution.py:161
  40.1 0.0 collective-permute-done.9
  40.1 0.4 collective-permute-start.13
  40.5 0.2 collective-permute-done.8
  40.7 1.4 %collective-permute-done.7 = bf16[128,512]{1,0:T(8,128)(2,1)S(1)} collective-permute-done((bf16[128,512]{1,0:T(8,128)(2,1)S(1)}, bf16[128,512]{1,0:T(8,128)(2,1)S(1)}, u32[]{:S(2)}, u32[]{:S(2)}) %collective-permute-start.7) | collective-permute-done | bytes 131104 | tf_op jit(solution)/shard_map/ppermute | solution.py:161
  42.1 1.2 %collective-permute-start.6 = (bf16[64,512]{1,0:T(8,128)(2,1)S(1)}, bf16[64,512]{1,0:T(8,128)(2,1)S(1)}, u32[]{:S(2)}, u32[]{:S(2)}) collective-permute-start(bf16[64,512]{1,0:T(8,128)(2,1)S(1)} %add_convert_fusion.6), channel_id=1, source_target_pairs={{0,4},{2,6},{4,0},{6,2},{8,12},{10,14},{12,8},{14,10},{1,5},{3,7},... | collective-permute-start | bytes 196616 | tf_op jit(solution)/shard_map/ppermute | solution.py:161
  43.4 1.0 %convert_add_fusion = f32[128,512]{1,0:T(8,128)S(1)} fusion(bf16[128,512]{1,0:T(8,128)(2,1)S(1)} %collective-permute-done.8, f32[256,512]{1,0:T(8,128)} %copy-done.4, s32[]{:T(128)S(6)} %select_n.132), kind=kLoop, calls=%fused_computation.8 | loop fusion | flops 131072 | bytes 655364 | tf_op jit(solution)/shard_map/add | solution.py:197
  44.4 0.9 %collective-permute-start.12 = (bf16[64,512]{1,0:T(8,128)(2,1)S(1)}, bf16[64,512]{1,0:T(8,128)(2,1)S(1)}, u32[]{:S(2)}, u32[]{:S(2)}) collective-permute-start(bf16[64,512]{1,0:T(8,128)(2,1)S(1)} %dynamic-slice_convert_fusion.4), channel_id=1, source_target_pairs={{0,4},{2,6},{4,0},{6,2},{8,12},{10,14},{12,8},{14,10},{1,5},{3,7},... | collective-permute-start | bytes 196616 | tf_op jit(solution)/shard_map/ppermute | solution.py:161
  45.3 0.0 copy-done.3
  45.4 1.2 %collective-permute-start.11 = (bf16[64,512]{1,0:T(8,128)(2,1)S(1)}, bf16[64,512]{1,0:T(8,128)(2,1)S(1)}, u32[]{:S(2)}, u32[]{:S(2)}) collective-permute-start(bf16[64,512]{1,0:T(8,128)(2,1)S(1)} %dynamic-slice_convert_fusion.5), channel_id=1, source_target_pairs={{0,4},{2,6},{4,0},{6,2},{8,12},{10,14},{12,8},{14,10},{1,5},{3,7},... | collective-permute-start | bytes 196616 | tf_op jit(solution)/shard_map/ppermute | solution.py:161
  46.6 0.0 collective-permute-done.6
  46.6 0.0 collective-permute-done.13
  46.6 2.7 %collective-permute-done.12 = bf16[64,512]{1,0:T(8,128)(2,1)S(1)} collective-permute-done((bf16[64,512]{1,0:T(8,128)(2,1)S(1)}, bf16[64,512]{1,0:T(8,128)(2,1)S(1)}, u32[]{:S(2)}, u32[]{:S(2)}) %collective-permute-start.12) | collective-permute-done | bytes 65568 | tf_op jit(solution)/shard_map/ppermute | solution.py:161
  49.3 2.1 %collective-permute-start.15 = (bf16[64,512]{1,0:T(8,128)(2,1)S(1)}, bf16[64,512]{1,0:T(8,128)(2,1)S(1)}, u32[]{:S(2)}, u32[]{:S(2)}) collective-permute-start(bf16[64,512]{1,0:T(8,128)(2,1)S(1)} %add_convert_fusion.2), channel_id=1, source_target_pairs={{0,8},{2,10},{4,12},{6,14},{8,0},{10,2},{12,4},{14,6},{1,9},{3,11}... | collective-permute-start | bytes 196616 | tf_op jit(solution)/shard_map/ppermute | solution.py:161
  51.4 0.0 collective-permute-done.11
  51.4 1.4 %collective-permute-start.14 = (bf16[64,512]{1,0:T(8,128)(2,1)S(1)}, bf16[64,512]{1,0:T(8,128)(2,1)S(1)}, u32[]{:S(2)}, u32[]{:S(2)}) collective-permute-start(bf16[64,512]{1,0:T(8,128)(2,1)S(1)} %add_convert_fusion.3), channel_id=1, source_target_pairs={{0,8},{2,10},{4,12},{6,14},{8,0},{10,2},{12,4},{14,6},{1,9},{3,11}... | collective-permute-start | bytes 196616 | tf_op jit(solution)/shard_map/ppermute | solution.py:161
  52.9 1.6 %collective-permute-start.16 = (bf16[128,512]{1,0:T(8,128)(2,1)S(1)}, bf16[128,512]{1,0:T(8,128)(2,1)S(1)}, u32[]{:S(2)}, u32[]{:S(2)}) collective-permute-start(bf16[128,512]{1,0:T(8,128)(2,1)S(1)} %pad_maximum_fusion.1), channel_id=1, source_target_pairs={{0,2},{2,0},{4,6},{6,4},{8,10},{10,8},{12,14},{14,12},{1,3},{3,1},... | collective-permute-start | bytes 393224 | tf_op jit(solution)/shard_map/ppermute | solution.py:161
  54.5 0.6 collective-permute-start.10
  55.1 0.0 collective-permute-done.15
  55.1 2.2 %collective-permute-done.14 = bf16[64,512]{1,0:T(8,128)(2,1)S(1)} collective-permute-done((bf16[64,512]{1,0:T(8,128)(2,1)S(1)}, bf16[64,512]{1,0:T(8,128)(2,1)S(1)}, u32[]{:S(2)}, u32[]{:S(2)}) %collective-permute-start.14) | collective-permute-done | bytes 65568 | tf_op jit(solution)/shard_map/ppermute | solution.py:161
  57.4 0.7 collective-permute-start.17
  58.1 1.4 %collective-permute-start.19 = (bf16[64,512]{1,0:T(8,128)(2,1)S(1)}, bf16[64,512]{1,0:T(8,128)(2,1)S(1)}, u32[]{:S(2)}, u32[]{:S(2)}) collective-permute-start(bf16[64,512]{1,0:T(8,128)(2,1)S(1)} %add_convert_fusion), channel_id=1, source_target_pairs={{0,4},{2,6},{4,0},{6,2},{8,12},{10,14},{12,8},{14,10},{1,5},{3,7},... | collective-permute-start | bytes 196616 | tf_op jit(solution)/shard_map/ppermute | solution.py:161
  59.5 0.1 collective-permute-done.10
  59.5 0.0 collective-permute-done.16
  59.6 2.2 %collective-permute-done.17 = bf16[64,512]{1,0:T(8,128)(2,1)S(1)} collective-permute-done((bf16[64,512]{1,0:T(8,128)(2,1)S(1)}, bf16[64,512]{1,0:T(8,128)(2,1)S(1)}, u32[]{:S(2)}, u32[]{:S(2)}) %collective-permute-start.17) | collective-permute-done | bytes 65568 | tf_op jit(solution)/shard_map/ppermute | solution.py:161
  61.7 0.7 collective-permute-done.19
  62.5 1.6 %collective-permute-start.20 = (bf16[128,512]{1,0:T(8,128)(2,1)S(1)}, bf16[128,512]{1,0:T(8,128)(2,1)S(1)}, u32[]{:S(2)}, u32[]{:S(2)}) collective-permute-start(bf16[128,512]{1,0:T(8,128)(2,1)S(1)} %pad_maximum_fusion.3), channel_id=1, source_target_pairs={{0,2},{2,0},{4,6},{6,4},{8,10},{10,8},{12,14},{14,12},{1,3},{3,1},... | collective-permute-start | bytes 393224 | tf_op jit(solution)/shard_map/ppermute | solution.py:161
  64.1 0.6 collective-permute-start.18
  64.8 0.0 copy-start.7
  64.8 0.0 copy-start.8
  64.8 0.1 broadcast_in_dim.2
  65.0 2.5 %collective-permute-done.20 = bf16[128,512]{1,0:T(8,128)(2,1)S(1)} collective-permute-done((bf16[128,512]{1,0:T(8,128)(2,1)S(1)}, bf16[128,512]{1,0:T(8,128)(2,1)S(1)}, u32[]{:S(2)}, u32[]{:S(2)}) %collective-permute-start.20) | collective-permute-done | bytes 131104 | tf_op jit(solution)/shard_map/ppermute | solution.py:161
  67.5 1.6 %collective-permute-done.18 = bf16[128,512]{1,0:T(8,128)(2,1)S(1)} collective-permute-done((bf16[128,512]{1,0:T(8,128)(2,1)S(1)}, bf16[128,512]{1,0:T(8,128)(2,1)S(1)}, u32[]{:S(2)}, u32[]{:S(2)}) %collective-permute-start.18) | collective-permute-done | bytes 131104 | tf_op jit(solution)/shard_map/ppermute | solution.py:161
  69.2 0.0 copy-start.6
  69.3 1.1 %convolution_convert_fusion = bf16[128,1024]{1,0:T(8,128)(2,1)} fusion(bf16[512,1024]{1,0:T(8,128)(2,1)S(1)} %maximum_dynamic-update-slice_fusion.3, s32[512]{0:T(512)S(1)} %copy-done.7, s32[128]{0:T(128)S(1)} %copy-done.8), kind=kOutput, calls=%fused_computation | convolution fusion | flops 134742016 | bytes 1313280 | tf_op jit(solution)/shard_map/dot_general | solution.py:284
  70.3 0.0 copy-done.6
  (35 shorter events, 0.7 us)
Async XLA Ops:
  0.6 1.6 %copy-start.5 = (bf16[1,256,4096]{2,1,0:T(8,128)(2,1)S(1)}, bf16[1,256,4096]{2,1,0:T(8,128)(2,1)}, u32[]{:S(2)}) copy-start(bf16[1,256,4096]{2,1,0:T(8,128)(2,1)} %rows_ref.1) | copy-start | bytes 6291460
  6.6 11.4 %collective-permute-start.1 = (bf16[256,4096]{1,0:T(8,128)(2,1)}, bf16[256,4096]{1,0:T(8,128)(2,1)S(1)}, u32[]{:S(2)}, u32[]{:S(2)}) collective-permute-start(bf16[256,4096]{1,0:T(8,128)(2,1)} %shard_map.77.pre_ref), channel_id=1, source_target_pairs={{1,0},{0,1},{3,2},{2,3},{5,4},{4,5},{7,6},{6,7},{9,8},{8,9},{11,10... | collective-permute-start | bytes 6291464 | tf_op jit(solution)/shard_map/ppermute | solution.py:259
  7.1 3.4 %copy-start = (bf16[1,1024,4096]{2,1,0:T(8,128)(2,1)S(1)}, bf16[1,1024,4096]{2,1,0:T(8,128)(2,1)}, u32[]{:S(2)}) copy-start(bf16[1,1024,4096]{2,1,0:T(8,128)(2,1)} %store_ref.3) | copy-start | bytes 25165828
  14.6 9.3 %collective-permute-start = (bf16[128,512]{1,0:T(8,128)(2,1)S(1)}, bf16[128,512]{1,0:T(8,128)(2,1)S(1)}, u32[]{:S(2)}, u32[]{:S(2)}) collective-permute-start(bf16[128,512]{1,0:T(8,128)(2,1)S(1)} %dynamic-slice_convert_fusion.3), channel_id=1, source_target_pairs={{0,2},{2,0},{4,6},{6,4},{8,10},{10,8},{12,14},{14,12},{1,3},{3,1},... | collective-permute-start | bytes 393224 | tf_op jit(solution)/shard_map/ppermute | solution.py:161
  17.9 6.3 %collective-permute-start.3 = (bf16[128,512]{1,0:T(8,128)(2,1)}, bf16[128,512]{1,0:T(8,128)(2,1)S(1)}, u32[]{:S(2)}, u32[]{:S(2)}) collective-permute-start(bf16[128,512]{1,0:T(8,128)(2,1)} %dynamic-slice_convert_fusion.2), channel_id=1, source_target_pairs={{0,2},{2,0},{4,6},{6,4},{8,10},{10,8},{12,14},{14,12},{1,3},{3,1},... | collective-permute-start | bytes 393224 | tf_op jit(solution)/shard_map/ppermute | solution.py:161
  17.9 3.4 %copy-start.1 = (bf16[1,1024,4096]{2,1,0:T(8,128)(2,1)S(1)}, bf16[1,1024,4096]{2,1,0:T(8,128)(2,1)}, u32[]{:S(2)}) copy-start(bf16[1,1024,4096]{2,1,0:T(8,128)(2,1)} %store_ref.3) | copy-start | bytes 25165828
  23.9 0.8 %copy-start.2 = (f32[256,512]{1,0:T(8,128)}, f32[256,512]{1,0:T(8,128)S(1)}, u32[]{:S(2)}) copy-start(f32[256,512]{1,0:T(8,128)S(1)} %get-tuple-element.86) | copy-start | bytes 1572868
  23.9 1.0 %copy-start.4 = (f32[256,512]{1,0:T(8,128)}, f32[256,512]{1,0:T(8,128)S(1)}, u32[]{:S(2)}) copy-start(f32[256,512]{1,0:T(8,128)S(1)} %get-tuple-element.88) | copy-start | bytes 1572868
  24.9 20.5 %copy-start.3 = (f32[256,512]{1,0:T(8,128)S(1)}, f32[256,512]{1,0:T(8,128)}, u32[]{:S(2)}) copy-start(f32[256,512]{1,0:T(8,128)} %copy-done.2) | copy-start | bytes 1572868
  24.9 4.4 %collective-permute-start.2 = (bf16[64,512]{1,0:T(8,128)(2,1)S(1)}, bf16[64,512]{1,0:T(8,128)(2,1)S(1)}, u32[]{:S(2)}, u32[]{:S(2)}) collective-permute-start(bf16[64,512]{1,0:T(8,128)(2,1)S(1)} %dynamic-slice_convert_fusion.7), channel_id=1, source_target_pairs={{0,4},{2,6},{4,0},{6,2},{8,12},{10,14},{12,8},{14,10},{1,5},{3,7},... | collective-permute-start | bytes 196616 | tf_op jit(solution)/shard_map/ppermute | solution.py:161
  27.0 4.3 %collective-permute-start.5 = (bf16[64,512]{1,0:T(8,128)(2,1)S(1)}, bf16[64,512]{1,0:T(8,128)(2,1)S(1)}, u32[]{:S(2)}, u32[]{:S(2)}) collective-permute-start(bf16[64,512]{1,0:T(8,128)(2,1)S(1)} %dynamic-slice_convert_fusion.6), channel_id=1, source_target_pairs={{0,4},{2,6},{4,0},{6,2},{8,12},{10,14},{12,8},{14,10},{1,5},{3,7},... | collective-permute-start | bytes 196616 | tf_op jit(solution)/shard_map/ppermute | solution.py:161
  31.3 8.7 %collective-permute-start.9 = (bf16[64,512]{1,0:T(8,128)(2,1)S(1)}, bf16[64,512]{1,0:T(8,128)(2,1)S(1)}, u32[]{:S(2)}, u32[]{:S(2)}) collective-permute-start(bf16[64,512]{1,0:T(8,128)(2,1)S(1)} %add_convert_fusion.5), channel_id=1, source_target_pairs={{0,8},{2,10},{4,12},{6,14},{8,0},{10,2},{12,4},{14,6},{1,9},{3,11}... | collective-permute-start | bytes 196616 | tf_op jit(solution)/shard_map/ppermute | solution.py:161
  34.0 6.1 %collective-permute-start.4 = (bf16[64,512]{1,0:T(8,128)(2,1)S(1)}, bf16[64,512]{1,0:T(8,128)(2,1)S(1)}, u32[]{:S(2)}, u32[]{:S(2)}) collective-permute-start(bf16[64,512]{1,0:T(8,128)(2,1)S(1)} %add_convert_fusion.7), channel_id=1, source_target_pairs={{0,8},{2,10},{4,12},{6,14},{8,0},{10,2},{12,4},{14,6},{1,9},{3,11}... | collective-permute-start | bytes 196616 | tf_op jit(solution)/shard_map/ppermute | solution.py:161
  35.5 5.3 %collective-permute-start.8 = (bf16[128,512]{1,0:T(8,128)(2,1)S(1)}, bf16[128,512]{1,0:T(8,128)(2,1)S(1)}, u32[]{:S(2)}, u32[]{:S(2)}) collective-permute-start(bf16[128,512]{1,0:T(8,128)(2,1)S(1)} %get-tuple-element.89), channel_id=1, source_target_pairs={{0,2},{2,0},{4,6},{6,4},{8,10},{10,8},{12,14},{14,12},{1,3},{3,1},... | collective-permute-start | bytes 393224 | tf_op jit(solution)/shard_map/ppermute | solution.py:161
  37.0 5.1 %collective-permute-start.7 = (bf16[128,512]{1,0:T(8,128)(2,1)S(1)}, bf16[128,512]{1,0:T(8,128)(2,1)S(1)}, u32[]{:S(2)}, u32[]{:S(2)}) collective-permute-start(bf16[128,512]{1,0:T(8,128)(2,1)S(1)} %get-tuple-element.87), channel_id=1, source_target_pairs={{0,2},{2,0},{4,6},{6,4},{8,10},{10,8},{12,14},{14,12},{1,3},{3,1},... | collective-permute-start | bytes 393224 | tf_op jit(solution)/shard_map/ppermute | solution.py:161
  40.1 6.5 %collective-permute-start.13 = (bf16[64,512]{1,0:T(8,128)(2,1)S(1)}, bf16[64,512]{1,0:T(8,128)(2,1)S(1)}, u32[]{:S(2)}, u32[]{:S(2)}) collective-permute-start(bf16[64,512]{1,0:T(8,128)(2,1)S(1)} %add_convert_fusion.4), channel_id=1, source_target_pairs={{0,4},{2,6},{4,0},{6,2},{8,12},{10,14},{12,8},{14,10},{1,5},{3,7},... | collective-permute-start | bytes 196616 | tf_op jit(solution)/shard_map/ppermute | solution.py:161
  42.1 4.5 %collective-permute-start.6 = (bf16[64,512]{1,0:T(8,128)(2,1)S(1)}, bf16[64,512]{1,0:T(8,128)(2,1)S(1)}, u32[]{:S(2)}, u32[]{:S(2)}) collective-permute-start(bf16[64,512]{1,0:T(8,128)(2,1)S(1)} %add_convert_fusion.6), channel_id=1, source_target_pairs={{0,4},{2,6},{4,0},{6,2},{8,12},{10,14},{12,8},{14,10},{1,5},{3,7},... | collective-permute-start | bytes 196616 | tf_op jit(solution)/shard_map/ppermute | solution.py:161
  44.4 4.9 %collective-permute-start.12 = (bf16[64,512]{1,0:T(8,128)(2,1)S(1)}, bf16[64,512]{1,0:T(8,128)(2,1)S(1)}, u32[]{:S(2)}, u32[]{:S(2)}) collective-permute-start(bf16[64,512]{1,0:T(8,128)(2,1)S(1)} %dynamic-slice_convert_fusion.4), channel_id=1, source_target_pairs={{0,4},{2,6},{4,0},{6,2},{8,12},{10,14},{12,8},{14,10},{1,5},{3,7},... | collective-permute-start | bytes 196616 | tf_op jit(solution)/shard_map/ppermute | solution.py:161
  45.4 6.0 %collective-permute-start.11 = (bf16[64,512]{1,0:T(8,128)(2,1)S(1)}, bf16[64,512]{1,0:T(8,128)(2,1)S(1)}, u32[]{:S(2)}, u32[]{:S(2)}) collective-permute-start(bf16[64,512]{1,0:T(8,128)(2,1)S(1)} %dynamic-slice_convert_fusion.5), channel_id=1, source_target_pairs={{0,4},{2,6},{4,0},{6,2},{8,12},{10,14},{12,8},{14,10},{1,5},{3,7},... | collective-permute-start | bytes 196616 | tf_op jit(solution)/shard_map/ppermute | solution.py:161
  49.3 5.8 %collective-permute-start.15 = (bf16[64,512]{1,0:T(8,128)(2,1)S(1)}, bf16[64,512]{1,0:T(8,128)(2,1)S(1)}, u32[]{:S(2)}, u32[]{:S(2)}) collective-permute-start(bf16[64,512]{1,0:T(8,128)(2,1)S(1)} %add_convert_fusion.2), channel_id=1, source_target_pairs={{0,8},{2,10},{4,12},{6,14},{8,0},{10,2},{12,4},{14,6},{1,9},{3,11}... | collective-permute-start | bytes 196616 | tf_op jit(solution)/shard_map/ppermute | solution.py:161
  51.4 5.9 %collective-permute-start.14 = (bf16[64,512]{1,0:T(8,128)(2,1)S(1)}, bf16[64,512]{1,0:T(8,128)(2,1)S(1)}, u32[]{:S(2)}, u32[]{:S(2)}) collective-permute-start(bf16[64,512]{1,0:T(8,128)(2,1)S(1)} %add_convert_fusion.3), channel_id=1, source_target_pairs={{0,8},{2,10},{4,12},{6,14},{8,0},{10,2},{12,4},{14,6},{1,9},{3,11}... | collective-permute-start | bytes 196616 | tf_op jit(solution)/shard_map/ppermute | solution.py:161
  52.9 6.7 %collective-permute-start.16 = (bf16[128,512]{1,0:T(8,128)(2,1)S(1)}, bf16[128,512]{1,0:T(8,128)(2,1)S(1)}, u32[]{:S(2)}, u32[]{:S(2)}) collective-permute-start(bf16[128,512]{1,0:T(8,128)(2,1)S(1)} %pad_maximum_fusion.1), channel_id=1, source_target_pairs={{0,2},{2,0},{4,6},{6,4},{8,10},{10,8},{12,14},{14,12},{1,3},{3,1},... | collective-permute-start | bytes 393224 | tf_op jit(solution)/shard_map/ppermute | solution.py:161
  54.5 5.0 %collective-permute-start.10 = (bf16[128,512]{1,0:T(8,128)(2,1)S(1)}, bf16[128,512]{1,0:T(8,128)(2,1)S(1)}, u32[]{:S(2)}, u32[]{:S(2)}) collective-permute-start(bf16[128,512]{1,0:T(8,128)(2,1)S(1)} %pad_maximum_fusion), channel_id=1, source_target_pairs={{0,2},{2,0},{4,6},{6,4},{8,10},{10,8},{12,14},{14,12},{1,3},{3,1},... | collective-permute-start | bytes 393224 | tf_op jit(solution)/shard_map/ppermute | solution.py:161
  57.4 4.3 %collective-permute-start.17 = (bf16[64,512]{1,0:T(8,128)(2,1)S(1)}, bf16[64,512]{1,0:T(8,128)(2,1)S(1)}, u32[]{:S(2)}, u32[]{:S(2)}) collective-permute-start(bf16[64,512]{1,0:T(8,128)(2,1)S(1)} %add_convert_fusion.1), channel_id=1, source_target_pairs={{0,4},{2,6},{4,0},{6,2},{8,12},{10,14},{12,8},{14,10},{1,5},{3,7},... | collective-permute-start | bytes 196616 | tf_op jit(solution)/shard_map/ppermute | solution.py:161
  58.1 4.3 %collective-permute-start.19 = (bf16[64,512]{1,0:T(8,128)(2,1)S(1)}, bf16[64,512]{1,0:T(8,128)(2,1)S(1)}, u32[]{:S(2)}, u32[]{:S(2)}) collective-permute-start(bf16[64,512]{1,0:T(8,128)(2,1)S(1)} %add_convert_fusion), channel_id=1, source_target_pairs={{0,4},{2,6},{4,0},{6,2},{8,12},{10,14},{12,8},{14,10},{1,5},{3,7},... | collective-permute-start | bytes 196616 | tf_op jit(solution)/shard_map/ppermute | solution.py:161
  62.5 5.0 %collective-permute-start.20 = (bf16[128,512]{1,0:T(8,128)(2,1)S(1)}, bf16[128,512]{1,0:T(8,128)(2,1)S(1)}, u32[]{:S(2)}, u32[]{:S(2)}) collective-permute-start(bf16[128,512]{1,0:T(8,128)(2,1)S(1)} %pad_maximum_fusion.3), channel_id=1, source_target_pairs={{0,2},{2,0},{4,6},{6,4},{8,10},{10,8},{12,14},{14,12},{1,3},{3,1},... | collective-permute-start | bytes 393224 | tf_op jit(solution)/shard_map/ppermute | solution.py:161
  64.1 5.0 %collective-permute-start.18 = (bf16[128,512]{1,0:T(8,128)(2,1)S(1)}, bf16[128,512]{1,0:T(8,128)(2,1)S(1)}, u32[]{:S(2)}, u32[]{:S(2)}) collective-permute-start(bf16[128,512]{1,0:T(8,128)(2,1)S(1)} %pad_maximum_fusion.2), channel_id=1, source_target_pairs={{0,2},{2,0},{4,6},{6,4},{8,10},{10,8},{12,14},{14,12},{1,3},{3,1},... | collective-permute-start | bytes 393224 | tf_op jit(solution)/shard_map/ppermute | solution.py:161
  64.8 4.5 %copy-start.7 = (s32[512]{0:T(512)S(1)}, s32[512]{0:T(512)}, u32[]{:S(2)}) copy-start(s32[512]{0:T(512)} %param.10) | copy-start | bytes 6148
  64.8 4.5 %copy-start.8 = (s32[128]{0:T(128)S(1)}, s32[128]{0:T(128)}, u32[]{:S(2)}) copy-start(s32[128]{0:T(128)} %param.11) | copy-start | bytes 1540
  69.2 1.1 %copy-start.6 = (bf16[512,1024]{1,0:T(8,128)(2,1)}, bf16[512,1024]{1,0:T(8,128)(2,1)S(1)}, u32[]{:S(2)}) copy-start(bf16[512,1024]{1,0:T(8,128)(2,1)S(1)} %maximum_dynamic-update-slice_fusion.3) | copy-start | bytes 3145732

commit v11 on v9

--- a/solution.py
+++ b/solution.py
@@ -13,10 +13,10 @@
 ROWS = 8
 WIDE = KIN * ROWS
 PAIR = 2 * KOUT
-DEPTH_BLOCK = 512
+DEPTH_BLOCK = 1024
+TOGETHER = 4
 COLUMNS = 512
-COPY_ROWS = 32
-QUEUES = 2
+CUTS = ((False,), (True, True))
 VMEM_LIMIT = 32 * 1024 * 1024
 NT = (((1,), (1,)), ((), ()))
 
@@ -47,17 +47,25 @@
 def precondition(rows_ref, left, right, half_ref, pre_ref):
     count = rows_ref.shape[0]
     both = right_matrix(right)
-    together = 4
-    for start in range(0, KIN // 2, together):
+
+    def pairs(step, carry):
+        first = step * TOGETHER
         block = jnp.concatenate(
-            [rows_ref[:, p * PAIR : (p + 1) * PAIR] for p in range(start, start + together)], 0
+            [
+                rows_ref[:, pl.ds(pl.multiple_of((first + k) * PAIR, PAIR), PAIR)]
+                for k in range(TOGETHER)
+            ],
+            0,
         )
         half = jnp.dot(block, both, preferred_element_type=jnp.float32)
-        for k in range(together):
-            at = 2 * ROWS * (start + k)
-            half_ref[:, at : at + 2 * ROWS, :] = side_by_side_to_stacked(
+        for k in range(TOGETHER):
+            at = pl.ds(pl.multiple_of((first + k) * 2 * ROWS, 2 * ROWS), 2 * ROWS)
+            half_ref[:, at, :] = side_by_side_to_stacked(
                 half[k * count : (k + 1) * count]
             ).astype(jnp.bfloat16)
+        return carry
+
+    lax.fori_loop(0, KIN // 2 // TOGETHER, pairs, 0)
     mixer = left_matrix(left)
 
     def groups(index, carry):
@@ -74,22 +82,19 @@
 
 
 def dot(pre_ref, store_ref, first, total_ref, out_ref):
-    depth = pre_ref.shape[1]
-    columns = total_ref.shape[0]
-    for at in range(0, depth, DEPTH_BLOCK):
-        block = slice(at, at + DEPTH_BLOCK)
-        term = lax.dot_general(
-            store_ref[first : first + columns, block],
-            pre_ref[:, block],
-            NT,
-            preferred_element_type=jnp.float32,
+    columns, count = total_ref.shape
+    rows = pl.ds(pl.multiple_of(first, columns), columns)
+    total_ref[...] = jnp.zeros_like(total_ref)
+
+    def depth_blocks(step, carry):
+        at = pl.ds(pl.multiple_of(step * DEPTH_BLOCK, DEPTH_BLOCK), DEPTH_BLOCK)
+        total_ref[...] += lax.dot_general(
+            store_ref[rows, at], pre_ref[:, at], NT, preferred_element_type=jnp.float32
         )
-        if at == 0:
-            total_ref[...] = term
-        elif at + DEPTH_BLOCK < depth:
-            total_ref[...] += term
-        else:
-            out_ref[...] = (total_ref[...] + term).T
+        return carry
+
+    lax.fori_loop(0, pre_ref.shape[1] // DEPTH_BLOCK, depth_blocks, 0)
+    out_ref[:, rows] = total_ref[...].T
 
 
 def copies_of(source_ref, target_ref, sems):
@@ -103,29 +108,28 @@
 
 
 def score_kernel(
-    fetch, rows_ref, left_ref, right_ref, store_ref, *refs,
+    fetch, rows_ref, left_ref, right_ref, store_ref, out_ref,
+    left_vmem, right_vmem, rows_vmem, store_vmem, half_ref, total_ref,
+    left_sems, right_sems, rows_sems, store_sems,
 ):
-    *out_refs, left_vmem, right_vmem, rows_vmem, store_vmem, half_ref, total_ref = refs[:-4]
-    left_sems, right_sems, rows_sems, store_sems = refs[-4:]
-    heads = (
-        copies_of(right_ref, right_vmem, right_sems)
-        + copies_of(left_ref, left_vmem, left_sems)
-        + (copies_of(rows_ref, rows_vmem, rows_sems) if fetch else [])
-    )
+    heads = copies_of(right_ref, right_vmem, right_sems) + copies_of(left_ref, left_vmem, left_sems)
+    if fetch:
+        heads += copies_of(rows_ref, rows_vmem, rows_sems)
     copies = copies_of(store_ref, store_vmem, store_sems)
-    for k, copy in enumerate(heads + copies):
-        copy.start(priority=k % QUEUES)
+    for copy in heads + copies:
+        copy.start()
     for copy in heads:
         copy.wait()
-    pre_ref = rows_vmem
     given_ref = rows_vmem if fetch else rows_ref.at[0]
-    precondition(given_ref, left_vmem[...], right_vmem[...], half_ref, pre_ref)
-    share = len(copies) // len(out_refs)
-    columns = total_ref.shape[0]
-    for k, out_ref in enumerate(out_refs):
-        for copy in copies[k * share : (k + 1) * share]:
-            copy.wait()
-        dot(pre_ref, store_vmem, k * columns, total_ref, out_ref)
+    precondition(given_ref, left_vmem[...], right_vmem[...], half_ref, rows_vmem)
+    for copy in copies:
+        copy.wait()
+
+    def blocks(step, carry):
+        dot(rows_vmem, store_vmem, step * total_ref.shape[0], total_ref, out_ref)
+        return carry
+
+    lax.fori_loop(0, out_ref.shape[1] // total_ref.shape[0], blocks, 0)
 
 
 VMEM = pl.BlockSpec(memory_space=pltpu.VMEM)
@@ -136,38 +140,33 @@
     return pltpu.with_memory_space_constraint(array, pltpu.HBM)
 
 
-def in_vmem(array):
-    return pltpu.with_memory_space_constraint(array, pltpu.VMEM)
-
-
-def score(queries, fetch, left_inv, right_inv, store, columns):
+def score(queries, fetch, left_inv, right_inv, store):
     count, depth = queries.shape[1:]
     examples = store.shape[1]
-    blocks = examples // columns
     return pl.pallas_call(
         functools.partial(score_kernel, fetch),
-        out_shape=(pltpu.VMEM((count, columns), jnp.float32),) * blocks,
+        out_shape=jax.ShapeDtypeStruct((count, examples), jnp.float32),
         in_specs=[HBM if fetch else VMEM] + [HBM] * 3,
-        out_specs=(VMEM,) * blocks,
+        out_specs=VMEM,
         scratch_shapes=[
             pltpu.VMEM((KIN, KIN), jnp.bfloat16),
             pltpu.VMEM((KOUT, KOUT), jnp.bfloat16),
             pltpu.VMEM((count, depth), jnp.bfloat16),
             pltpu.VMEM((examples, depth), jnp.bfloat16),
             pltpu.VMEM((count // ROWS, WIDE, KOUT), jnp.bfloat16),
-            pltpu.VMEM((columns, count), jnp.float32),
+            pltpu.VMEM((min(COLUMNS, examples), count), jnp.float32),
             pltpu.SemaphoreType.DMA((1,)),
             pltpu.SemaphoreType.DMA((1,)),
-            pltpu.SemaphoreType.DMA((count // COPY_ROWS,)),
-            pltpu.SemaphoreType.DMA((examples // COPY_ROWS,)),
+            pltpu.SemaphoreType.DMA((2,)),
+            pltpu.SemaphoreType.DMA((2,)),
         ],
         compiler_params=pltpu.CompilerParams(vmem_limit_bytes=VMEM_LIMIT),
         cost_estimate=pl.CostEstimate(
             flops=2 * count * depth * (examples + 1024),
-            bytes_accessed=2 * depth * (2 * count + examples),
+            bytes_accessed=2 * depth * (count + examples),
             transcendentals=0,
         ),
-    )(in_hbm(queries) if fetch else in_vmem(queries), *map(in_hbm, (left_inv, right_inv, store)))
+    )(in_hbm(queries) if fetch else queries, *map(in_hbm, (left_inv, right_inv, store)))
 
 
 def swap(block, bit):
@@ -241,16 +240,16 @@
         yield at
 
 
-def sum_layers(makers, bits, index):
+def sum_layers(makers, index):
     order = Order()
     chunks = {}
     events = []
-    for number, (start, ready, size, _) in enumerate(makers):
+    for number, (start, ready, size, bits, _) in enumerate(makers):
         events.append((start, number))
-        events.extend((ready + 2 + at, number) for at in step_times(size, len(bits)) if bits)
+        events.extend((ready + at, number) for at in step_times(size, len(bits)) if bits)
     for _, number in sorted(events):
         if number not in chunks:
-            chunk = chunks[number] = LayerSum(makers[number][3](order), bits, index)
+            chunk = chunks[number] = LayerSum(makers[number][4](order), makers[number][3], index)
         else:
             chunk = chunks[number]
             chunk.take(order)
@@ -262,9 +261,11 @@
 def shards(store, queries, left_inv, right_inv, query_prompt, winner):
     rows = queries.shape[1]
     columns = store.shape[1]
-    width = min(COLUMNS, columns)
     ex_count = lax.axis_size("ex")
     position = lax.axis_index("ex")
+    count = lax.axis_size("layer")
+    bits = [1 << k for k in range(count.bit_length() - 1)]
+    swapped = bits[1:2] + bits[:1] + bits[2:]
     places, makers = [], []
     current = queries
     for step in range(ex_count):
@@ -272,21 +273,21 @@
             route = [((i - 1) % ex_count, i) for i in range(ex_count)]
             current = lax.ppermute(current, "ex", route)
         made = []
-        for number, first in enumerate(range(0, columns, width)):
-
-            def make(order, number=number, step=step, current=current, made=made):
+        cuts = CUTS[min(step, len(CUTS) - 1)]
+        width = columns // len(cuts)
+        for number, y_first in enumerate(cuts):
+
+            def make(order, number=number, width=width, step=step, current=current, made=made):
                 if number == 0:
                     block = order.after(current) if step else current
-                    made.extend(score(block, step == 0, left_inv, right_inv, store, width))
-                    if step:
-                        made[0] = order.mark(made[0])
-                return made[number]
-
-            makers.append((6.0 + 2.0 * step, 6.0 + 7.0 * step, rows * width, make))
-            places.append(((position - step) % ex_count * rows, jnp.int32(first)))
-    count = lax.axis_size("layer")
-    bits = [1 << k for k in range(count.bit_length() - 1)]
-    done = sum_layers(makers, bits, lax.axis_index("layer"))
+                    part = score(block, step == 0, left_inv, right_inv, store)
+                    made.append(order.mark(part) if step else part)
+                return made[0][:, number * width : (number + 1) * width]
+
+            start, ready = 6.0 + 2.0 * step, 6.0 + 7.0 * step + 1.0 * number
+            makers.append((start, ready, rows * width, bits if y_first else swapped, make))
+            places.append(((position - step) % ex_count * rows, jnp.int32(number * width)))
+    done = sum_layers(makers, lax.axis_index("layer"))
     scores = jnp.zeros((rows * ex_count, columns), jnp.bfloat16)
     for place, block in zip(places, done):
         scores = lax.dynamic_update_slice(scores, block, place)

time: 73.6 us -> 68.2 us (0.927)
  local copies, waits for them, and re-layouts: 3.89 us -> 1.06 us
  Pallas kernels: 22 us -> 19.3 us
  starting transfers between devices: 24.7 us -> 23.2 us
  waiting for transfers between devices: 20.3 us -> 21.8 us
    unnamed x10 -> x6, local copies, waits for them, and re-layouts: 2.96 us -> 0.02 us
    pallas_call x2, Pallas kernels: 22 us -> 19.3 us  [score(): pl.pallas_call(functools.partial(score_kernel, fetch), out_shape=jax.Shap...]
    ppermute x20 -> x15, waiting for transfers between devices: 20.3 us -> 21.8 us  [swap(): return lax.ppermute(block, 'layer', route)]
    ppermute x20 -> x15, starting transfers between devices: 24.2 us -> 22.7 us  [swap(): return lax.ppermute(block, 'layer', route)]
  transfers between devices with their start and end apart: 21 -> 16, of which waited for: 11 -> 12; matrix products, arithmetic and copies ran while one was open for 2% -> 2% of each run, Pallas kernels for 30% -> 28%
where the time goes in v11:
time: 68.2 us; the launch traced here: 68.1 us
  starting transfers between devices  23.2 us (34%)
  waiting for transfers between devices  21.8 us (32%)
  Pallas kernels  19.3 us (28%)
  matrix products  1.08 us (2%)
  local copies, waits for them, and re-layouts  1.06 us (2%)
  between operations  0.87 us (1%)
    ppermute x15, starting transfers between devices, swap(): return lax.ppermute(block, 'layer', route)  22.7 us
    ppermute x15, waiting for transfers between devices, swap(): return lax.ppermute(block, 'layer', route)  21.8 us
    pallas_call x2, Pallas kernels, score(): pl.pallas_call(functools.partial(score_kernel, fetch), out_shape=jax.Shap...  19.3 us
  transfers between devices with their start and end apart: 16, of which 12 were waited for; matrix products, arithmetic and copies ran while one was open for 2% of the time, Pallas kernels for 28%

profile of v11, /device:TPU:0, one launch (start us, length us, event | category | flops | bytes accessed | tf_op | source)
XLA Modules:
  0.0 68.1 jit_solution(6088652157941469564)
XLA Ops:
  0.6 0.5 collective-permute-start.1
  1.1 10.0 %shard_map.77 = f32[256,1024]{1,0:T(8,128)S(1)} custom-call(bf16[1,256,4096]{2,1,0:T(8,128)(2,1)} %rows_ref.1, bf16[1,32,32]{2,1,0:T(8,128)(2,1)} %left_ref.3, bf16[1,128,128]{2,1,0:T(8,128)(2,1)} %right_ref.3, bf16[1,1024,4096]{2,1,0:T(8,128)(2,1)} %store_ref.3), custom_call_target="tpu_custom_call" | custom-call | flops 4294967296 | bytes 10485760 | tf_op jit(solution)/shard_map/pallas_call | solution.py:146
  11.2 0.7 %dynamic-slice_convert_fusion = bf16[128,1024]{1,0:T(8,128)(2,1)} fusion(f32[256,1024]{1,0:T(8,128)S(1)} %shard_map.77, s32[]{:T(128)S(6)} %select_n.125), kind=kLoop, calls=%fused_computation.3 | loop fusion | bytes 524292 | tf_op jit(solution)/shard_map/convert_element_type | solution.py:196
  11.9 2.7 %collective-permute-start = (bf16[128,1024]{1,0:T(8,128)(2,1)}, bf16[128,1024]{1,0:T(8,128)(2,1)S(1)}, u32[]{:S(2)}, u32[]{:S(2)}) collective-permute-start(bf16[128,1024]{1,0:T(8,128)(2,1)} %dynamic-slice_convert_fusion), channel_id=1, source_target_pairs={{0,4},{2,6},{4,0},{6,2},{8,12},{10,14},{12,8},{14,10},{1,5},{3,7},... | collective-permute-start | bytes 786440 | tf_op jit(solution)/shard_map/ppermute | solution.py:174
  14.6 0.0 collective-permute-done.1.rows_ref
  14.6 9.3 %shard_map.78 = f32[256,1024]{1,0:T(8,128)S(1)} custom-call(bf16[1,256,4096]{2,1,0:T(8,128)(2,1)S(1)} %collective-permute-done.1.rows_ref, bf16[1,32,32]{2,1,0:T(8,128)(2,1)} %left_ref.3, bf16[1,128,128]{2,1,0:T(8,128)(2,1)} %right_ref.3, bf16[1,1024,4096]{2,1,0:T(8,128)(2,1)} %store_ref.3), custom_call_target="tpu_custom_call" | custom-call | flops 4294967296 | bytes 10485760 | tf_op jit(solution)/shard_map/pallas_call | solution.py:146
  23.9 0.0 collective-permute-done
  23.9 0.1 convert_add_fusion
  24.0 1.5 %collective-permute-start.2 = (bf16[64,1024]{1,0:T(8,128)(2,1)S(1)}, bf16[64,1024]{1,0:T(8,128)(2,1)S(1)}, u32[]{:S(2)}, u32[]{:S(2)}) collective-permute-start(bf16[64,1024]{1,0:T(8,128)(2,1)S(1)} %dynamic-slice_convert_fusion.3), channel_id=1, source_target_pairs={{0,2},{2,0},{4,6},{6,4},{8,10},{10,8},{12,14},{14,12},{1,3},{3,1},... | collective-permute-start | bytes 393224 | tf_op jit(solution)/shard_map/ppermute | solution.py:174
  25.6 0.1 fusion.6
  25.7 0.6 collective-permute-start.5
  26.3 1.5 %collective-permute-start.4 = (bf16[128,512]{1,0:T(8,128)(2,1)S(1)}, bf16[128,512]{1,0:T(8,128)(2,1)S(1)}, u32[]{:S(2)}, u32[]{:S(2)}) collective-permute-start(bf16[128,512]{1,0:T(8,128)(2,1)S(1)} %dynamic-slice_convert_fusion.2), channel_id=1, source_target_pairs={{0,2},{2,0},{4,6},{6,4},{8,10},{10,8},{12,14},{14,12},{1,3},{3,1},... | collective-permute-start | bytes 393224 | tf_op jit(solution)/shard_map/ppermute | solution.py:174
  27.9 2.6 %collective-permute-done.2 = bf16[64,1024]{1,0:T(8,128)(2,1)S(1)} collective-permute-done((bf16[64,1024]{1,0:T(8,128)(2,1)S(1)}, bf16[64,1024]{1,0:T(8,128)(2,1)S(1)}, u32[]{:S(2)}, u32[]{:S(2)}) %collective-permute-start.2) | collective-permute-done | bytes 131104 | tf_op jit(solution)/shard_map/ppermute | solution.py:174
  30.4 2.8 %collective-permute-done.5 = bf16[128,512]{1,0:T(8,128)(2,1)S(1)} collective-permute-done((bf16[128,512]{1,0:T(8,128)(2,1)S(1)}, bf16[128,512]{1,0:T(8,128)(2,1)S(1)}, u32[]{:S(2)}, u32[]{:S(2)}) %collective-permute-start.5) | collective-permute-done | bytes 131104 | tf_op jit(solution)/shard_map/ppermute | solution.py:174
  33.3 2.0 %collective-permute-done.4 = bf16[128,512]{1,0:T(8,128)(2,1)S(1)} collective-permute-done((bf16[128,512]{1,0:T(8,128)(2,1)S(1)}, bf16[128,512]{1,0:T(8,128)(2,1)S(1)}, u32[]{:S(2)}, u32[]{:S(2)}) %collective-permute-start.4) | collective-permute-done | bytes 131104 | tf_op jit(solution)/shard_map/ppermute | solution.py:174
  35.3 0.1 convert_add_fusion.1
  35.4 0.3 collective-permute-start.7
  35.7 1.8 %collective-permute-start.6 = (bf16[64,512]{1,0:T(8,128)(2,1)S(1)}, bf16[64,512]{1,0:T(8,128)(2,1)S(1)}, u32[]{:S(2)}, u32[]{:S(2)}) collective-permute-start(bf16[64,512]{1,0:T(8,128)(2,1)S(1)} %dynamic-slice_convert_fusion.5), channel_id=1, source_target_pairs={{0,4},{2,6},{4,0},{6,2},{8,12},{10,14},{12,8},{14,10},{1,5},{3,7},... | collective-permute-start | bytes 196616 | tf_op jit(solution)/shard_map/ppermute | solution.py:174
  37.6 2.7 %collective-permute-start.3 = (bf16[64,1024]{1,0:T(8,128)(2,1)S(1)}, bf16[64,1024]{1,0:T(8,128)(2,1)S(1)}, u32[]{:S(2)}, u32[]{:S(2)}) collective-permute-start(bf16[64,1024]{1,0:T(8,128)(2,1)S(1)} %add_convert_fusion.1), channel_id=1, source_target_pairs={{0,8},{2,10},{4,12},{6,14},{8,0},{10,2},{12,4},{14,6},{1,9},{3,11}... | collective-permute-start | bytes 393224 | tf_op jit(solution)/shard_map/ppermute | solution.py:174
  40.2 0.0 collective-permute-done.7
  40.3 2.9 %collective-permute-start.10 = (bf16[64,512]{1,0:T(8,128)(2,1)S(1)}, bf16[64,512]{1,0:T(8,128)(2,1)S(1)}, u32[]{:S(2)}, u32[]{:S(2)}) collective-permute-start(bf16[64,512]{1,0:T(8,128)(2,1)S(1)} %add_convert_fusion.4), channel_id=1, source_target_pairs={{0,8},{2,10},{4,12},{6,14},{8,0},{10,2},{12,4},{14,6},{1,9},{3,11}... | collective-permute-start | bytes 196616 | tf_op jit(solution)/shard_map/ppermute | solution.py:174
  43.1 0.0 collective-permute-done.6
  43.2 1.4 %collective-permute-start.9 = (bf16[64,512]{1,0:T(8,128)(2,1)S(1)}, bf16[64,512]{1,0:T(8,128)(2,1)S(1)}, u32[]{:S(2)}, u32[]{:S(2)}) collective-permute-start(bf16[64,512]{1,0:T(8,128)(2,1)S(1)} %add_convert_fusion.5), channel_id=1, source_target_pairs={{0,8},{2,10},{4,12},{6,14},{8,0},{10,2},{12,4},{14,6},{1,9},{3,11}... | collective-permute-start | bytes 196616 | tf_op jit(solution)/shard_map/ppermute | solution.py:174
  44.5 5.1 %collective-permute-done.3 = bf16[64,1024]{1,0:T(8,128)(2,1)S(1)} collective-permute-done((bf16[64,1024]{1,0:T(8,128)(2,1)S(1)}, bf16[64,1024]{1,0:T(8,128)(2,1)S(1)}, u32[]{:S(2)}, u32[]{:S(2)}) %collective-permute-start.3) | collective-permute-done | bytes 131104 | tf_op jit(solution)/shard_map/ppermute | solution.py:174
  49.6 0.8 %collective-permute-done.10 = bf16[64,512]{1,0:T(8,128)(2,1)S(1)} collective-permute-done((bf16[64,512]{1,0:T(8,128)(2,1)S(1)}, bf16[64,512]{1,0:T(8,128)(2,1)S(1)}, u32[]{:S(2)}, u32[]{:S(2)}) %collective-permute-start.10) | collective-permute-done | bytes 65568 | tf_op jit(solution)/shard_map/ppermute | solution.py:174
  50.4 0.7 %collective-permute-done.9 = bf16[64,512]{1,0:T(8,128)(2,1)S(1)} collective-permute-done((bf16[64,512]{1,0:T(8,128)(2,1)S(1)}, bf16[64,512]{1,0:T(8,128)(2,1)S(1)}, u32[]{:S(2)}, u32[]{:S(2)}) %collective-permute-start.9) | collective-permute-done | bytes 65568 | tf_op jit(solution)/shard_map/ppermute | solution.py:174
  51.2 1.6 %collective-permute-start.8 = (bf16[64,1024]{1,0:T(8,128)(2,1)S(1)}, bf16[64,1024]{1,0:T(8,128)(2,1)S(1)}, u32[]{:S(2)}, u32[]{:S(2)}) collective-permute-start(bf16[64,1024]{1,0:T(8,128)(2,1)S(1)} %add_convert_fusion), channel_id=1, source_target_pairs={{0,2},{2,0},{4,6},{6,4},{8,10},{10,8},{12,14},{14,12},{1,3},{3,1},... | collective-permute-start | bytes 393224 | tf_op jit(solution)/shard_map/ppermute | solution.py:174
  52.8 0.1 collective-permute-start.12
  52.9 2.0 %collective-permute-start.14 = (bf16[64,512]{1,0:T(8,128)(2,1)S(1)}, bf16[64,512]{1,0:T(8,128)(2,1)S(1)}, u32[]{:S(2)}, u32[]{:S(2)}) collective-permute-start(bf16[64,512]{1,0:T(8,128)(2,1)S(1)} %add_convert_fusion.2), channel_id=1, source_target_pairs={{0,4},{2,6},{4,0},{6,2},{8,12},{10,14},{12,8},{14,10},{1,5},{3,7},... | collective-permute-start | bytes 196616 | tf_op jit(solution)/shard_map/ppermute | solution.py:174
  54.9 1.3 %collective-permute-done.8 = bf16[64,1024]{1,0:T(8,128)(2,1)S(1)} collective-permute-done((bf16[64,1024]{1,0:T(8,128)(2,1)S(1)}, bf16[64,1024]{1,0:T(8,128)(2,1)S(1)}, u32[]{:S(2)}, u32[]{:S(2)}) %collective-permute-start.8) | collective-permute-done | bytes 131104 | tf_op jit(solution)/shard_map/ppermute | solution.py:174
  56.2 1.0 %collective-permute-done.12 = bf16[64,512]{1,0:T(8,128)(2,1)S(1)} collective-permute-done((bf16[64,512]{1,0:T(8,128)(2,1)S(1)}, bf16[64,512]{1,0:T(8,128)(2,1)S(1)}, u32[]{:S(2)}, u32[]{:S(2)}) %collective-permute-start.12) | collective-permute-done | bytes 65568 | tf_op jit(solution)/shard_map/ppermute | solution.py:174
  57.2 0.7 %collective-permute-done.14 = bf16[64,512]{1,0:T(8,128)(2,1)S(1)} collective-permute-done((bf16[64,512]{1,0:T(8,128)(2,1)S(1)}, bf16[64,512]{1,0:T(8,128)(2,1)S(1)}, u32[]{:S(2)}, u32[]{:S(2)}) %collective-permute-start.14) | collective-permute-done | bytes 65568 | tf_op jit(solution)/shard_map/ppermute | solution.py:174
  57.9 0.5 collective-permute-start.15
  58.5 1.6 %collective-permute-start.13 = (bf16[128,512]{1,0:T(8,128)(2,1)S(1)}, bf16[128,512]{1,0:T(8,128)(2,1)S(1)}, u32[]{:S(2)}, u32[]{:S(2)}) collective-permute-start(bf16[128,512]{1,0:T(8,128)(2,1)S(1)} %pad_maximum_fusion.1), channel_id=1, source_target_pairs={{0,2},{2,0},{4,6},{6,4},{8,10},{10,8},{12,14},{14,12},{1,3},{3,1},... | collective-permute-start | bytes 393224 | tf_op jit(solution)/shard_map/ppermute | solution.py:174
  60.2 1.4 %collective-permute-start.11 = (bf16[128,1024]{1,0:T(8,128)(2,1)S(1)}, bf16[128,1024]{1,0:T(8,128)(2,1)S(1)}, u32[]{:S(2)}, u32[]{:S(2)}) collective-permute-start(bf16[128,1024]{1,0:T(8,128)(2,1)S(1)} %pad_maximum_fusion), channel_id=1, source_target_pairs={{0,4},{2,6},{4,0},{6,2},{8,12},{10,14},{12,8},{14,10},{1,5},{3,7},... | collective-permute-start | bytes 786440 | tf_op jit(solution)/shard_map/ppermute | solution.py:174
  61.6 1.4 %collective-permute-done.15 = bf16[128,512]{1,0:T(8,128)(2,1)S(1)} collective-permute-done((bf16[128,512]{1,0:T(8,128)(2,1)S(1)}, bf16[128,512]{1,0:T(8,128)(2,1)S(1)}, u32[]{:S(2)}, u32[]{:S(2)}) %collective-permute-start.15) | collective-permute-done | bytes 131104 | tf_op jit(solution)/shard_map/ppermute | solution.py:174
  63.0 1.4 %collective-permute-done.13 = bf16[128,512]{1,0:T(8,128)(2,1)S(1)} collective-permute-done((bf16[128,512]{1,0:T(8,128)(2,1)S(1)}, bf16[128,512]{1,0:T(8,128)(2,1)S(1)}, u32[]{:S(2)}, u32[]{:S(2)}) %collective-permute-start.13) | collective-permute-done | bytes 131104 | tf_op jit(solution)/shard_map/ppermute | solution.py:174
  64.4 0.0 copy-start.1
  64.4 0.0 copy-start.2
  64.4 2.2 %collective-permute-done.11 = bf16[128,1024]{1,0:T(8,128)(2,1)S(1)} collective-permute-done((bf16[128,1024]{1,0:T(8,128)(2,1)S(1)}, bf16[128,1024]{1,0:T(8,128)(2,1)S(1)}, u32[]{:S(2)}, u32[]{:S(2)}) %collective-permute-start.11) | collective-permute-done | bytes 262176 | tf_op jit(solution)/shard_map/ppermute | solution.py:174
  66.6 0.1 broadcast_select_fusion.1
  66.7 0.1 broadcast_in_dim.2
  67.0 0.0 copy-done.1
  67.0 0.0 copy-done.2
  67.0 0.0 copy-start
  67.0 1.1 %convolution_convert_fusion = bf16[128,1024]{1,0:T(8,128)(2,1)} fusion(bf16[512,1024]{1,0:T(8,128)(2,1)S(1)} %maximum_dynamic-update-slice_fusion.2, s32[512]{0:T(512)S(1)} %copy-done.1, s32[128]{0:T(128)S(1)} %copy-done.2), kind=kOutput, calls=%fused_computation | convolution fusion | flops 134742016 | bytes 1313280 | tf_op jit(solution)/shard_map/dot_general | solution.py:299
  68.1 0.0 copy-done
  (22 shorter events, 0.5 us)
Async XLA Ops:
  0.6 14.0 %collective-permute-start.1 = (bf16[1,256,4096]{2,1,0:T(8,128)(2,1)}, bf16[1,256,4096]{2,1,0:T(8,128)(2,1)S(1)}, u32[]{:S(2)}, u32[]{:S(2)}) collective-permute-start(bf16[1,256,4096]{2,1,0:T(8,128)(2,1)} %rows_ref.1), channel_id=1, source_target_pairs={{1,0},{0,1},{3,2},{2,3},{5,4},{4,5},{7,6},{6,7},{9,8},{8,9},{11,10... | collective-permute-start | bytes 6291464 | tf_op jit(solution)/shard_map/ppermute | solution.py:274
  11.9 12.0 %collective-permute-start = (bf16[128,1024]{1,0:T(8,128)(2,1)}, bf16[128,1024]{1,0:T(8,128)(2,1)S(1)}, u32[]{:S(2)}, u32[]{:S(2)}) collective-permute-start(bf16[128,1024]{1,0:T(8,128)(2,1)} %dynamic-slice_convert_fusion), channel_id=1, source_target_pairs={{0,4},{2,6},{4,0},{6,2},{8,12},{10,14},{12,8},{14,10},{1,5},{3,7},... | collective-permute-start | bytes 786440 | tf_op jit(solution)/shard_map/ppermute | solution.py:174
  24.0 6.4 %collective-permute-start.2 = (bf16[64,1024]{1,0:T(8,128)(2,1)S(1)}, bf16[64,1024]{1,0:T(8,128)(2,1)S(1)}, u32[]{:S(2)}, u32[]{:S(2)}) collective-permute-start(bf16[64,1024]{1,0:T(8,128)(2,1)S(1)} %dynamic-slice_convert_fusion.3), channel_id=1, source_target_pairs={{0,2},{2,0},{4,6},{6,4},{8,10},{10,8},{12,14},{14,12},{1,3},{3,1},... | collective-permute-start | bytes 393224 | tf_op jit(solution)/shard_map/ppermute | solution.py:174
  25.7 7.6 %collective-permute-start.5 = (bf16[128,512]{1,0:T(8,128)(2,1)S(1)}, bf16[128,512]{1,0:T(8,128)(2,1)S(1)}, u32[]{:S(2)}, u32[]{:S(2)}) collective-permute-start(bf16[128,512]{1,0:T(8,128)(2,1)S(1)} %dynamic-slice_convert_fusion.1), channel_id=1, source_target_pairs={{0,2},{2,0},{4,6},{6,4},{8,10},{10,8},{12,14},{14,12},{1,3},{3,1},... | collective-permute-start | bytes 393224 | tf_op jit(solution)/shard_map/ppermute | solution.py:174
  26.3 8.9 %collective-permute-start.4 = (bf16[128,512]{1,0:T(8,128)(2,1)S(1)}, bf16[128,512]{1,0:T(8,128)(2,1)S(1)}, u32[]{:S(2)}, u32[]{:S(2)}) collective-permute-start(bf16[128,512]{1,0:T(8,128)(2,1)S(1)} %dynamic-slice_convert_fusion.2), channel_id=1, source_target_pairs={{0,2},{2,0},{4,6},{6,4},{8,10},{10,8},{12,14},{14,12},{1,3},{3,1},... | collective-permute-start | bytes 393224 | tf_op jit(solution)/shard_map/ppermute | solution.py:174
  35.4 4.9 %collective-permute-start.7 = (bf16[64,512]{1,0:T(8,128)(2,1)S(1)}, bf16[64,512]{1,0:T(8,128)(2,1)S(1)}, u32[]{:S(2)}, u32[]{:S(2)}) collective-permute-start(bf16[64,512]{1,0:T(8,128)(2,1)S(1)} %dynamic-slice_convert_fusion.4), channel_id=1, source_target_pairs={{0,4},{2,6},{4,0},{6,2},{8,12},{10,14},{12,8},{14,10},{1,5},{3,7},... | collective-permute-start | bytes 196616 | tf_op jit(solution)/shard_map/ppermute | solution.py:174
  35.7 7.4 %collective-permute-start.6 = (bf16[64,512]{1,0:T(8,128)(2,1)S(1)}, bf16[64,512]{1,0:T(8,128)(2,1)S(1)}, u32[]{:S(2)}, u32[]{:S(2)}) collective-permute-start(bf16[64,512]{1,0:T(8,128)(2,1)S(1)} %dynamic-slice_convert_fusion.5), channel_id=1, source_target_pairs={{0,4},{2,6},{4,0},{6,2},{8,12},{10,14},{12,8},{14,10},{1,5},{3,7},... | collective-permute-start | bytes 196616 | tf_op jit(solution)/shard_map/ppermute | solution.py:174
  37.6 12.0 %collective-permute-start.3 = (bf16[64,1024]{1,0:T(8,128)(2,1)S(1)}, bf16[64,1024]{1,0:T(8,128)(2,1)S(1)}, u32[]{:S(2)}, u32[]{:S(2)}) collective-permute-start(bf16[64,1024]{1,0:T(8,128)(2,1)S(1)} %add_convert_fusion.1), channel_id=1, source_target_pairs={{0,8},{2,10},{4,12},{6,14},{8,0},{10,2},{12,4},{14,6},{1,9},{3,11}... | collective-permute-start | bytes 393224 | tf_op jit(solution)/shard_map/ppermute | solution.py:174
  40.3 10.2 %collective-permute-start.10 = (bf16[64,512]{1,0:T(8,128)(2,1)S(1)}, bf16[64,512]{1,0:T(8,128)(2,1)S(1)}, u32[]{:S(2)}, u32[]{:S(2)}) collective-permute-start(bf16[64,512]{1,0:T(8,128)(2,1)S(1)} %add_convert_fusion.4), channel_id=1, source_target_pairs={{0,8},{2,10},{4,12},{6,14},{8,0},{10,2},{12,4},{14,6},{1,9},{3,11}... | collective-permute-start | bytes 196616 | tf_op jit(solution)/shard_map/ppermute | solution.py:174
  43.2 8.0 %collective-permute-start.9 = (bf16[64,512]{1,0:T(8,128)(2,1)S(1)}, bf16[64,512]{1,0:T(8,128)(2,1)S(1)}, u32[]{:S(2)}, u32[]{:S(2)}) collective-permute-start(bf16[64,512]{1,0:T(8,128)(2,1)S(1)} %add_convert_fusion.5), channel_id=1, source_target_pairs={{0,8},{2,10},{4,12},{6,14},{8,0},{10,2},{12,4},{14,6},{1,9},{3,11}... | collective-permute-start | bytes 196616 | tf_op jit(solution)/shard_map/ppermute | solution.py:174
  51.2 5.0 %collective-permute-start.8 = (bf16[64,1024]{1,0:T(8,128)(2,1)S(1)}, bf16[64,1024]{1,0:T(8,128)(2,1)S(1)}, u32[]{:S(2)}, u32[]{:S(2)}) collective-permute-start(bf16[64,1024]{1,0:T(8,128)(2,1)S(1)} %add_convert_fusion), channel_id=1, source_target_pairs={{0,2},{2,0},{4,6},{6,4},{8,10},{10,8},{12,14},{14,12},{1,3},{3,1},... | collective-permute-start | bytes 393224 | tf_op jit(solution)/shard_map/ppermute | solution.py:174
  52.8 4.3 %collective-permute-start.12 = (bf16[64,512]{1,0:T(8,128)(2,1)S(1)}, bf16[64,512]{1,0:T(8,128)(2,1)S(1)}, u32[]{:S(2)}, u32[]{:S(2)}) collective-permute-start(bf16[64,512]{1,0:T(8,128)(2,1)S(1)} %add_convert_fusion.3), channel_id=1, source_target_pairs={{0,4},{2,6},{4,0},{6,2},{8,12},{10,14},{12,8},{14,10},{1,5},{3,7},... | collective-permute-start | bytes 196616 | tf_op jit(solution)/shard_map/ppermute | solution.py:174
  52.9 5.0 %collective-permute-start.14 = (bf16[64,512]{1,0:T(8,128)(2,1)S(1)}, bf16[64,512]{1,0:T(8,128)(2,1)S(1)}, u32[]{:S(2)}, u32[]{:S(2)}) collective-permute-start(bf16[64,512]{1,0:T(8,128)(2,1)S(1)} %add_convert_fusion.2), channel_id=1, source_target_pairs={{0,4},{2,6},{4,0},{6,2},{8,12},{10,14},{12,8},{14,10},{1,5},{3,7},... | collective-permute-start | bytes 196616 | tf_op jit(solution)/shard_map/ppermute | solution.py:174
  57.9 5.0 %collective-permute-start.15 = (bf16[128,512]{1,0:T(8,128)(2,1)S(1)}, bf16[128,512]{1,0:T(8,128)(2,1)S(1)}, u32[]{:S(2)}, u32[]{:S(2)}) collective-permute-start(bf16[128,512]{1,0:T(8,128)(2,1)S(1)} %pad_maximum_fusion.2), channel_id=1, source_target_pairs={{0,2},{2,0},{4,6},{6,4},{8,10},{10,8},{12,14},{14,12},{1,3},{3,1},... | collective-permute-start | bytes 393224 | tf_op jit(solution)/shard_map/ppermute | solution.py:174
  58.5 5.9 %collective-permute-start.13 = (bf16[128,512]{1,0:T(8,128)(2,1)S(1)}, bf16[128,512]{1,0:T(8,128)(2,1)S(1)}, u32[]{:S(2)}, u32[]{:S(2)}) collective-permute-start(bf16[128,512]{1,0:T(8,128)(2,1)S(1)} %pad_maximum_fusion.1), channel_id=1, source_target_pairs={{0,2},{2,0},{4,6},{6,4},{8,10},{10,8},{12,14},{14,12},{1,3},{3,1},... | collective-permute-start | bytes 393224 | tf_op jit(solution)/shard_map/ppermute | solution.py:174
  60.2 6.4 %collective-permute-start.11 = (bf16[128,1024]{1,0:T(8,128)(2,1)S(1)}, bf16[128,1024]{1,0:T(8,128)(2,1)S(1)}, u32[]{:S(2)}, u32[]{:S(2)}) collective-permute-start(bf16[128,1024]{1,0:T(8,128)(2,1)S(1)} %pad_maximum_fusion), channel_id=1, source_target_pairs={{0,4},{2,6},{4,0},{6,2},{8,12},{10,14},{12,8},{14,10},{1,5},{3,7},... | collective-permute-start | bytes 786440 | tf_op jit(solution)/shard_map/ppermute | solution.py:174
  64.4 2.6 %copy-start.1 = (s32[512]{0:T(512)S(1)}, s32[512]{0:T(512)}, u32[]{:S(2)}) copy-start(s32[512]{0:T(512)} %param.10) | copy-start | bytes 6148
  64.4 2.6 %copy-start.2 = (s32[128]{0:T(128)S(1)}, s32[128]{0:T(128)}, u32[]{:S(2)}) copy-start(s32[128]{0:T(128)} %param.11) | copy-start | bytes 1540
  67.0 1.1 %copy-start = (bf16[512,1024]{1,0:T(8,128)(2,1)}, bf16[512,1024]{1,0:T(8,128)(2,1)S(1)}, u32[]{:S(2)}) copy-start(bf16[512,1024]{1,0:T(8,128)(2,1)S(1)} %maximum_dynamic-update-slice_fusion.2) | copy-start | bytes 3145732

commit v12 on v11

--- a/solution.py
+++ b/solution.py
@@ -108,8 +108,8 @@
 
 
 def score_kernel(
-    fetch, rows_ref, left_ref, right_ref, store_ref, out_ref,
-    left_vmem, right_vmem, rows_vmem, store_vmem, half_ref, total_ref,
+    fetch, rows_ref, left_ref, right_ref, store_ref, out_ref, rows_vmem, store_vmem,
+    left_vmem, right_vmem, half_ref, total_ref,
     left_sems, right_sems, rows_sems, store_sems,
 ):
     heads = copies_of(right_ref, right_vmem, right_sems) + copies_of(left_ref, left_vmem, left_sems)
@@ -145,14 +145,16 @@
     examples = store.shape[1]
     return pl.pallas_call(
         functools.partial(score_kernel, fetch),
-        out_shape=jax.ShapeDtypeStruct((count, examples), jnp.float32),
+        out_shape=(
+            pltpu.VMEM((count, examples), jnp.float32),
+            pltpu.VMEM((count, depth), jnp.bfloat16),
+            pltpu.VMEM((examples, depth), jnp.bfloat16),
+        ),
         in_specs=[HBM if fetch else VMEM] + [HBM] * 3,
-        out_specs=VMEM,
+        out_specs=(VMEM,) * 3,
         scratch_shapes=[
             pltpu.VMEM((KIN, KIN), jnp.bfloat16),
             pltpu.VMEM((KOUT, KOUT), jnp.bfloat16),
-            pltpu.VMEM((count, depth), jnp.bfloat16),
-            pltpu.VMEM((examples, depth), jnp.bfloat16),
             pltpu.VMEM((count // ROWS, WIDE, KOUT), jnp.bfloat16),
             pltpu.VMEM((min(COLUMNS, examples), count), jnp.float32),
             pltpu.SemaphoreType.DMA((1,)),
@@ -166,7 +168,7 @@
             bytes_accessed=2 * depth * (count + examples),
             transcendentals=0,
         ),
-    )(in_hbm(queries) if fetch else queries, *map(in_hbm, (left_inv, right_inv, store)))
+    )(in_hbm(queries) if fetch else queries, *map(in_hbm, (left_inv, right_inv, store)))[0]
 
 
 def swap(block, bit):

time: 68.2 us -> 75.6 us (1.11)
  Pallas kernels: 19.3 us -> 26.8 us
  starting transfers between devices: 23.2 us -> 21.7 us
  waiting for transfers between devices: 21.8 us -> 23.3 us
    pallas_call x2, Pallas kernels: 19.3 us -> 26.8 us  [score(): pl.pallas_call(functools.partial(score_kernel, fetch), out_shape=(pltpu.V...]
    ppermute x15, starting transfers between devices: 22.7 us -> 21.2 us  [swap(): return lax.ppermute(block, 'layer', route)]
    ppermute x15, waiting for transfers between devices: 21.8 us -> 23.3 us  [swap(): return lax.ppermute(block, 'layer', route)]
  transfers between devices with their start and end apart: 16 -> 16, of which waited for: 12 -> 11; matrix products, arithmetic and copies ran while one was open for 2% -> 2% of each run, Pallas kernels for 28% -> 35%
where the time goes in v12:
time: 75.6 us; the launch traced here: 75.5 us
  Pallas kernels  26.8 us (35%)
  waiting for transfers between devices  23.3 us (31%)
  starting transfers between devices  21.7 us (29%)
  matrix products  1.07 us (1%)
  local copies, waits for them, and re-layouts  1.06 us (1%)
  between operations  0.89 us (1%)
    pallas_call x2, Pallas kernels, score(): pl.pallas_call(functools.partial(score_kernel, fetch), out_shape=(pltpu.V...  26.8 us
    ppermute x15, waiting for transfers between devices, swap(): return lax.ppermute(block, 'layer', route)  23.3 us
    ppermute x15, starting transfers between devices, swap(): return lax.ppermute(block, 'layer', route)  21.2 us
  transfers between devices with their start and end apart: 16, of which 11 were waited for; matrix products, arithmetic and copies ran while one was open for 2% of the time, Pallas kernels for 35%

profile of v12, /device:TPU:0, one launch (start us, length us, event | category | flops | bytes accessed | tf_op | source)
XLA Modules:
  0.0 75.5 jit_solution(4960050011088739391)
XLA Ops:
  0.6 0.5 collective-permute-start.1
  1.1 13.8 %shard_map.77 = (f32[256,1024]{1,0:T(8,128)S(1)}, bf16[256,4096]{1,0:T(8,128)(2,1)}, bf16[1024,4096]{1,0:T(8,128)(2,1)}) custom-call(bf16[1,256,4096]{2,1,0:T(8,128)(2,1)} %rows_ref.1, bf16[1,32,32]{2,1,0:T(8,128)(2,1)} %left_ref.3, bf16[1,128,128]{2,1,0:T(8,128)(2,1)} %right_ref.3, bf16[1,1024,4096]{2,1,0:T(8,128)(2,1)} %store_ref.3), custom_call_target="tpu_custom_call" | custom-call | flops 4294967296 | bytes 10485760 | tf_op jit(solution)/shard_map/pallas_call | solution.py:146
  15.0 0.7 dynamic-slice_convert_fusion
  15.7 2.6 %collective-permute-start = (bf16[128,1024]{1,0:T(8,128)(2,1)}, bf16[128,1024]{1,0:T(8,128)(2,1)S(1)}, u32[]{:S(2)}, u32[]{:S(2)}) collective-permute-start(bf16[128,1024]{1,0:T(8,128)(2,1)} %dynamic-slice_convert_fusion), channel_id=1, source_target_pairs={{0,4},{2,6},{4,0},{6,2},{8,12},{10,14},{12,8},{14,10},{1,5},{3,7},... | collective-permute-start | bytes 786440 | tf_op jit(solution)/shard_map/ppermute | solution.py:176
  18.3 0.0 collective-permute-done.1.rows_ref
  18.3 13.0 %shard_map.78 = (f32[256,1024]{1,0:T(8,128)S(1)}, bf16[256,4096]{1,0:T(8,128)(2,1)}, bf16[1024,4096]{1,0:T(8,128)(2,1)}) custom-call(bf16[1,256,4096]{2,1,0:T(8,128)(2,1)S(1)} %collective-permute-done.1.rows_ref, bf16[1,32,32]{2,1,0:T(8,128)(2,1)} %left_ref.3, bf16[1,128,128]{2,1,0:T(8,128)(2,1)} %right_ref.3, bf16[1,1024,4096]{2,1,0:T(8,128)(2,1)} %store_ref.3), custom_call_target="tpu_custom_call" | custom-call | flops 4294967296 | bytes 10485760 | tf_op jit(solution)/shard_map/pallas_call | solution.py:146
  31.3 0.1 fusion.6
  31.4 0.0 collective-permute-done
  31.4 0.1 convert_add_fusion
  31.5 1.6 %collective-permute-start.2 = (bf16[64,1024]{1,0:T(8,128)(2,1)S(1)}, bf16[64,1024]{1,0:T(8,128)(2,1)S(1)}, u32[]{:S(2)}, u32[]{:S(2)}) collective-permute-start(bf16[64,1024]{1,0:T(8,128)(2,1)S(1)} %dynamic-slice_convert_fusion.3), channel_id=1, source_target_pairs={{0,2},{2,0},{4,6},{6,4},{8,10},{10,8},{12,14},{14,12},{1,3},{3,1},... | collective-permute-start | bytes 393224 | tf_op jit(solution)/shard_map/ppermute | solution.py:176
  33.2 0.6 collective-permute-start.4
  33.8 1.5 %collective-permute-start.5 = (bf16[128,512]{1,0:T(8,128)(2,1)S(1)}, bf16[128,512]{1,0:T(8,128)(2,1)S(1)}, u32[]{:S(2)}, u32[]{:S(2)}) collective-permute-start(bf16[128,512]{1,0:T(8,128)(2,1)S(1)} %dynamic-slice_convert_fusion.1), channel_id=1, source_target_pairs={{0,2},{2,0},{4,6},{6,4},{8,10},{10,8},{12,14},{14,12},{1,3},{3,1},... | collective-permute-start | bytes 393224 | tf_op jit(solution)/shard_map/ppermute | solution.py:176
  35.3 2.7 %collective-permute-done.2 = bf16[64,1024]{1,0:T(8,128)(2,1)S(1)} collective-permute-done((bf16[64,1024]{1,0:T(8,128)(2,1)S(1)}, bf16[64,1024]{1,0:T(8,128)(2,1)S(1)}, u32[]{:S(2)}, u32[]{:S(2)}) %collective-permute-start.2) | collective-permute-done | bytes 131104 | tf_op jit(solution)/shard_map/ppermute | solution.py:176
  38.0 4.8 %collective-permute-done.5 = bf16[128,512]{1,0:T(8,128)(2,1)S(1)} collective-permute-done((bf16[128,512]{1,0:T(8,128)(2,1)S(1)}, bf16[128,512]{1,0:T(8,128)(2,1)S(1)}, u32[]{:S(2)}, u32[]{:S(2)}) %collective-permute-start.5) | collective-permute-done | bytes 131104 | tf_op jit(solution)/shard_map/ppermute | solution.py:176
  42.8 0.0 collective-permute-done.4
  42.8 0.1 convert_add_fusion.1
  42.9 0.4 collective-permute-start.7
  43.3 1.8 %collective-permute-start.6 = (bf16[64,512]{1,0:T(8,128)(2,1)S(1)}, bf16[64,512]{1,0:T(8,128)(2,1)S(1)}, u32[]{:S(2)}, u32[]{:S(2)}) collective-permute-start(bf16[64,512]{1,0:T(8,128)(2,1)S(1)} %dynamic-slice_convert_fusion.5), channel_id=1, source_target_pairs={{0,4},{2,6},{4,0},{6,2},{8,12},{10,14},{12,8},{14,10},{1,5},{3,7},... | collective-permute-start | bytes 196616 | tf_op jit(solution)/shard_map/ppermute | solution.py:176
  45.1 2.6 %collective-permute-start.3 = (bf16[64,1024]{1,0:T(8,128)(2,1)S(1)}, bf16[64,1024]{1,0:T(8,128)(2,1)S(1)}, u32[]{:S(2)}, u32[]{:S(2)}) collective-permute-start(bf16[64,1024]{1,0:T(8,128)(2,1)S(1)} %add_convert_fusion.1), channel_id=1, source_target_pairs={{0,8},{2,10},{4,12},{6,14},{8,0},{10,2},{12,4},{14,6},{1,9},{3,11}... | collective-permute-start | bytes 393224 | tf_op jit(solution)/shard_map/ppermute | solution.py:176
  47.7 0.0 collective-permute-done.7
  47.7 1.5 %collective-permute-done.6 = bf16[64,512]{1,0:T(8,128)(2,1)S(1)} collective-permute-done((bf16[64,512]{1,0:T(8,128)(2,1)S(1)}, bf16[64,512]{1,0:T(8,128)(2,1)S(1)}, u32[]{:S(2)}, u32[]{:S(2)}) %collective-permute-start.6) | collective-permute-done | bytes 65568 | tf_op jit(solution)/shard_map/ppermute | solution.py:176
  49.2 2.6 %collective-permute-start.9 = (bf16[64,512]{1,0:T(8,128)(2,1)S(1)}, bf16[64,512]{1,0:T(8,128)(2,1)S(1)}, u32[]{:S(2)}, u32[]{:S(2)}) collective-permute-start(bf16[64,512]{1,0:T(8,128)(2,1)S(1)} %add_convert_fusion.5), channel_id=1, source_target_pairs={{0,8},{2,10},{4,12},{6,14},{8,0},{10,2},{12,4},{14,6},{1,9},{3,11}... | collective-permute-start | bytes 196616 | tf_op jit(solution)/shard_map/ppermute | solution.py:176
  51.8 0.4 collective-permute-start.10
  52.2 4.2 %collective-permute-done.3 = bf16[64,1024]{1,0:T(8,128)(2,1)S(1)} collective-permute-done((bf16[64,1024]{1,0:T(8,128)(2,1)S(1)}, bf16[64,1024]{1,0:T(8,128)(2,1)S(1)}, u32[]{:S(2)}, u32[]{:S(2)}) %collective-permute-start.3) | collective-permute-done | bytes 131104 | tf_op jit(solution)/shard_map/ppermute | solution.py:176
  56.5 2.2 %collective-permute-done.10 = bf16[64,512]{1,0:T(8,128)(2,1)S(1)} collective-permute-done((bf16[64,512]{1,0:T(8,128)(2,1)S(1)}, bf16[64,512]{1,0:T(8,128)(2,1)S(1)}, u32[]{:S(2)}, u32[]{:S(2)}) %collective-permute-start.10) | collective-permute-done | bytes 65568 | tf_op jit(solution)/shard_map/ppermute | solution.py:176
  58.7 0.0 collective-permute-done.9
  58.7 1.6 %collective-permute-start.8 = (bf16[64,1024]{1,0:T(8,128)(2,1)S(1)}, bf16[64,1024]{1,0:T(8,128)(2,1)S(1)}, u32[]{:S(2)}, u32[]{:S(2)}) collective-permute-start(bf16[64,1024]{1,0:T(8,128)(2,1)S(1)} %add_convert_fusion), channel_id=1, source_target_pairs={{0,2},{2,0},{4,6},{6,4},{8,10},{10,8},{12,14},{14,12},{1,3},{3,1},... | collective-permute-start | bytes 393224 | tf_op jit(solution)/shard_map/ppermute | solution.py:176
  60.3 0.1 collective-permute-start.12
  60.4 2.0 %collective-permute-start.14 = (bf16[64,512]{1,0:T(8,128)(2,1)S(1)}, bf16[64,512]{1,0:T(8,128)(2,1)S(1)}, u32[]{:S(2)}, u32[]{:S(2)}) collective-permute-start(bf16[64,512]{1,0:T(8,128)(2,1)S(1)} %add_convert_fusion.2), channel_id=1, source_target_pairs={{0,4},{2,6},{4,0},{6,2},{8,12},{10,14},{12,8},{14,10},{1,5},{3,7},... | collective-permute-start | bytes 196616 | tf_op jit(solution)/shard_map/ppermute | solution.py:176
  62.4 1.3 %collective-permute-done.8 = bf16[64,1024]{1,0:T(8,128)(2,1)S(1)} collective-permute-done((bf16[64,1024]{1,0:T(8,128)(2,1)S(1)}, bf16[64,1024]{1,0:T(8,128)(2,1)S(1)}, u32[]{:S(2)}, u32[]{:S(2)}) %collective-permute-start.8) | collective-permute-done | bytes 131104 | tf_op jit(solution)/shard_map/ppermute | solution.py:176
  63.7 0.9 %collective-permute-done.12 = bf16[64,512]{1,0:T(8,128)(2,1)S(1)} collective-permute-done((bf16[64,512]{1,0:T(8,128)(2,1)S(1)}, bf16[64,512]{1,0:T(8,128)(2,1)S(1)}, u32[]{:S(2)}, u32[]{:S(2)}) %collective-permute-start.12) | collective-permute-done | bytes 65568 | tf_op jit(solution)/shard_map/ppermute | solution.py:176
  64.6 0.7 collective-permute-done.14
  65.4 0.6 collective-permute-start.13
  66.0 1.5 %collective-permute-start.15 = (bf16[128,512]{1,0:T(8,128)(2,1)S(1)}, bf16[128,512]{1,0:T(8,128)(2,1)S(1)}, u32[]{:S(2)}, u32[]{:S(2)}) collective-permute-start(bf16[128,512]{1,0:T(8,128)(2,1)S(1)} %pad_maximum_fusion.2), channel_id=1, source_target_pairs={{0,2},{2,0},{4,6},{6,4},{8,10},{10,8},{12,14},{14,12},{1,3},{3,1},... | collective-permute-start | bytes 393224 | tf_op jit(solution)/shard_map/ppermute | solution.py:176
  67.6 1.4 %collective-permute-start.11 = (bf16[128,1024]{1,0:T(8,128)(2,1)S(1)}, bf16[128,1024]{1,0:T(8,128)(2,1)S(1)}, u32[]{:S(2)}, u32[]{:S(2)}) collective-permute-start(bf16[128,1024]{1,0:T(8,128)(2,1)S(1)} %pad_maximum_fusion), channel_id=1, source_target_pairs={{0,4},{2,6},{4,0},{6,2},{8,12},{10,14},{12,8},{14,10},{1,5},{3,7},... | collective-permute-start | bytes 786440 | tf_op jit(solution)/shard_map/ppermute | solution.py:176
  68.9 1.5 %collective-permute-done.13 = bf16[128,512]{1,0:T(8,128)(2,1)S(1)} collective-permute-done((bf16[128,512]{1,0:T(8,128)(2,1)S(1)}, bf16[128,512]{1,0:T(8,128)(2,1)S(1)}, u32[]{:S(2)}, u32[]{:S(2)}) %collective-permute-start.13) | collective-permute-done | bytes 131104 | tf_op jit(solution)/shard_map/ppermute | solution.py:176
  70.5 1.4 %collective-permute-done.15 = bf16[128,512]{1,0:T(8,128)(2,1)S(1)} collective-permute-done((bf16[128,512]{1,0:T(8,128)(2,1)S(1)}, bf16[128,512]{1,0:T(8,128)(2,1)S(1)}, u32[]{:S(2)}, u32[]{:S(2)}) %collective-permute-start.15) | collective-permute-done | bytes 131104 | tf_op jit(solution)/shard_map/ppermute | solution.py:176
  71.9 0.0 copy-start.1
  71.9 0.0 copy-start.2
  71.9 2.1 %collective-permute-done.11 = bf16[128,1024]{1,0:T(8,128)(2,1)S(1)} collective-permute-done((bf16[128,1024]{1,0:T(8,128)(2,1)S(1)}, bf16[128,1024]{1,0:T(8,128)(2,1)S(1)}, u32[]{:S(2)}, u32[]{:S(2)}) %collective-permute-start.11) | collective-permute-done | bytes 262176 | tf_op jit(solution)/shard_map/ppermute | solution.py:176
  74.0 0.1 broadcast_select_fusion.1
  74.1 0.1 broadcast_in_dim.2
  74.4 0.0 copy-done.1
  74.4 0.0 copy-done.2
  74.4 0.0 copy-start
  74.4 1.1 %convolution_convert_fusion = bf16[128,1024]{1,0:T(8,128)(2,1)} fusion(bf16[512,1024]{1,0:T(8,128)(2,1)S(1)} %maximum_dynamic-update-slice_fusion.2, s32[512]{0:T(512)S(1)} %copy-done.1, s32[128]{0:T(128)S(1)} %copy-done.2), kind=kOutput, calls=%fused_computation | convolution fusion | flops 134742016 | bytes 1313280 | tf_op jit(solution)/shard_map/dot_general | solution.py:301
  75.5 0.0 copy-done
  (22 shorter events, 0.5 us)
Async XLA Ops:
  0.6 17.7 %collective-permute-start.1 = (bf16[1,256,4096]{2,1,0:T(8,128)(2,1)}, bf16[1,256,4096]{2,1,0:T(8,128)(2,1)S(1)}, u32[]{:S(2)}, u32[]{:S(2)}) collective-permute-start(bf16[1,256,4096]{2,1,0:T(8,128)(2,1)} %rows_ref.1), channel_id=1, source_target_pairs={{1,0},{0,1},{3,2},{2,3},{5,4},{4,5},{7,6},{6,7},{9,8},{8,9},{11,10... | collective-permute-start | bytes 6291464 | tf_op jit(solution)/shard_map/ppermute | solution.py:276
  15.7 15.7 %collective-permute-start = (bf16[128,1024]{1,0:T(8,128)(2,1)}, bf16[128,1024]{1,0:T(8,128)(2,1)S(1)}, u32[]{:S(2)}, u32[]{:S(2)}) collective-permute-start(bf16[128,1024]{1,0:T(8,128)(2,1)} %dynamic-slice_convert_fusion), channel_id=1, source_target_pairs={{0,4},{2,6},{4,0},{6,2},{8,12},{10,14},{12,8},{14,10},{1,5},{3,7},... | collective-permute-start | bytes 786440 | tf_op jit(solution)/shard_map/ppermute | solution.py:176
  31.5 6.4 %collective-permute-start.2 = (bf16[64,1024]{1,0:T(8,128)(2,1)S(1)}, bf16[64,1024]{1,0:T(8,128)(2,1)S(1)}, u32[]{:S(2)}, u32[]{:S(2)}) collective-permute-start(bf16[64,1024]{1,0:T(8,128)(2,1)S(1)} %dynamic-slice_convert_fusion.3), channel_id=1, source_target_pairs={{0,2},{2,0},{4,6},{6,4},{8,10},{10,8},{12,14},{14,12},{1,3},{3,1},... | collective-permute-start | bytes 393224 | tf_op jit(solution)/shard_map/ppermute | solution.py:176
  33.2 9.6 %collective-permute-start.4 = (bf16[128,512]{1,0:T(8,128)(2,1)S(1)}, bf16[128,512]{1,0:T(8,128)(2,1)S(1)}, u32[]{:S(2)}, u32[]{:S(2)}) collective-permute-start(bf16[128,512]{1,0:T(8,128)(2,1)S(1)} %dynamic-slice_convert_fusion.2), channel_id=1, source_target_pairs={{0,2},{2,0},{4,6},{6,4},{8,10},{10,8},{12,14},{14,12},{1,3},{3,1},... | collective-permute-start | bytes 393224 | tf_op jit(solution)/shard_map/ppermute | solution.py:176
  33.8 9.1 %collective-permute-start.5 = (bf16[128,512]{1,0:T(8,128)(2,1)S(1)}, bf16[128,512]{1,0:T(8,128)(2,1)S(1)}, u32[]{:S(2)}, u32[]{:S(2)}) collective-permute-start(bf16[128,512]{1,0:T(8,128)(2,1)S(1)} %dynamic-slice_convert_fusion.1), channel_id=1, source_target_pairs={{0,2},{2,0},{4,6},{6,4},{8,10},{10,8},{12,14},{14,12},{1,3},{3,1},... | collective-permute-start | bytes 393224 | tf_op jit(solution)/shard_map/ppermute | solution.py:176
  42.9 4.7 %collective-permute-start.7 = (bf16[64,512]{1,0:T(8,128)(2,1)S(1)}, bf16[64,512]{1,0:T(8,128)(2,1)S(1)}, u32[]{:S(2)}, u32[]{:S(2)}) collective-permute-start(bf16[64,512]{1,0:T(8,128)(2,1)S(1)} %dynamic-slice_convert_fusion.4), channel_id=1, source_target_pairs={{0,4},{2,6},{4,0},{6,2},{8,12},{10,14},{12,8},{14,10},{1,5},{3,7},... | collective-permute-start | bytes 196616 | tf_op jit(solution)/shard_map/ppermute | solution.py:176
  43.3 5.9 %collective-permute-start.6 = (bf16[64,512]{1,0:T(8,128)(2,1)S(1)}, bf16[64,512]{1,0:T(8,128)(2,1)S(1)}, u32[]{:S(2)}, u32[]{:S(2)}) collective-permute-start(bf16[64,512]{1,0:T(8,128)(2,1)S(1)} %dynamic-slice_convert_fusion.5), channel_id=1, source_target_pairs={{0,4},{2,6},{4,0},{6,2},{8,12},{10,14},{12,8},{14,10},{1,5},{3,7},... | collective-permute-start | bytes 196616 | tf_op jit(solution)/shard_map/ppermute | solution.py:176
  45.1 11.3 %collective-permute-start.3 = (bf16[64,1024]{1,0:T(8,128)(2,1)S(1)}, bf16[64,1024]{1,0:T(8,128)(2,1)S(1)}, u32[]{:S(2)}, u32[]{:S(2)}) collective-permute-start(bf16[64,1024]{1,0:T(8,128)(2,1)S(1)} %add_convert_fusion.1), channel_id=1, source_target_pairs={{0,8},{2,10},{4,12},{6,14},{8,0},{10,2},{12,4},{14,6},{1,9},{3,11}... | collective-permute-start | bytes 393224 | tf_op jit(solution)/shard_map/ppermute | solution.py:176
  49.2 9.4 %collective-permute-start.9 = (bf16[64,512]{1,0:T(8,128)(2,1)S(1)}, bf16[64,512]{1,0:T(8,128)(2,1)S(1)}, u32[]{:S(2)}, u32[]{:S(2)}) collective-permute-start(bf16[64,512]{1,0:T(8,128)(2,1)S(1)} %add_convert_fusion.5), channel_id=1, source_target_pairs={{0,8},{2,10},{4,12},{6,14},{8,0},{10,2},{12,4},{14,6},{1,9},{3,11}... | collective-permute-start | bytes 196616 | tf_op jit(solution)/shard_map/ppermute | solution.py:176
  51.8 6.8 %collective-permute-start.10 = (bf16[64,512]{1,0:T(8,128)(2,1)S(1)}, bf16[64,512]{1,0:T(8,128)(2,1)S(1)}, u32[]{:S(2)}, u32[]{:S(2)}) collective-permute-start(bf16[64,512]{1,0:T(8,128)(2,1)S(1)} %add_convert_fusion.4), channel_id=1, source_target_pairs={{0,8},{2,10},{4,12},{6,14},{8,0},{10,2},{12,4},{14,6},{1,9},{3,11}... | collective-permute-start | bytes 196616 | tf_op jit(solution)/shard_map/ppermute | solution.py:176
  58.7 5.0 %collective-permute-start.8 = (bf16[64,1024]{1,0:T(8,128)(2,1)S(1)}, bf16[64,1024]{1,0:T(8,128)(2,1)S(1)}, u32[]{:S(2)}, u32[]{:S(2)}) collective-permute-start(bf16[64,1024]{1,0:T(8,128)(2,1)S(1)} %add_convert_fusion), channel_id=1, source_target_pairs={{0,2},{2,0},{4,6},{6,4},{8,10},{10,8},{12,14},{14,12},{1,3},{3,1},... | collective-permute-start | bytes 393224 | tf_op jit(solution)/shard_map/ppermute | solution.py:176
  60.3 4.3 %collective-permute-start.12 = (bf16[64,512]{1,0:T(8,128)(2,1)S(1)}, bf16[64,512]{1,0:T(8,128)(2,1)S(1)}, u32[]{:S(2)}, u32[]{:S(2)}) collective-permute-start(bf16[64,512]{1,0:T(8,128)(2,1)S(1)} %add_convert_fusion.3), channel_id=1, source_target_pairs={{0,4},{2,6},{4,0},{6,2},{8,12},{10,14},{12,8},{14,10},{1,5},{3,7},... | collective-permute-start | bytes 196616 | tf_op jit(solution)/shard_map/ppermute | solution.py:176
  60.4 5.0 %collective-permute-start.14 = (bf16[64,512]{1,0:T(8,128)(2,1)S(1)}, bf16[64,512]{1,0:T(8,128)(2,1)S(1)}, u32[]{:S(2)}, u32[]{:S(2)}) collective-permute-start(bf16[64,512]{1,0:T(8,128)(2,1)S(1)} %add_convert_fusion.2), channel_id=1, source_target_pairs={{0,4},{2,6},{4,0},{6,2},{8,12},{10,14},{12,8},{14,10},{1,5},{3,7},... | collective-permute-start | bytes 196616 | tf_op jit(solution)/shard_map/ppermute | solution.py:176
  65.4 5.0 %collective-permute-start.13 = (bf16[128,512]{1,0:T(8,128)(2,1)S(1)}, bf16[128,512]{1,0:T(8,128)(2,1)S(1)}, u32[]{:S(2)}, u32[]{:S(2)}) collective-permute-start(bf16[128,512]{1,0:T(8,128)(2,1)S(1)} %pad_maximum_fusion.1), channel_id=1, source_target_pairs={{0,2},{2,0},{4,6},{6,4},{8,10},{10,8},{12,14},{14,12},{1,3},{3,1},... | collective-permute-start | bytes 393224 | tf_op jit(solution)/shard_map/ppermute | solution.py:176
  66.0 5.9 %collective-permute-start.15 = (bf16[128,512]{1,0:T(8,128)(2,1)S(1)}, bf16[128,512]{1,0:T(8,128)(2,1)S(1)}, u32[]{:S(2)}, u32[]{:S(2)}) collective-permute-start(bf16[128,512]{1,0:T(8,128)(2,1)S(1)} %pad_maximum_fusion.2), channel_id=1, source_target_pairs={{0,2},{2,0},{4,6},{6,4},{8,10},{10,8},{12,14},{14,12},{1,3},{3,1},... | collective-permute-start | bytes 393224 | tf_op jit(solution)/shard_map/ppermute | solution.py:176
  67.6 6.4 %collective-permute-start.11 = (bf16[128,1024]{1,0:T(8,128)(2,1)S(1)}, bf16[128,1024]{1,0:T(8,128)(2,1)S(1)}, u32[]{:S(2)}, u32[]{:S(2)}) collective-permute-start(bf16[128,1024]{1,0:T(8,128)(2,1)S(1)} %pad_maximum_fusion), channel_id=1, source_target_pairs={{0,4},{2,6},{4,0},{6,2},{8,12},{10,14},{12,8},{14,10},{1,5},{3,7},... | collective-permute-start | bytes 786440 | tf_op jit(solution)/shard_map/ppermute | solution.py:176
  71.9 2.5 %copy-start.1 = (s32[512]{0:T(512)S(1)}, s32[512]{0:T(512)}, u32[]{:S(2)}) copy-start(s32[512]{0:T(512)} %param.10) | copy-start | bytes 6148
  71.9 2.5 %copy-start.2 = (s32[128]{0:T(128)S(1)}, s32[128]{0:T(128)}, u32[]{:S(2)}) copy-start(s32[128]{0:T(128)} %param.11) | copy-start | bytes 1540
  74.4 1.1 %copy-start = (bf16[512,1024]{1,0:T(8,128)(2,1)}, bf16[512,1024]{1,0:T(8,128)(2,1)S(1)}, u32[]{:S(2)}) copy-start(bf16[512,1024]{1,0:T(8,128)(2,1)S(1)} %maximum_dynamic-update-slice_fusion.2) | copy-start | bytes 3145732

commit v13 on v11

--- a/solution.py
+++ b/solution.py
@@ -17,7 +17,7 @@
 TOGETHER = 4
 COLUMNS = 512
 CUTS = ((False,), (True, True))
-VMEM_LIMIT = 32 * 1024 * 1024
+VMEM_LIMIT = 16 * 1024 * 1024
 NT = (((1,), (1,)), ((), ()))
 
 
@@ -97,36 +97,21 @@
     out_ref[:, rows] = total_ref[...].T
 
 
-def copies_of(source_ref, target_ref, sems):
-    rows = target_ref.shape[0] // sems.shape[0]
-    return [
-        pltpu.make_async_copy(
-            source_ref.at[0, pl.ds(k * rows, rows)], target_ref.at[pl.ds(k * rows, rows)], sems.at[k]
-        )
-        for k in range(sems.shape[0])
+def precondition_kernel(rows_ref, left_ref, right_ref, pre_ref, left_vmem, right_vmem, half_ref, sems):
+    heads = [
+        pltpu.make_async_copy(source.at[0], target, sems.at[k])
+        for k, (source, target) in enumerate(((right_ref, right_vmem), (left_ref, left_vmem)))
     ]
-
-
-def score_kernel(
-    fetch, rows_ref, left_ref, right_ref, store_ref, out_ref,
-    left_vmem, right_vmem, rows_vmem, store_vmem, half_ref, total_ref,
-    left_sems, right_sems, rows_sems, store_sems,
-):
-    heads = copies_of(right_ref, right_vmem, right_sems) + copies_of(left_ref, left_vmem, left_sems)
-    if fetch:
-        heads += copies_of(rows_ref, rows_vmem, rows_sems)
-    copies = copies_of(store_ref, store_vmem, store_sems)
-    for copy in heads + copies:
+    for copy in heads:
         copy.start()
     for copy in heads:
         copy.wait()
-    given_ref = rows_vmem if fetch else rows_ref.at[0]
-    precondition(given_ref, left_vmem[...], right_vmem[...], half_ref, rows_vmem)
-    for copy in copies:
-        copy.wait()
-
+    precondition(rows_ref.at[0], left_vmem[...], right_vmem[...], half_ref, pre_ref)
+
+
+def score_kernel(pre_ref, store_ref, out_ref, total_ref):
     def blocks(step, carry):
-        dot(rows_vmem, store_vmem, step * total_ref.shape[0], total_ref, out_ref)
+        dot(pre_ref, store_ref.at[0], step * total_ref.shape[0], total_ref, out_ref)
         return carry
 
     lax.fori_loop(0, out_ref.shape[1] // total_ref.shape[0], blocks, 0)
@@ -140,33 +125,42 @@
     return pltpu.with_memory_space_constraint(array, pltpu.HBM)
 
 
-def score(queries, fetch, left_inv, right_inv, store):
+def preconditioned(queries, left_inv, right_inv):
     count, depth = queries.shape[1:]
-    examples = store.shape[1]
     return pl.pallas_call(
-        functools.partial(score_kernel, fetch),
-        out_shape=jax.ShapeDtypeStruct((count, examples), jnp.float32),
-        in_specs=[HBM if fetch else VMEM] + [HBM] * 3,
+        precondition_kernel,
+        out_shape=jax.ShapeDtypeStruct((count, depth), jnp.bfloat16),
+        in_specs=[VMEM, HBM, HBM],
         out_specs=VMEM,
         scratch_shapes=[
             pltpu.VMEM((KIN, KIN), jnp.bfloat16),
             pltpu.VMEM((KOUT, KOUT), jnp.bfloat16),
-            pltpu.VMEM((count, depth), jnp.bfloat16),
-            pltpu.VMEM((examples, depth), jnp.bfloat16),
             pltpu.VMEM((count // ROWS, WIDE, KOUT), jnp.bfloat16),
-            pltpu.VMEM((min(COLUMNS, examples), count), jnp.float32),
-            pltpu.SemaphoreType.DMA((1,)),
-            pltpu.SemaphoreType.DMA((1,)),
-            pltpu.SemaphoreType.DMA((2,)),
             pltpu.SemaphoreType.DMA((2,)),
         ],
         compiler_params=pltpu.CompilerParams(vmem_limit_bytes=VMEM_LIMIT),
         cost_estimate=pl.CostEstimate(
-            flops=2 * count * depth * (examples + 1024),
+            flops=2 * count * depth * 1024, bytes_accessed=4 * depth * count, transcendentals=0
+        ),
+    )(queries, in_hbm(left_inv), in_hbm(right_inv))
+
+
+def score(pre, store):
+    count, depth = pre.shape
+    examples = store.shape[1]
+    return pl.pallas_call(
+        score_kernel,
+        out_shape=jax.ShapeDtypeStruct((count, examples), jnp.float32),
+        in_specs=[VMEM] * 2,
+        out_specs=VMEM,
+        scratch_shapes=[pltpu.VMEM((min(COLUMNS, examples), count), jnp.float32)],
+        compiler_params=pltpu.CompilerParams(vmem_limit_bytes=VMEM_LIMIT),
+        cost_estimate=pl.CostEstimate(
+            flops=2 * count * depth * examples,
             bytes_accessed=2 * depth * (count + examples),
             transcendentals=0,
         ),
-    )(in_hbm(queries) if fetch else queries, *map(in_hbm, (left_inv, right_inv, store)))
+    )(pre, store)
 
 
 def swap(block, bit):
@@ -267,7 +261,7 @@
     bits = [1 << k for k in range(count.bit_length() - 1)]
     swapped = bits[1:2] + bits[:1] + bits[2:]
     places, makers = [], []
-    current = queries
+    current = preconditioned(queries, left_inv, right_inv)
     for step in range(ex_count):
         if step > 0:
             route = [((i - 1) % ex_count, i) for i in range(ex_count)]
@@ -280,7 +274,7 @@
             def make(order, number=number, width=width, step=step, current=current, made=made):
                 if number == 0:
                     block = order.after(current) if step else current
-                    part = score(block, step == 0, left_inv, right_inv, store)
+                    part = score(block, store)
                     made.append(order.mark(part) if step else part)
                 return made[0][:, number * width : (number + 1) * width]
 

time: 68.2 us -> 72.6 us (1.065)
  local copies, waits for them, and re-layouts: 1.06 us -> 9.41 us
  Pallas kernels: 19.3 us -> 15.1 us
    unnamed x6 -> x12, local copies, waits for them, and re-layouts: 0.02 us -> 8.37 us
    pallas_call x2 -> x3, Pallas kernels: 19.3 us -> 15.1 us  [the longest x2 10.1 us: score(): pl.pallas_call(score_kernel, out_shape=jax.ShapeDtypeStruct((count, examp...]
  transfers between devices with their start and end apart: 16 -> 16, of which waited for: 12 -> 12; matrix products, arithmetic and copies ran while one was open for 2% -> 2% of each run, Pallas kernels for 28% -> 14%
where the time goes in v13:
time: 72.6 us; the launch traced here: 72.3 us
  starting transfers between devices  23.2 us (32%)
  waiting for transfers between devices  21.9 us (30%)
  Pallas kernels  15.1 us (21%)
  local copies, waits for them, and re-layouts  9.41 us (13%)
  matrix products  1.08 us (1%)
  between operations  0.89 us (1%)
    ppermute x15, starting transfers between devices, swap(): return lax.ppermute(block, 'layer', route)  22.7 us
    ppermute x15, waiting for transfers between devices, swap(): return lax.ppermute(block, 'layer', route)  21.9 us
    pallas_call x2, Pallas kernels, score(): pl.pallas_call(score_kernel, out_shape=jax.ShapeDtypeStruct((count, examp...  10.1 us
    unnamed x12, local copies, waits for them, and re-layouts  8.37 us
    pallas_call x1, Pallas kernels, preconditioned(): pl.pallas_call(precondition_kernel, out_shape=jax.ShapeDtypeStruct((count...  5.08 us
  transfers between devices with their start and end apart: 16, of which 12 were waited for; matrix products, arithmetic and copies ran while one was open for 2% of the time, Pallas kernels for 14%

profile of v13, /device:TPU:0, one launch (start us, length us, event | category | flops | bytes accessed | tf_op | source)
XLA Modules:
  0.0 72.3 jit_solution(398256894547188014)
XLA Ops:
  0.6 0.0 copy-start.2
  0.6 1.6 %copy-done.2 = bf16[1,256,4096]{2,1,0:T(8,128)(2,1)S(1)} copy-done((bf16[1,256,4096]{2,1,0:T(8,128)(2,1)S(1)}, bf16[1,256,4096]{2,1,0:T(8,128)(2,1)}, u32[]{:S(2)}) %copy-start.2) | copy-done | bytes 2097176
  2.2 5.1 %shard_map.77.pre_ref = bf16[256,4096]{1,0:T(8,128)(2,1)} custom-call(bf16[1,256,4096]{2,1,0:T(8,128)(2,1)S(1)} %copy-done.2, bf16[1,32,32]{2,1,0:T(8,128)(2,1)} %left_ref.1, bf16[1,128,128]{2,1,0:T(8,128)(2,1)} %right_ref.1), custom_call_target="tpu_custom_call" | custom-call | flops 2147483648 | bytes 4194304 | tf_op jit(solution)/shard_map/pallas_call | solution.py:130
  7.3 0.5 collective-permute-start.1
  7.8 0.0 copy-start
  7.8 3.4 %copy-done = bf16[1,1024,4096]{2,1,0:T(8,128)(2,1)S(1)} copy-done((bf16[1,1024,4096]{2,1,0:T(8,128)(2,1)S(1)}, bf16[1,1024,4096]{2,1,0:T(8,128)(2,1)}, u32[]{:S(2)}) %copy-start) | copy-done | bytes 8388632
  11.2 5.8 %shard_map.78 = f32[256,1024]{1,0:T(8,128)S(1)} custom-call(bf16[256,4096]{1,0:T(8,128)(2,1)} %shard_map.77.pre_ref, bf16[1,1024,4096]{2,1,0:T(8,128)(2,1)S(1)} %copy-done), custom_call_target="tpu_custom_call" | custom-call | flops 2147483648 | bytes 10485760 | tf_op jit(solution)/shard_map/pallas_call | solution.py:151
  17.0 0.7 %dynamic-slice_convert_fusion = bf16[128,1024]{1,0:T(8,128)(2,1)} fusion(f32[256,1024]{1,0:T(8,128)S(1)} %shard_map.78, s32[]{:T(128)S(6)} %select_n.125), kind=kLoop, calls=%fused_computation.3 | loop fusion | bytes 524292 | tf_op jit(solution)/shard_map/convert_element_type | solution.py:190
  17.8 2.6 %collective-permute-start = (bf16[128,1024]{1,0:T(8,128)(2,1)}, bf16[128,1024]{1,0:T(8,128)(2,1)S(1)}, u32[]{:S(2)}, u32[]{:S(2)}) collective-permute-start(bf16[128,1024]{1,0:T(8,128)(2,1)} %dynamic-slice_convert_fusion), channel_id=1, source_target_pairs={{0,4},{2,6},{4,0},{6,2},{8,12},{10,14},{12,8},{14,10},{1,5},{3,7},... | collective-permute-start | bytes 786440 | tf_op jit(solution)/shard_map/ppermute | solution.py:168
  20.4 0.0 collective-permute-done.1.pre_ref
  20.4 0.0 copy-start.1
  20.4 3.4 %copy-done.1 = bf16[1,1024,4096]{2,1,0:T(8,128)(2,1)S(1)} copy-done((bf16[1,1024,4096]{2,1,0:T(8,128)(2,1)S(1)}, bf16[1,1024,4096]{2,1,0:T(8,128)(2,1)}, u32[]{:S(2)}) %copy-start.1) | copy-done | bytes 8388632
  23.7 4.2 %shard_map.79 = f32[256,1024]{1,0:T(8,128)S(1)} custom-call(bf16[256,4096]{1,0:T(8,128)(2,1)S(1)} %collective-permute-done.1.pre_ref, bf16[1,1024,4096]{2,1,0:T(8,128)(2,1)S(1)} %copy-done.1), custom_call_target="tpu_custom_call" | custom-call | flops 2147483648 | bytes 10485760 | tf_op jit(solution)/shard_map/pallas_call | solution.py:151
  28.0 0.0 collective-permute-done
  28.0 0.1 convert_add_fusion
  28.1 1.6 %collective-permute-start.2 = (bf16[64,1024]{1,0:T(8,128)(2,1)S(1)}, bf16[64,1024]{1,0:T(8,128)(2,1)S(1)}, u32[]{:S(2)}, u32[]{:S(2)}) collective-permute-start(bf16[64,1024]{1,0:T(8,128)(2,1)S(1)} %dynamic-slice_convert_fusion.3), channel_id=1, source_target_pairs={{0,2},{2,0},{4,6},{6,4},{8,10},{10,8},{12,14},{14,12},{1,3},{3,1},... | collective-permute-start | bytes 393224 | tf_op jit(solution)/shard_map/ppermute | solution.py:168
  29.7 0.1 fusion.6
  29.8 0.5 collective-permute-start.5
  30.4 1.6 %collective-permute-start.4 = (bf16[128,512]{1,0:T(8,128)(2,1)S(1)}, bf16[128,512]{1,0:T(8,128)(2,1)S(1)}, u32[]{:S(2)}, u32[]{:S(2)}) collective-permute-start(bf16[128,512]{1,0:T(8,128)(2,1)S(1)} %dynamic-slice_convert_fusion.2), channel_id=1, source_target_pairs={{0,2},{2,0},{4,6},{6,4},{8,10},{10,8},{12,14},{14,12},{1,3},{3,1},... | collective-permute-start | bytes 393224 | tf_op jit(solution)/shard_map/ppermute | solution.py:168
  32.0 2.5 %collective-permute-done.2 = bf16[64,1024]{1,0:T(8,128)(2,1)S(1)} collective-permute-done((bf16[64,1024]{1,0:T(8,128)(2,1)S(1)}, bf16[64,1024]{1,0:T(8,128)(2,1)S(1)}, u32[]{:S(2)}, u32[]{:S(2)}) %collective-permute-start.2) | collective-permute-done | bytes 131104 | tf_op jit(solution)/shard_map/ppermute | solution.py:168
  34.5 2.8 %collective-permute-done.5 = bf16[128,512]{1,0:T(8,128)(2,1)S(1)} collective-permute-done((bf16[128,512]{1,0:T(8,128)(2,1)S(1)}, bf16[128,512]{1,0:T(8,128)(2,1)S(1)}, u32[]{:S(2)}, u32[]{:S(2)}) %collective-permute-start.5) | collective-permute-done | bytes 131104 | tf_op jit(solution)/shard_map/ppermute | solution.py:168
  37.3 2.1 %collective-permute-done.4 = bf16[128,512]{1,0:T(8,128)(2,1)S(1)} collective-permute-done((bf16[128,512]{1,0:T(8,128)(2,1)S(1)}, bf16[128,512]{1,0:T(8,128)(2,1)S(1)}, u32[]{:S(2)}, u32[]{:S(2)}) %collective-permute-start.4) | collective-permute-done | bytes 131104 | tf_op jit(solution)/shard_map/ppermute | solution.py:168
  39.4 0.1 convert_add_fusion.1
  39.5 0.8 %collective-permute-start.7 = (bf16[64,512]{1,0:T(8,128)(2,1)S(1)}, bf16[64,512]{1,0:T(8,128)(2,1)S(1)}, u32[]{:S(2)}, u32[]{:S(2)}) collective-permute-start(bf16[64,512]{1,0:T(8,128)(2,1)S(1)} %dynamic-slice_convert_fusion.4), channel_id=1, source_target_pairs={{0,4},{2,6},{4,0},{6,2},{8,12},{10,14},{12,8},{14,10},{1,5},{3,7},... | collective-permute-start | bytes 196616 | tf_op jit(solution)/shard_map/ppermute | solution.py:168
  40.3 1.3 %collective-permute-start.6 = (bf16[64,512]{1,0:T(8,128)(2,1)S(1)}, bf16[64,512]{1,0:T(8,128)(2,1)S(1)}, u32[]{:S(2)}, u32[]{:S(2)}) collective-permute-start(bf16[64,512]{1,0:T(8,128)(2,1)S(1)} %dynamic-slice_convert_fusion.5), channel_id=1, source_target_pairs={{0,4},{2,6},{4,0},{6,2},{8,12},{10,14},{12,8},{14,10},{1,5},{3,7},... | collective-permute-start | bytes 196616 | tf_op jit(solution)/shard_map/ppermute | solution.py:168
  41.7 2.7 %collective-permute-start.3 = (bf16[64,1024]{1,0:T(8,128)(2,1)S(1)}, bf16[64,1024]{1,0:T(8,128)(2,1)S(1)}, u32[]{:S(2)}, u32[]{:S(2)}) collective-permute-start(bf16[64,1024]{1,0:T(8,128)(2,1)S(1)} %add_convert_fusion.1), channel_id=1, source_target_pairs={{0,8},{2,10},{4,12},{6,14},{8,0},{10,2},{12,4},{14,6},{1,9},{3,11}... | collective-permute-start | bytes 393224 | tf_op jit(solution)/shard_map/ppermute | solution.py:168
  44.4 0.0 collective-permute-done.7
  44.4 2.9 %collective-permute-start.10 = (bf16[64,512]{1,0:T(8,128)(2,1)S(1)}, bf16[64,512]{1,0:T(8,128)(2,1)S(1)}, u32[]{:S(2)}, u32[]{:S(2)}) collective-permute-start(bf16[64,512]{1,0:T(8,128)(2,1)S(1)} %add_convert_fusion.4), channel_id=1, source_target_pairs={{0,8},{2,10},{4,12},{6,14},{8,0},{10,2},{12,4},{14,6},{1,9},{3,11}... | collective-permute-start | bytes 196616 | tf_op jit(solution)/shard_map/ppermute | solution.py:168
  47.3 0.0 collective-permute-done.6
  47.3 1.4 %collective-permute-start.9 = (bf16[64,512]{1,0:T(8,128)(2,1)S(1)}, bf16[64,512]{1,0:T(8,128)(2,1)S(1)}, u32[]{:S(2)}, u32[]{:S(2)}) collective-permute-start(bf16[64,512]{1,0:T(8,128)(2,1)S(1)} %add_convert_fusion.5), channel_id=1, source_target_pairs={{0,8},{2,10},{4,12},{6,14},{8,0},{10,2},{12,4},{14,6},{1,9},{3,11}... | collective-permute-start | bytes 196616 | tf_op jit(solution)/shard_map/ppermute | solution.py:168
  48.7 5.1 %collective-permute-done.3 = bf16[64,1024]{1,0:T(8,128)(2,1)S(1)} collective-permute-done((bf16[64,1024]{1,0:T(8,128)(2,1)S(1)}, bf16[64,1024]{1,0:T(8,128)(2,1)S(1)}, u32[]{:S(2)}, u32[]{:S(2)}) %collective-permute-start.3) | collective-permute-done | bytes 131104 | tf_op jit(solution)/shard_map/ppermute | solution.py:168
  53.8 0.8 %collective-permute-done.10 = bf16[64,512]{1,0:T(8,128)(2,1)S(1)} collective-permute-done((bf16[64,512]{1,0:T(8,128)(2,1)S(1)}, bf16[64,512]{1,0:T(8,128)(2,1)S(1)}, u32[]{:S(2)}, u32[]{:S(2)}) %collective-permute-start.10) | collective-permute-done | bytes 65568 | tf_op jit(solution)/shard_map/ppermute | solution.py:168
  54.6 0.7 collective-permute-done.9
  55.4 1.6 %collective-permute-start.8 = (bf16[64,1024]{1,0:T(8,128)(2,1)S(1)}, bf16[64,1024]{1,0:T(8,128)(2,1)S(1)}, u32[]{:S(2)}, u32[]{:S(2)}) collective-permute-start(bf16[64,1024]{1,0:T(8,128)(2,1)S(1)} %add_convert_fusion), channel_id=1, source_target_pairs={{0,2},{2,0},{4,6},{6,4},{8,10},{10,8},{12,14},{14,12},{1,3},{3,1},... | collective-permute-start | bytes 393224 | tf_op jit(solution)/shard_map/ppermute | solution.py:168
  57.0 0.1 collective-permute-start.12
  57.1 2.0 %collective-permute-start.14 = (bf16[64,512]{1,0:T(8,128)(2,1)S(1)}, bf16[64,512]{1,0:T(8,128)(2,1)S(1)}, u32[]{:S(2)}, u32[]{:S(2)}) collective-permute-start(bf16[64,512]{1,0:T(8,128)(2,1)S(1)} %add_convert_fusion.2), channel_id=1, source_target_pairs={{0,4},{2,6},{4,0},{6,2},{8,12},{10,14},{12,8},{14,10},{1,5},{3,7},... | collective-permute-start | bytes 196616 | tf_op jit(solution)/shard_map/ppermute | solution.py:168
  59.1 1.3 %collective-permute-done.8 = bf16[64,1024]{1,0:T(8,128)(2,1)S(1)} collective-permute-done((bf16[64,1024]{1,0:T(8,128)(2,1)S(1)}, bf16[64,1024]{1,0:T(8,128)(2,1)S(1)}, u32[]{:S(2)}, u32[]{:S(2)}) %collective-permute-start.8) | collective-permute-done | bytes 131104 | tf_op jit(solution)/shard_map/ppermute | solution.py:168
  60.4 0.9 %collective-permute-done.12 = bf16[64,512]{1,0:T(8,128)(2,1)S(1)} collective-permute-done((bf16[64,512]{1,0:T(8,128)(2,1)S(1)}, bf16[64,512]{1,0:T(8,128)(2,1)S(1)}, u32[]{:S(2)}, u32[]{:S(2)}) %collective-permute-start.12) | collective-permute-done | bytes 65568 | tf_op jit(solution)/shard_map/ppermute | solution.py:168
  61.3 0.7 collective-permute-done.14
  62.1 0.5 collective-permute-start.15
  62.6 1.6 %collective-permute-start.13 = (bf16[128,512]{1,0:T(8,128)(2,1)S(1)}, bf16[128,512]{1,0:T(8,128)(2,1)S(1)}, u32[]{:S(2)}, u32[]{:S(2)}) collective-permute-start(bf16[128,512]{1,0:T(8,128)(2,1)S(1)} %pad_maximum_fusion.1), channel_id=1, source_target_pairs={{0,2},{2,0},{4,6},{6,4},{8,10},{10,8},{12,14},{14,12},{1,3},{3,1},... | collective-permute-start | bytes 393224 | tf_op jit(solution)/shard_map/ppermute | solution.py:168
  64.3 1.4 %collective-permute-start.11 = (bf16[128,1024]{1,0:T(8,128)(2,1)S(1)}, bf16[128,1024]{1,0:T(8,128)(2,1)S(1)}, u32[]{:S(2)}, u32[]{:S(2)}) collective-permute-start(bf16[128,1024]{1,0:T(8,128)(2,1)S(1)} %pad_maximum_fusion), channel_id=1, source_target_pairs={{0,4},{2,6},{4,0},{6,2},{8,12},{10,14},{12,8},{14,10},{1,5},{3,7},... | collective-permute-start | bytes 786440 | tf_op jit(solution)/shard_map/ppermute | solution.py:168
  65.7 1.4 %collective-permute-done.15 = bf16[128,512]{1,0:T(8,128)(2,1)S(1)} collective-permute-done((bf16[128,512]{1,0:T(8,128)(2,1)S(1)}, bf16[128,512]{1,0:T(8,128)(2,1)S(1)}, u32[]{:S(2)}, u32[]{:S(2)}) %collective-permute-start.15) | collective-permute-done | bytes 131104 | tf_op jit(solution)/shard_map/ppermute | solution.py:168
  67.2 1.4 %collective-permute-done.13 = bf16[128,512]{1,0:T(8,128)(2,1)S(1)} collective-permute-done((bf16[128,512]{1,0:T(8,128)(2,1)S(1)}, bf16[128,512]{1,0:T(8,128)(2,1)S(1)}, u32[]{:S(2)}, u32[]{:S(2)}) %collective-permute-start.13) | collective-permute-done | bytes 131104 | tf_op jit(solution)/shard_map/ppermute | solution.py:168
  68.6 0.0 copy-start.4
  68.6 0.0 copy-start.5
  68.6 2.2 %collective-permute-done.11 = bf16[128,1024]{1,0:T(8,128)(2,1)S(1)} collective-permute-done((bf16[128,1024]{1,0:T(8,128)(2,1)S(1)}, bf16[128,1024]{1,0:T(8,128)(2,1)S(1)}, u32[]{:S(2)}, u32[]{:S(2)}) %collective-permute-start.11) | collective-permute-done | bytes 262176 | tf_op jit(solution)/shard_map/ppermute | solution.py:168
  70.8 0.1 broadcast_select_fusion.1
  70.9 0.1 broadcast_in_dim.2
  71.1 0.0 copy-done.4
  71.1 0.0 copy-done.5
  71.2 0.0 copy-start.3
  71.2 1.1 %convolution_convert_fusion = bf16[128,1024]{1,0:T(8,128)(2,1)} fusion(bf16[512,1024]{1,0:T(8,128)(2,1)S(1)} %maximum_dynamic-update-slice_fusion.2, s32[512]{0:T(512)S(1)} %copy-done.4, s32[128]{0:T(128)S(1)} %copy-done.5), kind=kOutput, calls=%fused_computation | convolution fusion | flops 134742016 | bytes 1313280 | tf_op jit(solution)/shard_map/dot_general | solution.py:293
  72.2 0.0 copy-done.3
  (22 shorter events, 0.5 us)
Async XLA Ops:
  0.6 1.6 %copy-start.2 = (bf16[1,256,4096]{2,1,0:T(8,128)(2,1)S(1)}, bf16[1,256,4096]{2,1,0:T(8,128)(2,1)}, u32[]{:S(2)}) copy-start(bf16[1,256,4096]{2,1,0:T(8,128)(2,1)} %rows_ref.1) | copy-start | bytes 6291460
  7.3 13.1 %collective-permute-start.1 = (bf16[256,4096]{1,0:T(8,128)(2,1)}, bf16[256,4096]{1,0:T(8,128)(2,1)S(1)}, u32[]{:S(2)}, u32[]{:S(2)}) collective-permute-start(bf16[256,4096]{1,0:T(8,128)(2,1)} %shard_map.77.pre_ref), channel_id=1, source_target_pairs={{1,0},{0,1},{3,2},{2,3},{5,4},{4,5},{7,6},{6,7},{9,8},{8,9},{11,10... | collective-permute-start | bytes 6291464 | tf_op jit(solution)/shard_map/ppermute | solution.py:268
  7.8 3.4 %copy-start = (bf16[1,1024,4096]{2,1,0:T(8,128)(2,1)S(1)}, bf16[1,1024,4096]{2,1,0:T(8,128)(2,1)}, u32[]{:S(2)}) copy-start(bf16[1,1024,4096]{2,1,0:T(8,128)(2,1)} %store_ref.3) | copy-start | bytes 25165828
  17.8 10.2 %collective-permute-start = (bf16[128,1024]{1,0:T(8,128)(2,1)}, bf16[128,1024]{1,0:T(8,128)(2,1)S(1)}, u32[]{:S(2)}, u32[]{:S(2)}) collective-permute-start(bf16[128,1024]{1,0:T(8,128)(2,1)} %dynamic-slice_convert_fusion), channel_id=1, source_target_pairs={{0,4},{2,6},{4,0},{6,2},{8,12},{10,14},{12,8},{14,10},{1,5},{3,7},... | collective-permute-start | bytes 786440 | tf_op jit(solution)/shard_map/ppermute | solution.py:168
  20.4 3.4 %copy-start.1 = (bf16[1,1024,4096]{2,1,0:T(8,128)(2,1)S(1)}, bf16[1,1024,4096]{2,1,0:T(8,128)(2,1)}, u32[]{:S(2)}) copy-start(bf16[1,1024,4096]{2,1,0:T(8,128)(2,1)} %store_ref.3) | copy-start | bytes 25165828
  28.1 6.4 %collective-permute-start.2 = (bf16[64,1024]{1,0:T(8,128)(2,1)S(1)}, bf16[64,1024]{1,0:T(8,128)(2,1)S(1)}, u32[]{:S(2)}, u32[]{:S(2)}) collective-permute-start(bf16[64,1024]{1,0:T(8,128)(2,1)S(1)} %dynamic-slice_convert_fusion.3), channel_id=1, source_target_pairs={{0,2},{2,0},{4,6},{6,4},{8,10},{10,8},{12,14},{14,12},{1,3},{3,1},... | collective-permute-start | bytes 393224 | tf_op jit(solution)/shard_map/ppermute | solution.py:168
  29.8 7.5 %collective-permute-start.5 = (bf16[128,512]{1,0:T(8,128)(2,1)S(1)}, bf16[128,512]{1,0:T(8,128)(2,1)S(1)}, u32[]{:S(2)}, u32[]{:S(2)}) collective-permute-start(bf16[128,512]{1,0:T(8,128)(2,1)S(1)} %dynamic-slice_convert_fusion.1), channel_id=1, source_target_pairs={{0,2},{2,0},{4,6},{6,4},{8,10},{10,8},{12,14},{14,12},{1,3},{3,1},... | collective-permute-start | bytes 393224 | tf_op jit(solution)/shard_map/ppermute | solution.py:168
  30.4 9.0 %collective-permute-start.4 = (bf16[128,512]{1,0:T(8,128)(2,1)S(1)}, bf16[128,512]{1,0:T(8,128)(2,1)S(1)}, u32[]{:S(2)}, u32[]{:S(2)}) collective-permute-start(bf16[128,512]{1,0:T(8,128)(2,1)S(1)} %dynamic-slice_convert_fusion.2), channel_id=1, source_target_pairs={{0,2},{2,0},{4,6},{6,4},{8,10},{10,8},{12,14},{14,12},{1,3},{3,1},... | collective-permute-start | bytes 393224 | tf_op jit(solution)/shard_map/ppermute | solution.py:168
  39.5 4.9 %collective-permute-start.7 = (bf16[64,512]{1,0:T(8,128)(2,1)S(1)}, bf16[64,512]{1,0:T(8,128)(2,1)S(1)}, u32[]{:S(2)}, u32[]{:S(2)}) collective-permute-start(bf16[64,512]{1,0:T(8,128)(2,1)S(1)} %dynamic-slice_convert_fusion.4), channel_id=1, source_target_pairs={{0,4},{2,6},{4,0},{6,2},{8,12},{10,14},{12,8},{14,10},{1,5},{3,7},... | collective-permute-start | bytes 196616 | tf_op jit(solution)/shard_map/ppermute | solution.py:168
  40.3 6.9 %collective-permute-start.6 = (bf16[64,512]{1,0:T(8,128)(2,1)S(1)}, bf16[64,512]{1,0:T(8,128)(2,1)S(1)}, u32[]{:S(2)}, u32[]{:S(2)}) collective-permute-start(bf16[64,512]{1,0:T(8,128)(2,1)S(1)} %dynamic-slice_convert_fusion.5), channel_id=1, source_target_pairs={{0,4},{2,6},{4,0},{6,2},{8,12},{10,14},{12,8},{14,10},{1,5},{3,7},... | collective-permute-start | bytes 196616 | tf_op jit(solution)/shard_map/ppermute | solution.py:168
  41.7 12.1 %collective-permute-start.3 = (bf16[64,1024]{1,0:T(8,128)(2,1)S(1)}, bf16[64,1024]{1,0:T(8,128)(2,1)S(1)}, u32[]{:S(2)}, u32[]{:S(2)}) collective-permute-start(bf16[64,1024]{1,0:T(8,128)(2,1)S(1)} %add_convert_fusion.1), channel_id=1, source_target_pairs={{0,8},{2,10},{4,12},{6,14},{8,0},{10,2},{12,4},{14,6},{1,9},{3,11}... | collective-permute-start | bytes 393224 | tf_op jit(solution)/shard_map/ppermute | solution.py:168
  44.4 10.2 %collective-permute-start.10 = (bf16[64,512]{1,0:T(8,128)(2,1)S(1)}, bf16[64,512]{1,0:T(8,128)(2,1)S(1)}, u32[]{:S(2)}, u32[]{:S(2)}) collective-permute-start(bf16[64,512]{1,0:T(8,128)(2,1)S(1)} %add_convert_fusion.4), channel_id=1, source_target_pairs={{0,8},{2,10},{4,12},{6,14},{8,0},{10,2},{12,4},{14,6},{1,9},{3,11}... | collective-permute-start | bytes 196616 | tf_op jit(solution)/shard_map/ppermute | solution.py:168
  47.3 8.0 %collective-permute-start.9 = (bf16[64,512]{1,0:T(8,128)(2,1)S(1)}, bf16[64,512]{1,0:T(8,128)(2,1)S(1)}, u32[]{:S(2)}, u32[]{:S(2)}) collective-permute-start(bf16[64,512]{1,0:T(8,128)(2,1)S(1)} %add_convert_fusion.5), channel_id=1, source_target_pairs={{0,8},{2,10},{4,12},{6,14},{8,0},{10,2},{12,4},{14,6},{1,9},{3,11}... | collective-permute-start | bytes 196616 | tf_op jit(solution)/shard_map/ppermute | solution.py:168
  55.4 5.0 %collective-permute-start.8 = (bf16[64,1024]{1,0:T(8,128)(2,1)S(1)}, bf16[64,1024]{1,0:T(8,128)(2,1)S(1)}, u32[]{:S(2)}, u32[]{:S(2)}) collective-permute-start(bf16[64,1024]{1,0:T(8,128)(2,1)S(1)} %add_convert_fusion), channel_id=1, source_target_pairs={{0,2},{2,0},{4,6},{6,4},{8,10},{10,8},{12,14},{14,12},{1,3},{3,1},... | collective-permute-start | bytes 393224 | tf_op jit(solution)/shard_map/ppermute | solution.py:168
  57.0 4.3 %collective-permute-start.12 = (bf16[64,512]{1,0:T(8,128)(2,1)S(1)}, bf16[64,512]{1,0:T(8,128)(2,1)S(1)}, u32[]{:S(2)}, u32[]{:S(2)}) collective-permute-start(bf16[64,512]{1,0:T(8,128)(2,1)S(1)} %add_convert_fusion.3), channel_id=1, source_target_pairs={{0,4},{2,6},{4,0},{6,2},{8,12},{10,14},{12,8},{14,10},{1,5},{3,7},... | collective-permute-start | bytes 196616 | tf_op jit(solution)/shard_map/ppermute | solution.py:168
  57.1 5.0 %collective-permute-start.14 = (bf16[64,512]{1,0:T(8,128)(2,1)S(1)}, bf16[64,512]{1,0:T(8,128)(2,1)S(1)}, u32[]{:S(2)}, u32[]{:S(2)}) collective-permute-start(bf16[64,512]{1,0:T(8,128)(2,1)S(1)} %add_convert_fusion.2), channel_id=1, source_target_pairs={{0,4},{2,6},{4,0},{6,2},{8,12},{10,14},{12,8},{14,10},{1,5},{3,7},... | collective-permute-start | bytes 196616 | tf_op jit(solution)/shard_map/ppermute | solution.py:168
  62.1 5.0 %collective-permute-start.15 = (bf16[128,512]{1,0:T(8,128)(2,1)S(1)}, bf16[128,512]{1,0:T(8,128)(2,1)S(1)}, u32[]{:S(2)}, u32[]{:S(2)}) collective-permute-start(bf16[128,512]{1,0:T(8,128)(2,1)S(1)} %pad_maximum_fusion.2), channel_id=1, source_target_pairs={{0,2},{2,0},{4,6},{6,4},{8,10},{10,8},{12,14},{14,12},{1,3},{3,1},... | collective-permute-start | bytes 393224 | tf_op jit(solution)/shard_map/ppermute | solution.py:168
  62.6 5.9 %collective-permute-start.13 = (bf16[128,512]{1,0:T(8,128)(2,1)S(1)}, bf16[128,512]{1,0:T(8,128)(2,1)S(1)}, u32[]{:S(2)}, u32[]{:S(2)}) collective-permute-start(bf16[128,512]{1,0:T(8,128)(2,1)S(1)} %pad_maximum_fusion.1), channel_id=1, source_target_pairs={{0,2},{2,0},{4,6},{6,4},{8,10},{10,8},{12,14},{14,12},{1,3},{3,1},... | collective-permute-start | bytes 393224 | tf_op jit(solution)/shard_map/ppermute | solution.py:168
  64.3 6.4 %collective-permute-start.11 = (bf16[128,1024]{1,0:T(8,128)(2,1)S(1)}, bf16[128,1024]{1,0:T(8,128)(2,1)S(1)}, u32[]{:S(2)}, u32[]{:S(2)}) collective-permute-start(bf16[128,1024]{1,0:T(8,128)(2,1)S(1)} %pad_maximum_fusion), channel_id=1, source_target_pairs={{0,4},{2,6},{4,0},{6,2},{8,12},{10,14},{12,8},{14,10},{1,5},{3,7},... | collective-permute-start | bytes 786440 | tf_op jit(solution)/shard_map/ppermute | solution.py:168
  68.6 2.6 %copy-start.4 = (s32[512]{0:T(512)S(1)}, s32[512]{0:T(512)}, u32[]{:S(2)}) copy-start(s32[512]{0:T(512)} %param.10) | copy-start | bytes 6148
  68.6 2.6 %copy-start.5 = (s32[128]{0:T(128)S(1)}, s32[128]{0:T(128)}, u32[]{:S(2)}) copy-start(s32[128]{0:T(128)} %param.11) | copy-start | bytes 1540
  71.2 1.1 %copy-start.3 = (bf16[512,1024]{1,0:T(8,128)(2,1)}, bf16[512,1024]{1,0:T(8,128)(2,1)S(1)}, u32[]{:S(2)}) copy-start(bf16[512,1024]{1,0:T(8,128)(2,1)S(1)} %maximum_dynamic-update-slice_fusion.2) | copy-start | bytes 3145732

commit v14 on v8

--- a/solution.py
+++ b/solution.py
@@ -15,7 +15,9 @@
 PAIR = 2 * KOUT
 DEPTH_BLOCK = 512
 COLUMNS = 512
-COPY_ROWS = 32
+CUTS = 1
+ROW_COPIES = 2
+STORE_COPIES = 4
 VMEM_LIMIT = 32 * 1024 * 1024
 NT = (((1,), (1,)), ((), ()))
 
@@ -43,9 +45,8 @@
     return jnp.concatenate([tiles[:, :, :KOUT], tiles[:, :, KOUT:]], 1)
 
 
-def precondition(rows_ref, left, right, half_ref, pre_ref):
+def precondition(rows_ref, both, mixer, half_ref, pre_ref):
     count = rows_ref.shape[0]
-    both = right_matrix(right)
     together = 4
     for start in range(0, KIN // 2, together):
         block = jnp.concatenate(
@@ -57,7 +58,6 @@
             half_ref[:, at : at + 2 * ROWS, :] = side_by_side_to_stacked(
                 half[k * count : (k + 1) * count]
             ).astype(jnp.bfloat16)
-    mixer = left_matrix(left)
 
     def groups(index, carry):
         stacked = jnp.concatenate([half_ref[2 * index], half_ref[2 * index + 1]], 1)
@@ -88,81 +88,123 @@
         elif at + DEPTH_BLOCK < depth:
             total_ref[...] += term
         else:
-            out_ref[...] = (total_ref[...] + term).T
+            out_ref[:, first : first + columns] = (total_ref[...] + term).T
 
 
 def copies_of(source_ref, target_ref, sems):
     rows = target_ref.shape[0] // sems.shape[0]
     return [
         pltpu.make_async_copy(
-            source_ref.at[0, pl.ds(k * rows, rows)], target_ref.at[pl.ds(k * rows, rows)], sems.at[k]
+            source_ref.at[pl.ds(k * rows, rows)], target_ref.at[pl.ds(k * rows, rows)], sems.at[k]
         )
         for k in range(sems.shape[0])
     ]
 
 
-def score_kernel(
-    rows_ref, left_ref, right_ref, store_ref, *refs,
+def start(copies):
+    for copy in copies:
+        copy.start()
+
+
+def wait(copies):
+    for copy in copies:
+        copy.wait()
+
+
+def dots(pre_ref, store_vmem, copies, total_ref, out_ref):
+    columns = total_ref.shape[0]
+    share = len(copies) * columns // store_vmem.shape[0]
+    for k, first in enumerate(range(0, store_vmem.shape[0], columns)):
+        wait(copies[k * share : (k + 1) * share])
+        dot(pre_ref, store_vmem, first, total_ref, out_ref)
+
+
+def first_kernel(
+    rows_ref, left_ref, right_ref, store_ref, out_ref, both_ref, mixer_ref,
+    left_vmem, right_vmem, rows_vmem, store_vmem, half_ref, total_ref,
+    left_sems, right_sems, rows_sems, store_sems,
 ):
-    *out_refs, left_vmem, right_vmem, rows_vmem, store_vmem, half_ref, total_ref = refs[:-4]
-    left_sems, right_sems, rows_sems, store_sems = refs[-4:]
-    heads = (
-        copies_of(right_ref, right_vmem, right_sems)
-        + copies_of(left_ref, left_vmem, left_sems)
-        + copies_of(rows_ref, rows_vmem, rows_sems)
-    )
-    copies = copies_of(store_ref, store_vmem, store_sems)
-    for copy in heads + copies:
-        copy.start()
-    for copy in heads:
-        copy.wait()
-    pre_ref = rows_vmem
-    precondition(rows_vmem, left_vmem[...], right_vmem[...], half_ref, pre_ref)
-    share = len(copies) // len(out_refs)
-    columns = total_ref.shape[0]
-    for k, out_ref in enumerate(out_refs):
-        for copy in copies[k * share : (k + 1) * share]:
-            copy.wait()
-        dot(pre_ref, store_vmem, k * columns, total_ref, out_ref)
+    heads = copies_of(right_ref.at[0], right_vmem, right_sems)
+    heads += copies_of(left_ref.at[0], left_vmem, left_sems)
+    rows = copies_of(rows_ref.at[0], rows_vmem, rows_sems)
+    copies = copies_of(store_ref.at[0], store_vmem, store_sems)
+    start(heads + rows)
+    wait(heads)
+    both_ref[...] = right_matrix(right_vmem[...])
+    mixer_ref[...] = left_matrix(left_vmem[...])
+    wait(rows)
+    start(copies)
+    precondition(rows_vmem, both_ref[...], mixer_ref[...], half_ref, rows_vmem)
+    dots(rows_vmem, store_vmem, copies, total_ref, out_ref)
+
+
+def later_kernel(
+    rows_ref, both_ref, mixer_ref, store_ref, out_ref,
+    pre_ref, store_vmem, half_ref, total_ref, store_sems,
+):
+    copies = copies_of(store_ref.at[0], store_vmem, store_sems)
+    start(copies)
+    precondition(rows_ref.at[0], both_ref[...], mixer_ref[...], half_ref, pre_ref)
+    dots(pre_ref, store_vmem, copies, total_ref, out_ref)
 
 
 VMEM = pl.BlockSpec(memory_space=pltpu.VMEM)
 HBM = pl.BlockSpec(memory_space=pltpu.HBM)
-ANYWHERE = pl.BlockSpec(memory_space=pl.ANY)
 
 
 def in_hbm(array):
     return pltpu.with_memory_space_constraint(array, pltpu.HBM)
 
 
-def score(queries, left_inv, right_inv, store, columns):
+def call(kernel, queries, store, outs, in_specs, scratch, operands):
     count, depth = queries.shape[1:]
     examples = store.shape[1]
-    blocks = examples // columns
     return pl.pallas_call(
-        score_kernel,
-        out_shape=(pltpu.VMEM((count, columns), jnp.float32),) * blocks,
-        in_specs=[ANYWHERE] + [HBM] * 3,
-        out_specs=(VMEM,) * blocks,
-        scratch_shapes=[
-            pltpu.VMEM((KIN, KIN), jnp.bfloat16),
-            pltpu.VMEM((KOUT, KOUT), jnp.bfloat16),
-            pltpu.VMEM((count, depth), jnp.bfloat16),
-            pltpu.VMEM((examples, depth), jnp.bfloat16),
-            pltpu.VMEM((count // ROWS, WIDE, KOUT), jnp.bfloat16),
-            pltpu.VMEM((columns, count), jnp.float32),
-            pltpu.SemaphoreType.DMA((1,)),
-            pltpu.SemaphoreType.DMA((1,)),
-            pltpu.SemaphoreType.DMA((count // COPY_ROWS,)),
-            pltpu.SemaphoreType.DMA((examples // COPY_ROWS,)),
-        ],
+        kernel,
+        out_shape=(jax.ShapeDtypeStruct((count, examples), jnp.float32),) + outs,
+        in_specs=in_specs,
+        out_specs=(VMEM,) * (1 + len(outs)),
+        scratch_shapes=scratch,
         compiler_params=pltpu.CompilerParams(vmem_limit_bytes=VMEM_LIMIT),
         cost_estimate=pl.CostEstimate(
             flops=2 * count * depth * (examples + 1024),
-            bytes_accessed=2 * depth * (2 * count + examples),
+            bytes_accessed=2 * depth * (count + examples),
             transcendentals=0,
         ),
-    )(queries, *map(in_hbm, (left_inv, right_inv, store)))
+    )(*operands)
+
+
+def buffers(queries, store):
+    count, depth = queries.shape[1:]
+    examples = store.shape[1]
+    return [
+        pltpu.VMEM((count, depth), jnp.bfloat16),
+        pltpu.VMEM((examples, depth), jnp.bfloat16),
+        pltpu.VMEM((count // ROWS, WIDE, KOUT), jnp.bfloat16),
+        pltpu.VMEM((min(COLUMNS, examples), count), jnp.float32),
+    ]
+
+
+def first_scores(queries, left_inv, right_inv, store):
+    small = [pltpu.VMEM((KIN, KIN), jnp.bfloat16), pltpu.VMEM((KOUT, KOUT), jnp.bfloat16)]
+    sems = [pltpu.SemaphoreType.DMA((n,)) for n in (1, 1, ROW_COPIES, STORE_COPIES)]
+    outs = (
+        jax.ShapeDtypeStruct((PAIR, PAIR), jnp.bfloat16),
+        jax.ShapeDtypeStruct((WIDE, WIDE), jnp.bfloat16),
+    )
+    operands = [in_hbm(a) for a in (queries, left_inv, right_inv, store)]
+    return call(
+        first_kernel, queries, store, outs, [HBM] * 4,
+        small + buffers(queries, store) + sems, operands,
+    )
+
+
+def later_scores(queries, both, mixer, store):
+    sems = [pltpu.SemaphoreType.DMA((STORE_COPIES,))]
+    return call(
+        later_kernel, queries, store, (), [VMEM] * 3 + [HBM],
+        buffers(queries, store) + sems, [queries, both, mixer, in_hbm(store)],
+    )[0]
 
 
 def swap(block, bit):
@@ -221,67 +263,48 @@
         return value
 
 
-STEP_US = 1.7
-BYTES_PER_US = 50000
-
-
-def step_times(size, bits):
-    at, sent = 0.0, size
-    sizes = []
-    for _ in range(bits - 1):
-        sent //= 2
-        sizes.append(sent)
-    for size in sizes + [sent] + sizes[::-1]:
-        at += STEP_US + 2 * size / BYTES_PER_US
-        yield at
-
-
-def sum_layers(makers, bits, index):
-    order = Order()
-    chunks = {}
-    events = []
-    for number, (start, ready, size, _) in enumerate(makers):
-        events.append((start, number))
-        events.extend((ready + 2 + at, number) for at in step_times(size, len(bits)) if bits)
-    for _, number in sorted(events):
-        if number not in chunks:
-            chunk = chunks[number] = LayerSum(makers[number][3](order), bits, index)
-        else:
-            chunk = chunks[number]
+def cut(columns):
+    return [columns * k // CUTS for k in range(CUTS + 1)]
+
+
+def rotate(chunks, order):
+    for chunk in chunks:
+        if chunk.moves:
             chunk.take(order)
-        if chunk.moves:
-            chunk.send(order)
-    return [chunks[number].block for number in range(len(makers))]
+            if chunk.moves:
+                chunk.send(order)
 
 
 def shards(store, queries, left_inv, right_inv, query_prompt, winner):
     rows = queries.shape[1]
     columns = store.shape[1]
-    width = min(COLUMNS, columns)
     ex_count = lax.axis_size("ex")
     position = lax.axis_index("ex")
-    places, makers = [], []
+    count = lax.axis_size("layer")
+    index = lax.axis_index("layer")
+    bits = [1 << k for k in range(count.bit_length() - 1)]
+    bits = bits[1:2] + bits[:1] + bits[2:]
+    order = Order()
+    chunks, places = [], []
     current = queries
+    cuts = cut(columns)
     for step in range(ex_count):
-        if step > 0:
+        if step == 0:
+            part, both, mixer = first_scores(queries, left_inv, right_inv, store)
+        else:
             route = [((i - 1) % ex_count, i) for i in range(ex_count)]
             current = lax.ppermute(current, "ex", route)
-        made = []
-        for number, first in enumerate(range(0, columns, width)):
-
-            def make(order, number=number, step=step, current=current, made=made):
-                if number == 0:
-                    block = order.after(current) if step else in_hbm(current)
-                    made.extend(score(block, left_inv, right_inv, store, width))
-                    if step:
-                        made[0] = order.mark(made[0])
-                return made[number]
-
-            makers.append((6.0 + 2.0 * step, 6.0 + 7.0 * step, rows * width, make))
+            part = order.mark(later_scores(order.after(current), both, mixer, store))
+            rotate(chunks, order)
+        for first, end in zip(cuts[:-1], cuts[1:]):
+            chunk = LayerSum(part[:, first:end], bits, index)
+            if chunk.moves:
+                chunk.send(order)
+            chunks.append(chunk)
             places.append(((position - step) % ex_count * rows, jnp.int32(first)))
-    count = lax.axis_size("layer")
-    bits = [1 << k for k in range(count.bit_length() - 1)]
-    done = sum_layers(makers, bits, lax.axis_index("layer"))
+    while any(chunk.moves for chunk in chunks):
+        rotate(chunks, order)
+    done = [chunk.block for chunk in chunks]
     scores = jnp.zeros((rows * ex_count, columns), jnp.bfloat16)
     for place, block in zip(places, done):
         scores = lax.dynamic_update_slice(scores, block, place)

time: 71.2 us -> 65.4 us (0.919)
  starting transfers between devices: 24.7 us -> 20.3 us
  waiting for transfers between devices: 20.3 us -> 24.7 us
  local copies, waits for them, and re-layouts: 3.89 us -> 0.26 us
  Pallas kernels: 19.5 us -> 17.4 us
    ppermute x20 -> x10, waiting for transfers between devices: 20.3 us -> 24.7 us  [swap(): return lax.ppermute(block, 'layer', route)]
    ppermute x20 -> x10, starting transfers between devices: 24.2 us -> 19.8 us  [swap(): return lax.ppermute(block, 'layer', route)]
    unnamed x10 -> x6, local copies, waits for them, and re-layouts: 2.96 us -> 0.02 us
    pallas_call x2, Pallas kernels: 19.5 us -> 17.4 us  [call(): pl.pallas_call(kernel, out_shape=(jax.ShapeDtypeStruct((count, examples),...]
  transfers between devices with their start and end apart: 21 -> 11, of which waited for: 11 -> 9; matrix products, arithmetic and copies ran while one was open for 2% -> 1% of each run, Pallas kernels for 27% -> 13%
where the time goes in v14:
time: 65.4 us; the launch traced here: 65.3 us
  waiting for transfers between devices  24.7 us (38%)
  starting transfers between devices  20.3 us (31%)
  Pallas kernels  17.4 us (27%)
  matrix products  1.07 us (2%)
  between operations  0.83 us (1%)
  other arithmetic  0.66 us (1%)
    ppermute x10, waiting for transfers between devices, swap(): return lax.ppermute(block, 'layer', route)  24.7 us
    ppermute x10, starting transfers between devices, swap(): return lax.ppermute(block, 'layer', route)  19.8 us
    pallas_call x2, Pallas kernels, call(): pl.pallas_call(kernel, out_shape=(jax.ShapeDtypeStruct((count, examples),...  17.4 us
  transfers between devices with their start and end apart: 11, of which 9 were waited for; matrix products, arithmetic and copies ran while one was open for 1% of the time, Pallas kernels for 13%

profile of v14, /device:TPU:0, one launch (start us, length us, event | category | flops | bytes accessed | tf_op | source)
XLA Modules:
  0.0 65.3 jit_solution(16255582037658872294)
XLA Ops:
  0.6 0.5 collective-permute-start.1
  1.1 8.7 %shard_map.77 = (f32[256,1024]{1,0:T(8,128)S(1)}, bf16[256,256]{1,0:T(8,128)(2,1)S(1)}, bf16[256,256]{1,0:T(8,128)(2,1)S(1)}) custom-call(bf16[1,256,4096]{2,1,0:T(8,128)(2,1)} %rows_ref.1, bf16[1,32,32]{2,1,0:T(8,128)(2,1)} %left_ref.1, bf16[1,128,128]{2,1,0:T(8,128)(2,1)} %right_ref.1, bf16[1,1024,4096]{2,1,0:T(8,128)(2,1)} %store_ref.3), custom_call_target="tpu_custom_call" | custom-call | flops 4294967296 | bytes 10485760 | tf_op jit(solution)/shard_map/pallas_call | solution.py:162
  9.9 0.0 collective-permute-done.1.rows_ref
  9.9 8.7 %shard_map.78 = f32[256,1024]{1,0:T(8,128)S(1)} custom-call(bf16[1,256,4096]{2,1,0:T(8,128)(2,1)} %collective-permute-done.1.rows_ref, bf16[256,256]{1,0:T(8,128)(2,1)S(1)} %get-tuple-element.40.both_ref, bf16[256,256]{1,0:T(8,128)(2,1)S(1)} %get-tuple-element.41.mixer_ref, bf16[1,1024,4096]{2,1,0:T(8,128)(2,1)} %store_ref.3), custom_call_target="tpu_custom_call" | custom-call | flops 4294967296 | bytes 10485760 | tf_op jit(solution)/shard_map/pallas_call | solution.py:162
  18.6 0.1 dynamic-slice_convert_fusion
  18.6 2.7 %collective-permute-start = (bf16[128,1024]{1,0:T(8,128)(2,1)S(1)}, bf16[128,1024]{1,0:T(8,128)(2,1)S(1)}, u32[]{:S(2)}, u32[]{:S(2)}) collective-permute-start(bf16[128,1024]{1,0:T(8,128)(2,1)S(1)} %get-tuple-element.38), channel_id=1, source_target_pairs={{0,4},{2,6},{4,0},{6,2},{8,12},{10,14},{12,8},{14,10},{1,5},{3,7},... | collective-permute-start | bytes 786440 | tf_op jit(solution)/shard_map/ppermute | solution.py:212
  21.3 6.9 %collective-permute-done = bf16[128,1024]{1,0:T(8,128)(2,1)S(1)} collective-permute-done((bf16[128,1024]{1,0:T(8,128)(2,1)S(1)}, bf16[128,1024]{1,0:T(8,128)(2,1)S(1)}, u32[]{:S(2)}, u32[]{:S(2)}) %collective-permute-start) | collective-permute-done | bytes 262176 | tf_op jit(solution)/shard_map/ppermute | solution.py:212
  28.3 0.1 convert_add_fusion.1
  28.4 1.7 %collective-permute-start.2 = (bf16[64,1024]{1,0:T(8,128)(2,1)S(1)}, bf16[64,1024]{1,0:T(8,128)(2,1)S(1)}, u32[]{:S(2)}, u32[]{:S(2)}) collective-permute-start(bf16[64,1024]{1,0:T(8,128)(2,1)S(1)} %dynamic-slice_convert_fusion.3), channel_id=1, source_target_pairs={{0,2},{2,0},{4,6},{6,4},{8,10},{10,8},{12,14},{14,12},{1,3},{3,1},... | collective-permute-start | bytes 393224 | tf_op jit(solution)/shard_map/ppermute | solution.py:212
  30.1 1.6 %collective-permute-start.4 = (bf16[128,1024]{1,0:T(8,128)(2,1)S(1)}, bf16[128,1024]{1,0:T(8,128)(2,1)S(1)}, u32[]{:S(2)}, u32[]{:S(2)}) collective-permute-start(bf16[128,1024]{1,0:T(8,128)(2,1)S(1)} %get-tuple-element.50), channel_id=1, source_target_pairs={{0,4},{2,6},{4,0},{6,2},{8,12},{10,14},{12,8},{14,10},{1,5},{3,7},... | collective-permute-start | bytes 786440 | tf_op jit(solution)/shard_map/ppermute | solution.py:212
  31.7 2.0 %collective-permute-done.2 = bf16[64,1024]{1,0:T(8,128)(2,1)S(1)} collective-permute-done((bf16[64,1024]{1,0:T(8,128)(2,1)S(1)}, bf16[64,1024]{1,0:T(8,128)(2,1)S(1)}, u32[]{:S(2)}, u32[]{:S(2)}) %collective-permute-start.2) | collective-permute-done | bytes 131104 | tf_op jit(solution)/shard_map/ppermute | solution.py:212
  33.7 2.6 %collective-permute-start.3 = (bf16[64,1024]{1,0:T(8,128)(2,1)S(1)}, bf16[64,1024]{1,0:T(8,128)(2,1)S(1)}, u32[]{:S(2)}, u32[]{:S(2)}) collective-permute-start(bf16[64,1024]{1,0:T(8,128)(2,1)S(1)} %add_convert_fusion.3), channel_id=1, source_target_pairs={{0,8},{2,10},{4,12},{6,14},{8,0},{10,2},{12,4},{14,6},{1,9},{3,11}... | collective-permute-start | bytes 393224 | tf_op jit(solution)/shard_map/ppermute | solution.py:212
  36.4 3.6 %collective-permute-done.4 = bf16[128,1024]{1,0:T(8,128)(2,1)S(1)} collective-permute-done((bf16[128,1024]{1,0:T(8,128)(2,1)S(1)}, bf16[128,1024]{1,0:T(8,128)(2,1)S(1)}, u32[]{:S(2)}, u32[]{:S(2)}) %collective-permute-start.4) | collective-permute-done | bytes 262176 | tf_op jit(solution)/shard_map/ppermute | solution.py:212
  40.0 0.1 convert_add_fusion
  40.1 0.1 collective-permute-start.6
  40.2 0.8 %collective-permute-done.3 = bf16[64,1024]{1,0:T(8,128)(2,1)S(1)} collective-permute-done((bf16[64,1024]{1,0:T(8,128)(2,1)S(1)}, bf16[64,1024]{1,0:T(8,128)(2,1)S(1)}, u32[]{:S(2)}, u32[]{:S(2)}) %collective-permute-start.3) | collective-permute-done | bytes 131104 | tf_op jit(solution)/shard_map/ppermute | solution.py:212
  41.0 2.5 %collective-permute-start.5 = (bf16[64,1024]{1,0:T(8,128)(2,1)S(1)}, bf16[64,1024]{1,0:T(8,128)(2,1)S(1)}, u32[]{:S(2)}, u32[]{:S(2)}) collective-permute-start(bf16[64,1024]{1,0:T(8,128)(2,1)S(1)} %add_convert_fusion.2), channel_id=1, source_target_pairs={{0,2},{2,0},{4,6},{6,4},{8,10},{10,8},{12,14},{14,12},{1,3},{3,1},... | collective-permute-start | bytes 393224 | tf_op jit(solution)/shard_map/ppermute | solution.py:212
  43.5 1.6 %collective-permute-done.6 = bf16[64,1024]{1,0:T(8,128)(2,1)S(1)} collective-permute-done((bf16[64,1024]{1,0:T(8,128)(2,1)S(1)}, bf16[64,1024]{1,0:T(8,128)(2,1)S(1)}, u32[]{:S(2)}, u32[]{:S(2)}) %collective-permute-start.6) | collective-permute-done | bytes 131104 | tf_op jit(solution)/shard_map/ppermute | solution.py:212
  45.2 1.8 %collective-permute-start.8 = (bf16[64,1024]{1,0:T(8,128)(2,1)S(1)}, bf16[64,1024]{1,0:T(8,128)(2,1)S(1)}, u32[]{:S(2)}, u32[]{:S(2)}) collective-permute-start(bf16[64,1024]{1,0:T(8,128)(2,1)S(1)} %add_convert_fusion.1), channel_id=1, source_target_pairs={{0,8},{2,10},{4,12},{6,14},{8,0},{10,2},{12,4},{14,6},{1,9},{3,11}... | collective-permute-start | bytes 393224 | tf_op jit(solution)/shard_map/ppermute | solution.py:212
  47.0 0.0 collective-permute-done.5
  47.0 2.8 %collective-permute-start.7 = (bf16[128,1024]{1,0:T(8,128)(2,1)S(1)}, bf16[128,1024]{1,0:T(8,128)(2,1)S(1)}, u32[]{:S(2)}, u32[]{:S(2)}) collective-permute-start(bf16[128,1024]{1,0:T(8,128)(2,1)S(1)} %pad_maximum_fusion), channel_id=1, source_target_pairs={{0,4},{2,6},{4,0},{6,2},{8,12},{10,14},{12,8},{14,10},{1,5},{3,7},... | collective-permute-start | bytes 786440 | tf_op jit(solution)/shard_map/ppermute | solution.py:212
  49.8 1.4 %collective-permute-done.8 = bf16[64,1024]{1,0:T(8,128)(2,1)S(1)} collective-permute-done((bf16[64,1024]{1,0:T(8,128)(2,1)S(1)}, bf16[64,1024]{1,0:T(8,128)(2,1)S(1)}, u32[]{:S(2)}, u32[]{:S(2)}) %collective-permute-start.8) | collective-permute-done | bytes 131104 | tf_op jit(solution)/shard_map/ppermute | solution.py:212
  51.2 0.8 %collective-permute-start.9 = (bf16[64,1024]{1,0:T(8,128)(2,1)S(1)}, bf16[64,1024]{1,0:T(8,128)(2,1)S(1)}, u32[]{:S(2)}, u32[]{:S(2)}) collective-permute-start(bf16[64,1024]{1,0:T(8,128)(2,1)S(1)} %add_convert_fusion), channel_id=1, source_target_pairs={{0,2},{2,0},{4,6},{6,4},{8,10},{10,8},{12,14},{14,12},{1,3},{3,1},... | collective-permute-start | bytes 393224 | tf_op jit(solution)/shard_map/ppermute | solution.py:212
  52.0 3.0 %collective-permute-done.7 = bf16[128,1024]{1,0:T(8,128)(2,1)S(1)} collective-permute-done((bf16[128,1024]{1,0:T(8,128)(2,1)S(1)}, bf16[128,1024]{1,0:T(8,128)(2,1)S(1)}, u32[]{:S(2)}, u32[]{:S(2)}) %collective-permute-start.7) | collective-permute-done | bytes 262176 | tf_op jit(solution)/shard_map/ppermute | solution.py:212
  55.0 1.3 %collective-permute-done.9 = bf16[64,1024]{1,0:T(8,128)(2,1)S(1)} collective-permute-done((bf16[64,1024]{1,0:T(8,128)(2,1)S(1)}, bf16[64,1024]{1,0:T(8,128)(2,1)S(1)}, u32[]{:S(2)}, u32[]{:S(2)}) %collective-permute-start.9) | collective-permute-done | bytes 131104 | tf_op jit(solution)/shard_map/ppermute | solution.py:212
  56.3 3.3 %collective-permute-start.10 = (bf16[128,1024]{1,0:T(8,128)(2,1)S(1)}, bf16[128,1024]{1,0:T(8,128)(2,1)S(1)}, u32[]{:S(2)}, u32[]{:S(2)}) collective-permute-start(bf16[128,1024]{1,0:T(8,128)(2,1)S(1)} %pad_maximum_fusion.1), channel_id=1, source_target_pairs={{0,4},{2,6},{4,0},{6,2},{8,12},{10,14},{12,8},{14,10},{1,5},{3,7},... | collective-permute-start | bytes 786440 | tf_op jit(solution)/shard_map/ppermute | solution.py:212
  59.6 0.1 broadcast_select_fusion.3
  59.7 0.0 copy-start.1
  59.8 0.0 copy-start.2
  59.8 0.1 broadcast_in_dim.2
  60.0 4.0 %collective-permute-done.10 = bf16[128,1024]{1,0:T(8,128)(2,1)S(1)} collective-permute-done((bf16[128,1024]{1,0:T(8,128)(2,1)S(1)}, bf16[128,1024]{1,0:T(8,128)(2,1)S(1)}, u32[]{:S(2)}, u32[]{:S(2)}) %collective-permute-start.10) | collective-permute-done | bytes 262176 | tf_op jit(solution)/shard_map/ppermute | solution.py:212
  64.0 0.1 broadcast_select_fusion.1
  64.2 0.0 copy-done.1
  64.2 0.0 copy-done.2
  64.2 0.0 copy-start
  64.2 1.1 %convolution_convert_fusion = bf16[128,1024]{1,0:T(8,128)(2,1)} fusion(bf16[512,1024]{1,0:T(8,128)(2,1)S(1)} %maximum_dynamic-update-slice_fusion.1, s32[512]{0:T(512)S(1)} %copy-done.1, s32[128]{0:T(128)S(1)} %copy-done.2), kind=kOutput, calls=%fused_computation | convolution fusion | flops 134742016 | bytes 1313280 | tf_op jit(solution)/shard_map/dot_general | solution.py:316
  65.3 0.0 copy-done
  (12 shorter events, 0.4 us)
Async XLA Ops:
  0.6 9.2 %collective-permute-start.1 = (bf16[1,256,4096]{2,1,0:T(8,128)(2,1)}, bf16[1,256,4096]{2,1,0:T(8,128)(2,1)}, u32[]{:S(2)}, u32[]{:S(2)}) collective-permute-start(bf16[1,256,4096]{2,1,0:T(8,128)(2,1)} %rows_ref.1), channel_id=1, source_target_pairs={{1,0},{0,1},{3,2},{2,3},{5,4},{4,5},{7,6},{6,7},{9,8},{8,9},{11,10... | collective-permute-start | bytes 6291464 | tf_op jit(solution)/shard_map/ppermute | solution.py:296
  18.6 9.6 %collective-permute-start = (bf16[128,1024]{1,0:T(8,128)(2,1)S(1)}, bf16[128,1024]{1,0:T(8,128)(2,1)S(1)}, u32[]{:S(2)}, u32[]{:S(2)}) collective-permute-start(bf16[128,1024]{1,0:T(8,128)(2,1)S(1)} %get-tuple-element.38), channel_id=1, source_target_pairs={{0,4},{2,6},{4,0},{6,2},{8,12},{10,14},{12,8},{14,10},{1,5},{3,7},... | collective-permute-start | bytes 786440 | tf_op jit(solution)/shard_map/ppermute | solution.py:212
  28.4 5.4 %collective-permute-start.2 = (bf16[64,1024]{1,0:T(8,128)(2,1)S(1)}, bf16[64,1024]{1,0:T(8,128)(2,1)S(1)}, u32[]{:S(2)}, u32[]{:S(2)}) collective-permute-start(bf16[64,1024]{1,0:T(8,128)(2,1)S(1)} %dynamic-slice_convert_fusion.3), channel_id=1, source_target_pairs={{0,2},{2,0},{4,6},{6,4},{8,10},{10,8},{12,14},{14,12},{1,3},{3,1},... | collective-permute-start | bytes 393224 | tf_op jit(solution)/shard_map/ppermute | solution.py:212
  30.1 9.9 %collective-permute-start.4 = (bf16[128,1024]{1,0:T(8,128)(2,1)S(1)}, bf16[128,1024]{1,0:T(8,128)(2,1)S(1)}, u32[]{:S(2)}, u32[]{:S(2)}) collective-permute-start(bf16[128,1024]{1,0:T(8,128)(2,1)S(1)} %get-tuple-element.50), channel_id=1, source_target_pairs={{0,4},{2,6},{4,0},{6,2},{8,12},{10,14},{12,8},{14,10},{1,5},{3,7},... | collective-permute-start | bytes 786440 | tf_op jit(solution)/shard_map/ppermute | solution.py:212
  33.7 7.3 %collective-permute-start.3 = (bf16[64,1024]{1,0:T(8,128)(2,1)S(1)}, bf16[64,1024]{1,0:T(8,128)(2,1)S(1)}, u32[]{:S(2)}, u32[]{:S(2)}) collective-permute-start(bf16[64,1024]{1,0:T(8,128)(2,1)S(1)} %add_convert_fusion.3), channel_id=1, source_target_pairs={{0,8},{2,10},{4,12},{6,14},{8,0},{10,2},{12,4},{14,6},{1,9},{3,11}... | collective-permute-start | bytes 393224 | tf_op jit(solution)/shard_map/ppermute | solution.py:212
  40.1 5.0 %collective-permute-start.6 = (bf16[64,1024]{1,0:T(8,128)(2,1)S(1)}, bf16[64,1024]{1,0:T(8,128)(2,1)S(1)}, u32[]{:S(2)}, u32[]{:S(2)}) collective-permute-start(bf16[64,1024]{1,0:T(8,128)(2,1)S(1)} %dynamic-slice_convert_fusion.2), channel_id=1, source_target_pairs={{0,2},{2,0},{4,6},{6,4},{8,10},{10,8},{12,14},{14,12},{1,3},{3,1},... | collective-permute-start | bytes 393224 | tf_op jit(solution)/shard_map/ppermute | solution.py:212
  41.0 5.9 %collective-permute-start.5 = (bf16[64,1024]{1,0:T(8,128)(2,1)S(1)}, bf16[64,1024]{1,0:T(8,128)(2,1)S(1)}, u32[]{:S(2)}, u32[]{:S(2)}) collective-permute-start(bf16[64,1024]{1,0:T(8,128)(2,1)S(1)} %add_convert_fusion.2), channel_id=1, source_target_pairs={{0,2},{2,0},{4,6},{6,4},{8,10},{10,8},{12,14},{14,12},{1,3},{3,1},... | collective-permute-start | bytes 393224 | tf_op jit(solution)/shard_map/ppermute | solution.py:212
  45.2 6.0 %collective-permute-start.8 = (bf16[64,1024]{1,0:T(8,128)(2,1)S(1)}, bf16[64,1024]{1,0:T(8,128)(2,1)S(1)}, u32[]{:S(2)}, u32[]{:S(2)}) collective-permute-start(bf16[64,1024]{1,0:T(8,128)(2,1)S(1)} %add_convert_fusion.1), channel_id=1, source_target_pairs={{0,8},{2,10},{4,12},{6,14},{8,0},{10,2},{12,4},{14,6},{1,9},{3,11}... | collective-permute-start | bytes 393224 | tf_op jit(solution)/shard_map/ppermute | solution.py:212
  47.0 8.0 %collective-permute-start.7 = (bf16[128,1024]{1,0:T(8,128)(2,1)S(1)}, bf16[128,1024]{1,0:T(8,128)(2,1)S(1)}, u32[]{:S(2)}, u32[]{:S(2)}) collective-permute-start(bf16[128,1024]{1,0:T(8,128)(2,1)S(1)} %pad_maximum_fusion), channel_id=1, source_target_pairs={{0,4},{2,6},{4,0},{6,2},{8,12},{10,14},{12,8},{14,10},{1,5},{3,7},... | collective-permute-start | bytes 786440 | tf_op jit(solution)/shard_map/ppermute | solution.py:212
  51.2 5.0 %collective-permute-start.9 = (bf16[64,1024]{1,0:T(8,128)(2,1)S(1)}, bf16[64,1024]{1,0:T(8,128)(2,1)S(1)}, u32[]{:S(2)}, u32[]{:S(2)}) collective-permute-start(bf16[64,1024]{1,0:T(8,128)(2,1)S(1)} %add_convert_fusion), channel_id=1, source_target_pairs={{0,2},{2,0},{4,6},{6,4},{8,10},{10,8},{12,14},{14,12},{1,3},{3,1},... | collective-permute-start | bytes 393224 | tf_op jit(solution)/shard_map/ppermute | solution.py:212
  56.3 7.7 %collective-permute-start.10 = (bf16[128,1024]{1,0:T(8,128)(2,1)S(1)}, bf16[128,1024]{1,0:T(8,128)(2,1)S(1)}, u32[]{:S(2)}, u32[]{:S(2)}) collective-permute-start(bf16[128,1024]{1,0:T(8,128)(2,1)S(1)} %pad_maximum_fusion.1), channel_id=1, source_target_pairs={{0,4},{2,6},{4,0},{6,2},{8,12},{10,14},{12,8},{14,10},{1,5},{3,7},... | collective-permute-start | bytes 786440 | tf_op jit(solution)/shard_map/ppermute | solution.py:212
  59.7 4.4 %copy-start.1 = (s32[512]{0:T(512)S(1)}, s32[512]{0:T(512)}, u32[]{:S(2)}) copy-start(s32[512]{0:T(512)} %param.10) | copy-start | bytes 6148
  59.8 4.4 %copy-start.2 = (s32[128]{0:T(128)S(1)}, s32[128]{0:T(128)}, u32[]{:S(2)}) copy-start(s32[128]{0:T(128)} %param.11) | copy-start | bytes 1540
  64.2 1.1 %copy-start = (bf16[512,1024]{1,0:T(8,128)(2,1)}, bf16[512,1024]{1,0:T(8,128)(2,1)S(1)}, u32[]{:S(2)}) copy-start(bf16[512,1024]{1,0:T(8,128)(2,1)S(1)} %maximum_dynamic-update-slice_fusion.1) | copy-start | bytes 3145732

commit v15 on v14

--- a/solution.py
+++ b/solution.py
@@ -15,7 +15,7 @@
 PAIR = 2 * KOUT
 DEPTH_BLOCK = 512
 COLUMNS = 512
-CUTS = 1
+CUTS = 2
 ROW_COPIES = 2
 STORE_COPIES = 4
 VMEM_LIMIT = 32 * 1024 * 1024
@@ -139,9 +139,9 @@
 
 
 def later_kernel(
-    rows_ref, both_ref, mixer_ref, store_ref, out_ref,
-    pre_ref, store_vmem, half_ref, total_ref, store_sems,
+    sent, rows_ref, both_ref, mixer_ref, store_ref, *refs,
 ):
+    out_ref, pre_ref, store_vmem, half_ref, total_ref, store_sems = refs[sent:]
     copies = copies_of(store_ref.at[0], store_vmem, store_sems)
     start(copies)
     precondition(rows_ref.at[0], both_ref[...], mixer_ref[...], half_ref, pre_ref)
@@ -150,6 +150,7 @@
 
 VMEM = pl.BlockSpec(memory_space=pltpu.VMEM)
 HBM = pl.BlockSpec(memory_space=pltpu.HBM)
+ANYWHERE = pl.BlockSpec(memory_space=pl.ANY)
 
 
 def in_hbm(array):
@@ -199,11 +200,12 @@
     )
 
 
-def later_scores(queries, both, mixer, store):
+def later_scores(queries, both, mixer, store, sent):
     sems = [pltpu.SemaphoreType.DMA((STORE_COPIES,))]
     return call(
-        later_kernel, queries, store, (), [VMEM] * 3 + [HBM],
-        buffers(queries, store) + sems, [queries, both, mixer, in_hbm(store)],
+        functools.partial(later_kernel, len(sent)), queries, store, (),
+        [VMEM] * 3 + [HBM] + [ANYWHERE] * len(sent), buffers(queries, store) + sems,
+        [queries, both, mixer, in_hbm(store), *sent],
     )[0]
 
 
@@ -233,7 +235,8 @@
             sent = lax.dynamic_slice_in_dim(self.block, (1 - upper) * rows, rows, 0)
             sent = sent.astype(jnp.bfloat16)
             self.block = lax.dynamic_slice_in_dim(self.block, upper * rows, rows, 0)
-        self.received = swap(order.after(sent), bit)
+        self.sent = order.mark(sent)
+        self.received = swap(self.sent, bit)
 
     def take(self, order):
         bit, kind = self.moves.pop(0)
@@ -283,7 +286,7 @@
     count = lax.axis_size("layer")
     index = lax.axis_index("layer")
     bits = [1 << k for k in range(count.bit_length() - 1)]
-    bits = bits[1:2] + bits[:1] + bits[2:]
+    orders = [bits[1:2] + bits[:1] + bits[2:], bits]
     order = Order()
     chunks, places = [], []
     current = queries
@@ -294,10 +297,11 @@
         else:
             route = [((i - 1) % ex_count, i) for i in range(ex_count)]
             current = lax.ppermute(current, "ex", route)
-            part = order.mark(later_scores(order.after(current), both, mixer, store))
+            sent = [chunk.sent for chunk in chunks if chunk.moves]
+            part = order.mark(later_scores(order.after(current), both, mixer, store, sent))
             rotate(chunks, order)
-        for first, end in zip(cuts[:-1], cuts[1:]):
-            chunk = LayerSum(part[:, first:end], bits, index)
+        for number, (first, end) in enumerate(zip(cuts[:-1], cuts[1:])):
+            chunk = LayerSum(part[:, first:end], orders[number % 2], index)
             if chunk.moves:
                 chunk.send(order)
             chunks.append(chunk)

time: 65.4 us -> 56.6 us (0.87)
  waiting for transfers between devices: 24.7 us -> 11.9 us
  starting transfers between devices: 20.3 us -> 24.6 us
  Pallas kernels: 17.4 us -> 16.4 us
    ppermute x10 -> x20, waiting for transfers between devices: 24.7 us -> 11.9 us  [swap(): return lax.ppermute(block, 'layer', route)]
    ppermute x10 -> x20, starting transfers between devices: 19.8 us -> 24.1 us  [swap(): return lax.ppermute(block, 'layer', route)]
    pallas_call x2, Pallas kernels: 17.4 us -> 16.4 us  [call(): pl.pallas_call(kernel, out_shape=(jax.ShapeDtypeStruct((count, examples),...]
  transfers between devices with their start and end apart: 11 -> 21, of which waited for: 9 -> 9; matrix products, arithmetic and copies ran while one was open for 1% -> 2% of each run, Pallas kernels for 13% -> 29%
where the time goes in v15:
time: 56.6 us; the launch traced here: 56.4 us
  starting transfers between devices  24.6 us (43%)
  Pallas kernels  16.4 us (29%)
  waiting for transfers between devices  11.9 us (21%)
  matrix products  1.08 us (2%)
  between operations  0.96 us (2%)
  local copies, waits for them, and re-layouts  0.8 us (1%)
  other arithmetic  0.66 us (1%)
    ppermute x20, starting transfers between devices, swap(): return lax.ppermute(block, 'layer', route)  24.1 us
    pallas_call x2, Pallas kernels, call(): pl.pallas_call(kernel, out_shape=(jax.ShapeDtypeStruct((count, examples),...  16.4 us
    ppermute x20, waiting for transfers between devices, swap(): return lax.ppermute(block, 'layer', route)  11.9 us
  transfers between devices with their start and end apart: 21, of which 9 were waited for; matrix products, arithmetic and copies ran while one was open for 2% of the time, Pallas kernels for 29%

profile of v15, /device:TPU:0, one launch (start us, length us, event | category | flops | bytes accessed | tf_op | source)
XLA Modules:
  0.0 56.4 jit_solution(12898121679642630364)
XLA Ops:
  0.6 0.5 collective-permute-start.1
  1.1 8.7 %shard_map.77 = (f32[256,1024]{1,0:T(8,128)S(1)}, bf16[256,256]{1,0:T(8,128)(2,1)S(1)}, bf16[256,256]{1,0:T(8,128)(2,1)S(1)}) custom-call(bf16[1,256,4096]{2,1,0:T(8,128)(2,1)} %rows_ref.1, bf16[1,32,32]{2,1,0:T(8,128)(2,1)} %left_ref.1, bf16[1,128,128]{2,1,0:T(8,128)(2,1)} %right_ref.1, bf16[1,1024,4096]{2,1,0:T(8,128)(2,1)} %store_ref.3), custom_call_target="tpu_custom_call" | custom-call | flops 4294967296 | bytes 10485760 | tf_op jit(solution)/shard_map/pallas_call | solution.py:163
  9.9 0.1 fusion.7
  9.9 0.0 copy-start.1
  10.0 2.7 %collective-permute-start = (bf16[128,512]{1,0:T(8,128)(2,1)S(1)}, bf16[128,512]{1,0:T(8,128)(2,1)S(1)}, u32[]{:S(2)}, u32[]{:S(2)}) collective-permute-start(bf16[128,512]{1,0:T(8,128)(2,1)S(1)} %get-tuple-element.60.refs_0_), channel_id=1, source_target_pairs={{0,4},{2,6},{4,0},{6,2},{8,12},{10,14},{12,8},{14,10},{1,5},{3,7},... | collective-permute-start | bytes 393224 | tf_op jit(solution)/shard_map/ppermute | solution.py:214
  12.7 0.0 copy-done.1
  12.7 1.5 %collective-permute-start.3 = (bf16[128,512]{1,0:T(8,128)(2,1)S(1)}, bf16[128,512]{1,0:T(8,128)(2,1)S(1)}, u32[]{:S(2)}, u32[]{:S(2)}) collective-permute-start(bf16[128,512]{1,0:T(8,128)(2,1)S(1)} %get-tuple-element.66.refs_1_), channel_id=1, source_target_pairs={{0,2},{2,0},{4,6},{6,4},{8,10},{10,8},{12,14},{14,12},{1,3},{3,1},... | collective-permute-start | bytes 393224 | tf_op jit(solution)/shard_map/ppermute | solution.py:214
  14.2 0.0 collective-permute-done.1.rows_ref
  14.2 7.7 %shard_map.78 = f32[256,1024]{1,0:T(8,128)S(1)} custom-call(bf16[1,256,4096]{2,1,0:T(8,128)(2,1)S(1)} %collective-permute-done.1.rows_ref, bf16[256,256]{1,0:T(8,128)(2,1)S(1)} %get-tuple-element.64.both_ref, bf16[256,256]{1,0:T(8,128)(2,1)S(1)} %get-tuple-element.65.mixer_ref, bf16[1,1024,4096]{2,1,0:T(8,128)(2,1)} %store_ref.3, ...), custom_call_target="tpu_custom_call" | custom-call | flops 4294967296 | bytes 10485760 | tf_op jit(solution)/shard_map/pallas_call | solution.py:163
  21.9 0.0 copy-start.2
  21.9 0.1 fusion.6
  22.0 0.6 %collective-permute-start.5 = (bf16[128,512]{1,0:T(8,128)(2,1)S(1)}, bf16[128,512]{1,0:T(8,128)(2,1)S(1)}, u32[]{:S(2)}, u32[]{:S(2)}) collective-permute-start(bf16[128,512]{1,0:T(8,128)(2,1)S(1)} %dynamic-slice_convert_fusion.1), channel_id=1, source_target_pairs={{0,2},{2,0},{4,6},{6,4},{8,10},{10,8},{12,14},{14,12},{1,3},{3,1},... | collective-permute-start | bytes 393224 | tf_op jit(solution)/shard_map/ppermute | solution.py:214
  22.6 0.0 collective-permute-done
  22.6 0.3 copy-done.2
  23.0 0.0 collective-permute-done.3
  23.0 0.7 %collective-permute-start.7 = (bf16[64,512]{1,0:T(8,128)(2,1)S(1)}, bf16[64,512]{1,0:T(8,128)(2,1)S(1)}, u32[]{:S(2)}, u32[]{:S(2)}) collective-permute-start(bf16[64,512]{1,0:T(8,128)(2,1)S(1)} %dynamic-slice_convert_fusion.6), channel_id=1, source_target_pairs={{0,4},{2,6},{4,0},{6,2},{8,12},{10,14},{12,8},{14,10},{1,5},{3,7},... | collective-permute-start | bytes 196616 | tf_op jit(solution)/shard_map/ppermute | solution.py:214
  23.8 1.4 %collective-permute-start.6 = (bf16[128,512]{1,0:T(8,128)(2,1)S(1)}, bf16[128,512]{1,0:T(8,128)(2,1)S(1)}, u32[]{:S(2)}, u32[]{:S(2)}) collective-permute-start(bf16[128,512]{1,0:T(8,128)(2,1)S(1)} %dynamic-slice_convert_fusion), channel_id=1, source_target_pairs={{0,4},{2,6},{4,0},{6,2},{8,12},{10,14},{12,8},{14,10},{1,5},{3,7},... | collective-permute-start | bytes 393224 | tf_op jit(solution)/shard_map/ppermute | solution.py:214
  25.2 1.2 %collective-permute-start.2 = (bf16[64,512]{1,0:T(8,128)(2,1)S(1)}, bf16[64,512]{1,0:T(8,128)(2,1)S(1)}, u32[]{:S(2)}, u32[]{:S(2)}) collective-permute-start(bf16[64,512]{1,0:T(8,128)(2,1)S(1)} %dynamic-slice_convert_fusion.7), channel_id=1, source_target_pairs={{0,2},{2,0},{4,6},{6,4},{8,10},{10,8},{12,14},{14,12},{1,3},{3,1},... | collective-permute-start | bytes 196616 | tf_op jit(solution)/shard_map/ppermute | solution.py:214
  26.4 1.6 %collective-permute-done.7 = bf16[64,512]{1,0:T(8,128)(2,1)S(1)} collective-permute-done((bf16[64,512]{1,0:T(8,128)(2,1)S(1)}, bf16[64,512]{1,0:T(8,128)(2,1)S(1)}, u32[]{:S(2)}, u32[]{:S(2)}) %collective-permute-start.7) | collective-permute-done | bytes 65568 | tf_op jit(solution)/shard_map/ppermute | solution.py:214
  28.1 2.7 %collective-permute-start.11 = (bf16[64,512]{1,0:T(8,128)(2,1)S(1)}, bf16[64,512]{1,0:T(8,128)(2,1)S(1)}, u32[]{:S(2)}, u32[]{:S(2)}) collective-permute-start(bf16[64,512]{1,0:T(8,128)(2,1)S(1)} %add_convert_fusion.6), channel_id=1, source_target_pairs={{0,8},{2,10},{4,12},{6,14},{8,0},{10,2},{12,4},{14,6},{1,9},{3,11}... | collective-permute-start | bytes 196616 | tf_op jit(solution)/shard_map/ppermute | solution.py:214
  30.8 0.0 collective-permute-done.2
  30.8 1.4 %collective-permute-start.4 = (bf16[64,512]{1,0:T(8,128)(2,1)S(1)}, bf16[64,512]{1,0:T(8,128)(2,1)S(1)}, u32[]{:S(2)}, u32[]{:S(2)}) collective-permute-start(bf16[64,512]{1,0:T(8,128)(2,1)S(1)} %add_convert_fusion.7), channel_id=1, source_target_pairs={{0,8},{2,10},{4,12},{6,14},{8,0},{10,2},{12,4},{14,6},{1,9},{3,11}... | collective-permute-start | bytes 196616 | tf_op jit(solution)/shard_map/ppermute | solution.py:214
  32.2 0.0 collective-permute-done.5
  32.2 0.7 %collective-permute-start.9 = (bf16[64,512]{1,0:T(8,128)(2,1)S(1)}, bf16[64,512]{1,0:T(8,128)(2,1)S(1)}, u32[]{:S(2)}, u32[]{:S(2)}) collective-permute-start(bf16[64,512]{1,0:T(8,128)(2,1)S(1)} %dynamic-slice_convert_fusion.4), channel_id=1, source_target_pairs={{0,4},{2,6},{4,0},{6,2},{8,12},{10,14},{12,8},{14,10},{1,5},{3,7},... | collective-permute-start | bytes 196616 | tf_op jit(solution)/shard_map/ppermute | solution.py:214
  33.0 0.0 collective-permute-done.6
  33.0 1.3 %collective-permute-start.10 = (bf16[64,512]{1,0:T(8,128)(2,1)S(1)}, bf16[64,512]{1,0:T(8,128)(2,1)S(1)}, u32[]{:S(2)}, u32[]{:S(2)}) collective-permute-start(bf16[64,512]{1,0:T(8,128)(2,1)S(1)} %dynamic-slice_convert_fusion.5), channel_id=1, source_target_pairs={{0,2},{2,0},{4,6},{6,4},{8,10},{10,8},{12,14},{14,12},{1,3},{3,1},... | collective-permute-start | bytes 196616 | tf_op jit(solution)/shard_map/ppermute | solution.py:214
  34.3 1.0 %collective-permute-done.11 = bf16[64,512]{1,0:T(8,128)(2,1)S(1)} collective-permute-done((bf16[64,512]{1,0:T(8,128)(2,1)S(1)}, bf16[64,512]{1,0:T(8,128)(2,1)S(1)}, u32[]{:S(2)}, u32[]{:S(2)}) %collective-permute-start.11) | collective-permute-done | bytes 65568 | tf_op jit(solution)/shard_map/ppermute | solution.py:214
  35.3 0.5 collective-permute-start.13
  35.8 1.0 %collective-permute-done.4 = bf16[64,512]{1,0:T(8,128)(2,1)S(1)} collective-permute-done((bf16[64,512]{1,0:T(8,128)(2,1)S(1)}, bf16[64,512]{1,0:T(8,128)(2,1)S(1)}, u32[]{:S(2)}, u32[]{:S(2)}) %collective-permute-start.4) | collective-permute-done | bytes 65568 | tf_op jit(solution)/shard_map/ppermute | solution.py:214
  36.7 1.0 %collective-permute-start.8 = (bf16[64,512]{1,0:T(8,128)(2,1)S(1)}, bf16[64,512]{1,0:T(8,128)(2,1)S(1)}, u32[]{:S(2)}, u32[]{:S(2)}) collective-permute-start(bf16[64,512]{1,0:T(8,128)(2,1)S(1)} %add_convert_fusion.5), channel_id=1, source_target_pairs={{0,2},{2,0},{4,6},{6,4},{8,10},{10,8},{12,14},{14,12},{1,3},{3,1},... | collective-permute-start | bytes 196616 | tf_op jit(solution)/shard_map/ppermute | solution.py:214
  37.7 0.0 collective-permute-done.9
  37.8 1.6 %collective-permute-start.18 = (bf16[64,512]{1,0:T(8,128)(2,1)S(1)}, bf16[64,512]{1,0:T(8,128)(2,1)S(1)}, u32[]{:S(2)}, u32[]{:S(2)}) collective-permute-start(bf16[64,512]{1,0:T(8,128)(2,1)S(1)} %add_convert_fusion.2), channel_id=1, source_target_pairs={{0,8},{2,10},{4,12},{6,14},{8,0},{10,2},{12,4},{14,6},{1,9},{3,11}... | collective-permute-start | bytes 196616 | tf_op jit(solution)/shard_map/ppermute | solution.py:214
  39.3 0.0 collective-permute-done.10
  39.4 1.5 %collective-permute-start.15 = (bf16[64,512]{1,0:T(8,128)(2,1)S(1)}, bf16[64,512]{1,0:T(8,128)(2,1)S(1)}, u32[]{:S(2)}, u32[]{:S(2)}) collective-permute-start(bf16[64,512]{1,0:T(8,128)(2,1)S(1)} %add_convert_fusion.3), channel_id=1, source_target_pairs={{0,8},{2,10},{4,12},{6,14},{8,0},{10,2},{12,4},{14,6},{1,9},{3,11}... | collective-permute-start | bytes 196616 | tf_op jit(solution)/shard_map/ppermute | solution.py:214
  40.8 0.0 collective-permute-done.13
  40.9 1.2 %collective-permute-start.14 = (bf16[128,512]{1,0:T(8,128)(2,1)S(1)}, bf16[128,512]{1,0:T(8,128)(2,1)S(1)}, u32[]{:S(2)}, u32[]{:S(2)}) collective-permute-start(bf16[128,512]{1,0:T(8,128)(2,1)S(1)} %pad_maximum_fusion.1), channel_id=1, source_target_pairs={{0,2},{2,0},{4,6},{6,4},{8,10},{10,8},{12,14},{14,12},{1,3},{3,1},... | collective-permute-start | bytes 393224 | tf_op jit(solution)/shard_map/ppermute | solution.py:214
  42.0 0.0 collective-permute-done.8
  42.1 0.8 %collective-permute-start.12 = (bf16[128,512]{1,0:T(8,128)(2,1)S(1)}, bf16[128,512]{1,0:T(8,128)(2,1)S(1)}, u32[]{:S(2)}, u32[]{:S(2)}) collective-permute-start(bf16[128,512]{1,0:T(8,128)(2,1)S(1)} %pad_maximum_fusion), channel_id=1, source_target_pairs={{0,4},{2,6},{4,0},{6,2},{8,12},{10,14},{12,8},{14,10},{1,5},{3,7},... | collective-permute-start | bytes 393224 | tf_op jit(solution)/shard_map/ppermute | solution.py:214
  42.8 0.7 %collective-permute-done.18 = bf16[64,512]{1,0:T(8,128)(2,1)S(1)} collective-permute-done((bf16[64,512]{1,0:T(8,128)(2,1)S(1)}, bf16[64,512]{1,0:T(8,128)(2,1)S(1)}, u32[]{:S(2)}, u32[]{:S(2)}) %collective-permute-start.18) | collective-permute-done | bytes 65568 | tf_op jit(solution)/shard_map/ppermute | solution.py:214
  43.6 0.9 %collective-permute-start.19 = (bf16[64,512]{1,0:T(8,128)(2,1)S(1)}, bf16[64,512]{1,0:T(8,128)(2,1)S(1)}, u32[]{:S(2)}, u32[]{:S(2)}) collective-permute-start(bf16[64,512]{1,0:T(8,128)(2,1)S(1)} %add_convert_fusion), channel_id=1, source_target_pairs={{0,4},{2,6},{4,0},{6,2},{8,12},{10,14},{12,8},{14,10},{1,5},{3,7},... | collective-permute-start | bytes 196616 | tf_op jit(solution)/shard_map/ppermute | solution.py:214
  44.5 0.6 %collective-permute-done.15 = bf16[64,512]{1,0:T(8,128)(2,1)S(1)} collective-permute-done((bf16[64,512]{1,0:T(8,128)(2,1)S(1)}, bf16[64,512]{1,0:T(8,128)(2,1)S(1)}, u32[]{:S(2)}, u32[]{:S(2)}) %collective-permute-start.15) | collective-permute-done | bytes 65568 | tf_op jit(solution)/shard_map/ppermute | solution.py:214
  45.1 0.8 %collective-permute-start.16 = (bf16[64,512]{1,0:T(8,128)(2,1)S(1)}, bf16[64,512]{1,0:T(8,128)(2,1)S(1)}, u32[]{:S(2)}, u32[]{:S(2)}) collective-permute-start(bf16[64,512]{1,0:T(8,128)(2,1)S(1)} %add_convert_fusion.1), channel_id=1, source_target_pairs={{0,2},{2,0},{4,6},{6,4},{8,10},{10,8},{12,14},{14,12},{1,3},{3,1},... | collective-permute-start | bytes 196616 | tf_op jit(solution)/shard_map/ppermute | solution.py:214
  46.0 2.0 %collective-permute-done.19 = bf16[64,512]{1,0:T(8,128)(2,1)S(1)} collective-permute-done((bf16[64,512]{1,0:T(8,128)(2,1)S(1)}, bf16[64,512]{1,0:T(8,128)(2,1)S(1)}, u32[]{:S(2)}, u32[]{:S(2)}) %collective-permute-start.19) | collective-permute-done | bytes 65568 | tf_op jit(solution)/shard_map/ppermute | solution.py:214
  48.0 1.1 %collective-permute-start.20 = (bf16[128,512]{1,0:T(8,128)(2,1)S(1)}, bf16[128,512]{1,0:T(8,128)(2,1)S(1)}, u32[]{:S(2)}, u32[]{:S(2)}) collective-permute-start(bf16[128,512]{1,0:T(8,128)(2,1)S(1)} %pad_maximum_fusion.3), channel_id=1, source_target_pairs={{0,2},{2,0},{4,6},{6,4},{8,10},{10,8},{12,14},{14,12},{1,3},{3,1},... | collective-permute-start | bytes 393224 | tf_op jit(solution)/shard_map/ppermute | solution.py:214
  49.1 1.0 %collective-permute-done.16 = bf16[64,512]{1,0:T(8,128)(2,1)S(1)} collective-permute-done((bf16[64,512]{1,0:T(8,128)(2,1)S(1)}, bf16[64,512]{1,0:T(8,128)(2,1)S(1)}, u32[]{:S(2)}, u32[]{:S(2)}) %collective-permute-start.16) | collective-permute-done | bytes 65568 | tf_op jit(solution)/shard_map/ppermute | solution.py:214
  50.1 0.7 %collective-permute-start.17 = (bf16[128,512]{1,0:T(8,128)(2,1)S(1)}, bf16[128,512]{1,0:T(8,128)(2,1)S(1)}, u32[]{:S(2)}, u32[]{:S(2)}) collective-permute-start(bf16[128,512]{1,0:T(8,128)(2,1)S(1)} %pad_maximum_fusion.2), channel_id=1, source_target_pairs={{0,4},{2,6},{4,0},{6,2},{8,12},{10,14},{12,8},{14,10},{1,5},{3,7},... | collective-permute-start | bytes 393224 | tf_op jit(solution)/shard_map/ppermute | solution.py:214
  50.8 0.0 collective-permute-done.14
  50.8 0.0 collective-permute-done.12
  50.9 0.0 copy-start.3
  50.9 0.0 copy-start.4
  50.9 0.1 broadcast_in_dim.2
  51.1 1.9 %collective-permute-done.20 = bf16[128,512]{1,0:T(8,128)(2,1)S(1)} collective-permute-done((bf16[128,512]{1,0:T(8,128)(2,1)S(1)}, bf16[128,512]{1,0:T(8,128)(2,1)S(1)}, u32[]{:S(2)}, u32[]{:S(2)}) %collective-permute-start.20) | collective-permute-done | bytes 131104 | tf_op jit(solution)/shard_map/ppermute | solution.py:214
  53.0 2.1 %collective-permute-done.17 = bf16[128,512]{1,0:T(8,128)(2,1)S(1)} collective-permute-done((bf16[128,512]{1,0:T(8,128)(2,1)S(1)}, bf16[128,512]{1,0:T(8,128)(2,1)S(1)}, u32[]{:S(2)}, u32[]{:S(2)}) %collective-permute-start.17) | collective-permute-done | bytes 131104 | tf_op jit(solution)/shard_map/ppermute | solution.py:214
  55.3 0.0 copy-done.3
  55.3 0.0 copy-done.4
  55.3 0.0 copy-start
  55.3 1.1 %convolution_convert_fusion = bf16[128,1024]{1,0:T(8,128)(2,1)} fusion(bf16[512,1024]{1,0:T(8,128)(2,1)S(1)} %maximum_dynamic-update-slice_fusion.3, s32[512]{0:T(512)S(1)} %copy-done.3, s32[128]{0:T(128)S(1)} %copy-done.4), kind=kOutput, calls=%fused_computation | convolution fusion | flops 134742016 | bytes 1313280 | tf_op jit(solution)/shard_map/dot_general | solution.py:320
  56.4 0.0 copy-done
  (35 shorter events, 0.8 us)
Async XLA Ops:
  0.6 13.6 %collective-permute-start.1 = (bf16[1,256,4096]{2,1,0:T(8,128)(2,1)}, bf16[1,256,4096]{2,1,0:T(8,128)(2,1)S(1)}, u32[]{:S(2)}, u32[]{:S(2)}) collective-permute-start(bf16[1,256,4096]{2,1,0:T(8,128)(2,1)} %rows_ref.1), channel_id=1, source_target_pairs={{1,0},{0,1},{3,2},{2,3},{5,4},{4,5},{7,6},{6,7},{9,8},{8,9},{11,10... | collective-permute-start | bytes 6291464 | tf_op jit(solution)/shard_map/ppermute | solution.py:299
  9.9 2.7 %copy-start.1 = (f32[256,512]{1,0:T(8,128)}, f32[256,512]{1,0:T(8,128)S(1)}, u32[]{:S(2)}) copy-start(f32[256,512]{1,0:T(8,128)S(1)} %get-tuple-element.119) | copy-start | bytes 1572868
  10.0 12.6 %collective-permute-start = (bf16[128,512]{1,0:T(8,128)(2,1)S(1)}, bf16[128,512]{1,0:T(8,128)(2,1)S(1)}, u32[]{:S(2)}, u32[]{:S(2)}) collective-permute-start(bf16[128,512]{1,0:T(8,128)(2,1)S(1)} %get-tuple-element.60.refs_0_), channel_id=1, source_target_pairs={{0,4},{2,6},{4,0},{6,2},{8,12},{10,14},{12,8},{14,10},{1,5},{3,7},... | collective-permute-start | bytes 393224 | tf_op jit(solution)/shard_map/ppermute | solution.py:214
  12.7 10.3 %collective-permute-start.3 = (bf16[128,512]{1,0:T(8,128)(2,1)S(1)}, bf16[128,512]{1,0:T(8,128)(2,1)S(1)}, u32[]{:S(2)}, u32[]{:S(2)}) collective-permute-start(bf16[128,512]{1,0:T(8,128)(2,1)S(1)} %get-tuple-element.66.refs_1_), channel_id=1, source_target_pairs={{0,2},{2,0},{4,6},{6,4},{8,10},{10,8},{12,14},{14,12},{1,3},{3,1},... | collective-permute-start | bytes 393224 | tf_op jit(solution)/shard_map/ppermute | solution.py:214
  21.9 1.0 %copy-start.2 = (f32[256,512]{1,0:T(8,128)S(1)}, f32[256,512]{1,0:T(8,128)}, u32[]{:S(2)}) copy-start(f32[256,512]{1,0:T(8,128)} %copy-done.1) | copy-start | bytes 1572868
  22.0 10.2 %collective-permute-start.5 = (bf16[128,512]{1,0:T(8,128)(2,1)S(1)}, bf16[128,512]{1,0:T(8,128)(2,1)S(1)}, u32[]{:S(2)}, u32[]{:S(2)}) collective-permute-start(bf16[128,512]{1,0:T(8,128)(2,1)S(1)} %dynamic-slice_convert_fusion.1), channel_id=1, source_target_pairs={{0,2},{2,0},{4,6},{6,4},{8,10},{10,8},{12,14},{14,12},{1,3},{3,1},... | collective-permute-start | bytes 393224 | tf_op jit(solution)/shard_map/ppermute | solution.py:214
  23.0 5.0 %collective-permute-start.7 = (bf16[64,512]{1,0:T(8,128)(2,1)S(1)}, bf16[64,512]{1,0:T(8,128)(2,1)S(1)}, u32[]{:S(2)}, u32[]{:S(2)}) collective-permute-start(bf16[64,512]{1,0:T(8,128)(2,1)S(1)} %dynamic-slice_convert_fusion.6), channel_id=1, source_target_pairs={{0,4},{2,6},{4,0},{6,2},{8,12},{10,14},{12,8},{14,10},{1,5},{3,7},... | collective-permute-start | bytes 196616 | tf_op jit(solution)/shard_map/ppermute | solution.py:214
  23.8 9.2 %collective-permute-start.6 = (bf16[128,512]{1,0:T(8,128)(2,1)S(1)}, bf16[128,512]{1,0:T(8,128)(2,1)S(1)}, u32[]{:S(2)}, u32[]{:S(2)}) collective-permute-start(bf16[128,512]{1,0:T(8,128)(2,1)S(1)} %dynamic-slice_convert_fusion), channel_id=1, source_target_pairs={{0,4},{2,6},{4,0},{6,2},{8,12},{10,14},{12,8},{14,10},{1,5},{3,7},... | collective-permute-start | bytes 393224 | tf_op jit(solution)/shard_map/ppermute | solution.py:214
  25.2 5.5 %collective-permute-start.2 = (bf16[64,512]{1,0:T(8,128)(2,1)S(1)}, bf16[64,512]{1,0:T(8,128)(2,1)S(1)}, u32[]{:S(2)}, u32[]{:S(2)}) collective-permute-start(bf16[64,512]{1,0:T(8,128)(2,1)S(1)} %dynamic-slice_convert_fusion.7), channel_id=1, source_target_pairs={{0,2},{2,0},{4,6},{6,4},{8,10},{10,8},{12,14},{14,12},{1,3},{3,1},... | collective-permute-start | bytes 196616 | tf_op jit(solution)/shard_map/ppermute | solution.py:214
  28.1 7.2 %collective-permute-start.11 = (bf16[64,512]{1,0:T(8,128)(2,1)S(1)}, bf16[64,512]{1,0:T(8,128)(2,1)S(1)}, u32[]{:S(2)}, u32[]{:S(2)}) collective-permute-start(bf16[64,512]{1,0:T(8,128)(2,1)S(1)} %add_convert_fusion.6), channel_id=1, source_target_pairs={{0,8},{2,10},{4,12},{6,14},{8,0},{10,2},{12,4},{14,6},{1,9},{3,11}... | collective-permute-start | bytes 196616 | tf_op jit(solution)/shard_map/ppermute | solution.py:214
  30.8 5.9 %collective-permute-start.4 = (bf16[64,512]{1,0:T(8,128)(2,1)S(1)}, bf16[64,512]{1,0:T(8,128)(2,1)S(1)}, u32[]{:S(2)}, u32[]{:S(2)}) collective-permute-start(bf16[64,512]{1,0:T(8,128)(2,1)S(1)} %add_convert_fusion.7), channel_id=1, source_target_pairs={{0,8},{2,10},{4,12},{6,14},{8,0},{10,2},{12,4},{14,6},{1,9},{3,11}... | collective-permute-start | bytes 196616 | tf_op jit(solution)/shard_map/ppermute | solution.py:214
  32.2 5.5 %collective-permute-start.9 = (bf16[64,512]{1,0:T(8,128)(2,1)S(1)}, bf16[64,512]{1,0:T(8,128)(2,1)S(1)}, u32[]{:S(2)}, u32[]{:S(2)}) collective-permute-start(bf16[64,512]{1,0:T(8,128)(2,1)S(1)} %dynamic-slice_convert_fusion.4), channel_id=1, source_target_pairs={{0,4},{2,6},{4,0},{6,2},{8,12},{10,14},{12,8},{14,10},{1,5},{3,7},... | collective-permute-start | bytes 196616 | tf_op jit(solution)/shard_map/ppermute | solution.py:214
  33.0 6.3 %collective-permute-start.10 = (bf16[64,512]{1,0:T(8,128)(2,1)S(1)}, bf16[64,512]{1,0:T(8,128)(2,1)S(1)}, u32[]{:S(2)}, u32[]{:S(2)}) collective-permute-start(bf16[64,512]{1,0:T(8,128)(2,1)S(1)} %dynamic-slice_convert_fusion.5), channel_id=1, source_target_pairs={{0,2},{2,0},{4,6},{6,4},{8,10},{10,8},{12,14},{14,12},{1,3},{3,1},... | collective-permute-start | bytes 196616 | tf_op jit(solution)/shard_map/ppermute | solution.py:214
  35.3 5.5 %collective-permute-start.13 = (bf16[64,512]{1,0:T(8,128)(2,1)S(1)}, bf16[64,512]{1,0:T(8,128)(2,1)S(1)}, u32[]{:S(2)}, u32[]{:S(2)}) collective-permute-start(bf16[64,512]{1,0:T(8,128)(2,1)S(1)} %add_convert_fusion.4), channel_id=1, source_target_pairs={{0,4},{2,6},{4,0},{6,2},{8,12},{10,14},{12,8},{14,10},{1,5},{3,7},... | collective-permute-start | bytes 196616 | tf_op jit(solution)/shard_map/ppermute | solution.py:214
  36.7 5.3 %collective-permute-start.8 = (bf16[64,512]{1,0:T(8,128)(2,1)S(1)}, bf16[64,512]{1,0:T(8,128)(2,1)S(1)}, u32[]{:S(2)}, u32[]{:S(2)}) collective-permute-start(bf16[64,512]{1,0:T(8,128)(2,1)S(1)} %add_convert_fusion.5), channel_id=1, source_target_pairs={{0,2},{2,0},{4,6},{6,4},{8,10},{10,8},{12,14},{14,12},{1,3},{3,1},... | collective-permute-start | bytes 196616 | tf_op jit(solution)/shard_map/ppermute | solution.py:214
  37.8 5.8 %collective-permute-start.18 = (bf16[64,512]{1,0:T(8,128)(2,1)S(1)}, bf16[64,512]{1,0:T(8,128)(2,1)S(1)}, u32[]{:S(2)}, u32[]{:S(2)}) collective-permute-start(bf16[64,512]{1,0:T(8,128)(2,1)S(1)} %add_convert_fusion.2), channel_id=1, source_target_pairs={{0,8},{2,10},{4,12},{6,14},{8,0},{10,2},{12,4},{14,6},{1,9},{3,11}... | collective-permute-start | bytes 196616 | tf_op jit(solution)/shard_map/ppermute | solution.py:214
  39.4 5.8 %collective-permute-start.15 = (bf16[64,512]{1,0:T(8,128)(2,1)S(1)}, bf16[64,512]{1,0:T(8,128)(2,1)S(1)}, u32[]{:S(2)}, u32[]{:S(2)}) collective-permute-start(bf16[64,512]{1,0:T(8,128)(2,1)S(1)} %add_convert_fusion.3), channel_id=1, source_target_pairs={{0,8},{2,10},{4,12},{6,14},{8,0},{10,2},{12,4},{14,6},{1,9},{3,11}... | collective-permute-start | bytes 196616 | tf_op jit(solution)/shard_map/ppermute | solution.py:214
  40.9 9.9 %collective-permute-start.14 = (bf16[128,512]{1,0:T(8,128)(2,1)S(1)}, bf16[128,512]{1,0:T(8,128)(2,1)S(1)}, u32[]{:S(2)}, u32[]{:S(2)}) collective-permute-start(bf16[128,512]{1,0:T(8,128)(2,1)S(1)} %pad_maximum_fusion.1), channel_id=1, source_target_pairs={{0,2},{2,0},{4,6},{6,4},{8,10},{10,8},{12,14},{14,12},{1,3},{3,1},... | collective-permute-start | bytes 393224 | tf_op jit(solution)/shard_map/ppermute | solution.py:214
  42.1 8.8 %collective-permute-start.12 = (bf16[128,512]{1,0:T(8,128)(2,1)S(1)}, bf16[128,512]{1,0:T(8,128)(2,1)S(1)}, u32[]{:S(2)}, u32[]{:S(2)}) collective-permute-start(bf16[128,512]{1,0:T(8,128)(2,1)S(1)} %pad_maximum_fusion), channel_id=1, source_target_pairs={{0,4},{2,6},{4,0},{6,2},{8,12},{10,14},{12,8},{14,10},{1,5},{3,7},... | collective-permute-start | bytes 393224 | tf_op jit(solution)/shard_map/ppermute | solution.py:214
  43.6 4.3 %collective-permute-start.19 = (bf16[64,512]{1,0:T(8,128)(2,1)S(1)}, bf16[64,512]{1,0:T(8,128)(2,1)S(1)}, u32[]{:S(2)}, u32[]{:S(2)}) collective-permute-start(bf16[64,512]{1,0:T(8,128)(2,1)S(1)} %add_convert_fusion), channel_id=1, source_target_pairs={{0,4},{2,6},{4,0},{6,2},{8,12},{10,14},{12,8},{14,10},{1,5},{3,7},... | collective-permute-start | bytes 196616 | tf_op jit(solution)/shard_map/ppermute | solution.py:214
  45.1 5.0 %collective-permute-start.16 = (bf16[64,512]{1,0:T(8,128)(2,1)S(1)}, bf16[64,512]{1,0:T(8,128)(2,1)S(1)}, u32[]{:S(2)}, u32[]{:S(2)}) collective-permute-start(bf16[64,512]{1,0:T(8,128)(2,1)S(1)} %add_convert_fusion.1), channel_id=1, source_target_pairs={{0,2},{2,0},{4,6},{6,4},{8,10},{10,8},{12,14},{14,12},{1,3},{3,1},... | collective-permute-start | bytes 196616 | tf_op jit(solution)/shard_map/ppermute | solution.py:214
  48.0 5.0 %collective-permute-start.20 = (bf16[128,512]{1,0:T(8,128)(2,1)S(1)}, bf16[128,512]{1,0:T(8,128)(2,1)S(1)}, u32[]{:S(2)}, u32[]{:S(2)}) collective-permute-start(bf16[128,512]{1,0:T(8,128)(2,1)S(1)} %pad_maximum_fusion.3), channel_id=1, source_target_pairs={{0,2},{2,0},{4,6},{6,4},{8,10},{10,8},{12,14},{14,12},{1,3},{3,1},... | collective-permute-start | bytes 393224 | tf_op jit(solution)/shard_map/ppermute | solution.py:214
  50.1 5.0 %collective-permute-start.17 = (bf16[128,512]{1,0:T(8,128)(2,1)S(1)}, bf16[128,512]{1,0:T(8,128)(2,1)S(1)}, u32[]{:S(2)}, u32[]{:S(2)}) collective-permute-start(bf16[128,512]{1,0:T(8,128)(2,1)S(1)} %pad_maximum_fusion.2), channel_id=1, source_target_pairs={{0,4},{2,6},{4,0},{6,2},{8,12},{10,14},{12,8},{14,10},{1,5},{3,7},... | collective-permute-start | bytes 393224 | tf_op jit(solution)/shard_map/ppermute | solution.py:214
  50.9 4.4 %copy-start.3 = (s32[512]{0:T(512)S(1)}, s32[512]{0:T(512)}, u32[]{:S(2)}) copy-start(s32[512]{0:T(512)} %param.10) | copy-start | bytes 6148
  50.9 4.4 %copy-start.4 = (s32[128]{0:T(128)S(1)}, s32[128]{0:T(128)}, u32[]{:S(2)}) copy-start(s32[128]{0:T(128)} %param.11) | copy-start | bytes 1540
  55.3 1.1 %copy-start = (bf16[512,1024]{1,0:T(8,128)(2,1)}, bf16[512,1024]{1,0:T(8,128)(2,1)S(1)}, u32[]{:S(2)}) copy-start(bf16[512,1024]{1,0:T(8,128)(2,1)S(1)} %maximum_dynamic-update-slice_fusion.3) | copy-start | bytes 3145732

commit v16 on v15

--- a/solution.py
+++ b/solution.py
@@ -16,8 +16,8 @@
 DEPTH_BLOCK = 512
 COLUMNS = 512
 CUTS = 2
-ROW_COPIES = 2
-STORE_COPIES = 4
+PIECES = 4
+STORE_COPIES = 8
 VMEM_LIMIT = 32 * 1024 * 1024
 NT = (((1,), (1,)), ((), ()))
 
@@ -45,19 +45,24 @@
     return jnp.concatenate([tiles[:, :, :KOUT], tiles[:, :, KOUT:]], 1)
 
 
-def precondition(rows_ref, both, mixer, half_ref, pre_ref):
-    count = rows_ref.shape[0]
-    together = 4
-    for start in range(0, KIN // 2, together):
+def precondition(rows_ref, both, mixer, half_ref, pre_ref, before):
+    rows = rows_ref.shape[0] // PIECES
+
+    def piece(step, carry):
+        before(step)
+        at = pl.ds(pl.multiple_of(step * rows, rows), rows)
         block = jnp.concatenate(
-            [rows_ref[:, p * PAIR : (p + 1) * PAIR] for p in range(start, start + together)], 0
+            [rows_ref[at, p * PAIR : (p + 1) * PAIR] for p in range(KIN // 2)], 0
         )
         half = jnp.dot(block, both, preferred_element_type=jnp.float32)
-        for k in range(together):
-            at = 2 * ROWS * (start + k)
-            half_ref[:, at : at + 2 * ROWS, :] = side_by_side_to_stacked(
-                half[k * count : (k + 1) * count]
+        groups = pl.ds(step * (rows // ROWS), rows // ROWS)
+        for p in range(KIN // 2):
+            half_ref[groups, 2 * ROWS * p : 2 * ROWS * (p + 1), :] = side_by_side_to_stacked(
+                half[p * rows : (p + 1) * rows]
             ).astype(jnp.bfloat16)
+        return carry
+
+    lax.fori_loop(0, PIECES, piece, 0)
 
     def groups(index, carry):
         stacked = jnp.concatenate([half_ref[2 * index], half_ref[2 * index + 1]], 1)
@@ -69,54 +74,47 @@
             pre_ref[at, i * KOUT : (i + 1) * KOUT] = mixed[i]
         return carry
 
-    lax.fori_loop(0, count // (2 * ROWS), groups, 0, unroll=4)
-
-
-def dot(pre_ref, store_ref, first, total_ref, out_ref):
+    lax.fori_loop(0, rows_ref.shape[0] // (2 * ROWS), groups, 0, unroll=4)
+
+
+def copy_of(source_ref, target_ref, sems, step):
+    rows = target_ref.shape[0] // sems.shape[0]
+    at = pl.ds(pl.multiple_of(step * rows, rows), rows)
+    return pltpu.make_async_copy(source_ref.at[at], target_ref.at[at], sems.at[step])
+
+
+def start_store(store_ref, store_vmem, sems, step):
+    share = sems.shape[0] // PIECES
+    for k in range(share):
+        copy_of(store_ref.at[0], store_vmem, sems, step * share + k).start()
+
+
+def dots(pre_ref, store_ref, store_vmem, sems, total_ref, out_ref):
+    columns = total_ref.shape[0]
     depth = pre_ref.shape[1]
-    columns = total_ref.shape[0]
-    for at in range(0, depth, DEPTH_BLOCK):
-        block = slice(at, at + DEPTH_BLOCK)
-        term = lax.dot_general(
-            store_ref[first : first + columns, block],
-            pre_ref[:, block],
-            NT,
-            preferred_element_type=jnp.float32,
-        )
-        if at == 0:
-            total_ref[...] = term
-        elif at + DEPTH_BLOCK < depth:
-            total_ref[...] += term
-        else:
-            out_ref[:, first : first + columns] = (total_ref[...] + term).T
-
-
-def copies_of(source_ref, target_ref, sems):
-    rows = target_ref.shape[0] // sems.shape[0]
-    return [
-        pltpu.make_async_copy(
-            source_ref.at[pl.ds(k * rows, rows)], target_ref.at[pl.ds(k * rows, rows)], sems.at[k]
-        )
-        for k in range(sems.shape[0])
-    ]
-
-
-def start(copies):
-    for copy in copies:
-        copy.start()
-
-
-def wait(copies):
-    for copy in copies:
-        copy.wait()
-
-
-def dots(pre_ref, store_vmem, copies, total_ref, out_ref):
-    columns = total_ref.shape[0]
-    share = len(copies) * columns // store_vmem.shape[0]
-    for k, first in enumerate(range(0, store_vmem.shape[0], columns)):
-        wait(copies[k * share : (k + 1) * share])
-        dot(pre_ref, store_vmem, first, total_ref, out_ref)
+    blocks = store_vmem.shape[0] // columns
+    share = sems.shape[0] // blocks
+
+    def block(step, carry):
+        for k in range(share):
+            copy_of(store_ref.at[0], store_vmem, sems, step * share + k).wait()
+        rows = pl.ds(pl.multiple_of(step * columns, columns), columns)
+        for at in range(0, depth, DEPTH_BLOCK):
+            term = lax.dot_general(
+                store_vmem[rows, at : at + DEPTH_BLOCK],
+                pre_ref[:, at : at + DEPTH_BLOCK],
+                NT,
+                preferred_element_type=jnp.float32,
+            )
+            if at == 0:
+                total_ref[...] = term
+            elif at + DEPTH_BLOCK < depth:
+                total_ref[...] += term
+            else:
+                out_ref[:, rows] = (total_ref[...] + term).T
+        return carry
+
+    lax.fori_loop(0, blocks, block, 0)
 
 
 def first_kernel(
@@ -124,28 +122,35 @@
     left_vmem, right_vmem, rows_vmem, store_vmem, half_ref, total_ref,
     left_sems, right_sems, rows_sems, store_sems,
 ):
-    heads = copies_of(right_ref.at[0], right_vmem, right_sems)
-    heads += copies_of(left_ref.at[0], left_vmem, left_sems)
-    rows = copies_of(rows_ref.at[0], rows_vmem, rows_sems)
-    copies = copies_of(store_ref.at[0], store_vmem, store_sems)
-    start(heads + rows)
-    wait(heads)
+    right = copy_of(right_ref.at[0], right_vmem, right_sems, 0)
+    left = copy_of(left_ref.at[0], left_vmem, left_sems, 0)
+    right.start()
+    left.start()
+    for step in range(PIECES):
+        copy_of(rows_ref.at[0], rows_vmem, rows_sems, step).start()
+    right.wait()
     both_ref[...] = right_matrix(right_vmem[...])
+    left.wait()
     mixer_ref[...] = left_matrix(left_vmem[...])
-    wait(rows)
-    start(copies)
-    precondition(rows_vmem, both_ref[...], mixer_ref[...], half_ref, rows_vmem)
-    dots(rows_vmem, store_vmem, copies, total_ref, out_ref)
+
+    def before(step):
+        copy_of(rows_ref.at[0], rows_vmem, rows_sems, step).wait()
+        start_store(store_ref, store_vmem, store_sems, step)
+
+    precondition(rows_vmem, both_ref[...], mixer_ref[...], half_ref, rows_vmem, before)
+    dots(rows_vmem, store_ref, store_vmem, store_sems, total_ref, out_ref)
 
 
 def later_kernel(
     sent, rows_ref, both_ref, mixer_ref, store_ref, *refs,
 ):
     out_ref, pre_ref, store_vmem, half_ref, total_ref, store_sems = refs[sent:]
-    copies = copies_of(store_ref.at[0], store_vmem, store_sems)
-    start(copies)
-    precondition(rows_ref.at[0], both_ref[...], mixer_ref[...], half_ref, pre_ref)
-    dots(pre_ref, store_vmem, copies, total_ref, out_ref)
+
+    def before(step):
+        start_store(store_ref, store_vmem, store_sems, step)
+
+    precondition(rows_ref.at[0], both_ref[...], mixer_ref[...], half_ref, pre_ref, before)
+    dots(pre_ref, store_ref, store_vmem, store_sems, total_ref, out_ref)
 
 
 VMEM = pl.BlockSpec(memory_space=pltpu.VMEM)
@@ -188,7 +193,7 @@
 
 def first_scores(queries, left_inv, right_inv, store):
     small = [pltpu.VMEM((KIN, KIN), jnp.bfloat16), pltpu.VMEM((KOUT, KOUT), jnp.bfloat16)]
-    sems = [pltpu.SemaphoreType.DMA((n,)) for n in (1, 1, ROW_COPIES, STORE_COPIES)]
+    sems = [pltpu.SemaphoreType.DMA((n,)) for n in (1, 1, PIECES, STORE_COPIES)]
     outs = (
         jax.ShapeDtypeStruct((PAIR, PAIR), jnp.bfloat16),
         jax.ShapeDtypeStruct((WIDE, WIDE), jnp.bfloat16),

time: 56.6 us -> 52.4 us (0.926)
  Pallas kernels: 16.4 us -> 12.2 us
    pallas_call x2, Pallas kernels: 16.4 us -> 12.2 us  [call(): pl.pallas_call(kernel, out_shape=(jax.ShapeDtypeStruct((count, examples),...]
  transfers between devices with their start and end apart: 21 -> 21, of which waited for: 9 -> 9; matrix products, arithmetic and copies ran while one was open for 2% -> 2% of each run, Pallas kernels for 29% -> 23%
where the time goes in v16:
time: 52.4 us; the launch traced here: 52.2 us
  starting transfers between devices  24.6 us (47%)
  Pallas kernels  12.2 us (23%)
  waiting for transfers between devices  12 us (23%)
  matrix products  1.07 us (2%)
  between operations  0.96 us (2%)
  local copies, waits for them, and re-layouts  0.79 us (2%)
  other arithmetic  0.66 us (1%)
    ppermute x20, starting transfers between devices, swap(): return lax.ppermute(block, 'layer', route)  24 us
    pallas_call x2, Pallas kernels, call(): pl.pallas_call(kernel, out_shape=(jax.ShapeDtypeStruct((count, examples),...  12.2 us
    ppermute x20, waiting for transfers between devices, swap(): return lax.ppermute(block, 'layer', route)  12 us
    dot_general x1, matrix products, shards(): advantage = jnp.dot(weights, scores, preferred_element_type=jnp.float32)  1.07 us
  transfers between devices with their start and end apart: 21, of which 9 were waited for; matrix products, arithmetic and copies ran while one was open for 2% of the time, Pallas kernels for 23%

profile of v16, /device:TPU:0, one launch (start us, length us, event | category | flops | bytes accessed | tf_op | source)
XLA Modules:
  0.0 52.2 jit_solution(11834291993593862973)
XLA Ops:
  0.6 0.5 collective-permute-start.1
  1.1 6.9 %shard_map.77 = (f32[256,1024]{1,0:T(8,128)S(1)}, bf16[256,256]{1,0:T(8,128)(2,1)S(1)}, bf16[256,256]{1,0:T(8,128)(2,1)S(1)}) custom-call(bf16[1,256,4096]{2,1,0:T(8,128)(2,1)} %rows_ref.1, bf16[1,32,32]{2,1,0:T(8,128)(2,1)} %left_ref.1, bf16[1,128,128]{2,1,0:T(8,128)(2,1)} %right_ref.1, bf16[1,1024,4096]{2,1,0:T(8,128)(2,1)} %store_ref.3), custom_call_target="tpu_custom_call" | custom-call | flops 4294967296 | bytes 10485760 | tf_op jit(solution)/shard_map/pallas_call | solution.py:168
  8.1 0.1 fusion.7
  8.1 0.0 copy-start.1
  8.2 2.7 %collective-permute-start = (bf16[128,512]{1,0:T(8,128)(2,1)S(1)}, bf16[128,512]{1,0:T(8,128)(2,1)S(1)}, u32[]{:S(2)}, u32[]{:S(2)}) collective-permute-start(bf16[128,512]{1,0:T(8,128)(2,1)S(1)} %get-tuple-element.60.refs_0_), channel_id=1, source_target_pairs={{0,4},{2,6},{4,0},{6,2},{8,12},{10,14},{12,8},{14,10},{1,5},{3,7},... | collective-permute-start | bytes 393224 | tf_op jit(solution)/shard_map/ppermute | solution.py:219
  10.9 0.0 copy-done.1
  10.9 1.5 %collective-permute-start.3 = (bf16[128,512]{1,0:T(8,128)(2,1)S(1)}, bf16[128,512]{1,0:T(8,128)(2,1)S(1)}, u32[]{:S(2)}, u32[]{:S(2)}) collective-permute-start(bf16[128,512]{1,0:T(8,128)(2,1)S(1)} %get-tuple-element.66.refs_1_), channel_id=1, source_target_pairs={{0,2},{2,0},{4,6},{6,4},{8,10},{10,8},{12,14},{14,12},{1,3},{3,1},... | collective-permute-start | bytes 393224 | tf_op jit(solution)/shard_map/ppermute | solution.py:219
  12.4 0.0 collective-permute-done.1.rows_ref
  12.4 5.3 %shard_map.78 = f32[256,1024]{1,0:T(8,128)S(1)} custom-call(bf16[1,256,4096]{2,1,0:T(8,128)(2,1)S(1)} %collective-permute-done.1.rows_ref, bf16[256,256]{1,0:T(8,128)(2,1)S(1)} %get-tuple-element.64.both_ref, bf16[256,256]{1,0:T(8,128)(2,1)S(1)} %get-tuple-element.65.mixer_ref, bf16[1,1024,4096]{2,1,0:T(8,128)(2,1)} %store_ref.3, ...), custom_call_target="tpu_custom_call" | custom-call | flops 4294967296 | bytes 10485760 | tf_op jit(solution)/shard_map/pallas_call | solution.py:168
  17.7 0.0 copy-start.2
  17.7 0.1 fusion.6
  17.8 0.6 %collective-permute-start.5 = (bf16[128,512]{1,0:T(8,128)(2,1)S(1)}, bf16[128,512]{1,0:T(8,128)(2,1)S(1)}, u32[]{:S(2)}, u32[]{:S(2)}) collective-permute-start(bf16[128,512]{1,0:T(8,128)(2,1)S(1)} %dynamic-slice_convert_fusion.1), channel_id=1, source_target_pairs={{0,2},{2,0},{4,6},{6,4},{8,10},{10,8},{12,14},{14,12},{1,3},{3,1},... | collective-permute-start | bytes 393224 | tf_op jit(solution)/shard_map/ppermute | solution.py:219
  18.4 0.0 collective-permute-done
  18.4 0.3 copy-done.2
  18.8 0.0 collective-permute-done.3
  18.9 0.7 %collective-permute-start.7 = (bf16[64,512]{1,0:T(8,128)(2,1)S(1)}, bf16[64,512]{1,0:T(8,128)(2,1)S(1)}, u32[]{:S(2)}, u32[]{:S(2)}) collective-permute-start(bf16[64,512]{1,0:T(8,128)(2,1)S(1)} %dynamic-slice_convert_fusion.6), channel_id=1, source_target_pairs={{0,4},{2,6},{4,0},{6,2},{8,12},{10,14},{12,8},{14,10},{1,5},{3,7},... | collective-permute-start | bytes 196616 | tf_op jit(solution)/shard_map/ppermute | solution.py:219
  19.6 1.4 %collective-permute-start.6 = (bf16[128,512]{1,0:T(8,128)(2,1)S(1)}, bf16[128,512]{1,0:T(8,128)(2,1)S(1)}, u32[]{:S(2)}, u32[]{:S(2)}) collective-permute-start(bf16[128,512]{1,0:T(8,128)(2,1)S(1)} %dynamic-slice_convert_fusion), channel_id=1, source_target_pairs={{0,4},{2,6},{4,0},{6,2},{8,12},{10,14},{12,8},{14,10},{1,5},{3,7},... | collective-permute-start | bytes 393224 | tf_op jit(solution)/shard_map/ppermute | solution.py:219
  21.1 1.2 %collective-permute-start.2 = (bf16[64,512]{1,0:T(8,128)(2,1)S(1)}, bf16[64,512]{1,0:T(8,128)(2,1)S(1)}, u32[]{:S(2)}, u32[]{:S(2)}) collective-permute-start(bf16[64,512]{1,0:T(8,128)(2,1)S(1)} %dynamic-slice_convert_fusion.7), channel_id=1, source_target_pairs={{0,2},{2,0},{4,6},{6,4},{8,10},{10,8},{12,14},{14,12},{1,3},{3,1},... | collective-permute-start | bytes 196616 | tf_op jit(solution)/shard_map/ppermute | solution.py:219
  22.3 1.7 %collective-permute-done.7 = bf16[64,512]{1,0:T(8,128)(2,1)S(1)} collective-permute-done((bf16[64,512]{1,0:T(8,128)(2,1)S(1)}, bf16[64,512]{1,0:T(8,128)(2,1)S(1)}, u32[]{:S(2)}, u32[]{:S(2)}) %collective-permute-start.7) | collective-permute-done | bytes 65568 | tf_op jit(solution)/shard_map/ppermute | solution.py:219
  23.9 2.6 %collective-permute-start.11 = (bf16[64,512]{1,0:T(8,128)(2,1)S(1)}, bf16[64,512]{1,0:T(8,128)(2,1)S(1)}, u32[]{:S(2)}, u32[]{:S(2)}) collective-permute-start(bf16[64,512]{1,0:T(8,128)(2,1)S(1)} %add_convert_fusion.6), channel_id=1, source_target_pairs={{0,8},{2,10},{4,12},{6,14},{8,0},{10,2},{12,4},{14,6},{1,9},{3,11}... | collective-permute-start | bytes 196616 | tf_op jit(solution)/shard_map/ppermute | solution.py:219
  26.6 0.0 collective-permute-done.2
  26.6 1.4 %collective-permute-start.4 = (bf16[64,512]{1,0:T(8,128)(2,1)S(1)}, bf16[64,512]{1,0:T(8,128)(2,1)S(1)}, u32[]{:S(2)}, u32[]{:S(2)}) collective-permute-start(bf16[64,512]{1,0:T(8,128)(2,1)S(1)} %add_convert_fusion.7), channel_id=1, source_target_pairs={{0,8},{2,10},{4,12},{6,14},{8,0},{10,2},{12,4},{14,6},{1,9},{3,11}... | collective-permute-start | bytes 196616 | tf_op jit(solution)/shard_map/ppermute | solution.py:219
  28.0 0.0 collective-permute-done.5
  28.1 0.7 %collective-permute-start.9 = (bf16[64,512]{1,0:T(8,128)(2,1)S(1)}, bf16[64,512]{1,0:T(8,128)(2,1)S(1)}, u32[]{:S(2)}, u32[]{:S(2)}) collective-permute-start(bf16[64,512]{1,0:T(8,128)(2,1)S(1)} %dynamic-slice_convert_fusion.4), channel_id=1, source_target_pairs={{0,4},{2,6},{4,0},{6,2},{8,12},{10,14},{12,8},{14,10},{1,5},{3,7},... | collective-permute-start | bytes 196616 | tf_op jit(solution)/shard_map/ppermute | solution.py:219
  28.8 0.0 collective-permute-done.6
  28.9 1.3 %collective-permute-start.10 = (bf16[64,512]{1,0:T(8,128)(2,1)S(1)}, bf16[64,512]{1,0:T(8,128)(2,1)S(1)}, u32[]{:S(2)}, u32[]{:S(2)}) collective-permute-start(bf16[64,512]{1,0:T(8,128)(2,1)S(1)} %dynamic-slice_convert_fusion.5), channel_id=1, source_target_pairs={{0,2},{2,0},{4,6},{6,4},{8,10},{10,8},{12,14},{14,12},{1,3},{3,1},... | collective-permute-start | bytes 196616 | tf_op jit(solution)/shard_map/ppermute | solution.py:219
  30.1 1.0 %collective-permute-done.11 = bf16[64,512]{1,0:T(8,128)(2,1)S(1)} collective-permute-done((bf16[64,512]{1,0:T(8,128)(2,1)S(1)}, bf16[64,512]{1,0:T(8,128)(2,1)S(1)}, u32[]{:S(2)}, u32[]{:S(2)}) %collective-permute-start.11) | collective-permute-done | bytes 65568 | tf_op jit(solution)/shard_map/ppermute | solution.py:219
  31.1 0.5 collective-permute-start.13
  31.6 1.0 %collective-permute-done.4 = bf16[64,512]{1,0:T(8,128)(2,1)S(1)} collective-permute-done((bf16[64,512]{1,0:T(8,128)(2,1)S(1)}, bf16[64,512]{1,0:T(8,128)(2,1)S(1)}, u32[]{:S(2)}, u32[]{:S(2)}) %collective-permute-start.4) | collective-permute-done | bytes 65568 | tf_op jit(solution)/shard_map/ppermute | solution.py:219
  32.6 1.0 %collective-permute-start.8 = (bf16[64,512]{1,0:T(8,128)(2,1)S(1)}, bf16[64,512]{1,0:T(8,128)(2,1)S(1)}, u32[]{:S(2)}, u32[]{:S(2)}) collective-permute-start(bf16[64,512]{1,0:T(8,128)(2,1)S(1)} %add_convert_fusion.5), channel_id=1, source_target_pairs={{0,2},{2,0},{4,6},{6,4},{8,10},{10,8},{12,14},{14,12},{1,3},{3,1},... | collective-permute-start | bytes 196616 | tf_op jit(solution)/shard_map/ppermute | solution.py:219
  33.6 0.0 collective-permute-done.9
  33.6 1.6 %collective-permute-start.18 = (bf16[64,512]{1,0:T(8,128)(2,1)S(1)}, bf16[64,512]{1,0:T(8,128)(2,1)S(1)}, u32[]{:S(2)}, u32[]{:S(2)}) collective-permute-start(bf16[64,512]{1,0:T(8,128)(2,1)S(1)} %add_convert_fusion.2), channel_id=1, source_target_pairs={{0,8},{2,10},{4,12},{6,14},{8,0},{10,2},{12,4},{14,6},{1,9},{3,11}... | collective-permute-start | bytes 196616 | tf_op jit(solution)/shard_map/ppermute | solution.py:219
  35.2 0.0 collective-permute-done.10
  35.2 1.5 %collective-permute-start.15 = (bf16[64,512]{1,0:T(8,128)(2,1)S(1)}, bf16[64,512]{1,0:T(8,128)(2,1)S(1)}, u32[]{:S(2)}, u32[]{:S(2)}) collective-permute-start(bf16[64,512]{1,0:T(8,128)(2,1)S(1)} %add_convert_fusion.3), channel_id=1, source_target_pairs={{0,8},{2,10},{4,12},{6,14},{8,0},{10,2},{12,4},{14,6},{1,9},{3,11}... | collective-permute-start | bytes 196616 | tf_op jit(solution)/shard_map/ppermute | solution.py:219
  36.7 0.0 collective-permute-done.13
  36.7 1.1 %collective-permute-start.14 = (bf16[128,512]{1,0:T(8,128)(2,1)S(1)}, bf16[128,512]{1,0:T(8,128)(2,1)S(1)}, u32[]{:S(2)}, u32[]{:S(2)}) collective-permute-start(bf16[128,512]{1,0:T(8,128)(2,1)S(1)} %pad_maximum_fusion.1), channel_id=1, source_target_pairs={{0,2},{2,0},{4,6},{6,4},{8,10},{10,8},{12,14},{14,12},{1,3},{3,1},... | collective-permute-start | bytes 393224 | tf_op jit(solution)/shard_map/ppermute | solution.py:219
  37.9 0.0 collective-permute-done.8
  37.9 0.8 %collective-permute-start.12 = (bf16[128,512]{1,0:T(8,128)(2,1)S(1)}, bf16[128,512]{1,0:T(8,128)(2,1)S(1)}, u32[]{:S(2)}, u32[]{:S(2)}) collective-permute-start(bf16[128,512]{1,0:T(8,128)(2,1)S(1)} %pad_maximum_fusion), channel_id=1, source_target_pairs={{0,4},{2,6},{4,0},{6,2},{8,12},{10,14},{12,8},{14,10},{1,5},{3,7},... | collective-permute-start | bytes 393224 | tf_op jit(solution)/shard_map/ppermute | solution.py:219
  38.7 0.7 %collective-permute-done.18 = bf16[64,512]{1,0:T(8,128)(2,1)S(1)} collective-permute-done((bf16[64,512]{1,0:T(8,128)(2,1)S(1)}, bf16[64,512]{1,0:T(8,128)(2,1)S(1)}, u32[]{:S(2)}, u32[]{:S(2)}) %collective-permute-start.18) | collective-permute-done | bytes 65568 | tf_op jit(solution)/shard_map/ppermute | solution.py:219
  39.4 0.9 %collective-permute-start.19 = (bf16[64,512]{1,0:T(8,128)(2,1)S(1)}, bf16[64,512]{1,0:T(8,128)(2,1)S(1)}, u32[]{:S(2)}, u32[]{:S(2)}) collective-permute-start(bf16[64,512]{1,0:T(8,128)(2,1)S(1)} %add_convert_fusion), channel_id=1, source_target_pairs={{0,4},{2,6},{4,0},{6,2},{8,12},{10,14},{12,8},{14,10},{1,5},{3,7},... | collective-permute-start | bytes 196616 | tf_op jit(solution)/shard_map/ppermute | solution.py:219
  40.3 0.6 %collective-permute-done.15 = bf16[64,512]{1,0:T(8,128)(2,1)S(1)} collective-permute-done((bf16[64,512]{1,0:T(8,128)(2,1)S(1)}, bf16[64,512]{1,0:T(8,128)(2,1)S(1)}, u32[]{:S(2)}, u32[]{:S(2)}) %collective-permute-start.15) | collective-permute-done | bytes 65568 | tf_op jit(solution)/shard_map/ppermute | solution.py:219
  41.0 0.8 %collective-permute-start.16 = (bf16[64,512]{1,0:T(8,128)(2,1)S(1)}, bf16[64,512]{1,0:T(8,128)(2,1)S(1)}, u32[]{:S(2)}, u32[]{:S(2)}) collective-permute-start(bf16[64,512]{1,0:T(8,128)(2,1)S(1)} %add_convert_fusion.1), channel_id=1, source_target_pairs={{0,2},{2,0},{4,6},{6,4},{8,10},{10,8},{12,14},{14,12},{1,3},{3,1},... | collective-permute-start | bytes 196616 | tf_op jit(solution)/shard_map/ppermute | solution.py:219
  41.8 2.0 %collective-permute-done.19 = bf16[64,512]{1,0:T(8,128)(2,1)S(1)} collective-permute-done((bf16[64,512]{1,0:T(8,128)(2,1)S(1)}, bf16[64,512]{1,0:T(8,128)(2,1)S(1)}, u32[]{:S(2)}, u32[]{:S(2)}) %collective-permute-start.19) | collective-permute-done | bytes 65568 | tf_op jit(solution)/shard_map/ppermute | solution.py:219
  43.8 1.1 %collective-permute-start.20 = (bf16[128,512]{1,0:T(8,128)(2,1)S(1)}, bf16[128,512]{1,0:T(8,128)(2,1)S(1)}, u32[]{:S(2)}, u32[]{:S(2)}) collective-permute-start(bf16[128,512]{1,0:T(8,128)(2,1)S(1)} %pad_maximum_fusion.3), channel_id=1, source_target_pairs={{0,2},{2,0},{4,6},{6,4},{8,10},{10,8},{12,14},{14,12},{1,3},{3,1},... | collective-permute-start | bytes 393224 | tf_op jit(solution)/shard_map/ppermute | solution.py:219
  44.9 1.0 %collective-permute-done.16 = bf16[64,512]{1,0:T(8,128)(2,1)S(1)} collective-permute-done((bf16[64,512]{1,0:T(8,128)(2,1)S(1)}, bf16[64,512]{1,0:T(8,128)(2,1)S(1)}, u32[]{:S(2)}, u32[]{:S(2)}) %collective-permute-start.16) | collective-permute-done | bytes 65568 | tf_op jit(solution)/shard_map/ppermute | solution.py:219
  46.0 0.6 %collective-permute-start.17 = (bf16[128,512]{1,0:T(8,128)(2,1)S(1)}, bf16[128,512]{1,0:T(8,128)(2,1)S(1)}, u32[]{:S(2)}, u32[]{:S(2)}) collective-permute-start(bf16[128,512]{1,0:T(8,128)(2,1)S(1)} %pad_maximum_fusion.2), channel_id=1, source_target_pairs={{0,4},{2,6},{4,0},{6,2},{8,12},{10,14},{12,8},{14,10},{1,5},{3,7},... | collective-permute-start | bytes 393224 | tf_op jit(solution)/shard_map/ppermute | solution.py:219
  46.6 0.0 collective-permute-done.14
  46.6 0.0 collective-permute-done.12
  46.7 0.0 copy-start.3
  46.7 0.0 copy-start.4
  46.7 0.1 broadcast_in_dim.2
  46.9 1.9 %collective-permute-done.20 = bf16[128,512]{1,0:T(8,128)(2,1)S(1)} collective-permute-done((bf16[128,512]{1,0:T(8,128)(2,1)S(1)}, bf16[128,512]{1,0:T(8,128)(2,1)S(1)}, u32[]{:S(2)}, u32[]{:S(2)}) %collective-permute-start.20) | collective-permute-done | bytes 131104 | tf_op jit(solution)/shard_map/ppermute | solution.py:219
  48.9 2.1 %collective-permute-done.17 = bf16[128,512]{1,0:T(8,128)(2,1)S(1)} collective-permute-done((bf16[128,512]{1,0:T(8,128)(2,1)S(1)}, bf16[128,512]{1,0:T(8,128)(2,1)S(1)}, u32[]{:S(2)}, u32[]{:S(2)}) %collective-permute-start.17) | collective-permute-done | bytes 131104 | tf_op jit(solution)/shard_map/ppermute | solution.py:219
  51.1 0.0 copy-done.3
  51.1 0.0 copy-done.4
  51.1 0.0 copy-start
  51.1 1.1 %convolution_convert_fusion = bf16[128,1024]{1,0:T(8,128)(2,1)} fusion(bf16[512,1024]{1,0:T(8,128)(2,1)S(1)} %maximum_dynamic-update-slice_fusion.3, s32[512]{0:T(512)S(1)} %copy-done.3, s32[128]{0:T(128)S(1)} %copy-done.4), kind=kOutput, calls=%fused_computation | convolution fusion | flops 134742016 | bytes 1313280 | tf_op jit(solution)/shard_map/dot_general | solution.py:325
  52.2 0.0 copy-done
  (35 shorter events, 0.8 us)
Async XLA Ops:
  0.6 11.8 %collective-permute-start.1 = (bf16[1,256,4096]{2,1,0:T(8,128)(2,1)}, bf16[1,256,4096]{2,1,0:T(8,128)(2,1)S(1)}, u32[]{:S(2)}, u32[]{:S(2)}) collective-permute-start(bf16[1,256,4096]{2,1,0:T(8,128)(2,1)} %rows_ref.1), channel_id=1, source_target_pairs={{1,0},{0,1},{3,2},{2,3},{5,4},{4,5},{7,6},{6,7},{9,8},{8,9},{11,10... | collective-permute-start | bytes 6291464 | tf_op jit(solution)/shard_map/ppermute | solution.py:304
  8.1 2.8 %copy-start.1 = (f32[256,512]{1,0:T(8,128)}, f32[256,512]{1,0:T(8,128)S(1)}, u32[]{:S(2)}) copy-start(f32[256,512]{1,0:T(8,128)S(1)} %get-tuple-element.119) | copy-start | bytes 1572868
  8.2 10.2 %collective-permute-start = (bf16[128,512]{1,0:T(8,128)(2,1)S(1)}, bf16[128,512]{1,0:T(8,128)(2,1)S(1)}, u32[]{:S(2)}, u32[]{:S(2)}) collective-permute-start(bf16[128,512]{1,0:T(8,128)(2,1)S(1)} %get-tuple-element.60.refs_0_), channel_id=1, source_target_pairs={{0,4},{2,6},{4,0},{6,2},{8,12},{10,14},{12,8},{14,10},{1,5},{3,7},... | collective-permute-start | bytes 393224 | tf_op jit(solution)/shard_map/ppermute | solution.py:219
  10.9 7.9 %collective-permute-start.3 = (bf16[128,512]{1,0:T(8,128)(2,1)S(1)}, bf16[128,512]{1,0:T(8,128)(2,1)S(1)}, u32[]{:S(2)}, u32[]{:S(2)}) collective-permute-start(bf16[128,512]{1,0:T(8,128)(2,1)S(1)} %get-tuple-element.66.refs_1_), channel_id=1, source_target_pairs={{0,2},{2,0},{4,6},{6,4},{8,10},{10,8},{12,14},{14,12},{1,3},{3,1},... | collective-permute-start | bytes 393224 | tf_op jit(solution)/shard_map/ppermute | solution.py:219
  17.7 1.0 %copy-start.2 = (f32[256,512]{1,0:T(8,128)S(1)}, f32[256,512]{1,0:T(8,128)}, u32[]{:S(2)}) copy-start(f32[256,512]{1,0:T(8,128)} %copy-done.1) | copy-start | bytes 1572868
  17.8 10.2 %collective-permute-start.5 = (bf16[128,512]{1,0:T(8,128)(2,1)S(1)}, bf16[128,512]{1,0:T(8,128)(2,1)S(1)}, u32[]{:S(2)}, u32[]{:S(2)}) collective-permute-start(bf16[128,512]{1,0:T(8,128)(2,1)S(1)} %dynamic-slice_convert_fusion.1), channel_id=1, source_target_pairs={{0,2},{2,0},{4,6},{6,4},{8,10},{10,8},{12,14},{14,12},{1,3},{3,1},... | collective-permute-start | bytes 393224 | tf_op jit(solution)/shard_map/ppermute | solution.py:219
  18.9 5.0 %collective-permute-start.7 = (bf16[64,512]{1,0:T(8,128)(2,1)S(1)}, bf16[64,512]{1,0:T(8,128)(2,1)S(1)}, u32[]{:S(2)}, u32[]{:S(2)}) collective-permute-start(bf16[64,512]{1,0:T(8,128)(2,1)S(1)} %dynamic-slice_convert_fusion.6), channel_id=1, source_target_pairs={{0,4},{2,6},{4,0},{6,2},{8,12},{10,14},{12,8},{14,10},{1,5},{3,7},... | collective-permute-start | bytes 196616 | tf_op jit(solution)/shard_map/ppermute | solution.py:219
  19.6 9.2 %collective-permute-start.6 = (bf16[128,512]{1,0:T(8,128)(2,1)S(1)}, bf16[128,512]{1,0:T(8,128)(2,1)S(1)}, u32[]{:S(2)}, u32[]{:S(2)}) collective-permute-start(bf16[128,512]{1,0:T(8,128)(2,1)S(1)} %dynamic-slice_convert_fusion), channel_id=1, source_target_pairs={{0,4},{2,6},{4,0},{6,2},{8,12},{10,14},{12,8},{14,10},{1,5},{3,7},... | collective-permute-start | bytes 393224 | tf_op jit(solution)/shard_map/ppermute | solution.py:219
  21.1 5.5 %collective-permute-start.2 = (bf16[64,512]{1,0:T(8,128)(2,1)S(1)}, bf16[64,512]{1,0:T(8,128)(2,1)S(1)}, u32[]{:S(2)}, u32[]{:S(2)}) collective-permute-start(bf16[64,512]{1,0:T(8,128)(2,1)S(1)} %dynamic-slice_convert_fusion.7), channel_id=1, source_target_pairs={{0,2},{2,0},{4,6},{6,4},{8,10},{10,8},{12,14},{14,12},{1,3},{3,1},... | collective-permute-start | bytes 196616 | tf_op jit(solution)/shard_map/ppermute | solution.py:219
  23.9 7.2 %collective-permute-start.11 = (bf16[64,512]{1,0:T(8,128)(2,1)S(1)}, bf16[64,512]{1,0:T(8,128)(2,1)S(1)}, u32[]{:S(2)}, u32[]{:S(2)}) collective-permute-start(bf16[64,512]{1,0:T(8,128)(2,1)S(1)} %add_convert_fusion.6), channel_id=1, source_target_pairs={{0,8},{2,10},{4,12},{6,14},{8,0},{10,2},{12,4},{14,6},{1,9},{3,11}... | collective-permute-start | bytes 196616 | tf_op jit(solution)/shard_map/ppermute | solution.py:219
  26.6 5.9 %collective-permute-start.4 = (bf16[64,512]{1,0:T(8,128)(2,1)S(1)}, bf16[64,512]{1,0:T(8,128)(2,1)S(1)}, u32[]{:S(2)}, u32[]{:S(2)}) collective-permute-start(bf16[64,512]{1,0:T(8,128)(2,1)S(1)} %add_convert_fusion.7), channel_id=1, source_target_pairs={{0,8},{2,10},{4,12},{6,14},{8,0},{10,2},{12,4},{14,6},{1,9},{3,11}... | collective-permute-start | bytes 196616 | tf_op jit(solution)/shard_map/ppermute | solution.py:219
  28.1 5.5 %collective-permute-start.9 = (bf16[64,512]{1,0:T(8,128)(2,1)S(1)}, bf16[64,512]{1,0:T(8,128)(2,1)S(1)}, u32[]{:S(2)}, u32[]{:S(2)}) collective-permute-start(bf16[64,512]{1,0:T(8,128)(2,1)S(1)} %dynamic-slice_convert_fusion.4), channel_id=1, source_target_pairs={{0,4},{2,6},{4,0},{6,2},{8,12},{10,14},{12,8},{14,10},{1,5},{3,7},... | collective-permute-start | bytes 196616 | tf_op jit(solution)/shard_map/ppermute | solution.py:219
  28.9 6.3 %collective-permute-start.10 = (bf16[64,512]{1,0:T(8,128)(2,1)S(1)}, bf16[64,512]{1,0:T(8,128)(2,1)S(1)}, u32[]{:S(2)}, u32[]{:S(2)}) collective-permute-start(bf16[64,512]{1,0:T(8,128)(2,1)S(1)} %dynamic-slice_convert_fusion.5), channel_id=1, source_target_pairs={{0,2},{2,0},{4,6},{6,4},{8,10},{10,8},{12,14},{14,12},{1,3},{3,1},... | collective-permute-start | bytes 196616 | tf_op jit(solution)/shard_map/ppermute | solution.py:219
  31.1 5.5 %collective-permute-start.13 = (bf16[64,512]{1,0:T(8,128)(2,1)S(1)}, bf16[64,512]{1,0:T(8,128)(2,1)S(1)}, u32[]{:S(2)}, u32[]{:S(2)}) collective-permute-start(bf16[64,512]{1,0:T(8,128)(2,1)S(1)} %add_convert_fusion.4), channel_id=1, source_target_pairs={{0,4},{2,6},{4,0},{6,2},{8,12},{10,14},{12,8},{14,10},{1,5},{3,7},... | collective-permute-start | bytes 196616 | tf_op jit(solution)/shard_map/ppermute | solution.py:219
  32.6 5.3 %collective-permute-start.8 = (bf16[64,512]{1,0:T(8,128)(2,1)S(1)}, bf16[64,512]{1,0:T(8,128)(2,1)S(1)}, u32[]{:S(2)}, u32[]{:S(2)}) collective-permute-start(bf16[64,512]{1,0:T(8,128)(2,1)S(1)} %add_convert_fusion.5), channel_id=1, source_target_pairs={{0,2},{2,0},{4,6},{6,4},{8,10},{10,8},{12,14},{14,12},{1,3},{3,1},... | collective-permute-start | bytes 196616 | tf_op jit(solution)/shard_map/ppermute | solution.py:219
  33.6 5.8 %collective-permute-start.18 = (bf16[64,512]{1,0:T(8,128)(2,1)S(1)}, bf16[64,512]{1,0:T(8,128)(2,1)S(1)}, u32[]{:S(2)}, u32[]{:S(2)}) collective-permute-start(bf16[64,512]{1,0:T(8,128)(2,1)S(1)} %add_convert_fusion.2), channel_id=1, source_target_pairs={{0,8},{2,10},{4,12},{6,14},{8,0},{10,2},{12,4},{14,6},{1,9},{3,11}... | collective-permute-start | bytes 196616 | tf_op jit(solution)/shard_map/ppermute | solution.py:219
  35.2 5.8 %collective-permute-start.15 = (bf16[64,512]{1,0:T(8,128)(2,1)S(1)}, bf16[64,512]{1,0:T(8,128)(2,1)S(1)}, u32[]{:S(2)}, u32[]{:S(2)}) collective-permute-start(bf16[64,512]{1,0:T(8,128)(2,1)S(1)} %add_convert_fusion.3), channel_id=1, source_target_pairs={{0,8},{2,10},{4,12},{6,14},{8,0},{10,2},{12,4},{14,6},{1,9},{3,11}... | collective-permute-start | bytes 196616 | tf_op jit(solution)/shard_map/ppermute | solution.py:219
  36.7 9.9 %collective-permute-start.14 = (bf16[128,512]{1,0:T(8,128)(2,1)S(1)}, bf16[128,512]{1,0:T(8,128)(2,1)S(1)}, u32[]{:S(2)}, u32[]{:S(2)}) collective-permute-start(bf16[128,512]{1,0:T(8,128)(2,1)S(1)} %pad_maximum_fusion.1), channel_id=1, source_target_pairs={{0,2},{2,0},{4,6},{6,4},{8,10},{10,8},{12,14},{14,12},{1,3},{3,1},... | collective-permute-start | bytes 393224 | tf_op jit(solution)/shard_map/ppermute | solution.py:219
  37.9 8.7 %collective-permute-start.12 = (bf16[128,512]{1,0:T(8,128)(2,1)S(1)}, bf16[128,512]{1,0:T(8,128)(2,1)S(1)}, u32[]{:S(2)}, u32[]{:S(2)}) collective-permute-start(bf16[128,512]{1,0:T(8,128)(2,1)S(1)} %pad_maximum_fusion), channel_id=1, source_target_pairs={{0,4},{2,6},{4,0},{6,2},{8,12},{10,14},{12,8},{14,10},{1,5},{3,7},... | collective-permute-start | bytes 393224 | tf_op jit(solution)/shard_map/ppermute | solution.py:219
  39.4 4.3 %collective-permute-start.19 = (bf16[64,512]{1,0:T(8,128)(2,1)S(1)}, bf16[64,512]{1,0:T(8,128)(2,1)S(1)}, u32[]{:S(2)}, u32[]{:S(2)}) collective-permute-start(bf16[64,512]{1,0:T(8,128)(2,1)S(1)} %add_convert_fusion), channel_id=1, source_target_pairs={{0,4},{2,6},{4,0},{6,2},{8,12},{10,14},{12,8},{14,10},{1,5},{3,7},... | collective-permute-start | bytes 196616 | tf_op jit(solution)/shard_map/ppermute | solution.py:219
  41.0 5.0 %collective-permute-start.16 = (bf16[64,512]{1,0:T(8,128)(2,1)S(1)}, bf16[64,512]{1,0:T(8,128)(2,1)S(1)}, u32[]{:S(2)}, u32[]{:S(2)}) collective-permute-start(bf16[64,512]{1,0:T(8,128)(2,1)S(1)} %add_convert_fusion.1), channel_id=1, source_target_pairs={{0,2},{2,0},{4,6},{6,4},{8,10},{10,8},{12,14},{14,12},{1,3},{3,1},... | collective-permute-start | bytes 196616 | tf_op jit(solution)/shard_map/ppermute | solution.py:219
  43.8 5.0 %collective-permute-start.20 = (bf16[128,512]{1,0:T(8,128)(2,1)S(1)}, bf16[128,512]{1,0:T(8,128)(2,1)S(1)}, u32[]{:S(2)}, u32[]{:S(2)}) collective-permute-start(bf16[128,512]{1,0:T(8,128)(2,1)S(1)} %pad_maximum_fusion.3), channel_id=1, source_target_pairs={{0,2},{2,0},{4,6},{6,4},{8,10},{10,8},{12,14},{14,12},{1,3},{3,1},... | collective-permute-start | bytes 393224 | tf_op jit(solution)/shard_map/ppermute | solution.py:219
  46.0 5.0 %collective-permute-start.17 = (bf16[128,512]{1,0:T(8,128)(2,1)S(1)}, bf16[128,512]{1,0:T(8,128)(2,1)S(1)}, u32[]{:S(2)}, u32[]{:S(2)}) collective-permute-start(bf16[128,512]{1,0:T(8,128)(2,1)S(1)} %pad_maximum_fusion.2), channel_id=1, source_target_pairs={{0,4},{2,6},{4,0},{6,2},{8,12},{10,14},{12,8},{14,10},{1,5},{3,7},... | collective-permute-start | bytes 393224 | tf_op jit(solution)/shard_map/ppermute | solution.py:219
  46.7 4.4 %copy-start.3 = (s32[512]{0:T(512)S(1)}, s32[512]{0:T(512)}, u32[]{:S(2)}) copy-start(s32[512]{0:T(512)} %param.10) | copy-start | bytes 6148
  46.7 4.4 %copy-start.4 = (s32[128]{0:T(128)S(1)}, s32[128]{0:T(128)}, u32[]{:S(2)}) copy-start(s32[128]{0:T(128)} %param.11) | copy-start | bytes 1540
  51.1 1.1 %copy-start = (bf16[512,1024]{1,0:T(8,128)(2,1)}, bf16[512,1024]{1,0:T(8,128)(2,1)S(1)}, u32[]{:S(2)}) copy-start(bf16[512,1024]{1,0:T(8,128)(2,1)S(1)} %maximum_dynamic-update-slice_fusion.3) | copy-start | bytes 3145732

commit v17 on v16

--- a/solution.py
+++ b/solution.py
@@ -15,7 +15,14 @@
 PAIR = 2 * KOUT
 DEPTH_BLOCK = 512
 COLUMNS = 512
-CUTS = 2
+ORDERS = ((0,), (1, 0))
+LANES = 128
+NEAR_START_US = 1.1
+FAR_START_US = 1.5
+LATENCY_US = 0.5
+NEAR_BYTES_PER_US = 50000
+FAR_BYTES_PER_US = 25000
+KERNEL_US = 5.3
 PIECES = 4
 STORE_COPIES = 8
 VMEM_LIMIT = 32 * 1024 * 1024
@@ -240,8 +247,13 @@
             sent = lax.dynamic_slice_in_dim(self.block, (1 - upper) * rows, rows, 0)
             sent = sent.astype(jnp.bfloat16)
             self.block = lax.dynamic_slice_in_dim(self.block, upper * rows, rows, 0)
-        self.sent = order.mark(sent)
-        self.received = swap(self.sent, bit)
+        sent = order.mark(sent)
+        self.token = sent[: 2 * ROWS, :LANES]
+        self.received = swap(sent, bit)
+
+    def bytes_of_move(self):
+        size = self.block.size
+        return size if self.moves[0][1] == HALVE else 2 * size
 
     def take(self, order):
         bit, kind = self.moves.pop(0)
@@ -271,16 +283,29 @@
         return value
 
 
-def cut(columns):
-    return [columns * k // CUTS for k in range(CUTS + 1)]
-
-
-def rotate(chunks, order):
-    for chunk in chunks:
-        if chunk.moves:
-            chunk.take(order)
-            if chunk.moves:
-                chunk.send(order)
+class Clock:
+    def __init__(self):
+        self.now = 0.0
+        self.links = {}
+        self.arrivals = {}
+
+    def send(self, chunk):
+        bit, _ = chunk.moves[0]
+        far = bit > 2
+        self.now += FAR_START_US if far else NEAR_START_US
+        begin = max(self.now, self.links.get(bit, 0.0))
+        end = begin + chunk.bytes_of_move() / (FAR_BYTES_PER_US if far else NEAR_BYTES_PER_US)
+        self.links[bit] = end
+        self.arrivals[chunk] = end + (2 * LATENCY_US if far else LATENCY_US)
+
+    def take(self, chunk):
+        self.now = max(self.now, self.arrivals.pop(chunk))
+
+
+def send(chunk, order, clock):
+    if chunk.moves:
+        clock.send(chunk)
+        chunk.send(order)
 
 
 def shards(store, queries, left_inv, right_inv, query_prompt, winner):
@@ -291,28 +316,32 @@
     count = lax.axis_size("layer")
     index = lax.axis_index("layer")
     bits = [1 << k for k in range(count.bit_length() - 1)]
-    orders = [bits[1:2] + bits[:1] + bits[2:], bits]
-    order = Order()
+    orders = [bits, bits[1:2] + bits[:1] + bits[2:]]
+    order, clock = Order(), Clock()
     chunks, places = [], []
     current = queries
-    cuts = cut(columns)
     for step in range(ex_count):
         if step == 0:
             part, both, mixer = first_scores(queries, left_inv, right_inv, store)
         else:
             route = [((i - 1) % ex_count, i) for i in range(ex_count)]
             current = lax.ppermute(current, "ex", route)
-            sent = [chunk.sent for chunk in chunks if chunk.moves]
-            part = order.mark(later_scores(order.after(current), both, mixer, store, sent))
-            rotate(chunks, order)
-        for number, (first, end) in enumerate(zip(cuts[:-1], cuts[1:])):
-            chunk = LayerSum(part[:, first:end], orders[number % 2], index)
-            if chunk.moves:
-                chunk.send(order)
+            tokens = [chunk.token for chunk in chunks if chunk.moves]
+            part = order.mark(later_scores(order.after(current), both, mixer, store, tokens))
+            clock.now += KERNEL_US
+        choices = ORDERS[min(step, len(ORDERS) - 1)]
+        width = columns // len(choices)
+        for number, choice in enumerate(choices):
+            first = number * width
+            chunk = LayerSum(part[:, first : first + width], orders[choice], index)
+            send(chunk, order, clock)
             chunks.append(chunk)
             places.append(((position - step) % ex_count * rows, jnp.int32(first)))
-    while any(chunk.moves for chunk in chunks):
-        rotate(chunks, order)
+    while clock.arrivals:
+        chunk = min(clock.arrivals, key=clock.arrivals.get)
+        clock.take(chunk)
+        chunk.take(order)
+        send(chunk, order, clock)
     done = [chunk.block for chunk in chunks]
     scores = jnp.zeros((rows * ex_count, columns), jnp.bfloat16)
     for place, block in zip(places, done):

time: 52.4 us -> 80.9 us (1.54)
  waiting for transfers between devices: 12 us -> 36.1 us
  other arithmetic: 0.66 us -> 2.56 us
  local copies, waits for them, and re-layouts: 0.79 us -> 2.53 us
    ppermute x20 -> x15, waiting for transfers between devices: 12 us -> 36.1 us  [swap(): return lax.ppermute(block, 'layer', route)]
    ppermute x20 -> x15, starting transfers between devices: 24 us -> 25.4 us  [swap(): return lax.ppermute(block, 'layer', route)]
    add x4 -> x2, other arithmetic: 0.12 us -> 1.08 us  [take(): self.block = mine.astype(jnp.float32) + received.astype(jnp.float32)]
    convert_element_type x8 -> x6, other arithmetic: 0.14 us -> 1.08 us  [take(): self.block = self.block.astype(jnp.bfloat16)]
  transfers between devices with their start and end apart: 21 -> 16, of which waited for: 9 -> 14; matrix products, arithmetic and copies ran while one was open for 2% -> 4% of each run, Pallas kernels for 23% -> 0%
where the time goes in v17:
time: 80.9 us; the launch traced here: 80.7 us
  waiting for transfers between devices  36.1 us (45%)
  starting transfers between devices  25.4 us (31%)
  Pallas kernels  12.2 us (15%)
  other arithmetic  2.56 us (3%)
  local copies, waits for them, and re-layouts  2.53 us (3%)
  matrix products  1.07 us (1%)
  between operations  0.87 us (1%)
    ppermute x15, waiting for transfers between devices, swap(): return lax.ppermute(block, 'layer', route)  36.1 us
    ppermute x15, starting transfers between devices, swap(): return lax.ppermute(block, 'layer', route)  25.4 us
    pallas_call x2, Pallas kernels, call(): pl.pallas_call(kernel, out_shape=(jax.ShapeDtypeStruct((count, examples),...  12.2 us
  transfers between devices with their start and end apart: 16, of which 14 were waited for; matrix products, arithmetic and copies ran while one was open for 4% of the time, Pallas kernels for 0%

profile of v17, /device:TPU:0, one launch (start us, length us, event | category | flops | bytes accessed | tf_op | source)
XLA Modules:
  0.0 80.7 jit_solution(9735481901890562563)
XLA Ops:
  0.6 6.9 %shard_map.77 = (f32[256,1024]{1,0:T(8,128)S(1)}, bf16[256,256]{1,0:T(8,128)(2,1)S(1)}, bf16[256,256]{1,0:T(8,128)(2,1)S(1)}) custom-call(bf16[1,256,4096]{2,1,0:T(8,128)(2,1)} %rows_ref.1, bf16[1,32,32]{2,1,0:T(8,128)(2,1)} %left_ref.1, bf16[1,128,128]{2,1,0:T(8,128)(2,1)} %right_ref.1, bf16[1,1024,4096]{2,1,0:T(8,128)(2,1)} %store_ref.3), custom_call_target="tpu_custom_call" | custom-call | flops 4294967296 | bytes 10485760 | tf_op jit(solution)/shard_map/pallas_call | solution.py:175
  7.6 0.7 dynamic-slice_convert_fusion
  8.3 3.0 %collective-permute-start = (bf16[128,1024]{1,0:T(8,128)(2,1)}, bf16[128,1024]{1,0:T(8,128)(2,1)}, u32[]{:S(2)}, u32[]{:S(2)}) collective-permute-start(bf16[128,1024]{1,0:T(8,128)(2,1)} %dynamic-slice_convert_fusion), channel_id=1, source_target_pairs={{0,2},{2,0},{4,6},{6,4},{8,10},{10,8},{12,14},{14,12},{1,3},{3,1},... | collective-permute-start | bytes 786440 | tf_op jit(solution)/shard_map/ppermute | solution.py:226
  11.3 0.0 collective-permute-start.1
  11.3 6.6 %collective-permute-done = bf16[128,1024]{1,0:T(8,128)(2,1)} collective-permute-done((bf16[128,1024]{1,0:T(8,128)(2,1)}, bf16[128,1024]{1,0:T(8,128)(2,1)}, u32[]{:S(2)}, u32[]{:S(2)}) %collective-permute-start) | collective-permute-done | bytes 262176 | tf_op jit(solution)/shard_map/ppermute | solution.py:226
  17.9 1.0 %convert_add_fusion = f32[128,1024]{1,0:T(8,128)S(1)} fusion(bf16[128,1024]{1,0:T(8,128)(2,1)} %collective-permute-done, f32[256,1024]{1,0:T(8,128)S(1)} %get-tuple-element.39, s32[]{:T(128)S(6)} %select_n.127), kind=kLoop, calls=%fused_computation.2 | loop fusion | flops 262144 | bytes 1310724 | tf_op jit(solution)/shard_map/add | solution.py:268
  18.9 0.0 copy-start.1
  18.9 0.8 copy-done.1
  19.7 1.9 %collective-permute-start.2 = (bf16[64,1024]{1,0:T(8,128)(2,1)S(1)}, bf16[64,1024]{1,0:T(8,128)(2,1)S(1)}, u32[]{:S(2)}, u32[]{:S(2)}) collective-permute-start(bf16[64,1024]{1,0:T(8,128)(2,1)S(1)} %dynamic-slice_convert_fusion.1), channel_id=1, source_target_pairs={{0,4},{2,6},{4,0},{6,2},{8,12},{10,14},{12,8},{14,10},{1,5},{3,7},... | collective-permute-start | bytes 393224 | tf_op jit(solution)/shard_map/ppermute | solution.py:226
  21.6 3.2 %collective-permute-done.2 = bf16[64,1024]{1,0:T(8,128)(2,1)S(1)} collective-permute-done((bf16[64,1024]{1,0:T(8,128)(2,1)S(1)}, bf16[64,1024]{1,0:T(8,128)(2,1)S(1)}, u32[]{:S(2)}, u32[]{:S(2)}) %collective-permute-start.2) | collective-permute-done | bytes 131104 | tf_op jit(solution)/shard_map/ppermute | solution.py:226
  24.8 1.0 %add_convert_fusion.1 = bf16[64,1024]{1,0:T(8,128)(2,1)S(1)} fusion(bf16[64,1024]{1,0:T(8,128)(2,1)S(1)} %collective-permute-done.2, f32[128,1024]{1,0:T(8,128)} %copy-done.1, s32[]{:T(128)S(6)} %select_n.131), kind=kLoop, calls=%fused_computation.11 | loop fusion | flops 196608 | bytes 524292 | tf_op jit(solution)/shard_map/convert_element_type | solution.py:270
  25.7 2.9 %collective-permute-start.5 = (bf16[64,1024]{1,0:T(8,128)(2,1)S(1)}, bf16[64,1024]{1,0:T(8,128)(2,1)S(1)}, u32[]{:S(2)}, u32[]{:S(2)}) collective-permute-start(bf16[64,1024]{1,0:T(8,128)(2,1)S(1)} %add_convert_fusion.1), channel_id=1, source_target_pairs={{0,8},{2,10},{4,12},{6,14},{8,0},{10,2},{12,4},{14,6},{1,9},{3,11}... | collective-permute-start | bytes 393224 | tf_op jit(solution)/shard_map/ppermute | solution.py:226
  28.6 4.5 %collective-permute-done.5 = bf16[64,1024]{1,0:T(8,128)(2,1)S(1)} collective-permute-done((bf16[64,1024]{1,0:T(8,128)(2,1)S(1)}, bf16[64,1024]{1,0:T(8,128)(2,1)S(1)}, u32[]{:S(2)}, u32[]{:S(2)}) %collective-permute-start.5) | collective-permute-done | bytes 131104 | tf_op jit(solution)/shard_map/ppermute | solution.py:226
  33.2 0.9 %collective-permute-start.8 = (bf16[64,1024]{1,0:T(8,128)(2,1)S(1)}, bf16[64,1024]{1,0:T(8,128)(2,1)S(1)}, u32[]{:S(2)}, u32[]{:S(2)}) collective-permute-start(bf16[64,1024]{1,0:T(8,128)(2,1)S(1)} %add_convert_fusion), channel_id=1, source_target_pairs={{0,4},{2,6},{4,0},{6,2},{8,12},{10,14},{12,8},{14,10},{1,5},{3,7},... | collective-permute-start | bytes 393224 | tf_op jit(solution)/shard_map/ppermute | solution.py:226
  34.1 4.2 %collective-permute-done.8 = bf16[64,1024]{1,0:T(8,128)(2,1)S(1)} collective-permute-done((bf16[64,1024]{1,0:T(8,128)(2,1)S(1)}, bf16[64,1024]{1,0:T(8,128)(2,1)S(1)}, u32[]{:S(2)}, u32[]{:S(2)}) %collective-permute-start.8) | collective-permute-done | bytes 131104 | tf_op jit(solution)/shard_map/ppermute | solution.py:226
  38.3 1.8 %collective-permute-start.9 = (bf16[128,1024]{1,0:T(8,128)(2,1)S(1)}, bf16[128,1024]{1,0:T(8,128)(2,1)S(1)}, u32[]{:S(2)}, u32[]{:S(2)}) collective-permute-start(bf16[128,1024]{1,0:T(8,128)(2,1)S(1)} %pad_maximum_fusion), channel_id=1, source_target_pairs={{0,2},{2,0},{4,6},{6,4},{8,10},{10,8},{12,14},{14,12},{1,3},{3,1},... | collective-permute-start | bytes 786440 | tf_op jit(solution)/shard_map/ppermute | solution.py:226
  40.1 0.7 slice.9.refs_0_
  40.8 3.9 %collective-permute-done.9 = bf16[128,1024]{1,0:T(8,128)(2,1)S(1)} collective-permute-done((bf16[128,1024]{1,0:T(8,128)(2,1)S(1)}, bf16[128,1024]{1,0:T(8,128)(2,1)S(1)}, u32[]{:S(2)}, u32[]{:S(2)}) %collective-permute-start.9) | collective-permute-done | bytes 262176 | tf_op jit(solution)/shard_map/ppermute | solution.py:226
  44.7 0.0 collective-permute-done.1.rows_ref
  44.7 5.3 %shard_map.78 = f32[256,1024]{1,0:T(8,128)S(1)} custom-call(bf16[1,256,4096]{2,1,0:T(8,128)(2,1)S(1)} %collective-permute-done.1.rows_ref, bf16[256,256]{1,0:T(8,128)(2,1)S(1)} %get-tuple-element.43.both_ref, bf16[256,256]{1,0:T(8,128)(2,1)S(1)} %get-tuple-element.44.mixer_ref, bf16[1,1024,4096]{2,1,0:T(8,128)(2,1)} %store_ref.3, ...), custom_call_target="tpu_custom_call" | custom-call | flops 4294967296 | bytes 10485760 | tf_op jit(solution)/shard_map/pallas_call | solution.py:175
  50.0 0.1 fusion.6
  50.2 0.9 %collective-permute-start.4 = (bf16[128,512]{1,0:T(8,128)(2,1)S(1)}, bf16[128,512]{1,0:T(8,128)(2,1)S(1)}, u32[]{:S(2)}, u32[]{:S(2)}) collective-permute-start(bf16[128,512]{1,0:T(8,128)(2,1)S(1)} %dynamic-slice_convert_fusion.2), channel_id=1, source_target_pairs={{0,4},{2,6},{4,0},{6,2},{8,12},{10,14},{12,8},{14,10},{1,5},{3,7},... | collective-permute-start | bytes 393224 | tf_op jit(solution)/shard_map/ppermute | solution.py:226
  51.1 1.5 %collective-permute-start.3 = (bf16[128,512]{1,0:T(8,128)(2,1)S(1)}, bf16[128,512]{1,0:T(8,128)(2,1)S(1)}, u32[]{:S(2)}, u32[]{:S(2)}) collective-permute-start(bf16[128,512]{1,0:T(8,128)(2,1)S(1)} %dynamic-slice_convert_fusion.3), channel_id=1, source_target_pairs={{0,2},{2,0},{4,6},{6,4},{8,10},{10,8},{12,14},{14,12},{1,3},{3,1},... | collective-permute-start | bytes 393224 | tf_op jit(solution)/shard_map/ppermute | solution.py:226
  52.6 0.1 broadcast_select_fusion.1
  52.7 0.1 broadcast_in_dim.2
  52.9 2.6 %collective-permute-done.4 = bf16[128,512]{1,0:T(8,128)(2,1)S(1)} collective-permute-done((bf16[128,512]{1,0:T(8,128)(2,1)S(1)}, bf16[128,512]{1,0:T(8,128)(2,1)S(1)}, u32[]{:S(2)}, u32[]{:S(2)}) %collective-permute-start.4) | collective-permute-done | bytes 131104 | tf_op jit(solution)/shard_map/ppermute | solution.py:226
  55.5 0.6 collective-permute-done.3
  56.0 0.1 convert_add_fusion.1
  56.1 1.6 %collective-permute-start.7 = (bf16[64,512]{1,0:T(8,128)(2,1)S(1)}, bf16[64,512]{1,0:T(8,128)(2,1)S(1)}, u32[]{:S(2)}, u32[]{:S(2)}) collective-permute-start(bf16[64,512]{1,0:T(8,128)(2,1)S(1)} %dynamic-slice_convert_fusion.5), channel_id=1, source_target_pairs={{0,2},{2,0},{4,6},{6,4},{8,10},{10,8},{12,14},{14,12},{1,3},{3,1},... | collective-permute-start | bytes 196616 | tf_op jit(solution)/shard_map/ppermute | solution.py:226
  57.7 0.0 copy-start.2
  57.7 0.0 copy-start.3
  57.7 1.5 %collective-permute-start.6 = (bf16[64,512]{1,0:T(8,128)(2,1)S(1)}, bf16[64,512]{1,0:T(8,128)(2,1)S(1)}, u32[]{:S(2)}, u32[]{:S(2)}) collective-permute-start(bf16[64,512]{1,0:T(8,128)(2,1)S(1)} %dynamic-slice_convert_fusion.4), channel_id=1, source_target_pairs={{0,4},{2,6},{4,0},{6,2},{8,12},{10,14},{12,8},{14,10},{1,5},{3,7},... | collective-permute-start | bytes 196616 | tf_op jit(solution)/shard_map/ppermute | solution.py:226
  59.2 1.2 %collective-permute-done.7 = bf16[64,512]{1,0:T(8,128)(2,1)S(1)} collective-permute-done((bf16[64,512]{1,0:T(8,128)(2,1)S(1)}, bf16[64,512]{1,0:T(8,128)(2,1)S(1)}, u32[]{:S(2)}, u32[]{:S(2)}) %collective-permute-start.7) | collective-permute-done | bytes 65568 | tf_op jit(solution)/shard_map/ppermute | solution.py:226
  60.5 4.0 %collective-permute-start.10 = (bf16[64,512]{1,0:T(8,128)(2,1)S(1)}, bf16[64,512]{1,0:T(8,128)(2,1)S(1)}, u32[]{:S(2)}, u32[]{:S(2)}) collective-permute-start(bf16[64,512]{1,0:T(8,128)(2,1)S(1)} %add_convert_fusion.5), channel_id=1, source_target_pairs={{0,8},{2,10},{4,12},{6,14},{8,0},{10,2},{12,4},{14,6},{1,9},{3,11}... | collective-permute-start | bytes 196616 | tf_op jit(solution)/shard_map/ppermute | solution.py:226
  64.5 0.0 collective-permute-done.6
  64.5 1.5 %collective-permute-start.13 = (bf16[64,512]{1,0:T(8,128)(2,1)S(1)}, bf16[64,512]{1,0:T(8,128)(2,1)S(1)}, u32[]{:S(2)}, u32[]{:S(2)}) collective-permute-start(bf16[64,512]{1,0:T(8,128)(2,1)S(1)} %add_convert_fusion.4), channel_id=1, source_target_pairs={{0,8},{2,10},{4,12},{6,14},{8,0},{10,2},{12,4},{14,6},{1,9},{3,11}... | collective-permute-start | bytes 196616 | tf_op jit(solution)/shard_map/ppermute | solution.py:226
  66.0 1.3 %collective-permute-done.10 = bf16[64,512]{1,0:T(8,128)(2,1)S(1)} collective-permute-done((bf16[64,512]{1,0:T(8,128)(2,1)S(1)}, bf16[64,512]{1,0:T(8,128)(2,1)S(1)}, u32[]{:S(2)}, u32[]{:S(2)}) %collective-permute-start.10) | collective-permute-done | bytes 65568 | tf_op jit(solution)/shard_map/ppermute | solution.py:226
  67.4 1.7 %collective-permute-start.11 = (bf16[64,512]{1,0:T(8,128)(2,1)S(1)}, bf16[64,512]{1,0:T(8,128)(2,1)S(1)}, u32[]{:S(2)}, u32[]{:S(2)}) collective-permute-start(bf16[64,512]{1,0:T(8,128)(2,1)S(1)} %add_convert_fusion.3), channel_id=1, source_target_pairs={{0,2},{2,0},{4,6},{6,4},{8,10},{10,8},{12,14},{14,12},{1,3},{3,1},... | collective-permute-start | bytes 196616 | tf_op jit(solution)/shard_map/ppermute | solution.py:226
  69.1 0.9 %collective-permute-done.13 = bf16[64,512]{1,0:T(8,128)(2,1)S(1)} collective-permute-done((bf16[64,512]{1,0:T(8,128)(2,1)S(1)}, bf16[64,512]{1,0:T(8,128)(2,1)S(1)}, u32[]{:S(2)}, u32[]{:S(2)}) %collective-permute-start.13) | collective-permute-done | bytes 65568 | tf_op jit(solution)/shard_map/ppermute | solution.py:226
  70.1 0.1 collective-permute-start.14
  70.1 1.6 %collective-permute-done.11 = bf16[64,512]{1,0:T(8,128)(2,1)S(1)} collective-permute-done((bf16[64,512]{1,0:T(8,128)(2,1)S(1)}, bf16[64,512]{1,0:T(8,128)(2,1)S(1)}, u32[]{:S(2)}, u32[]{:S(2)}) %collective-permute-start.11) | collective-permute-done | bytes 65568 | tf_op jit(solution)/shard_map/ppermute | solution.py:226
  71.7 0.5 collective-permute-start.12
  72.3 2.1 %collective-permute-done.14 = bf16[64,512]{1,0:T(8,128)(2,1)S(1)} collective-permute-done((bf16[64,512]{1,0:T(8,128)(2,1)S(1)}, bf16[64,512]{1,0:T(8,128)(2,1)S(1)}, u32[]{:S(2)}, u32[]{:S(2)}) %collective-permute-start.14) | collective-permute-done | bytes 65568 | tf_op jit(solution)/shard_map/ppermute | solution.py:226
  74.4 1.6 %collective-permute-start.15 = (bf16[128,512]{1,0:T(8,128)(2,1)S(1)}, bf16[128,512]{1,0:T(8,128)(2,1)S(1)}, u32[]{:S(2)}, u32[]{:S(2)}) collective-permute-start(bf16[128,512]{1,0:T(8,128)(2,1)S(1)} %pad_maximum_fusion.2), channel_id=1, source_target_pairs={{0,2},{2,0},{4,6},{6,4},{8,10},{10,8},{12,14},{14,12},{1,3},{3,1},... | collective-permute-start | bytes 393224 | tf_op jit(solution)/shard_map/ppermute | solution.py:226
  76.0 0.8 collective-permute-done.12
  76.8 2.6 %collective-permute-done.15 = bf16[128,512]{1,0:T(8,128)(2,1)S(1)} collective-permute-done((bf16[128,512]{1,0:T(8,128)(2,1)S(1)}, bf16[128,512]{1,0:T(8,128)(2,1)S(1)}, u32[]{:S(2)}, u32[]{:S(2)}) %collective-permute-start.15) | collective-permute-done | bytes 131104 | tf_op jit(solution)/shard_map/ppermute | solution.py:226
  79.6 0.0 copy-done.2
  79.6 0.0 copy-done.3
  79.6 0.0 copy-start
  79.6 1.1 %convolution_convert_fusion = bf16[128,1024]{1,0:T(8,128)(2,1)} fusion(bf16[512,1024]{1,0:T(8,128)(2,1)S(1)} %maximum_dynamic-update-slice_fusion.2, s32[512]{0:T(512)S(1)} %copy-done.2, s32[128]{0:T(128)S(1)} %copy-done.3), kind=kOutput, calls=%fused_computation | convolution fusion | flops 134742016 | bytes 1313280 | tf_op jit(solution)/shard_map/dot_general | solution.py:354
  80.7 0.0 copy-done
  (21 shorter events, 0.5 us)
Async XLA Ops:
  8.3 9.6 %collective-permute-start = (bf16[128,1024]{1,0:T(8,128)(2,1)}, bf16[128,1024]{1,0:T(8,128)(2,1)}, u32[]{:S(2)}, u32[]{:S(2)}) collective-permute-start(bf16[128,1024]{1,0:T(8,128)(2,1)} %dynamic-slice_convert_fusion), channel_id=1, source_target_pairs={{0,2},{2,0},{4,6},{6,4},{8,10},{10,8},{12,14},{14,12},{1,3},{3,1},... | collective-permute-start | bytes 786440 | tf_op jit(solution)/shard_map/ppermute | solution.py:226
  11.3 33.5 %collective-permute-start.1 = (bf16[1,256,4096]{2,1,0:T(8,128)(2,1)}, bf16[1,256,4096]{2,1,0:T(8,128)(2,1)S(1)}, u32[]{:S(2)}, u32[]{:S(2)}) collective-permute-start(bf16[1,256,4096]{2,1,0:T(8,128)(2,1)} %rows_ref.1), channel_id=1, source_target_pairs={{1,0},{0,1},{3,2},{2,3},{5,4},{4,5},{7,6},{6,7},{9,8},{8,9},{11,10... | collective-permute-start | bytes 6291464 | tf_op jit(solution)/shard_map/ppermute | solution.py:328
  18.9 0.8 copy-start.1
  19.7 5.0 %collective-permute-start.2 = (bf16[64,1024]{1,0:T(8,128)(2,1)S(1)}, bf16[64,1024]{1,0:T(8,128)(2,1)S(1)}, u32[]{:S(2)}, u32[]{:S(2)}) collective-permute-start(bf16[64,1024]{1,0:T(8,128)(2,1)S(1)} %dynamic-slice_convert_fusion.1), channel_id=1, source_target_pairs={{0,4},{2,6},{4,0},{6,2},{8,12},{10,14},{12,8},{14,10},{1,5},{3,7},... | collective-permute-start | bytes 393224 | tf_op jit(solution)/shard_map/ppermute | solution.py:226
  25.7 7.4 %collective-permute-start.5 = (bf16[64,1024]{1,0:T(8,128)(2,1)S(1)}, bf16[64,1024]{1,0:T(8,128)(2,1)S(1)}, u32[]{:S(2)}, u32[]{:S(2)}) collective-permute-start(bf16[64,1024]{1,0:T(8,128)(2,1)S(1)} %add_convert_fusion.1), channel_id=1, source_target_pairs={{0,8},{2,10},{4,12},{6,14},{8,0},{10,2},{12,4},{14,6},{1,9},{3,11}... | collective-permute-start | bytes 393224 | tf_op jit(solution)/shard_map/ppermute | solution.py:226
  33.2 5.0 %collective-permute-start.8 = (bf16[64,1024]{1,0:T(8,128)(2,1)S(1)}, bf16[64,1024]{1,0:T(8,128)(2,1)S(1)}, u32[]{:S(2)}, u32[]{:S(2)}) collective-permute-start(bf16[64,1024]{1,0:T(8,128)(2,1)S(1)} %add_convert_fusion), channel_id=1, source_target_pairs={{0,4},{2,6},{4,0},{6,2},{8,12},{10,14},{12,8},{14,10},{1,5},{3,7},... | collective-permute-start | bytes 393224 | tf_op jit(solution)/shard_map/ppermute | solution.py:226
  38.3 6.4 %collective-permute-start.9 = (bf16[128,1024]{1,0:T(8,128)(2,1)S(1)}, bf16[128,1024]{1,0:T(8,128)(2,1)S(1)}, u32[]{:S(2)}, u32[]{:S(2)}) collective-permute-start(bf16[128,1024]{1,0:T(8,128)(2,1)S(1)} %pad_maximum_fusion), channel_id=1, source_target_pairs={{0,2},{2,0},{4,6},{6,4},{8,10},{10,8},{12,14},{14,12},{1,3},{3,1},... | collective-permute-start | bytes 786440 | tf_op jit(solution)/shard_map/ppermute | solution.py:226
  50.2 5.3 %collective-permute-start.4 = (bf16[128,512]{1,0:T(8,128)(2,1)S(1)}, bf16[128,512]{1,0:T(8,128)(2,1)S(1)}, u32[]{:S(2)}, u32[]{:S(2)}) collective-permute-start(bf16[128,512]{1,0:T(8,128)(2,1)S(1)} %dynamic-slice_convert_fusion.2), channel_id=1, source_target_pairs={{0,4},{2,6},{4,0},{6,2},{8,12},{10,14},{12,8},{14,10},{1,5},{3,7},... | collective-permute-start | bytes 393224 | tf_op jit(solution)/shard_map/ppermute | solution.py:226
  51.1 5.0 %collective-permute-start.3 = (bf16[128,512]{1,0:T(8,128)(2,1)S(1)}, bf16[128,512]{1,0:T(8,128)(2,1)S(1)}, u32[]{:S(2)}, u32[]{:S(2)}) collective-permute-start(bf16[128,512]{1,0:T(8,128)(2,1)S(1)} %dynamic-slice_convert_fusion.3), channel_id=1, source_target_pairs={{0,2},{2,0},{4,6},{6,4},{8,10},{10,8},{12,14},{14,12},{1,3},{3,1},... | collective-permute-start | bytes 393224 | tf_op jit(solution)/shard_map/ppermute | solution.py:226
  56.1 4.3 %collective-permute-start.7 = (bf16[64,512]{1,0:T(8,128)(2,1)S(1)}, bf16[64,512]{1,0:T(8,128)(2,1)S(1)}, u32[]{:S(2)}, u32[]{:S(2)}) collective-permute-start(bf16[64,512]{1,0:T(8,128)(2,1)S(1)} %dynamic-slice_convert_fusion.5), channel_id=1, source_target_pairs={{0,2},{2,0},{4,6},{6,4},{8,10},{10,8},{12,14},{14,12},{1,3},{3,1},... | collective-permute-start | bytes 196616 | tf_op jit(solution)/shard_map/ppermute | solution.py:226
  57.7 21.9 %copy-start.2 = (s32[512]{0:T(512)S(1)}, s32[512]{0:T(512)}, u32[]{:S(2)}) copy-start(s32[512]{0:T(512)} %param.10) | copy-start | bytes 6148
  57.7 21.9 %copy-start.3 = (s32[128]{0:T(128)S(1)}, s32[128]{0:T(128)}, u32[]{:S(2)}) copy-start(s32[128]{0:T(128)} %param.11) | copy-start | bytes 1540
  57.7 6.8 %collective-permute-start.6 = (bf16[64,512]{1,0:T(8,128)(2,1)S(1)}, bf16[64,512]{1,0:T(8,128)(2,1)S(1)}, u32[]{:S(2)}, u32[]{:S(2)}) collective-permute-start(bf16[64,512]{1,0:T(8,128)(2,1)S(1)} %dynamic-slice_convert_fusion.4), channel_id=1, source_target_pairs={{0,4},{2,6},{4,0},{6,2},{8,12},{10,14},{12,8},{14,10},{1,5},{3,7},... | collective-permute-start | bytes 196616 | tf_op jit(solution)/shard_map/ppermute | solution.py:226
  60.5 6.9 %collective-permute-start.10 = (bf16[64,512]{1,0:T(8,128)(2,1)S(1)}, bf16[64,512]{1,0:T(8,128)(2,1)S(1)}, u32[]{:S(2)}, u32[]{:S(2)}) collective-permute-start(bf16[64,512]{1,0:T(8,128)(2,1)S(1)} %add_convert_fusion.5), channel_id=1, source_target_pairs={{0,8},{2,10},{4,12},{6,14},{8,0},{10,2},{12,4},{14,6},{1,9},{3,11}... | collective-permute-start | bytes 196616 | tf_op jit(solution)/shard_map/ppermute | solution.py:226
  64.5 5.5 %collective-permute-start.13 = (bf16[64,512]{1,0:T(8,128)(2,1)S(1)}, bf16[64,512]{1,0:T(8,128)(2,1)S(1)}, u32[]{:S(2)}, u32[]{:S(2)}) collective-permute-start(bf16[64,512]{1,0:T(8,128)(2,1)S(1)} %add_convert_fusion.4), channel_id=1, source_target_pairs={{0,8},{2,10},{4,12},{6,14},{8,0},{10,2},{12,4},{14,6},{1,9},{3,11}... | collective-permute-start | bytes 196616 | tf_op jit(solution)/shard_map/ppermute | solution.py:226
  67.4 4.3 %collective-permute-start.11 = (bf16[64,512]{1,0:T(8,128)(2,1)S(1)}, bf16[64,512]{1,0:T(8,128)(2,1)S(1)}, u32[]{:S(2)}, u32[]{:S(2)}) collective-permute-start(bf16[64,512]{1,0:T(8,128)(2,1)S(1)} %add_convert_fusion.3), channel_id=1, source_target_pairs={{0,2},{2,0},{4,6},{6,4},{8,10},{10,8},{12,14},{14,12},{1,3},{3,1},... | collective-permute-start | bytes 196616 | tf_op jit(solution)/shard_map/ppermute | solution.py:226
  70.1 4.3 %collective-permute-start.14 = (bf16[64,512]{1,0:T(8,128)(2,1)S(1)}, bf16[64,512]{1,0:T(8,128)(2,1)S(1)}, u32[]{:S(2)}, u32[]{:S(2)}) collective-permute-start(bf16[64,512]{1,0:T(8,128)(2,1)S(1)} %add_convert_fusion.2), channel_id=1, source_target_pairs={{0,4},{2,6},{4,0},{6,2},{8,12},{10,14},{12,8},{14,10},{1,5},{3,7},... | collective-permute-start | bytes 196616 | tf_op jit(solution)/shard_map/ppermute | solution.py:226
  71.7 5.0 %collective-permute-start.12 = (bf16[128,512]{1,0:T(8,128)(2,1)S(1)}, bf16[128,512]{1,0:T(8,128)(2,1)S(1)}, u32[]{:S(2)}, u32[]{:S(2)}) collective-permute-start(bf16[128,512]{1,0:T(8,128)(2,1)S(1)} %pad_maximum_fusion.1), channel_id=1, source_target_pairs={{0,4},{2,6},{4,0},{6,2},{8,12},{10,14},{12,8},{14,10},{1,5},{3,7},... | collective-permute-start | bytes 393224 | tf_op jit(solution)/shard_map/ppermute | solution.py:226
  74.4 5.0 %collective-permute-start.15 = (bf16[128,512]{1,0:T(8,128)(2,1)S(1)}, bf16[128,512]{1,0:T(8,128)(2,1)S(1)}, u32[]{:S(2)}, u32[]{:S(2)}) collective-permute-start(bf16[128,512]{1,0:T(8,128)(2,1)S(1)} %pad_maximum_fusion.2), channel_id=1, source_target_pairs={{0,2},{2,0},{4,6},{6,4},{8,10},{10,8},{12,14},{14,12},{1,3},{3,1},... | collective-permute-start | bytes 393224 | tf_op jit(solution)/shard_map/ppermute | solution.py:226
  79.6 1.1 %copy-start = (bf16[512,1024]{1,0:T(8,128)(2,1)}, bf16[512,1024]{1,0:T(8,128)(2,1)S(1)}, u32[]{:S(2)}) copy-start(bf16[512,1024]{1,0:T(8,128)(2,1)S(1)} %maximum_dynamic-update-slice_fusion.2) | copy-start | bytes 3145732

commit v18 on v17

--- a/solution.py
+++ b/solution.py
@@ -15,7 +15,7 @@
 PAIR = 2 * KOUT
 DEPTH_BLOCK = 512
 COLUMNS = 512
-ORDERS = ((0,), (1, 0))
+ORDERS = ((1, 0), (1, 0))
 LANES = 128
 NEAR_START_US = 1.1
 FAR_START_US = 1.5
@@ -149,9 +149,10 @@
 
 
 def later_kernel(
-    sent, rows_ref, both_ref, mixer_ref, store_ref, *refs,
+    held, rows_ref, both_ref, mixer_ref, store_ref, *refs,
 ):
-    out_ref, pre_ref, store_vmem, half_ref, total_ref, store_sems = refs[sent:]
+    out_ref, *refs = refs[held:]
+    pre_ref, store_vmem, half_ref, total_ref, store_sems = refs[held:]
 
     def before(step):
         start_store(store_ref, store_vmem, store_sems, step)
@@ -169,14 +170,15 @@
     return pltpu.with_memory_space_constraint(array, pltpu.HBM)
 
 
-def call(kernel, queries, store, outs, in_specs, scratch, operands):
+def call(kernel, queries, store, outs, in_specs, scratch, operands, out_specs, aliases):
     count, depth = queries.shape[1:]
     examples = store.shape[1]
     return pl.pallas_call(
         kernel,
         out_shape=(jax.ShapeDtypeStruct((count, examples), jnp.float32),) + outs,
         in_specs=in_specs,
-        out_specs=(VMEM,) * (1 + len(outs)),
+        out_specs=out_specs,
+        input_output_aliases=aliases,
         scratch_shapes=scratch,
         compiler_params=pltpu.CompilerParams(vmem_limit_bytes=VMEM_LIMIT),
         cost_estimate=pl.CostEstimate(
@@ -208,17 +210,19 @@
     operands = [in_hbm(a) for a in (queries, left_inv, right_inv, store)]
     return call(
         first_kernel, queries, store, outs, [HBM] * 4,
-        small + buffers(queries, store) + sems, operands,
-    )
-
-
-def later_scores(queries, both, mixer, store, sent):
+        small + buffers(queries, store) + sems, operands, (VMEM,) * 3, {},
+    )
+
+
+def later_scores(queries, both, mixer, store, held):
     sems = [pltpu.SemaphoreType.DMA((STORE_COPIES,))]
+    outs = tuple(jax.ShapeDtypeStruct(a.shape, a.dtype) for a in held)
     return call(
-        functools.partial(later_kernel, len(sent)), queries, store, (),
-        [VMEM] * 3 + [HBM] + [ANYWHERE] * len(sent), buffers(queries, store) + sems,
-        [queries, both, mixer, in_hbm(store), *sent],
-    )[0]
+        functools.partial(later_kernel, len(held)), queries, store, outs,
+        [VMEM] * 3 + [HBM] + [ANYWHERE] * len(held), buffers(queries, store) + sems,
+        [queries, both, mixer, in_hbm(store), *held],
+        (VMEM,) + (ANYWHERE,) * len(held), {4 + k: 1 + k for k in range(len(held))},
+    )
 
 
 def swap(block, bit):
@@ -247,9 +251,7 @@
             sent = lax.dynamic_slice_in_dim(self.block, (1 - upper) * rows, rows, 0)
             sent = sent.astype(jnp.bfloat16)
             self.block = lax.dynamic_slice_in_dim(self.block, upper * rows, rows, 0)
-        sent = order.mark(sent)
-        self.token = sent[: 2 * ROWS, :LANES]
-        self.received = swap(sent, bit)
+        self.received = swap(order.mark(sent), bit)
 
     def bytes_of_move(self):
         size = self.block.size
@@ -326,9 +328,16 @@
         else:
             route = [((i - 1) % ex_count, i) for i in range(ex_count)]
             current = lax.ppermute(current, "ex", route)
-            tokens = [chunk.token for chunk in chunks if chunk.moves]
-            part = order.mark(later_scores(order.after(current), both, mixer, store, tokens))
+            held = [chunk.block for chunk in chunks]
+            part, *held = later_scores(order.after(current), both, mixer, store, held)
+            part = order.mark(part)
+            for chunk, block in zip(chunks, held):
+                chunk.block = block
             clock.now += KERNEL_US
+            for chunk in chunks:
+                clock.take(chunk)
+                chunk.take(order)
+                send(chunk, order, clock)
         choices = ORDERS[min(step, len(ORDERS) - 1)]
         width = columns // len(choices)
         for number, choice in enumerate(choices):
@@ -338,7 +347,8 @@
             chunks.append(chunk)
             places.append(((position - step) % ex_count * rows, jnp.int32(first)))
     while clock.arrivals:
-        chunk = min(clock.arrivals, key=clock.arrivals.get)
+        there = [c for c, at in clock.arrivals.items() if at <= clock.now]
+        chunk = there[-1] if there else min(clock.arrivals, key=clock.arrivals.get)
         clock.take(chunk)
         chunk.take(order)
         send(chunk, order, clock)

time: 80.9 us -> 53.3 us (0.66)
  waiting for transfers between devices: 36.1 us -> 11.6 us
  local copies, waits for them, and re-layouts: 2.53 us -> 1.2 us
  other arithmetic: 2.56 us -> 1.56 us
  starting transfers between devices: 25.4 us -> 24.5 us
    ppermute x15 -> x20, waiting for transfers between devices: 36.1 us -> 11.6 us  [swap(): return lax.ppermute(block, 'layer', route)]
    ppermute x15 -> x20, starting transfers between devices: 25.4 us -> 24 us  [swap(): return lax.ppermute(block, 'layer', route)]
    convert_element_type x6 -> x8, other arithmetic: 1.08 us -> 0.14 us  [take(): self.block = self.block.astype(jnp.bfloat16)]
  transfers between devices with their start and end apart: 16 -> 21, of which waited for: 14 -> 9; matrix products, arithmetic and copies ran while one was open for 4% -> 5% of each run, Pallas kernels for 0% -> 23%
where the time goes in v18:
time: 53.3 us; the launch traced here: 53.2 us
  starting transfers between devices  24.5 us (46%)
  Pallas kernels  12.2 us (23%)
  waiting for transfers between devices  11.6 us (22%)
  other arithmetic  1.56 us (3%)
  local copies, waits for them, and re-layouts  1.2 us (2%)
  matrix products  1.08 us (2%)
  between operations  0.96 us (2%)
    ppermute x20, starting transfers between devices, swap(): return lax.ppermute(block, 'layer', route)  24 us
    pallas_call x2, Pallas kernels, call(): pl.pallas_call(kernel, out_shape=(jax.ShapeDtypeStruct((count, examples),...  12.2 us
    ppermute x20, waiting for transfers between devices, swap(): return lax.ppermute(block, 'layer', route)  11.6 us
    dot_general x1, matrix products, shards(): advantage = jnp.dot(weights, scores, preferred_element_type=jnp.float32)  1.08 us
  transfers between devices with their start and end apart: 21, of which 9 were waited for; matrix products, arithmetic and copies ran while one was open for 5% of the time, Pallas kernels for 23%

profile of v18, /device:TPU:0, one launch (start us, length us, event | category | flops | bytes accessed | tf_op | source)
XLA Modules:
  0.0 53.2 jit_solution(18417485543994095650)
XLA Ops:
  0.6 0.5 collective-permute-start
  1.1 6.9 %shard_map.77 = (f32[256,1024]{1,0:T(8,128)S(1)}, bf16[256,256]{1,0:T(8,128)(2,1)S(1)}, bf16[256,256]{1,0:T(8,128)(2,1)S(1)}) custom-call(bf16[1,256,4096]{2,1,0:T(8,128)(2,1)} %rows_ref.1, bf16[1,32,32]{2,1,0:T(8,128)(2,1)} %left_ref.1, bf16[1,128,128]{2,1,0:T(8,128)(2,1)} %right_ref.1, bf16[1,1024,4096]{2,1,0:T(8,128)(2,1)} %store_ref.3), custom_call_target="tpu_custom_call" | custom-call | flops 4294967296 | bytes 10485760 | tf_op jit(solution)/shard_map/pallas_call | solution.py:176
  8.1 0.1 fusion.7
  8.1 0.7 %dynamic-slice_convert_fusion.2 = (bf16[128,512]{1,0:T(8,128)(2,1)}, bf16[128,512]{1,0:T(8,128)(2,1)}) fusion(f32[256,512]{1,0:T(8,128)S(1)} %get-tuple-element.124, s32[]{:T(128)S(6)} %select_n.146, f32[256,512]{1,0:T(8,128)S(1)} %get-tuple-element.125, s32[]{:T(128)S(6)} %select_n.144), kind=kLoop, calls=%fused_computation.14 | loop fusion | bytes 524296 | tf_op jit(solution)/shard_map/convert_element_type | solution.py:252
  8.9 2.6 %collective-permute-start.1 = (bf16[128,512]{1,0:T(8,128)(2,1)}, bf16[128,512]{1,0:T(8,128)(2,1)}, u32[]{:S(2)}, u32[]{:S(2)}) collective-permute-start(bf16[128,512]{1,0:T(8,128)(2,1)} %get-tuple-element.69), channel_id=1, source_target_pairs={{0,4},{2,6},{4,0},{6,2},{8,12},{10,14},{12,8},{14,10},{1,5},{3,7},... | collective-permute-start | bytes 393224 | tf_op jit(solution)/shard_map/ppermute | solution.py:230
  11.5 1.5 %collective-permute-start.3 = (bf16[128,512]{1,0:T(8,128)(2,1)}, bf16[128,512]{1,0:T(8,128)(2,1)S(1)}, u32[]{:S(2)}, u32[]{:S(2)}) collective-permute-start(bf16[128,512]{1,0:T(8,128)(2,1)} %get-tuple-element.76), channel_id=1, source_target_pairs={{0,2},{2,0},{4,6},{6,4},{8,10},{10,8},{12,14},{14,12},{1,3},{3,1},... | collective-permute-start | bytes 393224 | tf_op jit(solution)/shard_map/ppermute | solution.py:230
  13.1 0.0 collective-permute-done.rows_ref
  13.1 5.3 %shard_map.78 = (f32[256,1024]{1,0:T(8,128)S(1)}, f32[128,512]{1,0:T(8,128)S(1)}, f32[128,512]{1,0:T(8,128)S(1)}) custom-call(bf16[1,256,4096]{2,1,0:T(8,128)(2,1)S(1)} %collective-permute-done.rows_ref, bf16[256,256]{1,0:T(8,128)(2,1)S(1)} %get-tuple-element.66.both_ref, ...), custom_call_target="tpu_custom_call", output_to_operand_aliasing={{1}: (4, {}), {2}: (5, {})} | custom-call | flops 4294967296 | bytes 10485760 | tf_op jit(solution)/shard_map/pallas_call | solution.py:176
  18.4 0.1 fusion.6
  18.5 0.6 %collective-permute-start.7 = (bf16[128,512]{1,0:T(8,128)(2,1)S(1)}, bf16[128,512]{1,0:T(8,128)(2,1)S(1)}, u32[]{:S(2)}, u32[]{:S(2)}) collective-permute-start(bf16[128,512]{1,0:T(8,128)(2,1)S(1)} %dynamic-slice_convert_fusion.1), channel_id=1, source_target_pairs={{0,2},{2,0},{4,6},{6,4},{8,10},{10,8},{12,14},{14,12},{1,3},{3,1},... | collective-permute-start | bytes 393224 | tf_op jit(solution)/shard_map/ppermute | solution.py:230
  19.0 0.0 collective-permute-done.1
  19.0 0.9 %convert_add_fusion.3 = f32[128,512]{1,0:T(8,128)S(1)} fusion(f32[128,512]{1,0:T(8,128)S(1)} %get-tuple-element.68, bf16[128,512]{1,0:T(8,128)(2,1)} %collective-permute-done.1), kind=kLoop, calls=%fused_computation.13 | loop fusion | flops 131072 | bytes 655360 | tf_op jit(solution)/shard_map/add | solution.py:270
  20.0 0.0 collective-permute-done.3
  20.1 0.1 collective-permute-start.4
  20.2 2.1 %collective-permute-start.8 = (bf16[128,512]{1,0:T(8,128)(2,1)S(1)}, bf16[128,512]{1,0:T(8,128)(2,1)S(1)}, u32[]{:S(2)}, u32[]{:S(2)}) collective-permute-start(bf16[128,512]{1,0:T(8,128)(2,1)S(1)} %dynamic-slice_convert_fusion), channel_id=1, source_target_pairs={{0,4},{2,6},{4,0},{6,2},{8,12},{10,14},{12,8},{14,10},{1,5},{3,7},... | collective-permute-start | bytes 393224 | tf_op jit(solution)/shard_map/ppermute | solution.py:230
  22.3 1.5 %collective-permute-start.2 = (bf16[64,512]{1,0:T(8,128)(2,1)S(1)}, bf16[64,512]{1,0:T(8,128)(2,1)S(1)}, u32[]{:S(2)}, u32[]{:S(2)}) collective-permute-start(bf16[64,512]{1,0:T(8,128)(2,1)S(1)} %dynamic-slice_convert_fusion.7), channel_id=1, source_target_pairs={{0,2},{2,0},{4,6},{6,4},{8,10},{10,8},{12,14},{14,12},{1,3},{3,1},... | collective-permute-start | bytes 196616 | tf_op jit(solution)/shard_map/ppermute | solution.py:230
  23.8 1.4 %collective-permute-done.4 = bf16[64,512]{1,0:T(8,128)(2,1)S(1)} collective-permute-done((bf16[64,512]{1,0:T(8,128)(2,1)S(1)}, bf16[64,512]{1,0:T(8,128)(2,1)S(1)}, u32[]{:S(2)}, u32[]{:S(2)}) %collective-permute-start.4) | collective-permute-done | bytes 65568 | tf_op jit(solution)/shard_map/ppermute | solution.py:230
  25.2 2.6 %collective-permute-start.6 = (bf16[64,512]{1,0:T(8,128)(2,1)S(1)}, bf16[64,512]{1,0:T(8,128)(2,1)S(1)}, u32[]{:S(2)}, u32[]{:S(2)}) collective-permute-start(bf16[64,512]{1,0:T(8,128)(2,1)S(1)} %add_convert_fusion.7), channel_id=1, source_target_pairs={{0,8},{2,10},{4,12},{6,14},{8,0},{10,2},{12,4},{14,6},{1,9},{3,11}... | collective-permute-start | bytes 196616 | tf_op jit(solution)/shard_map/ppermute | solution.py:230
  27.8 0.0 collective-permute-done.2
  27.8 1.3 %collective-permute-start.5 = (bf16[64,512]{1,0:T(8,128)(2,1)S(1)}, bf16[64,512]{1,0:T(8,128)(2,1)S(1)}, u32[]{:S(2)}, u32[]{:S(2)}) collective-permute-start(bf16[64,512]{1,0:T(8,128)(2,1)S(1)} %add_convert_fusion.6), channel_id=1, source_target_pairs={{0,8},{2,10},{4,12},{6,14},{8,0},{10,2},{12,4},{14,6},{1,9},{3,11}... | collective-permute-start | bytes 196616 | tf_op jit(solution)/shard_map/ppermute | solution.py:230
  29.2 0.0 collective-permute-done.7
  29.3 0.5 %collective-permute-start.10 = (bf16[64,512]{1,0:T(8,128)(2,1)S(1)}, bf16[64,512]{1,0:T(8,128)(2,1)S(1)}, u32[]{:S(2)}, u32[]{:S(2)}) collective-permute-start(bf16[64,512]{1,0:T(8,128)(2,1)S(1)} %dynamic-slice_convert_fusion.4), channel_id=1, source_target_pairs={{0,4},{2,6},{4,0},{6,2},{8,12},{10,14},{12,8},{14,10},{1,5},{3,7},... | collective-permute-start | bytes 196616 | tf_op jit(solution)/shard_map/ppermute | solution.py:230
  29.8 0.0 collective-permute-done.8
  29.9 1.6 %collective-permute-start.11 = (bf16[64,512]{1,0:T(8,128)(2,1)S(1)}, bf16[64,512]{1,0:T(8,128)(2,1)S(1)}, u32[]{:S(2)}, u32[]{:S(2)}) collective-permute-start(bf16[64,512]{1,0:T(8,128)(2,1)S(1)} %dynamic-slice_convert_fusion.5), channel_id=1, source_target_pairs={{0,2},{2,0},{4,6},{6,4},{8,10},{10,8},{12,14},{14,12},{1,3},{3,1},... | collective-permute-start | bytes 196616 | tf_op jit(solution)/shard_map/ppermute | solution.py:230
  31.4 0.6 %collective-permute-done.6 = bf16[64,512]{1,0:T(8,128)(2,1)S(1)} collective-permute-done((bf16[64,512]{1,0:T(8,128)(2,1)S(1)}, bf16[64,512]{1,0:T(8,128)(2,1)S(1)}, u32[]{:S(2)}, u32[]{:S(2)}) %collective-permute-start.6) | collective-permute-done | bytes 65568 | tf_op jit(solution)/shard_map/ppermute | solution.py:230
  32.0 1.1 %collective-permute-start.9 = (bf16[64,512]{1,0:T(8,128)(2,1)S(1)}, bf16[64,512]{1,0:T(8,128)(2,1)S(1)}, u32[]{:S(2)}, u32[]{:S(2)}) collective-permute-start(bf16[64,512]{1,0:T(8,128)(2,1)S(1)} %add_convert_fusion.5), channel_id=1, source_target_pairs={{0,4},{2,6},{4,0},{6,2},{8,12},{10,14},{12,8},{14,10},{1,5},{3,7},... | collective-permute-start | bytes 196616 | tf_op jit(solution)/shard_map/ppermute | solution.py:230
  33.1 0.6 %collective-permute-done.5 = bf16[64,512]{1,0:T(8,128)(2,1)S(1)} collective-permute-done((bf16[64,512]{1,0:T(8,128)(2,1)S(1)}, bf16[64,512]{1,0:T(8,128)(2,1)S(1)}, u32[]{:S(2)}, u32[]{:S(2)}) %collective-permute-start.5) | collective-permute-done | bytes 65568 | tf_op jit(solution)/shard_map/ppermute | solution.py:230
  33.7 1.6 %collective-permute-start.12 = (bf16[64,512]{1,0:T(8,128)(2,1)S(1)}, bf16[64,512]{1,0:T(8,128)(2,1)S(1)}, u32[]{:S(2)}, u32[]{:S(2)}) collective-permute-start(bf16[64,512]{1,0:T(8,128)(2,1)S(1)} %add_convert_fusion.2), channel_id=1, source_target_pairs={{0,2},{2,0},{4,6},{6,4},{8,10},{10,8},{12,14},{14,12},{1,3},{3,1},... | collective-permute-start | bytes 196616 | tf_op jit(solution)/shard_map/ppermute | solution.py:230
  35.3 0.0 collective-permute-done.10
  35.3 0.8 %collective-permute-start.18 = (bf16[64,512]{1,0:T(8,128)(2,1)S(1)}, bf16[64,512]{1,0:T(8,128)(2,1)S(1)}, u32[]{:S(2)}, u32[]{:S(2)}) collective-permute-start(bf16[64,512]{1,0:T(8,128)(2,1)S(1)} %add_convert_fusion.3), channel_id=1, source_target_pairs={{0,8},{2,10},{4,12},{6,14},{8,0},{10,2},{12,4},{14,6},{1,9},{3,11}... | collective-permute-start | bytes 196616 | tf_op jit(solution)/shard_map/ppermute | solution.py:230
  36.1 0.0 collective-permute-done.11
  36.2 2.2 %collective-permute-start.15 = (bf16[64,512]{1,0:T(8,128)(2,1)S(1)}, bf16[64,512]{1,0:T(8,128)(2,1)S(1)}, u32[]{:S(2)}, u32[]{:S(2)}) collective-permute-start(bf16[64,512]{1,0:T(8,128)(2,1)S(1)} %add_convert_fusion.4), channel_id=1, source_target_pairs={{0,8},{2,10},{4,12},{6,14},{8,0},{10,2},{12,4},{14,6},{1,9},{3,11}... | collective-permute-start | bytes 196616 | tf_op jit(solution)/shard_map/ppermute | solution.py:230
  38.4 0.0 collective-permute-done.9
  38.4 0.6 %collective-permute-start.14 = (bf16[128,512]{1,0:T(8,128)(2,1)S(1)}, bf16[128,512]{1,0:T(8,128)(2,1)S(1)}, u32[]{:S(2)}, u32[]{:S(2)}) collective-permute-start(bf16[128,512]{1,0:T(8,128)(2,1)S(1)} %pad_maximum_fusion.1), channel_id=1, source_target_pairs={{0,2},{2,0},{4,6},{6,4},{8,10},{10,8},{12,14},{14,12},{1,3},{3,1},... | collective-permute-start | bytes 393224 | tf_op jit(solution)/shard_map/ppermute | solution.py:230
  39.0 0.0 collective-permute-done.12
  39.1 0.5 collective-permute-start.13
  39.6 1.7 %collective-permute-done.18 = bf16[64,512]{1,0:T(8,128)(2,1)S(1)} collective-permute-done((bf16[64,512]{1,0:T(8,128)(2,1)S(1)}, bf16[64,512]{1,0:T(8,128)(2,1)S(1)}, u32[]{:S(2)}, u32[]{:S(2)}) %collective-permute-start.18) | collective-permute-done | bytes 65568 | tf_op jit(solution)/shard_map/ppermute | solution.py:230
  41.3 0.3 collective-permute-start.19
  41.6 0.9 %collective-permute-done.15 = bf16[64,512]{1,0:T(8,128)(2,1)S(1)} collective-permute-done((bf16[64,512]{1,0:T(8,128)(2,1)S(1)}, bf16[64,512]{1,0:T(8,128)(2,1)S(1)}, u32[]{:S(2)}, u32[]{:S(2)}) %collective-permute-start.15) | collective-permute-done | bytes 65568 | tf_op jit(solution)/shard_map/ppermute | solution.py:230
  42.5 0.7 %collective-permute-start.16 = (bf16[64,512]{1,0:T(8,128)(2,1)S(1)}, bf16[64,512]{1,0:T(8,128)(2,1)S(1)}, u32[]{:S(2)}, u32[]{:S(2)}) collective-permute-start(bf16[64,512]{1,0:T(8,128)(2,1)S(1)} %add_convert_fusion.1), channel_id=1, source_target_pairs={{0,2},{2,0},{4,6},{6,4},{8,10},{10,8},{12,14},{14,12},{1,3},{3,1},... | collective-permute-start | bytes 196616 | tf_op jit(solution)/shard_map/ppermute | solution.py:230
  43.3 2.3 %collective-permute-done.19 = bf16[64,512]{1,0:T(8,128)(2,1)S(1)} collective-permute-done((bf16[64,512]{1,0:T(8,128)(2,1)S(1)}, bf16[64,512]{1,0:T(8,128)(2,1)S(1)}, u32[]{:S(2)}, u32[]{:S(2)}) %collective-permute-start.19) | collective-permute-done | bytes 65568 | tf_op jit(solution)/shard_map/ppermute | solution.py:230
  45.6 0.8 %collective-permute-start.20 = (bf16[128,512]{1,0:T(8,128)(2,1)S(1)}, bf16[128,512]{1,0:T(8,128)(2,1)S(1)}, u32[]{:S(2)}, u32[]{:S(2)}) collective-permute-start(bf16[128,512]{1,0:T(8,128)(2,1)S(1)} %pad_maximum_fusion.3), channel_id=1, source_target_pairs={{0,2},{2,0},{4,6},{6,4},{8,10},{10,8},{12,14},{14,12},{1,3},{3,1},... | collective-permute-start | bytes 393224 | tf_op jit(solution)/shard_map/ppermute | solution.py:230
  46.4 0.4 collective-permute-done.16
  46.9 0.9 %collective-permute-start.17 = (bf16[128,512]{1,0:T(8,128)(2,1)S(1)}, bf16[128,512]{1,0:T(8,128)(2,1)S(1)}, u32[]{:S(2)}, u32[]{:S(2)}) collective-permute-start(bf16[128,512]{1,0:T(8,128)(2,1)S(1)} %pad_maximum_fusion.2), channel_id=1, source_target_pairs={{0,4},{2,6},{4,0},{6,2},{8,12},{10,14},{12,8},{14,10},{1,5},{3,7},... | collective-permute-start | bytes 393224 | tf_op jit(solution)/shard_map/ppermute | solution.py:230
  47.8 0.0 collective-permute-done.14
  47.9 0.0 collective-permute-done.13
  47.9 0.0 copy-start.1
  48.0 0.0 copy-start.2
  48.0 0.1 broadcast_in_dim.2
  48.2 2.5 %collective-permute-done.20 = bf16[128,512]{1,0:T(8,128)(2,1)S(1)} collective-permute-done((bf16[128,512]{1,0:T(8,128)(2,1)S(1)}, bf16[128,512]{1,0:T(8,128)(2,1)S(1)}, u32[]{:S(2)}, u32[]{:S(2)}) %collective-permute-start.20) | collective-permute-done | bytes 131104 | tf_op jit(solution)/shard_map/ppermute | solution.py:230
  50.7 1.2 %collective-permute-done.17 = bf16[128,512]{1,0:T(8,128)(2,1)S(1)} collective-permute-done((bf16[128,512]{1,0:T(8,128)(2,1)S(1)}, bf16[128,512]{1,0:T(8,128)(2,1)S(1)}, u32[]{:S(2)}, u32[]{:S(2)}) %collective-permute-start.17) | collective-permute-done | bytes 131104 | tf_op jit(solution)/shard_map/ppermute | solution.py:230
  52.1 0.0 copy-done.1
  52.1 0.0 copy-done.2
  52.1 0.0 copy-start
  52.1 1.1 %convolution_convert_fusion = bf16[128,1024]{1,0:T(8,128)(2,1)} fusion(bf16[512,1024]{1,0:T(8,128)(2,1)S(1)} %maximum_dynamic-update-slice_fusion.3, s32[512]{0:T(512)S(1)} %copy-done.1, s32[128]{0:T(128)S(1)} %copy-done.2), kind=kOutput, calls=%fused_computation | convolution fusion | flops 134742016 | bytes 1313280 | tf_op jit(solution)/shard_map/dot_general | solution.py:364
  53.2 0.0 copy-done
  (34 shorter events, 0.8 us)
Async XLA Ops:
  0.6 12.4 %collective-permute-start = (bf16[1,256,4096]{2,1,0:T(8,128)(2,1)}, bf16[1,256,4096]{2,1,0:T(8,128)(2,1)S(1)}, u32[]{:S(2)}, u32[]{:S(2)}) collective-permute-start(bf16[1,256,4096]{2,1,0:T(8,128)(2,1)} %rows_ref.1), channel_id=1, source_target_pairs={{1,0},{0,1},{3,2},{2,3},{5,4},{4,5},{7,6},{6,7},{9,8},{8,9},{11,10... | collective-permute-start | bytes 6291464 | tf_op jit(solution)/shard_map/ppermute | solution.py:330
  8.9 10.2 %collective-permute-start.1 = (bf16[128,512]{1,0:T(8,128)(2,1)}, bf16[128,512]{1,0:T(8,128)(2,1)}, u32[]{:S(2)}, u32[]{:S(2)}) collective-permute-start(bf16[128,512]{1,0:T(8,128)(2,1)} %get-tuple-element.69), channel_id=1, source_target_pairs={{0,4},{2,6},{4,0},{6,2},{8,12},{10,14},{12,8},{14,10},{1,5},{3,7},... | collective-permute-start | bytes 393224 | tf_op jit(solution)/shard_map/ppermute | solution.py:230
  11.5 8.5 %collective-permute-start.3 = (bf16[128,512]{1,0:T(8,128)(2,1)}, bf16[128,512]{1,0:T(8,128)(2,1)S(1)}, u32[]{:S(2)}, u32[]{:S(2)}) collective-permute-start(bf16[128,512]{1,0:T(8,128)(2,1)} %get-tuple-element.76), channel_id=1, source_target_pairs={{0,2},{2,0},{4,6},{6,4},{8,10},{10,8},{12,14},{14,12},{1,3},{3,1},... | collective-permute-start | bytes 393224 | tf_op jit(solution)/shard_map/ppermute | solution.py:230
  18.5 10.7 %collective-permute-start.7 = (bf16[128,512]{1,0:T(8,128)(2,1)S(1)}, bf16[128,512]{1,0:T(8,128)(2,1)S(1)}, u32[]{:S(2)}, u32[]{:S(2)}) collective-permute-start(bf16[128,512]{1,0:T(8,128)(2,1)S(1)} %dynamic-slice_convert_fusion.1), channel_id=1, source_target_pairs={{0,2},{2,0},{4,6},{6,4},{8,10},{10,8},{12,14},{14,12},{1,3},{3,1},... | collective-permute-start | bytes 393224 | tf_op jit(solution)/shard_map/ppermute | solution.py:230
  20.1 5.1 %collective-permute-start.4 = (bf16[64,512]{1,0:T(8,128)(2,1)S(1)}, bf16[64,512]{1,0:T(8,128)(2,1)S(1)}, u32[]{:S(2)}, u32[]{:S(2)}) collective-permute-start(bf16[64,512]{1,0:T(8,128)(2,1)S(1)} %dynamic-slice_convert_fusion.6), channel_id=1, source_target_pairs={{0,4},{2,6},{4,0},{6,2},{8,12},{10,14},{12,8},{14,10},{1,5},{3,7},... | collective-permute-start | bytes 196616 | tf_op jit(solution)/shard_map/ppermute | solution.py:230
  20.2 9.6 %collective-permute-start.8 = (bf16[128,512]{1,0:T(8,128)(2,1)S(1)}, bf16[128,512]{1,0:T(8,128)(2,1)S(1)}, u32[]{:S(2)}, u32[]{:S(2)}) collective-permute-start(bf16[128,512]{1,0:T(8,128)(2,1)S(1)} %dynamic-slice_convert_fusion), channel_id=1, source_target_pairs={{0,4},{2,6},{4,0},{6,2},{8,12},{10,14},{12,8},{14,10},{1,5},{3,7},... | collective-permute-start | bytes 393224 | tf_op jit(solution)/shard_map/ppermute | solution.py:230
  22.3 5.6 %collective-permute-start.2 = (bf16[64,512]{1,0:T(8,128)(2,1)S(1)}, bf16[64,512]{1,0:T(8,128)(2,1)S(1)}, u32[]{:S(2)}, u32[]{:S(2)}) collective-permute-start(bf16[64,512]{1,0:T(8,128)(2,1)S(1)} %dynamic-slice_convert_fusion.7), channel_id=1, source_target_pairs={{0,2},{2,0},{4,6},{6,4},{8,10},{10,8},{12,14},{14,12},{1,3},{3,1},... | collective-permute-start | bytes 196616 | tf_op jit(solution)/shard_map/ppermute | solution.py:230
  25.2 6.8 %collective-permute-start.6 = (bf16[64,512]{1,0:T(8,128)(2,1)S(1)}, bf16[64,512]{1,0:T(8,128)(2,1)S(1)}, u32[]{:S(2)}, u32[]{:S(2)}) collective-permute-start(bf16[64,512]{1,0:T(8,128)(2,1)S(1)} %add_convert_fusion.7), channel_id=1, source_target_pairs={{0,8},{2,10},{4,12},{6,14},{8,0},{10,2},{12,4},{14,6},{1,9},{3,11}... | collective-permute-start | bytes 196616 | tf_op jit(solution)/shard_map/ppermute | solution.py:230
  27.8 5.9 %collective-permute-start.5 = (bf16[64,512]{1,0:T(8,128)(2,1)S(1)}, bf16[64,512]{1,0:T(8,128)(2,1)S(1)}, u32[]{:S(2)}, u32[]{:S(2)}) collective-permute-start(bf16[64,512]{1,0:T(8,128)(2,1)S(1)} %add_convert_fusion.6), channel_id=1, source_target_pairs={{0,8},{2,10},{4,12},{6,14},{8,0},{10,2},{12,4},{14,6},{1,9},{3,11}... | collective-permute-start | bytes 196616 | tf_op jit(solution)/shard_map/ppermute | solution.py:230
  29.3 6.0 %collective-permute-start.10 = (bf16[64,512]{1,0:T(8,128)(2,1)S(1)}, bf16[64,512]{1,0:T(8,128)(2,1)S(1)}, u32[]{:S(2)}, u32[]{:S(2)}) collective-permute-start(bf16[64,512]{1,0:T(8,128)(2,1)S(1)} %dynamic-slice_convert_fusion.4), channel_id=1, source_target_pairs={{0,4},{2,6},{4,0},{6,2},{8,12},{10,14},{12,8},{14,10},{1,5},{3,7},... | collective-permute-start | bytes 196616 | tf_op jit(solution)/shard_map/ppermute | solution.py:230
  29.9 6.3 %collective-permute-start.11 = (bf16[64,512]{1,0:T(8,128)(2,1)S(1)}, bf16[64,512]{1,0:T(8,128)(2,1)S(1)}, u32[]{:S(2)}, u32[]{:S(2)}) collective-permute-start(bf16[64,512]{1,0:T(8,128)(2,1)S(1)} %dynamic-slice_convert_fusion.5), channel_id=1, source_target_pairs={{0,2},{2,0},{4,6},{6,4},{8,10},{10,8},{12,14},{14,12},{1,3},{3,1},... | collective-permute-start | bytes 196616 | tf_op jit(solution)/shard_map/ppermute | solution.py:230
  32.0 6.4 %collective-permute-start.9 = (bf16[64,512]{1,0:T(8,128)(2,1)S(1)}, bf16[64,512]{1,0:T(8,128)(2,1)S(1)}, u32[]{:S(2)}, u32[]{:S(2)}) collective-permute-start(bf16[64,512]{1,0:T(8,128)(2,1)S(1)} %add_convert_fusion.5), channel_id=1, source_target_pairs={{0,4},{2,6},{4,0},{6,2},{8,12},{10,14},{12,8},{14,10},{1,5},{3,7},... | collective-permute-start | bytes 196616 | tf_op jit(solution)/shard_map/ppermute | solution.py:230
  33.7 5.3 %collective-permute-start.12 = (bf16[64,512]{1,0:T(8,128)(2,1)S(1)}, bf16[64,512]{1,0:T(8,128)(2,1)S(1)}, u32[]{:S(2)}, u32[]{:S(2)}) collective-permute-start(bf16[64,512]{1,0:T(8,128)(2,1)S(1)} %add_convert_fusion.2), channel_id=1, source_target_pairs={{0,2},{2,0},{4,6},{6,4},{8,10},{10,8},{12,14},{14,12},{1,3},{3,1},... | collective-permute-start | bytes 196616 | tf_op jit(solution)/shard_map/ppermute | solution.py:230
  35.3 5.9 %collective-permute-start.18 = (bf16[64,512]{1,0:T(8,128)(2,1)S(1)}, bf16[64,512]{1,0:T(8,128)(2,1)S(1)}, u32[]{:S(2)}, u32[]{:S(2)}) collective-permute-start(bf16[64,512]{1,0:T(8,128)(2,1)S(1)} %add_convert_fusion.3), channel_id=1, source_target_pairs={{0,8},{2,10},{4,12},{6,14},{8,0},{10,2},{12,4},{14,6},{1,9},{3,11}... | collective-permute-start | bytes 196616 | tf_op jit(solution)/shard_map/ppermute | solution.py:230
  36.2 6.4 %collective-permute-start.15 = (bf16[64,512]{1,0:T(8,128)(2,1)S(1)}, bf16[64,512]{1,0:T(8,128)(2,1)S(1)}, u32[]{:S(2)}, u32[]{:S(2)}) collective-permute-start(bf16[64,512]{1,0:T(8,128)(2,1)S(1)} %add_convert_fusion.4), channel_id=1, source_target_pairs={{0,8},{2,10},{4,12},{6,14},{8,0},{10,2},{12,4},{14,6},{1,9},{3,11}... | collective-permute-start | bytes 196616 | tf_op jit(solution)/shard_map/ppermute | solution.py:230
  38.4 9.4 %collective-permute-start.14 = (bf16[128,512]{1,0:T(8,128)(2,1)S(1)}, bf16[128,512]{1,0:T(8,128)(2,1)S(1)}, u32[]{:S(2)}, u32[]{:S(2)}) collective-permute-start(bf16[128,512]{1,0:T(8,128)(2,1)S(1)} %pad_maximum_fusion.1), channel_id=1, source_target_pairs={{0,2},{2,0},{4,6},{6,4},{8,10},{10,8},{12,14},{14,12},{1,3},{3,1},... | collective-permute-start | bytes 393224 | tf_op jit(solution)/shard_map/ppermute | solution.py:230
  39.1 8.8 %collective-permute-start.13 = (bf16[128,512]{1,0:T(8,128)(2,1)S(1)}, bf16[128,512]{1,0:T(8,128)(2,1)S(1)}, u32[]{:S(2)}, u32[]{:S(2)}) collective-permute-start(bf16[128,512]{1,0:T(8,128)(2,1)S(1)} %pad_maximum_fusion), channel_id=1, source_target_pairs={{0,4},{2,6},{4,0},{6,2},{8,12},{10,14},{12,8},{14,10},{1,5},{3,7},... | collective-permute-start | bytes 393224 | tf_op jit(solution)/shard_map/ppermute | solution.py:230
  41.3 4.3 %collective-permute-start.19 = (bf16[64,512]{1,0:T(8,128)(2,1)S(1)}, bf16[64,512]{1,0:T(8,128)(2,1)S(1)}, u32[]{:S(2)}, u32[]{:S(2)}) collective-permute-start(bf16[64,512]{1,0:T(8,128)(2,1)S(1)} %add_convert_fusion), channel_id=1, source_target_pairs={{0,4},{2,6},{4,0},{6,2},{8,12},{10,14},{12,8},{14,10},{1,5},{3,7},... | collective-permute-start | bytes 196616 | tf_op jit(solution)/shard_map/ppermute | solution.py:230
  42.5 4.3 %collective-permute-start.16 = (bf16[64,512]{1,0:T(8,128)(2,1)S(1)}, bf16[64,512]{1,0:T(8,128)(2,1)S(1)}, u32[]{:S(2)}, u32[]{:S(2)}) collective-permute-start(bf16[64,512]{1,0:T(8,128)(2,1)S(1)} %add_convert_fusion.1), channel_id=1, source_target_pairs={{0,2},{2,0},{4,6},{6,4},{8,10},{10,8},{12,14},{14,12},{1,3},{3,1},... | collective-permute-start | bytes 196616 | tf_op jit(solution)/shard_map/ppermute | solution.py:230
  45.6 5.0 %collective-permute-start.20 = (bf16[128,512]{1,0:T(8,128)(2,1)S(1)}, bf16[128,512]{1,0:T(8,128)(2,1)S(1)}, u32[]{:S(2)}, u32[]{:S(2)}) collective-permute-start(bf16[128,512]{1,0:T(8,128)(2,1)S(1)} %pad_maximum_fusion.3), channel_id=1, source_target_pairs={{0,2},{2,0},{4,6},{6,4},{8,10},{10,8},{12,14},{14,12},{1,3},{3,1},... | collective-permute-start | bytes 393224 | tf_op jit(solution)/shard_map/ppermute | solution.py:230
  46.9 5.0 %collective-permute-start.17 = (bf16[128,512]{1,0:T(8,128)(2,1)S(1)}, bf16[128,512]{1,0:T(8,128)(2,1)S(1)}, u32[]{:S(2)}, u32[]{:S(2)}) collective-permute-start(bf16[128,512]{1,0:T(8,128)(2,1)S(1)} %pad_maximum_fusion.2), channel_id=1, source_target_pairs={{0,4},{2,6},{4,0},{6,2},{8,12},{10,14},{12,8},{14,10},{1,5},{3,7},... | collective-permute-start | bytes 393224 | tf_op jit(solution)/shard_map/ppermute | solution.py:230
  47.9 4.1 %copy-start.1 = (s32[512]{0:T(512)S(1)}, s32[512]{0:T(512)}, u32[]{:S(2)}) copy-start(s32[512]{0:T(512)} %param.10) | copy-start | bytes 6148
  48.0 4.1 %copy-start.2 = (s32[128]{0:T(128)S(1)}, s32[128]{0:T(128)}, u32[]{:S(2)}) copy-start(s32[128]{0:T(128)} %param.11) | copy-start | bytes 1540
  52.1 1.1 %copy-start = (bf16[512,1024]{1,0:T(8,128)(2,1)}, bf16[512,1024]{1,0:T(8,128)(2,1)S(1)}, u32[]{:S(2)}) copy-start(bf16[512,1024]{1,0:T(8,128)(2,1)S(1)} %maximum_dynamic-update-slice_fusion.3) | copy-start | bytes 3145732

commit v19 on v17

--- a/solution.py
+++ b/solution.py
@@ -15,8 +15,7 @@
 PAIR = 2 * KOUT
 DEPTH_BLOCK = 512
 COLUMNS = 512
-ORDERS = ((0,), (1, 0))
-LANES = 128
+ORDERS = ((1, 0), (1, 0))
 NEAR_START_US = 1.1
 FAR_START_US = 1.5
 LATENCY_US = 0.5
@@ -162,7 +161,6 @@
 
 VMEM = pl.BlockSpec(memory_space=pltpu.VMEM)
 HBM = pl.BlockSpec(memory_space=pltpu.HBM)
-ANYWHERE = pl.BlockSpec(memory_space=pl.ANY)
 
 
 def in_hbm(array):
@@ -216,7 +214,7 @@
     sems = [pltpu.SemaphoreType.DMA((STORE_COPIES,))]
     return call(
         functools.partial(later_kernel, len(sent)), queries, store, (),
-        [VMEM] * 3 + [HBM] + [ANYWHERE] * len(sent), buffers(queries, store) + sems,
+        [VMEM] * 3 + [HBM] + [VMEM] * len(sent), buffers(queries, store) + sems,
         [queries, both, mixer, in_hbm(store), *sent],
     )[0]
 
@@ -247,9 +245,8 @@
             sent = lax.dynamic_slice_in_dim(self.block, (1 - upper) * rows, rows, 0)
             sent = sent.astype(jnp.bfloat16)
             self.block = lax.dynamic_slice_in_dim(self.block, upper * rows, rows, 0)
-        sent = order.mark(sent)
-        self.token = sent[: 2 * ROWS, :LANES]
-        self.received = swap(sent, bit)
+        self.sent = order.mark(sent)
+        self.received = swap(self.sent, bit)
 
     def bytes_of_move(self):
         size = self.block.size
@@ -297,6 +294,10 @@
         end = begin + chunk.bytes_of_move() / (FAR_BYTES_PER_US if far else NEAR_BYTES_PER_US)
         self.links[bit] = end
         self.arrivals[chunk] = end + (2 * LATENCY_US if far else LATENCY_US)
+
+    def next(self):
+        there = [chunk for chunk, at in self.arrivals.items() if at <= self.now]
+        return there[-1] if there else min(self.arrivals, key=self.arrivals.get)
 
     def take(self, chunk):
         self.now = max(self.now, self.arrivals.pop(chunk))
@@ -326,9 +327,13 @@
         else:
             route = [((i - 1) % ex_count, i) for i in range(ex_count)]
             current = lax.ppermute(current, "ex", route)
-            tokens = [chunk.token for chunk in chunks if chunk.moves]
-            part = order.mark(later_scores(order.after(current), both, mixer, store, tokens))
+            sent = [chunk.sent for chunk in chunks if chunk.moves]
+            part = order.mark(later_scores(order.after(current), both, mixer, store, sent))
             clock.now += KERNEL_US
+            for chunk in chunks:
+                clock.take(chunk)
+                chunk.take(order)
+                send(chunk, order, clock)
         choices = ORDERS[min(step, len(ORDERS) - 1)]
         width = columns // len(choices)
         for number, choice in enumerate(choices):
@@ -338,7 +343,7 @@
             chunks.append(chunk)
             places.append(((position - step) % ex_count * rows, jnp.int32(first)))
     while clock.arrivals:
-        chunk = min(clock.arrivals, key=clock.arrivals.get)
+        chunk = clock.next()
         clock.take(chunk)
         chunk.take(order)
         send(chunk, order, clock)

time: 80.9 us -> 52.4 us (0.65)
  waiting for transfers between devices: 36.1 us -> 12 us
  other arithmetic: 2.56 us -> 0.66 us
  local copies, waits for them, and re-layouts: 2.53 us -> 0.79 us
    ppermute x15 -> x20, waiting for transfers between devices: 36.1 us -> 12 us  [swap(): return lax.ppermute(block, 'layer', route)]
    ppermute x15 -> x20, starting transfers between devices: 25.4 us -> 24 us  [swap(): return lax.ppermute(block, 'layer', route)]
    add x2 -> x4, other arithmetic: 1.08 us -> 0.12 us  [take(): self.block = mine.astype(jnp.float32) + received.astype(jnp.float32)]
    convert_element_type x6 -> x8, other arithmetic: 1.08 us -> 0.14 us  [take(): self.block = self.block.astype(jnp.bfloat16)]
  transfers between devices with their start and end apart: 16 -> 21, of which waited for: 14 -> 9; matrix products, arithmetic and copies ran while one was open for 4% -> 2% of each run, Pallas kernels for 0% -> 23%
where the time goes in v19:
time: 52.4 us; the launch traced here: 52.2 us
  starting transfers between devices  24.6 us (47%)
  Pallas kernels  12.2 us (23%)
  waiting for transfers between devices  12 us (23%)
  matrix products  1.08 us (2%)
  between operations  0.96 us (2%)
  local copies, waits for them, and re-layouts  0.79 us (2%)
  other arithmetic  0.66 us (1%)
    ppermute x20, starting transfers between devices, swap(): return lax.ppermute(block, 'layer', route)  24 us
    pallas_call x2, Pallas kernels, call(): pl.pallas_call(kernel, out_shape=(jax.ShapeDtypeStruct((count, examples),...  12.2 us
    ppermute x20, waiting for transfers between devices, swap(): return lax.ppermute(block, 'layer', route)  12 us
    dot_general x1, matrix products, shards(): advantage = jnp.dot(weights, scores, preferred_element_type=jnp.float32)  1.08 us
  transfers between devices with their start and end apart: 21, of which 9 were waited for; matrix products, arithmetic and copies ran while one was open for 2% of the time, Pallas kernels for 23%

profile of v19, /device:TPU:0, one launch (start us, length us, event | category | flops | bytes accessed | tf_op | source)
XLA Modules:
  0.0 52.2 jit_solution(13250664774651499757)
XLA Ops:
  0.6 0.5 collective-permute-start.1
  1.1 6.9 %shard_map.77 = (f32[256,1024]{1,0:T(8,128)S(1)}, bf16[256,256]{1,0:T(8,128)(2,1)S(1)}, bf16[256,256]{1,0:T(8,128)(2,1)S(1)}) custom-call(bf16[1,256,4096]{2,1,0:T(8,128)(2,1)} %rows_ref.1, bf16[1,32,32]{2,1,0:T(8,128)(2,1)} %left_ref.1, bf16[1,128,128]{2,1,0:T(8,128)(2,1)} %right_ref.1, bf16[1,1024,4096]{2,1,0:T(8,128)(2,1)} %store_ref.3), custom_call_target="tpu_custom_call" | custom-call | flops 4294967296 | bytes 10485760 | tf_op jit(solution)/shard_map/pallas_call | solution.py:173
  8.1 0.1 fusion.7
  8.1 0.0 copy-start.1
  8.2 2.7 %collective-permute-start = (bf16[128,512]{1,0:T(8,128)(2,1)S(1)}, bf16[128,512]{1,0:T(8,128)(2,1)S(1)}, u32[]{:S(2)}, u32[]{:S(2)}) collective-permute-start(bf16[128,512]{1,0:T(8,128)(2,1)S(1)} %get-tuple-element.60.refs_0_), channel_id=1, source_target_pairs={{0,4},{2,6},{4,0},{6,2},{8,12},{10,14},{12,8},{14,10},{1,5},{3,7},... | collective-permute-start | bytes 393224 | tf_op jit(solution)/shard_map/ppermute | solution.py:224
  10.9 0.0 copy-done.1
  10.9 1.5 %collective-permute-start.3 = (bf16[128,512]{1,0:T(8,128)(2,1)S(1)}, bf16[128,512]{1,0:T(8,128)(2,1)S(1)}, u32[]{:S(2)}, u32[]{:S(2)}) collective-permute-start(bf16[128,512]{1,0:T(8,128)(2,1)S(1)} %get-tuple-element.66.refs_1_), channel_id=1, source_target_pairs={{0,2},{2,0},{4,6},{6,4},{8,10},{10,8},{12,14},{14,12},{1,3},{3,1},... | collective-permute-start | bytes 393224 | tf_op jit(solution)/shard_map/ppermute | solution.py:224
  12.4 0.0 collective-permute-done.1.rows_ref
  12.4 5.3 %shard_map.78 = f32[256,1024]{1,0:T(8,128)S(1)} custom-call(bf16[1,256,4096]{2,1,0:T(8,128)(2,1)S(1)} %collective-permute-done.1.rows_ref, bf16[256,256]{1,0:T(8,128)(2,1)S(1)} %get-tuple-element.64.both_ref, bf16[256,256]{1,0:T(8,128)(2,1)S(1)} %get-tuple-element.65.mixer_ref, bf16[1,1024,4096]{2,1,0:T(8,128)(2,1)} %store_ref.3, ...), custom_call_target="tpu_custom_call" | custom-call | flops 4294967296 | bytes 10485760 | tf_op jit(solution)/shard_map/pallas_call | solution.py:173
  17.7 0.0 copy-start.2
  17.7 0.1 fusion.6
  17.8 0.6 %collective-permute-start.7 = (bf16[128,512]{1,0:T(8,128)(2,1)S(1)}, bf16[128,512]{1,0:T(8,128)(2,1)S(1)}, u32[]{:S(2)}, u32[]{:S(2)}) collective-permute-start(bf16[128,512]{1,0:T(8,128)(2,1)S(1)} %dynamic-slice_convert_fusion.1), channel_id=1, source_target_pairs={{0,2},{2,0},{4,6},{6,4},{8,10},{10,8},{12,14},{14,12},{1,3},{3,1},... | collective-permute-start | bytes 393224 | tf_op jit(solution)/shard_map/ppermute | solution.py:224
  18.4 0.0 collective-permute-done
  18.4 0.3 copy-done.2
  18.8 0.0 collective-permute-done.3
  18.9 0.7 %collective-permute-start.4 = (bf16[64,512]{1,0:T(8,128)(2,1)S(1)}, bf16[64,512]{1,0:T(8,128)(2,1)S(1)}, u32[]{:S(2)}, u32[]{:S(2)}) collective-permute-start(bf16[64,512]{1,0:T(8,128)(2,1)S(1)} %dynamic-slice_convert_fusion.6), channel_id=1, source_target_pairs={{0,4},{2,6},{4,0},{6,2},{8,12},{10,14},{12,8},{14,10},{1,5},{3,7},... | collective-permute-start | bytes 196616 | tf_op jit(solution)/shard_map/ppermute | solution.py:224
  19.6 1.4 %collective-permute-start.8 = (bf16[128,512]{1,0:T(8,128)(2,1)S(1)}, bf16[128,512]{1,0:T(8,128)(2,1)S(1)}, u32[]{:S(2)}, u32[]{:S(2)}) collective-permute-start(bf16[128,512]{1,0:T(8,128)(2,1)S(1)} %dynamic-slice_convert_fusion), channel_id=1, source_target_pairs={{0,4},{2,6},{4,0},{6,2},{8,12},{10,14},{12,8},{14,10},{1,5},{3,7},... | collective-permute-start | bytes 393224 | tf_op jit(solution)/shard_map/ppermute | solution.py:224
  21.1 1.2 %collective-permute-start.2 = (bf16[64,512]{1,0:T(8,128)(2,1)S(1)}, bf16[64,512]{1,0:T(8,128)(2,1)S(1)}, u32[]{:S(2)}, u32[]{:S(2)}) collective-permute-start(bf16[64,512]{1,0:T(8,128)(2,1)S(1)} %dynamic-slice_convert_fusion.7), channel_id=1, source_target_pairs={{0,2},{2,0},{4,6},{6,4},{8,10},{10,8},{12,14},{14,12},{1,3},{3,1},... | collective-permute-start | bytes 196616 | tf_op jit(solution)/shard_map/ppermute | solution.py:224
  22.3 1.7 %collective-permute-done.4 = bf16[64,512]{1,0:T(8,128)(2,1)S(1)} collective-permute-done((bf16[64,512]{1,0:T(8,128)(2,1)S(1)}, bf16[64,512]{1,0:T(8,128)(2,1)S(1)}, u32[]{:S(2)}, u32[]{:S(2)}) %collective-permute-start.4) | collective-permute-done | bytes 65568 | tf_op jit(solution)/shard_map/ppermute | solution.py:224
  23.9 2.6 %collective-permute-start.6 = (bf16[64,512]{1,0:T(8,128)(2,1)S(1)}, bf16[64,512]{1,0:T(8,128)(2,1)S(1)}, u32[]{:S(2)}, u32[]{:S(2)}) collective-permute-start(bf16[64,512]{1,0:T(8,128)(2,1)S(1)} %add_convert_fusion.7), channel_id=1, source_target_pairs={{0,8},{2,10},{4,12},{6,14},{8,0},{10,2},{12,4},{14,6},{1,9},{3,11}... | collective-permute-start | bytes 196616 | tf_op jit(solution)/shard_map/ppermute | solution.py:224
  26.6 0.0 collective-permute-done.2
  26.6 1.4 %collective-permute-start.5 = (bf16[64,512]{1,0:T(8,128)(2,1)S(1)}, bf16[64,512]{1,0:T(8,128)(2,1)S(1)}, u32[]{:S(2)}, u32[]{:S(2)}) collective-permute-start(bf16[64,512]{1,0:T(8,128)(2,1)S(1)} %add_convert_fusion.6), channel_id=1, source_target_pairs={{0,8},{2,10},{4,12},{6,14},{8,0},{10,2},{12,4},{14,6},{1,9},{3,11}... | collective-permute-start | bytes 196616 | tf_op jit(solution)/shard_map/ppermute | solution.py:224
  28.0 0.0 collective-permute-done.7
  28.1 0.7 %collective-permute-start.10 = (bf16[64,512]{1,0:T(8,128)(2,1)S(1)}, bf16[64,512]{1,0:T(8,128)(2,1)S(1)}, u32[]{:S(2)}, u32[]{:S(2)}) collective-permute-start(bf16[64,512]{1,0:T(8,128)(2,1)S(1)} %dynamic-slice_convert_fusion.4), channel_id=1, source_target_pairs={{0,4},{2,6},{4,0},{6,2},{8,12},{10,14},{12,8},{14,10},{1,5},{3,7},... | collective-permute-start | bytes 196616 | tf_op jit(solution)/shard_map/ppermute | solution.py:224
  28.8 0.0 collective-permute-done.8
  28.9 1.3 %collective-permute-start.11 = (bf16[64,512]{1,0:T(8,128)(2,1)S(1)}, bf16[64,512]{1,0:T(8,128)(2,1)S(1)}, u32[]{:S(2)}, u32[]{:S(2)}) collective-permute-start(bf16[64,512]{1,0:T(8,128)(2,1)S(1)} %dynamic-slice_convert_fusion.5), channel_id=1, source_target_pairs={{0,2},{2,0},{4,6},{6,4},{8,10},{10,8},{12,14},{14,12},{1,3},{3,1},... | collective-permute-start | bytes 196616 | tf_op jit(solution)/shard_map/ppermute | solution.py:224
  30.1 1.0 %collective-permute-done.6 = bf16[64,512]{1,0:T(8,128)(2,1)S(1)} collective-permute-done((bf16[64,512]{1,0:T(8,128)(2,1)S(1)}, bf16[64,512]{1,0:T(8,128)(2,1)S(1)}, u32[]{:S(2)}, u32[]{:S(2)}) %collective-permute-start.6) | collective-permute-done | bytes 65568 | tf_op jit(solution)/shard_map/ppermute | solution.py:224
  31.1 0.5 collective-permute-start.9
  31.6 1.0 %collective-permute-done.5 = bf16[64,512]{1,0:T(8,128)(2,1)S(1)} collective-permute-done((bf16[64,512]{1,0:T(8,128)(2,1)S(1)}, bf16[64,512]{1,0:T(8,128)(2,1)S(1)}, u32[]{:S(2)}, u32[]{:S(2)}) %collective-permute-start.5) | collective-permute-done | bytes 65568 | tf_op jit(solution)/shard_map/ppermute | solution.py:224
  32.6 1.0 %collective-permute-start.12 = (bf16[64,512]{1,0:T(8,128)(2,1)S(1)}, bf16[64,512]{1,0:T(8,128)(2,1)S(1)}, u32[]{:S(2)}, u32[]{:S(2)}) collective-permute-start(bf16[64,512]{1,0:T(8,128)(2,1)S(1)} %add_convert_fusion.2), channel_id=1, source_target_pairs={{0,2},{2,0},{4,6},{6,4},{8,10},{10,8},{12,14},{14,12},{1,3},{3,1},... | collective-permute-start | bytes 196616 | tf_op jit(solution)/shard_map/ppermute | solution.py:224
  33.6 0.0 collective-permute-done.10
  33.6 1.6 %collective-permute-start.18 = (bf16[64,512]{1,0:T(8,128)(2,1)S(1)}, bf16[64,512]{1,0:T(8,128)(2,1)S(1)}, u32[]{:S(2)}, u32[]{:S(2)}) collective-permute-start(bf16[64,512]{1,0:T(8,128)(2,1)S(1)} %add_convert_fusion.3), channel_id=1, source_target_pairs={{0,8},{2,10},{4,12},{6,14},{8,0},{10,2},{12,4},{14,6},{1,9},{3,11}... | collective-permute-start | bytes 196616 | tf_op jit(solution)/shard_map/ppermute | solution.py:224
  35.2 0.0 collective-permute-done.11
  35.2 1.5 %collective-permute-start.15 = (bf16[64,512]{1,0:T(8,128)(2,1)S(1)}, bf16[64,512]{1,0:T(8,128)(2,1)S(1)}, u32[]{:S(2)}, u32[]{:S(2)}) collective-permute-start(bf16[64,512]{1,0:T(8,128)(2,1)S(1)} %add_convert_fusion.4), channel_id=1, source_target_pairs={{0,8},{2,10},{4,12},{6,14},{8,0},{10,2},{12,4},{14,6},{1,9},{3,11}... | collective-permute-start | bytes 196616 | tf_op jit(solution)/shard_map/ppermute | solution.py:224
  36.7 0.0 collective-permute-done.9
  36.7 1.2 %collective-permute-start.14 = (bf16[128,512]{1,0:T(8,128)(2,1)S(1)}, bf16[128,512]{1,0:T(8,128)(2,1)S(1)}, u32[]{:S(2)}, u32[]{:S(2)}) collective-permute-start(bf16[128,512]{1,0:T(8,128)(2,1)S(1)} %pad_maximum_fusion.1), channel_id=1, source_target_pairs={{0,2},{2,0},{4,6},{6,4},{8,10},{10,8},{12,14},{14,12},{1,3},{3,1},... | collective-permute-start | bytes 393224 | tf_op jit(solution)/shard_map/ppermute | solution.py:224
  37.9 0.0 collective-permute-done.12
  37.9 0.8 %collective-permute-start.13 = (bf16[128,512]{1,0:T(8,128)(2,1)S(1)}, bf16[128,512]{1,0:T(8,128)(2,1)S(1)}, u32[]{:S(2)}, u32[]{:S(2)}) collective-permute-start(bf16[128,512]{1,0:T(8,128)(2,1)S(1)} %pad_maximum_fusion), channel_id=1, source_target_pairs={{0,4},{2,6},{4,0},{6,2},{8,12},{10,14},{12,8},{14,10},{1,5},{3,7},... | collective-permute-start | bytes 393224 | tf_op jit(solution)/shard_map/ppermute | solution.py:224
  38.7 0.7 %collective-permute-done.18 = bf16[64,512]{1,0:T(8,128)(2,1)S(1)} collective-permute-done((bf16[64,512]{1,0:T(8,128)(2,1)S(1)}, bf16[64,512]{1,0:T(8,128)(2,1)S(1)}, u32[]{:S(2)}, u32[]{:S(2)}) %collective-permute-start.18) | collective-permute-done | bytes 65568 | tf_op jit(solution)/shard_map/ppermute | solution.py:224
  39.4 0.9 %collective-permute-start.19 = (bf16[64,512]{1,0:T(8,128)(2,1)S(1)}, bf16[64,512]{1,0:T(8,128)(2,1)S(1)}, u32[]{:S(2)}, u32[]{:S(2)}) collective-permute-start(bf16[64,512]{1,0:T(8,128)(2,1)S(1)} %add_convert_fusion), channel_id=1, source_target_pairs={{0,4},{2,6},{4,0},{6,2},{8,12},{10,14},{12,8},{14,10},{1,5},{3,7},... | collective-permute-start | bytes 196616 | tf_op jit(solution)/shard_map/ppermute | solution.py:224
  40.3 0.6 %collective-permute-done.15 = bf16[64,512]{1,0:T(8,128)(2,1)S(1)} collective-permute-done((bf16[64,512]{1,0:T(8,128)(2,1)S(1)}, bf16[64,512]{1,0:T(8,128)(2,1)S(1)}, u32[]{:S(2)}, u32[]{:S(2)}) %collective-permute-start.15) | collective-permute-done | bytes 65568 | tf_op jit(solution)/shard_map/ppermute | solution.py:224
  41.0 0.8 %collective-permute-start.16 = (bf16[64,512]{1,0:T(8,128)(2,1)S(1)}, bf16[64,512]{1,0:T(8,128)(2,1)S(1)}, u32[]{:S(2)}, u32[]{:S(2)}) collective-permute-start(bf16[64,512]{1,0:T(8,128)(2,1)S(1)} %add_convert_fusion.1), channel_id=1, source_target_pairs={{0,2},{2,0},{4,6},{6,4},{8,10},{10,8},{12,14},{14,12},{1,3},{3,1},... | collective-permute-start | bytes 196616 | tf_op jit(solution)/shard_map/ppermute | solution.py:224
  41.8 2.0 %collective-permute-done.19 = bf16[64,512]{1,0:T(8,128)(2,1)S(1)} collective-permute-done((bf16[64,512]{1,0:T(8,128)(2,1)S(1)}, bf16[64,512]{1,0:T(8,128)(2,1)S(1)}, u32[]{:S(2)}, u32[]{:S(2)}) %collective-permute-start.19) | collective-permute-done | bytes 65568 | tf_op jit(solution)/shard_map/ppermute | solution.py:224
  43.8 1.1 %collective-permute-start.20 = (bf16[128,512]{1,0:T(8,128)(2,1)S(1)}, bf16[128,512]{1,0:T(8,128)(2,1)S(1)}, u32[]{:S(2)}, u32[]{:S(2)}) collective-permute-start(bf16[128,512]{1,0:T(8,128)(2,1)S(1)} %pad_maximum_fusion.3), channel_id=1, source_target_pairs={{0,2},{2,0},{4,6},{6,4},{8,10},{10,8},{12,14},{14,12},{1,3},{3,1},... | collective-permute-start | bytes 393224 | tf_op jit(solution)/shard_map/ppermute | solution.py:224
  44.9 1.0 %collective-permute-done.16 = bf16[64,512]{1,0:T(8,128)(2,1)S(1)} collective-permute-done((bf16[64,512]{1,0:T(8,128)(2,1)S(1)}, bf16[64,512]{1,0:T(8,128)(2,1)S(1)}, u32[]{:S(2)}, u32[]{:S(2)}) %collective-permute-start.16) | collective-permute-done | bytes 65568 | tf_op jit(solution)/shard_map/ppermute | solution.py:224
  46.0 0.6 %collective-permute-start.17 = (bf16[128,512]{1,0:T(8,128)(2,1)S(1)}, bf16[128,512]{1,0:T(8,128)(2,1)S(1)}, u32[]{:S(2)}, u32[]{:S(2)}) collective-permute-start(bf16[128,512]{1,0:T(8,128)(2,1)S(1)} %pad_maximum_fusion.2), channel_id=1, source_target_pairs={{0,4},{2,6},{4,0},{6,2},{8,12},{10,14},{12,8},{14,10},{1,5},{3,7},... | collective-permute-start | bytes 393224 | tf_op jit(solution)/shard_map/ppermute | solution.py:224
  46.6 0.0 collective-permute-done.14
  46.7 0.0 collective-permute-done.13
  46.7 0.0 copy-start.3
  46.7 0.0 copy-start.4
  46.7 0.1 broadcast_in_dim.2
  46.9 1.9 %collective-permute-done.20 = bf16[128,512]{1,0:T(8,128)(2,1)S(1)} collective-permute-done((bf16[128,512]{1,0:T(8,128)(2,1)S(1)}, bf16[128,512]{1,0:T(8,128)(2,1)S(1)}, u32[]{:S(2)}, u32[]{:S(2)}) %collective-permute-start.20) | collective-permute-done | bytes 131104 | tf_op jit(solution)/shard_map/ppermute | solution.py:224
  48.9 2.1 %collective-permute-done.17 = bf16[128,512]{1,0:T(8,128)(2,1)S(1)} collective-permute-done((bf16[128,512]{1,0:T(8,128)(2,1)S(1)}, bf16[128,512]{1,0:T(8,128)(2,1)S(1)}, u32[]{:S(2)}, u32[]{:S(2)}) %collective-permute-start.17) | collective-permute-done | bytes 131104 | tf_op jit(solution)/shard_map/ppermute | solution.py:224
  51.1 0.0 copy-done.3
  51.1 0.0 copy-done.4
  51.1 0.0 copy-start
  51.1 1.1 %convolution_convert_fusion = bf16[128,1024]{1,0:T(8,128)(2,1)} fusion(bf16[512,1024]{1,0:T(8,128)(2,1)S(1)} %maximum_dynamic-update-slice_fusion.3, s32[512]{0:T(512)S(1)} %copy-done.3, s32[128]{0:T(128)S(1)} %copy-done.4), kind=kOutput, calls=%fused_computation | convolution fusion | flops 134742016 | bytes 1313280 | tf_op jit(solution)/shard_map/dot_general | solution.py:359
  52.2 0.0 copy-done
  (35 shorter events, 0.8 us)
Async XLA Ops:
  0.6 11.8 %collective-permute-start.1 = (bf16[1,256,4096]{2,1,0:T(8,128)(2,1)}, bf16[1,256,4096]{2,1,0:T(8,128)(2,1)S(1)}, u32[]{:S(2)}, u32[]{:S(2)}) collective-permute-start(bf16[1,256,4096]{2,1,0:T(8,128)(2,1)} %rows_ref.1), channel_id=1, source_target_pairs={{1,0},{0,1},{3,2},{2,3},{5,4},{4,5},{7,6},{6,7},{9,8},{8,9},{11,10... | collective-permute-start | bytes 6291464 | tf_op jit(solution)/shard_map/ppermute | solution.py:329
  8.1 2.8 %copy-start.1 = (f32[256,512]{1,0:T(8,128)}, f32[256,512]{1,0:T(8,128)S(1)}, u32[]{:S(2)}) copy-start(f32[256,512]{1,0:T(8,128)S(1)} %get-tuple-element.119) | copy-start | bytes 1572868
  8.2 10.2 %collective-permute-start = (bf16[128,512]{1,0:T(8,128)(2,1)S(1)}, bf16[128,512]{1,0:T(8,128)(2,1)S(1)}, u32[]{:S(2)}, u32[]{:S(2)}) collective-permute-start(bf16[128,512]{1,0:T(8,128)(2,1)S(1)} %get-tuple-element.60.refs_0_), channel_id=1, source_target_pairs={{0,4},{2,6},{4,0},{6,2},{8,12},{10,14},{12,8},{14,10},{1,5},{3,7},... | collective-permute-start | bytes 393224 | tf_op jit(solution)/shard_map/ppermute | solution.py:224
  10.9 7.9 %collective-permute-start.3 = (bf16[128,512]{1,0:T(8,128)(2,1)S(1)}, bf16[128,512]{1,0:T(8,128)(2,1)S(1)}, u32[]{:S(2)}, u32[]{:S(2)}) collective-permute-start(bf16[128,512]{1,0:T(8,128)(2,1)S(1)} %get-tuple-element.66.refs_1_), channel_id=1, source_target_pairs={{0,2},{2,0},{4,6},{6,4},{8,10},{10,8},{12,14},{14,12},{1,3},{3,1},... | collective-permute-start | bytes 393224 | tf_op jit(solution)/shard_map/ppermute | solution.py:224
  17.7 1.0 %copy-start.2 = (f32[256,512]{1,0:T(8,128)S(1)}, f32[256,512]{1,0:T(8,128)}, u32[]{:S(2)}) copy-start(f32[256,512]{1,0:T(8,128)} %copy-done.1) | copy-start | bytes 1572868
  17.8 10.2 %collective-permute-start.7 = (bf16[128,512]{1,0:T(8,128)(2,1)S(1)}, bf16[128,512]{1,0:T(8,128)(2,1)S(1)}, u32[]{:S(2)}, u32[]{:S(2)}) collective-permute-start(bf16[128,512]{1,0:T(8,128)(2,1)S(1)} %dynamic-slice_convert_fusion.1), channel_id=1, source_target_pairs={{0,2},{2,0},{4,6},{6,4},{8,10},{10,8},{12,14},{14,12},{1,3},{3,1},... | collective-permute-start | bytes 393224 | tf_op jit(solution)/shard_map/ppermute | solution.py:224
  18.9 5.0 %collective-permute-start.4 = (bf16[64,512]{1,0:T(8,128)(2,1)S(1)}, bf16[64,512]{1,0:T(8,128)(2,1)S(1)}, u32[]{:S(2)}, u32[]{:S(2)}) collective-permute-start(bf16[64,512]{1,0:T(8,128)(2,1)S(1)} %dynamic-slice_convert_fusion.6), channel_id=1, source_target_pairs={{0,4},{2,6},{4,0},{6,2},{8,12},{10,14},{12,8},{14,10},{1,5},{3,7},... | collective-permute-start | bytes 196616 | tf_op jit(solution)/shard_map/ppermute | solution.py:224
  19.6 9.2 %collective-permute-start.8 = (bf16[128,512]{1,0:T(8,128)(2,1)S(1)}, bf16[128,512]{1,0:T(8,128)(2,1)S(1)}, u32[]{:S(2)}, u32[]{:S(2)}) collective-permute-start(bf16[128,512]{1,0:T(8,128)(2,1)S(1)} %dynamic-slice_convert_fusion), channel_id=1, source_target_pairs={{0,4},{2,6},{4,0},{6,2},{8,12},{10,14},{12,8},{14,10},{1,5},{3,7},... | collective-permute-start | bytes 393224 | tf_op jit(solution)/shard_map/ppermute | solution.py:224
  21.1 5.5 %collective-permute-start.2 = (bf16[64,512]{1,0:T(8,128)(2,1)S(1)}, bf16[64,512]{1,0:T(8,128)(2,1)S(1)}, u32[]{:S(2)}, u32[]{:S(2)}) collective-permute-start(bf16[64,512]{1,0:T(8,128)(2,1)S(1)} %dynamic-slice_convert_fusion.7), channel_id=1, source_target_pairs={{0,2},{2,0},{4,6},{6,4},{8,10},{10,8},{12,14},{14,12},{1,3},{3,1},... | collective-permute-start | bytes 196616 | tf_op jit(solution)/shard_map/ppermute | solution.py:224
  23.9 7.2 %collective-permute-start.6 = (bf16[64,512]{1,0:T(8,128)(2,1)S(1)}, bf16[64,512]{1,0:T(8,128)(2,1)S(1)}, u32[]{:S(2)}, u32[]{:S(2)}) collective-permute-start(bf16[64,512]{1,0:T(8,128)(2,1)S(1)} %add_convert_fusion.7), channel_id=1, source_target_pairs={{0,8},{2,10},{4,12},{6,14},{8,0},{10,2},{12,4},{14,6},{1,9},{3,11}... | collective-permute-start | bytes 196616 | tf_op jit(solution)/shard_map/ppermute | solution.py:224
  26.6 5.9 %collective-permute-start.5 = (bf16[64,512]{1,0:T(8,128)(2,1)S(1)}, bf16[64,512]{1,0:T(8,128)(2,1)S(1)}, u32[]{:S(2)}, u32[]{:S(2)}) collective-permute-start(bf16[64,512]{1,0:T(8,128)(2,1)S(1)} %add_convert_fusion.6), channel_id=1, source_target_pairs={{0,8},{2,10},{4,12},{6,14},{8,0},{10,2},{12,4},{14,6},{1,9},{3,11}... | collective-permute-start | bytes 196616 | tf_op jit(solution)/shard_map/ppermute | solution.py:224
  28.1 5.5 %collective-permute-start.10 = (bf16[64,512]{1,0:T(8,128)(2,1)S(1)}, bf16[64,512]{1,0:T(8,128)(2,1)S(1)}, u32[]{:S(2)}, u32[]{:S(2)}) collective-permute-start(bf16[64,512]{1,0:T(8,128)(2,1)S(1)} %dynamic-slice_convert_fusion.4), channel_id=1, source_target_pairs={{0,4},{2,6},{4,0},{6,2},{8,12},{10,14},{12,8},{14,10},{1,5},{3,7},... | collective-permute-start | bytes 196616 | tf_op jit(solution)/shard_map/ppermute | solution.py:224
  28.9 6.3 %collective-permute-start.11 = (bf16[64,512]{1,0:T(8,128)(2,1)S(1)}, bf16[64,512]{1,0:T(8,128)(2,1)S(1)}, u32[]{:S(2)}, u32[]{:S(2)}) collective-permute-start(bf16[64,512]{1,0:T(8,128)(2,1)S(1)} %dynamic-slice_convert_fusion.5), channel_id=1, source_target_pairs={{0,2},{2,0},{4,6},{6,4},{8,10},{10,8},{12,14},{14,12},{1,3},{3,1},... | collective-permute-start | bytes 196616 | tf_op jit(solution)/shard_map/ppermute | solution.py:224
  31.1 5.5 %collective-permute-start.9 = (bf16[64,512]{1,0:T(8,128)(2,1)S(1)}, bf16[64,512]{1,0:T(8,128)(2,1)S(1)}, u32[]{:S(2)}, u32[]{:S(2)}) collective-permute-start(bf16[64,512]{1,0:T(8,128)(2,1)S(1)} %add_convert_fusion.5), channel_id=1, source_target_pairs={{0,4},{2,6},{4,0},{6,2},{8,12},{10,14},{12,8},{14,10},{1,5},{3,7},... | collective-permute-start | bytes 196616 | tf_op jit(solution)/shard_map/ppermute | solution.py:224
  32.6 5.3 %collective-permute-start.12 = (bf16[64,512]{1,0:T(8,128)(2,1)S(1)}, bf16[64,512]{1,0:T(8,128)(2,1)S(1)}, u32[]{:S(2)}, u32[]{:S(2)}) collective-permute-start(bf16[64,512]{1,0:T(8,128)(2,1)S(1)} %add_convert_fusion.2), channel_id=1, source_target_pairs={{0,2},{2,0},{4,6},{6,4},{8,10},{10,8},{12,14},{14,12},{1,3},{3,1},... | collective-permute-start | bytes 196616 | tf_op jit(solution)/shard_map/ppermute | solution.py:224
  33.6 5.8 %collective-permute-start.18 = (bf16[64,512]{1,0:T(8,128)(2,1)S(1)}, bf16[64,512]{1,0:T(8,128)(2,1)S(1)}, u32[]{:S(2)}, u32[]{:S(2)}) collective-permute-start(bf16[64,512]{1,0:T(8,128)(2,1)S(1)} %add_convert_fusion.3), channel_id=1, source_target_pairs={{0,8},{2,10},{4,12},{6,14},{8,0},{10,2},{12,4},{14,6},{1,9},{3,11}... | collective-permute-start | bytes 196616 | tf_op jit(solution)/shard_map/ppermute | solution.py:224
  35.2 5.8 %collective-permute-start.15 = (bf16[64,512]{1,0:T(8,128)(2,1)S(1)}, bf16[64,512]{1,0:T(8,128)(2,1)S(1)}, u32[]{:S(2)}, u32[]{:S(2)}) collective-permute-start(bf16[64,512]{1,0:T(8,128)(2,1)S(1)} %add_convert_fusion.4), channel_id=1, source_target_pairs={{0,8},{2,10},{4,12},{6,14},{8,0},{10,2},{12,4},{14,6},{1,9},{3,11}... | collective-permute-start | bytes 196616 | tf_op jit(solution)/shard_map/ppermute | solution.py:224
  36.7 9.9 %collective-permute-start.14 = (bf16[128,512]{1,0:T(8,128)(2,1)S(1)}, bf16[128,512]{1,0:T(8,128)(2,1)S(1)}, u32[]{:S(2)}, u32[]{:S(2)}) collective-permute-start(bf16[128,512]{1,0:T(8,128)(2,1)S(1)} %pad_maximum_fusion.1), channel_id=1, source_target_pairs={{0,2},{2,0},{4,6},{6,4},{8,10},{10,8},{12,14},{14,12},{1,3},{3,1},... | collective-permute-start | bytes 393224 | tf_op jit(solution)/shard_map/ppermute | solution.py:224
  37.9 8.7 %collective-permute-start.13 = (bf16[128,512]{1,0:T(8,128)(2,1)S(1)}, bf16[128,512]{1,0:T(8,128)(2,1)S(1)}, u32[]{:S(2)}, u32[]{:S(2)}) collective-permute-start(bf16[128,512]{1,0:T(8,128)(2,1)S(1)} %pad_maximum_fusion), channel_id=1, source_target_pairs={{0,4},{2,6},{4,0},{6,2},{8,12},{10,14},{12,8},{14,10},{1,5},{3,7},... | collective-permute-start | bytes 393224 | tf_op jit(solution)/shard_map/ppermute | solution.py:224
  39.4 4.3 %collective-permute-start.19 = (bf16[64,512]{1,0:T(8,128)(2,1)S(1)}, bf16[64,512]{1,0:T(8,128)(2,1)S(1)}, u32[]{:S(2)}, u32[]{:S(2)}) collective-permute-start(bf16[64,512]{1,0:T(8,128)(2,1)S(1)} %add_convert_fusion), channel_id=1, source_target_pairs={{0,4},{2,6},{4,0},{6,2},{8,12},{10,14},{12,8},{14,10},{1,5},{3,7},... | collective-permute-start | bytes 196616 | tf_op jit(solution)/shard_map/ppermute | solution.py:224
  41.0 5.0 %collective-permute-start.16 = (bf16[64,512]{1,0:T(8,128)(2,1)S(1)}, bf16[64,512]{1,0:T(8,128)(2,1)S(1)}, u32[]{:S(2)}, u32[]{:S(2)}) collective-permute-start(bf16[64,512]{1,0:T(8,128)(2,1)S(1)} %add_convert_fusion.1), channel_id=1, source_target_pairs={{0,2},{2,0},{4,6},{6,4},{8,10},{10,8},{12,14},{14,12},{1,3},{3,1},... | collective-permute-start | bytes 196616 | tf_op jit(solution)/shard_map/ppermute | solution.py:224
  43.8 5.0 %collective-permute-start.20 = (bf16[128,512]{1,0:T(8,128)(2,1)S(1)}, bf16[128,512]{1,0:T(8,128)(2,1)S(1)}, u32[]{:S(2)}, u32[]{:S(2)}) collective-permute-start(bf16[128,512]{1,0:T(8,128)(2,1)S(1)} %pad_maximum_fusion.3), channel_id=1, source_target_pairs={{0,2},{2,0},{4,6},{6,4},{8,10},{10,8},{12,14},{14,12},{1,3},{3,1},... | collective-permute-start | bytes 393224 | tf_op jit(solution)/shard_map/ppermute | solution.py:224
  46.0 5.0 %collective-permute-start.17 = (bf16[128,512]{1,0:T(8,128)(2,1)S(1)}, bf16[128,512]{1,0:T(8,128)(2,1)S(1)}, u32[]{:S(2)}, u32[]{:S(2)}) collective-permute-start(bf16[128,512]{1,0:T(8,128)(2,1)S(1)} %pad_maximum_fusion.2), channel_id=1, source_target_pairs={{0,4},{2,6},{4,0},{6,2},{8,12},{10,14},{12,8},{14,10},{1,5},{3,7},... | collective-permute-start | bytes 393224 | tf_op jit(solution)/shard_map/ppermute | solution.py:224
  46.7 4.4 %copy-start.3 = (s32[512]{0:T(512)S(1)}, s32[512]{0:T(512)}, u32[]{:S(2)}) copy-start(s32[512]{0:T(512)} %param.10) | copy-start | bytes 6148
  46.7 4.4 %copy-start.4 = (s32[128]{0:T(128)S(1)}, s32[128]{0:T(128)}, u32[]{:S(2)}) copy-start(s32[128]{0:T(128)} %param.11) | copy-start | bytes 1540
  51.1 1.1 %copy-start = (bf16[512,1024]{1,0:T(8,128)(2,1)}, bf16[512,1024]{1,0:T(8,128)(2,1)S(1)}, u32[]{:S(2)}) copy-start(bf16[512,1024]{1,0:T(8,128)(2,1)S(1)} %maximum_dynamic-update-slice_fusion.3) | copy-start | bytes 3145732

commit v20 on v19

--- a/solution.py
+++ b/solution.py
@@ -13,7 +13,7 @@
 ROWS = 8
 WIDE = KIN * ROWS
 PAIR = 2 * KOUT
-DEPTH_BLOCK = 512
+DEPTH_BLOCK = 2048
 COLUMNS = 512
 ORDERS = ((1, 0), (1, 0))
 NEAR_START_US = 1.1
@@ -80,7 +80,7 @@
             pre_ref[at, i * KOUT : (i + 1) * KOUT] = mixed[i]
         return carry
 
-    lax.fori_loop(0, rows_ref.shape[0] // (2 * ROWS), groups, 0, unroll=4)
+    lax.fori_loop(0, rows_ref.shape[0] // (2 * ROWS), groups, 0, unroll=8)
 
 
 def copy_of(source_ref, target_ref, sems, step):
@@ -319,6 +319,7 @@
     bits = [1 << k for k in range(count.bit_length() - 1)]
     orders = [bits, bits[1:2] + bits[:1] + bits[2:]]
     order, clock = Order(), Clock()
+    weights = lax.optimization_barrier(prompt_weights(query_prompt, winner))
     chunks, places = [], []
     current = queries
     for step in range(ex_count):
@@ -341,23 +342,37 @@
             chunk = LayerSum(part[:, first : first + width], orders[choice], index)
             send(chunk, order, clock)
             chunks.append(chunk)
-            places.append(((position - step) % ex_count * rows, jnp.int32(first)))
+            places.append((step, first))
     while clock.arrivals:
         chunk = clock.next()
         clock.take(chunk)
         chunk.take(order)
         send(chunk, order, clock)
     done = [chunk.block for chunk in chunks]
-    scores = jnp.zeros((rows * ex_count, columns), jnp.bfloat16)
-    for place, block in zip(places, done):
-        scores = lax.dynamic_update_slice(scores, block, place)
-    ids = jnp.arange(scores.shape[0], dtype=jnp.int32)
+    blocks = [
+        jnp.concatenate([block for block, (at, _) in zip(done, places) if at == step], 1)
+        for step in range(ex_count)
+    ]
+    scores = jnp.concatenate(
+        [pick(blocks, (position - core) % ex_count) for core in range(ex_count)], 0
+    )
+    advantage = jnp.dot(weights, scores, preferred_element_type=jnp.float32)
+    return (scores, advantage.astype(jnp.bfloat16))
+
+
+def pick(blocks, step):
+    out = blocks[0]
+    for k, block in enumerate(blocks[1:], 1):
+        out = jnp.where(step == k, block, out)
+    return out
+
+
+def prompt_weights(query_prompt, winner):
+    ids = jnp.arange(query_prompt.shape[0], dtype=jnp.int32)
     prompts = jnp.arange(winner.shape[0], dtype=jnp.int32)
     picks = (winner[:, None] == ids[None, :]).astype(jnp.float32)
     member = (query_prompt[None, :] == prompts[:, None]).astype(jnp.float32)
-    weights = (picks - member / BEST).astype(jnp.bfloat16)
-    advantage = jnp.dot(weights, scores, preferred_element_type=jnp.float32)
-    return (scores, advantage.astype(jnp.bfloat16))
+    return (picks - member / BEST).astype(jnp.bfloat16)
 
 
 def solution(mesh):

time: 52.4 us -> 53.1 us (1.013)
    unnamed x10, local copies, waits for them, and re-layouts: 0.36 us -> 0.97 us
  transfers between devices with their start and end apart: 21 -> 21, of which waited for: 9 -> 8; matrix products, arithmetic and copies ran while one was open for 2% -> 2% of each run, Pallas kernels for 23% -> 22%
where the time goes in v20:
time: 53.1 us; the launch traced here: 52.9 us
  starting transfers between devices  24.5 us (46%)
  waiting for transfers between devices  12.5 us (24%)
  Pallas kernels  11.7 us (22%)
  local copies, waits for them, and re-layouts  1.29 us (2%)
  matrix products  1.04 us (2%)
  other arithmetic  0.96 us (2%)
  between operations  0.96 us (2%)
    ppermute x20, starting transfers between devices, swap(): return lax.ppermute(block, 'layer', route)  23.9 us
    ppermute x20, waiting for transfers between devices, swap(): return lax.ppermute(block, 'layer', route)  12.5 us
    pallas_call x2, Pallas kernels, call(): pl.pallas_call(kernel, out_shape=(jax.ShapeDtypeStruct((count, examples),...  11.7 us
  transfers between devices with their start and end apart: 21, of which 8 were waited for; matrix products, arithmetic and copies ran while one was open for 2% of the time, Pallas kernels for 22%

profile of v20, /device:TPU:0, one launch (start us, length us, event | category | flops | bytes accessed | tf_op | source)
XLA Modules:
  0.0 52.9 jit_solution(16833246799516707004)
XLA Ops:
  0.6 0.5 collective-permute-start
  1.1 6.6 %shard_map.77 = (f32[256,1024]{1,0:T(8,128)S(1)}, bf16[256,256]{1,0:T(8,128)(2,1)S(1)}, bf16[256,256]{1,0:T(8,128)(2,1)S(1)}) custom-call(bf16[1,256,4096]{2,1,0:T(8,128)(2,1)} %rows_ref.1, bf16[1,32,32]{2,1,0:T(8,128)(2,1)} %left_ref.1, bf16[1,128,128]{2,1,0:T(8,128)(2,1)} %right_ref.1, bf16[1,1024,4096]{2,1,0:T(8,128)(2,1)} %store_ref.3), custom_call_target="tpu_custom_call" | custom-call | flops 4294967296 | bytes 10485760 | tf_op jit(solution)/shard_map/pallas_call | solution.py:173
  7.8 0.0 copy-start.3
  7.8 0.0 copy-start.4
  7.8 0.1 fusion.1
  7.9 0.0 copy-start.1
  8.0 2.7 %collective-permute-start.2 = (bf16[128,512]{1,0:T(8,128)(2,1)S(1)}, bf16[128,512]{1,0:T(8,128)(2,1)S(1)}, u32[]{:S(2)}, u32[]{:S(2)}) collective-permute-start(bf16[128,512]{1,0:T(8,128)(2,1)S(1)} %get-tuple-element.65.refs_0_), channel_id=1, source_target_pairs={{0,4},{2,6},{4,0},{6,2},{8,12},{10,14},{12,8},{14,10},{1,5},{3,7},... | collective-permute-start | bytes 393224 | tf_op jit(solution)/shard_map/ppermute | solution.py:224
  10.6 0.0 copy-done.1
  10.6 1.5 %collective-permute-start.1 = (bf16[128,512]{1,0:T(8,128)(2,1)S(1)}, bf16[128,512]{1,0:T(8,128)(2,1)S(1)}, u32[]{:S(2)}, u32[]{:S(2)}) collective-permute-start(bf16[128,512]{1,0:T(8,128)(2,1)S(1)} %get-tuple-element.66.refs_1_), channel_id=1, source_target_pairs={{0,2},{2,0},{4,6},{6,4},{8,10},{10,8},{12,14},{14,12},{1,3},{3,1},... | collective-permute-start | bytes 393224 | tf_op jit(solution)/shard_map/ppermute | solution.py:224
  12.2 0.0 copy-done.3
  12.2 0.0 copy-done.4
  12.2 0.1 subtract_convert_fusion
  12.3 0.0 collective-permute-done.rows_ref
  12.3 5.1 %shard_map.78 = f32[256,1024]{1,0:T(8,128)S(1)} custom-call(bf16[1,256,4096]{2,1,0:T(8,128)(2,1)S(1)} %collective-permute-done.rows_ref, bf16[256,256]{1,0:T(8,128)(2,1)S(1)} %get-tuple-element.63.both_ref, bf16[256,256]{1,0:T(8,128)(2,1)S(1)} %get-tuple-element.64.mixer_ref, bf16[1,1024,4096]{2,1,0:T(8,128)(2,1)} %store_ref.3, ...), custom_call_target="tpu_custom_call" | custom-call | flops 4294967296 | bytes 10485760 | tf_op jit(solution)/shard_map/pallas_call | solution.py:173
  17.4 0.0 copy-start.2
  17.4 0.1 fusion
  17.5 0.0 collective-permute-done.2
  17.5 0.9 %copy-done.2 = f32[256,512]{1,0:T(8,128)S(1)} copy-done((f32[256,512]{1,0:T(8,128)S(1)}, f32[256,512]{1,0:T(8,128)}, u32[]{:S(2)}) %copy-start.2) | copy-done | bytes 524312
  18.5 0.0 collective-permute-done.1
  18.6 0.7 %collective-permute-start.3 = (bf16[128,512]{1,0:T(8,128)(2,1)S(1)}, bf16[128,512]{1,0:T(8,128)(2,1)S(1)}, u32[]{:S(2)}, u32[]{:S(2)}) collective-permute-start(bf16[128,512]{1,0:T(8,128)(2,1)S(1)} %dynamic-slice_convert_fusion.1), channel_id=1, source_target_pairs={{0,4},{2,6},{4,0},{6,2},{8,12},{10,14},{12,8},{14,10},{1,5},{3,7},... | collective-permute-start | bytes 393224 | tf_op jit(solution)/shard_map/ppermute | solution.py:224
  19.3 0.5 collective-permute-start.4
  19.8 1.6 %collective-permute-start.8 = (bf16[128,512]{1,0:T(8,128)(2,1)S(1)}, bf16[128,512]{1,0:T(8,128)(2,1)S(1)}, u32[]{:S(2)}, u32[]{:S(2)}) collective-permute-start(bf16[128,512]{1,0:T(8,128)(2,1)S(1)} %dynamic-slice_convert_fusion), channel_id=1, source_target_pairs={{0,2},{2,0},{4,6},{6,4},{8,10},{10,8},{12,14},{14,12},{1,3},{3,1},... | collective-permute-start | bytes 393224 | tf_op jit(solution)/shard_map/ppermute | solution.py:224
  21.4 1.4 %collective-permute-start.5 = (bf16[64,512]{1,0:T(8,128)(2,1)S(1)}, bf16[64,512]{1,0:T(8,128)(2,1)S(1)}, u32[]{:S(2)}, u32[]{:S(2)}) collective-permute-start(bf16[64,512]{1,0:T(8,128)(2,1)S(1)} %dynamic-slice_convert_fusion.6), channel_id=1, source_target_pairs={{0,4},{2,6},{4,0},{6,2},{8,12},{10,14},{12,8},{14,10},{1,5},{3,7},... | collective-permute-start | bytes 196616 | tf_op jit(solution)/shard_map/ppermute | solution.py:224
  22.8 1.5 %collective-permute-done.4 = bf16[64,512]{1,0:T(8,128)(2,1)S(1)} collective-permute-done((bf16[64,512]{1,0:T(8,128)(2,1)S(1)}, bf16[64,512]{1,0:T(8,128)(2,1)S(1)}, u32[]{:S(2)}, u32[]{:S(2)}) %collective-permute-start.4) | collective-permute-done | bytes 65568 | tf_op jit(solution)/shard_map/ppermute | solution.py:224
  24.3 2.7 %collective-permute-start.16 = (bf16[64,512]{1,0:T(8,128)(2,1)S(1)}, bf16[64,512]{1,0:T(8,128)(2,1)S(1)}, u32[]{:S(2)}, u32[]{:S(2)}) collective-permute-start(bf16[64,512]{1,0:T(8,128)(2,1)S(1)} %add_convert_fusion.6), channel_id=1, source_target_pairs={{0,8},{2,10},{4,12},{6,14},{8,0},{10,2},{12,4},{14,6},{1,9},{3,11}... | collective-permute-start | bytes 196616 | tf_op jit(solution)/shard_map/ppermute | solution.py:224
  27.0 0.0 collective-permute-done.5
  27.0 1.8 %collective-permute-start.7 = (bf16[64,512]{1,0:T(8,128)(2,1)S(1)}, bf16[64,512]{1,0:T(8,128)(2,1)S(1)}, u32[]{:S(2)}, u32[]{:S(2)}) collective-permute-start(bf16[64,512]{1,0:T(8,128)(2,1)S(1)} %add_convert_fusion.7), channel_id=1, source_target_pairs={{0,8},{2,10},{4,12},{6,14},{8,0},{10,2},{12,4},{14,6},{1,9},{3,11}... | collective-permute-start | bytes 196616 | tf_op jit(solution)/shard_map/ppermute | solution.py:224
  28.8 0.0 collective-permute-done.3
  28.9 0.6 %collective-permute-start.6 = (bf16[64,512]{1,0:T(8,128)(2,1)S(1)}, bf16[64,512]{1,0:T(8,128)(2,1)S(1)}, u32[]{:S(2)}, u32[]{:S(2)}) collective-permute-start(bf16[64,512]{1,0:T(8,128)(2,1)S(1)} %dynamic-slice_convert_fusion.5), channel_id=1, source_target_pairs={{0,2},{2,0},{4,6},{6,4},{8,10},{10,8},{12,14},{14,12},{1,3},{3,1},... | collective-permute-start | bytes 196616 | tf_op jit(solution)/shard_map/ppermute | solution.py:224
  29.4 0.0 collective-permute-done.8
  29.5 1.0 %collective-permute-start.12 = (bf16[64,512]{1,0:T(8,128)(2,1)S(1)}, bf16[64,512]{1,0:T(8,128)(2,1)S(1)}, u32[]{:S(2)}, u32[]{:S(2)}) collective-permute-start(bf16[64,512]{1,0:T(8,128)(2,1)S(1)} %dynamic-slice_convert_fusion.4), channel_id=1, source_target_pairs={{0,4},{2,6},{4,0},{6,2},{8,12},{10,14},{12,8},{14,10},{1,5},{3,7},... | collective-permute-start | bytes 196616 | tf_op jit(solution)/shard_map/ppermute | solution.py:224
  30.5 1.0 %collective-permute-done.16 = bf16[64,512]{1,0:T(8,128)(2,1)S(1)} collective-permute-done((bf16[64,512]{1,0:T(8,128)(2,1)S(1)}, bf16[64,512]{1,0:T(8,128)(2,1)S(1)}, u32[]{:S(2)}, u32[]{:S(2)}) %collective-permute-start.16) | collective-permute-done | bytes 65568 | tf_op jit(solution)/shard_map/ppermute | solution.py:224
  31.6 0.5 %collective-permute-start.18 = (bf16[64,512]{1,0:T(8,128)(2,1)S(1)}, bf16[64,512]{1,0:T(8,128)(2,1)S(1)}, u32[]{:S(2)}, u32[]{:S(2)}) collective-permute-start(bf16[64,512]{1,0:T(8,128)(2,1)S(1)} %add_convert_fusion), channel_id=1, source_target_pairs={{0,2},{2,0},{4,6},{6,4},{8,10},{10,8},{12,14},{14,12},{1,3},{3,1},... | collective-permute-start | bytes 196616 | tf_op jit(solution)/shard_map/ppermute | solution.py:224
  32.1 0.2 collective-permute-done.7
  32.3 1.4 %collective-permute-start.17 = (bf16[64,512]{1,0:T(8,128)(2,1)S(1)}, bf16[64,512]{1,0:T(8,128)(2,1)S(1)}, u32[]{:S(2)}, u32[]{:S(2)}) collective-permute-start(bf16[64,512]{1,0:T(8,128)(2,1)S(1)} %add_convert_fusion.5), channel_id=1, source_target_pairs={{0,4},{2,6},{4,0},{6,2},{8,12},{10,14},{12,8},{14,10},{1,5},{3,7},... | collective-permute-start | bytes 196616 | tf_op jit(solution)/shard_map/ppermute | solution.py:224
  33.7 0.0 collective-permute-done.6
  33.7 2.6 %collective-permute-start.9 = (bf16[64,512]{1,0:T(8,128)(2,1)S(1)}, bf16[64,512]{1,0:T(8,128)(2,1)S(1)}, u32[]{:S(2)}, u32[]{:S(2)}) collective-permute-start(bf16[64,512]{1,0:T(8,128)(2,1)S(1)} %add_convert_fusion.4), channel_id=1, source_target_pairs={{0,8},{2,10},{4,12},{6,14},{8,0},{10,2},{12,4},{14,6},{1,9},{3,11}... | collective-permute-start | bytes 196616 | tf_op jit(solution)/shard_map/ppermute | solution.py:224
  36.3 0.0 collective-permute-done.12
  36.4 0.5 collective-permute-start.13
  36.8 0.0 collective-permute-done.18
  36.9 0.8 %collective-permute-start.19 = (bf16[128,512]{1,0:T(8,128)(2,1)S(1)}, bf16[128,512]{1,0:T(8,128)(2,1)S(1)}, u32[]{:S(2)}, u32[]{:S(2)}) collective-permute-start(bf16[128,512]{1,0:T(8,128)(2,1)S(1)} %pad_maximum_fusion.3), channel_id=1, source_target_pairs={{0,4},{2,6},{4,0},{6,2},{8,12},{10,14},{12,8},{14,10},{1,5},{3,7},... | collective-permute-start | bytes 393224 | tf_op jit(solution)/shard_map/ppermute | solution.py:224
  37.6 0.0 collective-permute-done.17
  37.6 2.5 %collective-permute-start.20 = (bf16[128,512]{1,0:T(8,128)(2,1)S(1)}, bf16[128,512]{1,0:T(8,128)(2,1)S(1)}, u32[]{:S(2)}, u32[]{:S(2)}) collective-permute-start(bf16[128,512]{1,0:T(8,128)(2,1)S(1)} %pad_maximum_fusion.4), channel_id=1, source_target_pairs={{0,2},{2,0},{4,6},{6,4},{8,10},{10,8},{12,14},{14,12},{1,3},{3,1},... | collective-permute-start | bytes 393224 | tf_op jit(solution)/shard_map/ppermute | solution.py:224
  40.1 0.0 collective-permute-done.9
  40.1 0.1 collective-permute-start.10
  40.2 1.8 %collective-permute-done.13 = bf16[64,512]{1,0:T(8,128)(2,1)S(1)} collective-permute-done((bf16[64,512]{1,0:T(8,128)(2,1)S(1)}, bf16[64,512]{1,0:T(8,128)(2,1)S(1)}, u32[]{:S(2)}, u32[]{:S(2)}) %collective-permute-start.13) | collective-permute-done | bytes 65568 | tf_op jit(solution)/shard_map/ppermute | solution.py:224
  42.1 0.1 collective-permute-start.14
  42.2 2.3 %collective-permute-done.10 = bf16[64,512]{1,0:T(8,128)(2,1)S(1)} collective-permute-done((bf16[64,512]{1,0:T(8,128)(2,1)S(1)}, bf16[64,512]{1,0:T(8,128)(2,1)S(1)}, u32[]{:S(2)}, u32[]{:S(2)}) %collective-permute-start.10) | collective-permute-done | bytes 65568 | tf_op jit(solution)/shard_map/ppermute | solution.py:224
  44.5 0.3 collective-permute-start.11
  44.8 1.6 %collective-permute-done.14 = bf16[64,512]{1,0:T(8,128)(2,1)S(1)} collective-permute-done((bf16[64,512]{1,0:T(8,128)(2,1)S(1)}, bf16[64,512]{1,0:T(8,128)(2,1)S(1)}, u32[]{:S(2)}, u32[]{:S(2)}) %collective-permute-start.14) | collective-permute-done | bytes 65568 | tf_op jit(solution)/shard_map/ppermute | solution.py:224
  46.4 0.8 %collective-permute-start.15 = (bf16[128,512]{1,0:T(8,128)(2,1)S(1)}, bf16[128,512]{1,0:T(8,128)(2,1)S(1)}, u32[]{:S(2)}, u32[]{:S(2)}) collective-permute-start(bf16[128,512]{1,0:T(8,128)(2,1)S(1)} %pad_maximum_fusion.2), channel_id=1, source_target_pairs={{0,2},{2,0},{4,6},{6,4},{8,10},{10,8},{12,14},{14,12},{1,3},{3,1},... | collective-permute-start | bytes 393224 | tf_op jit(solution)/shard_map/ppermute | solution.py:224
  47.3 0.0 collective-permute-done.19
  47.3 0.0 collective-permute-done.20
  47.4 2.1 %collective-permute-done.11 = bf16[128,512]{1,0:T(8,128)(2,1)S(1)} collective-permute-done((bf16[128,512]{1,0:T(8,128)(2,1)S(1)}, bf16[128,512]{1,0:T(8,128)(2,1)S(1)}, u32[]{:S(2)}, u32[]{:S(2)}) %collective-permute-start.11) | collective-permute-done | bytes 131104 | tf_op jit(solution)/shard_map/ppermute | solution.py:224
  49.6 1.9 %collective-permute-done.15 = bf16[128,512]{1,0:T(8,128)(2,1)S(1)} collective-permute-done((bf16[128,512]{1,0:T(8,128)(2,1)S(1)}, bf16[128,512]{1,0:T(8,128)(2,1)S(1)}, u32[]{:S(2)}, u32[]{:S(2)}) %collective-permute-start.15) | collective-permute-done | bytes 131104 | tf_op jit(solution)/shard_map/ppermute | solution.py:224
  51.5 0.2 broadcast_select_fusion.1
  51.8 0.1 pad_maximum_fusion
  51.8 0.0 copy-start
  51.9 1.0 %convolution_convert_fusion = bf16[128,1024]{1,0:T(8,128)(2,1)} fusion(bf16[128,512]{1,0:T(8,128)(2,1)S(1)} %subtract_convert_fusion, bf16[512,1024]{1,0:T(8,128)(2,1)S(1)} %pad_maximum_fusion), kind=kOutput, calls=%fused_computation | convolution fusion | flops 134348800 | bytes 1441792 | tf_op jit(solution)/shard_map/dot_general | solution.py:359
  52.9 0.0 copy-done
  (31 shorter events, 0.7 us)
Async XLA Ops:
  0.6 11.7 %collective-permute-start = (bf16[1,256,4096]{2,1,0:T(8,128)(2,1)}, bf16[1,256,4096]{2,1,0:T(8,128)(2,1)S(1)}, u32[]{:S(2)}, u32[]{:S(2)}) collective-permute-start(bf16[1,256,4096]{2,1,0:T(8,128)(2,1)} %rows_ref.1), channel_id=1, source_target_pairs={{1,0},{0,1},{3,2},{2,3},{5,4},{4,5},{7,6},{6,7},{9,8},{8,9},{11,10... | collective-permute-start | bytes 6291464 | tf_op jit(solution)/shard_map/ppermute | solution.py:330
  7.8 4.4 %copy-start.3 = (s32[512]{0:T(512)S(1)}, s32[512]{0:T(512)}, u32[]{:S(2)}) copy-start(s32[512]{0:T(512)} %param.10) | copy-start | bytes 6148
  7.8 4.4 %copy-start.4 = (s32[128]{0:T(128)S(1)}, s32[128]{0:T(128)}, u32[]{:S(2)}) copy-start(s32[128]{0:T(128)} %param.11) | copy-start | bytes 1540
  7.9 2.7 %copy-start.1 = (f32[256,512]{1,0:T(8,128)}, f32[256,512]{1,0:T(8,128)S(1)}, u32[]{:S(2)}) copy-start(f32[256,512]{1,0:T(8,128)S(1)} %get-tuple-element.120) | copy-start | bytes 1572868
  8.0 9.5 %collective-permute-start.2 = (bf16[128,512]{1,0:T(8,128)(2,1)S(1)}, bf16[128,512]{1,0:T(8,128)(2,1)S(1)}, u32[]{:S(2)}, u32[]{:S(2)}) collective-permute-start(bf16[128,512]{1,0:T(8,128)(2,1)S(1)} %get-tuple-element.65.refs_0_), channel_id=1, source_target_pairs={{0,4},{2,6},{4,0},{6,2},{8,12},{10,14},{12,8},{14,10},{1,5},{3,7},... | collective-permute-start | bytes 393224 | tf_op jit(solution)/shard_map/ppermute | solution.py:224
  10.6 7.9 %collective-permute-start.1 = (bf16[128,512]{1,0:T(8,128)(2,1)S(1)}, bf16[128,512]{1,0:T(8,128)(2,1)S(1)}, u32[]{:S(2)}, u32[]{:S(2)}) collective-permute-start(bf16[128,512]{1,0:T(8,128)(2,1)S(1)} %get-tuple-element.66.refs_1_), channel_id=1, source_target_pairs={{0,2},{2,0},{4,6},{6,4},{8,10},{10,8},{12,14},{14,12},{1,3},{3,1},... | collective-permute-start | bytes 393224 | tf_op jit(solution)/shard_map/ppermute | solution.py:224
  17.4 1.0 %copy-start.2 = (f32[256,512]{1,0:T(8,128)S(1)}, f32[256,512]{1,0:T(8,128)}, u32[]{:S(2)}) copy-start(f32[256,512]{1,0:T(8,128)} %copy-done.1) | copy-start | bytes 1572868
  18.6 10.2 %collective-permute-start.3 = (bf16[128,512]{1,0:T(8,128)(2,1)S(1)}, bf16[128,512]{1,0:T(8,128)(2,1)S(1)}, u32[]{:S(2)}, u32[]{:S(2)}) collective-permute-start(bf16[128,512]{1,0:T(8,128)(2,1)S(1)} %dynamic-slice_convert_fusion.1), channel_id=1, source_target_pairs={{0,4},{2,6},{4,0},{6,2},{8,12},{10,14},{12,8},{14,10},{1,5},{3,7},... | collective-permute-start | bytes 393224 | tf_op jit(solution)/shard_map/ppermute | solution.py:224
  19.3 5.0 %collective-permute-start.4 = (bf16[64,512]{1,0:T(8,128)(2,1)S(1)}, bf16[64,512]{1,0:T(8,128)(2,1)S(1)}, u32[]{:S(2)}, u32[]{:S(2)}) collective-permute-start(bf16[64,512]{1,0:T(8,128)(2,1)S(1)} %dynamic-slice_convert_fusion.7), channel_id=1, source_target_pairs={{0,2},{2,0},{4,6},{6,4},{8,10},{10,8},{12,14},{14,12},{1,3},{3,1},... | collective-permute-start | bytes 196616 | tf_op jit(solution)/shard_map/ppermute | solution.py:224
  19.8 9.6 %collective-permute-start.8 = (bf16[128,512]{1,0:T(8,128)(2,1)S(1)}, bf16[128,512]{1,0:T(8,128)(2,1)S(1)}, u32[]{:S(2)}, u32[]{:S(2)}) collective-permute-start(bf16[128,512]{1,0:T(8,128)(2,1)S(1)} %dynamic-slice_convert_fusion), channel_id=1, source_target_pairs={{0,2},{2,0},{4,6},{6,4},{8,10},{10,8},{12,14},{14,12},{1,3},{3,1},... | collective-permute-start | bytes 393224 | tf_op jit(solution)/shard_map/ppermute | solution.py:224
  21.4 5.5 %collective-permute-start.5 = (bf16[64,512]{1,0:T(8,128)(2,1)S(1)}, bf16[64,512]{1,0:T(8,128)(2,1)S(1)}, u32[]{:S(2)}, u32[]{:S(2)}) collective-permute-start(bf16[64,512]{1,0:T(8,128)(2,1)S(1)} %dynamic-slice_convert_fusion.6), channel_id=1, source_target_pairs={{0,4},{2,6},{4,0},{6,2},{8,12},{10,14},{12,8},{14,10},{1,5},{3,7},... | collective-permute-start | bytes 196616 | tf_op jit(solution)/shard_map/ppermute | solution.py:224
  24.3 7.2 %collective-permute-start.16 = (bf16[64,512]{1,0:T(8,128)(2,1)S(1)}, bf16[64,512]{1,0:T(8,128)(2,1)S(1)}, u32[]{:S(2)}, u32[]{:S(2)}) collective-permute-start(bf16[64,512]{1,0:T(8,128)(2,1)S(1)} %add_convert_fusion.6), channel_id=1, source_target_pairs={{0,8},{2,10},{4,12},{6,14},{8,0},{10,2},{12,4},{14,6},{1,9},{3,11}... | collective-permute-start | bytes 196616 | tf_op jit(solution)/shard_map/ppermute | solution.py:224
  27.0 5.3 %collective-permute-start.7 = (bf16[64,512]{1,0:T(8,128)(2,1)S(1)}, bf16[64,512]{1,0:T(8,128)(2,1)S(1)}, u32[]{:S(2)}, u32[]{:S(2)}) collective-permute-start(bf16[64,512]{1,0:T(8,128)(2,1)S(1)} %add_convert_fusion.7), channel_id=1, source_target_pairs={{0,8},{2,10},{4,12},{6,14},{8,0},{10,2},{12,4},{14,6},{1,9},{3,11}... | collective-permute-start | bytes 196616 | tf_op jit(solution)/shard_map/ppermute | solution.py:224
  28.9 4.8 %collective-permute-start.6 = (bf16[64,512]{1,0:T(8,128)(2,1)S(1)}, bf16[64,512]{1,0:T(8,128)(2,1)S(1)}, u32[]{:S(2)}, u32[]{:S(2)}) collective-permute-start(bf16[64,512]{1,0:T(8,128)(2,1)S(1)} %dynamic-slice_convert_fusion.5), channel_id=1, source_target_pairs={{0,2},{2,0},{4,6},{6,4},{8,10},{10,8},{12,14},{14,12},{1,3},{3,1},... | collective-permute-start | bytes 196616 | tf_op jit(solution)/shard_map/ppermute | solution.py:224
  29.5 6.8 %collective-permute-start.12 = (bf16[64,512]{1,0:T(8,128)(2,1)S(1)}, bf16[64,512]{1,0:T(8,128)(2,1)S(1)}, u32[]{:S(2)}, u32[]{:S(2)}) collective-permute-start(bf16[64,512]{1,0:T(8,128)(2,1)S(1)} %dynamic-slice_convert_fusion.4), channel_id=1, source_target_pairs={{0,4},{2,6},{4,0},{6,2},{8,12},{10,14},{12,8},{14,10},{1,5},{3,7},... | collective-permute-start | bytes 196616 | tf_op jit(solution)/shard_map/ppermute | solution.py:224
  31.6 5.3 %collective-permute-start.18 = (bf16[64,512]{1,0:T(8,128)(2,1)S(1)}, bf16[64,512]{1,0:T(8,128)(2,1)S(1)}, u32[]{:S(2)}, u32[]{:S(2)}) collective-permute-start(bf16[64,512]{1,0:T(8,128)(2,1)S(1)} %add_convert_fusion), channel_id=1, source_target_pairs={{0,2},{2,0},{4,6},{6,4},{8,10},{10,8},{12,14},{14,12},{1,3},{3,1},... | collective-permute-start | bytes 196616 | tf_op jit(solution)/shard_map/ppermute | solution.py:224
  32.3 5.3 %collective-permute-start.17 = (bf16[64,512]{1,0:T(8,128)(2,1)S(1)}, bf16[64,512]{1,0:T(8,128)(2,1)S(1)}, u32[]{:S(2)}, u32[]{:S(2)}) collective-permute-start(bf16[64,512]{1,0:T(8,128)(2,1)S(1)} %add_convert_fusion.5), channel_id=1, source_target_pairs={{0,4},{2,6},{4,0},{6,2},{8,12},{10,14},{12,8},{14,10},{1,5},{3,7},... | collective-permute-start | bytes 196616 | tf_op jit(solution)/shard_map/ppermute | solution.py:224
  33.7 6.4 %collective-permute-start.9 = (bf16[64,512]{1,0:T(8,128)(2,1)S(1)}, bf16[64,512]{1,0:T(8,128)(2,1)S(1)}, u32[]{:S(2)}, u32[]{:S(2)}) collective-permute-start(bf16[64,512]{1,0:T(8,128)(2,1)S(1)} %add_convert_fusion.4), channel_id=1, source_target_pairs={{0,8},{2,10},{4,12},{6,14},{8,0},{10,2},{12,4},{14,6},{1,9},{3,11}... | collective-permute-start | bytes 196616 | tf_op jit(solution)/shard_map/ppermute | solution.py:224
  36.4 5.7 %collective-permute-start.13 = (bf16[64,512]{1,0:T(8,128)(2,1)S(1)}, bf16[64,512]{1,0:T(8,128)(2,1)S(1)}, u32[]{:S(2)}, u32[]{:S(2)}) collective-permute-start(bf16[64,512]{1,0:T(8,128)(2,1)S(1)} %add_convert_fusion.2), channel_id=1, source_target_pairs={{0,8},{2,10},{4,12},{6,14},{8,0},{10,2},{12,4},{14,6},{1,9},{3,11}... | collective-permute-start | bytes 196616 | tf_op jit(solution)/shard_map/ppermute | solution.py:224
  36.9 10.4 %collective-permute-start.19 = (bf16[128,512]{1,0:T(8,128)(2,1)S(1)}, bf16[128,512]{1,0:T(8,128)(2,1)S(1)}, u32[]{:S(2)}, u32[]{:S(2)}) collective-permute-start(bf16[128,512]{1,0:T(8,128)(2,1)S(1)} %pad_maximum_fusion.3), channel_id=1, source_target_pairs={{0,4},{2,6},{4,0},{6,2},{8,12},{10,14},{12,8},{14,10},{1,5},{3,7},... | collective-permute-start | bytes 393224 | tf_op jit(solution)/shard_map/ppermute | solution.py:224
  37.6 9.7 %collective-permute-start.20 = (bf16[128,512]{1,0:T(8,128)(2,1)S(1)}, bf16[128,512]{1,0:T(8,128)(2,1)S(1)}, u32[]{:S(2)}, u32[]{:S(2)}) collective-permute-start(bf16[128,512]{1,0:T(8,128)(2,1)S(1)} %pad_maximum_fusion.4), channel_id=1, source_target_pairs={{0,2},{2,0},{4,6},{6,4},{8,10},{10,8},{12,14},{14,12},{1,3},{3,1},... | collective-permute-start | bytes 393224 | tf_op jit(solution)/shard_map/ppermute | solution.py:224
  40.1 4.3 %collective-permute-start.10 = (bf16[64,512]{1,0:T(8,128)(2,1)S(1)}, bf16[64,512]{1,0:T(8,128)(2,1)S(1)}, u32[]{:S(2)}, u32[]{:S(2)}) collective-permute-start(bf16[64,512]{1,0:T(8,128)(2,1)S(1)} %add_convert_fusion.3), channel_id=1, source_target_pairs={{0,2},{2,0},{4,6},{6,4},{8,10},{10,8},{12,14},{14,12},{1,3},{3,1},... | collective-permute-start | bytes 196616 | tf_op jit(solution)/shard_map/ppermute | solution.py:224
  42.1 4.3 %collective-permute-start.14 = (bf16[64,512]{1,0:T(8,128)(2,1)S(1)}, bf16[64,512]{1,0:T(8,128)(2,1)S(1)}, u32[]{:S(2)}, u32[]{:S(2)}) collective-permute-start(bf16[64,512]{1,0:T(8,128)(2,1)S(1)} %add_convert_fusion.1), channel_id=1, source_target_pairs={{0,4},{2,6},{4,0},{6,2},{8,12},{10,14},{12,8},{14,10},{1,5},{3,7},... | collective-permute-start | bytes 196616 | tf_op jit(solution)/shard_map/ppermute | solution.py:224
  44.5 5.0 %collective-permute-start.11 = (bf16[128,512]{1,0:T(8,128)(2,1)S(1)}, bf16[128,512]{1,0:T(8,128)(2,1)S(1)}, u32[]{:S(2)}, u32[]{:S(2)}) collective-permute-start(bf16[128,512]{1,0:T(8,128)(2,1)S(1)} %pad_maximum_fusion.1), channel_id=1, source_target_pairs={{0,4},{2,6},{4,0},{6,2},{8,12},{10,14},{12,8},{14,10},{1,5},{3,7},... | collective-permute-start | bytes 393224 | tf_op jit(solution)/shard_map/ppermute | solution.py:224
  46.4 5.0 %collective-permute-start.15 = (bf16[128,512]{1,0:T(8,128)(2,1)S(1)}, bf16[128,512]{1,0:T(8,128)(2,1)S(1)}, u32[]{:S(2)}, u32[]{:S(2)}) collective-permute-start(bf16[128,512]{1,0:T(8,128)(2,1)S(1)} %pad_maximum_fusion.2), channel_id=1, source_target_pairs={{0,2},{2,0},{4,6},{6,4},{8,10},{10,8},{12,14},{14,12},{1,3},{3,1},... | collective-permute-start | bytes 393224 | tf_op jit(solution)/shard_map/ppermute | solution.py:224
  51.8 1.1 %copy-start = (bf16[512,1024]{1,0:T(8,128)(2,1)}, bf16[512,1024]{1,0:T(8,128)(2,1)S(1)}, u32[]{:S(2)}) copy-start(bf16[512,1024]{1,0:T(8,128)(2,1)S(1)} %pad_maximum_fusion) | copy-start | bytes 3145732

commit v21 on v19

--- a/solution.py
+++ b/solution.py
@@ -13,7 +13,7 @@
 ROWS = 8
 WIDE = KIN * ROWS
 PAIR = 2 * KOUT
-DEPTH_BLOCK = 512
+DEPTH_BLOCK = 2048
 COLUMNS = 512
 ORDERS = ((1, 0), (1, 0))
 NEAR_START_US = 1.1
@@ -80,7 +80,7 @@
             pre_ref[at, i * KOUT : (i + 1) * KOUT] = mixed[i]
         return carry
 
-    lax.fori_loop(0, rows_ref.shape[0] // (2 * ROWS), groups, 0, unroll=4)
+    lax.fori_loop(0, rows_ref.shape[0] // (2 * ROWS), groups, 0, unroll=8)
 
 
 def copy_of(source_ref, target_ref, sems, step):
@@ -219,17 +219,26 @@
     )[0]
 
 
-def swap(block, bit):
-    route = [(i, i ^ bit) for i in range(lax.axis_size("layer"))]
-    return lax.ppermute(block, "layer", route)
+def swap(block, bit, cores):
+    ex_count = lax.axis_size("ex")
+    route = [
+        (i * ex_count + core, (i ^ bit) * ex_count + core)
+        for i in range(lax.axis_size("layer"))
+        for core in cores
+    ]
+    return lax.ppermute(block, ("layer", "ex"), route)
+
+
+def hand_over(block, source, target):
+    return lax.ppermute(block, "ex", [(source, target)])
 
 
 HALVE, EXCHANGE, DOUBLE = range(3)
 
 
 class LayerSum:
-    def __init__(self, block, bits, index):
-        self.block, self.index = block, index
+    def __init__(self, block, bits, index, cores):
+        self.block, self.index, self.cores = block, index, cores
         self.moves = [(bit, HALVE) for bit in bits[:-1]]
         self.moves += [(bit, EXCHANGE) for bit in bits[-1:]]
         self.moves += [(bit, DOUBLE) for bit in reversed(bits[:-1])]
@@ -246,11 +255,12 @@
             sent = sent.astype(jnp.bfloat16)
             self.block = lax.dynamic_slice_in_dim(self.block, upper * rows, rows, 0)
         self.sent = order.mark(sent)
-        self.received = swap(self.sent, bit)
+        self.received = swap(self.sent, bit, self.cores)
 
     def bytes_of_move(self):
         size = self.block.size
-        return size if self.moves[0][1] == HALVE else 2 * size
+        size = size if self.moves[0][1] == HALVE else 2 * size
+        return size * len(self.cores) // lax.axis_size("ex")
 
     def take(self, order):
         bit, kind = self.moves.pop(0)
@@ -319,6 +329,7 @@
     bits = [1 << k for k in range(count.bit_length() - 1)]
     orders = [bits, bits[1:2] + bits[:1] + bits[2:]]
     order, clock = Order(), Clock()
+    shared = None
     chunks, places = [], []
     current = queries
     for step in range(ex_count):
@@ -338,16 +349,30 @@
         width = columns // len(choices)
         for number, choice in enumerate(choices):
             first = number * width
-            chunk = LayerSum(part[:, first : first + width], orders[choice], index)
+            block, cores = part[:, first : first + width], range(ex_count)
+            if step == 0 and number == 1 and ex_count == 2:
+                given = hand_over(order.mark(block.astype(jnp.bfloat16)), 0, 1)
+                shared, given_block = len(chunks), block
+                places.append(((position - step) % ex_count * rows, jnp.int32(first)))
+                chunks.append(None)
+                continue
+            chunk = LayerSum(block, orders[choice], index, cores)
             send(chunk, order, clock)
             chunks.append(chunk)
             places.append(((position - step) % ex_count * rows, jnp.int32(first)))
+        if step == 0 and shared is not None:
+            block = jnp.concatenate([given_block, order.mark(given).astype(jnp.float32)], 1)
+            chunks[shared] = LayerSum(block, orders[choices[1]], index, (1,))
+            send(chunks[shared], order, clock)
     while clock.arrivals:
         chunk = clock.next()
         clock.take(chunk)
         chunk.take(order)
         send(chunk, order, clock)
     done = [chunk.block for chunk in chunks]
+    if shared is not None:
+        mine, theirs = jnp.split(done[shared], 2, 1)
+        done[shared] = jnp.where(position == 1, mine, hand_over(theirs, 1, 0))
     scores = jnp.zeros((rows * ex_count, columns), jnp.bfloat16)
     for place, block in zip(places, done):
         scores = lax.dynamic_update_slice(scores, block, place)

time: 52.4 us -> 68.5 us (1.31)
  starting transfers between devices: 24.6 us -> 33.6 us
  waiting for transfers between devices: 12 us -> 16.1 us
  local copies, waits for them, and re-layouts: 0.79 us -> 2.76 us
  other arithmetic: 0.66 us -> 1.91 us
    ppermute x20 -> x22, starting transfers between devices: 24 us -> 33.1 us  [the longest x20 29.8 us: swap(): return lax.ppermute(block, ('layer', 'ex'), route)]
    ppermute x20 -> x22, waiting for transfers between devices: 12 us -> 16.1 us  [the longest x20 11.2 us: swap(): return lax.ppermute(block, ('layer', 'ex'), route)]
    slice x2 -> x3, local copies, waits for them, and re-layouts: 0.15 us -> 1.69 us  [shards(): block, cores = (part[:, first:first + width], range(ex_count))]
    convert_element_type x0 -> x2, other arithmetic: none -> 1.04 us  [the longest x1 0.99 us: send(): sent = sent.astype(jnp.bfloat16)]
  transfers between devices with their start and end apart: 21 -> 23, of which waited for: 9 -> 9; matrix products, arithmetic and copies ran while one was open for 2% -> 5% of each run, Pallas kernels for 23% -> 17%
where the time goes in v21:
time: 68.5 us; the launch traced here: 68.2 us
  starting transfers between devices  33.6 us (49%)
  waiting for transfers between devices  16.1 us (24%)
  Pallas kernels  11.7 us (17%)
  local copies, waits for them, and re-layouts  2.76 us (4%)
  other arithmetic  1.91 us (3%)
  matrix products  1.07 us (2%)
  between operations  1.06 us (2%)
    ppermute x20, starting transfers between devices, swap(): return lax.ppermute(block, ('layer', 'ex'), route)  29.8 us
    pallas_call x2, Pallas kernels, call(): pl.pallas_call(kernel, out_shape=(jax.ShapeDtypeStruct((count, examples),...  11.7 us
    ppermute x20, waiting for transfers between devices, swap(): return lax.ppermute(block, ('layer', 'ex'), route)  11.2 us
    ppermute x2, waiting for transfers between devices, hand_over(): return lax.ppermute(block, 'ex', [(source, target)])  4.95 us
    ppermute x2, starting transfers between devices, hand_over(): return lax.ppermute(block, 'ex', [(source, target)])  3.26 us
    slice x3, local copies, waits for them, and re-layouts, shards(): block, cores = (part[:, first:first + width], range(ex_count))  1.69 us
  transfers between devices with their start and end apart: 23, of which 9 were waited for; matrix products, arithmetic and copies ran while one was open for 5% of the time, Pallas kernels for 17%

profile of v21, /device:TPU:0, one launch (start us, length us, event | category | flops | bytes accessed | tf_op | source)
XLA Modules:
  0.0 68.2 jit_solution(3409191950824852796)
XLA Ops:
  0.6 0.5 collective-permute-start.1
  1.1 6.6 %shard_map.77 = (f32[256,1024]{1,0:T(8,128)S(1)}, bf16[256,256]{1,0:T(8,128)(2,1)S(1)}, bf16[256,256]{1,0:T(8,128)(2,1)S(1)}) custom-call(bf16[1,256,4096]{2,1,0:T(8,128)(2,1)} %rows_ref.1, bf16[1,32,32]{2,1,0:T(8,128)(2,1)} %left_ref.1, bf16[1,128,128]{2,1,0:T(8,128)(2,1)} %right_ref.1, bf16[1,1024,4096]{2,1,0:T(8,128)(2,1)} %store_ref.3), custom_call_target="tpu_custom_call" | custom-call | flops 4294967296 | bytes 10485760 | tf_op jit(solution)/shard_map/pallas_call | solution.py:173
  7.8 0.7 %slice.17 = bf16[256,512]{1,0:T(8,128)(2,1)} slice(f32[256,1024]{1,0:T(8,128)S(1)} %get-tuple-element.63), slice={[0:256], [512:1024]} | slice | bytes 524288 | tf_op jit(solution)/shard_map/slice | solution.py:352
  8.5 0.9 %fusion.14 = (f32[256,512]{1,0:T(8,128)}, f32[256,512]{1,0:T(8,128)S(1)}) fusion(f32[256,1024]{1,0:T(8,128)S(1)} %get-tuple-element.63), kind=kLoop, calls=%fused_computation.67 | loop fusion | bytes 2097152 | tf_op jit(solution)/shard_map/slice | solution.py:352
  9.4 0.8 %copy-done.2 = f32[256,512]{1,0:T(8,128)} copy-done((f32[256,512]{1,0:T(8,128)}, f32[256,512]{1,0:T(8,128)S(1)}, u32[]{:S(2)}) %copy-start.2) | copy-done | bytes 524312
  10.2 2.0 %collective-permute-start.2 = (bf16[256,512]{1,0:T(8,128)(2,1)}, bf16[256,512]{1,0:T(8,128)(2,1)S(1)}, u32[]{:S(2)}, u32[]{:S(2)}) collective-permute-start(bf16[256,512]{1,0:T(8,128)(2,1)} %slice.17), channel_id=1, source_target_pairs={{0,1},{2,3},{4,5},{6,7},{8,9},{10,11},{12,13},{14,15},{16,17},{18,... | collective-permute-start | bytes 786440 | tf_op jit(solution)/shard_map/ppermute | solution.py:233
  12.2 3.1 %collective-permute-start = (bf16[128,512]{1,0:T(8,128)(2,1)S(1)}, bf16[128,512]{1,0:T(8,128)(2,1)S(1)}, u32[]{:S(2)}, u32[]{:S(2)}) collective-permute-start(bf16[128,512]{1,0:T(8,128)(2,1)S(1)} %dynamic-slice_convert_fusion.3.refs_0_), channel_id=1, source_target_pairs={{0,4},{1,5},{2,6},{3,7},{4,0},{5,1},{6,2},{7,3},{8,12},{9,13},{10,... | collective-permute-start | bytes 393224 | tf_op jit(solution)/shard_map/ppermute | solution.py:229
  15.3 0.0 collective-permute-done.2
  15.3 0.1 convert_element_type.114
  15.3 1.0 %fusion.3.refs_1_ = bf16[128,1024]{1,0:T(8,128)(2,1)S(1)} fusion(s32[]{:T(128)S(6)} %select_n.163, f32[256,512]{1,0:T(8,128)} %get-tuple-element.126, f32[256,512]{1,0:T(8,128)S(1)} %convert_element_type.114), kind=kLoop, calls=%fused_computation.8 | loop fusion | flops 524288 | bytes 1310724 | tf_op jit(solution)/shard_map/convert_element_type | solution.py:255
  16.3 0.7 collective-permute-start.4
  17.0 0.0 collective-permute-done.1.rows_ref
  17.0 5.1 %shard_map.78 = f32[256,1024]{1,0:T(8,128)S(1)} custom-call(bf16[1,256,4096]{2,1,0:T(8,128)(2,1)S(1)} %collective-permute-done.1.rows_ref, bf16[256,256]{1,0:T(8,128)(2,1)S(1)} %get-tuple-element.72.both_ref, bf16[256,256]{1,0:T(8,128)(2,1)S(1)} %get-tuple-element.73.mixer_ref, bf16[1,1024,4096]{2,1,0:T(8,128)(2,1)} %store_ref.3, ...), custom_call_target="tpu_custom_call" | custom-call | flops 4294967296 | bytes 10485760 | tf_op jit(solution)/shard_map/pallas_call | solution.py:173
  22.1 0.0 copy-start
  22.1 0.1 fusion.13
  22.2 1.6 %collective-permute-start.8 = (bf16[128,512]{1,0:T(8,128)(2,1)S(1)}, bf16[128,512]{1,0:T(8,128)(2,1)S(1)}, u32[]{:S(2)}, u32[]{:S(2)}) collective-permute-start(bf16[128,512]{1,0:T(8,128)(2,1)S(1)} %dynamic-slice_convert_fusion.1), channel_id=1, source_target_pairs={{0,2},{1,3},{2,0},{3,1},{4,6},{5,7},{6,4},{7,5},{8,10},{9,11},{10,... | collective-permute-start | bytes 393224 | tf_op jit(solution)/shard_map/ppermute | solution.py:229
  23.8 0.0 collective-permute-done
  23.9 0.0 collective-permute-done.4
  23.9 0.0 copy-done
  23.9 0.1 fusion.1
  24.0 1.0 %collective-permute-start.3 = (bf16[64,512]{1,0:T(8,128)(2,1)S(1)}, bf16[64,512]{1,0:T(8,128)(2,1)S(1)}, u32[]{:S(2)}, u32[]{:S(2)}) collective-permute-start(bf16[64,512]{1,0:T(8,128)(2,1)S(1)} %dynamic-slice_convert_fusion.6), channel_id=1, source_target_pairs={{0,2},{1,3},{2,0},{3,1},{4,6},{5,7},{6,4},{7,5},{8,10},{9,11},{10,... | collective-permute-start | bytes 196616 | tf_op jit(solution)/shard_map/ppermute | solution.py:229
  25.0 1.3 %collective-permute-start.9 = (bf16[128,512]{1,0:T(8,128)(2,1)S(1)}, bf16[128,512]{1,0:T(8,128)(2,1)S(1)}, u32[]{:S(2)}, u32[]{:S(2)}) collective-permute-start(bf16[128,512]{1,0:T(8,128)(2,1)S(1)} %dynamic-slice_convert_fusion), channel_id=1, source_target_pairs={{0,4},{1,5},{2,6},{3,7},{4,0},{5,1},{6,2},{7,3},{8,12},{9,13},{10,... | collective-permute-start | bytes 393224 | tf_op jit(solution)/shard_map/ppermute | solution.py:229
  26.3 0.7 collective-permute-start.5
  27.0 2.0 %collective-permute-done.3 = bf16[64,512]{1,0:T(8,128)(2,1)S(1)} collective-permute-done((bf16[64,512]{1,0:T(8,128)(2,1)S(1)}, bf16[64,512]{1,0:T(8,128)(2,1)S(1)}, u32[]{:S(2)}, u32[]{:S(2)}) %collective-permute-start.3) | collective-permute-done | bytes 65568 | tf_op jit(solution)/shard_map/ppermute | solution.py:229
  29.0 0.0 collective-permute-done.8
  29.1 1.2 %collective-permute-start.11 = (bf16[64,512]{1,0:T(8,128)(2,1)S(1)}, bf16[64,512]{1,0:T(8,128)(2,1)S(1)}, u32[]{:S(2)}, u32[]{:S(2)}) collective-permute-start(bf16[64,512]{1,0:T(8,128)(2,1)S(1)} %dynamic-slice_convert_fusion.4), channel_id=1, source_target_pairs={{0,4},{1,5},{2,6},{3,7},{4,0},{5,1},{6,2},{7,3},{8,12},{9,13},{10,... | collective-permute-start | bytes 196616 | tf_op jit(solution)/shard_map/ppermute | solution.py:229
  30.3 0.5 collective-permute-done.9
  30.9 1.3 %collective-permute-start.12 = (bf16[64,512]{1,0:T(8,128)(2,1)S(1)}, bf16[64,512]{1,0:T(8,128)(2,1)S(1)}, u32[]{:S(2)}, u32[]{:S(2)}) collective-permute-start(bf16[64,512]{1,0:T(8,128)(2,1)S(1)} %dynamic-slice_convert_fusion.5), channel_id=1, source_target_pairs={{0,2},{1,3},{2,0},{3,1},{4,6},{5,7},{6,4},{7,5},{8,10},{9,11},{10,... | collective-permute-start | bytes 196616 | tf_op jit(solution)/shard_map/ppermute | solution.py:229
  32.3 0.0 collective-permute-done.5
  32.3 0.7 collective-permute-start.7
  33.0 1.1 %collective-permute-done.11 = bf16[64,512]{1,0:T(8,128)(2,1)S(1)} collective-permute-done((bf16[64,512]{1,0:T(8,128)(2,1)S(1)}, bf16[64,512]{1,0:T(8,128)(2,1)S(1)}, u32[]{:S(2)}, u32[]{:S(2)}) %collective-permute-start.11) | collective-permute-done | bytes 65568 | tf_op jit(solution)/shard_map/ppermute | solution.py:229
  34.2 2.7 %collective-permute-start.20 = (bf16[64,512]{1,0:T(8,128)(2,1)S(1)}, bf16[64,512]{1,0:T(8,128)(2,1)S(1)}, u32[]{:S(2)}, u32[]{:S(2)}) collective-permute-start(bf16[64,512]{1,0:T(8,128)(2,1)S(1)} %add_convert_fusion.5), channel_id=1, source_target_pairs={{0,8},{1,9},{2,10},{3,11},{4,12},{5,13},{6,14},{7,15},{8,0},{9,1},... | collective-permute-start | bytes 196616 | tf_op jit(solution)/shard_map/ppermute | solution.py:229
  36.8 0.0 collective-permute-done.12
  36.9 1.6 %collective-permute-start.17 = (bf16[64,512]{1,0:T(8,128)(2,1)S(1)}, bf16[64,512]{1,0:T(8,128)(2,1)S(1)}, u32[]{:S(2)}, u32[]{:S(2)}) collective-permute-start(bf16[64,512]{1,0:T(8,128)(2,1)S(1)} %get-tuple-element.122), channel_id=1, source_target_pairs={{0,8},{1,9},{2,10},{3,11},{4,12},{5,13},{6,14},{7,15},{8,0},{9,1},... | collective-permute-start | bytes 196616 | tf_op jit(solution)/shard_map/ppermute | solution.py:229
  38.5 1.3 %collective-permute-start.6 = (bf16[64,512]{1,0:T(8,128)(2,1)S(1)}, bf16[64,512]{1,0:T(8,128)(2,1)S(1)}, u32[]{:S(2)}, u32[]{:S(2)}) collective-permute-start(bf16[64,512]{1,0:T(8,128)(2,1)S(1)} %get-tuple-element.92), channel_id=1, source_target_pairs={{0,8},{1,9},{2,10},{3,11},{4,12},{5,13},{6,14},{7,15},{8,0},{9,1},... | collective-permute-start | bytes 196616 | tf_op jit(solution)/shard_map/ppermute | solution.py:229
  39.8 0.0 collective-permute-done.20
  39.9 5.9 %collective-permute-start.21 = (bf16[64,512]{1,0:T(8,128)(2,1)S(1)}, bf16[64,512]{1,0:T(8,128)(2,1)S(1)}, u32[]{:S(2)}, u32[]{:S(2)}) collective-permute-start(bf16[64,512]{1,0:T(8,128)(2,1)S(1)} %add_convert_fusion.2), channel_id=1, source_target_pairs={{0,4},{1,5},{2,6},{3,7},{4,0},{5,1},{6,2},{7,3},{8,12},{9,13},{10,... | collective-permute-start | bytes 196616 | tf_op jit(solution)/shard_map/ppermute | solution.py:229
  45.7 0.7 collective-permute-done.17
  46.4 2.2 %collective-permute-start.18 = (bf16[64,512]{1,0:T(8,128)(2,1)S(1)}, bf16[64,512]{1,0:T(8,128)(2,1)S(1)}, u32[]{:S(2)}, u32[]{:S(2)}) collective-permute-start(bf16[64,512]{1,0:T(8,128)(2,1)S(1)} %add_convert_fusion.3), channel_id=1, source_target_pairs={{0,2},{1,3},{2,0},{3,1},{4,6},{5,7},{6,4},{7,5},{8,10},{9,11},{10,... | collective-permute-start | bytes 196616 | tf_op jit(solution)/shard_map/ppermute | solution.py:229
  48.7 0.0 collective-permute-done.7
  48.7 0.7 collective-permute-start.10
  49.4 0.0 collective-permute-done.6
  49.4 0.6 collective-permute-start.13
  50.1 0.6 collective-permute-done.21
  50.7 1.5 %collective-permute-start.22 = (bf16[128,512]{1,0:T(8,128)(2,1)S(1)}, bf16[128,512]{1,0:T(8,128)(2,1)S(1)}, u32[]{:S(2)}, u32[]{:S(2)}) collective-permute-start(bf16[128,512]{1,0:T(8,128)(2,1)S(1)} %pad_maximum_fusion.4), channel_id=1, source_target_pairs={{0,2},{1,3},{2,0},{3,1},{4,6},{5,7},{6,4},{7,5},{8,10},{9,11},{10,... | collective-permute-start | bytes 393224 | tf_op jit(solution)/shard_map/ppermute | solution.py:229
  52.2 0.0 collective-permute-done.18
  52.2 0.2 collective-permute-start.19
  52.4 1.3 %collective-permute-done.13 = bf16[64,512]{1,0:T(8,128)(2,1)S(1)} collective-permute-done((bf16[64,512]{1,0:T(8,128)(2,1)S(1)}, bf16[64,512]{1,0:T(8,128)(2,1)S(1)}, u32[]{:S(2)}, u32[]{:S(2)}) %collective-permute-start.13) | collective-permute-done | bytes 65568 | tf_op jit(solution)/shard_map/ppermute | solution.py:229
  53.8 0.8 %collective-permute-start.14 = (bf16[128,512]{1,0:T(8,128)(2,1)S(1)}, bf16[128,512]{1,0:T(8,128)(2,1)S(1)}, u32[]{:S(2)}, u32[]{:S(2)}) collective-permute-start(bf16[128,512]{1,0:T(8,128)(2,1)S(1)} %pad_maximum_fusion.2), channel_id=1, source_target_pairs={{0,4},{1,5},{2,6},{3,7},{4,0},{5,1},{6,2},{7,3},{8,12},{9,13},{10,... | collective-permute-start | bytes 393224 | tf_op jit(solution)/shard_map/ppermute | solution.py:229
  54.6 0.0 collective-permute-done.10
  54.6 0.7 collective-permute-start.15
  55.3 0.4 collective-permute-done.22
  55.7 4.5 %collective-permute-done.14 = bf16[128,512]{1,0:T(8,128)(2,1)S(1)} collective-permute-done((bf16[128,512]{1,0:T(8,128)(2,1)S(1)}, bf16[128,512]{1,0:T(8,128)(2,1)S(1)}, u32[]{:S(2)}, u32[]{:S(2)}) %collective-permute-start.14) | collective-permute-done | bytes 131104 | tf_op jit(solution)/shard_map/ppermute | solution.py:229
  60.3 0.0 collective-permute-done.15
  60.3 0.1 broadcast_select_fusion.1
  60.5 1.3 %collective-permute-start.16 = (bf16[256,512]{1,0:T(8,128)(2,1)S(1)}, bf16[256,512]{1,0:T(8,128)(2,1)S(1)}, u32[]{:S(2)}, u32[]{:S(2)}) collective-permute-start(bf16[256,512]{1,0:T(8,128)(2,1)S(1)} %pad_maximum_fusion), channel_id=1, source_target_pairs={{1,0},{3,2},{5,4},{7,6},{9,8},{11,10},{13,12},{15,14},{17,16},{19,... | collective-permute-start | bytes 786440 | tf_op jit(solution)/shard_map/ppermute | solution.py:233
  61.8 0.0 copy-start.4
  61.8 0.0 copy-start.5
  61.8 0.1 broadcast_in_dim.2
  61.9 0.0 collective-permute-done.19
  62.0 4.9 %collective-permute-done.16 = bf16[256,512]{1,0:T(8,128)(2,1)S(1)} collective-permute-done((bf16[256,512]{1,0:T(8,128)(2,1)S(1)}, bf16[256,512]{1,0:T(8,128)(2,1)S(1)}, u32[]{:S(2)}, u32[]{:S(2)}) %collective-permute-start.16) | collective-permute-done | bytes 262176 | tf_op jit(solution)/shard_map/ppermute | solution.py:233
  67.0 0.1 fusion.6
  67.1 0.0 copy-start.1
  67.1 1.1 %convolution_convert_fusion = bf16[128,1024]{1,0:T(8,128)(2,1)} fusion(bf16[512,1024]{1,0:T(8,128)(2,1)S(1)} %maximum_dynamic-update-slice_fusion.2, s32[512]{0:T(512)S(1)} %copy-done.4, s32[128]{0:T(128)S(1)} %copy-done.5), kind=kOutput, calls=%fused_computation.4 | convolution fusion | flops 134742016 | bytes 1313280 | tf_op jit(solution)/shard_map/dot_general | solution.py:384
  (38 shorter events, 0.8 us)
Async XLA Ops:
  0.6 16.4 %collective-permute-start.1 = (bf16[1,256,4096]{2,1,0:T(8,128)(2,1)}, bf16[1,256,4096]{2,1,0:T(8,128)(2,1)S(1)}, u32[]{:S(2)}, u32[]{:S(2)}) collective-permute-start(bf16[1,256,4096]{2,1,0:T(8,128)(2,1)} %rows_ref.1), channel_id=1, source_target_pairs={{1,0},{0,1},{3,2},{2,3},{5,4},{4,5},{7,6},{6,7},{9,8},{8,9},{11,10... | collective-permute-start | bytes 6291464 | tf_op jit(solution)/shard_map/ppermute | solution.py:340
  9.4 0.8 %copy-start.2 = (f32[256,512]{1,0:T(8,128)}, f32[256,512]{1,0:T(8,128)S(1)}, u32[]{:S(2)}) copy-start(f32[256,512]{1,0:T(8,128)S(1)} %get-tuple-element.127) | copy-start | bytes 1572868
  10.2 5.1 %collective-permute-start.2 = (bf16[256,512]{1,0:T(8,128)(2,1)}, bf16[256,512]{1,0:T(8,128)(2,1)S(1)}, u32[]{:S(2)}, u32[]{:S(2)}) collective-permute-start(bf16[256,512]{1,0:T(8,128)(2,1)} %slice.17), channel_id=1, source_target_pairs={{0,1},{2,3},{4,5},{6,7},{8,9},{10,11},{12,13},{14,15},{16,17},{18,... | collective-permute-start | bytes 786440 | tf_op jit(solution)/shard_map/ppermute | solution.py:233
  12.2 11.6 %collective-permute-start = (bf16[128,512]{1,0:T(8,128)(2,1)S(1)}, bf16[128,512]{1,0:T(8,128)(2,1)S(1)}, u32[]{:S(2)}, u32[]{:S(2)}) collective-permute-start(bf16[128,512]{1,0:T(8,128)(2,1)S(1)} %dynamic-slice_convert_fusion.3.refs_0_), channel_id=1, source_target_pairs={{0,4},{1,5},{2,6},{3,7},{4,0},{5,1},{6,2},{7,3},{8,12},{9,13},{10,... | collective-permute-start | bytes 393224 | tf_op jit(solution)/shard_map/ppermute | solution.py:229
  16.3 7.6 %collective-permute-start.4 = (bf16[128,1024]{1,0:T(8,128)(2,1)S(1)}, bf16[128,1024]{1,0:T(8,128)(2,1)S(1)}, u32[]{:S(2)}, u32[]{:S(2)}) collective-permute-start(bf16[128,1024]{1,0:T(8,128)(2,1)S(1)} %fusion.3.refs_1_), channel_id=1, source_target_pairs={{1,3},{3,1},{5,7},{7,5},{9,11},{11,9},{13,15},{15,13},{17,19},{19,... | collective-permute-start | bytes 786440 | tf_op jit(solution)/shard_map/ppermute | solution.py:229
  22.1 1.7 %copy-start.3 = (f32[256,512]{1,0:T(8,128)S(1)}, f32[256,512]{1,0:T(8,128)}, u32[]{:S(2)}) copy-start(f32[256,512]{1,0:T(8,128)} %copy-done.2) | copy-start | bytes 1572868
  22.1 1.8 %copy-start = (f32[256,512]{1,0:T(8,128)S(1)}, f32[256,512]{1,0:T(8,128)}, u32[]{:S(2)}) copy-start(f32[256,512]{1,0:T(8,128)} %get-tuple-element.126) | copy-start | bytes 1572868
  22.2 6.8 %collective-permute-start.8 = (bf16[128,512]{1,0:T(8,128)(2,1)S(1)}, bf16[128,512]{1,0:T(8,128)(2,1)S(1)}, u32[]{:S(2)}, u32[]{:S(2)}) collective-permute-start(bf16[128,512]{1,0:T(8,128)(2,1)S(1)} %dynamic-slice_convert_fusion.1), channel_id=1, source_target_pairs={{0,2},{1,3},{2,0},{3,1},{4,6},{5,7},{6,4},{7,5},{8,10},{9,11},{10,... | collective-permute-start | bytes 393224 | tf_op jit(solution)/shard_map/ppermute | solution.py:229
  24.0 5.0 %collective-permute-start.3 = (bf16[64,512]{1,0:T(8,128)(2,1)S(1)}, bf16[64,512]{1,0:T(8,128)(2,1)S(1)}, u32[]{:S(2)}, u32[]{:S(2)}) collective-permute-start(bf16[64,512]{1,0:T(8,128)(2,1)S(1)} %dynamic-slice_convert_fusion.6), channel_id=1, source_target_pairs={{0,2},{1,3},{2,0},{3,1},{4,6},{5,7},{6,4},{7,5},{8,10},{9,11},{10,... | collective-permute-start | bytes 196616 | tf_op jit(solution)/shard_map/ppermute | solution.py:229
  25.0 5.9 %collective-permute-start.9 = (bf16[128,512]{1,0:T(8,128)(2,1)S(1)}, bf16[128,512]{1,0:T(8,128)(2,1)S(1)}, u32[]{:S(2)}, u32[]{:S(2)}) collective-permute-start(bf16[128,512]{1,0:T(8,128)(2,1)S(1)} %dynamic-slice_convert_fusion), channel_id=1, source_target_pairs={{0,4},{1,5},{2,6},{3,7},{4,0},{5,1},{6,2},{7,3},{8,12},{9,13},{10,... | collective-permute-start | bytes 393224 | tf_op jit(solution)/shard_map/ppermute | solution.py:229
  26.3 6.0 %collective-permute-start.5 = (bf16[64,1024]{1,0:T(8,128)(2,1)S(1)}, bf16[64,1024]{1,0:T(8,128)(2,1)S(1)}, u32[]{:S(2)}, u32[]{:S(2)}) collective-permute-start(bf16[64,1024]{1,0:T(8,128)(2,1)S(1)} %dynamic-slice_convert_fusion.2), channel_id=1, source_target_pairs={{1,5},{3,7},{5,1},{7,3},{9,13},{11,15},{13,9},{15,11},{17,21},{19,... | collective-permute-start | bytes 393224 | tf_op jit(solution)/shard_map/ppermute | solution.py:229
  29.1 5.0 %collective-permute-start.11 = (bf16[64,512]{1,0:T(8,128)(2,1)S(1)}, bf16[64,512]{1,0:T(8,128)(2,1)S(1)}, u32[]{:S(2)}, u32[]{:S(2)}) collective-permute-start(bf16[64,512]{1,0:T(8,128)(2,1)S(1)} %dynamic-slice_convert_fusion.4), channel_id=1, source_target_pairs={{0,4},{1,5},{2,6},{3,7},{4,0},{5,1},{6,2},{7,3},{8,12},{9,13},{10,... | collective-permute-start | bytes 196616 | tf_op jit(solution)/shard_map/ppermute | solution.py:229
  30.9 5.9 %collective-permute-start.12 = (bf16[64,512]{1,0:T(8,128)(2,1)S(1)}, bf16[64,512]{1,0:T(8,128)(2,1)S(1)}, u32[]{:S(2)}, u32[]{:S(2)}) collective-permute-start(bf16[64,512]{1,0:T(8,128)(2,1)S(1)} %dynamic-slice_convert_fusion.5), channel_id=1, source_target_pairs={{0,2},{1,3},{2,0},{3,1},{4,6},{5,7},{6,4},{7,5},{8,10},{9,11},{10,... | collective-permute-start | bytes 196616 | tf_op jit(solution)/shard_map/ppermute | solution.py:229
  32.3 16.3 %collective-permute-start.7 = (bf16[64,1024]{1,0:T(8,128)(2,1)S(1)}, bf16[64,1024]{1,0:T(8,128)(2,1)S(1)}, u32[]{:S(2)}, u32[]{:S(2)}) collective-permute-start(bf16[64,1024]{1,0:T(8,128)(2,1)S(1)} %add_convert_fusion.1), channel_id=1, source_target_pairs={{1,9},{3,11},{5,13},{7,15},{9,1},{11,3},{13,5},{15,7},{17,25},{19,... | collective-permute-start | bytes 393224 | tf_op jit(solution)/shard_map/ppermute | solution.py:229
  34.2 5.7 %collective-permute-start.20 = (bf16[64,512]{1,0:T(8,128)(2,1)S(1)}, bf16[64,512]{1,0:T(8,128)(2,1)S(1)}, u32[]{:S(2)}, u32[]{:S(2)}) collective-permute-start(bf16[64,512]{1,0:T(8,128)(2,1)S(1)} %add_convert_fusion.5), channel_id=1, source_target_pairs={{0,8},{1,9},{2,10},{3,11},{4,12},{5,13},{6,14},{7,15},{8,0},{9,1},... | collective-permute-start | bytes 196616 | tf_op jit(solution)/shard_map/ppermute | solution.py:229
  36.9 9.6 %collective-permute-start.17 = (bf16[64,512]{1,0:T(8,128)(2,1)S(1)}, bf16[64,512]{1,0:T(8,128)(2,1)S(1)}, u32[]{:S(2)}, u32[]{:S(2)}) collective-permute-start(bf16[64,512]{1,0:T(8,128)(2,1)S(1)} %get-tuple-element.122), channel_id=1, source_target_pairs={{0,8},{1,9},{2,10},{3,11},{4,12},{5,13},{6,14},{7,15},{8,0},{9,1},... | collective-permute-start | bytes 196616 | tf_op jit(solution)/shard_map/ppermute | solution.py:229
  38.5 10.9 %collective-permute-start.6 = (bf16[64,512]{1,0:T(8,128)(2,1)S(1)}, bf16[64,512]{1,0:T(8,128)(2,1)S(1)}, u32[]{:S(2)}, u32[]{:S(2)}) collective-permute-start(bf16[64,512]{1,0:T(8,128)(2,1)S(1)} %get-tuple-element.92), channel_id=1, source_target_pairs={{0,8},{1,9},{2,10},{3,11},{4,12},{5,13},{6,14},{7,15},{8,0},{9,1},... | collective-permute-start | bytes 196616 | tf_op jit(solution)/shard_map/ppermute | solution.py:229
  39.9 10.7 %collective-permute-start.21 = (bf16[64,512]{1,0:T(8,128)(2,1)S(1)}, bf16[64,512]{1,0:T(8,128)(2,1)S(1)}, u32[]{:S(2)}, u32[]{:S(2)}) collective-permute-start(bf16[64,512]{1,0:T(8,128)(2,1)S(1)} %add_convert_fusion.2), channel_id=1, source_target_pairs={{0,4},{1,5},{2,6},{3,7},{4,0},{5,1},{6,2},{7,3},{8,12},{9,13},{10,... | collective-permute-start | bytes 196616 | tf_op jit(solution)/shard_map/ppermute | solution.py:229
  46.4 5.7 %collective-permute-start.18 = (bf16[64,512]{1,0:T(8,128)(2,1)S(1)}, bf16[64,512]{1,0:T(8,128)(2,1)S(1)}, u32[]{:S(2)}, u32[]{:S(2)}) collective-permute-start(bf16[64,512]{1,0:T(8,128)(2,1)S(1)} %add_convert_fusion.3), channel_id=1, source_target_pairs={{0,2},{1,3},{2,0},{3,1},{4,6},{5,7},{6,4},{7,5},{8,10},{9,11},{10,... | collective-permute-start | bytes 196616 | tf_op jit(solution)/shard_map/ppermute | solution.py:229
  48.7 5.9 %collective-permute-start.10 = (bf16[64,1024]{1,0:T(8,128)(2,1)S(1)}, bf16[64,1024]{1,0:T(8,128)(2,1)S(1)}, u32[]{:S(2)}, u32[]{:S(2)}) collective-permute-start(bf16[64,1024]{1,0:T(8,128)(2,1)S(1)} %add_convert_fusion), channel_id=1, source_target_pairs={{1,5},{3,7},{5,1},{7,3},{9,13},{11,15},{13,9},{15,11},{17,21},{19,... | collective-permute-start | bytes 393224 | tf_op jit(solution)/shard_map/ppermute | solution.py:229
  49.4 4.3 %collective-permute-start.13 = (bf16[64,512]{1,0:T(8,128)(2,1)S(1)}, bf16[64,512]{1,0:T(8,128)(2,1)S(1)}, u32[]{:S(2)}, u32[]{:S(2)}) collective-permute-start(bf16[64,512]{1,0:T(8,128)(2,1)S(1)} %add_convert_fusion.4), channel_id=1, source_target_pairs={{0,2},{1,3},{2,0},{3,1},{4,6},{5,7},{6,4},{7,5},{8,10},{9,11},{10,... | collective-permute-start | bytes 196616 | tf_op jit(solution)/shard_map/ppermute | solution.py:229
  50.7 5.0 %collective-permute-start.22 = (bf16[128,512]{1,0:T(8,128)(2,1)S(1)}, bf16[128,512]{1,0:T(8,128)(2,1)S(1)}, u32[]{:S(2)}, u32[]{:S(2)}) collective-permute-start(bf16[128,512]{1,0:T(8,128)(2,1)S(1)} %pad_maximum_fusion.4), channel_id=1, source_target_pairs={{0,2},{1,3},{2,0},{3,1},{4,6},{5,7},{6,4},{7,5},{8,10},{9,11},{10,... | collective-permute-start | bytes 393224 | tf_op jit(solution)/shard_map/ppermute | solution.py:229
  52.2 9.7 %collective-permute-start.19 = (bf16[128,512]{1,0:T(8,128)(2,1)S(1)}, bf16[128,512]{1,0:T(8,128)(2,1)S(1)}, u32[]{:S(2)}, u32[]{:S(2)}) collective-permute-start(bf16[128,512]{1,0:T(8,128)(2,1)S(1)} %pad_maximum_fusion.3), channel_id=1, source_target_pairs={{0,4},{1,5},{2,6},{3,7},{4,0},{5,1},{6,2},{7,3},{8,12},{9,13},{10,... | collective-permute-start | bytes 393224 | tf_op jit(solution)/shard_map/ppermute | solution.py:229
  53.8 6.5 %collective-permute-start.14 = (bf16[128,512]{1,0:T(8,128)(2,1)S(1)}, bf16[128,512]{1,0:T(8,128)(2,1)S(1)}, u32[]{:S(2)}, u32[]{:S(2)}) collective-permute-start(bf16[128,512]{1,0:T(8,128)(2,1)S(1)} %pad_maximum_fusion.2), channel_id=1, source_target_pairs={{0,4},{1,5},{2,6},{3,7},{4,0},{5,1},{6,2},{7,3},{8,12},{9,13},{10,... | collective-permute-start | bytes 393224 | tf_op jit(solution)/shard_map/ppermute | solution.py:229
  54.6 5.7 %collective-permute-start.15 = (bf16[128,1024]{1,0:T(8,128)(2,1)S(1)}, bf16[128,1024]{1,0:T(8,128)(2,1)S(1)}, u32[]{:S(2)}, u32[]{:S(2)}) collective-permute-start(bf16[128,1024]{1,0:T(8,128)(2,1)S(1)} %pad_maximum_fusion.1), channel_id=1, source_target_pairs={{1,3},{3,1},{5,7},{7,5},{9,11},{11,9},{13,15},{15,13},{17,19},{19,... | collective-permute-start | bytes 786440 | tf_op jit(solution)/shard_map/ppermute | solution.py:229
  60.5 6.5 %collective-permute-start.16 = (bf16[256,512]{1,0:T(8,128)(2,1)S(1)}, bf16[256,512]{1,0:T(8,128)(2,1)S(1)}, u32[]{:S(2)}, u32[]{:S(2)}) collective-permute-start(bf16[256,512]{1,0:T(8,128)(2,1)S(1)} %pad_maximum_fusion), channel_id=1, source_target_pairs={{1,0},{3,2},{5,4},{7,6},{9,8},{11,10},{13,12},{15,14},{17,16},{19,... | collective-permute-start | bytes 786440 | tf_op jit(solution)/shard_map/ppermute | solution.py:233
  61.8 5.4 %copy-start.4 = (s32[512]{0:T(512)S(1)}, s32[512]{0:T(512)}, u32[]{:S(2)}) copy-start(s32[512]{0:T(512)} %param.10) | copy-start | bytes 6148
  61.8 5.4 %copy-start.5 = (s32[128]{0:T(128)S(1)}, s32[128]{0:T(128)}, u32[]{:S(2)}) copy-start(s32[128]{0:T(128)} %param.11) | copy-start | bytes 1540
  67.1 1.1 %copy-start.1 = (bf16[512,1024]{1,0:T(8,128)(2,1)}, bf16[512,1024]{1,0:T(8,128)(2,1)S(1)}, u32[]{:S(2)}) copy-start(bf16[512,1024]{1,0:T(8,128)(2,1)S(1)} %maximum_dynamic-update-slice_fusion.2) | copy-start | bytes 3145732

commit v22 on v19

--- a/solution.py
+++ b/solution.py
@@ -13,9 +13,9 @@
 ROWS = 8
 WIDE = KIN * ROWS
 PAIR = 2 * KOUT
-DEPTH_BLOCK = 512
+DEPTH_BLOCK = 2048
 COLUMNS = 512
-ORDERS = ((1, 0), (1, 0))
+ORDERS = (((1, 1), (0, 1)), ((1, 1), (0, 1)))
 NEAR_START_US = 1.1
 FAR_START_US = 1.5
 LATENCY_US = 0.5
@@ -24,7 +24,7 @@
 KERNEL_US = 5.3
 PIECES = 4
 STORE_COPIES = 8
-VMEM_LIMIT = 32 * 1024 * 1024
+VMEM_LIMIT = 20 * 1024 * 1024
 NT = (((1,), (1,)), ((), ()))
 
 
@@ -80,7 +80,7 @@
             pre_ref[at, i * KOUT : (i + 1) * KOUT] = mixed[i]
         return carry
 
-    lax.fori_loop(0, rows_ref.shape[0] // (2 * ROWS), groups, 0, unroll=4)
+    lax.fori_loop(0, rows_ref.shape[0] // (2 * ROWS), groups, 0, unroll=8)
 
 
 def copy_of(source_ref, target_ref, sems, step):
@@ -228,12 +228,13 @@
 
 
 class LayerSum:
-    def __init__(self, block, bits, index):
+    def __init__(self, block, bits, index, exchanges):
         self.block, self.index = block, index
-        self.moves = [(bit, HALVE) for bit in bits[:-1]]
-        self.moves += [(bit, EXCHANGE) for bit in bits[-1:]]
-        self.moves += [(bit, DOUBLE) for bit in reversed(bits[:-1])]
-        if len(bits) < 2:
+        halved, exchanged = bits[:-exchanges], bits[-exchanges:]
+        self.moves = [(bit, HALVE) for bit in halved]
+        self.moves += [(bit, EXCHANGE) for bit in exchanged]
+        self.moves += [(bit, DOUBLE) for bit in reversed(halved)]
+        if not halved:
             self.block = block.astype(jnp.bfloat16)
 
     def send(self, order):
@@ -336,9 +337,9 @@
                 send(chunk, order, clock)
         choices = ORDERS[min(step, len(ORDERS) - 1)]
         width = columns // len(choices)
-        for number, choice in enumerate(choices):
+        for number, (choice, exchanges) in enumerate(choices):
             first = number * width
-            chunk = LayerSum(part[:, first : first + width], orders[choice], index)
+            chunk = LayerSum(part[:, first : first + width], orders[choice], index, exchanges)
             send(chunk, order, clock)
             chunks.append(chunk)
             places.append(((position - step) % ex_count * rows, jnp.int32(first)))

time: 52.4 us -> 51.9 us (level)
  no operation moved by 1% of the time
where the time goes in v22:
time: 51.9 us; the launch traced here: 51.7 us
  starting transfers between devices  24.6 us (47%)
  waiting for transfers between devices  11.9 us (23%)
  Pallas kernels  11.7 us (23%)
  matrix products  1.08 us (2%)
  between operations  0.96 us (2%)
  local copies, waits for them, and re-layouts  0.8 us (2%)
  other arithmetic  0.66 us (1%)
    ppermute x20, starting transfers between devices, swap(): return lax.ppermute(block, 'layer', route)  24.1 us
    ppermute x20, waiting for transfers between devices, swap(): return lax.ppermute(block, 'layer', route)  11.9 us
    pallas_call x2, Pallas kernels, call(): pl.pallas_call(kernel, out_shape=(jax.ShapeDtypeStruct((count, examples),...  11.7 us
    dot_general x1, matrix products, shards(): advantage = jnp.dot(weights, scores, preferred_element_type=jnp.float32)  1.08 us
  transfers between devices with their start and end apart: 21, of which 9 were waited for; matrix products, arithmetic and copies ran while one was open for 2% of the time, Pallas kernels for 23%

profile of v22, /device:TPU:0, one launch (start us, length us, event | category | flops | bytes accessed | tf_op | source)
XLA Modules:
  0.0 51.7 jit_solution(11342391570423513844)
XLA Ops:
  0.6 0.5 %collective-permute-start.1 = (bf16[1,256,4096]{2,1,0:T(8,128)(2,1)}, bf16[1,256,4096]{2,1,0:T(8,128)(2,1)S(1)}, u32[]{:S(2)}, u32[]{:S(2)}) collective-permute-start(bf16[1,256,4096]{2,1,0:T(8,128)(2,1)} %rows_ref.1), channel_id=1, source_target_pairs={{1,0},{0,1},{3,2},{2,3},{5,4},{4,5},{7,6},{6,7},{9,8},{8,9},{11,10... | collective-permute-start | bytes 6291464 | tf_op jit(solution)/shard_map/ppermute | solution.py:330
  1.1 6.6 %shard_map.77 = (f32[256,1024]{1,0:T(8,128)S(1)}, bf16[256,256]{1,0:T(8,128)(2,1)S(1)}, bf16[256,256]{1,0:T(8,128)(2,1)S(1)}) custom-call(bf16[1,256,4096]{2,1,0:T(8,128)(2,1)} %rows_ref.1, bf16[1,32,32]{2,1,0:T(8,128)(2,1)} %left_ref.1, bf16[1,128,128]{2,1,0:T(8,128)(2,1)} %right_ref.1, bf16[1,1024,4096]{2,1,0:T(8,128)(2,1)} %store_ref.3), custom_call_target="tpu_custom_call" | custom-call | flops 4294967296 | bytes 10485760 | tf_op jit(solution)/shard_map/pallas_call | solution.py:173
  7.8 0.1 fusion.7
  7.9 0.0 copy-start.1
  7.9 2.7 %collective-permute-start = (bf16[128,512]{1,0:T(8,128)(2,1)S(1)}, bf16[128,512]{1,0:T(8,128)(2,1)S(1)}, u32[]{:S(2)}, u32[]{:S(2)}) collective-permute-start(bf16[128,512]{1,0:T(8,128)(2,1)S(1)} %get-tuple-element.60.refs_0_), channel_id=1, source_target_pairs={{0,4},{2,6},{4,0},{6,2},{8,12},{10,14},{12,8},{14,10},{1,5},{3,7},... | collective-permute-start | bytes 393224 | tf_op jit(solution)/shard_map/ppermute | solution.py:224
  10.6 0.0 copy-done.1
  10.6 1.5 %collective-permute-start.3 = (bf16[128,512]{1,0:T(8,128)(2,1)S(1)}, bf16[128,512]{1,0:T(8,128)(2,1)S(1)}, u32[]{:S(2)}, u32[]{:S(2)}) collective-permute-start(bf16[128,512]{1,0:T(8,128)(2,1)S(1)} %get-tuple-element.66.refs_1_), channel_id=1, source_target_pairs={{0,2},{2,0},{4,6},{6,4},{8,10},{10,8},{12,14},{14,12},{1,3},{3,1},... | collective-permute-start | bytes 393224 | tf_op jit(solution)/shard_map/ppermute | solution.py:224
  12.1 0.0 collective-permute-done.1.rows_ref
  12.1 5.1 %shard_map.78 = f32[256,1024]{1,0:T(8,128)S(1)} custom-call(bf16[1,256,4096]{2,1,0:T(8,128)(2,1)S(1)} %collective-permute-done.1.rows_ref, bf16[256,256]{1,0:T(8,128)(2,1)S(1)} %get-tuple-element.64.both_ref, bf16[256,256]{1,0:T(8,128)(2,1)S(1)} %get-tuple-element.65.mixer_ref, bf16[1,1024,4096]{2,1,0:T(8,128)(2,1)} %store_ref.3, ...), custom_call_target="tpu_custom_call" | custom-call | flops 4294967296 | bytes 10485760 | tf_op jit(solution)/shard_map/pallas_call | solution.py:173
  17.2 0.0 copy-start.2
  17.2 0.1 fusion.6
  17.3 0.6 %collective-permute-start.7 = (bf16[128,512]{1,0:T(8,128)(2,1)S(1)}, bf16[128,512]{1,0:T(8,128)(2,1)S(1)}, u32[]{:S(2)}, u32[]{:S(2)}) collective-permute-start(bf16[128,512]{1,0:T(8,128)(2,1)S(1)} %dynamic-slice_convert_fusion.1), channel_id=1, source_target_pairs={{0,2},{2,0},{4,6},{6,4},{8,10},{10,8},{12,14},{14,12},{1,3},{3,1},... | collective-permute-start | bytes 393224 | tf_op jit(solution)/shard_map/ppermute | solution.py:224
  17.9 0.0 collective-permute-done
  17.9 0.3 copy-done.2
  18.3 0.0 collective-permute-done.3
  18.4 0.7 %collective-permute-start.4 = (bf16[64,512]{1,0:T(8,128)(2,1)S(1)}, bf16[64,512]{1,0:T(8,128)(2,1)S(1)}, u32[]{:S(2)}, u32[]{:S(2)}) collective-permute-start(bf16[64,512]{1,0:T(8,128)(2,1)S(1)} %dynamic-slice_convert_fusion.6), channel_id=1, source_target_pairs={{0,4},{2,6},{4,0},{6,2},{8,12},{10,14},{12,8},{14,10},{1,5},{3,7},... | collective-permute-start | bytes 196616 | tf_op jit(solution)/shard_map/ppermute | solution.py:224
  19.1 1.4 %collective-permute-start.8 = (bf16[128,512]{1,0:T(8,128)(2,1)S(1)}, bf16[128,512]{1,0:T(8,128)(2,1)S(1)}, u32[]{:S(2)}, u32[]{:S(2)}) collective-permute-start(bf16[128,512]{1,0:T(8,128)(2,1)S(1)} %dynamic-slice_convert_fusion), channel_id=1, source_target_pairs={{0,4},{2,6},{4,0},{6,2},{8,12},{10,14},{12,8},{14,10},{1,5},{3,7},... | collective-permute-start | bytes 393224 | tf_op jit(solution)/shard_map/ppermute | solution.py:224
  20.6 1.2 %collective-permute-start.2 = (bf16[64,512]{1,0:T(8,128)(2,1)S(1)}, bf16[64,512]{1,0:T(8,128)(2,1)S(1)}, u32[]{:S(2)}, u32[]{:S(2)}) collective-permute-start(bf16[64,512]{1,0:T(8,128)(2,1)S(1)} %dynamic-slice_convert_fusion.7), channel_id=1, source_target_pairs={{0,2},{2,0},{4,6},{6,4},{8,10},{10,8},{12,14},{14,12},{1,3},{3,1},... | collective-permute-start | bytes 196616 | tf_op jit(solution)/shard_map/ppermute | solution.py:224
  21.8 1.6 %collective-permute-done.4 = bf16[64,512]{1,0:T(8,128)(2,1)S(1)} collective-permute-done((bf16[64,512]{1,0:T(8,128)(2,1)S(1)}, bf16[64,512]{1,0:T(8,128)(2,1)S(1)}, u32[]{:S(2)}, u32[]{:S(2)}) %collective-permute-start.4) | collective-permute-done | bytes 65568 | tf_op jit(solution)/shard_map/ppermute | solution.py:224
  23.4 2.7 %collective-permute-start.6 = (bf16[64,512]{1,0:T(8,128)(2,1)S(1)}, bf16[64,512]{1,0:T(8,128)(2,1)S(1)}, u32[]{:S(2)}, u32[]{:S(2)}) collective-permute-start(bf16[64,512]{1,0:T(8,128)(2,1)S(1)} %add_convert_fusion.7), channel_id=1, source_target_pairs={{0,8},{2,10},{4,12},{6,14},{8,0},{10,2},{12,4},{14,6},{1,9},{3,11}... | collective-permute-start | bytes 196616 | tf_op jit(solution)/shard_map/ppermute | solution.py:224
  26.1 0.0 collective-permute-done.2
  26.1 1.4 %collective-permute-start.5 = (bf16[64,512]{1,0:T(8,128)(2,1)S(1)}, bf16[64,512]{1,0:T(8,128)(2,1)S(1)}, u32[]{:S(2)}, u32[]{:S(2)}) collective-permute-start(bf16[64,512]{1,0:T(8,128)(2,1)S(1)} %add_convert_fusion.6), channel_id=1, source_target_pairs={{0,8},{2,10},{4,12},{6,14},{8,0},{10,2},{12,4},{14,6},{1,9},{3,11}... | collective-permute-start | bytes 196616 | tf_op jit(solution)/shard_map/ppermute | solution.py:224
  27.5 0.0 collective-permute-done.7
  27.6 0.7 %collective-permute-start.10 = (bf16[64,512]{1,0:T(8,128)(2,1)S(1)}, bf16[64,512]{1,0:T(8,128)(2,1)S(1)}, u32[]{:S(2)}, u32[]{:S(2)}) collective-permute-start(bf16[64,512]{1,0:T(8,128)(2,1)S(1)} %dynamic-slice_convert_fusion.4), channel_id=1, source_target_pairs={{0,4},{2,6},{4,0},{6,2},{8,12},{10,14},{12,8},{14,10},{1,5},{3,7},... | collective-permute-start | bytes 196616 | tf_op jit(solution)/shard_map/ppermute | solution.py:224
  28.3 0.0 collective-permute-done.8
  28.4 1.3 %collective-permute-start.11 = (bf16[64,512]{1,0:T(8,128)(2,1)S(1)}, bf16[64,512]{1,0:T(8,128)(2,1)S(1)}, u32[]{:S(2)}, u32[]{:S(2)}) collective-permute-start(bf16[64,512]{1,0:T(8,128)(2,1)S(1)} %dynamic-slice_convert_fusion.5), channel_id=1, source_target_pairs={{0,2},{2,0},{4,6},{6,4},{8,10},{10,8},{12,14},{14,12},{1,3},{3,1},... | collective-permute-start | bytes 196616 | tf_op jit(solution)/shard_map/ppermute | solution.py:224
  29.6 1.0 %collective-permute-done.6 = bf16[64,512]{1,0:T(8,128)(2,1)S(1)} collective-permute-done((bf16[64,512]{1,0:T(8,128)(2,1)S(1)}, bf16[64,512]{1,0:T(8,128)(2,1)S(1)}, u32[]{:S(2)}, u32[]{:S(2)}) %collective-permute-start.6) | collective-permute-done | bytes 65568 | tf_op jit(solution)/shard_map/ppermute | solution.py:224
  30.6 0.5 collective-permute-start.9
  31.1 1.0 %collective-permute-done.5 = bf16[64,512]{1,0:T(8,128)(2,1)S(1)} collective-permute-done((bf16[64,512]{1,0:T(8,128)(2,1)S(1)}, bf16[64,512]{1,0:T(8,128)(2,1)S(1)}, u32[]{:S(2)}, u32[]{:S(2)}) %collective-permute-start.5) | collective-permute-done | bytes 65568 | tf_op jit(solution)/shard_map/ppermute | solution.py:224
  32.1 1.0 %collective-permute-start.12 = (bf16[64,512]{1,0:T(8,128)(2,1)S(1)}, bf16[64,512]{1,0:T(8,128)(2,1)S(1)}, u32[]{:S(2)}, u32[]{:S(2)}) collective-permute-start(bf16[64,512]{1,0:T(8,128)(2,1)S(1)} %add_convert_fusion.2), channel_id=1, source_target_pairs={{0,2},{2,0},{4,6},{6,4},{8,10},{10,8},{12,14},{14,12},{1,3},{3,1},... | collective-permute-start | bytes 196616 | tf_op jit(solution)/shard_map/ppermute | solution.py:224
  33.1 0.0 collective-permute-done.10
  33.1 1.6 %collective-permute-start.18 = (bf16[64,512]{1,0:T(8,128)(2,1)S(1)}, bf16[64,512]{1,0:T(8,128)(2,1)S(1)}, u32[]{:S(2)}, u32[]{:S(2)}) collective-permute-start(bf16[64,512]{1,0:T(8,128)(2,1)S(1)} %add_convert_fusion.3), channel_id=1, source_target_pairs={{0,8},{2,10},{4,12},{6,14},{8,0},{10,2},{12,4},{14,6},{1,9},{3,11}... | collective-permute-start | bytes 196616 | tf_op jit(solution)/shard_map/ppermute | solution.py:224
  34.7 0.0 collective-permute-done.11
  34.7 1.5 %collective-permute-start.15 = (bf16[64,512]{1,0:T(8,128)(2,1)S(1)}, bf16[64,512]{1,0:T(8,128)(2,1)S(1)}, u32[]{:S(2)}, u32[]{:S(2)}) collective-permute-start(bf16[64,512]{1,0:T(8,128)(2,1)S(1)} %add_convert_fusion.4), channel_id=1, source_target_pairs={{0,8},{2,10},{4,12},{6,14},{8,0},{10,2},{12,4},{14,6},{1,9},{3,11}... | collective-permute-start | bytes 196616 | tf_op jit(solution)/shard_map/ppermute | solution.py:224
  36.2 0.0 collective-permute-done.9
  36.2 1.2 %collective-permute-start.14 = (bf16[128,512]{1,0:T(8,128)(2,1)S(1)}, bf16[128,512]{1,0:T(8,128)(2,1)S(1)}, u32[]{:S(2)}, u32[]{:S(2)}) collective-permute-start(bf16[128,512]{1,0:T(8,128)(2,1)S(1)} %pad_maximum_fusion.1), channel_id=1, source_target_pairs={{0,2},{2,0},{4,6},{6,4},{8,10},{10,8},{12,14},{14,12},{1,3},{3,1},... | collective-permute-start | bytes 393224 | tf_op jit(solution)/shard_map/ppermute | solution.py:224
  37.4 0.0 collective-permute-done.12
  37.4 0.8 %collective-permute-start.13 = (bf16[128,512]{1,0:T(8,128)(2,1)S(1)}, bf16[128,512]{1,0:T(8,128)(2,1)S(1)}, u32[]{:S(2)}, u32[]{:S(2)}) collective-permute-start(bf16[128,512]{1,0:T(8,128)(2,1)S(1)} %pad_maximum_fusion), channel_id=1, source_target_pairs={{0,4},{2,6},{4,0},{6,2},{8,12},{10,14},{12,8},{14,10},{1,5},{3,7},... | collective-permute-start | bytes 393224 | tf_op jit(solution)/shard_map/ppermute | solution.py:224
  38.2 0.7 %collective-permute-done.18 = bf16[64,512]{1,0:T(8,128)(2,1)S(1)} collective-permute-done((bf16[64,512]{1,0:T(8,128)(2,1)S(1)}, bf16[64,512]{1,0:T(8,128)(2,1)S(1)}, u32[]{:S(2)}, u32[]{:S(2)}) %collective-permute-start.18) | collective-permute-done | bytes 65568 | tf_op jit(solution)/shard_map/ppermute | solution.py:224
  38.9 0.9 %collective-permute-start.19 = (bf16[64,512]{1,0:T(8,128)(2,1)S(1)}, bf16[64,512]{1,0:T(8,128)(2,1)S(1)}, u32[]{:S(2)}, u32[]{:S(2)}) collective-permute-start(bf16[64,512]{1,0:T(8,128)(2,1)S(1)} %add_convert_fusion), channel_id=1, source_target_pairs={{0,4},{2,6},{4,0},{6,2},{8,12},{10,14},{12,8},{14,10},{1,5},{3,7},... | collective-permute-start | bytes 196616 | tf_op jit(solution)/shard_map/ppermute | solution.py:224
  39.8 0.6 %collective-permute-done.15 = bf16[64,512]{1,0:T(8,128)(2,1)S(1)} collective-permute-done((bf16[64,512]{1,0:T(8,128)(2,1)S(1)}, bf16[64,512]{1,0:T(8,128)(2,1)S(1)}, u32[]{:S(2)}, u32[]{:S(2)}) %collective-permute-start.15) | collective-permute-done | bytes 65568 | tf_op jit(solution)/shard_map/ppermute | solution.py:224
  40.5 0.8 %collective-permute-start.16 = (bf16[64,512]{1,0:T(8,128)(2,1)S(1)}, bf16[64,512]{1,0:T(8,128)(2,1)S(1)}, u32[]{:S(2)}, u32[]{:S(2)}) collective-permute-start(bf16[64,512]{1,0:T(8,128)(2,1)S(1)} %add_convert_fusion.1), channel_id=1, source_target_pairs={{0,2},{2,0},{4,6},{6,4},{8,10},{10,8},{12,14},{14,12},{1,3},{3,1},... | collective-permute-start | bytes 196616 | tf_op jit(solution)/shard_map/ppermute | solution.py:224
  41.3 1.9 %collective-permute-done.19 = bf16[64,512]{1,0:T(8,128)(2,1)S(1)} collective-permute-done((bf16[64,512]{1,0:T(8,128)(2,1)S(1)}, bf16[64,512]{1,0:T(8,128)(2,1)S(1)}, u32[]{:S(2)}, u32[]{:S(2)}) %collective-permute-start.19) | collective-permute-done | bytes 65568 | tf_op jit(solution)/shard_map/ppermute | solution.py:224
  43.3 1.1 %collective-permute-start.20 = (bf16[128,512]{1,0:T(8,128)(2,1)S(1)}, bf16[128,512]{1,0:T(8,128)(2,1)S(1)}, u32[]{:S(2)}, u32[]{:S(2)}) collective-permute-start(bf16[128,512]{1,0:T(8,128)(2,1)S(1)} %pad_maximum_fusion.3), channel_id=1, source_target_pairs={{0,2},{2,0},{4,6},{6,4},{8,10},{10,8},{12,14},{14,12},{1,3},{3,1},... | collective-permute-start | bytes 393224 | tf_op jit(solution)/shard_map/ppermute | solution.py:224
  44.4 1.0 %collective-permute-done.16 = bf16[64,512]{1,0:T(8,128)(2,1)S(1)} collective-permute-done((bf16[64,512]{1,0:T(8,128)(2,1)S(1)}, bf16[64,512]{1,0:T(8,128)(2,1)S(1)}, u32[]{:S(2)}, u32[]{:S(2)}) %collective-permute-start.16) | collective-permute-done | bytes 65568 | tf_op jit(solution)/shard_map/ppermute | solution.py:224
  45.5 0.7 %collective-permute-start.17 = (bf16[128,512]{1,0:T(8,128)(2,1)S(1)}, bf16[128,512]{1,0:T(8,128)(2,1)S(1)}, u32[]{:S(2)}, u32[]{:S(2)}) collective-permute-start(bf16[128,512]{1,0:T(8,128)(2,1)S(1)} %pad_maximum_fusion.2), channel_id=1, source_target_pairs={{0,4},{2,6},{4,0},{6,2},{8,12},{10,14},{12,8},{14,10},{1,5},{3,7},... | collective-permute-start | bytes 393224 | tf_op jit(solution)/shard_map/ppermute | solution.py:224
  46.1 0.0 collective-permute-done.14
  46.2 0.0 collective-permute-done.13
  46.3 0.0 copy-start.3
  46.3 0.0 copy-start.4
  46.3 0.1 broadcast_in_dim.2
  46.5 1.8 %collective-permute-done.20 = bf16[128,512]{1,0:T(8,128)(2,1)S(1)} collective-permute-done((bf16[128,512]{1,0:T(8,128)(2,1)S(1)}, bf16[128,512]{1,0:T(8,128)(2,1)S(1)}, u32[]{:S(2)}, u32[]{:S(2)}) %collective-permute-start.20) | collective-permute-done | bytes 131104 | tf_op jit(solution)/shard_map/ppermute | solution.py:224
  48.4 2.1 %collective-permute-done.17 = bf16[128,512]{1,0:T(8,128)(2,1)S(1)} collective-permute-done((bf16[128,512]{1,0:T(8,128)(2,1)S(1)}, bf16[128,512]{1,0:T(8,128)(2,1)S(1)}, u32[]{:S(2)}, u32[]{:S(2)}) %collective-permute-start.17) | collective-permute-done | bytes 131104 | tf_op jit(solution)/shard_map/ppermute | solution.py:224
  50.6 0.0 copy-done.3
  50.6 0.0 copy-done.4
  50.6 0.0 copy-start
  50.7 1.1 %convolution_convert_fusion = bf16[128,1024]{1,0:T(8,128)(2,1)} fusion(bf16[512,1024]{1,0:T(8,128)(2,1)S(1)} %maximum_dynamic-update-slice_fusion.3, s32[512]{0:T(512)S(1)} %copy-done.3, s32[128]{0:T(128)S(1)} %copy-done.4), kind=kOutput, calls=%fused_computation | convolution fusion | flops 134742016 | bytes 1313280 | tf_op jit(solution)/shard_map/dot_general | solution.py:360
  51.7 0.0 copy-done
  (35 shorter events, 0.8 us)
Async XLA Ops:
  0.6 11.5 %collective-permute-start.1 = (bf16[1,256,4096]{2,1,0:T(8,128)(2,1)}, bf16[1,256,4096]{2,1,0:T(8,128)(2,1)S(1)}, u32[]{:S(2)}, u32[]{:S(2)}) collective-permute-start(bf16[1,256,4096]{2,1,0:T(8,128)(2,1)} %rows_ref.1), channel_id=1, source_target_pairs={{1,0},{0,1},{3,2},{2,3},{5,4},{4,5},{7,6},{6,7},{9,8},{8,9},{11,10... | collective-permute-start | bytes 6291464 | tf_op jit(solution)/shard_map/ppermute | solution.py:330
  7.9 2.7 %copy-start.1 = (f32[256,512]{1,0:T(8,128)}, f32[256,512]{1,0:T(8,128)S(1)}, u32[]{:S(2)}) copy-start(f32[256,512]{1,0:T(8,128)S(1)} %get-tuple-element.119) | copy-start | bytes 1572868
  7.9 10.0 %collective-permute-start = (bf16[128,512]{1,0:T(8,128)(2,1)S(1)}, bf16[128,512]{1,0:T(8,128)(2,1)S(1)}, u32[]{:S(2)}, u32[]{:S(2)}) collective-permute-start(bf16[128,512]{1,0:T(8,128)(2,1)S(1)} %get-tuple-element.60.refs_0_), channel_id=1, source_target_pairs={{0,4},{2,6},{4,0},{6,2},{8,12},{10,14},{12,8},{14,10},{1,5},{3,7},... | collective-permute-start | bytes 393224 | tf_op jit(solution)/shard_map/ppermute | solution.py:224
  10.6 7.7 %collective-permute-start.3 = (bf16[128,512]{1,0:T(8,128)(2,1)S(1)}, bf16[128,512]{1,0:T(8,128)(2,1)S(1)}, u32[]{:S(2)}, u32[]{:S(2)}) collective-permute-start(bf16[128,512]{1,0:T(8,128)(2,1)S(1)} %get-tuple-element.66.refs_1_), channel_id=1, source_target_pairs={{0,2},{2,0},{4,6},{6,4},{8,10},{10,8},{12,14},{14,12},{1,3},{3,1},... | collective-permute-start | bytes 393224 | tf_op jit(solution)/shard_map/ppermute | solution.py:224
  17.2 1.0 %copy-start.2 = (f32[256,512]{1,0:T(8,128)S(1)}, f32[256,512]{1,0:T(8,128)}, u32[]{:S(2)}) copy-start(f32[256,512]{1,0:T(8,128)} %copy-done.1) | copy-start | bytes 1572868
  17.3 10.2 %collective-permute-start.7 = (bf16[128,512]{1,0:T(8,128)(2,1)S(1)}, bf16[128,512]{1,0:T(8,128)(2,1)S(1)}, u32[]{:S(2)}, u32[]{:S(2)}) collective-permute-start(bf16[128,512]{1,0:T(8,128)(2,1)S(1)} %dynamic-slice_convert_fusion.1), channel_id=1, source_target_pairs={{0,2},{2,0},{4,6},{6,4},{8,10},{10,8},{12,14},{14,12},{1,3},{3,1},... | collective-permute-start | bytes 393224 | tf_op jit(solution)/shard_map/ppermute | solution.py:224
  18.4 5.0 %collective-permute-start.4 = (bf16[64,512]{1,0:T(8,128)(2,1)S(1)}, bf16[64,512]{1,0:T(8,128)(2,1)S(1)}, u32[]{:S(2)}, u32[]{:S(2)}) collective-permute-start(bf16[64,512]{1,0:T(8,128)(2,1)S(1)} %dynamic-slice_convert_fusion.6), channel_id=1, source_target_pairs={{0,4},{2,6},{4,0},{6,2},{8,12},{10,14},{12,8},{14,10},{1,5},{3,7},... | collective-permute-start | bytes 196616 | tf_op jit(solution)/shard_map/ppermute | solution.py:224
  19.1 9.2 %collective-permute-start.8 = (bf16[128,512]{1,0:T(8,128)(2,1)S(1)}, bf16[128,512]{1,0:T(8,128)(2,1)S(1)}, u32[]{:S(2)}, u32[]{:S(2)}) collective-permute-start(bf16[128,512]{1,0:T(8,128)(2,1)S(1)} %dynamic-slice_convert_fusion), channel_id=1, source_target_pairs={{0,4},{2,6},{4,0},{6,2},{8,12},{10,14},{12,8},{14,10},{1,5},{3,7},... | collective-permute-start | bytes 393224 | tf_op jit(solution)/shard_map/ppermute | solution.py:224
  20.6 5.5 %collective-permute-start.2 = (bf16[64,512]{1,0:T(8,128)(2,1)S(1)}, bf16[64,512]{1,0:T(8,128)(2,1)S(1)}, u32[]{:S(2)}, u32[]{:S(2)}) collective-permute-start(bf16[64,512]{1,0:T(8,128)(2,1)S(1)} %dynamic-slice_convert_fusion.7), channel_id=1, source_target_pairs={{0,2},{2,0},{4,6},{6,4},{8,10},{10,8},{12,14},{14,12},{1,3},{3,1},... | collective-permute-start | bytes 196616 | tf_op jit(solution)/shard_map/ppermute | solution.py:224
  23.4 7.2 %collective-permute-start.6 = (bf16[64,512]{1,0:T(8,128)(2,1)S(1)}, bf16[64,512]{1,0:T(8,128)(2,1)S(1)}, u32[]{:S(2)}, u32[]{:S(2)}) collective-permute-start(bf16[64,512]{1,0:T(8,128)(2,1)S(1)} %add_convert_fusion.7), channel_id=1, source_target_pairs={{0,8},{2,10},{4,12},{6,14},{8,0},{10,2},{12,4},{14,6},{1,9},{3,11}... | collective-permute-start | bytes 196616 | tf_op jit(solution)/shard_map/ppermute | solution.py:224
  26.1 5.9 %collective-permute-start.5 = (bf16[64,512]{1,0:T(8,128)(2,1)S(1)}, bf16[64,512]{1,0:T(8,128)(2,1)S(1)}, u32[]{:S(2)}, u32[]{:S(2)}) collective-permute-start(bf16[64,512]{1,0:T(8,128)(2,1)S(1)} %add_convert_fusion.6), channel_id=1, source_target_pairs={{0,8},{2,10},{4,12},{6,14},{8,0},{10,2},{12,4},{14,6},{1,9},{3,11}... | collective-permute-start | bytes 196616 | tf_op jit(solution)/shard_map/ppermute | solution.py:224
  27.6 5.5 %collective-permute-start.10 = (bf16[64,512]{1,0:T(8,128)(2,1)S(1)}, bf16[64,512]{1,0:T(8,128)(2,1)S(1)}, u32[]{:S(2)}, u32[]{:S(2)}) collective-permute-start(bf16[64,512]{1,0:T(8,128)(2,1)S(1)} %dynamic-slice_convert_fusion.4), channel_id=1, source_target_pairs={{0,4},{2,6},{4,0},{6,2},{8,12},{10,14},{12,8},{14,10},{1,5},{3,7},... | collective-permute-start | bytes 196616 | tf_op jit(solution)/shard_map/ppermute | solution.py:224
  28.4 6.3 %collective-permute-start.11 = (bf16[64,512]{1,0:T(8,128)(2,1)S(1)}, bf16[64,512]{1,0:T(8,128)(2,1)S(1)}, u32[]{:S(2)}, u32[]{:S(2)}) collective-permute-start(bf16[64,512]{1,0:T(8,128)(2,1)S(1)} %dynamic-slice_convert_fusion.5), channel_id=1, source_target_pairs={{0,2},{2,0},{4,6},{6,4},{8,10},{10,8},{12,14},{14,12},{1,3},{3,1},... | collective-permute-start | bytes 196616 | tf_op jit(solution)/shard_map/ppermute | solution.py:224
  30.6 5.5 %collective-permute-start.9 = (bf16[64,512]{1,0:T(8,128)(2,1)S(1)}, bf16[64,512]{1,0:T(8,128)(2,1)S(1)}, u32[]{:S(2)}, u32[]{:S(2)}) collective-permute-start(bf16[64,512]{1,0:T(8,128)(2,1)S(1)} %add_convert_fusion.5), channel_id=1, source_target_pairs={{0,4},{2,6},{4,0},{6,2},{8,12},{10,14},{12,8},{14,10},{1,5},{3,7},... | collective-permute-start | bytes 196616 | tf_op jit(solution)/shard_map/ppermute | solution.py:224
  32.1 5.3 %collective-permute-start.12 = (bf16[64,512]{1,0:T(8,128)(2,1)S(1)}, bf16[64,512]{1,0:T(8,128)(2,1)S(1)}, u32[]{:S(2)}, u32[]{:S(2)}) collective-permute-start(bf16[64,512]{1,0:T(8,128)(2,1)S(1)} %add_convert_fusion.2), channel_id=1, source_target_pairs={{0,2},{2,0},{4,6},{6,4},{8,10},{10,8},{12,14},{14,12},{1,3},{3,1},... | collective-permute-start | bytes 196616 | tf_op jit(solution)/shard_map/ppermute | solution.py:224
  33.1 5.8 %collective-permute-start.18 = (bf16[64,512]{1,0:T(8,128)(2,1)S(1)}, bf16[64,512]{1,0:T(8,128)(2,1)S(1)}, u32[]{:S(2)}, u32[]{:S(2)}) collective-permute-start(bf16[64,512]{1,0:T(8,128)(2,1)S(1)} %add_convert_fusion.3), channel_id=1, source_target_pairs={{0,8},{2,10},{4,12},{6,14},{8,0},{10,2},{12,4},{14,6},{1,9},{3,11}... | collective-permute-start | bytes 196616 | tf_op jit(solution)/shard_map/ppermute | solution.py:224
  34.7 5.8 %collective-permute-start.15 = (bf16[64,512]{1,0:T(8,128)(2,1)S(1)}, bf16[64,512]{1,0:T(8,128)(2,1)S(1)}, u32[]{:S(2)}, u32[]{:S(2)}) collective-permute-start(bf16[64,512]{1,0:T(8,128)(2,1)S(1)} %add_convert_fusion.4), channel_id=1, source_target_pairs={{0,8},{2,10},{4,12},{6,14},{8,0},{10,2},{12,4},{14,6},{1,9},{3,11}... | collective-permute-start | bytes 196616 | tf_op jit(solution)/shard_map/ppermute | solution.py:224
  36.2 9.9 %collective-permute-start.14 = (bf16[128,512]{1,0:T(8,128)(2,1)S(1)}, bf16[128,512]{1,0:T(8,128)(2,1)S(1)}, u32[]{:S(2)}, u32[]{:S(2)}) collective-permute-start(bf16[128,512]{1,0:T(8,128)(2,1)S(1)} %pad_maximum_fusion.1), channel_id=1, source_target_pairs={{0,2},{2,0},{4,6},{6,4},{8,10},{10,8},{12,14},{14,12},{1,3},{3,1},... | collective-permute-start | bytes 393224 | tf_op jit(solution)/shard_map/ppermute | solution.py:224
  37.4 8.8 %collective-permute-start.13 = (bf16[128,512]{1,0:T(8,128)(2,1)S(1)}, bf16[128,512]{1,0:T(8,128)(2,1)S(1)}, u32[]{:S(2)}, u32[]{:S(2)}) collective-permute-start(bf16[128,512]{1,0:T(8,128)(2,1)S(1)} %pad_maximum_fusion), channel_id=1, source_target_pairs={{0,4},{2,6},{4,0},{6,2},{8,12},{10,14},{12,8},{14,10},{1,5},{3,7},... | collective-permute-start | bytes 393224 | tf_op jit(solution)/shard_map/ppermute | solution.py:224
  38.9 4.3 %collective-permute-start.19 = (bf16[64,512]{1,0:T(8,128)(2,1)S(1)}, bf16[64,512]{1,0:T(8,128)(2,1)S(1)}, u32[]{:S(2)}, u32[]{:S(2)}) collective-permute-start(bf16[64,512]{1,0:T(8,128)(2,1)S(1)} %add_convert_fusion), channel_id=1, source_target_pairs={{0,4},{2,6},{4,0},{6,2},{8,12},{10,14},{12,8},{14,10},{1,5},{3,7},... | collective-permute-start | bytes 196616 | tf_op jit(solution)/shard_map/ppermute | solution.py:224
  40.5 5.0 %collective-permute-start.16 = (bf16[64,512]{1,0:T(8,128)(2,1)S(1)}, bf16[64,512]{1,0:T(8,128)(2,1)S(1)}, u32[]{:S(2)}, u32[]{:S(2)}) collective-permute-start(bf16[64,512]{1,0:T(8,128)(2,1)S(1)} %add_convert_fusion.1), channel_id=1, source_target_pairs={{0,2},{2,0},{4,6},{6,4},{8,10},{10,8},{12,14},{14,12},{1,3},{3,1},... | collective-permute-start | bytes 196616 | tf_op jit(solution)/shard_map/ppermute | solution.py:224
  43.3 5.0 %collective-permute-start.20 = (bf16[128,512]{1,0:T(8,128)(2,1)S(1)}, bf16[128,512]{1,0:T(8,128)(2,1)S(1)}, u32[]{:S(2)}, u32[]{:S(2)}) collective-permute-start(bf16[128,512]{1,0:T(8,128)(2,1)S(1)} %pad_maximum_fusion.3), channel_id=1, source_target_pairs={{0,2},{2,0},{4,6},{6,4},{8,10},{10,8},{12,14},{14,12},{1,3},{3,1},... | collective-permute-start | bytes 393224 | tf_op jit(solution)/shard_map/ppermute | solution.py:224
  45.5 5.0 %collective-permute-start.17 = (bf16[128,512]{1,0:T(8,128)(2,1)S(1)}, bf16[128,512]{1,0:T(8,128)(2,1)S(1)}, u32[]{:S(2)}, u32[]{:S(2)}) collective-permute-start(bf16[128,512]{1,0:T(8,128)(2,1)S(1)} %pad_maximum_fusion.2), channel_id=1, source_target_pairs={{0,4},{2,6},{4,0},{6,2},{8,12},{10,14},{12,8},{14,10},{1,5},{3,7},... | collective-permute-start | bytes 393224 | tf_op jit(solution)/shard_map/ppermute | solution.py:224
  46.3 4.4 %copy-start.3 = (s32[512]{0:T(512)S(1)}, s32[512]{0:T(512)}, u32[]{:S(2)}) copy-start(s32[512]{0:T(512)} %param.10) | copy-start | bytes 6148
  46.3 4.4 %copy-start.4 = (s32[128]{0:T(128)S(1)}, s32[128]{0:T(128)}, u32[]{:S(2)}) copy-start(s32[128]{0:T(128)} %param.11) | copy-start | bytes 1540
  50.6 1.1 %copy-start = (bf16[512,1024]{1,0:T(8,128)(2,1)}, bf16[512,1024]{1,0:T(8,128)(2,1)S(1)}, u32[]{:S(2)}) copy-start(bf16[512,1024]{1,0:T(8,128)(2,1)S(1)} %maximum_dynamic-update-slice_fusion.3) | copy-start | bytes 3145732

commit v23 on v22

--- a/solution.py
+++ b/solution.py
@@ -13,7 +13,6 @@
 ROWS = 8
 WIDE = KIN * ROWS
 PAIR = 2 * KOUT
-DEPTH_BLOCK = 2048
 COLUMNS = 512
 ORDERS = (((1, 1), (0, 1)), ((1, 1), (0, 1)))
 NEAR_START_US = 1.1
@@ -68,7 +67,7 @@
             ).astype(jnp.bfloat16)
         return carry
 
-    lax.fori_loop(0, PIECES, piece, 0)
+    lax.fori_loop(0, PIECES, piece, 0, unroll=2)
 
     def groups(index, carry):
         stacked = jnp.concatenate([half_ref[2 * index], half_ref[2 * index + 1]], 1)
@@ -95,9 +94,8 @@
         copy_of(store_ref.at[0], store_vmem, sems, step * share + k).start()
 
 
-def dots(pre_ref, store_ref, store_vmem, sems, total_ref, out_ref):
-    columns = total_ref.shape[0]
-    depth = pre_ref.shape[1]
+def dots(pre_ref, store_ref, store_vmem, sems, out_ref):
+    columns = min(COLUMNS, store_vmem.shape[0])
     blocks = store_vmem.shape[0] // columns
     share = sems.shape[0] // blocks
 
@@ -105,19 +103,9 @@
         for k in range(share):
             copy_of(store_ref.at[0], store_vmem, sems, step * share + k).wait()
         rows = pl.ds(pl.multiple_of(step * columns, columns), columns)
-        for at in range(0, depth, DEPTH_BLOCK):
-            term = lax.dot_general(
-                store_vmem[rows, at : at + DEPTH_BLOCK],
-                pre_ref[:, at : at + DEPTH_BLOCK],
-                NT,
-                preferred_element_type=jnp.float32,
-            )
-            if at == 0:
-                total_ref[...] = term
-            elif at + DEPTH_BLOCK < depth:
-                total_ref[...] += term
-            else:
-                out_ref[:, rows] = (total_ref[...] + term).T
+        out_ref[:, rows] = lax.dot_general(
+            store_vmem[rows, :], pre_ref[...], NT, preferred_element_type=jnp.float32
+        ).T
         return carry
 
     lax.fori_loop(0, blocks, block, 0)
@@ -125,7 +113,7 @@
 
 def first_kernel(
     rows_ref, left_ref, right_ref, store_ref, out_ref, both_ref, mixer_ref,
-    left_vmem, right_vmem, rows_vmem, store_vmem, half_ref, total_ref,
+    left_vmem, right_vmem, rows_vmem, store_vmem, half_ref,
     left_sems, right_sems, rows_sems, store_sems,
 ):
     right = copy_of(right_ref.at[0], right_vmem, right_sems, 0)
@@ -144,19 +132,19 @@
         start_store(store_ref, store_vmem, store_sems, step)
 
     precondition(rows_vmem, both_ref[...], mixer_ref[...], half_ref, rows_vmem, before)
-    dots(rows_vmem, store_ref, store_vmem, store_sems, total_ref, out_ref)
+    dots(rows_vmem, store_ref, store_vmem, store_sems, out_ref)
 
 
 def later_kernel(
     sent, rows_ref, both_ref, mixer_ref, store_ref, *refs,
 ):
-    out_ref, pre_ref, store_vmem, half_ref, total_ref, store_sems = refs[sent:]
+    out_ref, pre_ref, store_vmem, half_ref, store_sems = refs[sent:]
 
     def before(step):
         start_store(store_ref, store_vmem, store_sems, step)
 
     precondition(rows_ref.at[0], both_ref[...], mixer_ref[...], half_ref, pre_ref, before)
-    dots(pre_ref, store_ref, store_vmem, store_sems, total_ref, out_ref)
+    dots(pre_ref, store_ref, store_vmem, store_sems, out_ref)
 
 
 VMEM = pl.BlockSpec(memory_space=pltpu.VMEM)
@@ -192,7 +180,6 @@
         pltpu.VMEM((count, depth), jnp.bfloat16),
         pltpu.VMEM((examples, depth), jnp.bfloat16),
         pltpu.VMEM((count // ROWS, WIDE, KOUT), jnp.bfloat16),
-        pltpu.VMEM((min(COLUMNS, examples), count), jnp.float32),
     ]
 
 

time: 51.9 us -> 52.3 us (level)
  no operation moved by 1% of the time
where the time goes in v23:
time: 52.3 us; the launch traced here: 52.1 us
  starting transfers between devices  24.5 us (47%)
  Pallas kernels  12.1 us (23%)
  waiting for transfers between devices  12.1 us (23%)
  matrix products  1.07 us (2%)
  between operations  0.96 us (2%)
  local copies, waits for them, and re-layouts  0.79 us (2%)
  other arithmetic  0.66 us (1%)
    ppermute x20, starting transfers between devices, swap(): return lax.ppermute(block, 'layer', route)  24 us
    ppermute x20, waiting for transfers between devices, swap(): return lax.ppermute(block, 'layer', route)  12.1 us
    pallas_call x2, Pallas kernels, call(): pl.pallas_call(kernel, out_shape=(jax.ShapeDtypeStruct((count, examples),...  12.1 us
    dot_general x1, matrix products, shards(): advantage = jnp.dot(weights, scores, preferred_element_type=jnp.float32)  1.07 us
  transfers between devices with their start and end apart: 21, of which 9 were waited for; matrix products, arithmetic and copies ran while one was open for 2% of the time, Pallas kernels for 23%

profile of v23, /device:TPU:0, one launch (start us, length us, event | category | flops | bytes accessed | tf_op | source)
XLA Modules:
  0.0 52.1 jit_solution(14426459445237275436)
XLA Ops:
  0.6 0.5 collective-permute-start.1
  1.1 7.0 %shard_map.77 = (f32[256,1024]{1,0:T(8,128)S(1)}, bf16[256,256]{1,0:T(8,128)(2,1)S(1)}, bf16[256,256]{1,0:T(8,128)(2,1)S(1)}) custom-call(bf16[1,256,4096]{2,1,0:T(8,128)(2,1)} %rows_ref.1, bf16[1,32,32]{2,1,0:T(8,128)(2,1)} %left_ref.1, bf16[1,128,128]{2,1,0:T(8,128)(2,1)} %right_ref.1, bf16[1,1024,4096]{2,1,0:T(8,128)(2,1)} %store_ref.3), custom_call_target="tpu_custom_call" | custom-call | flops 4294967296 | bytes 10485760 | tf_op jit(solution)/shard_map/pallas_call | solution.py:161
  8.2 0.1 fusion.7
  8.3 0.0 copy-start.1
  8.3 2.7 %collective-permute-start = (bf16[128,512]{1,0:T(8,128)(2,1)S(1)}, bf16[128,512]{1,0:T(8,128)(2,1)S(1)}, u32[]{:S(2)}, u32[]{:S(2)}) collective-permute-start(bf16[128,512]{1,0:T(8,128)(2,1)S(1)} %get-tuple-element.60.refs_0_), channel_id=1, source_target_pairs={{0,4},{2,6},{4,0},{6,2},{8,12},{10,14},{12,8},{14,10},{1,5},{3,7},... | collective-permute-start | bytes 393224 | tf_op jit(solution)/shard_map/ppermute | solution.py:211
  11.0 0.0 copy-done.1
  11.0 1.5 %collective-permute-start.3 = (bf16[128,512]{1,0:T(8,128)(2,1)S(1)}, bf16[128,512]{1,0:T(8,128)(2,1)S(1)}, u32[]{:S(2)}, u32[]{:S(2)}) collective-permute-start(bf16[128,512]{1,0:T(8,128)(2,1)S(1)} %get-tuple-element.66.refs_1_), channel_id=1, source_target_pairs={{0,2},{2,0},{4,6},{6,4},{8,10},{10,8},{12,14},{14,12},{1,3},{3,1},... | collective-permute-start | bytes 393224 | tf_op jit(solution)/shard_map/ppermute | solution.py:211
  12.5 0.0 collective-permute-done.1.rows_ref
  12.5 5.0 %shard_map.78 = f32[256,1024]{1,0:T(8,128)S(1)} custom-call(bf16[1,256,4096]{2,1,0:T(8,128)(2,1)S(1)} %collective-permute-done.1.rows_ref, bf16[256,256]{1,0:T(8,128)(2,1)S(1)} %get-tuple-element.64.both_ref, bf16[256,256]{1,0:T(8,128)(2,1)S(1)} %get-tuple-element.65.mixer_ref, bf16[1,1024,4096]{2,1,0:T(8,128)(2,1)} %store_ref.3, ...), custom_call_target="tpu_custom_call" | custom-call | flops 4294967296 | bytes 10485760 | tf_op jit(solution)/shard_map/pallas_call | solution.py:161
  17.6 0.0 copy-start.2
  17.6 0.1 fusion.6
  17.7 0.6 %collective-permute-start.7 = (bf16[128,512]{1,0:T(8,128)(2,1)S(1)}, bf16[128,512]{1,0:T(8,128)(2,1)S(1)}, u32[]{:S(2)}, u32[]{:S(2)}) collective-permute-start(bf16[128,512]{1,0:T(8,128)(2,1)S(1)} %dynamic-slice_convert_fusion.1), channel_id=1, source_target_pairs={{0,2},{2,0},{4,6},{6,4},{8,10},{10,8},{12,14},{14,12},{1,3},{3,1},... | collective-permute-start | bytes 393224 | tf_op jit(solution)/shard_map/ppermute | solution.py:211
  18.3 0.0 collective-permute-done
  18.3 0.3 copy-done.2
  18.7 0.0 collective-permute-done.3
  18.8 0.7 %collective-permute-start.4 = (bf16[64,512]{1,0:T(8,128)(2,1)S(1)}, bf16[64,512]{1,0:T(8,128)(2,1)S(1)}, u32[]{:S(2)}, u32[]{:S(2)}) collective-permute-start(bf16[64,512]{1,0:T(8,128)(2,1)S(1)} %dynamic-slice_convert_fusion.6), channel_id=1, source_target_pairs={{0,4},{2,6},{4,0},{6,2},{8,12},{10,14},{12,8},{14,10},{1,5},{3,7},... | collective-permute-start | bytes 196616 | tf_op jit(solution)/shard_map/ppermute | solution.py:211
  19.5 1.4 %collective-permute-start.8 = (bf16[128,512]{1,0:T(8,128)(2,1)S(1)}, bf16[128,512]{1,0:T(8,128)(2,1)S(1)}, u32[]{:S(2)}, u32[]{:S(2)}) collective-permute-start(bf16[128,512]{1,0:T(8,128)(2,1)S(1)} %dynamic-slice_convert_fusion), channel_id=1, source_target_pairs={{0,4},{2,6},{4,0},{6,2},{8,12},{10,14},{12,8},{14,10},{1,5},{3,7},... | collective-permute-start | bytes 393224 | tf_op jit(solution)/shard_map/ppermute | solution.py:211
  20.9 1.2 %collective-permute-start.2 = (bf16[64,512]{1,0:T(8,128)(2,1)S(1)}, bf16[64,512]{1,0:T(8,128)(2,1)S(1)}, u32[]{:S(2)}, u32[]{:S(2)}) collective-permute-start(bf16[64,512]{1,0:T(8,128)(2,1)S(1)} %dynamic-slice_convert_fusion.7), channel_id=1, source_target_pairs={{0,2},{2,0},{4,6},{6,4},{8,10},{10,8},{12,14},{14,12},{1,3},{3,1},... | collective-permute-start | bytes 196616 | tf_op jit(solution)/shard_map/ppermute | solution.py:211
  22.2 1.6 %collective-permute-done.4 = bf16[64,512]{1,0:T(8,128)(2,1)S(1)} collective-permute-done((bf16[64,512]{1,0:T(8,128)(2,1)S(1)}, bf16[64,512]{1,0:T(8,128)(2,1)S(1)}, u32[]{:S(2)}, u32[]{:S(2)}) %collective-permute-start.4) | collective-permute-done | bytes 65568 | tf_op jit(solution)/shard_map/ppermute | solution.py:211
  23.8 2.7 %collective-permute-start.6 = (bf16[64,512]{1,0:T(8,128)(2,1)S(1)}, bf16[64,512]{1,0:T(8,128)(2,1)S(1)}, u32[]{:S(2)}, u32[]{:S(2)}) collective-permute-start(bf16[64,512]{1,0:T(8,128)(2,1)S(1)} %add_convert_fusion.7), channel_id=1, source_target_pairs={{0,8},{2,10},{4,12},{6,14},{8,0},{10,2},{12,4},{14,6},{1,9},{3,11}... | collective-permute-start | bytes 196616 | tf_op jit(solution)/shard_map/ppermute | solution.py:211
  26.5 0.0 collective-permute-done.2
  26.5 1.4 %collective-permute-start.5 = (bf16[64,512]{1,0:T(8,128)(2,1)S(1)}, bf16[64,512]{1,0:T(8,128)(2,1)S(1)}, u32[]{:S(2)}, u32[]{:S(2)}) collective-permute-start(bf16[64,512]{1,0:T(8,128)(2,1)S(1)} %add_convert_fusion.6), channel_id=1, source_target_pairs={{0,8},{2,10},{4,12},{6,14},{8,0},{10,2},{12,4},{14,6},{1,9},{3,11}... | collective-permute-start | bytes 196616 | tf_op jit(solution)/shard_map/ppermute | solution.py:211
  27.9 0.0 collective-permute-done.7
  27.9 0.7 %collective-permute-start.10 = (bf16[64,512]{1,0:T(8,128)(2,1)S(1)}, bf16[64,512]{1,0:T(8,128)(2,1)S(1)}, u32[]{:S(2)}, u32[]{:S(2)}) collective-permute-start(bf16[64,512]{1,0:T(8,128)(2,1)S(1)} %dynamic-slice_convert_fusion.4), channel_id=1, source_target_pairs={{0,4},{2,6},{4,0},{6,2},{8,12},{10,14},{12,8},{14,10},{1,5},{3,7},... | collective-permute-start | bytes 196616 | tf_op jit(solution)/shard_map/ppermute | solution.py:211
  28.7 0.0 collective-permute-done.8
  28.7 1.3 %collective-permute-start.11 = (bf16[64,512]{1,0:T(8,128)(2,1)S(1)}, bf16[64,512]{1,0:T(8,128)(2,1)S(1)}, u32[]{:S(2)}, u32[]{:S(2)}) collective-permute-start(bf16[64,512]{1,0:T(8,128)(2,1)S(1)} %dynamic-slice_convert_fusion.5), channel_id=1, source_target_pairs={{0,2},{2,0},{4,6},{6,4},{8,10},{10,8},{12,14},{14,12},{1,3},{3,1},... | collective-permute-start | bytes 196616 | tf_op jit(solution)/shard_map/ppermute | solution.py:211
  30.0 1.0 %collective-permute-done.6 = bf16[64,512]{1,0:T(8,128)(2,1)S(1)} collective-permute-done((bf16[64,512]{1,0:T(8,128)(2,1)S(1)}, bf16[64,512]{1,0:T(8,128)(2,1)S(1)}, u32[]{:S(2)}, u32[]{:S(2)}) %collective-permute-start.6) | collective-permute-done | bytes 65568 | tf_op jit(solution)/shard_map/ppermute | solution.py:211
  31.0 0.5 collective-permute-start.9
  31.5 0.9 %collective-permute-done.5 = bf16[64,512]{1,0:T(8,128)(2,1)S(1)} collective-permute-done((bf16[64,512]{1,0:T(8,128)(2,1)S(1)}, bf16[64,512]{1,0:T(8,128)(2,1)S(1)}, u32[]{:S(2)}, u32[]{:S(2)}) %collective-permute-start.5) | collective-permute-done | bytes 65568 | tf_op jit(solution)/shard_map/ppermute | solution.py:211
  32.4 1.0 %collective-permute-start.12 = (bf16[64,512]{1,0:T(8,128)(2,1)S(1)}, bf16[64,512]{1,0:T(8,128)(2,1)S(1)}, u32[]{:S(2)}, u32[]{:S(2)}) collective-permute-start(bf16[64,512]{1,0:T(8,128)(2,1)S(1)} %add_convert_fusion.2), channel_id=1, source_target_pairs={{0,2},{2,0},{4,6},{6,4},{8,10},{10,8},{12,14},{14,12},{1,3},{3,1},... | collective-permute-start | bytes 196616 | tf_op jit(solution)/shard_map/ppermute | solution.py:211
  33.5 0.0 collective-permute-done.10
  33.5 1.6 %collective-permute-start.18 = (bf16[64,512]{1,0:T(8,128)(2,1)S(1)}, bf16[64,512]{1,0:T(8,128)(2,1)S(1)}, u32[]{:S(2)}, u32[]{:S(2)}) collective-permute-start(bf16[64,512]{1,0:T(8,128)(2,1)S(1)} %add_convert_fusion.3), channel_id=1, source_target_pairs={{0,8},{2,10},{4,12},{6,14},{8,0},{10,2},{12,4},{14,6},{1,9},{3,11}... | collective-permute-start | bytes 196616 | tf_op jit(solution)/shard_map/ppermute | solution.py:211
  35.1 0.0 collective-permute-done.11
  35.1 1.5 %collective-permute-start.15 = (bf16[64,512]{1,0:T(8,128)(2,1)S(1)}, bf16[64,512]{1,0:T(8,128)(2,1)S(1)}, u32[]{:S(2)}, u32[]{:S(2)}) collective-permute-start(bf16[64,512]{1,0:T(8,128)(2,1)S(1)} %add_convert_fusion.4), channel_id=1, source_target_pairs={{0,8},{2,10},{4,12},{6,14},{8,0},{10,2},{12,4},{14,6},{1,9},{3,11}... | collective-permute-start | bytes 196616 | tf_op jit(solution)/shard_map/ppermute | solution.py:211
  36.6 0.0 collective-permute-done.9
  36.6 1.1 %collective-permute-start.14 = (bf16[128,512]{1,0:T(8,128)(2,1)S(1)}, bf16[128,512]{1,0:T(8,128)(2,1)S(1)}, u32[]{:S(2)}, u32[]{:S(2)}) collective-permute-start(bf16[128,512]{1,0:T(8,128)(2,1)S(1)} %pad_maximum_fusion.1), channel_id=1, source_target_pairs={{0,2},{2,0},{4,6},{6,4},{8,10},{10,8},{12,14},{14,12},{1,3},{3,1},... | collective-permute-start | bytes 393224 | tf_op jit(solution)/shard_map/ppermute | solution.py:211
  37.7 0.0 collective-permute-done.12
  37.8 0.8 %collective-permute-start.13 = (bf16[128,512]{1,0:T(8,128)(2,1)S(1)}, bf16[128,512]{1,0:T(8,128)(2,1)S(1)}, u32[]{:S(2)}, u32[]{:S(2)}) collective-permute-start(bf16[128,512]{1,0:T(8,128)(2,1)S(1)} %pad_maximum_fusion), channel_id=1, source_target_pairs={{0,4},{2,6},{4,0},{6,2},{8,12},{10,14},{12,8},{14,10},{1,5},{3,7},... | collective-permute-start | bytes 393224 | tf_op jit(solution)/shard_map/ppermute | solution.py:211
  38.6 0.7 %collective-permute-done.18 = bf16[64,512]{1,0:T(8,128)(2,1)S(1)} collective-permute-done((bf16[64,512]{1,0:T(8,128)(2,1)S(1)}, bf16[64,512]{1,0:T(8,128)(2,1)S(1)}, u32[]{:S(2)}, u32[]{:S(2)}) %collective-permute-start.18) | collective-permute-done | bytes 65568 | tf_op jit(solution)/shard_map/ppermute | solution.py:211
  39.3 0.9 %collective-permute-start.19 = (bf16[64,512]{1,0:T(8,128)(2,1)S(1)}, bf16[64,512]{1,0:T(8,128)(2,1)S(1)}, u32[]{:S(2)}, u32[]{:S(2)}) collective-permute-start(bf16[64,512]{1,0:T(8,128)(2,1)S(1)} %add_convert_fusion), channel_id=1, source_target_pairs={{0,4},{2,6},{4,0},{6,2},{8,12},{10,14},{12,8},{14,10},{1,5},{3,7},... | collective-permute-start | bytes 196616 | tf_op jit(solution)/shard_map/ppermute | solution.py:211
  40.2 0.7 %collective-permute-done.15 = bf16[64,512]{1,0:T(8,128)(2,1)S(1)} collective-permute-done((bf16[64,512]{1,0:T(8,128)(2,1)S(1)}, bf16[64,512]{1,0:T(8,128)(2,1)S(1)}, u32[]{:S(2)}, u32[]{:S(2)}) %collective-permute-start.15) | collective-permute-done | bytes 65568 | tf_op jit(solution)/shard_map/ppermute | solution.py:211
  40.9 0.8 %collective-permute-start.16 = (bf16[64,512]{1,0:T(8,128)(2,1)S(1)}, bf16[64,512]{1,0:T(8,128)(2,1)S(1)}, u32[]{:S(2)}, u32[]{:S(2)}) collective-permute-start(bf16[64,512]{1,0:T(8,128)(2,1)S(1)} %add_convert_fusion.1), channel_id=1, source_target_pairs={{0,2},{2,0},{4,6},{6,4},{8,10},{10,8},{12,14},{14,12},{1,3},{3,1},... | collective-permute-start | bytes 196616 | tf_op jit(solution)/shard_map/ppermute | solution.py:211
  41.7 2.0 %collective-permute-done.19 = bf16[64,512]{1,0:T(8,128)(2,1)S(1)} collective-permute-done((bf16[64,512]{1,0:T(8,128)(2,1)S(1)}, bf16[64,512]{1,0:T(8,128)(2,1)S(1)}, u32[]{:S(2)}, u32[]{:S(2)}) %collective-permute-start.19) | collective-permute-done | bytes 65568 | tf_op jit(solution)/shard_map/ppermute | solution.py:211
  43.7 1.1 %collective-permute-start.20 = (bf16[128,512]{1,0:T(8,128)(2,1)S(1)}, bf16[128,512]{1,0:T(8,128)(2,1)S(1)}, u32[]{:S(2)}, u32[]{:S(2)}) collective-permute-start(bf16[128,512]{1,0:T(8,128)(2,1)S(1)} %pad_maximum_fusion.3), channel_id=1, source_target_pairs={{0,2},{2,0},{4,6},{6,4},{8,10},{10,8},{12,14},{14,12},{1,3},{3,1},... | collective-permute-start | bytes 393224 | tf_op jit(solution)/shard_map/ppermute | solution.py:211
  44.8 1.1 %collective-permute-done.16 = bf16[64,512]{1,0:T(8,128)(2,1)S(1)} collective-permute-done((bf16[64,512]{1,0:T(8,128)(2,1)S(1)}, bf16[64,512]{1,0:T(8,128)(2,1)S(1)}, u32[]{:S(2)}, u32[]{:S(2)}) %collective-permute-start.16) | collective-permute-done | bytes 65568 | tf_op jit(solution)/shard_map/ppermute | solution.py:211
  45.9 0.6 %collective-permute-start.17 = (bf16[128,512]{1,0:T(8,128)(2,1)S(1)}, bf16[128,512]{1,0:T(8,128)(2,1)S(1)}, u32[]{:S(2)}, u32[]{:S(2)}) collective-permute-start(bf16[128,512]{1,0:T(8,128)(2,1)S(1)} %pad_maximum_fusion.2), channel_id=1, source_target_pairs={{0,4},{2,6},{4,0},{6,2},{8,12},{10,14},{12,8},{14,10},{1,5},{3,7},... | collective-permute-start | bytes 393224 | tf_op jit(solution)/shard_map/ppermute | solution.py:211
  46.5 0.0 collective-permute-done.14
  46.6 0.0 collective-permute-done.13
  46.6 0.0 copy-start.3
  46.6 0.0 copy-start.4
  46.7 0.1 broadcast_in_dim.2
  46.9 1.9 %collective-permute-done.20 = bf16[128,512]{1,0:T(8,128)(2,1)S(1)} collective-permute-done((bf16[128,512]{1,0:T(8,128)(2,1)S(1)}, bf16[128,512]{1,0:T(8,128)(2,1)S(1)}, u32[]{:S(2)}, u32[]{:S(2)}) %collective-permute-start.20) | collective-permute-done | bytes 131104 | tf_op jit(solution)/shard_map/ppermute | solution.py:211
  48.8 2.1 %collective-permute-done.17 = bf16[128,512]{1,0:T(8,128)(2,1)S(1)} collective-permute-done((bf16[128,512]{1,0:T(8,128)(2,1)S(1)}, bf16[128,512]{1,0:T(8,128)(2,1)S(1)}, u32[]{:S(2)}, u32[]{:S(2)}) %collective-permute-start.17) | collective-permute-done | bytes 131104 | tf_op jit(solution)/shard_map/ppermute | solution.py:211
  51.0 0.0 copy-done.3
  51.0 0.0 copy-done.4
  51.0 0.0 copy-start
  51.0 1.1 %convolution_convert_fusion = bf16[128,1024]{1,0:T(8,128)(2,1)} fusion(bf16[512,1024]{1,0:T(8,128)(2,1)S(1)} %maximum_dynamic-update-slice_fusion.3, s32[512]{0:T(512)S(1)} %copy-done.3, s32[128]{0:T(128)S(1)} %copy-done.4), kind=kOutput, calls=%fused_computation | convolution fusion | flops 134742016 | bytes 1313280 | tf_op jit(solution)/shard_map/dot_general | solution.py:347
  52.1 0.0 copy-done
  (35 shorter events, 0.8 us)
Async XLA Ops:
  0.6 11.9 %collective-permute-start.1 = (bf16[1,256,4096]{2,1,0:T(8,128)(2,1)}, bf16[1,256,4096]{2,1,0:T(8,128)(2,1)S(1)}, u32[]{:S(2)}, u32[]{:S(2)}) collective-permute-start(bf16[1,256,4096]{2,1,0:T(8,128)(2,1)} %rows_ref.1), channel_id=1, source_target_pairs={{1,0},{0,1},{3,2},{2,3},{5,4},{4,5},{7,6},{6,7},{9,8},{8,9},{11,10... | collective-permute-start | bytes 6291464 | tf_op jit(solution)/shard_map/ppermute | solution.py:317
  8.3 2.8 %copy-start.1 = (f32[256,512]{1,0:T(8,128)}, f32[256,512]{1,0:T(8,128)S(1)}, u32[]{:S(2)}) copy-start(f32[256,512]{1,0:T(8,128)S(1)} %get-tuple-element.119) | copy-start | bytes 1572868
  8.3 10.0 %collective-permute-start = (bf16[128,512]{1,0:T(8,128)(2,1)S(1)}, bf16[128,512]{1,0:T(8,128)(2,1)S(1)}, u32[]{:S(2)}, u32[]{:S(2)}) collective-permute-start(bf16[128,512]{1,0:T(8,128)(2,1)S(1)} %get-tuple-element.60.refs_0_), channel_id=1, source_target_pairs={{0,4},{2,6},{4,0},{6,2},{8,12},{10,14},{12,8},{14,10},{1,5},{3,7},... | collective-permute-start | bytes 393224 | tf_op jit(solution)/shard_map/ppermute | solution.py:211
  11.0 7.7 %collective-permute-start.3 = (bf16[128,512]{1,0:T(8,128)(2,1)S(1)}, bf16[128,512]{1,0:T(8,128)(2,1)S(1)}, u32[]{:S(2)}, u32[]{:S(2)}) collective-permute-start(bf16[128,512]{1,0:T(8,128)(2,1)S(1)} %get-tuple-element.66.refs_1_), channel_id=1, source_target_pairs={{0,2},{2,0},{4,6},{6,4},{8,10},{10,8},{12,14},{14,12},{1,3},{3,1},... | collective-permute-start | bytes 393224 | tf_op jit(solution)/shard_map/ppermute | solution.py:211
  17.6 1.0 %copy-start.2 = (f32[256,512]{1,0:T(8,128)S(1)}, f32[256,512]{1,0:T(8,128)}, u32[]{:S(2)}) copy-start(f32[256,512]{1,0:T(8,128)} %copy-done.1) | copy-start | bytes 1572868
  17.7 10.2 %collective-permute-start.7 = (bf16[128,512]{1,0:T(8,128)(2,1)S(1)}, bf16[128,512]{1,0:T(8,128)(2,1)S(1)}, u32[]{:S(2)}, u32[]{:S(2)}) collective-permute-start(bf16[128,512]{1,0:T(8,128)(2,1)S(1)} %dynamic-slice_convert_fusion.1), channel_id=1, source_target_pairs={{0,2},{2,0},{4,6},{6,4},{8,10},{10,8},{12,14},{14,12},{1,3},{3,1},... | collective-permute-start | bytes 393224 | tf_op jit(solution)/shard_map/ppermute | solution.py:211
  18.8 5.0 %collective-permute-start.4 = (bf16[64,512]{1,0:T(8,128)(2,1)S(1)}, bf16[64,512]{1,0:T(8,128)(2,1)S(1)}, u32[]{:S(2)}, u32[]{:S(2)}) collective-permute-start(bf16[64,512]{1,0:T(8,128)(2,1)S(1)} %dynamic-slice_convert_fusion.6), channel_id=1, source_target_pairs={{0,4},{2,6},{4,0},{6,2},{8,12},{10,14},{12,8},{14,10},{1,5},{3,7},... | collective-permute-start | bytes 196616 | tf_op jit(solution)/shard_map/ppermute | solution.py:211
  19.5 9.2 %collective-permute-start.8 = (bf16[128,512]{1,0:T(8,128)(2,1)S(1)}, bf16[128,512]{1,0:T(8,128)(2,1)S(1)}, u32[]{:S(2)}, u32[]{:S(2)}) collective-permute-start(bf16[128,512]{1,0:T(8,128)(2,1)S(1)} %dynamic-slice_convert_fusion), channel_id=1, source_target_pairs={{0,4},{2,6},{4,0},{6,2},{8,12},{10,14},{12,8},{14,10},{1,5},{3,7},... | collective-permute-start | bytes 393224 | tf_op jit(solution)/shard_map/ppermute | solution.py:211
  20.9 5.5 %collective-permute-start.2 = (bf16[64,512]{1,0:T(8,128)(2,1)S(1)}, bf16[64,512]{1,0:T(8,128)(2,1)S(1)}, u32[]{:S(2)}, u32[]{:S(2)}) collective-permute-start(bf16[64,512]{1,0:T(8,128)(2,1)S(1)} %dynamic-slice_convert_fusion.7), channel_id=1, source_target_pairs={{0,2},{2,0},{4,6},{6,4},{8,10},{10,8},{12,14},{14,12},{1,3},{3,1},... | collective-permute-start | bytes 196616 | tf_op jit(solution)/shard_map/ppermute | solution.py:211
  23.8 7.2 %collective-permute-start.6 = (bf16[64,512]{1,0:T(8,128)(2,1)S(1)}, bf16[64,512]{1,0:T(8,128)(2,1)S(1)}, u32[]{:S(2)}, u32[]{:S(2)}) collective-permute-start(bf16[64,512]{1,0:T(8,128)(2,1)S(1)} %add_convert_fusion.7), channel_id=1, source_target_pairs={{0,8},{2,10},{4,12},{6,14},{8,0},{10,2},{12,4},{14,6},{1,9},{3,11}... | collective-permute-start | bytes 196616 | tf_op jit(solution)/shard_map/ppermute | solution.py:211
  26.5 5.9 %collective-permute-start.5 = (bf16[64,512]{1,0:T(8,128)(2,1)S(1)}, bf16[64,512]{1,0:T(8,128)(2,1)S(1)}, u32[]{:S(2)}, u32[]{:S(2)}) collective-permute-start(bf16[64,512]{1,0:T(8,128)(2,1)S(1)} %add_convert_fusion.6), channel_id=1, source_target_pairs={{0,8},{2,10},{4,12},{6,14},{8,0},{10,2},{12,4},{14,6},{1,9},{3,11}... | collective-permute-start | bytes 196616 | tf_op jit(solution)/shard_map/ppermute | solution.py:211
  27.9 5.5 %collective-permute-start.10 = (bf16[64,512]{1,0:T(8,128)(2,1)S(1)}, bf16[64,512]{1,0:T(8,128)(2,1)S(1)}, u32[]{:S(2)}, u32[]{:S(2)}) collective-permute-start(bf16[64,512]{1,0:T(8,128)(2,1)S(1)} %dynamic-slice_convert_fusion.4), channel_id=1, source_target_pairs={{0,4},{2,6},{4,0},{6,2},{8,12},{10,14},{12,8},{14,10},{1,5},{3,7},... | collective-permute-start | bytes 196616 | tf_op jit(solution)/shard_map/ppermute | solution.py:211
  28.7 6.3 %collective-permute-start.11 = (bf16[64,512]{1,0:T(8,128)(2,1)S(1)}, bf16[64,512]{1,0:T(8,128)(2,1)S(1)}, u32[]{:S(2)}, u32[]{:S(2)}) collective-permute-start(bf16[64,512]{1,0:T(8,128)(2,1)S(1)} %dynamic-slice_convert_fusion.5), channel_id=1, source_target_pairs={{0,2},{2,0},{4,6},{6,4},{8,10},{10,8},{12,14},{14,12},{1,3},{3,1},... | collective-permute-start | bytes 196616 | tf_op jit(solution)/shard_map/ppermute | solution.py:211
  31.0 5.6 %collective-permute-start.9 = (bf16[64,512]{1,0:T(8,128)(2,1)S(1)}, bf16[64,512]{1,0:T(8,128)(2,1)S(1)}, u32[]{:S(2)}, u32[]{:S(2)}) collective-permute-start(bf16[64,512]{1,0:T(8,128)(2,1)S(1)} %add_convert_fusion.5), channel_id=1, source_target_pairs={{0,4},{2,6},{4,0},{6,2},{8,12},{10,14},{12,8},{14,10},{1,5},{3,7},... | collective-permute-start | bytes 196616 | tf_op jit(solution)/shard_map/ppermute | solution.py:211
  32.4 5.3 %collective-permute-start.12 = (bf16[64,512]{1,0:T(8,128)(2,1)S(1)}, bf16[64,512]{1,0:T(8,128)(2,1)S(1)}, u32[]{:S(2)}, u32[]{:S(2)}) collective-permute-start(bf16[64,512]{1,0:T(8,128)(2,1)S(1)} %add_convert_fusion.2), channel_id=1, source_target_pairs={{0,2},{2,0},{4,6},{6,4},{8,10},{10,8},{12,14},{14,12},{1,3},{3,1},... | collective-permute-start | bytes 196616 | tf_op jit(solution)/shard_map/ppermute | solution.py:211
  33.5 5.8 %collective-permute-start.18 = (bf16[64,512]{1,0:T(8,128)(2,1)S(1)}, bf16[64,512]{1,0:T(8,128)(2,1)S(1)}, u32[]{:S(2)}, u32[]{:S(2)}) collective-permute-start(bf16[64,512]{1,0:T(8,128)(2,1)S(1)} %add_convert_fusion.3), channel_id=1, source_target_pairs={{0,8},{2,10},{4,12},{6,14},{8,0},{10,2},{12,4},{14,6},{1,9},{3,11}... | collective-permute-start | bytes 196616 | tf_op jit(solution)/shard_map/ppermute | solution.py:211
  35.1 5.8 %collective-permute-start.15 = (bf16[64,512]{1,0:T(8,128)(2,1)S(1)}, bf16[64,512]{1,0:T(8,128)(2,1)S(1)}, u32[]{:S(2)}, u32[]{:S(2)}) collective-permute-start(bf16[64,512]{1,0:T(8,128)(2,1)S(1)} %add_convert_fusion.4), channel_id=1, source_target_pairs={{0,8},{2,10},{4,12},{6,14},{8,0},{10,2},{12,4},{14,6},{1,9},{3,11}... | collective-permute-start | bytes 196616 | tf_op jit(solution)/shard_map/ppermute | solution.py:211
  36.6 9.9 %collective-permute-start.14 = (bf16[128,512]{1,0:T(8,128)(2,1)S(1)}, bf16[128,512]{1,0:T(8,128)(2,1)S(1)}, u32[]{:S(2)}, u32[]{:S(2)}) collective-permute-start(bf16[128,512]{1,0:T(8,128)(2,1)S(1)} %pad_maximum_fusion.1), channel_id=1, source_target_pairs={{0,2},{2,0},{4,6},{6,4},{8,10},{10,8},{12,14},{14,12},{1,3},{3,1},... | collective-permute-start | bytes 393224 | tf_op jit(solution)/shard_map/ppermute | solution.py:211
  37.8 8.8 %collective-permute-start.13 = (bf16[128,512]{1,0:T(8,128)(2,1)S(1)}, bf16[128,512]{1,0:T(8,128)(2,1)S(1)}, u32[]{:S(2)}, u32[]{:S(2)}) collective-permute-start(bf16[128,512]{1,0:T(8,128)(2,1)S(1)} %pad_maximum_fusion), channel_id=1, source_target_pairs={{0,4},{2,6},{4,0},{6,2},{8,12},{10,14},{12,8},{14,10},{1,5},{3,7},... | collective-permute-start | bytes 393224 | tf_op jit(solution)/shard_map/ppermute | solution.py:211
  39.3 4.3 %collective-permute-start.19 = (bf16[64,512]{1,0:T(8,128)(2,1)S(1)}, bf16[64,512]{1,0:T(8,128)(2,1)S(1)}, u32[]{:S(2)}, u32[]{:S(2)}) collective-permute-start(bf16[64,512]{1,0:T(8,128)(2,1)S(1)} %add_convert_fusion), channel_id=1, source_target_pairs={{0,4},{2,6},{4,0},{6,2},{8,12},{10,14},{12,8},{14,10},{1,5},{3,7},... | collective-permute-start | bytes 196616 | tf_op jit(solution)/shard_map/ppermute | solution.py:211
  40.9 5.0 %collective-permute-start.16 = (bf16[64,512]{1,0:T(8,128)(2,1)S(1)}, bf16[64,512]{1,0:T(8,128)(2,1)S(1)}, u32[]{:S(2)}, u32[]{:S(2)}) collective-permute-start(bf16[64,512]{1,0:T(8,128)(2,1)S(1)} %add_convert_fusion.1), channel_id=1, source_target_pairs={{0,2},{2,0},{4,6},{6,4},{8,10},{10,8},{12,14},{14,12},{1,3},{3,1},... | collective-permute-start | bytes 196616 | tf_op jit(solution)/shard_map/ppermute | solution.py:211
  43.7 5.0 %collective-permute-start.20 = (bf16[128,512]{1,0:T(8,128)(2,1)S(1)}, bf16[128,512]{1,0:T(8,128)(2,1)S(1)}, u32[]{:S(2)}, u32[]{:S(2)}) collective-permute-start(bf16[128,512]{1,0:T(8,128)(2,1)S(1)} %pad_maximum_fusion.3), channel_id=1, source_target_pairs={{0,2},{2,0},{4,6},{6,4},{8,10},{10,8},{12,14},{14,12},{1,3},{3,1},... | collective-permute-start | bytes 393224 | tf_op jit(solution)/shard_map/ppermute | solution.py:211
  45.9 5.0 %collective-permute-start.17 = (bf16[128,512]{1,0:T(8,128)(2,1)S(1)}, bf16[128,512]{1,0:T(8,128)(2,1)S(1)}, u32[]{:S(2)}, u32[]{:S(2)}) collective-permute-start(bf16[128,512]{1,0:T(8,128)(2,1)S(1)} %pad_maximum_fusion.2), channel_id=1, source_target_pairs={{0,4},{2,6},{4,0},{6,2},{8,12},{10,14},{12,8},{14,10},{1,5},{3,7},... | collective-permute-start | bytes 393224 | tf_op jit(solution)/shard_map/ppermute | solution.py:211
  46.6 4.4 %copy-start.3 = (s32[512]{0:T(512)S(1)}, s32[512]{0:T(512)}, u32[]{:S(2)}) copy-start(s32[512]{0:T(512)} %param.10) | copy-start | bytes 6148
  46.6 4.4 %copy-start.4 = (s32[128]{0:T(128)S(1)}, s32[128]{0:T(128)}, u32[]{:S(2)}) copy-start(s32[128]{0:T(128)} %param.11) | copy-start | bytes 1540
  51.0 1.1 %copy-start = (bf16[512,1024]{1,0:T(8,128)(2,1)}, bf16[512,1024]{1,0:T(8,128)(2,1)S(1)}, u32[]{:S(2)}) copy-start(bf16[512,1024]{1,0:T(8,128)(2,1)S(1)} %maximum_dynamic-update-slice_fusion.3) | copy-start | bytes 3145732

commit v24 on v22

--- a/solution.py
+++ b/solution.py
@@ -237,7 +237,7 @@
         if not halved:
             self.block = block.astype(jnp.bfloat16)
 
-    def send(self, order):
+    def piece(self):
         bit, kind = self.moves[0]
         sent = self.block
         if kind == HALVE:
@@ -246,8 +246,7 @@
             sent = lax.dynamic_slice_in_dim(self.block, (1 - upper) * rows, rows, 0)
             sent = sent.astype(jnp.bfloat16)
             self.block = lax.dynamic_slice_in_dim(self.block, upper * rows, rows, 0)
-        self.sent = order.mark(sent)
-        self.received = swap(self.sent, bit)
+        return sent
 
     def bytes_of_move(self):
         size = self.block.size
@@ -287,14 +286,15 @@
         self.links = {}
         self.arrivals = {}
 
-    def send(self, chunk):
-        bit, _ = chunk.moves[0]
+    def send(self, chunks):
+        bit, _ = chunks[0].moves[0]
         far = bit > 2
         self.now += FAR_START_US if far else NEAR_START_US
         begin = max(self.now, self.links.get(bit, 0.0))
-        end = begin + chunk.bytes_of_move() / (FAR_BYTES_PER_US if far else NEAR_BYTES_PER_US)
+        end = begin + sum(c.bytes_of_move() for c in chunks) / (FAR_BYTES_PER_US if far else NEAR_BYTES_PER_US)
         self.links[bit] = end
-        self.arrivals[chunk] = end + (2 * LATENCY_US if far else LATENCY_US)
+        for chunk in chunks:
+            self.arrivals[chunk] = end + (2 * LATENCY_US if far else LATENCY_US)
 
     def next(self):
         there = [chunk for chunk, at in self.arrivals.items() if at <= self.now]
@@ -304,10 +304,17 @@
         self.now = max(self.now, self.arrivals.pop(chunk))
 
 
-def send(chunk, order, clock):
-    if chunk.moves:
-        clock.send(chunk)
-        chunk.send(order)
+def send(chunks, order, clock):
+    if not chunks[0].moves:
+        return
+    clock.send(chunks)
+    pieces = [chunk.piece() for chunk in chunks]
+    sent = order.mark(jnp.concatenate(pieces, 0) if len(pieces) > 1 else pieces[0])
+    received, first = swap(sent, chunks[0].moves[0][0]), 0
+    for chunk, piece in zip(chunks, pieces):
+        chunk.sent = sent
+        chunk.received = received[first : first + piece.shape[0]]
+        first += piece.shape[0]
 
 
 def shards(store, queries, left_inv, right_inv, query_prompt, winner):
@@ -334,20 +341,29 @@
             for chunk in chunks:
                 clock.take(chunk)
                 chunk.take(order)
-                send(chunk, order, clock)
+        waiting = list(chunks)
         choices = ORDERS[min(step, len(ORDERS) - 1)]
         width = columns // len(choices)
         for number, (choice, exchanges) in enumerate(choices):
             first = number * width
             chunk = LayerSum(part[:, first : first + width], orders[choice], index, exchanges)
-            send(chunk, order, clock)
+            partners = [
+                early
+                for early in waiting
+                if early.moves and early.moves[0] == chunk.moves[0]
+                and early.block.shape[1] == chunk.block.shape[1]
+            ][:1]
+            send([chunk] + partners, order, clock)
+            waiting = [early for early in waiting if early not in partners]
             chunks.append(chunk)
             places.append(((position - step) % ex_count * rows, jnp.int32(first)))
+        for early in waiting:
+            send([early], order, clock)
     while clock.arrivals:
         chunk = clock.next()
         clock.take(chunk)
         chunk.take(order)
-        send(chunk, order, clock)
+        send([chunk], order, clock)
     done = [chunk.block for chunk in chunks]
     scores = jnp.zeros((rows * ex_count, columns), jnp.bfloat16)
     for place, block in zip(places, done):

time: 51.9 us -> 54 us (1.040)
  waiting for transfers between devices: 11.9 us -> 17.7 us
  starting transfers between devices: 24.6 us -> 19.4 us
  local copies, waits for them, and re-layouts: 0.8 us -> 2.16 us
    ppermute x20 -> x18, waiting for transfers between devices: 11.9 us -> 17.7 us  [swap(): return lax.ppermute(block, 'layer', route)]
    ppermute x20 -> x18, starting transfers between devices: 24.1 us -> 18.9 us  [swap(): return lax.ppermute(block, 'layer', route)]
    unnamed x10, local copies, waits for them, and re-layouts: 0.37 us -> 1.7 us
  transfers between devices with their start and end apart: 21 -> 19, of which waited for: 9 -> 11; matrix products, arithmetic and copies ran while one was open for 2% -> 2% of each run, Pallas kernels for 23% -> 22%
where the time goes in v24:
time: 54 us; the launch traced here: 53.8 us
  starting transfers between devices  19.4 us (36%)
  waiting for transfers between devices  17.7 us (33%)
  Pallas kernels  11.7 us (22%)
  local copies, waits for them, and re-layouts  2.16 us (4%)
  matrix products  1.08 us (2%)
  between operations  1 us (2%)
  other arithmetic  0.7 us (1%)
    ppermute x18, starting transfers between devices, swap(): return lax.ppermute(block, 'layer', route)  18.9 us
    ppermute x18, waiting for transfers between devices, swap(): return lax.ppermute(block, 'layer', route)  17.7 us
    pallas_call x2, Pallas kernels, call(): pl.pallas_call(kernel, out_shape=(jax.ShapeDtypeStruct((count, examples),...  11.7 us
    unnamed x10, local copies, waits for them, and re-layouts  1.7 us
    dot_general x1, matrix products, shards(): advantage = jnp.dot(weights, scores, preferred_element_type=jnp.float32)  1.08 us
  transfers between devices with their start and end apart: 19, of which 11 were waited for; matrix products, arithmetic and copies ran while one was open for 2% of the time, Pallas kernels for 22%

profile of v24, /device:TPU:0, one launch (start us, length us, event | category | flops | bytes accessed | tf_op | source)
XLA Modules:
  0.0 53.8 jit_solution(15661978903539997551)
XLA Ops:
  0.6 0.5 collective-permute-start.1
  1.1 6.6 %shard_map.77 = (f32[256,1024]{1,0:T(8,128)S(1)}, bf16[256,256]{1,0:T(8,128)(2,1)S(1)}, bf16[256,256]{1,0:T(8,128)(2,1)S(1)}) custom-call(bf16[1,256,4096]{2,1,0:T(8,128)(2,1)} %rows_ref.1, bf16[1,32,32]{2,1,0:T(8,128)(2,1)} %left_ref.1, bf16[1,128,128]{2,1,0:T(8,128)(2,1)} %right_ref.1, bf16[1,1024,4096]{2,1,0:T(8,128)(2,1)} %store_ref.3), custom_call_target="tpu_custom_call" | custom-call | flops 4294967296 | bytes 10485760 | tf_op jit(solution)/shard_map/pallas_call | solution.py:173
  7.8 0.1 fusion.7
  7.9 0.0 copy-start.1
  7.9 0.8 %copy-done.1 = f32[256,512]{1,0:T(8,128)} copy-done((f32[256,512]{1,0:T(8,128)}, f32[256,512]{1,0:T(8,128)S(1)}, u32[]{:S(2)}) %copy-start.1) | copy-done | bytes 524312
  8.7 2.7 %collective-permute-start = (bf16[128,512]{1,0:T(8,128)(2,1)S(1)}, bf16[128,512]{1,0:T(8,128)(2,1)S(1)}, u32[]{:S(2)}, u32[]{:S(2)}) collective-permute-start(bf16[128,512]{1,0:T(8,128)(2,1)S(1)} %dynamic-slice_convert_fusion.3.refs_0_), channel_id=1, source_target_pairs={{0,4},{2,6},{4,0},{6,2},{8,12},{10,14},{12,8},{14,10},{1,5},{3,7},... | collective-permute-start | bytes 393224 | tf_op jit(solution)/shard_map/ppermute | solution.py:224
  11.4 1.6 %collective-permute-start.2 = (bf16[128,512]{1,0:T(8,128)(2,1)S(1)}, bf16[128,512]{1,0:T(8,128)(2,1)S(1)}, u32[]{:S(2)}, u32[]{:S(2)}) collective-permute-start(bf16[128,512]{1,0:T(8,128)(2,1)S(1)} %dynamic-slice_convert_fusion.2.refs_1_), channel_id=1, source_target_pairs={{0,2},{2,0},{4,6},{6,4},{8,10},{10,8},{12,14},{14,12},{1,3},{3,1},... | collective-permute-start | bytes 393224 | tf_op jit(solution)/shard_map/ppermute | solution.py:224
  13.0 0.0 collective-permute-done.1.rows_ref
  13.0 5.1 %shard_map.78 = f32[256,1024]{1,0:T(8,128)S(1)} custom-call(bf16[1,256,4096]{2,1,0:T(8,128)(2,1)S(1)} %collective-permute-done.1.rows_ref, bf16[256,256]{1,0:T(8,128)(2,1)S(1)} %get-tuple-element.60.both_ref, bf16[256,256]{1,0:T(8,128)(2,1)S(1)} %get-tuple-element.61.mixer_ref, bf16[1,1024,4096]{2,1,0:T(8,128)(2,1)} %store_ref.3, ...), custom_call_target="tpu_custom_call" | custom-call | flops 4294967296 | bytes 10485760 | tf_op jit(solution)/shard_map/pallas_call | solution.py:173
  18.0 0.0 copy-start.2
  18.1 0.1 fusion.6
  18.1 0.0 collective-permute-done
  18.2 0.0 collective-permute-done.2
  18.2 0.9 %copy-done.2 = f32[256,512]{1,0:T(8,128)S(1)} copy-done((f32[256,512]{1,0:T(8,128)S(1)}, f32[256,512]{1,0:T(8,128)}, u32[]{:S(2)}) %copy-start.2) | copy-done | bytes 524312
  19.1 0.1 convert_add_fusion.2
  19.2 0.6 %collective-permute-start.3 = (bf16[192,512]{1,0:T(8,128)(2,1)S(1)}, bf16[192,512]{1,0:T(8,128)(2,1)S(1)}, u32[]{:S(2)}, u32[]{:S(2)}) collective-permute-start(bf16[192,512]{1,0:T(8,128)(2,1)S(1)} %pad_maximum_fusion), channel_id=1, source_target_pairs={{0,2},{2,0},{4,6},{6,4},{8,10},{10,8},{12,14},{14,12},{1,3},{3,1},... | collective-permute-start | bytes 589832 | tf_op jit(solution)/shard_map/ppermute | solution.py:224
  19.9 0.1 collective-permute-start.4
  20.0 6.0 %collective-permute-done.3 = bf16[192,512]{1,0:T(8,128)(2,1)S(1)} collective-permute-done((bf16[192,512]{1,0:T(8,128)(2,1)S(1)}, bf16[192,512]{1,0:T(8,128)(2,1)S(1)}, u32[]{:S(2)}, u32[]{:S(2)}) %collective-permute-start.3) | collective-permute-done | bytes 196640 | tf_op jit(solution)/shard_map/ppermute | solution.py:224
  26.1 0.5 collective-permute-start.6
  26.6 0.0 collective-permute-done.4
  26.7 1.3 %collective-permute-start.7 = (bf16[64,512]{1,0:T(8,128)(2,1)S(1)}, bf16[64,512]{1,0:T(8,128)(2,1)S(1)}, u32[]{:S(2)}, u32[]{:S(2)}) collective-permute-start(bf16[64,512]{1,0:T(8,128)(2,1)S(1)} %dynamic-slice_convert_fusion.5), channel_id=1, source_target_pairs={{0,2},{2,0},{4,6},{6,4},{8,10},{10,8},{12,14},{14,12},{1,3},{3,1},... | collective-permute-start | bytes 196616 | tf_op jit(solution)/shard_map/ppermute | solution.py:224
  28.1 2.7 %collective-permute-start.11 = (bf16[64,512]{1,0:T(8,128)(2,1)S(1)}, bf16[64,512]{1,0:T(8,128)(2,1)S(1)}, u32[]{:S(2)}, u32[]{:S(2)}) collective-permute-start(bf16[64,512]{1,0:T(8,128)(2,1)S(1)} %add_convert_fusion.5), channel_id=1, source_target_pairs={{0,8},{2,10},{4,12},{6,14},{8,0},{10,2},{12,4},{14,6},{1,9},{3,11}... | collective-permute-start | bytes 196616 | tf_op jit(solution)/shard_map/ppermute | solution.py:224
  30.7 0.4 collective-permute-start.5
  31.1 0.0 collective-permute-done.6
  31.2 2.7 %collective-permute-start.16 = (bf16[64,512]{1,0:T(8,128)(2,1)S(1)}, bf16[64,512]{1,0:T(8,128)(2,1)S(1)}, u32[]{:S(2)}, u32[]{:S(2)}) collective-permute-start(bf16[64,512]{1,0:T(8,128)(2,1)S(1)} %add_convert_fusion.4), channel_id=1, source_target_pairs={{0,8},{2,10},{4,12},{6,14},{8,0},{10,2},{12,4},{14,6},{1,9},{3,11}... | collective-permute-start | bytes 196616 | tf_op jit(solution)/shard_map/ppermute | solution.py:224
  33.8 0.0 collective-permute-done.7
  33.8 0.4 collective-permute-start.9
  34.2 4.0 %collective-permute-done.11 = bf16[64,512]{1,0:T(8,128)(2,1)S(1)} collective-permute-done((bf16[64,512]{1,0:T(8,128)(2,1)S(1)}, bf16[64,512]{1,0:T(8,128)(2,1)S(1)}, u32[]{:S(2)}, u32[]{:S(2)}) %collective-permute-start.11) | collective-permute-done | bytes 65568 | tf_op jit(solution)/shard_map/ppermute | solution.py:224
  38.2 0.1 collective-permute-start.12
  38.3 2.0 %collective-permute-done.5 = bf16[64,512]{1,0:T(8,128)(2,1)S(1)} collective-permute-done((bf16[64,512]{1,0:T(8,128)(2,1)S(1)}, bf16[64,512]{1,0:T(8,128)(2,1)S(1)}, u32[]{:S(2)}, u32[]{:S(2)}) %collective-permute-start.5) | collective-permute-done | bytes 65568 | tf_op jit(solution)/shard_map/ppermute | solution.py:224
  40.3 0.8 %collective-permute-start.8 = (bf16[64,512]{1,0:T(8,128)(2,1)S(1)}, bf16[64,512]{1,0:T(8,128)(2,1)S(1)}, u32[]{:S(2)}, u32[]{:S(2)}) collective-permute-start(bf16[64,512]{1,0:T(8,128)(2,1)S(1)} %add_convert_fusion.3), channel_id=1, source_target_pairs={{0,2},{2,0},{4,6},{6,4},{8,10},{10,8},{12,14},{14,12},{1,3},{3,1},... | collective-permute-start | bytes 196616 | tf_op jit(solution)/shard_map/ppermute | solution.py:224
  41.1 0.5 collective-permute-done.16
  41.6 0.1 collective-permute-start.17
  41.7 0.7 %collective-permute-done.9 = bf16[64,512]{1,0:T(8,128)(2,1)S(1)} collective-permute-done((bf16[64,512]{1,0:T(8,128)(2,1)S(1)}, bf16[64,512]{1,0:T(8,128)(2,1)S(1)}, u32[]{:S(2)}, u32[]{:S(2)}) %collective-permute-start.9) | collective-permute-done | bytes 65568 | tf_op jit(solution)/shard_map/ppermute | solution.py:224
  42.4 0.9 %collective-permute-start.14 = (bf16[64,512]{1,0:T(8,128)(2,1)S(1)}, bf16[64,512]{1,0:T(8,128)(2,1)S(1)}, u32[]{:S(2)}, u32[]{:S(2)}) collective-permute-start(bf16[64,512]{1,0:T(8,128)(2,1)S(1)} %add_convert_fusion.2), channel_id=1, source_target_pairs={{0,2},{2,0},{4,6},{6,4},{8,10},{10,8},{12,14},{14,12},{1,3},{3,1},... | collective-permute-start | bytes 196616 | tf_op jit(solution)/shard_map/ppermute | solution.py:224
  43.3 0.0 collective-permute-done.12
  43.3 1.2 %collective-permute-start.13 = (bf16[128,512]{1,0:T(8,128)(2,1)S(1)}, bf16[128,512]{1,0:T(8,128)(2,1)S(1)}, u32[]{:S(2)}, u32[]{:S(2)}) collective-permute-start(bf16[128,512]{1,0:T(8,128)(2,1)S(1)} %pad_maximum_fusion.3), channel_id=1, source_target_pairs={{0,2},{2,0},{4,6},{6,4},{8,10},{10,8},{12,14},{14,12},{1,3},{3,1},... | collective-permute-start | bytes 393224 | tf_op jit(solution)/shard_map/ppermute | solution.py:224
  44.6 0.4 collective-permute-done.8
  45.1 1.0 %collective-permute-start.10 = (bf16[128,512]{1,0:T(8,128)(2,1)S(1)}, bf16[128,512]{1,0:T(8,128)(2,1)S(1)}, u32[]{:S(2)}, u32[]{:S(2)}) collective-permute-start(bf16[128,512]{1,0:T(8,128)(2,1)S(1)} %pad_maximum_fusion.2), channel_id=1, source_target_pairs={{0,4},{2,6},{4,0},{6,2},{8,12},{10,14},{12,8},{14,10},{1,5},{3,7},... | collective-permute-start | bytes 393224 | tf_op jit(solution)/shard_map/ppermute | solution.py:224
  46.0 0.0 collective-permute-done.17
  46.1 0.9 %collective-permute-start.18 = (bf16[128,512]{1,0:T(8,128)(2,1)S(1)}, bf16[128,512]{1,0:T(8,128)(2,1)S(1)}, u32[]{:S(2)}, u32[]{:S(2)}) collective-permute-start(bf16[128,512]{1,0:T(8,128)(2,1)S(1)} %pad_maximum_fusion.5), channel_id=1, source_target_pairs={{0,2},{2,0},{4,6},{6,4},{8,10},{10,8},{12,14},{14,12},{1,3},{3,1},... | collective-permute-start | bytes 393224 | tf_op jit(solution)/shard_map/ppermute | solution.py:224
  47.0 0.5 collective-permute-done.14
  47.5 1.0 %collective-permute-start.15 = (bf16[128,512]{1,0:T(8,128)(2,1)S(1)}, bf16[128,512]{1,0:T(8,128)(2,1)S(1)}, u32[]{:S(2)}, u32[]{:S(2)}) collective-permute-start(bf16[128,512]{1,0:T(8,128)(2,1)S(1)} %pad_maximum_fusion.4), channel_id=1, source_target_pairs={{0,4},{2,6},{4,0},{6,2},{8,12},{10,14},{12,8},{14,10},{1,5},{3,7},... | collective-permute-start | bytes 393224 | tf_op jit(solution)/shard_map/ppermute | solution.py:224
  48.5 1.8 %collective-permute-done.13 = bf16[128,512]{1,0:T(8,128)(2,1)S(1)} collective-permute-done((bf16[128,512]{1,0:T(8,128)(2,1)S(1)}, bf16[128,512]{1,0:T(8,128)(2,1)S(1)}, u32[]{:S(2)}, u32[]{:S(2)}) %collective-permute-start.13) | collective-permute-done | bytes 131104 | tf_op jit(solution)/shard_map/ppermute | solution.py:224
  50.3 0.7 %collective-permute-done.10 = bf16[128,512]{1,0:T(8,128)(2,1)S(1)} collective-permute-done((bf16[128,512]{1,0:T(8,128)(2,1)S(1)}, bf16[128,512]{1,0:T(8,128)(2,1)S(1)}, u32[]{:S(2)}, u32[]{:S(2)}) %collective-permute-start.10) | collective-permute-done | bytes 131104 | tf_op jit(solution)/shard_map/ppermute | solution.py:224
  51.0 0.0 copy-start.3
  51.0 0.0 copy-start.4
  51.1 0.1 broadcast_in_dim.2
  51.3 0.4 collective-permute-done.18
  51.7 0.8 %collective-permute-done.15 = bf16[128,512]{1,0:T(8,128)(2,1)S(1)} collective-permute-done((bf16[128,512]{1,0:T(8,128)(2,1)S(1)}, bf16[128,512]{1,0:T(8,128)(2,1)S(1)}, u32[]{:S(2)}, u32[]{:S(2)}) %collective-permute-start.15) | collective-permute-done | bytes 131104 | tf_op jit(solution)/shard_map/ppermute | solution.py:224
  52.7 0.0 copy-done.3
  52.7 0.0 copy-done.4
  52.7 0.0 copy-start
  52.7 1.1 %convolution_convert_fusion = bf16[128,1024]{1,0:T(8,128)(2,1)} fusion(bf16[512,1024]{1,0:T(8,128)(2,1)S(1)} %maximum_dynamic-update-slice_fusion.3, s32[512]{0:T(512)S(1)} %copy-done.3, s32[128]{0:T(128)S(1)} %copy-done.4), kind=kOutput, calls=%fused_computation | convolution fusion | flops 134742016 | bytes 1313280 | tf_op jit(solution)/shard_map/dot_general | solution.py:376
  53.8 0.0 copy-done
  (40 shorter events, 0.8 us)
Async XLA Ops:
  0.6 12.4 %collective-permute-start.1 = (bf16[1,256,4096]{2,1,0:T(8,128)(2,1)}, bf16[1,256,4096]{2,1,0:T(8,128)(2,1)S(1)}, u32[]{:S(2)}, u32[]{:S(2)}) collective-permute-start(bf16[1,256,4096]{2,1,0:T(8,128)(2,1)} %rows_ref.1), channel_id=1, source_target_pairs={{1,0},{0,1},{3,2},{2,3},{5,4},{4,5},{7,6},{6,7},{9,8},{8,9},{11,10... | collective-permute-start | bytes 6291464 | tf_op jit(solution)/shard_map/ppermute | solution.py:337
  7.9 0.8 %copy-start.1 = (f32[256,512]{1,0:T(8,128)}, f32[256,512]{1,0:T(8,128)S(1)}, u32[]{:S(2)}) copy-start(f32[256,512]{1,0:T(8,128)S(1)} %get-tuple-element.111) | copy-start | bytes 1572868
  8.7 9.4 %collective-permute-start = (bf16[128,512]{1,0:T(8,128)(2,1)S(1)}, bf16[128,512]{1,0:T(8,128)(2,1)S(1)}, u32[]{:S(2)}, u32[]{:S(2)}) collective-permute-start(bf16[128,512]{1,0:T(8,128)(2,1)S(1)} %dynamic-slice_convert_fusion.3.refs_0_), channel_id=1, source_target_pairs={{0,4},{2,6},{4,0},{6,2},{8,12},{10,14},{12,8},{14,10},{1,5},{3,7},... | collective-permute-start | bytes 393224 | tf_op jit(solution)/shard_map/ppermute | solution.py:224
  11.4 6.8 %collective-permute-start.2 = (bf16[128,512]{1,0:T(8,128)(2,1)S(1)}, bf16[128,512]{1,0:T(8,128)(2,1)S(1)}, u32[]{:S(2)}, u32[]{:S(2)}) collective-permute-start(bf16[128,512]{1,0:T(8,128)(2,1)S(1)} %dynamic-slice_convert_fusion.2.refs_1_), channel_id=1, source_target_pairs={{0,2},{2,0},{4,6},{6,4},{8,10},{10,8},{12,14},{14,12},{1,3},{3,1},... | collective-permute-start | bytes 393224 | tf_op jit(solution)/shard_map/ppermute | solution.py:224
  18.0 1.0 %copy-start.2 = (f32[256,512]{1,0:T(8,128)S(1)}, f32[256,512]{1,0:T(8,128)}, u32[]{:S(2)}) copy-start(f32[256,512]{1,0:T(8,128)} %copy-done.1) | copy-start | bytes 1572868
  19.2 6.8 %collective-permute-start.3 = (bf16[192,512]{1,0:T(8,128)(2,1)S(1)}, bf16[192,512]{1,0:T(8,128)(2,1)S(1)}, u32[]{:S(2)}, u32[]{:S(2)}) collective-permute-start(bf16[192,512]{1,0:T(8,128)(2,1)S(1)} %pad_maximum_fusion), channel_id=1, source_target_pairs={{0,2},{2,0},{4,6},{6,4},{8,10},{10,8},{12,14},{14,12},{1,3},{3,1},... | collective-permute-start | bytes 589832 | tf_op jit(solution)/shard_map/ppermute | solution.py:224
  19.9 6.7 %collective-permute-start.4 = (bf16[192,512]{1,0:T(8,128)(2,1)S(1)}, bf16[192,512]{1,0:T(8,128)(2,1)S(1)}, u32[]{:S(2)}, u32[]{:S(2)}) collective-permute-start(bf16[192,512]{1,0:T(8,128)(2,1)S(1)} %pad_maximum_fusion.1), channel_id=1, source_target_pairs={{0,4},{2,6},{4,0},{6,2},{8,12},{10,14},{12,8},{14,10},{1,5},{3,7},... | collective-permute-start | bytes 589832 | tf_op jit(solution)/shard_map/ppermute | solution.py:224
  26.1 5.1 %collective-permute-start.6 = (bf16[64,512]{1,0:T(8,128)(2,1)S(1)}, bf16[64,512]{1,0:T(8,128)(2,1)S(1)}, u32[]{:S(2)}, u32[]{:S(2)}) collective-permute-start(bf16[64,512]{1,0:T(8,128)(2,1)S(1)} %dynamic-slice_convert_fusion.4), channel_id=1, source_target_pairs={{0,4},{2,6},{4,0},{6,2},{8,12},{10,14},{12,8},{14,10},{1,5},{3,7},... | collective-permute-start | bytes 196616 | tf_op jit(solution)/shard_map/ppermute | solution.py:224
  26.7 7.1 %collective-permute-start.7 = (bf16[64,512]{1,0:T(8,128)(2,1)S(1)}, bf16[64,512]{1,0:T(8,128)(2,1)S(1)}, u32[]{:S(2)}, u32[]{:S(2)}) collective-permute-start(bf16[64,512]{1,0:T(8,128)(2,1)S(1)} %dynamic-slice_convert_fusion.5), channel_id=1, source_target_pairs={{0,2},{2,0},{4,6},{6,4},{8,10},{10,8},{12,14},{14,12},{1,3},{3,1},... | collective-permute-start | bytes 196616 | tf_op jit(solution)/shard_map/ppermute | solution.py:224
  28.1 10.1 %collective-permute-start.11 = (bf16[64,512]{1,0:T(8,128)(2,1)S(1)}, bf16[64,512]{1,0:T(8,128)(2,1)S(1)}, u32[]{:S(2)}, u32[]{:S(2)}) collective-permute-start(bf16[64,512]{1,0:T(8,128)(2,1)S(1)} %add_convert_fusion.5), channel_id=1, source_target_pairs={{0,8},{2,10},{4,12},{6,14},{8,0},{10,2},{12,4},{14,6},{1,9},{3,11}... | collective-permute-start | bytes 196616 | tf_op jit(solution)/shard_map/ppermute | solution.py:224
  30.7 9.6 %collective-permute-start.5 = (bf16[64,512]{1,0:T(8,128)(2,1)S(1)}, bf16[64,512]{1,0:T(8,128)(2,1)S(1)}, u32[]{:S(2)}, u32[]{:S(2)}) collective-permute-start(bf16[64,512]{1,0:T(8,128)(2,1)S(1)} %add_convert_fusion.7), channel_id=1, source_target_pairs={{0,8},{2,10},{4,12},{6,14},{8,0},{10,2},{12,4},{14,6},{1,9},{3,11}... | collective-permute-start | bytes 196616 | tf_op jit(solution)/shard_map/ppermute | solution.py:224
  31.2 10.4 %collective-permute-start.16 = (bf16[64,512]{1,0:T(8,128)(2,1)S(1)}, bf16[64,512]{1,0:T(8,128)(2,1)S(1)}, u32[]{:S(2)}, u32[]{:S(2)}) collective-permute-start(bf16[64,512]{1,0:T(8,128)(2,1)S(1)} %add_convert_fusion.4), channel_id=1, source_target_pairs={{0,8},{2,10},{4,12},{6,14},{8,0},{10,2},{12,4},{14,6},{1,9},{3,11}... | collective-permute-start | bytes 196616 | tf_op jit(solution)/shard_map/ppermute | solution.py:224
  33.8 8.5 %collective-permute-start.9 = (bf16[64,512]{1,0:T(8,128)(2,1)S(1)}, bf16[64,512]{1,0:T(8,128)(2,1)S(1)}, u32[]{:S(2)}, u32[]{:S(2)}) collective-permute-start(bf16[64,512]{1,0:T(8,128)(2,1)S(1)} %add_convert_fusion.6), channel_id=1, source_target_pairs={{0,8},{2,10},{4,12},{6,14},{8,0},{10,2},{12,4},{14,6},{1,9},{3,11}... | collective-permute-start | bytes 196616 | tf_op jit(solution)/shard_map/ppermute | solution.py:224
  38.2 5.1 %collective-permute-start.12 = (bf16[64,512]{1,0:T(8,128)(2,1)S(1)}, bf16[64,512]{1,0:T(8,128)(2,1)S(1)}, u32[]{:S(2)}, u32[]{:S(2)}) collective-permute-start(bf16[64,512]{1,0:T(8,128)(2,1)S(1)} %add_convert_fusion.1), channel_id=1, source_target_pairs={{0,4},{2,6},{4,0},{6,2},{8,12},{10,14},{12,8},{14,10},{1,5},{3,7},... | collective-permute-start | bytes 196616 | tf_op jit(solution)/shard_map/ppermute | solution.py:224
  40.3 4.7 %collective-permute-start.8 = (bf16[64,512]{1,0:T(8,128)(2,1)S(1)}, bf16[64,512]{1,0:T(8,128)(2,1)S(1)}, u32[]{:S(2)}, u32[]{:S(2)}) collective-permute-start(bf16[64,512]{1,0:T(8,128)(2,1)S(1)} %add_convert_fusion.3), channel_id=1, source_target_pairs={{0,2},{2,0},{4,6},{6,4},{8,10},{10,8},{12,14},{14,12},{1,3},{3,1},... | collective-permute-start | bytes 196616 | tf_op jit(solution)/shard_map/ppermute | solution.py:224
  41.6 4.4 %collective-permute-start.17 = (bf16[64,512]{1,0:T(8,128)(2,1)S(1)}, bf16[64,512]{1,0:T(8,128)(2,1)S(1)}, u32[]{:S(2)}, u32[]{:S(2)}) collective-permute-start(bf16[64,512]{1,0:T(8,128)(2,1)S(1)} %add_convert_fusion), channel_id=1, source_target_pairs={{0,4},{2,6},{4,0},{6,2},{8,12},{10,14},{12,8},{14,10},{1,5},{3,7},... | collective-permute-start | bytes 196616 | tf_op jit(solution)/shard_map/ppermute | solution.py:224
  42.4 5.1 %collective-permute-start.14 = (bf16[64,512]{1,0:T(8,128)(2,1)S(1)}, bf16[64,512]{1,0:T(8,128)(2,1)S(1)}, u32[]{:S(2)}, u32[]{:S(2)}) collective-permute-start(bf16[64,512]{1,0:T(8,128)(2,1)S(1)} %add_convert_fusion.2), channel_id=1, source_target_pairs={{0,2},{2,0},{4,6},{6,4},{8,10},{10,8},{12,14},{14,12},{1,3},{3,1},... | collective-permute-start | bytes 196616 | tf_op jit(solution)/shard_map/ppermute | solution.py:224
  43.3 7.0 %collective-permute-start.13 = (bf16[128,512]{1,0:T(8,128)(2,1)S(1)}, bf16[128,512]{1,0:T(8,128)(2,1)S(1)}, u32[]{:S(2)}, u32[]{:S(2)}) collective-permute-start(bf16[128,512]{1,0:T(8,128)(2,1)S(1)} %pad_maximum_fusion.3), channel_id=1, source_target_pairs={{0,2},{2,0},{4,6},{6,4},{8,10},{10,8},{12,14},{14,12},{1,3},{3,1},... | collective-permute-start | bytes 393224 | tf_op jit(solution)/shard_map/ppermute | solution.py:224
  45.1 5.9 %collective-permute-start.10 = (bf16[128,512]{1,0:T(8,128)(2,1)S(1)}, bf16[128,512]{1,0:T(8,128)(2,1)S(1)}, u32[]{:S(2)}, u32[]{:S(2)}) collective-permute-start(bf16[128,512]{1,0:T(8,128)(2,1)S(1)} %pad_maximum_fusion.2), channel_id=1, source_target_pairs={{0,4},{2,6},{4,0},{6,2},{8,12},{10,14},{12,8},{14,10},{1,5},{3,7},... | collective-permute-start | bytes 393224 | tf_op jit(solution)/shard_map/ppermute | solution.py:224
  46.1 5.6 %collective-permute-start.18 = (bf16[128,512]{1,0:T(8,128)(2,1)S(1)}, bf16[128,512]{1,0:T(8,128)(2,1)S(1)}, u32[]{:S(2)}, u32[]{:S(2)}) collective-permute-start(bf16[128,512]{1,0:T(8,128)(2,1)S(1)} %pad_maximum_fusion.5), channel_id=1, source_target_pairs={{0,2},{2,0},{4,6},{6,4},{8,10},{10,8},{12,14},{14,12},{1,3},{3,1},... | collective-permute-start | bytes 393224 | tf_op jit(solution)/shard_map/ppermute | solution.py:224
  47.5 5.0 %collective-permute-start.15 = (bf16[128,512]{1,0:T(8,128)(2,1)S(1)}, bf16[128,512]{1,0:T(8,128)(2,1)S(1)}, u32[]{:S(2)}, u32[]{:S(2)}) collective-permute-start(bf16[128,512]{1,0:T(8,128)(2,1)S(1)} %pad_maximum_fusion.4), channel_id=1, source_target_pairs={{0,4},{2,6},{4,0},{6,2},{8,12},{10,14},{12,8},{14,10},{1,5},{3,7},... | collective-permute-start | bytes 393224 | tf_op jit(solution)/shard_map/ppermute | solution.py:224
  51.0 1.6 %copy-start.3 = (s32[512]{0:T(512)S(1)}, s32[512]{0:T(512)}, u32[]{:S(2)}) copy-start(s32[512]{0:T(512)} %param.10) | copy-start | bytes 6148
  51.0 1.6 %copy-start.4 = (s32[128]{0:T(128)S(1)}, s32[128]{0:T(128)}, u32[]{:S(2)}) copy-start(s32[128]{0:T(128)} %param.11) | copy-start | bytes 1540
  52.7 1.1 %copy-start = (bf16[512,1024]{1,0:T(8,128)(2,1)}, bf16[512,1024]{1,0:T(8,128)(2,1)S(1)}, u32[]{:S(2)}) copy-start(bf16[512,1024]{1,0:T(8,128)(2,1)S(1)} %maximum_dynamic-update-slice_fusion.3) | copy-start | bytes 3145732

commit v25 on v22

--- a/solution.py
+++ b/solution.py
@@ -117,7 +117,7 @@
             elif at + DEPTH_BLOCK < depth:
                 total_ref[...] += term
             else:
-                out_ref[:, rows] = (total_ref[...] + term).T
+                out_ref[step] = (total_ref[...] + term).T
         return carry
 
     lax.fori_loop(0, blocks, block, 0)
@@ -170,9 +170,11 @@
 def call(kernel, queries, store, outs, in_specs, scratch, operands):
     count, depth = queries.shape[1:]
     examples = store.shape[1]
+    columns = min(COLUMNS, examples)
+    scores = jax.ShapeDtypeStruct((examples // columns, count, columns), jnp.float32)
     return pl.pallas_call(
         kernel,
-        out_shape=(jax.ShapeDtypeStruct((count, examples), jnp.float32),) + outs,
+        out_shape=(scores,) + outs,
         in_specs=in_specs,
         out_specs=(VMEM,) * (1 + len(outs)),
         scratch_shapes=scratch,
@@ -336,10 +338,10 @@
                 chunk.take(order)
                 send(chunk, order, clock)
         choices = ORDERS[min(step, len(ORDERS) - 1)]
-        width = columns // len(choices)
+        width = part.shape[2]
         for number, (choice, exchanges) in enumerate(choices):
             first = number * width
-            chunk = LayerSum(part[:, first : first + width], orders[choice], index, exchanges)
+            chunk = LayerSum(part[number], orders[choice], index, exchanges)
             send(chunk, order, clock)
             chunks.append(chunk)
             places.append(((position - step) % ex_count * rows, jnp.int32(first)))

time: 51.9 us -> 51.9 us (level)
  no operation moved by 1% of the time
where the time goes in v25:
time: 51.9 us; the launch traced here: 51.7 us
  starting transfers between devices  24.6 us (47%)
  waiting for transfers between devices  11.9 us (23%)
  Pallas kernels  11.7 us (23%)
  matrix products  1.07 us (2%)
  between operations  0.96 us (2%)
  local copies, waits for them, and re-layouts  0.8 us (2%)
  other arithmetic  0.66 us (1%)
    ppermute x20, starting transfers between devices, swap(): return lax.ppermute(block, 'layer', route)  24.1 us
    ppermute x20, waiting for transfers between devices, swap(): return lax.ppermute(block, 'layer', route)  11.9 us
    pallas_call x2, Pallas kernels, call(): pl.pallas_call(kernel, out_shape=(scores,) + outs, in_specs=in_specs, out...  11.7 us
    dot_general x1, matrix products, shards(): advantage = jnp.dot(weights, scores, preferred_element_type=jnp.float32)  1.07 us
  transfers between devices with their start and end apart: 21, of which 9 were waited for; matrix products, arithmetic and copies ran while one was open for 2% of the time, Pallas kernels for 23%

profile of v25, /device:TPU:0, one launch (start us, length us, event | category | flops | bytes accessed | tf_op | source)
XLA Modules:
  0.0 51.7 jit_solution(3286954709520729655)
XLA Ops:
  0.6 0.5 %collective-permute-start.1 = (bf16[1,256,4096]{2,1,0:T(8,128)(2,1)}, bf16[1,256,4096]{2,1,0:T(8,128)(2,1)S(1)}, u32[]{:S(2)}, u32[]{:S(2)}) collective-permute-start(bf16[1,256,4096]{2,1,0:T(8,128)(2,1)} %rows_ref.1), channel_id=1, source_target_pairs={{1,0},{0,1},{3,2},{2,3},{5,4},{4,5},{7,6},{6,7},{9,8},{8,9},{11,10... | collective-permute-start | bytes 6291464 | tf_op jit(solution)/shard_map/ppermute | solution.py:332
  1.1 6.6 %shard_map.77 = (f32[2,256,512]{2,1,0:T(8,128)S(1)}, bf16[256,256]{1,0:T(8,128)(2,1)S(1)}, bf16[256,256]{1,0:T(8,128)(2,1)S(1)}) custom-call(bf16[1,256,4096]{2,1,0:T(8,128)(2,1)} %rows_ref.1, bf16[1,32,32]{2,1,0:T(8,128)(2,1)} %left_ref.1, bf16[1,128,128]{2,1,0:T(8,128)(2,1)} %right_ref.1, bf16[1,1024,4096]{2,1,0:T(8,128)(2,1)} %store_ref.3), custom_call_target="tpu_custom_call" | custom-call | flops 4294967296 | bytes 10485760 | tf_op jit(solution)/shard_map/pallas_call | solution.py:175
  7.8 0.1 fusion.11
  7.9 0.0 copy-start.1
  7.9 2.7 %collective-permute-start = (bf16[128,512]{1,0:T(8,128)(2,1)S(1)}, bf16[128,512]{1,0:T(8,128)(2,1)S(1)}, u32[]{:S(2)}, u32[]{:S(2)}) collective-permute-start(bf16[128,512]{1,0:T(8,128)(2,1)S(1)} %get-tuple-element.60.refs_0_), channel_id=1, source_target_pairs={{0,4},{2,6},{4,0},{6,2},{8,12},{10,14},{12,8},{14,10},{1,5},{3,7},... | collective-permute-start | bytes 393224 | tf_op jit(solution)/shard_map/ppermute | solution.py:226
  10.6 0.0 copy-done.1
  10.6 1.5 %collective-permute-start.3 = (bf16[128,512]{1,0:T(8,128)(2,1)S(1)}, bf16[128,512]{1,0:T(8,128)(2,1)S(1)}, u32[]{:S(2)}, u32[]{:S(2)}) collective-permute-start(bf16[128,512]{1,0:T(8,128)(2,1)S(1)} %get-tuple-element.66.refs_1_), channel_id=1, source_target_pairs={{0,2},{2,0},{4,6},{6,4},{8,10},{10,8},{12,14},{14,12},{1,3},{3,1},... | collective-permute-start | bytes 393224 | tf_op jit(solution)/shard_map/ppermute | solution.py:226
  12.1 0.0 collective-permute-done.1.rows_ref
  12.1 5.1 %shard_map.78 = f32[2,256,512]{2,1,0:T(8,128)S(1)} custom-call(bf16[1,256,4096]{2,1,0:T(8,128)(2,1)S(1)} %collective-permute-done.1.rows_ref, bf16[256,256]{1,0:T(8,128)(2,1)S(1)} %get-tuple-element.64.both_ref, bf16[256,256]{1,0:T(8,128)(2,1)S(1)} %get-tuple-element.65.mixer_ref, bf16[1,1024,4096]{2,1,0:T(8,128)(2,1)} %store_ref.3, ...), custom_call_target="tpu_custom_call" | custom-call | flops 4294967296 | bytes 10485760 | tf_op jit(solution)/shard_map/pallas_call | solution.py:175
  17.2 0.0 copy-start.2
  17.2 0.1 fusion.10
  17.3 0.6 %collective-permute-start.7 = (bf16[128,512]{1,0:T(8,128)(2,1)S(1)}, bf16[128,512]{1,0:T(8,128)(2,1)S(1)}, u32[]{:S(2)}, u32[]{:S(2)}) collective-permute-start(bf16[128,512]{1,0:T(8,128)(2,1)S(1)} %fusion.2), channel_id=1, source_target_pairs={{0,2},{2,0},{4,6},{6,4},{8,10},{10,8},{12,14},{14,12},{1,3},{3,1},... | collective-permute-start | bytes 393224 | tf_op jit(solution)/shard_map/ppermute | solution.py:226
  17.9 0.0 collective-permute-done
  17.9 0.3 copy-done.2
  18.3 0.0 collective-permute-done.3
  18.4 0.7 %collective-permute-start.4 = (bf16[64,512]{1,0:T(8,128)(2,1)S(1)}, bf16[64,512]{1,0:T(8,128)(2,1)S(1)}, u32[]{:S(2)}, u32[]{:S(2)}) collective-permute-start(bf16[64,512]{1,0:T(8,128)(2,1)S(1)} %dynamic-slice_convert_fusion.6), channel_id=1, source_target_pairs={{0,4},{2,6},{4,0},{6,2},{8,12},{10,14},{12,8},{14,10},{1,5},{3,7},... | collective-permute-start | bytes 196616 | tf_op jit(solution)/shard_map/ppermute | solution.py:226
  19.1 1.4 %collective-permute-start.8 = (bf16[128,512]{1,0:T(8,128)(2,1)S(1)}, bf16[128,512]{1,0:T(8,128)(2,1)S(1)}, u32[]{:S(2)}, u32[]{:S(2)}) collective-permute-start(bf16[128,512]{1,0:T(8,128)(2,1)S(1)} %fusion.3), channel_id=1, source_target_pairs={{0,4},{2,6},{4,0},{6,2},{8,12},{10,14},{12,8},{14,10},{1,5},{3,7},... | collective-permute-start | bytes 393224 | tf_op jit(solution)/shard_map/ppermute | solution.py:226
  20.6 1.2 %collective-permute-start.2 = (bf16[64,512]{1,0:T(8,128)(2,1)S(1)}, bf16[64,512]{1,0:T(8,128)(2,1)S(1)}, u32[]{:S(2)}, u32[]{:S(2)}) collective-permute-start(bf16[64,512]{1,0:T(8,128)(2,1)S(1)} %dynamic-slice_convert_fusion.7), channel_id=1, source_target_pairs={{0,2},{2,0},{4,6},{6,4},{8,10},{10,8},{12,14},{14,12},{1,3},{3,1},... | collective-permute-start | bytes 196616 | tf_op jit(solution)/shard_map/ppermute | solution.py:226
  21.8 1.6 %collective-permute-done.4 = bf16[64,512]{1,0:T(8,128)(2,1)S(1)} collective-permute-done((bf16[64,512]{1,0:T(8,128)(2,1)S(1)}, bf16[64,512]{1,0:T(8,128)(2,1)S(1)}, u32[]{:S(2)}, u32[]{:S(2)}) %collective-permute-start.4) | collective-permute-done | bytes 65568 | tf_op jit(solution)/shard_map/ppermute | solution.py:226
  23.4 2.7 %collective-permute-start.6 = (bf16[64,512]{1,0:T(8,128)(2,1)S(1)}, bf16[64,512]{1,0:T(8,128)(2,1)S(1)}, u32[]{:S(2)}, u32[]{:S(2)}) collective-permute-start(bf16[64,512]{1,0:T(8,128)(2,1)S(1)} %add_convert_fusion.7), channel_id=1, source_target_pairs={{0,8},{2,10},{4,12},{6,14},{8,0},{10,2},{12,4},{14,6},{1,9},{3,11}... | collective-permute-start | bytes 196616 | tf_op jit(solution)/shard_map/ppermute | solution.py:226
  26.1 0.0 collective-permute-done.2
  26.1 1.4 %collective-permute-start.5 = (bf16[64,512]{1,0:T(8,128)(2,1)S(1)}, bf16[64,512]{1,0:T(8,128)(2,1)S(1)}, u32[]{:S(2)}, u32[]{:S(2)}) collective-permute-start(bf16[64,512]{1,0:T(8,128)(2,1)S(1)} %add_convert_fusion.6), channel_id=1, source_target_pairs={{0,8},{2,10},{4,12},{6,14},{8,0},{10,2},{12,4},{14,6},{1,9},{3,11}... | collective-permute-start | bytes 196616 | tf_op jit(solution)/shard_map/ppermute | solution.py:226
  27.5 0.0 collective-permute-done.7
  27.6 0.7 %collective-permute-start.10 = (bf16[64,512]{1,0:T(8,128)(2,1)S(1)}, bf16[64,512]{1,0:T(8,128)(2,1)S(1)}, u32[]{:S(2)}, u32[]{:S(2)}) collective-permute-start(bf16[64,512]{1,0:T(8,128)(2,1)S(1)} %dynamic-slice_convert_fusion.4), channel_id=1, source_target_pairs={{0,4},{2,6},{4,0},{6,2},{8,12},{10,14},{12,8},{14,10},{1,5},{3,7},... | collective-permute-start | bytes 196616 | tf_op jit(solution)/shard_map/ppermute | solution.py:226
  28.3 0.0 collective-permute-done.8
  28.4 1.2 %collective-permute-start.11 = (bf16[64,512]{1,0:T(8,128)(2,1)S(1)}, bf16[64,512]{1,0:T(8,128)(2,1)S(1)}, u32[]{:S(2)}, u32[]{:S(2)}) collective-permute-start(bf16[64,512]{1,0:T(8,128)(2,1)S(1)} %dynamic-slice_convert_fusion.5), channel_id=1, source_target_pairs={{0,2},{2,0},{4,6},{6,4},{8,10},{10,8},{12,14},{14,12},{1,3},{3,1},... | collective-permute-start | bytes 196616 | tf_op jit(solution)/shard_map/ppermute | solution.py:226
  29.6 1.0 %collective-permute-done.6 = bf16[64,512]{1,0:T(8,128)(2,1)S(1)} collective-permute-done((bf16[64,512]{1,0:T(8,128)(2,1)S(1)}, bf16[64,512]{1,0:T(8,128)(2,1)S(1)}, u32[]{:S(2)}, u32[]{:S(2)}) %collective-permute-start.6) | collective-permute-done | bytes 65568 | tf_op jit(solution)/shard_map/ppermute | solution.py:226
  30.6 0.4 collective-permute-start.9
  31.1 1.0 %collective-permute-done.5 = bf16[64,512]{1,0:T(8,128)(2,1)S(1)} collective-permute-done((bf16[64,512]{1,0:T(8,128)(2,1)S(1)}, bf16[64,512]{1,0:T(8,128)(2,1)S(1)}, u32[]{:S(2)}, u32[]{:S(2)}) %collective-permute-start.5) | collective-permute-done | bytes 65568 | tf_op jit(solution)/shard_map/ppermute | solution.py:226
  32.1 1.0 %collective-permute-start.12 = (bf16[64,512]{1,0:T(8,128)(2,1)S(1)}, bf16[64,512]{1,0:T(8,128)(2,1)S(1)}, u32[]{:S(2)}, u32[]{:S(2)}) collective-permute-start(bf16[64,512]{1,0:T(8,128)(2,1)S(1)} %add_convert_fusion.2), channel_id=1, source_target_pairs={{0,2},{2,0},{4,6},{6,4},{8,10},{10,8},{12,14},{14,12},{1,3},{3,1},... | collective-permute-start | bytes 196616 | tf_op jit(solution)/shard_map/ppermute | solution.py:226
  33.1 0.0 collective-permute-done.10
  33.1 1.6 %collective-permute-start.18 = (bf16[64,512]{1,0:T(8,128)(2,1)S(1)}, bf16[64,512]{1,0:T(8,128)(2,1)S(1)}, u32[]{:S(2)}, u32[]{:S(2)}) collective-permute-start(bf16[64,512]{1,0:T(8,128)(2,1)S(1)} %add_convert_fusion.3), channel_id=1, source_target_pairs={{0,8},{2,10},{4,12},{6,14},{8,0},{10,2},{12,4},{14,6},{1,9},{3,11}... | collective-permute-start | bytes 196616 | tf_op jit(solution)/shard_map/ppermute | solution.py:226
  34.7 0.0 collective-permute-done.11
  34.7 1.5 %collective-permute-start.15 = (bf16[64,512]{1,0:T(8,128)(2,1)S(1)}, bf16[64,512]{1,0:T(8,128)(2,1)S(1)}, u32[]{:S(2)}, u32[]{:S(2)}) collective-permute-start(bf16[64,512]{1,0:T(8,128)(2,1)S(1)} %add_convert_fusion.4), channel_id=1, source_target_pairs={{0,8},{2,10},{4,12},{6,14},{8,0},{10,2},{12,4},{14,6},{1,9},{3,11}... | collective-permute-start | bytes 196616 | tf_op jit(solution)/shard_map/ppermute | solution.py:226
  36.2 0.0 collective-permute-done.9
  36.2 1.2 %collective-permute-start.14 = (bf16[128,512]{1,0:T(8,128)(2,1)S(1)}, bf16[128,512]{1,0:T(8,128)(2,1)S(1)}, u32[]{:S(2)}, u32[]{:S(2)}) collective-permute-start(bf16[128,512]{1,0:T(8,128)(2,1)S(1)} %pad_maximum_fusion.1), channel_id=1, source_target_pairs={{0,2},{2,0},{4,6},{6,4},{8,10},{10,8},{12,14},{14,12},{1,3},{3,1},... | collective-permute-start | bytes 393224 | tf_op jit(solution)/shard_map/ppermute | solution.py:226
  37.4 0.0 collective-permute-done.12
  37.4 0.8 %collective-permute-start.13 = (bf16[128,512]{1,0:T(8,128)(2,1)S(1)}, bf16[128,512]{1,0:T(8,128)(2,1)S(1)}, u32[]{:S(2)}, u32[]{:S(2)}) collective-permute-start(bf16[128,512]{1,0:T(8,128)(2,1)S(1)} %pad_maximum_fusion), channel_id=1, source_target_pairs={{0,4},{2,6},{4,0},{6,2},{8,12},{10,14},{12,8},{14,10},{1,5},{3,7},... | collective-permute-start | bytes 393224 | tf_op jit(solution)/shard_map/ppermute | solution.py:226
  38.2 0.7 %collective-permute-done.18 = bf16[64,512]{1,0:T(8,128)(2,1)S(1)} collective-permute-done((bf16[64,512]{1,0:T(8,128)(2,1)S(1)}, bf16[64,512]{1,0:T(8,128)(2,1)S(1)}, u32[]{:S(2)}, u32[]{:S(2)}) %collective-permute-start.18) | collective-permute-done | bytes 65568 | tf_op jit(solution)/shard_map/ppermute | solution.py:226
  38.9 0.9 %collective-permute-start.19 = (bf16[64,512]{1,0:T(8,128)(2,1)S(1)}, bf16[64,512]{1,0:T(8,128)(2,1)S(1)}, u32[]{:S(2)}, u32[]{:S(2)}) collective-permute-start(bf16[64,512]{1,0:T(8,128)(2,1)S(1)} %add_convert_fusion), channel_id=1, source_target_pairs={{0,4},{2,6},{4,0},{6,2},{8,12},{10,14},{12,8},{14,10},{1,5},{3,7},... | collective-permute-start | bytes 196616 | tf_op jit(solution)/shard_map/ppermute | solution.py:226
  39.8 0.6 %collective-permute-done.15 = bf16[64,512]{1,0:T(8,128)(2,1)S(1)} collective-permute-done((bf16[64,512]{1,0:T(8,128)(2,1)S(1)}, bf16[64,512]{1,0:T(8,128)(2,1)S(1)}, u32[]{:S(2)}, u32[]{:S(2)}) %collective-permute-start.15) | collective-permute-done | bytes 65568 | tf_op jit(solution)/shard_map/ppermute | solution.py:226
  40.5 0.8 %collective-permute-start.16 = (bf16[64,512]{1,0:T(8,128)(2,1)S(1)}, bf16[64,512]{1,0:T(8,128)(2,1)S(1)}, u32[]{:S(2)}, u32[]{:S(2)}) collective-permute-start(bf16[64,512]{1,0:T(8,128)(2,1)S(1)} %add_convert_fusion.1), channel_id=1, source_target_pairs={{0,2},{2,0},{4,6},{6,4},{8,10},{10,8},{12,14},{14,12},{1,3},{3,1},... | collective-permute-start | bytes 196616 | tf_op jit(solution)/shard_map/ppermute | solution.py:226
  41.3 2.0 %collective-permute-done.19 = bf16[64,512]{1,0:T(8,128)(2,1)S(1)} collective-permute-done((bf16[64,512]{1,0:T(8,128)(2,1)S(1)}, bf16[64,512]{1,0:T(8,128)(2,1)S(1)}, u32[]{:S(2)}, u32[]{:S(2)}) %collective-permute-start.19) | collective-permute-done | bytes 65568 | tf_op jit(solution)/shard_map/ppermute | solution.py:226
  43.3 1.1 %collective-permute-start.20 = (bf16[128,512]{1,0:T(8,128)(2,1)S(1)}, bf16[128,512]{1,0:T(8,128)(2,1)S(1)}, u32[]{:S(2)}, u32[]{:S(2)}) collective-permute-start(bf16[128,512]{1,0:T(8,128)(2,1)S(1)} %pad_maximum_fusion.3), channel_id=1, source_target_pairs={{0,2},{2,0},{4,6},{6,4},{8,10},{10,8},{12,14},{14,12},{1,3},{3,1},... | collective-permute-start | bytes 393224 | tf_op jit(solution)/shard_map/ppermute | solution.py:226
  44.4 1.0 %collective-permute-done.16 = bf16[64,512]{1,0:T(8,128)(2,1)S(1)} collective-permute-done((bf16[64,512]{1,0:T(8,128)(2,1)S(1)}, bf16[64,512]{1,0:T(8,128)(2,1)S(1)}, u32[]{:S(2)}, u32[]{:S(2)}) %collective-permute-start.16) | collective-permute-done | bytes 65568 | tf_op jit(solution)/shard_map/ppermute | solution.py:226
  45.4 0.7 %collective-permute-start.17 = (bf16[128,512]{1,0:T(8,128)(2,1)S(1)}, bf16[128,512]{1,0:T(8,128)(2,1)S(1)}, u32[]{:S(2)}, u32[]{:S(2)}) collective-permute-start(bf16[128,512]{1,0:T(8,128)(2,1)S(1)} %pad_maximum_fusion.2), channel_id=1, source_target_pairs={{0,4},{2,6},{4,0},{6,2},{8,12},{10,14},{12,8},{14,10},{1,5},{3,7},... | collective-permute-start | bytes 393224 | tf_op jit(solution)/shard_map/ppermute | solution.py:226
  46.2 0.0 collective-permute-done.14
  46.2 0.0 collective-permute-done.13
  46.3 0.0 copy-start.3
  46.3 0.0 copy-start.4
  46.3 0.1 broadcast_in_dim.2
  46.5 1.8 %collective-permute-done.20 = bf16[128,512]{1,0:T(8,128)(2,1)S(1)} collective-permute-done((bf16[128,512]{1,0:T(8,128)(2,1)S(1)}, bf16[128,512]{1,0:T(8,128)(2,1)S(1)}, u32[]{:S(2)}, u32[]{:S(2)}) %collective-permute-start.20) | collective-permute-done | bytes 131104 | tf_op jit(solution)/shard_map/ppermute | solution.py:226
  48.4 2.1 %collective-permute-done.17 = bf16[128,512]{1,0:T(8,128)(2,1)S(1)} collective-permute-done((bf16[128,512]{1,0:T(8,128)(2,1)S(1)}, bf16[128,512]{1,0:T(8,128)(2,1)S(1)}, u32[]{:S(2)}, u32[]{:S(2)}) %collective-permute-start.17) | collective-permute-done | bytes 131104 | tf_op jit(solution)/shard_map/ppermute | solution.py:226
  50.6 0.0 copy-done.3
  50.6 0.0 copy-done.4
  50.6 0.0 copy-start
  50.6 1.1 %convolution_convert_fusion = bf16[128,1024]{1,0:T(8,128)(2,1)} fusion(bf16[512,1024]{1,0:T(8,128)(2,1)S(1)} %maximum_dynamic-update-slice_fusion.3, s32[512]{0:T(512)S(1)} %copy-done.3, s32[128]{0:T(128)S(1)} %copy-done.4), kind=kOutput, calls=%fused_computation | convolution fusion | flops 134742016 | bytes 1313280 | tf_op jit(solution)/shard_map/dot_general | solution.py:362
  51.7 0.0 copy-done
  (35 shorter events, 0.8 us)
Async XLA Ops:
  0.6 11.5 %collective-permute-start.1 = (bf16[1,256,4096]{2,1,0:T(8,128)(2,1)}, bf16[1,256,4096]{2,1,0:T(8,128)(2,1)S(1)}, u32[]{:S(2)}, u32[]{:S(2)}) collective-permute-start(bf16[1,256,4096]{2,1,0:T(8,128)(2,1)} %rows_ref.1), channel_id=1, source_target_pairs={{1,0},{0,1},{3,2},{2,3},{5,4},{4,5},{7,6},{6,7},{9,8},{8,9},{11,10... | collective-permute-start | bytes 6291464 | tf_op jit(solution)/shard_map/ppermute | solution.py:332
  7.9 2.7 %copy-start.1 = (f32[1,256,512]{2,1,0:T(8,128)}, f32[1,256,512]{2,1,0:T(8,128)S(1)}, u32[]{:S(2)}) copy-start(f32[1,256,512]{2,1,0:T(8,128)S(1)} %get-tuple-element.119) | copy-start | bytes 1572868
  7.9 10.0 %collective-permute-start = (bf16[128,512]{1,0:T(8,128)(2,1)S(1)}, bf16[128,512]{1,0:T(8,128)(2,1)S(1)}, u32[]{:S(2)}, u32[]{:S(2)}) collective-permute-start(bf16[128,512]{1,0:T(8,128)(2,1)S(1)} %get-tuple-element.60.refs_0_), channel_id=1, source_target_pairs={{0,4},{2,6},{4,0},{6,2},{8,12},{10,14},{12,8},{14,10},{1,5},{3,7},... | collective-permute-start | bytes 393224 | tf_op jit(solution)/shard_map/ppermute | solution.py:226
  10.6 7.7 %collective-permute-start.3 = (bf16[128,512]{1,0:T(8,128)(2,1)S(1)}, bf16[128,512]{1,0:T(8,128)(2,1)S(1)}, u32[]{:S(2)}, u32[]{:S(2)}) collective-permute-start(bf16[128,512]{1,0:T(8,128)(2,1)S(1)} %get-tuple-element.66.refs_1_), channel_id=1, source_target_pairs={{0,2},{2,0},{4,6},{6,4},{8,10},{10,8},{12,14},{14,12},{1,3},{3,1},... | collective-permute-start | bytes 393224 | tf_op jit(solution)/shard_map/ppermute | solution.py:226
  17.2 1.0 %copy-start.2 = (f32[1,256,512]{2,1,0:T(8,128)S(1)}, f32[1,256,512]{2,1,0:T(8,128)}, u32[]{:S(2)}) copy-start(f32[1,256,512]{2,1,0:T(8,128)} %copy-done.1) | copy-start | bytes 1572868
  17.3 10.2 %collective-permute-start.7 = (bf16[128,512]{1,0:T(8,128)(2,1)S(1)}, bf16[128,512]{1,0:T(8,128)(2,1)S(1)}, u32[]{:S(2)}, u32[]{:S(2)}) collective-permute-start(bf16[128,512]{1,0:T(8,128)(2,1)S(1)} %fusion.2), channel_id=1, source_target_pairs={{0,2},{2,0},{4,6},{6,4},{8,10},{10,8},{12,14},{14,12},{1,3},{3,1},... | collective-permute-start | bytes 393224 | tf_op jit(solution)/shard_map/ppermute | solution.py:226
  18.4 5.0 %collective-permute-start.4 = (bf16[64,512]{1,0:T(8,128)(2,1)S(1)}, bf16[64,512]{1,0:T(8,128)(2,1)S(1)}, u32[]{:S(2)}, u32[]{:S(2)}) collective-permute-start(bf16[64,512]{1,0:T(8,128)(2,1)S(1)} %dynamic-slice_convert_fusion.6), channel_id=1, source_target_pairs={{0,4},{2,6},{4,0},{6,2},{8,12},{10,14},{12,8},{14,10},{1,5},{3,7},... | collective-permute-start | bytes 196616 | tf_op jit(solution)/shard_map/ppermute | solution.py:226
  19.1 9.2 %collective-permute-start.8 = (bf16[128,512]{1,0:T(8,128)(2,1)S(1)}, bf16[128,512]{1,0:T(8,128)(2,1)S(1)}, u32[]{:S(2)}, u32[]{:S(2)}) collective-permute-start(bf16[128,512]{1,0:T(8,128)(2,1)S(1)} %fusion.3), channel_id=1, source_target_pairs={{0,4},{2,6},{4,0},{6,2},{8,12},{10,14},{12,8},{14,10},{1,5},{3,7},... | collective-permute-start | bytes 393224 | tf_op jit(solution)/shard_map/ppermute | solution.py:226
  20.6 5.5 %collective-permute-start.2 = (bf16[64,512]{1,0:T(8,128)(2,1)S(1)}, bf16[64,512]{1,0:T(8,128)(2,1)S(1)}, u32[]{:S(2)}, u32[]{:S(2)}) collective-permute-start(bf16[64,512]{1,0:T(8,128)(2,1)S(1)} %dynamic-slice_convert_fusion.7), channel_id=1, source_target_pairs={{0,2},{2,0},{4,6},{6,4},{8,10},{10,8},{12,14},{14,12},{1,3},{3,1},... | collective-permute-start | bytes 196616 | tf_op jit(solution)/shard_map/ppermute | solution.py:226
  23.4 7.2 %collective-permute-start.6 = (bf16[64,512]{1,0:T(8,128)(2,1)S(1)}, bf16[64,512]{1,0:T(8,128)(2,1)S(1)}, u32[]{:S(2)}, u32[]{:S(2)}) collective-permute-start(bf16[64,512]{1,0:T(8,128)(2,1)S(1)} %add_convert_fusion.7), channel_id=1, source_target_pairs={{0,8},{2,10},{4,12},{6,14},{8,0},{10,2},{12,4},{14,6},{1,9},{3,11}... | collective-permute-start | bytes 196616 | tf_op jit(solution)/shard_map/ppermute | solution.py:226
  26.1 5.9 %collective-permute-start.5 = (bf16[64,512]{1,0:T(8,128)(2,1)S(1)}, bf16[64,512]{1,0:T(8,128)(2,1)S(1)}, u32[]{:S(2)}, u32[]{:S(2)}) collective-permute-start(bf16[64,512]{1,0:T(8,128)(2,1)S(1)} %add_convert_fusion.6), channel_id=1, source_target_pairs={{0,8},{2,10},{4,12},{6,14},{8,0},{10,2},{12,4},{14,6},{1,9},{3,11}... | collective-permute-start | bytes 196616 | tf_op jit(solution)/shard_map/ppermute | solution.py:226
  27.6 5.5 %collective-permute-start.10 = (bf16[64,512]{1,0:T(8,128)(2,1)S(1)}, bf16[64,512]{1,0:T(8,128)(2,1)S(1)}, u32[]{:S(2)}, u32[]{:S(2)}) collective-permute-start(bf16[64,512]{1,0:T(8,128)(2,1)S(1)} %dynamic-slice_convert_fusion.4), channel_id=1, source_target_pairs={{0,4},{2,6},{4,0},{6,2},{8,12},{10,14},{12,8},{14,10},{1,5},{3,7},... | collective-permute-start | bytes 196616 | tf_op jit(solution)/shard_map/ppermute | solution.py:226
  28.4 6.3 %collective-permute-start.11 = (bf16[64,512]{1,0:T(8,128)(2,1)S(1)}, bf16[64,512]{1,0:T(8,128)(2,1)S(1)}, u32[]{:S(2)}, u32[]{:S(2)}) collective-permute-start(bf16[64,512]{1,0:T(8,128)(2,1)S(1)} %dynamic-slice_convert_fusion.5), channel_id=1, source_target_pairs={{0,2},{2,0},{4,6},{6,4},{8,10},{10,8},{12,14},{14,12},{1,3},{3,1},... | collective-permute-start | bytes 196616 | tf_op jit(solution)/shard_map/ppermute | solution.py:226
  30.6 5.5 %collective-permute-start.9 = (bf16[64,512]{1,0:T(8,128)(2,1)S(1)}, bf16[64,512]{1,0:T(8,128)(2,1)S(1)}, u32[]{:S(2)}, u32[]{:S(2)}) collective-permute-start(bf16[64,512]{1,0:T(8,128)(2,1)S(1)} %add_convert_fusion.5), channel_id=1, source_target_pairs={{0,4},{2,6},{4,0},{6,2},{8,12},{10,14},{12,8},{14,10},{1,5},{3,7},... | collective-permute-start | bytes 196616 | tf_op jit(solution)/shard_map/ppermute | solution.py:226
  32.1 5.3 %collective-permute-start.12 = (bf16[64,512]{1,0:T(8,128)(2,1)S(1)}, bf16[64,512]{1,0:T(8,128)(2,1)S(1)}, u32[]{:S(2)}, u32[]{:S(2)}) collective-permute-start(bf16[64,512]{1,0:T(8,128)(2,1)S(1)} %add_convert_fusion.2), channel_id=1, source_target_pairs={{0,2},{2,0},{4,6},{6,4},{8,10},{10,8},{12,14},{14,12},{1,3},{3,1},... | collective-permute-start | bytes 196616 | tf_op jit(solution)/shard_map/ppermute | solution.py:226
  33.1 5.8 %collective-permute-start.18 = (bf16[64,512]{1,0:T(8,128)(2,1)S(1)}, bf16[64,512]{1,0:T(8,128)(2,1)S(1)}, u32[]{:S(2)}, u32[]{:S(2)}) collective-permute-start(bf16[64,512]{1,0:T(8,128)(2,1)S(1)} %add_convert_fusion.3), channel_id=1, source_target_pairs={{0,8},{2,10},{4,12},{6,14},{8,0},{10,2},{12,4},{14,6},{1,9},{3,11}... | collective-permute-start | bytes 196616 | tf_op jit(solution)/shard_map/ppermute | solution.py:226
  34.7 5.8 %collective-permute-start.15 = (bf16[64,512]{1,0:T(8,128)(2,1)S(1)}, bf16[64,512]{1,0:T(8,128)(2,1)S(1)}, u32[]{:S(2)}, u32[]{:S(2)}) collective-permute-start(bf16[64,512]{1,0:T(8,128)(2,1)S(1)} %add_convert_fusion.4), channel_id=1, source_target_pairs={{0,8},{2,10},{4,12},{6,14},{8,0},{10,2},{12,4},{14,6},{1,9},{3,11}... | collective-permute-start | bytes 196616 | tf_op jit(solution)/shard_map/ppermute | solution.py:226
  36.2 9.9 %collective-permute-start.14 = (bf16[128,512]{1,0:T(8,128)(2,1)S(1)}, bf16[128,512]{1,0:T(8,128)(2,1)S(1)}, u32[]{:S(2)}, u32[]{:S(2)}) collective-permute-start(bf16[128,512]{1,0:T(8,128)(2,1)S(1)} %pad_maximum_fusion.1), channel_id=1, source_target_pairs={{0,2},{2,0},{4,6},{6,4},{8,10},{10,8},{12,14},{14,12},{1,3},{3,1},... | collective-permute-start | bytes 393224 | tf_op jit(solution)/shard_map/ppermute | solution.py:226
  37.4 8.8 %collective-permute-start.13 = (bf16[128,512]{1,0:T(8,128)(2,1)S(1)}, bf16[128,512]{1,0:T(8,128)(2,1)S(1)}, u32[]{:S(2)}, u32[]{:S(2)}) collective-permute-start(bf16[128,512]{1,0:T(8,128)(2,1)S(1)} %pad_maximum_fusion), channel_id=1, source_target_pairs={{0,4},{2,6},{4,0},{6,2},{8,12},{10,14},{12,8},{14,10},{1,5},{3,7},... | collective-permute-start | bytes 393224 | tf_op jit(solution)/shard_map/ppermute | solution.py:226
  38.9 4.3 %collective-permute-start.19 = (bf16[64,512]{1,0:T(8,128)(2,1)S(1)}, bf16[64,512]{1,0:T(8,128)(2,1)S(1)}, u32[]{:S(2)}, u32[]{:S(2)}) collective-permute-start(bf16[64,512]{1,0:T(8,128)(2,1)S(1)} %add_convert_fusion), channel_id=1, source_target_pairs={{0,4},{2,6},{4,0},{6,2},{8,12},{10,14},{12,8},{14,10},{1,5},{3,7},... | collective-permute-start | bytes 196616 | tf_op jit(solution)/shard_map/ppermute | solution.py:226
  40.5 4.9 %collective-permute-start.16 = (bf16[64,512]{1,0:T(8,128)(2,1)S(1)}, bf16[64,512]{1,0:T(8,128)(2,1)S(1)}, u32[]{:S(2)}, u32[]{:S(2)}) collective-permute-start(bf16[64,512]{1,0:T(8,128)(2,1)S(1)} %add_convert_fusion.1), channel_id=1, source_target_pairs={{0,2},{2,0},{4,6},{6,4},{8,10},{10,8},{12,14},{14,12},{1,3},{3,1},... | collective-permute-start | bytes 196616 | tf_op jit(solution)/shard_map/ppermute | solution.py:226
  43.3 5.0 %collective-permute-start.20 = (bf16[128,512]{1,0:T(8,128)(2,1)S(1)}, bf16[128,512]{1,0:T(8,128)(2,1)S(1)}, u32[]{:S(2)}, u32[]{:S(2)}) collective-permute-start(bf16[128,512]{1,0:T(8,128)(2,1)S(1)} %pad_maximum_fusion.3), channel_id=1, source_target_pairs={{0,2},{2,0},{4,6},{6,4},{8,10},{10,8},{12,14},{14,12},{1,3},{3,1},... | collective-permute-start | bytes 393224 | tf_op jit(solution)/shard_map/ppermute | solution.py:226
  45.4 5.0 %collective-permute-start.17 = (bf16[128,512]{1,0:T(8,128)(2,1)S(1)}, bf16[128,512]{1,0:T(8,128)(2,1)S(1)}, u32[]{:S(2)}, u32[]{:S(2)}) collective-permute-start(bf16[128,512]{1,0:T(8,128)(2,1)S(1)} %pad_maximum_fusion.2), channel_id=1, source_target_pairs={{0,4},{2,6},{4,0},{6,2},{8,12},{10,14},{12,8},{14,10},{1,5},{3,7},... | collective-permute-start | bytes 393224 | tf_op jit(solution)/shard_map/ppermute | solution.py:226
  46.3 4.3 %copy-start.3 = (s32[512]{0:T(512)S(1)}, s32[512]{0:T(512)}, u32[]{:S(2)}) copy-start(s32[512]{0:T(512)} %param.10) | copy-start | bytes 6148
  46.3 4.3 %copy-start.4 = (s32[128]{0:T(128)S(1)}, s32[128]{0:T(128)}, u32[]{:S(2)}) copy-start(s32[128]{0:T(128)} %param.11) | copy-start | bytes 1540
  50.6 1.1 %copy-start = (bf16[512,1024]{1,0:T(8,128)(2,1)}, bf16[512,1024]{1,0:T(8,128)(2,1)S(1)}, u32[]{:S(2)}) copy-start(bf16[512,1024]{1,0:T(8,128)(2,1)S(1)} %maximum_dynamic-update-slice_fusion.3) | copy-start | bytes 3145732

commit v26 on v25

--- a/solution.py
+++ b/solution.py
@@ -231,7 +231,7 @@
 
 class LayerSum:
     def __init__(self, block, bits, index, exchanges):
-        self.block, self.index = block, index
+        self.block, self.index, self.sent = block, index, None
         halved, exchanged = bits[:-exchanges], bits[-exchanges:]
         self.moves = [(bit, HALVE) for bit in halved]
         self.moves += [(bit, EXCHANGE) for bit in exchanged]
@@ -248,6 +248,8 @@
             sent = lax.dynamic_slice_in_dim(self.block, (1 - upper) * rows, rows, 0)
             sent = sent.astype(jnp.bfloat16)
             self.block = lax.dynamic_slice_in_dim(self.block, upper * rows, rows, 0)
+            if self.sent is None:
+                self.block, sent = lax.optimization_barrier((self.block, sent))
         self.sent = order.mark(sent)
         self.received = swap(self.sent, bit)
 

time: 51.9 us -> 51.5 us (level)
  no operation moved by 1% of the time
where the time goes in v26:
time: 51.5 us; the launch traced here: 51.4 us
  starting transfers between devices  24.3 us (47%)
  waiting for transfers between devices  12.1 us (23%)
  Pallas kernels  11.7 us (23%)
  matrix products  1.08 us (2%)
  between operations  0.97 us (2%)
  other arithmetic  0.67 us (1%)
  local copies, waits for them, and re-layouts  0.54 us (1%)
    ppermute x20, starting transfers between devices, swap(): return lax.ppermute(block, 'layer', route)  23.8 us
    ppermute x20, waiting for transfers between devices, swap(): return lax.ppermute(block, 'layer', route)  12.1 us
    pallas_call x2, Pallas kernels, call(): pl.pallas_call(kernel, out_shape=(scores,) + outs, in_specs=in_specs, out...  11.7 us
    dot_general x1, matrix products, shards(): advantage = jnp.dot(weights, scores, preferred_element_type=jnp.float32)  1.08 us
  transfers between devices with their start and end apart: 21, of which 9 were waited for; matrix products, arithmetic and copies ran while one was open for 2% of the time, Pallas kernels for 23%

profile of v26, /device:TPU:0, one launch (start us, length us, event | category | flops | bytes accessed | tf_op | source)
XLA Modules:
  0.0 51.4 jit_solution(10714824335721642469)
XLA Ops:
  0.6 0.5 %collective-permute-start.1 = (bf16[1,256,4096]{2,1,0:T(8,128)(2,1)}, bf16[1,256,4096]{2,1,0:T(8,128)(2,1)S(1)}, u32[]{:S(2)}, u32[]{:S(2)}) collective-permute-start(bf16[1,256,4096]{2,1,0:T(8,128)(2,1)} %rows_ref.1), channel_id=1, source_target_pairs={{1,0},{0,1},{3,2},{2,3},{5,4},{4,5},{7,6},{6,7},{9,8},{8,9},{11,10... | collective-permute-start | bytes 6291464 | tf_op jit(solution)/shard_map/ppermute | solution.py:334
  1.1 6.6 %shard_map.77 = (f32[2,256,512]{2,1,0:T(8,128)S(1)}, bf16[256,256]{1,0:T(8,128)(2,1)S(1)}, bf16[256,256]{1,0:T(8,128)(2,1)S(1)}) custom-call(bf16[1,256,4096]{2,1,0:T(8,128)(2,1)} %rows_ref.1, bf16[1,32,32]{2,1,0:T(8,128)(2,1)} %left_ref.1, bf16[1,128,128]{2,1,0:T(8,128)(2,1)} %right_ref.1, bf16[1,1024,4096]{2,1,0:T(8,128)(2,1)} %store_ref.3), custom_call_target="tpu_custom_call" | custom-call | flops 4294967296 | bytes 10485760 | tf_op jit(solution)/shard_map/pallas_call | solution.py:175
  7.8 0.1 fusion.11
  8.0 2.7 %collective-permute-start = (bf16[128,512]{1,0:T(8,128)(2,1)S(1)}, bf16[128,512]{1,0:T(8,128)(2,1)S(1)}, u32[]{:S(2)}, u32[]{:S(2)}) collective-permute-start(bf16[128,512]{1,0:T(8,128)(2,1)S(1)} %get-tuple-element.70.refs_0_), channel_id=1, source_target_pairs={{0,4},{2,6},{4,0},{6,2},{8,12},{10,14},{12,8},{14,10},{1,5},{3,7},... | collective-permute-start | bytes 393224 | tf_op jit(solution)/shard_map/ppermute | solution.py:226
  10.7 1.5 %collective-permute-start.3 = (bf16[128,512]{1,0:T(8,128)(2,1)S(1)}, bf16[128,512]{1,0:T(8,128)(2,1)S(1)}, u32[]{:S(2)}, u32[]{:S(2)}) collective-permute-start(bf16[128,512]{1,0:T(8,128)(2,1)S(1)} %get-tuple-element.77.refs_1_), channel_id=1, source_target_pairs={{0,2},{2,0},{4,6},{6,4},{8,10},{10,8},{12,14},{14,12},{1,3},{3,1},... | collective-permute-start | bytes 393224 | tf_op jit(solution)/shard_map/ppermute | solution.py:226
  12.2 0.0 collective-permute-done.1.rows_ref
  12.2 5.1 %shard_map.78 = f32[2,256,512]{2,1,0:T(8,128)S(1)} custom-call(bf16[1,256,4096]{2,1,0:T(8,128)(2,1)S(1)} %collective-permute-done.1.rows_ref, bf16[256,256]{1,0:T(8,128)(2,1)S(1)} %get-tuple-element.75.both_ref, bf16[256,256]{1,0:T(8,128)(2,1)S(1)} %get-tuple-element.76.mixer_ref, bf16[1,1024,4096]{2,1,0:T(8,128)(2,1)} %store_ref.3, ...), custom_call_target="tpu_custom_call" | custom-call | flops 4294967296 | bytes 10485760 | tf_op jit(solution)/shard_map/pallas_call | solution.py:175
  17.2 0.1 fusion.10
  17.4 0.6 %collective-permute-start.7 = (bf16[128,512]{1,0:T(8,128)(2,1)S(1)}, bf16[128,512]{1,0:T(8,128)(2,1)S(1)}, u32[]{:S(2)}, u32[]{:S(2)}) collective-permute-start(bf16[128,512]{1,0:T(8,128)(2,1)S(1)} %fusion.2), channel_id=1, source_target_pairs={{0,2},{2,0},{4,6},{6,4},{8,10},{10,8},{12,14},{14,12},{1,3},{3,1},... | collective-permute-start | bytes 393224 | tf_op jit(solution)/shard_map/ppermute | solution.py:226
  18.0 0.0 collective-permute-done
  18.1 0.0 collective-permute-done.3
  18.1 0.1 collective-permute-start.4
  18.3 2.0 %collective-permute-start.8 = (bf16[128,512]{1,0:T(8,128)(2,1)S(1)}, bf16[128,512]{1,0:T(8,128)(2,1)S(1)}, u32[]{:S(2)}, u32[]{:S(2)}) collective-permute-start(bf16[128,512]{1,0:T(8,128)(2,1)S(1)} %fusion.3), channel_id=1, source_target_pairs={{0,4},{2,6},{4,0},{6,2},{8,12},{10,14},{12,8},{14,10},{1,5},{3,7},... | collective-permute-start | bytes 393224 | tf_op jit(solution)/shard_map/ppermute | solution.py:226
  20.3 1.5 %collective-permute-start.2 = (bf16[64,512]{1,0:T(8,128)(2,1)S(1)}, bf16[64,512]{1,0:T(8,128)(2,1)S(1)}, u32[]{:S(2)}, u32[]{:S(2)}) collective-permute-start(bf16[64,512]{1,0:T(8,128)(2,1)S(1)} %dynamic-slice_convert_fusion.7), channel_id=1, source_target_pairs={{0,2},{2,0},{4,6},{6,4},{8,10},{10,8},{12,14},{14,12},{1,3},{3,1},... | collective-permute-start | bytes 196616 | tf_op jit(solution)/shard_map/ppermute | solution.py:226
  21.8 1.4 %collective-permute-done.4 = bf16[64,512]{1,0:T(8,128)(2,1)S(1)} collective-permute-done((bf16[64,512]{1,0:T(8,128)(2,1)S(1)}, bf16[64,512]{1,0:T(8,128)(2,1)S(1)}, u32[]{:S(2)}, u32[]{:S(2)}) %collective-permute-start.4) | collective-permute-done | bytes 65568 | tf_op jit(solution)/shard_map/ppermute | solution.py:226
  23.2 2.6 %collective-permute-start.6 = (bf16[64,512]{1,0:T(8,128)(2,1)S(1)}, bf16[64,512]{1,0:T(8,128)(2,1)S(1)}, u32[]{:S(2)}, u32[]{:S(2)}) collective-permute-start(bf16[64,512]{1,0:T(8,128)(2,1)S(1)} %add_convert_fusion.7), channel_id=1, source_target_pairs={{0,8},{2,10},{4,12},{6,14},{8,0},{10,2},{12,4},{14,6},{1,9},{3,11}... | collective-permute-start | bytes 196616 | tf_op jit(solution)/shard_map/ppermute | solution.py:226
  25.9 0.0 collective-permute-done.2
  25.9 1.3 %collective-permute-start.5 = (bf16[64,512]{1,0:T(8,128)(2,1)S(1)}, bf16[64,512]{1,0:T(8,128)(2,1)S(1)}, u32[]{:S(2)}, u32[]{:S(2)}) collective-permute-start(bf16[64,512]{1,0:T(8,128)(2,1)S(1)} %add_convert_fusion.6), channel_id=1, source_target_pairs={{0,8},{2,10},{4,12},{6,14},{8,0},{10,2},{12,4},{14,6},{1,9},{3,11}... | collective-permute-start | bytes 196616 | tf_op jit(solution)/shard_map/ppermute | solution.py:226
  27.3 0.0 collective-permute-done.7
  27.3 0.5 %collective-permute-start.10 = (bf16[64,512]{1,0:T(8,128)(2,1)S(1)}, bf16[64,512]{1,0:T(8,128)(2,1)S(1)}, u32[]{:S(2)}, u32[]{:S(2)}) collective-permute-start(bf16[64,512]{1,0:T(8,128)(2,1)S(1)} %dynamic-slice_convert_fusion.4), channel_id=1, source_target_pairs={{0,4},{2,6},{4,0},{6,2},{8,12},{10,14},{12,8},{14,10},{1,5},{3,7},... | collective-permute-start | bytes 196616 | tf_op jit(solution)/shard_map/ppermute | solution.py:226
  27.9 0.0 collective-permute-done.8
  27.9 1.6 %collective-permute-start.11 = (bf16[64,512]{1,0:T(8,128)(2,1)S(1)}, bf16[64,512]{1,0:T(8,128)(2,1)S(1)}, u32[]{:S(2)}, u32[]{:S(2)}) collective-permute-start(bf16[64,512]{1,0:T(8,128)(2,1)S(1)} %dynamic-slice_convert_fusion.5), channel_id=1, source_target_pairs={{0,2},{2,0},{4,6},{6,4},{8,10},{10,8},{12,14},{14,12},{1,3},{3,1},... | collective-permute-start | bytes 196616 | tf_op jit(solution)/shard_map/ppermute | solution.py:226
  29.5 0.6 %collective-permute-done.6 = bf16[64,512]{1,0:T(8,128)(2,1)S(1)} collective-permute-done((bf16[64,512]{1,0:T(8,128)(2,1)S(1)}, bf16[64,512]{1,0:T(8,128)(2,1)S(1)}, u32[]{:S(2)}, u32[]{:S(2)}) %collective-permute-start.6) | collective-permute-done | bytes 65568 | tf_op jit(solution)/shard_map/ppermute | solution.py:226
  30.1 1.0 %collective-permute-start.9 = (bf16[64,512]{1,0:T(8,128)(2,1)S(1)}, bf16[64,512]{1,0:T(8,128)(2,1)S(1)}, u32[]{:S(2)}, u32[]{:S(2)}) collective-permute-start(bf16[64,512]{1,0:T(8,128)(2,1)S(1)} %add_convert_fusion.5), channel_id=1, source_target_pairs={{0,4},{2,6},{4,0},{6,2},{8,12},{10,14},{12,8},{14,10},{1,5},{3,7},... | collective-permute-start | bytes 196616 | tf_op jit(solution)/shard_map/ppermute | solution.py:226
  31.2 0.6 %collective-permute-done.5 = bf16[64,512]{1,0:T(8,128)(2,1)S(1)} collective-permute-done((bf16[64,512]{1,0:T(8,128)(2,1)S(1)}, bf16[64,512]{1,0:T(8,128)(2,1)S(1)}, u32[]{:S(2)}, u32[]{:S(2)}) %collective-permute-start.5) | collective-permute-done | bytes 65568 | tf_op jit(solution)/shard_map/ppermute | solution.py:226
  31.8 1.6 %collective-permute-start.12 = (bf16[64,512]{1,0:T(8,128)(2,1)S(1)}, bf16[64,512]{1,0:T(8,128)(2,1)S(1)}, u32[]{:S(2)}, u32[]{:S(2)}) collective-permute-start(bf16[64,512]{1,0:T(8,128)(2,1)S(1)} %add_convert_fusion.2), channel_id=1, source_target_pairs={{0,2},{2,0},{4,6},{6,4},{8,10},{10,8},{12,14},{14,12},{1,3},{3,1},... | collective-permute-start | bytes 196616 | tf_op jit(solution)/shard_map/ppermute | solution.py:226
  33.4 0.0 collective-permute-done.10
  33.4 1.4 %collective-permute-start.18 = (bf16[64,512]{1,0:T(8,128)(2,1)S(1)}, bf16[64,512]{1,0:T(8,128)(2,1)S(1)}, u32[]{:S(2)}, u32[]{:S(2)}) collective-permute-start(bf16[64,512]{1,0:T(8,128)(2,1)S(1)} %add_convert_fusion.3), channel_id=1, source_target_pairs={{0,8},{2,10},{4,12},{6,14},{8,0},{10,2},{12,4},{14,6},{1,9},{3,11}... | collective-permute-start | bytes 196616 | tf_op jit(solution)/shard_map/ppermute | solution.py:226
  34.8 0.0 collective-permute-done.11
  34.8 1.7 %collective-permute-start.15 = (bf16[64,512]{1,0:T(8,128)(2,1)S(1)}, bf16[64,512]{1,0:T(8,128)(2,1)S(1)}, u32[]{:S(2)}, u32[]{:S(2)}) collective-permute-start(bf16[64,512]{1,0:T(8,128)(2,1)S(1)} %add_convert_fusion.4), channel_id=1, source_target_pairs={{0,8},{2,10},{4,12},{6,14},{8,0},{10,2},{12,4},{14,6},{1,9},{3,11}... | collective-permute-start | bytes 196616 | tf_op jit(solution)/shard_map/ppermute | solution.py:226
  36.5 0.0 collective-permute-done.9
  36.5 0.7 %collective-permute-start.14 = (bf16[128,512]{1,0:T(8,128)(2,1)S(1)}, bf16[128,512]{1,0:T(8,128)(2,1)S(1)}, u32[]{:S(2)}, u32[]{:S(2)}) collective-permute-start(bf16[128,512]{1,0:T(8,128)(2,1)S(1)} %pad_maximum_fusion.1), channel_id=1, source_target_pairs={{0,2},{2,0},{4,6},{6,4},{8,10},{10,8},{12,14},{14,12},{1,3},{3,1},... | collective-permute-start | bytes 393224 | tf_op jit(solution)/shard_map/ppermute | solution.py:226
  37.2 0.0 collective-permute-done.12
  37.2 0.5 %collective-permute-start.13 = (bf16[128,512]{1,0:T(8,128)(2,1)S(1)}, bf16[128,512]{1,0:T(8,128)(2,1)S(1)}, u32[]{:S(2)}, u32[]{:S(2)}) collective-permute-start(bf16[128,512]{1,0:T(8,128)(2,1)S(1)} %pad_maximum_fusion), channel_id=1, source_target_pairs={{0,4},{2,6},{4,0},{6,2},{8,12},{10,14},{12,8},{14,10},{1,5},{3,7},... | collective-permute-start | bytes 393224 | tf_op jit(solution)/shard_map/ppermute | solution.py:226
  37.8 1.6 %collective-permute-done.18 = bf16[64,512]{1,0:T(8,128)(2,1)S(1)} collective-permute-done((bf16[64,512]{1,0:T(8,128)(2,1)S(1)}, bf16[64,512]{1,0:T(8,128)(2,1)S(1)}, u32[]{:S(2)}, u32[]{:S(2)}) %collective-permute-start.18) | collective-permute-done | bytes 65568 | tf_op jit(solution)/shard_map/ppermute | solution.py:226
  39.4 0.5 %collective-permute-start.19 = (bf16[64,512]{1,0:T(8,128)(2,1)S(1)}, bf16[64,512]{1,0:T(8,128)(2,1)S(1)}, u32[]{:S(2)}, u32[]{:S(2)}) collective-permute-start(bf16[64,512]{1,0:T(8,128)(2,1)S(1)} %add_convert_fusion), channel_id=1, source_target_pairs={{0,4},{2,6},{4,0},{6,2},{8,12},{10,14},{12,8},{14,10},{1,5},{3,7},... | collective-permute-start | bytes 196616 | tf_op jit(solution)/shard_map/ppermute | solution.py:226
  39.9 0.8 %collective-permute-done.15 = bf16[64,512]{1,0:T(8,128)(2,1)S(1)} collective-permute-done((bf16[64,512]{1,0:T(8,128)(2,1)S(1)}, bf16[64,512]{1,0:T(8,128)(2,1)S(1)}, u32[]{:S(2)}, u32[]{:S(2)}) %collective-permute-start.15) | collective-permute-done | bytes 65568 | tf_op jit(solution)/shard_map/ppermute | solution.py:226
  40.7 0.2 collective-permute-start.16
  40.9 2.8 %collective-permute-done.19 = bf16[64,512]{1,0:T(8,128)(2,1)S(1)} collective-permute-done((bf16[64,512]{1,0:T(8,128)(2,1)S(1)}, bf16[64,512]{1,0:T(8,128)(2,1)S(1)}, u32[]{:S(2)}, u32[]{:S(2)}) %collective-permute-start.19) | collective-permute-done | bytes 65568 | tf_op jit(solution)/shard_map/ppermute | solution.py:226
  43.7 0.8 %collective-permute-start.20 = (bf16[128,512]{1,0:T(8,128)(2,1)S(1)}, bf16[128,512]{1,0:T(8,128)(2,1)S(1)}, u32[]{:S(2)}, u32[]{:S(2)}) collective-permute-start(bf16[128,512]{1,0:T(8,128)(2,1)S(1)} %pad_maximum_fusion.3), channel_id=1, source_target_pairs={{0,2},{2,0},{4,6},{6,4},{8,10},{10,8},{12,14},{14,12},{1,3},{3,1},... | collective-permute-start | bytes 393224 | tf_op jit(solution)/shard_map/ppermute | solution.py:226
  44.5 0.6 %collective-permute-done.16 = bf16[64,512]{1,0:T(8,128)(2,1)S(1)} collective-permute-done((bf16[64,512]{1,0:T(8,128)(2,1)S(1)}, bf16[64,512]{1,0:T(8,128)(2,1)S(1)}, u32[]{:S(2)}, u32[]{:S(2)}) %collective-permute-start.16) | collective-permute-done | bytes 65568 | tf_op jit(solution)/shard_map/ppermute | solution.py:226
  45.1 0.8 %collective-permute-start.17 = (bf16[128,512]{1,0:T(8,128)(2,1)S(1)}, bf16[128,512]{1,0:T(8,128)(2,1)S(1)}, u32[]{:S(2)}, u32[]{:S(2)}) collective-permute-start(bf16[128,512]{1,0:T(8,128)(2,1)S(1)} %pad_maximum_fusion.2), channel_id=1, source_target_pairs={{0,4},{2,6},{4,0},{6,2},{8,12},{10,14},{12,8},{14,10},{1,5},{3,7},... | collective-permute-start | bytes 393224 | tf_op jit(solution)/shard_map/ppermute | solution.py:226
  45.9 0.0 collective-permute-done.14
  46.0 0.0 collective-permute-done.13
  46.0 0.0 copy-start.1
  46.0 0.0 copy-start.2
  46.0 0.1 broadcast_in_dim.2
  46.2 2.5 %collective-permute-done.20 = bf16[128,512]{1,0:T(8,128)(2,1)S(1)} collective-permute-done((bf16[128,512]{1,0:T(8,128)(2,1)S(1)}, bf16[128,512]{1,0:T(8,128)(2,1)S(1)}, u32[]{:S(2)}, u32[]{:S(2)}) %collective-permute-start.20) | collective-permute-done | bytes 131104 | tf_op jit(solution)/shard_map/ppermute | solution.py:226
  48.8 1.3 %collective-permute-done.17 = bf16[128,512]{1,0:T(8,128)(2,1)S(1)} collective-permute-done((bf16[128,512]{1,0:T(8,128)(2,1)S(1)}, bf16[128,512]{1,0:T(8,128)(2,1)S(1)}, u32[]{:S(2)}, u32[]{:S(2)}) %collective-permute-start.17) | collective-permute-done | bytes 131104 | tf_op jit(solution)/shard_map/ppermute | solution.py:226
  50.2 0.0 copy-done.1
  50.3 0.0 copy-done.2
  50.3 0.0 copy-start
  50.3 1.1 %convolution_convert_fusion = bf16[128,1024]{1,0:T(8,128)(2,1)} fusion(bf16[512,1024]{1,0:T(8,128)(2,1)S(1)} %maximum_dynamic-update-slice_fusion.3, s32[512]{0:T(512)S(1)} %copy-done.1, s32[128]{0:T(128)S(1)} %copy-done.2), kind=kOutput, calls=%fused_computation | convolution fusion | flops 134742016 | bytes 1313280 | tf_op jit(solution)/shard_map/dot_general | solution.py:364
  51.4 0.0 copy-done
  (38 shorter events, 0.9 us)
Async XLA Ops:
  0.6 11.6 %collective-permute-start.1 = (bf16[1,256,4096]{2,1,0:T(8,128)(2,1)}, bf16[1,256,4096]{2,1,0:T(8,128)(2,1)S(1)}, u32[]{:S(2)}, u32[]{:S(2)}) collective-permute-start(bf16[1,256,4096]{2,1,0:T(8,128)(2,1)} %rows_ref.1), channel_id=1, source_target_pairs={{1,0},{0,1},{3,2},{2,3},{5,4},{4,5},{7,6},{6,7},{9,8},{8,9},{11,10... | collective-permute-start | bytes 6291464 | tf_op jit(solution)/shard_map/ppermute | solution.py:334
  8.0 10.0 %collective-permute-start = (bf16[128,512]{1,0:T(8,128)(2,1)S(1)}, bf16[128,512]{1,0:T(8,128)(2,1)S(1)}, u32[]{:S(2)}, u32[]{:S(2)}) collective-permute-start(bf16[128,512]{1,0:T(8,128)(2,1)S(1)} %get-tuple-element.70.refs_0_), channel_id=1, source_target_pairs={{0,4},{2,6},{4,0},{6,2},{8,12},{10,14},{12,8},{14,10},{1,5},{3,7},... | collective-permute-start | bytes 393224 | tf_op jit(solution)/shard_map/ppermute | solution.py:226
  10.7 7.4 %collective-permute-start.3 = (bf16[128,512]{1,0:T(8,128)(2,1)S(1)}, bf16[128,512]{1,0:T(8,128)(2,1)S(1)}, u32[]{:S(2)}, u32[]{:S(2)}) collective-permute-start(bf16[128,512]{1,0:T(8,128)(2,1)S(1)} %get-tuple-element.77.refs_1_), channel_id=1, source_target_pairs={{0,2},{2,0},{4,6},{6,4},{8,10},{10,8},{12,14},{14,12},{1,3},{3,1},... | collective-permute-start | bytes 393224 | tf_op jit(solution)/shard_map/ppermute | solution.py:226
  17.4 9.9 %collective-permute-start.7 = (bf16[128,512]{1,0:T(8,128)(2,1)S(1)}, bf16[128,512]{1,0:T(8,128)(2,1)S(1)}, u32[]{:S(2)}, u32[]{:S(2)}) collective-permute-start(bf16[128,512]{1,0:T(8,128)(2,1)S(1)} %fusion.2), channel_id=1, source_target_pairs={{0,2},{2,0},{4,6},{6,4},{8,10},{10,8},{12,14},{14,12},{1,3},{3,1},... | collective-permute-start | bytes 393224 | tf_op jit(solution)/shard_map/ppermute | solution.py:226
  18.1 5.1 %collective-permute-start.4 = (bf16[64,512]{1,0:T(8,128)(2,1)S(1)}, bf16[64,512]{1,0:T(8,128)(2,1)S(1)}, u32[]{:S(2)}, u32[]{:S(2)}) collective-permute-start(bf16[64,512]{1,0:T(8,128)(2,1)S(1)} %dynamic-slice_convert_fusion.6), channel_id=1, source_target_pairs={{0,4},{2,6},{4,0},{6,2},{8,12},{10,14},{12,8},{14,10},{1,5},{3,7},... | collective-permute-start | bytes 196616 | tf_op jit(solution)/shard_map/ppermute | solution.py:226
  18.3 9.5 %collective-permute-start.8 = (bf16[128,512]{1,0:T(8,128)(2,1)S(1)}, bf16[128,512]{1,0:T(8,128)(2,1)S(1)}, u32[]{:S(2)}, u32[]{:S(2)}) collective-permute-start(bf16[128,512]{1,0:T(8,128)(2,1)S(1)} %fusion.3), channel_id=1, source_target_pairs={{0,4},{2,6},{4,0},{6,2},{8,12},{10,14},{12,8},{14,10},{1,5},{3,7},... | collective-permute-start | bytes 393224 | tf_op jit(solution)/shard_map/ppermute | solution.py:226
  20.3 5.6 %collective-permute-start.2 = (bf16[64,512]{1,0:T(8,128)(2,1)S(1)}, bf16[64,512]{1,0:T(8,128)(2,1)S(1)}, u32[]{:S(2)}, u32[]{:S(2)}) collective-permute-start(bf16[64,512]{1,0:T(8,128)(2,1)S(1)} %dynamic-slice_convert_fusion.7), channel_id=1, source_target_pairs={{0,2},{2,0},{4,6},{6,4},{8,10},{10,8},{12,14},{14,12},{1,3},{3,1},... | collective-permute-start | bytes 196616 | tf_op jit(solution)/shard_map/ppermute | solution.py:226
  23.2 6.9 %collective-permute-start.6 = (bf16[64,512]{1,0:T(8,128)(2,1)S(1)}, bf16[64,512]{1,0:T(8,128)(2,1)S(1)}, u32[]{:S(2)}, u32[]{:S(2)}) collective-permute-start(bf16[64,512]{1,0:T(8,128)(2,1)S(1)} %add_convert_fusion.7), channel_id=1, source_target_pairs={{0,8},{2,10},{4,12},{6,14},{8,0},{10,2},{12,4},{14,6},{1,9},{3,11}... | collective-permute-start | bytes 196616 | tf_op jit(solution)/shard_map/ppermute | solution.py:226
  25.9 5.8 %collective-permute-start.5 = (bf16[64,512]{1,0:T(8,128)(2,1)S(1)}, bf16[64,512]{1,0:T(8,128)(2,1)S(1)}, u32[]{:S(2)}, u32[]{:S(2)}) collective-permute-start(bf16[64,512]{1,0:T(8,128)(2,1)S(1)} %add_convert_fusion.6), channel_id=1, source_target_pairs={{0,8},{2,10},{4,12},{6,14},{8,0},{10,2},{12,4},{14,6},{1,9},{3,11}... | collective-permute-start | bytes 196616 | tf_op jit(solution)/shard_map/ppermute | solution.py:226
  27.3 6.0 %collective-permute-start.10 = (bf16[64,512]{1,0:T(8,128)(2,1)S(1)}, bf16[64,512]{1,0:T(8,128)(2,1)S(1)}, u32[]{:S(2)}, u32[]{:S(2)}) collective-permute-start(bf16[64,512]{1,0:T(8,128)(2,1)S(1)} %dynamic-slice_convert_fusion.4), channel_id=1, source_target_pairs={{0,4},{2,6},{4,0},{6,2},{8,12},{10,14},{12,8},{14,10},{1,5},{3,7},... | collective-permute-start | bytes 196616 | tf_op jit(solution)/shard_map/ppermute | solution.py:226
  27.9 6.9 %collective-permute-start.11 = (bf16[64,512]{1,0:T(8,128)(2,1)S(1)}, bf16[64,512]{1,0:T(8,128)(2,1)S(1)}, u32[]{:S(2)}, u32[]{:S(2)}) collective-permute-start(bf16[64,512]{1,0:T(8,128)(2,1)S(1)} %dynamic-slice_convert_fusion.5), channel_id=1, source_target_pairs={{0,2},{2,0},{4,6},{6,4},{8,10},{10,8},{12,14},{14,12},{1,3},{3,1},... | collective-permute-start | bytes 196616 | tf_op jit(solution)/shard_map/ppermute | solution.py:226
  30.1 6.3 %collective-permute-start.9 = (bf16[64,512]{1,0:T(8,128)(2,1)S(1)}, bf16[64,512]{1,0:T(8,128)(2,1)S(1)}, u32[]{:S(2)}, u32[]{:S(2)}) collective-permute-start(bf16[64,512]{1,0:T(8,128)(2,1)S(1)} %add_convert_fusion.5), channel_id=1, source_target_pairs={{0,4},{2,6},{4,0},{6,2},{8,12},{10,14},{12,8},{14,10},{1,5},{3,7},... | collective-permute-start | bytes 196616 | tf_op jit(solution)/shard_map/ppermute | solution.py:226
  31.8 5.4 %collective-permute-start.12 = (bf16[64,512]{1,0:T(8,128)(2,1)S(1)}, bf16[64,512]{1,0:T(8,128)(2,1)S(1)}, u32[]{:S(2)}, u32[]{:S(2)}) collective-permute-start(bf16[64,512]{1,0:T(8,128)(2,1)S(1)} %add_convert_fusion.2), channel_id=1, source_target_pairs={{0,2},{2,0},{4,6},{6,4},{8,10},{10,8},{12,14},{14,12},{1,3},{3,1},... | collective-permute-start | bytes 196616 | tf_op jit(solution)/shard_map/ppermute | solution.py:226
  33.4 5.9 %collective-permute-start.18 = (bf16[64,512]{1,0:T(8,128)(2,1)S(1)}, bf16[64,512]{1,0:T(8,128)(2,1)S(1)}, u32[]{:S(2)}, u32[]{:S(2)}) collective-permute-start(bf16[64,512]{1,0:T(8,128)(2,1)S(1)} %add_convert_fusion.3), channel_id=1, source_target_pairs={{0,8},{2,10},{4,12},{6,14},{8,0},{10,2},{12,4},{14,6},{1,9},{3,11}... | collective-permute-start | bytes 196616 | tf_op jit(solution)/shard_map/ppermute | solution.py:226
  34.8 5.9 %collective-permute-start.15 = (bf16[64,512]{1,0:T(8,128)(2,1)S(1)}, bf16[64,512]{1,0:T(8,128)(2,1)S(1)}, u32[]{:S(2)}, u32[]{:S(2)}) collective-permute-start(bf16[64,512]{1,0:T(8,128)(2,1)S(1)} %add_convert_fusion.4), channel_id=1, source_target_pairs={{0,8},{2,10},{4,12},{6,14},{8,0},{10,2},{12,4},{14,6},{1,9},{3,11}... | collective-permute-start | bytes 196616 | tf_op jit(solution)/shard_map/ppermute | solution.py:226
  36.5 9.4 %collective-permute-start.14 = (bf16[128,512]{1,0:T(8,128)(2,1)S(1)}, bf16[128,512]{1,0:T(8,128)(2,1)S(1)}, u32[]{:S(2)}, u32[]{:S(2)}) collective-permute-start(bf16[128,512]{1,0:T(8,128)(2,1)S(1)} %pad_maximum_fusion.1), channel_id=1, source_target_pairs={{0,2},{2,0},{4,6},{6,4},{8,10},{10,8},{12,14},{14,12},{1,3},{3,1},... | collective-permute-start | bytes 393224 | tf_op jit(solution)/shard_map/ppermute | solution.py:226
  37.2 8.7 %collective-permute-start.13 = (bf16[128,512]{1,0:T(8,128)(2,1)S(1)}, bf16[128,512]{1,0:T(8,128)(2,1)S(1)}, u32[]{:S(2)}, u32[]{:S(2)}) collective-permute-start(bf16[128,512]{1,0:T(8,128)(2,1)S(1)} %pad_maximum_fusion), channel_id=1, source_target_pairs={{0,4},{2,6},{4,0},{6,2},{8,12},{10,14},{12,8},{14,10},{1,5},{3,7},... | collective-permute-start | bytes 393224 | tf_op jit(solution)/shard_map/ppermute | solution.py:226
  39.4 4.3 %collective-permute-start.19 = (bf16[64,512]{1,0:T(8,128)(2,1)S(1)}, bf16[64,512]{1,0:T(8,128)(2,1)S(1)}, u32[]{:S(2)}, u32[]{:S(2)}) collective-permute-start(bf16[64,512]{1,0:T(8,128)(2,1)S(1)} %add_convert_fusion), channel_id=1, source_target_pairs={{0,4},{2,6},{4,0},{6,2},{8,12},{10,14},{12,8},{14,10},{1,5},{3,7},... | collective-permute-start | bytes 196616 | tf_op jit(solution)/shard_map/ppermute | solution.py:226
  40.7 4.3 %collective-permute-start.16 = (bf16[64,512]{1,0:T(8,128)(2,1)S(1)}, bf16[64,512]{1,0:T(8,128)(2,1)S(1)}, u32[]{:S(2)}, u32[]{:S(2)}) collective-permute-start(bf16[64,512]{1,0:T(8,128)(2,1)S(1)} %add_convert_fusion.1), channel_id=1, source_target_pairs={{0,2},{2,0},{4,6},{6,4},{8,10},{10,8},{12,14},{14,12},{1,3},{3,1},... | collective-permute-start | bytes 196616 | tf_op jit(solution)/shard_map/ppermute | solution.py:226
  43.7 5.0 %collective-permute-start.20 = (bf16[128,512]{1,0:T(8,128)(2,1)S(1)}, bf16[128,512]{1,0:T(8,128)(2,1)S(1)}, u32[]{:S(2)}, u32[]{:S(2)}) collective-permute-start(bf16[128,512]{1,0:T(8,128)(2,1)S(1)} %pad_maximum_fusion.3), channel_id=1, source_target_pairs={{0,2},{2,0},{4,6},{6,4},{8,10},{10,8},{12,14},{14,12},{1,3},{3,1},... | collective-permute-start | bytes 393224 | tf_op jit(solution)/shard_map/ppermute | solution.py:226
  45.1 5.0 %collective-permute-start.17 = (bf16[128,512]{1,0:T(8,128)(2,1)S(1)}, bf16[128,512]{1,0:T(8,128)(2,1)S(1)}, u32[]{:S(2)}, u32[]{:S(2)}) collective-permute-start(bf16[128,512]{1,0:T(8,128)(2,1)S(1)} %pad_maximum_fusion.2), channel_id=1, source_target_pairs={{0,4},{2,6},{4,0},{6,2},{8,12},{10,14},{12,8},{14,10},{1,5},{3,7},... | collective-permute-start | bytes 393224 | tf_op jit(solution)/shard_map/ppermute | solution.py:226
  46.0 4.2 %copy-start.1 = (s32[512]{0:T(512)S(1)}, s32[512]{0:T(512)}, u32[]{:S(2)}) copy-start(s32[512]{0:T(512)} %param.10) | copy-start | bytes 6148
  46.0 4.2 %copy-start.2 = (s32[128]{0:T(128)S(1)}, s32[128]{0:T(128)}, u32[]{:S(2)}) copy-start(s32[128]{0:T(128)} %param.11) | copy-start | bytes 1540
  50.3 1.1 %copy-start = (bf16[512,1024]{1,0:T(8,128)(2,1)}, bf16[512,1024]{1,0:T(8,128)(2,1)S(1)}, u32[]{:S(2)}) copy-start(bf16[512,1024]{1,0:T(8,128)(2,1)S(1)} %maximum_dynamic-update-slice_fusion.3) | copy-start | bytes 3145732

commit v27 on v26

--- a/solution.py
+++ b/solution.py
@@ -248,8 +248,7 @@
             sent = lax.dynamic_slice_in_dim(self.block, (1 - upper) * rows, rows, 0)
             sent = sent.astype(jnp.bfloat16)
             self.block = lax.dynamic_slice_in_dim(self.block, upper * rows, rows, 0)
-            if self.sent is None:
-                self.block, sent = lax.optimization_barrier((self.block, sent))
+            self.block, sent = lax.optimization_barrier((self.block, sent))
         self.sent = order.mark(sent)
         self.received = swap(self.sent, bit)
 

time: 51.5 us -> 51.5 us (level)
  no operation moved by 1% of the time
where the time goes in v27:
time: 51.5 us; the launch traced here: 51.4 us
  starting transfers between devices  24.3 us (47%)
  waiting for transfers between devices  12 us (23%)
  Pallas kernels  11.7 us (23%)
  matrix products  1.07 us (2%)
  between operations  1 us (2%)
  other arithmetic  0.66 us (1%)
  local copies, waits for them, and re-layouts  0.62 us (1%)
    ppermute x20, starting transfers between devices, swap(): return lax.ppermute(block, 'layer', route)  23.8 us
    ppermute x20, waiting for transfers between devices, swap(): return lax.ppermute(block, 'layer', route)  12 us
    pallas_call x2, Pallas kernels, call(): pl.pallas_call(kernel, out_shape=(scores,) + outs, in_specs=in_specs, out...  11.7 us
    dot_general x1, matrix products, shards(): advantage = jnp.dot(weights, scores, preferred_element_type=jnp.float32)  1.07 us
  transfers between devices with their start and end apart: 21, of which 9 were waited for; matrix products, arithmetic and copies ran while one was open for 2% of the time, Pallas kernels for 23%

profile of v27, /device:TPU:0, one launch (start us, length us, event | category | flops | bytes accessed | tf_op | source)
XLA Modules:
  0.0 51.4 jit_solution(11600592071638049506)
XLA Ops:
  0.6 0.5 %collective-permute-start.1 = (bf16[1,256,4096]{2,1,0:T(8,128)(2,1)}, bf16[1,256,4096]{2,1,0:T(8,128)(2,1)S(1)}, u32[]{:S(2)}, u32[]{:S(2)}) collective-permute-start(bf16[1,256,4096]{2,1,0:T(8,128)(2,1)} %rows_ref.1), channel_id=1, source_target_pairs={{1,0},{0,1},{3,2},{2,3},{5,4},{4,5},{7,6},{6,7},{9,8},{8,9},{11,10... | collective-permute-start | bytes 6291464 | tf_op jit(solution)/shard_map/ppermute | solution.py:333
  1.1 6.6 %shard_map.77 = (f32[2,256,512]{2,1,0:T(8,128)S(1)}, bf16[256,256]{1,0:T(8,128)(2,1)S(1)}, bf16[256,256]{1,0:T(8,128)(2,1)S(1)}) custom-call(bf16[1,256,4096]{2,1,0:T(8,128)(2,1)} %rows_ref.1, bf16[1,32,32]{2,1,0:T(8,128)(2,1)} %left_ref.1, bf16[1,128,128]{2,1,0:T(8,128)(2,1)} %right_ref.1, bf16[1,1024,4096]{2,1,0:T(8,128)(2,1)} %store_ref.3), custom_call_target="tpu_custom_call" | custom-call | flops 4294967296 | bytes 10485760 | tf_op jit(solution)/shard_map/pallas_call | solution.py:175
  7.8 0.1 fusion.11
  8.0 2.7 %collective-permute-start = (bf16[128,512]{1,0:T(8,128)(2,1)S(1)}, bf16[128,512]{1,0:T(8,128)(2,1)S(1)}, u32[]{:S(2)}, u32[]{:S(2)}) collective-permute-start(bf16[128,512]{1,0:T(8,128)(2,1)S(1)} %get-tuple-element.78.refs_0_), channel_id=1, source_target_pairs={{0,4},{2,6},{4,0},{6,2},{8,12},{10,14},{12,8},{14,10},{1,5},{3,7},... | collective-permute-start | bytes 393224 | tf_op jit(solution)/shard_map/ppermute | solution.py:226
  10.7 1.5 %collective-permute-start.3 = (bf16[128,512]{1,0:T(8,128)(2,1)S(1)}, bf16[128,512]{1,0:T(8,128)(2,1)S(1)}, u32[]{:S(2)}, u32[]{:S(2)}) collective-permute-start(bf16[128,512]{1,0:T(8,128)(2,1)S(1)} %get-tuple-element.85.refs_1_), channel_id=1, source_target_pairs={{0,2},{2,0},{4,6},{6,4},{8,10},{10,8},{12,14},{14,12},{1,3},{3,1},... | collective-permute-start | bytes 393224 | tf_op jit(solution)/shard_map/ppermute | solution.py:226
  12.2 0.0 collective-permute-done.1.rows_ref
  12.2 5.1 %shard_map.78 = f32[2,256,512]{2,1,0:T(8,128)S(1)} custom-call(bf16[1,256,4096]{2,1,0:T(8,128)(2,1)S(1)} %collective-permute-done.1.rows_ref, bf16[256,256]{1,0:T(8,128)(2,1)S(1)} %get-tuple-element.83.both_ref, bf16[256,256]{1,0:T(8,128)(2,1)S(1)} %get-tuple-element.84.mixer_ref, bf16[1,1024,4096]{2,1,0:T(8,128)(2,1)} %store_ref.3, ...), custom_call_target="tpu_custom_call" | custom-call | flops 4294967296 | bytes 10485760 | tf_op jit(solution)/shard_map/pallas_call | solution.py:175
  17.2 0.1 fusion.10
  17.4 0.6 %collective-permute-start.7 = (bf16[128,512]{1,0:T(8,128)(2,1)S(1)}, bf16[128,512]{1,0:T(8,128)(2,1)S(1)}, u32[]{:S(2)}, u32[]{:S(2)}) collective-permute-start(bf16[128,512]{1,0:T(8,128)(2,1)S(1)} %fusion.2), channel_id=1, source_target_pairs={{0,2},{2,0},{4,6},{6,4},{8,10},{10,8},{12,14},{14,12},{1,3},{3,1},... | collective-permute-start | bytes 393224 | tf_op jit(solution)/shard_map/ppermute | solution.py:226
  18.0 0.0 collective-permute-done
  18.1 0.0 collective-permute-done.3
  18.2 0.1 collective-permute-start.4
  18.4 2.0 %collective-permute-start.8 = (bf16[128,512]{1,0:T(8,128)(2,1)S(1)}, bf16[128,512]{1,0:T(8,128)(2,1)S(1)}, u32[]{:S(2)}, u32[]{:S(2)}) collective-permute-start(bf16[128,512]{1,0:T(8,128)(2,1)S(1)} %fusion.3), channel_id=1, source_target_pairs={{0,4},{2,6},{4,0},{6,2},{8,12},{10,14},{12,8},{14,10},{1,5},{3,7},... | collective-permute-start | bytes 393224 | tf_op jit(solution)/shard_map/ppermute | solution.py:226
  20.4 1.5 %collective-permute-start.2 = (bf16[64,512]{1,0:T(8,128)(2,1)S(1)}, bf16[64,512]{1,0:T(8,128)(2,1)S(1)}, u32[]{:S(2)}, u32[]{:S(2)}) collective-permute-start(bf16[64,512]{1,0:T(8,128)(2,1)S(1)} %dynamic-slice_convert_fusion.7), channel_id=1, source_target_pairs={{0,2},{2,0},{4,6},{6,4},{8,10},{10,8},{12,14},{14,12},{1,3},{3,1},... | collective-permute-start | bytes 196616 | tf_op jit(solution)/shard_map/ppermute | solution.py:226
  21.9 1.4 %collective-permute-done.4 = bf16[64,512]{1,0:T(8,128)(2,1)S(1)} collective-permute-done((bf16[64,512]{1,0:T(8,128)(2,1)S(1)}, bf16[64,512]{1,0:T(8,128)(2,1)S(1)}, u32[]{:S(2)}, u32[]{:S(2)}) %collective-permute-start.4) | collective-permute-done | bytes 65568 | tf_op jit(solution)/shard_map/ppermute | solution.py:226
  23.3 2.6 %collective-permute-start.6 = (bf16[64,512]{1,0:T(8,128)(2,1)S(1)}, bf16[64,512]{1,0:T(8,128)(2,1)S(1)}, u32[]{:S(2)}, u32[]{:S(2)}) collective-permute-start(bf16[64,512]{1,0:T(8,128)(2,1)S(1)} %add_convert_fusion.7), channel_id=1, source_target_pairs={{0,8},{2,10},{4,12},{6,14},{8,0},{10,2},{12,4},{14,6},{1,9},{3,11}... | collective-permute-start | bytes 196616 | tf_op jit(solution)/shard_map/ppermute | solution.py:226
  25.9 0.0 collective-permute-done.2
  26.0 1.3 %collective-permute-start.5 = (bf16[64,512]{1,0:T(8,128)(2,1)S(1)}, bf16[64,512]{1,0:T(8,128)(2,1)S(1)}, u32[]{:S(2)}, u32[]{:S(2)}) collective-permute-start(bf16[64,512]{1,0:T(8,128)(2,1)S(1)} %add_convert_fusion.6), channel_id=1, source_target_pairs={{0,8},{2,10},{4,12},{6,14},{8,0},{10,2},{12,4},{14,6},{1,9},{3,11}... | collective-permute-start | bytes 196616 | tf_op jit(solution)/shard_map/ppermute | solution.py:226
  27.3 0.0 collective-permute-done.7
  27.4 0.5 %collective-permute-start.10 = (bf16[64,512]{1,0:T(8,128)(2,1)S(1)}, bf16[64,512]{1,0:T(8,128)(2,1)S(1)}, u32[]{:S(2)}, u32[]{:S(2)}) collective-permute-start(bf16[64,512]{1,0:T(8,128)(2,1)S(1)} %dynamic-slice_convert_fusion.4), channel_id=1, source_target_pairs={{0,4},{2,6},{4,0},{6,2},{8,12},{10,14},{12,8},{14,10},{1,5},{3,7},... | collective-permute-start | bytes 196616 | tf_op jit(solution)/shard_map/ppermute | solution.py:226
  27.9 0.0 collective-permute-done.8
  28.0 1.6 %collective-permute-start.11 = (bf16[64,512]{1,0:T(8,128)(2,1)S(1)}, bf16[64,512]{1,0:T(8,128)(2,1)S(1)}, u32[]{:S(2)}, u32[]{:S(2)}) collective-permute-start(bf16[64,512]{1,0:T(8,128)(2,1)S(1)} %dynamic-slice_convert_fusion.5), channel_id=1, source_target_pairs={{0,2},{2,0},{4,6},{6,4},{8,10},{10,8},{12,14},{14,12},{1,3},{3,1},... | collective-permute-start | bytes 196616 | tf_op jit(solution)/shard_map/ppermute | solution.py:226
  29.6 0.6 %collective-permute-done.6 = bf16[64,512]{1,0:T(8,128)(2,1)S(1)} collective-permute-done((bf16[64,512]{1,0:T(8,128)(2,1)S(1)}, bf16[64,512]{1,0:T(8,128)(2,1)S(1)}, u32[]{:S(2)}, u32[]{:S(2)}) %collective-permute-start.6) | collective-permute-done | bytes 65568 | tf_op jit(solution)/shard_map/ppermute | solution.py:226
  30.2 1.1 %collective-permute-start.9 = (bf16[64,512]{1,0:T(8,128)(2,1)S(1)}, bf16[64,512]{1,0:T(8,128)(2,1)S(1)}, u32[]{:S(2)}, u32[]{:S(2)}) collective-permute-start(bf16[64,512]{1,0:T(8,128)(2,1)S(1)} %add_convert_fusion.5), channel_id=1, source_target_pairs={{0,4},{2,6},{4,0},{6,2},{8,12},{10,14},{12,8},{14,10},{1,5},{3,7},... | collective-permute-start | bytes 196616 | tf_op jit(solution)/shard_map/ppermute | solution.py:226
  31.3 0.5 %collective-permute-done.5 = bf16[64,512]{1,0:T(8,128)(2,1)S(1)} collective-permute-done((bf16[64,512]{1,0:T(8,128)(2,1)S(1)}, bf16[64,512]{1,0:T(8,128)(2,1)S(1)}, u32[]{:S(2)}, u32[]{:S(2)}) %collective-permute-start.5) | collective-permute-done | bytes 65568 | tf_op jit(solution)/shard_map/ppermute | solution.py:226
  31.8 1.6 %collective-permute-start.12 = (bf16[64,512]{1,0:T(8,128)(2,1)S(1)}, bf16[64,512]{1,0:T(8,128)(2,1)S(1)}, u32[]{:S(2)}, u32[]{:S(2)}) collective-permute-start(bf16[64,512]{1,0:T(8,128)(2,1)S(1)} %add_convert_fusion.2), channel_id=1, source_target_pairs={{0,2},{2,0},{4,6},{6,4},{8,10},{10,8},{12,14},{14,12},{1,3},{3,1},... | collective-permute-start | bytes 196616 | tf_op jit(solution)/shard_map/ppermute | solution.py:226
  33.4 0.0 collective-permute-done.10
  33.5 1.3 %collective-permute-start.18 = (bf16[64,512]{1,0:T(8,128)(2,1)S(1)}, bf16[64,512]{1,0:T(8,128)(2,1)S(1)}, u32[]{:S(2)}, u32[]{:S(2)}) collective-permute-start(bf16[64,512]{1,0:T(8,128)(2,1)S(1)} %add_convert_fusion.3), channel_id=1, source_target_pairs={{0,8},{2,10},{4,12},{6,14},{8,0},{10,2},{12,4},{14,6},{1,9},{3,11}... | collective-permute-start | bytes 196616 | tf_op jit(solution)/shard_map/ppermute | solution.py:226
  34.8 0.0 collective-permute-done.11
  34.8 1.7 %collective-permute-start.15 = (bf16[64,512]{1,0:T(8,128)(2,1)S(1)}, bf16[64,512]{1,0:T(8,128)(2,1)S(1)}, u32[]{:S(2)}, u32[]{:S(2)}) collective-permute-start(bf16[64,512]{1,0:T(8,128)(2,1)S(1)} %add_convert_fusion.4), channel_id=1, source_target_pairs={{0,8},{2,10},{4,12},{6,14},{8,0},{10,2},{12,4},{14,6},{1,9},{3,11}... | collective-permute-start | bytes 196616 | tf_op jit(solution)/shard_map/ppermute | solution.py:226
  36.5 0.0 collective-permute-done.9
  36.6 0.7 %collective-permute-start.14 = (bf16[128,512]{1,0:T(8,128)(2,1)S(1)}, bf16[128,512]{1,0:T(8,128)(2,1)S(1)}, u32[]{:S(2)}, u32[]{:S(2)}) collective-permute-start(bf16[128,512]{1,0:T(8,128)(2,1)S(1)} %pad_maximum_fusion.1), channel_id=1, source_target_pairs={{0,2},{2,0},{4,6},{6,4},{8,10},{10,8},{12,14},{14,12},{1,3},{3,1},... | collective-permute-start | bytes 393224 | tf_op jit(solution)/shard_map/ppermute | solution.py:226
  37.2 0.0 collective-permute-done.12
  37.3 0.5 %collective-permute-start.13 = (bf16[128,512]{1,0:T(8,128)(2,1)S(1)}, bf16[128,512]{1,0:T(8,128)(2,1)S(1)}, u32[]{:S(2)}, u32[]{:S(2)}) collective-permute-start(bf16[128,512]{1,0:T(8,128)(2,1)S(1)} %pad_maximum_fusion), channel_id=1, source_target_pairs={{0,4},{2,6},{4,0},{6,2},{8,12},{10,14},{12,8},{14,10},{1,5},{3,7},... | collective-permute-start | bytes 393224 | tf_op jit(solution)/shard_map/ppermute | solution.py:226
  37.8 1.6 %collective-permute-done.18 = bf16[64,512]{1,0:T(8,128)(2,1)S(1)} collective-permute-done((bf16[64,512]{1,0:T(8,128)(2,1)S(1)}, bf16[64,512]{1,0:T(8,128)(2,1)S(1)}, u32[]{:S(2)}, u32[]{:S(2)}) %collective-permute-start.18) | collective-permute-done | bytes 65568 | tf_op jit(solution)/shard_map/ppermute | solution.py:226
  39.4 0.5 collective-permute-start.19
  39.9 0.8 %collective-permute-done.15 = bf16[64,512]{1,0:T(8,128)(2,1)S(1)} collective-permute-done((bf16[64,512]{1,0:T(8,128)(2,1)S(1)}, bf16[64,512]{1,0:T(8,128)(2,1)S(1)}, u32[]{:S(2)}, u32[]{:S(2)}) %collective-permute-start.15) | collective-permute-done | bytes 65568 | tf_op jit(solution)/shard_map/ppermute | solution.py:226
  40.7 0.2 collective-permute-start.16
  41.0 2.8 %collective-permute-done.19 = bf16[64,512]{1,0:T(8,128)(2,1)S(1)} collective-permute-done((bf16[64,512]{1,0:T(8,128)(2,1)S(1)}, bf16[64,512]{1,0:T(8,128)(2,1)S(1)}, u32[]{:S(2)}, u32[]{:S(2)}) %collective-permute-start.19) | collective-permute-done | bytes 65568 | tf_op jit(solution)/shard_map/ppermute | solution.py:226
  43.8 0.8 %collective-permute-start.20 = (bf16[128,512]{1,0:T(8,128)(2,1)S(1)}, bf16[128,512]{1,0:T(8,128)(2,1)S(1)}, u32[]{:S(2)}, u32[]{:S(2)}) collective-permute-start(bf16[128,512]{1,0:T(8,128)(2,1)S(1)} %pad_maximum_fusion.3), channel_id=1, source_target_pairs={{0,2},{2,0},{4,6},{6,4},{8,10},{10,8},{12,14},{14,12},{1,3},{3,1},... | collective-permute-start | bytes 393224 | tf_op jit(solution)/shard_map/ppermute | solution.py:226
  44.5 0.5 %collective-permute-done.16 = bf16[64,512]{1,0:T(8,128)(2,1)S(1)} collective-permute-done((bf16[64,512]{1,0:T(8,128)(2,1)S(1)}, bf16[64,512]{1,0:T(8,128)(2,1)S(1)}, u32[]{:S(2)}, u32[]{:S(2)}) %collective-permute-start.16) | collective-permute-done | bytes 65568 | tf_op jit(solution)/shard_map/ppermute | solution.py:226
  45.1 0.8 %collective-permute-start.17 = (bf16[128,512]{1,0:T(8,128)(2,1)S(1)}, bf16[128,512]{1,0:T(8,128)(2,1)S(1)}, u32[]{:S(2)}, u32[]{:S(2)}) collective-permute-start(bf16[128,512]{1,0:T(8,128)(2,1)S(1)} %pad_maximum_fusion.2), channel_id=1, source_target_pairs={{0,4},{2,6},{4,0},{6,2},{8,12},{10,14},{12,8},{14,10},{1,5},{3,7},... | collective-permute-start | bytes 393224 | tf_op jit(solution)/shard_map/ppermute | solution.py:226
  46.0 0.0 collective-permute-done.14
  46.0 0.0 collective-permute-done.13
  46.1 0.0 copy-start.1
  46.1 0.0 copy-start.2
  46.1 0.1 broadcast_in_dim.2
  46.3 2.5 %collective-permute-done.20 = bf16[128,512]{1,0:T(8,128)(2,1)S(1)} collective-permute-done((bf16[128,512]{1,0:T(8,128)(2,1)S(1)}, bf16[128,512]{1,0:T(8,128)(2,1)S(1)}, u32[]{:S(2)}, u32[]{:S(2)}) %collective-permute-start.20) | collective-permute-done | bytes 131104 | tf_op jit(solution)/shard_map/ppermute | solution.py:226
  48.9 1.3 %collective-permute-done.17 = bf16[128,512]{1,0:T(8,128)(2,1)S(1)} collective-permute-done((bf16[128,512]{1,0:T(8,128)(2,1)S(1)}, bf16[128,512]{1,0:T(8,128)(2,1)S(1)}, u32[]{:S(2)}, u32[]{:S(2)}) %collective-permute-start.17) | collective-permute-done | bytes 131104 | tf_op jit(solution)/shard_map/ppermute | solution.py:226
  50.3 0.0 copy-done.1
  50.3 0.0 copy-done.2
  50.3 0.0 copy-start
  50.3 1.1 %convolution_convert_fusion = bf16[128,1024]{1,0:T(8,128)(2,1)} fusion(bf16[512,1024]{1,0:T(8,128)(2,1)S(1)} %maximum_dynamic-update-slice_fusion.3, s32[512]{0:T(512)S(1)} %copy-done.1, s32[128]{0:T(128)S(1)} %copy-done.2), kind=kOutput, calls=%fused_computation | convolution fusion | flops 134742016 | bytes 1313280 | tf_op jit(solution)/shard_map/dot_general | solution.py:363
  51.4 0.0 copy-done
  (42 shorter events, 1.0 us)
Async XLA Ops:
  0.6 11.6 %collective-permute-start.1 = (bf16[1,256,4096]{2,1,0:T(8,128)(2,1)}, bf16[1,256,4096]{2,1,0:T(8,128)(2,1)S(1)}, u32[]{:S(2)}, u32[]{:S(2)}) collective-permute-start(bf16[1,256,4096]{2,1,0:T(8,128)(2,1)} %rows_ref.1), channel_id=1, source_target_pairs={{1,0},{0,1},{3,2},{2,3},{5,4},{4,5},{7,6},{6,7},{9,8},{8,9},{11,10... | collective-permute-start | bytes 6291464 | tf_op jit(solution)/shard_map/ppermute | solution.py:333
  8.0 10.0 %collective-permute-start = (bf16[128,512]{1,0:T(8,128)(2,1)S(1)}, bf16[128,512]{1,0:T(8,128)(2,1)S(1)}, u32[]{:S(2)}, u32[]{:S(2)}) collective-permute-start(bf16[128,512]{1,0:T(8,128)(2,1)S(1)} %get-tuple-element.78.refs_0_), channel_id=1, source_target_pairs={{0,4},{2,6},{4,0},{6,2},{8,12},{10,14},{12,8},{14,10},{1,5},{3,7},... | collective-permute-start | bytes 393224 | tf_op jit(solution)/shard_map/ppermute | solution.py:226
  10.7 7.4 %collective-permute-start.3 = (bf16[128,512]{1,0:T(8,128)(2,1)S(1)}, bf16[128,512]{1,0:T(8,128)(2,1)S(1)}, u32[]{:S(2)}, u32[]{:S(2)}) collective-permute-start(bf16[128,512]{1,0:T(8,128)(2,1)S(1)} %get-tuple-element.85.refs_1_), channel_id=1, source_target_pairs={{0,2},{2,0},{4,6},{6,4},{8,10},{10,8},{12,14},{14,12},{1,3},{3,1},... | collective-permute-start | bytes 393224 | tf_op jit(solution)/shard_map/ppermute | solution.py:226
  17.4 9.9 %collective-permute-start.7 = (bf16[128,512]{1,0:T(8,128)(2,1)S(1)}, bf16[128,512]{1,0:T(8,128)(2,1)S(1)}, u32[]{:S(2)}, u32[]{:S(2)}) collective-permute-start(bf16[128,512]{1,0:T(8,128)(2,1)S(1)} %fusion.2), channel_id=1, source_target_pairs={{0,2},{2,0},{4,6},{6,4},{8,10},{10,8},{12,14},{14,12},{1,3},{3,1},... | collective-permute-start | bytes 393224 | tf_op jit(solution)/shard_map/ppermute | solution.py:226
  18.2 5.1 %collective-permute-start.4 = (bf16[64,512]{1,0:T(8,128)(2,1)S(1)}, bf16[64,512]{1,0:T(8,128)(2,1)S(1)}, u32[]{:S(2)}, u32[]{:S(2)}) collective-permute-start(bf16[64,512]{1,0:T(8,128)(2,1)S(1)} %dynamic-slice_convert_fusion.6), channel_id=1, source_target_pairs={{0,4},{2,6},{4,0},{6,2},{8,12},{10,14},{12,8},{14,10},{1,5},{3,7},... | collective-permute-start | bytes 196616 | tf_op jit(solution)/shard_map/ppermute | solution.py:226
  18.4 9.6 %collective-permute-start.8 = (bf16[128,512]{1,0:T(8,128)(2,1)S(1)}, bf16[128,512]{1,0:T(8,128)(2,1)S(1)}, u32[]{:S(2)}, u32[]{:S(2)}) collective-permute-start(bf16[128,512]{1,0:T(8,128)(2,1)S(1)} %fusion.3), channel_id=1, source_target_pairs={{0,4},{2,6},{4,0},{6,2},{8,12},{10,14},{12,8},{14,10},{1,5},{3,7},... | collective-permute-start | bytes 393224 | tf_op jit(solution)/shard_map/ppermute | solution.py:226
  20.4 5.6 %collective-permute-start.2 = (bf16[64,512]{1,0:T(8,128)(2,1)S(1)}, bf16[64,512]{1,0:T(8,128)(2,1)S(1)}, u32[]{:S(2)}, u32[]{:S(2)}) collective-permute-start(bf16[64,512]{1,0:T(8,128)(2,1)S(1)} %dynamic-slice_convert_fusion.7), channel_id=1, source_target_pairs={{0,2},{2,0},{4,6},{6,4},{8,10},{10,8},{12,14},{14,12},{1,3},{3,1},... | collective-permute-start | bytes 196616 | tf_op jit(solution)/shard_map/ppermute | solution.py:226
  23.3 6.9 %collective-permute-start.6 = (bf16[64,512]{1,0:T(8,128)(2,1)S(1)}, bf16[64,512]{1,0:T(8,128)(2,1)S(1)}, u32[]{:S(2)}, u32[]{:S(2)}) collective-permute-start(bf16[64,512]{1,0:T(8,128)(2,1)S(1)} %add_convert_fusion.7), channel_id=1, source_target_pairs={{0,8},{2,10},{4,12},{6,14},{8,0},{10,2},{12,4},{14,6},{1,9},{3,11}... | collective-permute-start | bytes 196616 | tf_op jit(solution)/shard_map/ppermute | solution.py:226
  26.0 5.8 %collective-permute-start.5 = (bf16[64,512]{1,0:T(8,128)(2,1)S(1)}, bf16[64,512]{1,0:T(8,128)(2,1)S(1)}, u32[]{:S(2)}, u32[]{:S(2)}) collective-permute-start(bf16[64,512]{1,0:T(8,128)(2,1)S(1)} %add_convert_fusion.6), channel_id=1, source_target_pairs={{0,8},{2,10},{4,12},{6,14},{8,0},{10,2},{12,4},{14,6},{1,9},{3,11}... | collective-permute-start | bytes 196616 | tf_op jit(solution)/shard_map/ppermute | solution.py:226
  27.4 6.0 %collective-permute-start.10 = (bf16[64,512]{1,0:T(8,128)(2,1)S(1)}, bf16[64,512]{1,0:T(8,128)(2,1)S(1)}, u32[]{:S(2)}, u32[]{:S(2)}) collective-permute-start(bf16[64,512]{1,0:T(8,128)(2,1)S(1)} %dynamic-slice_convert_fusion.4), channel_id=1, source_target_pairs={{0,4},{2,6},{4,0},{6,2},{8,12},{10,14},{12,8},{14,10},{1,5},{3,7},... | collective-permute-start | bytes 196616 | tf_op jit(solution)/shard_map/ppermute | solution.py:226
  28.0 6.8 %collective-permute-start.11 = (bf16[64,512]{1,0:T(8,128)(2,1)S(1)}, bf16[64,512]{1,0:T(8,128)(2,1)S(1)}, u32[]{:S(2)}, u32[]{:S(2)}) collective-permute-start(bf16[64,512]{1,0:T(8,128)(2,1)S(1)} %dynamic-slice_convert_fusion.5), channel_id=1, source_target_pairs={{0,2},{2,0},{4,6},{6,4},{8,10},{10,8},{12,14},{14,12},{1,3},{3,1},... | collective-permute-start | bytes 196616 | tf_op jit(solution)/shard_map/ppermute | solution.py:226
  30.2 6.3 %collective-permute-start.9 = (bf16[64,512]{1,0:T(8,128)(2,1)S(1)}, bf16[64,512]{1,0:T(8,128)(2,1)S(1)}, u32[]{:S(2)}, u32[]{:S(2)}) collective-permute-start(bf16[64,512]{1,0:T(8,128)(2,1)S(1)} %add_convert_fusion.5), channel_id=1, source_target_pairs={{0,4},{2,6},{4,0},{6,2},{8,12},{10,14},{12,8},{14,10},{1,5},{3,7},... | collective-permute-start | bytes 196616 | tf_op jit(solution)/shard_map/ppermute | solution.py:226
  31.8 5.4 %collective-permute-start.12 = (bf16[64,512]{1,0:T(8,128)(2,1)S(1)}, bf16[64,512]{1,0:T(8,128)(2,1)S(1)}, u32[]{:S(2)}, u32[]{:S(2)}) collective-permute-start(bf16[64,512]{1,0:T(8,128)(2,1)S(1)} %add_convert_fusion.2), channel_id=1, source_target_pairs={{0,2},{2,0},{4,6},{6,4},{8,10},{10,8},{12,14},{14,12},{1,3},{3,1},... | collective-permute-start | bytes 196616 | tf_op jit(solution)/shard_map/ppermute | solution.py:226
  33.5 5.9 %collective-permute-start.18 = (bf16[64,512]{1,0:T(8,128)(2,1)S(1)}, bf16[64,512]{1,0:T(8,128)(2,1)S(1)}, u32[]{:S(2)}, u32[]{:S(2)}) collective-permute-start(bf16[64,512]{1,0:T(8,128)(2,1)S(1)} %add_convert_fusion.3), channel_id=1, source_target_pairs={{0,8},{2,10},{4,12},{6,14},{8,0},{10,2},{12,4},{14,6},{1,9},{3,11}... | collective-permute-start | bytes 196616 | tf_op jit(solution)/shard_map/ppermute | solution.py:226
  34.8 5.9 %collective-permute-start.15 = (bf16[64,512]{1,0:T(8,128)(2,1)S(1)}, bf16[64,512]{1,0:T(8,128)(2,1)S(1)}, u32[]{:S(2)}, u32[]{:S(2)}) collective-permute-start(bf16[64,512]{1,0:T(8,128)(2,1)S(1)} %add_convert_fusion.4), channel_id=1, source_target_pairs={{0,8},{2,10},{4,12},{6,14},{8,0},{10,2},{12,4},{14,6},{1,9},{3,11}... | collective-permute-start | bytes 196616 | tf_op jit(solution)/shard_map/ppermute | solution.py:226
  36.6 9.4 %collective-permute-start.14 = (bf16[128,512]{1,0:T(8,128)(2,1)S(1)}, bf16[128,512]{1,0:T(8,128)(2,1)S(1)}, u32[]{:S(2)}, u32[]{:S(2)}) collective-permute-start(bf16[128,512]{1,0:T(8,128)(2,1)S(1)} %pad_maximum_fusion.1), channel_id=1, source_target_pairs={{0,2},{2,0},{4,6},{6,4},{8,10},{10,8},{12,14},{14,12},{1,3},{3,1},... | collective-permute-start | bytes 393224 | tf_op jit(solution)/shard_map/ppermute | solution.py:226
  37.3 8.7 %collective-permute-start.13 = (bf16[128,512]{1,0:T(8,128)(2,1)S(1)}, bf16[128,512]{1,0:T(8,128)(2,1)S(1)}, u32[]{:S(2)}, u32[]{:S(2)}) collective-permute-start(bf16[128,512]{1,0:T(8,128)(2,1)S(1)} %pad_maximum_fusion), channel_id=1, source_target_pairs={{0,4},{2,6},{4,0},{6,2},{8,12},{10,14},{12,8},{14,10},{1,5},{3,7},... | collective-permute-start | bytes 393224 | tf_op jit(solution)/shard_map/ppermute | solution.py:226
  39.4 4.3 %collective-permute-start.19 = (bf16[64,512]{1,0:T(8,128)(2,1)S(1)}, bf16[64,512]{1,0:T(8,128)(2,1)S(1)}, u32[]{:S(2)}, u32[]{:S(2)}) collective-permute-start(bf16[64,512]{1,0:T(8,128)(2,1)S(1)} %add_convert_fusion), channel_id=1, source_target_pairs={{0,4},{2,6},{4,0},{6,2},{8,12},{10,14},{12,8},{14,10},{1,5},{3,7},... | collective-permute-start | bytes 196616 | tf_op jit(solution)/shard_map/ppermute | solution.py:226
  40.7 4.3 %collective-permute-start.16 = (bf16[64,512]{1,0:T(8,128)(2,1)S(1)}, bf16[64,512]{1,0:T(8,128)(2,1)S(1)}, u32[]{:S(2)}, u32[]{:S(2)}) collective-permute-start(bf16[64,512]{1,0:T(8,128)(2,1)S(1)} %add_convert_fusion.1), channel_id=1, source_target_pairs={{0,2},{2,0},{4,6},{6,4},{8,10},{10,8},{12,14},{14,12},{1,3},{3,1},... | collective-permute-start | bytes 196616 | tf_op jit(solution)/shard_map/ppermute | solution.py:226
  43.8 5.0 %collective-permute-start.20 = (bf16[128,512]{1,0:T(8,128)(2,1)S(1)}, bf16[128,512]{1,0:T(8,128)(2,1)S(1)}, u32[]{:S(2)}, u32[]{:S(2)}) collective-permute-start(bf16[128,512]{1,0:T(8,128)(2,1)S(1)} %pad_maximum_fusion.3), channel_id=1, source_target_pairs={{0,2},{2,0},{4,6},{6,4},{8,10},{10,8},{12,14},{14,12},{1,3},{3,1},... | collective-permute-start | bytes 393224 | tf_op jit(solution)/shard_map/ppermute | solution.py:226
  45.1 5.0 %collective-permute-start.17 = (bf16[128,512]{1,0:T(8,128)(2,1)S(1)}, bf16[128,512]{1,0:T(8,128)(2,1)S(1)}, u32[]{:S(2)}, u32[]{:S(2)}) collective-permute-start(bf16[128,512]{1,0:T(8,128)(2,1)S(1)} %pad_maximum_fusion.2), channel_id=1, source_target_pairs={{0,4},{2,6},{4,0},{6,2},{8,12},{10,14},{12,8},{14,10},{1,5},{3,7},... | collective-permute-start | bytes 393224 | tf_op jit(solution)/shard_map/ppermute | solution.py:226
  46.1 4.2 %copy-start.1 = (s32[512]{0:T(512)S(1)}, s32[512]{0:T(512)}, u32[]{:S(2)}) copy-start(s32[512]{0:T(512)} %param.10) | copy-start | bytes 6148
  46.1 4.2 %copy-start.2 = (s32[128]{0:T(128)S(1)}, s32[128]{0:T(128)}, u32[]{:S(2)}) copy-start(s32[128]{0:T(128)} %param.11) | copy-start | bytes 1540
  50.3 1.1 %copy-start = (bf16[512,1024]{1,0:T(8,128)(2,1)}, bf16[512,1024]{1,0:T(8,128)(2,1)S(1)}, u32[]{:S(2)}) copy-start(bf16[512,1024]{1,0:T(8,128)(2,1)S(1)} %maximum_dynamic-update-slice_fusion.3) | copy-start | bytes 3145732
